TPU v7x, 32 devices: a whole 2x2x4 slice. The times are simulated.
32 devices in a mesh: groups: 2 (over x), expert: 16 (over z, y, core).
Axes of the slice: x: 2, y: 2, z: 4, core: 2. Of those that a mesh axis runs over, the one named last changes fastest.
Arguments:
- tokens: bfloat16 [2048, 4096], P(('groups', 'expert')), parts along dimension 0, may hold values from -6 to 6
- routes: int32 [2048, 8], P(('groups', 'expert')), parts along dimension 0, may hold values from 0 to 15, all different within a row; in each aligned block of 64 rows (0 to 63, 64 to 127, ...) at most 64 rows name the same one
- gate_num: int32 [2048, 8], P(('groups', 'expert')), parts along dimension 0, may hold values from 1 to 32767
- gate_up_q: bfloat16 [16, 4096, 1536], P('expert'), may hold values from -127 to 127
- gate_up_scale: float32 [16, 1536], P('expert'), may hold values from 5e-05 to 0.0005
- down_q: bfloat16 [16, 768, 4096], P('expert'), may hold values from -127 to 127
- down_scale: float32 [16, 4096], P('expert'), may hold values from 0.0003 to 0.003
Outputs:
- mixed: bfloat16 [2048, 4096], P(('groups', 'expert')), parts along dimension 0
There are 2 independent parts, one for each index of `groups`. A program takes and returns all parts, laid end to end along the dimension named above; an argument that names none is the same for every part. Nothing has to cross between parts.
Inputs may be any that keep to these rules, and one draw needn't show every extreme that they name: `routes`: each row names 8 different experts; among the 64 rows of one device no expert is named more than 64 times, a bound that some block reaches.
All inputs are finite; a program needn't handle non-finite values.
Results may differ from a plain program's by a relative error of at most 0.0057.
Values may be sent and summed in bfloat16 or wider, within the bound.
No kernel may reach another device: no remote copies, remote signals or barrier semaphores. Data moves between devices by JAX's collectives and lax.ppermute only.
A program may use at most 128 MiB of HBM per device.

v0:
```python
import jax
import jax.numpy as jnp
from jax import lax
from jax.sharding import PartitionSpec as P

FF = 768


denominator = 32768.0


def expert_ffn(inputs, gate_up_w, gate_up_s, down_w, down_s):
    gate_up = jnp.dot(inputs, gate_up_w, preferred_element_type=jnp.float32) * gate_up_s
    gate_part = gate_up[:, :FF]
    up_part = gate_up[:, FF:]
    hidden = (jax.nn.silu(gate_part) * up_part).astype(jnp.bfloat16)
    return (jnp.dot(hidden, down_w, preferred_element_type=jnp.float32) * down_s).astype(
        jnp.bfloat16
    )


def body(tokens, routes, gate_num, gate_up_q, gate_up_scale, down_q, down_scale):
    devices = lax.axis_size("expert")
    tok_rows = tokens.shape[0]
    picks = routes.shape[1]
    width = tokens.shape[1]
    capacity = 2 * tok_rows * picks // devices
    pair_count = tok_rows * picks
    flat_routes = routes.reshape(-1)
    positions = jnp.arange(pair_count, dtype=jnp.int32)
    slot_ids = jnp.arange(capacity, dtype=jnp.int32)
    onehot = (flat_routes[:, None] == jnp.arange(devices, dtype=jnp.int32)[None, :]).astype(
        jnp.int32
    )
    ranked = jnp.cumsum(onehot, axis=0) - 1
    slots_of = jnp.sum(ranked * onehot, axis=1)
    all_tokens, all_routes = (
        lax.all_gather(tokens, "expert", axis=0, tiled=True),
        lax.all_gather(routes, "expert", axis=0, tiled=True),
    )
    my_index = lax.axis_index("expert")
    route_table = all_routes.reshape(devices, pair_count)
    owned = (route_table == my_index).astype(jnp.int32)
    owned_rank = jnp.cumsum(owned, axis=1) - 1
    matches = (owned[:, None, :] == 1) & (owned_rank[:, None, :] == slot_ids[None, :, None])
    source = jnp.sum(jnp.where(matches, positions[None, None, :], 0), axis=2)
    filled = jnp.any(matches, axis=2)
    offsets = (jnp.arange(devices, dtype=jnp.int32) * tok_rows)[:, None]
    global_ids = offsets + source // picks
    row_block = jnp.where(filled[:, :, None], all_tokens[global_ids], jnp.zeros((), jnp.bfloat16))
    first, second, third = row_block.shape
    outputs = expert_ffn(
        row_block.reshape(first * second, third),
        gate_up_q[0],
        gate_up_scale[0],
        down_q[0],
        down_scale[0],
    )
    returned = lax.all_to_all(
        outputs.reshape(first, second, third), "expert", split_axis=0, concat_axis=0, tiled=True
    )
    chosen = returned.reshape(devices * capacity, width)[flat_routes * capacity + slots_of]
    chosen = chosen.reshape(tok_rows, picks, width)
    weights = gate_num.astype(jnp.float32) / denominator
    mixed = jnp.sum(chosen.astype(jnp.float32) * weights[:, :, None], axis=1)
    return mixed.astype(jnp.bfloat16)


def solution(mesh):
    in_specs = (
        P(("groups", "expert"), None),
        P(("groups", "expert"), None),
        P(("groups", "expert"), None),
        P("expert", None, None),
        P("expert", None),
        P("expert", None, None),
        P("expert", None),
    )
    out_specs = P(("groups", "expert"), None)
    return jax.shard_map(body, mesh=mesh, in_specs=in_specs, out_specs=out_specs, check_vma=False)
```

profile of v0, /device:TPU:13, one launch (start us, length us, event | category | flops | bytes accessed | tf_op | source)
XLA Modules:
  0.0 355.4 jit_solution(16963236903007873162)
XLA Ops:
  6.5 0.7 all-gather.3.cloned.1.call-update
  7.3 16.0 %all-gather = s32[16,64,8]{1,2,0:T(8,128)S(1)} all-gather(s32[1,64,8]{1,2,0:T(8,128)} %bitcast.65), channel_id=1, replica_groups=mesh['groups'=2,'expert'=16] {'expert'}, dimensions={0}, use_global_device_ids=true | all-gather | bytes 34816 | tf_op jit(solution)/shard_map/all_gather | solution.py:39
  23.3 0.2 copy.31
  23.5 0.1 copy.32
  23.6 1.1 reduce-window.14
  24.7 0.2 slice_reduce_fusion.1
  25.0 0.2 copy.29
  25.1 0.1 copy.30
  25.3 0.1 copy_bitcast_fusion
  25.3 0.5 select_reduce_fusion
  25.9 0.1 compare_select_fusion
  26.0 0.1 reshape.227
  26.0 0.7 reduce.1
  26.8 0.4 fusion.9
  27.2 57.4 %all-gather.3.cloned.1.call-done = bf16[1024,4096]{1,0:T(8,128)(2,1)} async-done(((bf16[64,4096]{1,0:T(8,128)(2,1)}), bf16[1024,4096]{1,0:T(8,128)(2,1)}) %all-gather.3.cloned.1.call-update) | async-done | bytes 8388624 | tf_op jit(solution)/shard_map/all_gather | solution.py:38
  84.6 19.5 %gather_fusion = bf16[1024,4096]{1,0:T(8,128)(2,1)} fusion(bf16[1024,4096]{1,0:T(8,128)(2,1)} %all-gather.3.cloned.1.call-done, s32[1024]{0:T(1024)S(1)} %broadcast_clamp_fusion), kind=kCustom, calls=%fused_computation | custom fusion | bytes 16781312 | tf_op jit(solution)/shard_map/gather | solution.py:50
  104.1 7.2 %broadcast_select_fusion = bf16[16,64,4096]{2,1,0:T(8,128)(2,1)} fusion(bf16[16,64,4096]{2,1,0:T(8,128)(2,1)} %bitcast.60, pred[16,64]{1,0:T(8,128)(4,1)S(1)} %fusion.9), kind=kLoop, calls=%fused_computation.7 | loop fusion | flops 4194304 | bytes 16778240 | tf_op jit(solution)/shard_map/jit(_where)/select_n | solution.py:50
  111.3 17.1 %fusion.4 = f32[1024,1536]{1,0:T(8,128)S(1)} fusion(bf16[1024,4096]{1,0:T(8,128)(2,1)} %bitcast.62, bf16[1,4096,1536]{2,1,0:T(8,128)(2,1)} %param.10, f32[1536]{0:T(1024)S(1)} %reduce.1), kind=kOutput, calls=%fused_computation.9 | convolution fusion | flops 12886474752 | bytes 27269120 | tf_op jit(solution)/shard_map/dot_general | solution.py:13
  128.4 11.7 %multiply_convert_fusion = bf16[1024,4096]{1,0:T(8,128)(2,1)} fusion(f32[4096]{0:T(1024)S(1)} %bitcast.68, bf16[1,768,4096]{2,1,0:T(8,128)(2,1)} %param.12, f32[1024,1536]{1,0:T(8,128)S(1)} %fusion.4), kind=kOutput, calls=%fused_computation.2 | convolution fusion | flops 6455558144 | bytes 20987904 | tf_op jit(solution)/shard_map/dot_general | solution.py:17
  140.2 6.6 %all-to-all-start = ((bf16[16,64,4096]{2,1,0:T(8,128)(2,1)}), bf16[16,64,4096]{2,1,0:T(8,128)(2,1)}, u32[]{:S(2)}, u32[]{:S(2)}) async-start(bf16[16,64,4096]{2,1,0:T(8,128)(2,1)} %bitcast.61), calls=%async_computation | async-start | bytes 16777216 | tf_op jit(solution)/shard_map/all_to_all | solution.py:59
  146.8 0.1 copy.35
  146.8 0.1 eq.77
  146.9 0.1 eq.73
  147.0 1.2 reduce-window.16
  148.2 0.2 slice_reduce_fusion
  148.4 0.1 copy.34
  148.5 0.1 mul.72
  148.7 0.1 copy.38
  148.7 0.1 fusion.13
  148.9 180.3 %all-to-all-done = bf16[16,64,4096]{2,1,0:T(8,128)(2,1)} async-done(((bf16[16,64,4096]{2,1,0:T(8,128)(2,1)}), bf16[16,64,4096]{2,1,0:T(8,128)(2,1)}, u32[]{:S(2)}, u32[]{:S(2)}) %all-to-all-start) | async-done | bytes 8388640 | tf_op jit(solution)/shard_map/all_to_all | solution.py:59
  329.1 13.0 %gather_fusion.1 = bf16[512,4096]{1,0:T(8,128)(2,1)} fusion(bf16[1024,4096]{1,0:T(8,128)(2,1)} %bitcast.10, s32[1024]{0:T(1024)S(1)} %pad_clamp_fusion), kind=kCustom, calls=%fused_computation.1 | custom fusion | bytes 8390656 | tf_op jit(solution)/shard_map/gather | solution.py:62
  342.1 6.5 %fusion.2 = bf16[64,4096]{1,0:T(8,128)(2,1)} fusion(bf16[512,4096]{1,0:T(8,128)(2,1)} %gather_fusion.1, f32[64,8]{1,0:T(8,128)S(1)} %copy.38), kind=kLoop, calls=%fused_computation.6 | loop fusion | flops 6029312 | bytes 4720640 | tf_op jit(solution)/shard_map/reduce_sum | solution.py:65
  (19 shorter events, 0.1 us)
Async XLA Ops:
  6.5 78.0 %all-gather.3.cloned.1.call-start = ((), (), s32[]{:S(2)}) async-start(), calls=%async_computation.1 | async-start | bytes 8912896 | tf_op jit(solution)/shard_map/all_gather | solution.py:38
  111.3 17.1 %copy-start.2 = (f32[1,4096]{1,0:T(1,128)S(1)}, f32[1,4096]{1,0:T(1,128)}, u32[]{:S(2)}) copy-start(f32[1,4096]{1,0:T(1,128)} %param.13) | copy-start | bytes 49156
  140.2 6.6 %copy-start = (s32[64,8]{0,1:T(8,128)S(1)}, s32[64,8]{0,1:T(8,128)}, u32[]{:S(2)}) copy-start(s32[64,8]{0,1:T(8,128)} %param.8) | copy-start | bytes 6148
  140.2 8.5 %copy-start.1 = (s32[64,8]{0,1:T(8,128)S(1)}, s32[64,8]{0,1:T(8,128)}, u32[]{:S(2)}) copy-start(s32[64,8]{0,1:T(8,128)} %param.9) | copy-start | bytes 6148
  140.2 188.9 %all-to-all-start = ((bf16[16,64,4096]{2,1,0:T(8,128)(2,1)}), bf16[16,64,4096]{2,1,0:T(8,128)(2,1)}, u32[]{:S(2)}, u32[]{:S(2)}) async-start(bf16[16,64,4096]{2,1,0:T(8,128)(2,1)} %bitcast.61), calls=%async_computation | async-start | bytes 16777216 | tf_op jit(solution)/shard_map/all_to_all | solution.py:59
Sparse Core Ops, SparseCore 0:
  9.5 74.9 all-gather.2
where the time goes:
time: 356 us; the launch traced here: 355 us
  waiting for transfers between devices  238 us (67%)
  local copies, waits for them, and re-layouts  34.2 us (10%)
  matrix products  28.8 us (8%)
  other arithmetic  18 us (5%)
  blocking collectives  16 us (4%)
  between operations  13.5 us (4%)
  starting transfers between devices  6.58 us (2%)
    all_to_all x1, waiting for transfers between devices, body(): lax.all_to_all(outputs.reshape(first, second, third), 'expert', split_axi...  180 us
    all_gather x1, waiting for transfers between devices, body(): lax.all_gather(tokens, 'expert', axis=0, tiled=True)  57.4 us
    gather x1, local copies, waits for them, and re-layouts, body(): all_tokens[global_ids]  19.5 us
    dot_general x1, matrix products, expert_ffn(): jnp.dot(inputs, gate_up_w, preferred_element_type=jnp.float32) * gate_up_s  17.1 us
    all_gather x1, blocking collectives, body(): lax.all_gather(routes, 'expert', axis=0, tiled=True)  16 us
    gather x1, local copies, waits for them, and re-layouts, body(): returned.reshape(devices * capacity, width)  13 us
    dot_general x1, matrix products, expert_ffn(): jnp.dot(hidden, down_w, preferred_element_type=jnp.float32) * down_s  11.7 us
    select_n x1, other arithmetic, body(): jnp.where(filled[:, :, None], all_tokens[global_ids], jnp.zeros((), jnp.b...  7.22 us
  transfers between devices with their start and end apart: 2, of which 2 were waited for; matrix products, arithmetic and copies ran while one was open for 2% of the time, Pallas kernels for 0%

commit v1 on v0

v1 whole, which is shorter than its diff:
```python
import jax
import jax.numpy as jnp
from jax import lax
from jax.sharding import PartitionSpec as P

DENOMINATOR = 32768.0
LANES = 128


def pack(tokens, routes, gate_num, experts):
    ids = jnp.arange(experts, dtype=jnp.int32)
    named = routes[:, :, None] == ids[None, None, :]
    dense = jnp.sum(jnp.where(named, gate_num[:, :, None], 0), axis=1)
    high = (dense >> 8).astype(jnp.bfloat16)
    low = (dense & 255).astype(jnp.bfloat16)
    spare = -(2 * experts) % LANES
    blank = jnp.zeros((tokens.shape[0], spare), jnp.bfloat16)
    return jnp.concatenate([tokens, high, low, blank], axis=1)


def gate_of(packed, width, experts, expert):
    mine = (jnp.arange(experts, dtype=jnp.int32) == expert)[None, :]
    high = packed[:, width : width + experts].astype(jnp.float32)
    low = packed[:, width + experts : width + 2 * experts].astype(jnp.float32)
    number = jnp.sum(jnp.where(mine, high * 256.0 + low, 0.0), axis=1, keepdims=True)
    return number / DENOMINATOR


def expert_part(packed, width, experts, expert, gate_up_w, gate_up_s, down_w, down_s):
    hidden_units = down_w.shape[0]
    gate_up = jnp.dot(packed[:, :width], gate_up_w, preferred_element_type=jnp.float32) * gate_up_s
    hidden = jax.nn.silu(gate_up[:, :hidden_units]) * gate_up[:, hidden_units:]
    out = jnp.dot(hidden.astype(jnp.bfloat16), down_w, preferred_element_type=jnp.float32) * down_s
    return (out * gate_of(packed, width, experts, expert)).astype(jnp.bfloat16)


def body(tokens, routes, gate_num, gate_up_q, gate_up_scale, down_q, down_scale):
    devices = lax.axis_size("expert")
    expert = lax.axis_index("expert")
    chips = devices // 2
    rows, width = tokens.shape
    same_core = [[2 * chip + core for chip in range(chips)] for core in range(2)]
    swap = [(i, i ^ 1) for i in range(devices)]
    weights = (gate_up_q[0], gate_up_scale[0], down_q[0], down_scale[0])

    packed = pack(tokens, routes, gate_num, devices)
    ours = lax.all_gather(packed, "expert", axis=0, tiled=True, axis_index_groups=same_core)
    theirs = lax.ppermute(ours, "expert", swap)
    for_them = expert_part(theirs, width, devices, expert, *weights)
    from_them = lax.ppermute(for_them, "expert", swap)
    for_us = expert_part(ours, width, devices, expert, *weights)
    total = (for_us.astype(jnp.float32) + from_them.astype(jnp.float32)).astype(jnp.bfloat16)
    return lax.psum_scatter(
        total.reshape(chips, rows, width),
        "expert",
        scatter_dimension=0,
        axis_index_groups=same_core,
        tiled=False,
    )


def solution(mesh):
    in_specs = (
        P(("groups", "expert"), None),
        P(("groups", "expert"), None),
        P(("groups", "expert"), None),
        P("expert", None, None),
        P("expert", None),
        P("expert", None, None),
        P("expert", None),
    )
    out_specs = P(("groups", "expert"), None)
    return jax.shard_map(body, mesh=mesh, in_specs=in_specs, out_specs=out_specs, check_vma=False)
```

time: 356 us -> 223 us (0.63)
  the two profiles are of different devices: /device:TPU:13 before, /device:TPU:0 now
where the time goes in v1:
time: 223 us; the launch traced here: 222 us
  waiting for transfers between devices  172 us (77%)
  matrix products  32.1 us (14%)
  between operations  13.5 us (6%)
  other arithmetic  2.86 us (1%)
    reduce_scatter x1, waiting for transfers between devices, body(): lax.psum_scatter(total.reshape(chips, rows, width), 'expert', scatter_dim...  86.8 us
    all_gather x1, waiting for transfers between devices, body(): lax.all_gather(packed, 'expert', axis=0, tiled=True, axis_index_groups=sa...  77.9 us
    dot_general x2, matrix products, expert_part(): jnp.dot(packed[:, :width], gate_up_w, preferred_element_type=jnp.float32)  19.9 us
    dot_general x2, matrix products, expert_part(): jnp.dot(hidden.astype(jnp.bfloat16), down_w, preferred_element_type=jnp.f...  12.2 us
    ppermute x1, waiting for transfers between devices, body(): theirs = lax.ppermute(ours, 'expert', swap)  6.96 us
  transfers between devices with their start and end apart: 4, of which 3 were waited for; matrix products, arithmetic and copies ran while one was open for 5% of the time, Pallas kernels for 0%

profile of v1, /device:TPU:0, one launch (start us, length us, event | category | flops | bytes accessed | tf_op | source)
XLA Modules:
  0.0 222.4 jit_solution(13824546860069942044)
XLA Ops:
  6.5 0.0 all-gather.2.cloned.1.call-start
  6.5 0.7 select_reduce_fusion.2
  7.3 0.1 copy.11
  7.4 0.1 copy.10
  7.5 1.8 concatenate.3
  9.3 0.0 all-gather.2.cloned.1.call-update
  9.4 0.0 reduce-scatter.2.cloned.1.call-start
  9.4 77.9 %all-gather.2.cloned.1.call-done = bf16[512,4224]{1,0:T(8,128)(2,1)} async-done(((bf16[64,4224]{1,0:T(8,128)(2,1)}), bf16[512,4224]{1,0:T(8,128)(2,1)}) %all-gather.2.cloned.1.call-update) | async-done | bytes 4325392 | tf_op jit(solution)/shard_map/all_gather | solution.py:47
  87.3 0.0 collective-permute-start
  87.3 0.7 reduce
  88.0 7.0 %collective-permute-done = bf16[512,4224]{1,0:T(8,128)(2,1)} collective-permute-done((bf16[512,4224]{1,0:T(8,128)(2,1)}, bf16[512,4224]{1,0:T(8,128)(2,1)}, u32[]{:S(2)}, u32[]{:S(2)}) %collective-permute-start) | collective-permute-done | bytes 4325408 | tf_op jit(solution)/shard_map/ppermute | solution.py:48
  95.0 1.4 select_reduce_fusion.1
  96.4 0.0 copy-start.1
  96.4 10.5 %fusion.15 = f32[512,1536]{1,0:T(8,128)S(1)} fusion(bf16[1,4096,1536]{2,1,0:T(8,128)(2,1)} %param.10, bf16[512,4224]{1,0:T(8,128)(2,1)} %collective-permute-done, f32[1536]{0:T(1024)S(1)} %reduce), kind=kOutput, calls=%fused_computation.12 | convolution fusion | flops 6443237376 | bytes 19929088 | tf_op jit(solution)/shard_map/dot_general | solution.py:31
  106.9 0.0 copy-done.1
  107.0 0.0 copy-start
  107.0 0.0 slice-start
  107.0 6.7 %multiply_convert_fusion = bf16[512,4096]{1,0:T(8,128)(2,1)S(1)} fusion(bf16[1,768,4096]{2,1,0:T(8,128)(2,1)} %param.12, f32[512]{0:T(512)S(1)} %broadcast_multiply_fusion, f32[4096]{0:T(1024)S(1)} %bitcast.22, f32[512,1536]{1,0:T(8,128)S(1)} %fusion.15), kind=kOutput, calls=%fused_computation.5 | convolution fusion | flops 3229876224 | bytes 13649920 | tf_op jit(solution)/shard_map/dot_general | solution.py:33
  113.7 0.0 slice-start.1
  113.7 0.2 collective-permute-start.1
  113.9 0.0 copy-done
  113.9 9.4 %fusion.10 = f32[512,1536]{1,0:T(8,128)S(1)} fusion(bf16[1,4096,1536]{2,1,0:T(8,128)(2,1)} %param.10, bf16[512,4224]{1,0:T(8,128)(2,1)S(1)} %copy-done, f32[1536]{0:T(1024)S(1)} %reduce), kind=kOutput, calls=%fused_computation.11 | convolution fusion | flops 6443237376 | bytes 19931136 | tf_op jit(solution)/shard_map/dot_general | solution.py:31
  123.3 0.0 collective-permute-done.1
  123.3 0.0 slice-done
  123.3 0.0 slice-done.1
  123.4 5.4 %add_convert_fusion = bf16[512,4096]{1,0:T(8,128)(2,1)} fusion(bf16[512,4096]{1,0:T(8,128)(2,1)S(1)} %collective-permute-done.1, bf16[1,768,4096]{2,1,0:T(8,128)(2,1)S(1)} %bitcast.21, f32[512]{0:T(512)S(1)} %broadcast_multiply_fusion.1, f32[4096]{0:T(1024)S(1)} %bitcast.23, f32[512,1536]{1,0:T(8,128)S(1)} %fusion.10), kind=kOutput, calls=%fused_computation.4 | convolution fusion | flops 3238264832 | bytes 17844224 | tf_op jit(solution)/shard_map/dot_general | solution.py:33
  128.8 0.0 reduce-scatter.2.cloned.1.call-update
  128.8 86.8 %reduce-scatter.2.cloned.1.call-done = bf16[1,64,4096]{2,1,0:T(8,128)(2,1)} async-done(((bf16[8,64,4096]{2,1,0:T(8,128)(2,1)}), bf16[1,64,4096]{2,1,0:T(8,128)(2,1)}) %reduce-scatter.2.cloned.1.call-update) | async-done | bytes 524304 | tf_op jit(solution)/shard_map/reduce_scatter | solution.py:53
  (6 shorter events, 0.0 us)
Async XLA Ops:
  6.5 80.8 %all-gather.2.cloned.1.call-start = ((), (), s32[]{:S(2)}) async-start(), calls=%async_computation.1 | async-start | bytes 4866048 | tf_op jit(solution)/shard_map/all_gather | solution.py:47
  9.4 206.2 %reduce-scatter.2.cloned.1.call-start = ((), (), s32[]{:S(2)}) async-start(), calls=%async_computation.2 | async-start | bytes 4718592 | tf_op jit(solution)/shard_map/reduce_scatter | solution.py:53
  87.3 7.7 %collective-permute-start = (bf16[512,4224]{1,0:T(8,128)(2,1)}, bf16[512,4224]{1,0:T(8,128)(2,1)}, u32[]{:S(2)}, u32[]{:S(2)}) collective-permute-start(bf16[512,4224]{1,0:T(8,128)(2,1)} %all-gather.2.cloned.1.call-done), channel_id=1, source_target_pairs={{0,1},{1,0},{2,3},{3,2},{4,5},{5,4},{6,7},{7,6},{8,9},{9,8},{10,11... | collective-permute-start | bytes 12976136 | tf_op jit(solution)/shard_map/ppermute | solution.py:48
  96.4 10.5 %copy-start.1 = (f32[1,4096]{1,0:T(1,128)S(1)}, f32[1,4096]{1,0:T(1,128)}, u32[]{:S(2)}) copy-start(f32[1,4096]{1,0:T(1,128)} %param.13) | copy-start | bytes 49156
  107.0 7.0 %copy-start = (bf16[512,4224]{1,0:T(8,128)(2,1)S(1)}, bf16[512,4224]{1,0:T(8,128)(2,1)}, u32[]{:S(2)}) copy-start(bf16[512,4224]{1,0:T(8,128)(2,1)} %all-gather.2.cloned.1.call-done) | copy-start | bytes 12976132
  107.0 16.4 %slice-start = ((s8[6291456]{0:T(1024)(128)(4,1)}), s8[4194304]{0:T(1024)(128)(4,1)S(1)}, s32[]{:S(2)}) async-start(s8[6291456]{0:T(1024)(128)(4,1)} %bitcast.20), calls=%async_computation.3 | async-start | bytes 8388608
  113.7 9.6 %slice-start.1 = ((s8[6291456]{0:T(1024)(128)(4,1)}), s8[2097152]{0:T(1024)(128)(4,1)S(1)}, s32[]{:S(2)}) async-start(s8[6291456]{0:T(1024)(128)(4,1)} %bitcast.20), calls=%async_computation.4 | async-start | bytes 4194304
  113.7 9.6 %collective-permute-start.1 = (bf16[512,4096]{1,0:T(8,128)(2,1)S(1)}, bf16[512,4096]{1,0:T(8,128)(2,1)S(1)}, u32[]{:S(2)}, u32[]{:S(2)}) collective-permute-start(bf16[512,4096]{1,0:T(8,128)(2,1)S(1)} %multiply_convert_fusion), channel_id=1, source_target_pairs={{0,1},{1,0},{2,3},{3,2},{4,5},{5,4},{6,7},{7,6},{8,9},{9,8},{10,11... | collective-permute-start | bytes 12582920 | tf_op jit(solution)/shard_map/ppermute | solution.py:50
Sparse Core Ops, SparseCore 0:
  9.5 77.6 all-gather.1
  128.9 86.5 reduce-scatter.1

commit v2 on v1

v2 whole, which is shorter than its diff:
```python
import functools

import jax
import jax.numpy as jnp
from jax import lax
from jax.experimental import pallas as pl
from jax.experimental.pallas import tpu as pltpu
from jax.sharding import PartitionSpec as P

DENOMINATOR = 32768.0
LANES = 128
DEPTH_STEPS = 8
WIDTH_STEPS = 8


def ring_of(chips):
    if chips == 8:
        return [0, 2, 4, 6, 7, 5, 3, 1]
    return list(range(chips))


def pack(tokens, routes, gate_num, experts):
    ids = jnp.arange(experts, dtype=jnp.int32)
    named = routes[:, :, None] == ids[None, None, :]
    dense = jnp.sum(jnp.where(named, gate_num[:, :, None], 0), axis=1)
    high = (dense >> 8).astype(jnp.bfloat16)
    low = (dense & 255).astype(jnp.bfloat16)
    spare = -(2 * experts) % LANES
    blank = jnp.zeros((tokens.shape[0], spare), jnp.bfloat16)
    return jnp.concatenate([tokens, high, low, blank], axis=1)


def expert_kernel(count, *refs):
    xs, gates = refs[:count], refs[count : 2 * count]
    pick, gate_up, gate_up_s, down, down_s = refs[2 * count : 2 * count + 5]
    outs = refs[2 * count + 5 : -3]
    total, hidden, weight = refs[-3:]
    step = pl.program_id(0)
    units = down.shape[0]

    @pl.when(step < DEPTH_STEPS)
    def _():
        x = jnp.concatenate([ref[...] for ref in xs], axis=0)
        part = jnp.dot(x, gate_up[...], preferred_element_type=jnp.float32)

        @pl.when(step == 0)
        def _():
            total[...] = part

        @pl.when(step > 0)
        def _():
            total[...] += part

    @pl.when(step == DEPTH_STEPS)
    def _():
        scaled = total[...] * gate_up_s[...]
        hidden[...] = (jax.nn.silu(scaled[:, :units]) * scaled[:, units:]).astype(jnp.bfloat16)
        digits = jnp.concatenate([ref[...] for ref in gates], axis=0).astype(jnp.float32)
        number = jnp.sum(digits * pick[...], axis=1, keepdims=True)
        weight[...] = jnp.broadcast_to(number / DENOMINATOR, weight.shape)

    @pl.when(step >= DEPTH_STEPS)
    def _():
        out = jnp.dot(hidden[...], down[...], preferred_element_type=jnp.float32)
        out = (out * down_s[...] * weight[:, :1]).astype(jnp.bfloat16)
        at = 0
        for ref in outs:
            ref[...] = out[at : at + ref.shape[0]]
            at += ref.shape[0]


def expert_part(blocks, split, pick, gate_up_w, gate_up_s, down_w, down_s):
    width, units2 = gate_up_w.shape
    units = down_w.shape[0]
    sizes = [block.shape[0] for block in blocks]
    rows = sum(sizes)
    deep, wide = width // DEPTH_STEPS, width // WIDTH_STEPS
    phase1 = lambda i: jnp.minimum(i, DEPTH_STEPS - 1)
    phase2 = lambda i: jnp.maximum(i - DEPTH_STEPS, 0)
    x_specs = [pl.BlockSpec((size, deep), lambda i: (0, phase1(i))) for size in sizes]
    gate_specs = [pl.BlockSpec((size, LANES), lambda i: (0, width // LANES)) for size in sizes]
    weight_specs = [
        pl.BlockSpec((1, LANES), lambda i: (0, 0)),
        pl.BlockSpec((deep, units2), lambda i: (phase1(i), 0)),
        pl.BlockSpec((1, units2), lambda i: (0, 0)),
        pl.BlockSpec((units, wide), lambda i: (0, phase2(i))),
        pl.BlockSpec((1, wide), lambda i: (0, phase2(i))),
    ]
    out_rows = [sum(sizes[:split]), sum(sizes[split:])]
    flops = 2 * rows * width * (units2 + units)
    moved = 2 * width * (units2 + units) + 4 * rows * width
    return pl.pallas_call(
        functools.partial(expert_kernel, len(sizes)),
        grid=(DEPTH_STEPS + WIDTH_STEPS,),
        in_specs=x_specs + gate_specs + weight_specs,
        out_specs=[pl.BlockSpec((size, wide), lambda i: (0, phase2(i))) for size in out_rows],
        out_shape=[jax.ShapeDtypeStruct((size, width), jnp.bfloat16) for size in out_rows],
        scratch_shapes=[
            pltpu.VMEM((rows, units2), jnp.float32),
            pltpu.VMEM((rows, units), jnp.bfloat16),
            pltpu.VMEM((rows, LANES), jnp.float32),
        ],
        compiler_params=pltpu.CompilerParams(vmem_limit_bytes=24 << 20),
        cost_estimate=pl.CostEstimate(flops=flops, bytes_accessed=moved, transcendentals=rows * units),
        name="expert",
    )(*blocks, *blocks, pick, gate_up_w, gate_up_s, down_w, down_s)


def add(*terms):
    total = terms[0].astype(jnp.float32)
    for term in terms[1:]:
        total = total + term.astype(jnp.float32)
    return total.astype(jnp.bfloat16)


def body(tokens, routes, gate_num, gate_up_q, gate_up_scale, down_q, down_scale):
    devices = lax.axis_size("expert")
    expert = lax.axis_index("expert")
    chips = devices // 2
    reach = chips // 2
    rows, width = tokens.shape
    half = rows // 2
    ring = ring_of(chips)

    def hop(way):
        pairs = []
        for place in range(chips):
            for core in range(2):
                pairs.append((2 * ring[place] + core, 2 * ring[(place + way) % chips] + core))
        return pairs

    upward, downward = hop(1), hop(-1)
    swap = [(i, i ^ 1) for i in range(devices)]
    send = functools.partial(lax.ppermute, axis_name="expert")

    lane = jnp.arange(LANES, dtype=jnp.int32)
    pick = jnp.where(lane == expert, 256.0, jnp.where(lane == devices + expert, 1.0, 0.0))
    pick = pick.astype(jnp.float32)[None, :]
    weights = (pick, gate_up_q[0], gate_up_scale, down_q[0], down_scale)

    packed = pack(tokens, routes, gate_num, devices)
    mine, theirs = {}, {}

    def run(distance, blocks):
        others = [send(block, perm=swap) for block in blocks]
        kept, given = expert_part(blocks + others, len(blocks), *weights)
        mine[distance] = kept
        theirs[distance] = send(given, perm=swap)

    from_below, from_above = packed, packed
    run(0, [packed])
    for distance in range(1, reach):
        from_below = send(from_below, perm=upward)
        from_above = send(from_above, perm=downward)
        run(distance, [from_below, from_above])
    last_below = send(from_below[:half], perm=upward)
    last_above = send(from_above[half:], perm=downward)
    run(reach, [last_below, last_above])

    to_above = send(add(mine[reach][:half], theirs[reach][:half]), perm=upward)
    to_below = send(add(mine[reach][half:], theirs[reach][half:]), perm=downward)
    for distance in range(reach - 1, 0, -1):
        if distance == reach - 1:
            to_above = jnp.pad(to_above, ((0, half), (0, 0)))
            to_below = jnp.pad(to_below, ((half, 0), (0, 0)))
        above = add(mine[distance][rows:], theirs[distance][rows:], to_above)
        below = add(mine[distance][:rows], theirs[distance][:rows], to_below)
        to_above = send(above, perm=upward)
        to_below = send(below, perm=downward)
    return add(mine[0], theirs[0], to_above, to_below)


def solution(mesh):
    in_specs = (
        P(("groups", "expert"), None),
        P(("groups", "expert"), None),
        P(("groups", "expert"), None),
        P("expert", None, None),
        P("expert", None),
        P("expert", None, None),
        P("expert", None),
    )
    out_specs = P(("groups", "expert"), None)
    return jax.shard_map(body, mesh=mesh, in_specs=in_specs, out_specs=out_specs, check_vma=False)
```

time: 223 us -> 151 us (0.68)
  waiting for transfers between devices: 172 us -> 57.2 us
  Pallas kernels: 0 us -> 56.2 us
  matrix products: 32.1 us -> 0 us
  starting transfers between devices: 0.24 us -> 20.4 us
  between operations: 13.5 us -> 0.18 us
  local copies, waits for them, and re-layouts: 2.08 us -> 12.8 us
    reduce_scatter x1 -> x0, waiting for transfers between devices: 86.8 us -> none  [body(): lax.psum_scatter(total.reshape(chips, rows, width), 'expert', scatter_dim...]
    all_gather x1 -> x0, waiting for transfers between devices: 77.9 us -> none  [body(): lax.all_gather(packed, 'expert', axis=0, tiled=True, axis_index_groups=sa...]
    pallas_call x0 -> x5, Pallas kernels: none -> 56.2 us  [expert_part(): pl.pallas_call(functools.partial(expert_kernel, len(sizes)), grid=(DEPTH_...]
    ppermute x2 -> x30, waiting for transfers between devices: 6.96 us -> 57.2 us  [the longest x3 34.1 us: body(): from_below = send(from_below, perm=upward)]
    dot_general x4 -> x0, matrix products: 32.1 us -> none  [the longest x2 19.9 us: expert_part(): jnp.dot(packed[:, :width], gate_up_w, preferred_element_type=jnp.float32)]
    ppermute x2 -> x30, starting transfers between devices: 0.2 us -> 20.4 us  [the longest x3 6.35 us: body(): from_below = send(from_below, perm=upward)]
    unnamed x8 -> x20, local copies, waits for them, and re-layouts: 0.03 us -> 11.6 us
    convert_element_type x0 -> x5, other arithmetic: none -> 2.46 us  [add(): return total.astype(jnp.bfloat16)]
  transfers between devices with their start and end apart: 4 -> 30, of which waited for: 3 -> 11; matrix products, arithmetic and copies ran while one was open for 5% -> 1% of each run, Pallas kernels for 0% -> 37%
where the time goes in v2:
time: 151 us; the launch traced here: 150 us
  waiting for transfers between devices  57.2 us (38%)
  Pallas kernels  56.2 us (37%)
  starting transfers between devices  20.4 us (14%)
  local copies, waits for them, and re-layouts  12.8 us (8%)
  other arithmetic  3.21 us (2%)
    pallas_call x5, Pallas kernels, expert_part(): pl.pallas_call(functools.partial(expert_kernel, len(sizes)), grid=(DEPTH_...  56.2 us
    ppermute x3, waiting for transfers between devices, body(): from_below = send(from_below, perm=upward)  34.1 us
    ppermute x3, waiting for transfers between devices, body(): to_below = send(below, perm=downward)  12.2 us
    unnamed x20, local copies, waits for them, and re-layouts  11.6 us
    ppermute x3, starting transfers between devices, body(): from_below = send(from_below, perm=upward)  6.35 us
    ppermute x3, starting transfers between devices, body(): to_above = send(above, perm=upward)  4.84 us
    ppermute x1, waiting for transfers between devices, body(): last_below = send(from_below[:half], perm=upward)  4.35 us
    ppermute x3, waiting for transfers between devices, body(): to_above = send(above, perm=upward)  3.32 us
  transfers between devices with their start and end apart: 30, of which 11 were waited for; matrix products, arithmetic and copies ran while one was open for 1% of the time, Pallas kernels for 37%

profile of v2, /device:TPU:0, one launch (start us, length us, event | category | flops | bytes accessed | tf_op | source)
XLA Modules:
  0.0 150.0 jit_solution(3481383300623255907)
XLA Ops:
  0.0 0.7 select_reduce_fusion
  0.8 1.1 concatenate.3.refs_0_.refs_2_
  2.0 3.1 %collective-permute-start.2 = (bf16[64,4224]{1,0:T(8,128)(2,1)S(1)}, bf16[64,4224]{1,0:T(8,128)(2,1)S(1)}, u32[]{:S(2)}, u32[]{:S(2)}) collective-permute-start(bf16[64,4224]{1,0:T(8,128)(2,1)S(1)} %concatenate.3.refs_0_.refs_2_), channel_id=1, source_target_pairs={{0,4},{1,5},{4,8},{5,9},{8,12},{9,13},{12,14},{13,15},{14,10},{15,... | collective-permute-start | bytes 1622024 | tf_op jit(solution)/shard_map/ppermute | solution.py:153
  5.1 12.2 %collective-permute-done.2.refs_0_.refs_4_ = bf16[64,4224]{1,0:T(8,128)(2,1)S(1)} collective-permute-done((bf16[64,4224]{1,0:T(8,128)(2,1)S(1)}, bf16[64,4224]{1,0:T(8,128)(2,1)S(1)}, u32[]{:S(2)}, u32[]{:S(2)}) %collective-permute-start.2) | collective-permute-done | bytes 540704 | tf_op jit(solution)/shard_map/ppermute | solution.py:153
  17.3 1.8 %collective-permute-start.7 = (bf16[64,4224]{1,0:T(8,128)(2,1)S(1)}, bf16[64,4224]{1,0:T(8,128)(2,1)S(1)}, u32[]{:S(2)}, u32[]{:S(2)}) collective-permute-start(bf16[64,4224]{1,0:T(8,128)(2,1)S(1)} %collective-permute-done.2.refs_0_.refs_4_), channel_id=1, source_target_pairs={{0,4},{1,5},{4,8},{5,9},{8,12},{9,13},{12,14},{13,15},{14,10},{15,... | collective-permute-start | bytes 1622024 | tf_op jit(solution)/shard_map/ppermute | solution.py:153
  19.3 11.4 %collective-permute-done.7.refs_0_.refs_4_ = bf16[64,4224]{1,0:T(8,128)(2,1)S(1)} collective-permute-done((bf16[64,4224]{1,0:T(8,128)(2,1)S(1)}, bf16[64,4224]{1,0:T(8,128)(2,1)S(1)}, u32[]{:S(2)}, u32[]{:S(2)}) %collective-permute-start.7) | collective-permute-done | bytes 540704 | tf_op jit(solution)/shard_map/ppermute | solution.py:153
  30.8 1.5 collective-permute-start.12
  32.8 10.5 %collective-permute-done.12.refs_0_.refs_4_ = bf16[64,4224]{1,0:T(8,128)(2,1)S(1)} collective-permute-done((bf16[64,4224]{1,0:T(8,128)(2,1)S(1)}, bf16[64,4224]{1,0:T(8,128)(2,1)S(1)}, u32[]{:S(2)}, u32[]{:S(2)}) %collective-permute-start.12) | collective-permute-done | bytes 540704 | tf_op jit(solution)/shard_map/ppermute | solution.py:153
  43.3 1.4 collective-permute-start.17
  44.7 0.8 collective-permute-start.18
  45.5 4.4 %collective-permute-done.17.refs_0_.refs_4_ = bf16[32,4224]{1,0:T(8,128)(2,1)S(1)} collective-permute-done((bf16[32,4224]{1,0:T(8,128)(2,1)S(1)}, bf16[32,4224]{1,0:T(8,128)(2,1)S(1)}, u32[]{:S(2)}, u32[]{:S(2)}) %collective-permute-start.17) | collective-permute-done | bytes 270368 | tf_op jit(solution)/shard_map/ppermute | solution.py:156
  49.8 1.5 collective-permute-done.18.refs_1_.refs_5_
  51.9 1.7 %collective-permute-done.20.refs_3_.refs_7_ = bf16[32,4224]{1,0:T(8,128)(2,1)} collective-permute-done((bf16[32,4224]{1,0:T(8,128)(2,1)}, bf16[32,4224]{1,0:T(8,128)(2,1)}, u32[]{:S(2)}, u32[]{:S(2)}) %collective-permute-start.20) | collective-permute-done | bytes 270368 | tf_op jit(solution)/shard_map/ppermute | solution.py:145
  53.5 4.6 %copy-done = bf16[1,4096,1536]{2,1,0:T(8,128)(2,1)S(1)} copy-done((bf16[1,4096,1536]{2,1,0:T(8,128)(2,1)S(1)}, bf16[1,4096,1536]{2,1,0:T(8,128)(2,1)}, u32[]{:S(2)}) %copy-start) | copy-done | bytes 12582936
  58.1 2.8 %copy-done.2 = bf16[1,768,4096]{2,1,0:T(8,128)(2,1)S(1)} copy-done((bf16[1,768,4096]{2,1,0:T(8,128)(2,1)S(1)}, bf16[1,768,4096]{2,1,0:T(8,128)(2,1)}, u32[]{:S(2)}) %copy-start.2) | copy-done | bytes 6291480
  60.9 0.7 copy-done.7
  61.6 0.7 copy-done.9
  62.3 11.5 %expert.9 = (bf16[64,4096]{1,0:T(8,128)(2,1)S(1)}, bf16[64,4096]{1,0:T(8,128)(2,1)}) custom-call(bf16[32,4224]{1,0:T(8,128)(2,1)S(1)} %collective-permute-done.17.refs_0_.refs_4_, bf16[32,4224]{1,0:T(8,128)(2,1)} %collective-permute-done.18.refs_1_.refs_5_, bf16[32,4224]{1,0:T(8,128)(2,1)} %collective-permute-done.19.refs_2_.refs_6_, ...), custom_call_target="tpu_custom_call" | custom-call | flops 2415919104 | bytes 20971520 | tf_op jit(solution)/shard_map/expert/pallas_call | solution.py:92
  75.0 2.8 %copy-done.3 = bf16[1,768,4096]{2,1,0:T(8,128)(2,1)S(1)} copy-done((bf16[1,768,4096]{2,1,0:T(8,128)(2,1)S(1)}, bf16[1,768,4096]{2,1,0:T(8,128)(2,1)}, u32[]{:S(2)}) %copy-start.3) | copy-done | bytes 6291480
  77.8 12.6 %expert.8 = (bf16[128,4096]{1,0:T(8,128)(2,1)S(1)}, bf16[128,4096]{1,0:T(8,128)(2,1)S(1)}) custom-call(bf16[64,4224]{1,0:T(8,128)(2,1)S(1)} %collective-permute-done.12.refs_0_.refs_4_, bf16[64,4224]{1,0:T(8,128)(2,1)S(1)} %collective-permute-done.13.refs_1_.refs_5_, bf16[64,4224]{1,0:T(8,128)(2,1)} %collective-permute-done.14.refs_2_.refs_6_, ...), custom_call_target="tpu_custom_call" | custom-call | flops 4831838208 | bytes 23068672 | tf_op jit(solution)/shard_map/expert/pallas_call | solution.py:92
  91.0 1.6 %collective-permute-start.22 = (bf16[32,4096]{1,0:T(8,128)(2,1)S(1)}, bf16[32,4096]{1,0:T(8,128)(2,1)S(1)}, u32[]{:S(2)}, u32[]{:S(2)}) collective-permute-start(bf16[32,4096]{1,0:T(8,128)(2,1)S(1)} %get-tuple-element.31), channel_id=1, source_target_pairs={{0,4},{1,5},{4,8},{5,9},{8,12},{9,13},{12,14},{13,15},{14,10},{15,... | collective-permute-start | bytes 786440 | tf_op jit(solution)/shard_map/ppermute | solution.py:160
  93.1 12.0 %expert.7 = (bf16[128,4096]{1,0:T(8,128)(2,1)S(1)}, bf16[128,4096]{1,0:T(8,128)(2,1)S(1)}) custom-call(bf16[64,4224]{1,0:T(8,128)(2,1)S(1)} %collective-permute-done.7.refs_0_.refs_4_, bf16[64,4224]{1,0:T(8,128)(2,1)S(1)} %copy-done.6, bf16[64,4224]{1,0:T(8,128)(2,1)S(1)} %collective-permute-done.9.refs_2_.refs_6_, ...), custom_call_target="tpu_custom_call" | custom-call | flops 4831838208 | bytes 23068672 | tf_op jit(solution)/shard_map/expert/pallas_call | solution.py:92
  105.6 1.6 %collective-permute-start.23 = (bf16[64,4096]{1,0:T(8,128)(2,1)S(1)}, bf16[64,4096]{1,0:T(8,128)(2,1)S(1)}, u32[]{:S(2)}, u32[]{:S(2)}) collective-permute-start(bf16[64,4096]{1,0:T(8,128)(2,1)S(1)} %get-tuple-element.29), channel_id=1, source_target_pairs={{0,4},{1,5},{4,8},{5,9},{8,12},{9,13},{12,14},{13,15},{14,10},{15,... | collective-permute-start | bytes 1572872 | tf_op jit(solution)/shard_map/ppermute | solution.py:168
  107.7 12.1 %expert.6 = (bf16[128,4096]{1,0:T(8,128)(2,1)S(1)}, bf16[128,4096]{1,0:T(8,128)(2,1)S(1)}) custom-call(bf16[64,4224]{1,0:T(8,128)(2,1)S(1)} %collective-permute-done.2.refs_0_.refs_4_, bf16[64,4224]{1,0:T(8,128)(2,1)S(1)} %collective-permute-done.3.refs_1_.refs_5_, bf16[64,4224]{1,0:T(8,128)(2,1)S(1)} %collective-permute-done.4.refs_2_.refs_6_, ...), custom_call_target="tpu_custom_call" | custom-call | flops 4831838208 | bytes 23068672 | tf_op jit(solution)/shard_map/expert/pallas_call | solution.py:92
  120.3 0.9 collective-permute-done.27
  121.7 1.6 %collective-permute-start.24 = (bf16[64,4096]{1,0:T(8,128)(2,1)S(1)}, bf16[64,4096]{1,0:T(8,128)(2,1)S(1)}, u32[]{:S(2)}, u32[]{:S(2)}) collective-permute-start(bf16[64,4096]{1,0:T(8,128)(2,1)S(1)} %get-tuple-element.27), channel_id=1, source_target_pairs={{0,4},{1,5},{4,8},{5,9},{8,12},{9,13},{12,14},{13,15},{14,10},{15,... | collective-permute-start | bytes 1572872 | tf_op jit(solution)/shard_map/ppermute | solution.py:168
  123.8 7.9 %expert.5 = (bf16[64,4096]{1,0:T(8,128)(2,1)S(1)}, bf16[64,4096]{1,0:T(8,128)(2,1)S(1)}) custom-call(bf16[64,4224]{1,0:T(8,128)(2,1)S(1)} %concatenate.3.refs_0_.refs_2_, bf16[64,4224]{1,0:T(8,128)(2,1)S(1)} %collective-permute-done.refs_1_.refs_3_, bf16[64,4224]{1,0:T(8,128)(2,1)S(1)} %concatenate.3.refs_0_.refs_2_, ...), custom_call_target="tpu_custom_call" | custom-call | flops 2415919104 | bytes 20971520 | tf_op jit(solution)/shard_map/expert/pallas_call | solution.py:92
  131.8 3.2 %collective-permute-done.24 = bf16[64,4096]{1,0:T(8,128)(2,1)S(1)} collective-permute-done((bf16[64,4096]{1,0:T(8,128)(2,1)S(1)}, bf16[64,4096]{1,0:T(8,128)(2,1)S(1)}, u32[]{:S(2)}, u32[]{:S(2)}) %collective-permute-start.24) | collective-permute-done | bytes 524320 | tf_op jit(solution)/shard_map/ppermute | solution.py:168
  134.9 1.3 collective-permute-done.28
  137.2 1.6 %collective-permute-start.25 = (bf16[64,4096]{1,0:T(8,128)(2,1)S(1)}, bf16[64,4096]{1,0:T(8,128)(2,1)S(1)}, u32[]{:S(2)}, u32[]{:S(2)}) collective-permute-start(bf16[64,4096]{1,0:T(8,128)(2,1)S(1)} %get-tuple-element.25), channel_id=1, source_target_pairs={{0,4},{1,5},{4,8},{5,9},{8,12},{9,13},{12,14},{13,15},{14,10},{15,... | collective-permute-start | bytes 1572872 | tf_op jit(solution)/shard_map/ppermute | solution.py:168
  138.8 10.0 %collective-permute-done.29 = bf16[64,4096]{1,0:T(8,128)(2,1)S(1)} collective-permute-done((bf16[64,4096]{1,0:T(8,128)(2,1)S(1)}, bf16[64,4096]{1,0:T(8,128)(2,1)S(1)}, u32[]{:S(2)}, u32[]{:S(2)}) %collective-permute-start.29) | collective-permute-done | bytes 524320 | tf_op jit(solution)/shard_map/ppermute | solution.py:169
  148.9 1.1 add_convert_fusion
  (66 shorter events, 7.2 us)
Async XLA Ops:
  0.0 75.0 %copy-start.8 = (f32[1,4096]{1,0:T(1,128)S(1)}, f32[1,4096]{1,0:T(1,128)}, u32[]{:S(2)}) copy-start(f32[1,4096]{1,0:T(1,128)} %refs_12_.7) | copy-start | bytes 49156
  2.0 15.3 %collective-permute-start.2 = (bf16[64,4224]{1,0:T(8,128)(2,1)S(1)}, bf16[64,4224]{1,0:T(8,128)(2,1)S(1)}, u32[]{:S(2)}, u32[]{:S(2)}) collective-permute-start(bf16[64,4224]{1,0:T(8,128)(2,1)S(1)} %concatenate.3.refs_0_.refs_2_), channel_id=1, source_target_pairs={{0,4},{1,5},{4,8},{5,9},{8,12},{9,13},{12,14},{13,15},{14,10},{15,... | collective-permute-start | bytes 1622024 | tf_op jit(solution)/shard_map/ppermute | solution.py:153
  5.1 14.0 %collective-permute-start.3 = (bf16[64,4224]{1,0:T(8,128)(2,1)S(1)}, bf16[64,4224]{1,0:T(8,128)(2,1)S(1)}, u32[]{:S(2)}, u32[]{:S(2)}) collective-permute-start(bf16[64,4224]{1,0:T(8,128)(2,1)S(1)} %concatenate.3.refs_0_.refs_2_), channel_id=1, source_target_pairs={{0,2},{1,3},{4,0},{5,1},{8,4},{9,5},{12,8},{13,9},{14,12},{15,13},... | collective-permute-start | bytes 1622024 | tf_op jit(solution)/shard_map/ppermute | solution.py:154
  17.3 13.5 %collective-permute-start.7 = (bf16[64,4224]{1,0:T(8,128)(2,1)S(1)}, bf16[64,4224]{1,0:T(8,128)(2,1)S(1)}, u32[]{:S(2)}, u32[]{:S(2)}) collective-permute-start(bf16[64,4224]{1,0:T(8,128)(2,1)S(1)} %collective-permute-done.2.refs_0_.refs_4_), channel_id=1, source_target_pairs={{0,4},{1,5},{4,8},{5,9},{8,12},{9,13},{12,14},{13,15},{14,10},{15,... | collective-permute-start | bytes 1622024 | tf_op jit(solution)/shard_map/ppermute | solution.py:153
  19.1 13.1 %collective-permute-start.8 = (bf16[64,4224]{1,0:T(8,128)(2,1)S(1)}, bf16[64,4224]{1,0:T(8,128)(2,1)S(1)}, u32[]{:S(2)}, u32[]{:S(2)}) collective-permute-start(bf16[64,4224]{1,0:T(8,128)(2,1)S(1)} %collective-permute-done.3.refs_1_.refs_5_), channel_id=1, source_target_pairs={{0,2},{1,3},{4,0},{5,1},{8,4},{9,5},{12,8},{13,9},{14,12},{15,13},... | collective-permute-start | bytes 1622024 | tf_op jit(solution)/shard_map/ppermute | solution.py:154
  30.8 12.5 %collective-permute-start.12 = (bf16[64,4224]{1,0:T(8,128)(2,1)S(1)}, bf16[64,4224]{1,0:T(8,128)(2,1)S(1)}, u32[]{:S(2)}, u32[]{:S(2)}) collective-permute-start(bf16[64,4224]{1,0:T(8,128)(2,1)S(1)} %collective-permute-done.7.refs_0_.refs_4_), channel_id=1, source_target_pairs={{0,4},{1,5},{4,8},{5,9},{8,12},{9,13},{12,14},{13,15},{14,10},{15,... | collective-permute-start | bytes 1622024 | tf_op jit(solution)/shard_map/ppermute | solution.py:153
  32.2 19.1 %copy-start.5 = (bf16[64,4224]{1,0:T(8,128)(2,1)}, bf16[64,4224]{1,0:T(8,128)(2,1)S(1)}, u32[]{:S(2)}) copy-start(bf16[64,4224]{1,0:T(8,128)(2,1)S(1)} %collective-permute-done.8.refs_1_.refs_5_) | copy-start | bytes 1622020
  32.2 12.4 %collective-permute-start.13 = (bf16[64,4224]{1,0:T(8,128)(2,1)S(1)}, bf16[64,4224]{1,0:T(8,128)(2,1)S(1)}, u32[]{:S(2)}, u32[]{:S(2)}) collective-permute-start(bf16[64,4224]{1,0:T(8,128)(2,1)S(1)} %collective-permute-done.8.refs_1_.refs_5_), channel_id=1, source_target_pairs={{0,2},{1,3},{4,0},{5,1},{8,4},{9,5},{12,8},{13,9},{14,12},{15,13},... | collective-permute-start | bytes 1622024 | tf_op jit(solution)/shard_map/ppermute | solution.py:154
  43.3 6.5 %collective-permute-start.17 = (bf16[32,4224]{1,0:T(8,128)(2,1)S(1)}, bf16[32,4224]{1,0:T(8,128)(2,1)S(1)}, u32[]{:S(2)}, u32[]{:S(2)}) collective-permute-start(bf16[32,4224]{1,0:T(8,128)(2,1)S(1)} %slice.75), channel_id=1, source_target_pairs={{0,4},{1,5},{4,8},{5,9},{8,12},{9,13},{12,14},{13,15},{14,10},{15,... | collective-permute-start | bytes 811016 | tf_op jit(solution)/shard_map/ppermute | solution.py:156
  44.7 6.6 %collective-permute-start.18 = (bf16[32,4224]{1,0:T(8,128)(2,1)S(1)}, bf16[32,4224]{1,0:T(8,128)(2,1)}, u32[]{:S(2)}, u32[]{:S(2)}) collective-permute-start(bf16[32,4224]{1,0:T(8,128)(2,1)S(1)} %slice.76), channel_id=1, source_target_pairs={{0,2},{1,3},{4,0},{5,1},{8,4},{9,5},{12,8},{13,9},{14,12},{15,13},... | collective-permute-start | bytes 811016 | tf_op jit(solution)/shard_map/ppermute | solution.py:157
  49.8 2.0 %collective-permute-start.19 = (bf16[32,4224]{1,0:T(8,128)(2,1)S(1)}, bf16[32,4224]{1,0:T(8,128)(2,1)}, u32[]{:S(2)}, u32[]{:S(2)}) collective-permute-start(bf16[32,4224]{1,0:T(8,128)(2,1)S(1)} %collective-permute-done.17.refs_0_.refs_4_), channel_id=1, source_target_pairs={{0,1},{1,0},{2,3},{3,2},{4,5},{5,4},{6,7},{7,6},{8,9},{9,8},{10,11... | collective-permute-start | bytes 811016 | tf_op jit(solution)/shard_map/ppermute | solution.py:145
  51.3 2.2 %collective-permute-start.20 = (bf16[32,4224]{1,0:T(8,128)(2,1)}, bf16[32,4224]{1,0:T(8,128)(2,1)}, u32[]{:S(2)}, u32[]{:S(2)}) collective-permute-start(bf16[32,4224]{1,0:T(8,128)(2,1)} %collective-permute-done.18.refs_1_.refs_5_), channel_id=1, source_target_pairs={{0,1},{1,0},{2,3},{3,2},{4,5},{5,4},{6,7},{7,6},{8,9},{9,8},{10,11... | collective-permute-start | bytes 811016 | tf_op jit(solution)/shard_map/ppermute | solution.py:145
  51.3 23.2 %collective-permute-start.14 = (bf16[64,4224]{1,0:T(8,128)(2,1)S(1)}, bf16[64,4224]{1,0:T(8,128)(2,1)}, u32[]{:S(2)}, u32[]{:S(2)}) collective-permute-start(bf16[64,4224]{1,0:T(8,128)(2,1)S(1)} %collective-permute-done.12.refs_0_.refs_4_), channel_id=1, source_target_pairs={{0,1},{1,0},{2,3},{3,2},{4,5},{5,4},{6,7},{7,6},{8,9},{9,8},{10,11... | collective-permute-start | bytes 1622024 | tf_op jit(solution)/shard_map/ppermute | solution.py:145
  51.8 23.0 %collective-permute-start.15 = (bf16[64,4224]{1,0:T(8,128)(2,1)S(1)}, bf16[64,4224]{1,0:T(8,128)(2,1)}, u32[]{:S(2)}, u32[]{:S(2)}) collective-permute-start(bf16[64,4224]{1,0:T(8,128)(2,1)S(1)} %collective-permute-done.13.refs_1_.refs_5_), channel_id=1, source_target_pairs={{0,1},{1,0},{2,3},{3,2},{4,5},{5,4},{6,7},{7,6},{8,9},{9,8},{10,11... | collective-permute-start | bytes 1622024 | tf_op jit(solution)/shard_map/ppermute | solution.py:145
  73.8 16.6 %collective-permute-start.21 = (bf16[64,4096]{1,0:T(8,128)(2,1)}, bf16[64,4096]{1,0:T(8,128)(2,1)S(1)}, u32[]{:S(2)}, u32[]{:S(2)}) collective-permute-start(bf16[64,4096]{1,0:T(8,128)(2,1)} %get-tuple-element.24), channel_id=1, source_target_pairs={{0,1},{1,0},{2,3},{3,2},{4,5},{5,4},{6,7},{7,6},{8,9},{9,8},{10,11... | collective-permute-start | bytes 1572872 | tf_op jit(solution)/shard_map/ppermute | solution.py:148
  74.0 33.7 %collective-permute-start.4 = (bf16[64,4224]{1,0:T(8,128)(2,1)S(1)}, bf16[64,4224]{1,0:T(8,128)(2,1)S(1)}, u32[]{:S(2)}, u32[]{:S(2)}) collective-permute-start(bf16[64,4224]{1,0:T(8,128)(2,1)S(1)} %collective-permute-done.2.refs_0_.refs_4_), channel_id=1, source_target_pairs={{0,1},{1,0},{2,3},{3,2},{4,5},{5,4},{6,7},{7,6},{8,9},{9,8},{10,11... | collective-permute-start | bytes 1622024 | tf_op jit(solution)/shard_map/ppermute | solution.py:145
  74.3 33.3 %collective-permute-start.5 = (bf16[64,4224]{1,0:T(8,128)(2,1)S(1)}, bf16[64,4224]{1,0:T(8,128)(2,1)S(1)}, u32[]{:S(2)}, u32[]{:S(2)}) collective-permute-start(bf16[64,4224]{1,0:T(8,128)(2,1)S(1)} %collective-permute-done.3.refs_1_.refs_5_), channel_id=1, source_target_pairs={{0,1},{1,0},{2,3},{3,2},{4,5},{5,4},{6,7},{7,6},{8,9},{9,8},{10,11... | collective-permute-start | bytes 1622024 | tf_op jit(solution)/shard_map/ppermute | solution.py:145
  74.5 16.5 %collective-permute-start.9 = (bf16[64,4224]{1,0:T(8,128)(2,1)S(1)}, bf16[64,4224]{1,0:T(8,128)(2,1)S(1)}, u32[]{:S(2)}, u32[]{:S(2)}) collective-permute-start(bf16[64,4224]{1,0:T(8,128)(2,1)S(1)} %collective-permute-done.7.refs_0_.refs_4_), channel_id=1, source_target_pairs={{0,1},{1,0},{2,3},{3,2},{4,5},{5,4},{6,7},{7,6},{8,9},{9,8},{10,11... | collective-permute-start | bytes 1622024 | tf_op jit(solution)/shard_map/ppermute | solution.py:145
  74.9 17.7 %collective-permute-start.10 = (bf16[64,4224]{1,0:T(8,128)(2,1)S(1)}, bf16[64,4224]{1,0:T(8,128)(2,1)S(1)}, u32[]{:S(2)}, u32[]{:S(2)}) collective-permute-start(bf16[64,4224]{1,0:T(8,128)(2,1)S(1)} %copy-done.6), channel_id=1, source_target_pairs={{0,1},{1,0},{2,3},{3,2},{4,5},{5,4},{6,7},{7,6},{8,9},{9,8},{10,11... | collective-permute-start | bytes 1622024 | tf_op jit(solution)/shard_map/ppermute | solution.py:145
  90.4 14.8 %collective-permute-start.16 = (bf16[128,4096]{1,0:T(8,128)(2,1)S(1)}, bf16[128,4096]{1,0:T(8,128)(2,1)S(1)}, u32[]{:S(2)}, u32[]{:S(2)}) collective-permute-start(bf16[128,4096]{1,0:T(8,128)(2,1)S(1)} %get-tuple-element.22), channel_id=1, source_target_pairs={{0,1},{1,0},{2,3},{3,2},{4,5},{5,4},{6,7},{7,6},{8,9},{9,8},{10,11... | collective-permute-start | bytes 3145736 | tf_op jit(solution)/shard_map/ppermute | solution.py:148
  91.0 14.1 %collective-permute-start.22 = (bf16[32,4096]{1,0:T(8,128)(2,1)S(1)}, bf16[32,4096]{1,0:T(8,128)(2,1)S(1)}, u32[]{:S(2)}, u32[]{:S(2)}) collective-permute-start(bf16[32,4096]{1,0:T(8,128)(2,1)S(1)} %get-tuple-element.31), channel_id=1, source_target_pairs={{0,4},{1,5},{4,8},{5,9},{8,12},{9,13},{12,14},{13,15},{14,10},{15,... | collective-permute-start | bytes 786440 | tf_op jit(solution)/shard_map/ppermute | solution.py:160
  92.6 12.6 %collective-permute-start.26 = (bf16[32,4096]{1,0:T(8,128)(2,1)S(1)}, bf16[32,4096]{1,0:T(8,128)(2,1)S(1)}, u32[]{:S(2)}, u32[]{:S(2)}) collective-permute-start(bf16[32,4096]{1,0:T(8,128)(2,1)S(1)} %get-tuple-element.32), channel_id=1, source_target_pairs={{0,2},{1,3},{4,0},{5,1},{8,4},{9,5},{12,8},{13,9},{14,12},{15,13},... | collective-permute-start | bytes 786440 | tf_op jit(solution)/shard_map/ppermute | solution.py:161
  105.1 15.2 %collective-permute-start.11 = (bf16[128,4096]{1,0:T(8,128)(2,1)S(1)}, bf16[128,4096]{1,0:T(8,128)(2,1)S(1)}, u32[]{:S(2)}, u32[]{:S(2)}) collective-permute-start(bf16[128,4096]{1,0:T(8,128)(2,1)S(1)} %get-tuple-element.20), channel_id=1, source_target_pairs={{0,1},{1,0},{2,3},{3,2},{4,5},{5,4},{6,7},{7,6},{8,9},{9,8},{10,11... | collective-permute-start | bytes 3145736 | tf_op jit(solution)/shard_map/ppermute | solution.py:148
  105.6 14.7 %collective-permute-start.23 = (bf16[64,4096]{1,0:T(8,128)(2,1)S(1)}, bf16[64,4096]{1,0:T(8,128)(2,1)S(1)}, u32[]{:S(2)}, u32[]{:S(2)}) collective-permute-start(bf16[64,4096]{1,0:T(8,128)(2,1)S(1)} %get-tuple-element.29), channel_id=1, source_target_pairs={{0,4},{1,5},{4,8},{5,9},{8,12},{9,13},{12,14},{13,15},{14,10},{15,... | collective-permute-start | bytes 1572872 | tf_op jit(solution)/shard_map/ppermute | solution.py:168
  107.2 14.0 %collective-permute-start.27 = (bf16[64,4096]{1,0:T(8,128)(2,1)S(1)}, bf16[64,4096]{1,0:T(8,128)(2,1)S(1)}, u32[]{:S(2)}, u32[]{:S(2)}) collective-permute-start(bf16[64,4096]{1,0:T(8,128)(2,1)S(1)} %get-tuple-element.30), channel_id=1, source_target_pairs={{0,2},{1,3},{4,0},{5,1},{8,4},{9,5},{12,8},{13,9},{14,12},{15,13},... | collective-permute-start | bytes 1572872 | tf_op jit(solution)/shard_map/ppermute | solution.py:169
  107.6 16.1 %collective-permute-start = (bf16[64,4224]{1,0:T(8,128)(2,1)S(1)}, bf16[64,4224]{1,0:T(8,128)(2,1)S(1)}, u32[]{:S(2)}, u32[]{:S(2)}) collective-permute-start(bf16[64,4224]{1,0:T(8,128)(2,1)S(1)} %concatenate.3.refs_0_.refs_2_), channel_id=1, source_target_pairs={{0,1},{1,0},{2,3},{3,2},{4,5},{5,4},{6,7},{7,6},{8,9},{9,8},{10,11... | collective-permute-start | bytes 1622024 | tf_op jit(solution)/shard_map/ppermute | solution.py:145
  119.8 12.0 %collective-permute-start.6 = (bf16[128,4096]{1,0:T(8,128)(2,1)S(1)}, bf16[128,4096]{1,0:T(8,128)(2,1)S(1)}, u32[]{:S(2)}, u32[]{:S(2)}) collective-permute-start(bf16[128,4096]{1,0:T(8,128)(2,1)S(1)} %get-tuple-element.18), channel_id=1, source_target_pairs={{0,1},{1,0},{2,3},{3,2},{4,5},{5,4},{6,7},{7,6},{8,9},{9,8},{10,11... | collective-permute-start | bytes 3145736 | tf_op jit(solution)/shard_map/ppermute | solution.py:148
  121.7 13.3 %collective-permute-start.24 = (bf16[64,4096]{1,0:T(8,128)(2,1)S(1)}, bf16[64,4096]{1,0:T(8,128)(2,1)S(1)}, u32[]{:S(2)}, u32[]{:S(2)}) collective-permute-start(bf16[64,4096]{1,0:T(8,128)(2,1)S(1)} %get-tuple-element.27), channel_id=1, source_target_pairs={{0,4},{1,5},{4,8},{5,9},{8,12},{9,13},{12,14},{13,15},{14,10},{15,... | collective-permute-start | bytes 1572872 | tf_op jit(solution)/shard_map/ppermute | solution.py:168
  123.3 12.9 %collective-permute-start.28 = (bf16[64,4096]{1,0:T(8,128)(2,1)S(1)}, bf16[64,4096]{1,0:T(8,128)(2,1)S(1)}, u32[]{:S(2)}, u32[]{:S(2)}) collective-permute-start(bf16[64,4096]{1,0:T(8,128)(2,1)S(1)} %get-tuple-element.28), channel_id=1, source_target_pairs={{0,2},{1,3},{4,0},{5,1},{8,4},{9,5},{12,8},{13,9},{14,12},{15,13},... | collective-permute-start | bytes 1572872 | tf_op jit(solution)/shard_map/ppermute | solution.py:169
  131.7 7.1 %collective-permute-start.1 = (bf16[64,4096]{1,0:T(8,128)(2,1)S(1)}, bf16[64,4096]{1,0:T(8,128)(2,1)S(1)}, u32[]{:S(2)}, u32[]{:S(2)}) collective-permute-start(bf16[64,4096]{1,0:T(8,128)(2,1)S(1)} %get-tuple-element.16), channel_id=1, source_target_pairs={{0,1},{1,0},{2,3},{3,2},{4,5},{5,4},{6,7},{7,6},{8,9},{9,8},{10,11... | collective-permute-start | bytes 1572872 | tf_op jit(solution)/shard_map/ppermute | solution.py:148
  136.7 12.1 %collective-permute-start.29 = (bf16[64,4096]{1,0:T(8,128)(2,1)S(1)}, bf16[64,4096]{1,0:T(8,128)(2,1)S(1)}, u32[]{:S(2)}, u32[]{:S(2)}) collective-permute-start(bf16[64,4096]{1,0:T(8,128)(2,1)S(1)} %get-tuple-element.26), channel_id=1, source_target_pairs={{0,2},{1,3},{4,0},{5,1},{8,4},{9,5},{12,8},{13,9},{14,12},{15,13},... | collective-permute-start | bytes 1572872 | tf_op jit(solution)/shard_map/ppermute | solution.py:169
  137.2 11.7 %collective-permute-start.25 = (bf16[64,4096]{1,0:T(8,128)(2,1)S(1)}, bf16[64,4096]{1,0:T(8,128)(2,1)S(1)}, u32[]{:S(2)}, u32[]{:S(2)}) collective-permute-start(bf16[64,4096]{1,0:T(8,128)(2,1)S(1)} %get-tuple-element.25), channel_id=1, source_target_pairs={{0,4},{1,5},{4,8},{5,9},{8,12},{9,13},{12,14},{13,15},{14,10},{15,... | collective-permute-start | bytes 1572872 | tf_op jit(solution)/shard_map/ppermute | solution.py:168
  (8 other events, 52.1 us)

commit v3 on v2

--- a/solution.py
+++ b/solution.py
@@ -9,8 +9,8 @@
 
 DENOMINATOR = 32768.0
 LANES = 128
-DEPTH_STEPS = 8
-WIDTH_STEPS = 8
+UNIT_CHUNK = 256
+WIDTH_CHUNK = 512
 
 
 def ring_of(chips):
@@ -30,80 +30,113 @@
     return jnp.concatenate([tokens, high, low, blank], axis=1)
 
 
-def expert_kernel(count, *refs):
-    xs, gates = refs[:count], refs[count : 2 * count]
-    pick, gate_up, gate_up_s, down, down_s = refs[2 * count : 2 * count + 5]
-    outs = refs[2 * count + 5 : -3]
-    total, hidden, weight = refs[-3:]
-    step = pl.program_id(0)
-    units = down.shape[0]
-
-    @pl.when(step < DEPTH_STEPS)
-    def _():
-        x = jnp.concatenate([ref[...] for ref in xs], axis=0)
-        part = jnp.dot(x, gate_up[...], preferred_element_type=jnp.float32)
-
-        @pl.when(step == 0)
-        def _():
-            total[...] = part
-
-        @pl.when(step > 0)
-        def _():
-            total[...] += part
-
-    @pl.when(step == DEPTH_STEPS)
-    def _():
-        scaled = total[...] * gate_up_s[...]
-        hidden[...] = (jax.nn.silu(scaled[:, :units]) * scaled[:, units:]).astype(jnp.bfloat16)
-        digits = jnp.concatenate([ref[...] for ref in gates], axis=0).astype(jnp.float32)
-        number = jnp.sum(digits * pick[...], axis=1, keepdims=True)
-        weight[...] = jnp.broadcast_to(number / DENOMINATOR, weight.shape)
-
-    @pl.when(step >= DEPTH_STEPS)
-    def _():
-        out = jnp.dot(hidden[...], down[...], preferred_element_type=jnp.float32)
-        out = (out * down_s[...] * weight[:, :1]).astype(jnp.bfloat16)
-        at = 0
-        for ref in outs:
-            ref[...] = out[at : at + ref.shape[0]]
-            at += ref.shape[0]
+def expert_kernel(sizes, *refs):
+    count = len(sizes)
+    xs = refs[:count]
+    pick, gate_up_s, down_s, gate_up, down = refs[count : count + 5]
+    outs = refs[count + 5 : count + 7]
+    x, gate_up_here, down_here, hidden, out, x_sem, gate_up_sem, down_sem, out_sem = refs[count + 7 :]
+    units, width = down.shape
+
+    starts = [sum(sizes[:i]) for i in range(count)]
+    x_copies = [
+        pltpu.make_async_copy(ref, x.at[pl.ds(start, size)], x_sem.at[i])
+        for i, (ref, start, size) in enumerate(zip(xs, starts, sizes))
+    ]
+
+    def gate_up_copy(chunk, side):
+        columns = pl.ds(pl.multiple_of(side * units + chunk * UNIT_CHUNK, UNIT_CHUNK), UNIT_CHUNK)
+        return pltpu.make_async_copy(
+            gate_up.at[:, columns], gate_up_here.at[:, columns], gate_up_sem.at[chunk, side]
+        )
+
+    def down_copy(chunk):
+        columns = pl.ds(pl.multiple_of(chunk * WIDTH_CHUNK, WIDTH_CHUNK), WIDTH_CHUNK)
+        return pltpu.make_async_copy(down.at[:, columns], down_here.at[:, columns], down_sem.at[chunk])
+
+    def out_copies(chunk):
+        columns = pl.ds(pl.multiple_of(chunk * WIDTH_CHUNK, WIDTH_CHUNK), WIDTH_CHUNK)
+        copies, start = [], 0
+        for i, ref in enumerate(outs):
+            size = ref.shape[0]
+            copies.append(
+                pltpu.make_async_copy(
+                    out.at[pl.ds(start, size), columns], ref.at[:, columns], out_sem.at[chunk, i]
+                )
+            )
+            start += size
+        return copies
+
+    for copy in x_copies:
+        copy.start()
+    for chunk in range(units // UNIT_CHUNK):
+        gate_up_copy(chunk, 0).start()
+        gate_up_copy(chunk, 1).start()
+    for chunk in range(width // WIDTH_CHUNK):
+        down_copy(chunk).start()
+    for copy in x_copies:
+        copy.wait()
+
+    digits = x[:, width:].astype(jnp.float32)
+    weight = jnp.sum(digits * pick[...], axis=1, keepdims=True) / DENOMINATOR
+
+    def unit_step(chunk, carry):
+        sides = []
+        for side in range(2):
+            gate_up_copy(chunk, side).wait()
+            columns = pl.ds(pl.multiple_of(side * units + chunk * UNIT_CHUNK, UNIT_CHUNK), UNIT_CHUNK)
+            part = jnp.dot(x[:, :width], gate_up_here[:, columns], preferred_element_type=jnp.float32)
+            sides.append(part * gate_up_s[:, columns])
+        here = pl.ds(pl.multiple_of(chunk * UNIT_CHUNK, UNIT_CHUNK), UNIT_CHUNK)
+        hidden[:, here] = (jax.nn.silu(sides[0]) * sides[1]).astype(jnp.bfloat16)
+        return carry
+
+    lax.fori_loop(0, units // UNIT_CHUNK, unit_step, 0)
+
+    def width_step(chunk, carry):
+        down_copy(chunk).wait()
+        columns = pl.ds(pl.multiple_of(chunk * WIDTH_CHUNK, WIDTH_CHUNK), WIDTH_CHUNK)
+        part = jnp.dot(hidden[...], down_here[:, columns], preferred_element_type=jnp.float32)
+        out[:, columns] = (part * down_s[:, columns] * weight).astype(jnp.bfloat16)
+        for copy in out_copies(chunk):
+            copy.start()
+        return carry
+
+    lax.fori_loop(0, width // WIDTH_CHUNK, width_step, 0)
+    for chunk in range(width // WIDTH_CHUNK):
+        for copy in out_copies(chunk):
+            copy.wait()
 
 
 def expert_part(blocks, split, pick, gate_up_w, gate_up_s, down_w, down_s):
     width, units2 = gate_up_w.shape
     units = down_w.shape[0]
     sizes = [block.shape[0] for block in blocks]
-    rows = sum(sizes)
-    deep, wide = width // DEPTH_STEPS, width // WIDTH_STEPS
-    phase1 = lambda i: jnp.minimum(i, DEPTH_STEPS - 1)
-    phase2 = lambda i: jnp.maximum(i - DEPTH_STEPS, 0)
-    x_specs = [pl.BlockSpec((size, deep), lambda i: (0, phase1(i))) for size in sizes]
-    gate_specs = [pl.BlockSpec((size, LANES), lambda i: (0, width // LANES)) for size in sizes]
-    weight_specs = [
-        pl.BlockSpec((1, LANES), lambda i: (0, 0)),
-        pl.BlockSpec((deep, units2), lambda i: (phase1(i), 0)),
-        pl.BlockSpec((1, units2), lambda i: (0, 0)),
-        pl.BlockSpec((units, wide), lambda i: (0, phase2(i))),
-        pl.BlockSpec((1, wide), lambda i: (0, phase2(i))),
-    ]
+    rows, packed_width = sum(sizes), blocks[0].shape[1]
     out_rows = [sum(sizes[:split]), sum(sizes[split:])]
+    anywhere, vmem = pl.BlockSpec(memory_space=pl.ANY), pl.BlockSpec(memory_space=pltpu.VMEM)
     flops = 2 * rows * width * (units2 + units)
     moved = 2 * width * (units2 + units) + 4 * rows * width
     return pl.pallas_call(
-        functools.partial(expert_kernel, len(sizes)),
-        grid=(DEPTH_STEPS + WIDTH_STEPS,),
-        in_specs=x_specs + gate_specs + weight_specs,
-        out_specs=[pl.BlockSpec((size, wide), lambda i: (0, phase2(i))) for size in out_rows],
+        functools.partial(expert_kernel, sizes),
+        in_specs=[anywhere] * len(blocks) + [vmem] * 3 + [anywhere] * 2,
+        out_specs=[anywhere] * 2,
         out_shape=[jax.ShapeDtypeStruct((size, width), jnp.bfloat16) for size in out_rows],
         scratch_shapes=[
-            pltpu.VMEM((rows, units2), jnp.float32),
+            pltpu.VMEM((rows, packed_width), jnp.bfloat16),
+            pltpu.VMEM((width, units2), jnp.bfloat16),
+            pltpu.VMEM((units, width), jnp.bfloat16),
             pltpu.VMEM((rows, units), jnp.bfloat16),
-            pltpu.VMEM((rows, LANES), jnp.float32),
+            pltpu.VMEM((rows, width), jnp.bfloat16),
+            pltpu.SemaphoreType.DMA((len(blocks),)),
+            pltpu.SemaphoreType.DMA((units // UNIT_CHUNK, 2)),
+            pltpu.SemaphoreType.DMA((width // WIDTH_CHUNK,)),
+            pltpu.SemaphoreType.DMA((width // WIDTH_CHUNK, 2)),
         ],
-        compiler_params=pltpu.CompilerParams(vmem_limit_bytes=24 << 20),
+        compiler_params=pltpu.CompilerParams(vmem_limit_bytes=52 << 20),
         cost_estimate=pl.CostEstimate(flops=flops, bytes_accessed=moved, transcendentals=rows * units),
         name="expert",
-    )(*blocks, *blocks, pick, gate_up_w, gate_up_s, down_w, down_s)
+    )(*blocks, pick, gate_up_s, down_s, gate_up_w, down_w)
 
 
 def add(*terms):

time: 151 us -> 162 us (1.073)
  Pallas kernels: 56.2 us -> 79 us
  local copies, waits for them, and re-layouts: 12.8 us -> 4.66 us
  waiting for transfers between devices: 57.2 us -> 54.2 us
    pallas_call x5, Pallas kernels: 56.2 us -> 79 us  [expert_part(): pl.pallas_call(functools.partial(expert_kernel, sizes), in_specs=[anywher...]
    unnamed x20, local copies, waits for them, and re-layouts: 11.6 us -> 3.39 us
    ppermute x3, waiting for transfers between devices: 3.32 us -> 0.17 us  [body(): to_above = send(above, perm=upward)]
  transfers between devices with their start and end apart: 30 -> 30, of which waited for: 11 -> 8; matrix products, arithmetic and copies ran while one was open for 1% -> 1% of each run, Pallas kernels for 37% -> 49%
where the time goes in v3:
time: 162 us
  Pallas kernels  79 us (49%)
  waiting for transfers between devices  54.2 us (33%)
  starting transfers between devices  20.5 us (13%)
  local copies, waits for them, and re-layouts  4.66 us (3%)
  other arithmetic  3.22 us (2%)
    pallas_call x5, Pallas kernels, expert_part(): pl.pallas_call(functools.partial(expert_kernel, sizes), in_specs=[anywher...  79 us
    ppermute x3, waiting for transfers between devices, body(): from_below = send(from_below, perm=upward)  34.1 us
    ppermute x3, waiting for transfers between devices, body(): to_below = send(below, perm=downward)  12.3 us
    ppermute x3, starting transfers between devices, body(): from_below = send(from_below, perm=upward)  6.35 us
    ppermute x3, starting transfers between devices, body(): to_above = send(above, perm=upward)  4.84 us
    ppermute x1, waiting for transfers between devices, body(): last_below = send(from_below[:half], perm=upward)  4.35 us
    unnamed x20, local copies, waits for them, and re-layouts  3.39 us
  transfers between devices with their start and end apart: 30, of which 8 were waited for; matrix products, arithmetic and copies ran while one was open for 1% of the time, Pallas kernels for 49%

profile of v3, /device:TPU:0, one launch (start us, length us, event | category | flops | bytes accessed | tf_op | source)
XLA Modules:
  0.0 161.8 jit_solution(9437272447113229663)
XLA Ops:
  0.0 0.7 select_reduce_fusion
  0.8 1.1 concatenate.3.refs_0_
  2.0 3.1 %collective-permute-start.2 = (bf16[64,4224]{1,0:T(8,128)(2,1)S(1)}, bf16[64,4224]{1,0:T(8,128)(2,1)S(1)}, u32[]{:S(2)}, u32[]{:S(2)}) collective-permute-start(bf16[64,4224]{1,0:T(8,128)(2,1)S(1)} %concatenate.3.refs_0_), channel_id=1, source_target_pairs={{0,4},{1,5},{4,8},{5,9},{8,12},{9,13},{12,14},{13,15},{14,10},{15,... | collective-permute-start | bytes 1622024 | tf_op jit(solution)/shard_map/ppermute | solution.py:186
  5.1 12.2 %collective-permute-done.2.refs_0_ = bf16[64,4224]{1,0:T(8,128)(2,1)S(1)} collective-permute-done((bf16[64,4224]{1,0:T(8,128)(2,1)S(1)}, bf16[64,4224]{1,0:T(8,128)(2,1)S(1)}, u32[]{:S(2)}, u32[]{:S(2)}) %collective-permute-start.2) | collective-permute-done | bytes 540704 | tf_op jit(solution)/shard_map/ppermute | solution.py:186
  17.3 1.8 %collective-permute-start.7 = (bf16[64,4224]{1,0:T(8,128)(2,1)S(1)}, bf16[64,4224]{1,0:T(8,128)(2,1)S(1)}, u32[]{:S(2)}, u32[]{:S(2)}) collective-permute-start(bf16[64,4224]{1,0:T(8,128)(2,1)S(1)} %collective-permute-done.2.refs_0_), channel_id=1, source_target_pairs={{0,4},{1,5},{4,8},{5,9},{8,12},{9,13},{12,14},{13,15},{14,10},{15,... | collective-permute-start | bytes 1622024 | tf_op jit(solution)/shard_map/ppermute | solution.py:186
  19.3 11.4 %collective-permute-done.7.refs_0_ = bf16[64,4224]{1,0:T(8,128)(2,1)S(1)} collective-permute-done((bf16[64,4224]{1,0:T(8,128)(2,1)S(1)}, bf16[64,4224]{1,0:T(8,128)(2,1)S(1)}, u32[]{:S(2)}, u32[]{:S(2)}) %collective-permute-start.7) | collective-permute-done | bytes 540704 | tf_op jit(solution)/shard_map/ppermute | solution.py:186
  30.7 1.5 collective-permute-start.12
  32.2 0.5 collective-permute-start.13
  32.8 10.5 %collective-permute-done.12.refs_0_ = bf16[64,4224]{1,0:T(8,128)(2,1)S(1)} collective-permute-done((bf16[64,4224]{1,0:T(8,128)(2,1)S(1)}, bf16[64,4224]{1,0:T(8,128)(2,1)S(1)}, u32[]{:S(2)}, u32[]{:S(2)}) %collective-permute-start.12) | collective-permute-done | bytes 540704 | tf_op jit(solution)/shard_map/ppermute | solution.py:186
  43.3 1.4 collective-permute-start.17
  44.7 0.8 collective-permute-start.18
  45.5 4.4 %collective-permute-done.17.refs_0_ = bf16[32,4224]{1,0:T(8,128)(2,1)S(1)} collective-permute-done((bf16[32,4224]{1,0:T(8,128)(2,1)S(1)}, bf16[32,4224]{1,0:T(8,128)(2,1)S(1)}, u32[]{:S(2)}, u32[]{:S(2)}) %collective-permute-start.17) | collective-permute-done | bytes 270368 | tf_op jit(solution)/shard_map/ppermute | solution.py:189
  49.8 1.5 collective-permute-done.18.refs_1_
  51.3 0.5 collective-permute-start.14
  51.8 1.7 %collective-permute-done.20.refs_3_ = bf16[32,4224]{1,0:T(8,128)(2,1)} collective-permute-done((bf16[32,4224]{1,0:T(8,128)(2,1)}, bf16[32,4224]{1,0:T(8,128)(2,1)}, u32[]{:S(2)}, u32[]{:S(2)}) %collective-permute-start.20) | collective-permute-done | bytes 270368 | tf_op jit(solution)/shard_map/ppermute | solution.py:178
  53.5 0.7 copy-done.2
  54.2 0.7 copy-done.3
  54.9 13.5 %expert.9 = (bf16[64,4096]{1,0:T(8,128)(2,1)S(1)}, bf16[64,4096]{1,0:T(8,128)(2,1)}) custom-call(bf16[32,4224]{1,0:T(8,128)(2,1)S(1)} %collective-permute-done.17.refs_0_, bf16[32,4224]{1,0:T(8,128)(2,1)} %collective-permute-done.18.refs_1_, bf16[32,4224]{1,0:T(8,128)(2,1)} %collective-permute-done.19.refs_2_, ...), custom_call_target="tpu_custom_call" | custom-call | flops 2415919104 | bytes 20971520 | tf_op jit(solution)/shard_map/expert/pallas_call | solution.py:120
  69.6 17.6 %expert.8 = (bf16[128,4096]{1,0:T(8,128)(2,1)}, bf16[128,4096]{1,0:T(8,128)(2,1)}) custom-call(bf16[64,4224]{1,0:T(8,128)(2,1)S(1)} %collective-permute-done.12.refs_0_, bf16[64,4224]{1,0:T(8,128)(2,1)S(1)} %collective-permute-done.13.refs_1_, bf16[64,4224]{1,0:T(8,128)(2,1)} %collective-permute-done.14.refs_2_, ...), custom_call_target="tpu_custom_call" | custom-call | flops 4831838208 | bytes 23068672 | tf_op jit(solution)/shard_map/expert/pallas_call | solution.py:120
  87.9 1.6 %collective-permute-start.22 = (bf16[32,4096]{1,0:T(8,128)(2,1)S(1)}, bf16[32,4096]{1,0:T(8,128)(2,1)S(1)}, u32[]{:S(2)}, u32[]{:S(2)}) collective-permute-start(bf16[32,4096]{1,0:T(8,128)(2,1)S(1)} %get-tuple-element.31), channel_id=1, source_target_pairs={{0,4},{1,5},{4,8},{5,9},{8,12},{9,13},{12,14},{13,15},{14,10},{15,... | collective-permute-start | bytes 786440 | tf_op jit(solution)/shard_map/ppermute | solution.py:193
  90.3 17.5 %expert.7 = (bf16[128,4096]{1,0:T(8,128)(2,1)}, bf16[128,4096]{1,0:T(8,128)(2,1)}) custom-call(bf16[64,4224]{1,0:T(8,128)(2,1)S(1)} %collective-permute-done.7.refs_0_, bf16[64,4224]{1,0:T(8,128)(2,1)S(1)} %copy-done.1, bf16[64,4224]{1,0:T(8,128)(2,1)S(1)} %collective-permute-done.9.refs_2_, bf16[64,4224]{1,0:T(8,128)(2,1)} %copy-done.8, ...), custom_call_target="tpu_custom_call" | custom-call | flops 4831838208 | bytes 23068672 | tf_op jit(solution)/shard_map/expert/pallas_call | solution.py:120
  108.3 1.6 %collective-permute-start.23 = (bf16[64,4096]{1,0:T(8,128)(2,1)S(1)}, bf16[64,4096]{1,0:T(8,128)(2,1)S(1)}, u32[]{:S(2)}, u32[]{:S(2)}) collective-permute-start(bf16[64,4096]{1,0:T(8,128)(2,1)S(1)} %get-tuple-element.29), channel_id=1, source_target_pairs={{0,4},{1,5},{4,8},{5,9},{8,12},{9,13},{12,14},{13,15},{14,10},{15,... | collective-permute-start | bytes 1572872 | tf_op jit(solution)/shard_map/ppermute | solution.py:201
  110.4 0.8 copy-done.7
  111.2 17.5 %expert.6 = (bf16[128,4096]{1,0:T(8,128)(2,1)}, bf16[128,4096]{1,0:T(8,128)(2,1)}) custom-call(bf16[64,4224]{1,0:T(8,128)(2,1)S(1)} %collective-permute-done.2.refs_0_, bf16[64,4224]{1,0:T(8,128)(2,1)S(1)} %collective-permute-done.3.refs_1_, bf16[64,4224]{1,0:T(8,128)(2,1)S(1)} %collective-permute-done.4.refs_2_, bf16[64,4224]{1,0:T(8,128)(2,1)} %copy-done.7, ...), custom_call_target="tpu_custom_call" | custom-call | flops 4831838208 | bytes 23068672 | tf_op jit(solution)/shard_map/expert/pallas_call | solution.py:120
  128.8 0.6 collective-permute-start.6
  129.9 1.6 %collective-permute-start.24 = (bf16[64,4096]{1,0:T(8,128)(2,1)S(1)}, bf16[64,4096]{1,0:T(8,128)(2,1)S(1)}, u32[]{:S(2)}, u32[]{:S(2)}) collective-permute-start(bf16[64,4096]{1,0:T(8,128)(2,1)S(1)} %get-tuple-element.27), channel_id=1, source_target_pairs={{0,4},{1,5},{4,8},{5,9},{8,12},{9,13},{12,14},{13,15},{14,10},{15,... | collective-permute-start | bytes 1572872 | tf_op jit(solution)/shard_map/ppermute | solution.py:201
  131.9 0.8 copy-done.9
  132.7 12.9 %expert.5 = (bf16[64,4096]{1,0:T(8,128)(2,1)S(1)}, bf16[64,4096]{1,0:T(8,128)(2,1)S(1)}) custom-call(bf16[64,4224]{1,0:T(8,128)(2,1)S(1)} %concatenate.3.refs_0_, bf16[64,4224]{1,0:T(8,128)(2,1)} %copy-done.9, f32[1,128]{1,0:T(1,128)S(1)} %compare_select_fusion.1.refs_2_.refs_4_, f32[1,1536]{1,0:T(1,128)S(1)} %copy-done.3, f32[1,4096]{1,0:T(1,128)S(1)} %copy-done.2, ...), custom_call_target="tpu_custom_call" | custom-call | flops 2415919104 | bytes 20971520 | tf_op jit(solution)/shard_map/expert/pallas_call | solution.py:120
  146.2 0.5 collective-permute-start.29
  146.7 1.6 collective-permute-start.25
  148.3 12.3 %collective-permute-done.29 = bf16[64,4096]{1,0:T(8,128)(2,1)S(1)} collective-permute-done((bf16[64,4096]{1,0:T(8,128)(2,1)S(1)}, bf16[64,4096]{1,0:T(8,128)(2,1)S(1)}, u32[]{:S(2)}, u32[]{:S(2)}) %collective-permute-start.29) | collective-permute-done | bytes 524320 | tf_op jit(solution)/shard_map/ppermute | solution.py:202
  160.7 1.1 add_convert_fusion
  (66 shorter events, 5.6 us)
Async XLA Ops:
  2.0 15.3 %collective-permute-start.2 = (bf16[64,4224]{1,0:T(8,128)(2,1)S(1)}, bf16[64,4224]{1,0:T(8,128)(2,1)S(1)}, u32[]{:S(2)}, u32[]{:S(2)}) collective-permute-start(bf16[64,4224]{1,0:T(8,128)(2,1)S(1)} %concatenate.3.refs_0_), channel_id=1, source_target_pairs={{0,4},{1,5},{4,8},{5,9},{8,12},{9,13},{12,14},{13,15},{14,10},{15,... | collective-permute-start | bytes 1622024 | tf_op jit(solution)/shard_map/ppermute | solution.py:186
  5.1 14.0 %collective-permute-start.3 = (bf16[64,4224]{1,0:T(8,128)(2,1)S(1)}, bf16[64,4224]{1,0:T(8,128)(2,1)S(1)}, u32[]{:S(2)}, u32[]{:S(2)}) collective-permute-start(bf16[64,4224]{1,0:T(8,128)(2,1)S(1)} %concatenate.3.refs_0_), channel_id=1, source_target_pairs={{0,2},{1,3},{4,0},{5,1},{8,4},{9,5},{12,8},{13,9},{14,12},{15,13},... | collective-permute-start | bytes 1622024 | tf_op jit(solution)/shard_map/ppermute | solution.py:187
  17.3 13.5 %collective-permute-start.7 = (bf16[64,4224]{1,0:T(8,128)(2,1)S(1)}, bf16[64,4224]{1,0:T(8,128)(2,1)S(1)}, u32[]{:S(2)}, u32[]{:S(2)}) collective-permute-start(bf16[64,4224]{1,0:T(8,128)(2,1)S(1)} %collective-permute-done.2.refs_0_), channel_id=1, source_target_pairs={{0,4},{1,5},{4,8},{5,9},{8,12},{9,13},{12,14},{13,15},{14,10},{15,... | collective-permute-start | bytes 1622024 | tf_op jit(solution)/shard_map/ppermute | solution.py:186
  19.1 13.1 %collective-permute-start.8 = (bf16[64,4224]{1,0:T(8,128)(2,1)S(1)}, bf16[64,4224]{1,0:T(8,128)(2,1)S(1)}, u32[]{:S(2)}, u32[]{:S(2)}) collective-permute-start(bf16[64,4224]{1,0:T(8,128)(2,1)S(1)} %collective-permute-done.3.refs_1_), channel_id=1, source_target_pairs={{0,2},{1,3},{4,0},{5,1},{8,4},{9,5},{12,8},{13,9},{14,12},{15,13},... | collective-permute-start | bytes 1622024 | tf_op jit(solution)/shard_map/ppermute | solution.py:187
  30.7 12.5 %collective-permute-start.12 = (bf16[64,4224]{1,0:T(8,128)(2,1)S(1)}, bf16[64,4224]{1,0:T(8,128)(2,1)S(1)}, u32[]{:S(2)}, u32[]{:S(2)}) collective-permute-start(bf16[64,4224]{1,0:T(8,128)(2,1)S(1)} %collective-permute-done.7.refs_0_), channel_id=1, source_target_pairs={{0,4},{1,5},{4,8},{5,9},{8,12},{9,13},{12,14},{13,15},{14,10},{15,... | collective-permute-start | bytes 1622024 | tf_op jit(solution)/shard_map/ppermute | solution.py:186
  32.2 12.4 %collective-permute-start.13 = (bf16[64,4224]{1,0:T(8,128)(2,1)S(1)}, bf16[64,4224]{1,0:T(8,128)(2,1)S(1)}, u32[]{:S(2)}, u32[]{:S(2)}) collective-permute-start(bf16[64,4224]{1,0:T(8,128)(2,1)S(1)} %collective-permute-done.8.refs_1_), channel_id=1, source_target_pairs={{0,2},{1,3},{4,0},{5,1},{8,4},{9,5},{12,8},{13,9},{14,12},{15,13},... | collective-permute-start | bytes 1622024 | tf_op jit(solution)/shard_map/ppermute | solution.py:187
  43.3 6.5 %collective-permute-start.17 = (bf16[32,4224]{1,0:T(8,128)(2,1)S(1)}, bf16[32,4224]{1,0:T(8,128)(2,1)S(1)}, u32[]{:S(2)}, u32[]{:S(2)}) collective-permute-start(bf16[32,4224]{1,0:T(8,128)(2,1)S(1)} %slice.75), channel_id=1, source_target_pairs={{0,4},{1,5},{4,8},{5,9},{8,12},{9,13},{12,14},{13,15},{14,10},{15,... | collective-permute-start | bytes 811016 | tf_op jit(solution)/shard_map/ppermute | solution.py:189
  44.7 6.6 %collective-permute-start.18 = (bf16[32,4224]{1,0:T(8,128)(2,1)S(1)}, bf16[32,4224]{1,0:T(8,128)(2,1)}, u32[]{:S(2)}, u32[]{:S(2)}) collective-permute-start(bf16[32,4224]{1,0:T(8,128)(2,1)S(1)} %slice.76), channel_id=1, source_target_pairs={{0,2},{1,3},{4,0},{5,1},{8,4},{9,5},{12,8},{13,9},{14,12},{15,13},... | collective-permute-start | bytes 811016 | tf_op jit(solution)/shard_map/ppermute | solution.py:190
  49.8 2.0 %collective-permute-start.19 = (bf16[32,4224]{1,0:T(8,128)(2,1)S(1)}, bf16[32,4224]{1,0:T(8,128)(2,1)}, u32[]{:S(2)}, u32[]{:S(2)}) collective-permute-start(bf16[32,4224]{1,0:T(8,128)(2,1)S(1)} %collective-permute-done.17.refs_0_), channel_id=1, source_target_pairs={{0,1},{1,0},{2,3},{3,2},{4,5},{5,4},{6,7},{7,6},{8,9},{9,8},{10,11... | collective-permute-start | bytes 811016 | tf_op jit(solution)/shard_map/ppermute | solution.py:178
  51.3 2.2 %collective-permute-start.20 = (bf16[32,4224]{1,0:T(8,128)(2,1)}, bf16[32,4224]{1,0:T(8,128)(2,1)}, u32[]{:S(2)}, u32[]{:S(2)}) collective-permute-start(bf16[32,4224]{1,0:T(8,128)(2,1)} %collective-permute-done.18.refs_1_), channel_id=1, source_target_pairs={{0,1},{1,0},{2,3},{3,2},{4,5},{5,4},{6,7},{7,6},{8,9},{9,8},{10,11... | collective-permute-start | bytes 811016 | tf_op jit(solution)/shard_map/ppermute | solution.py:178
  51.3 17.8 %collective-permute-start.14 = (bf16[64,4224]{1,0:T(8,128)(2,1)S(1)}, bf16[64,4224]{1,0:T(8,128)(2,1)}, u32[]{:S(2)}, u32[]{:S(2)}) collective-permute-start(bf16[64,4224]{1,0:T(8,128)(2,1)S(1)} %collective-permute-done.12.refs_0_), channel_id=1, source_target_pairs={{0,1},{1,0},{2,3},{3,2},{4,5},{5,4},{6,7},{7,6},{8,9},{9,8},{10,11... | collective-permute-start | bytes 1622024 | tf_op jit(solution)/shard_map/ppermute | solution.py:178
  51.8 17.7 %collective-permute-start.15 = (bf16[64,4224]{1,0:T(8,128)(2,1)S(1)}, bf16[64,4224]{1,0:T(8,128)(2,1)}, u32[]{:S(2)}, u32[]{:S(2)}) collective-permute-start(bf16[64,4224]{1,0:T(8,128)(2,1)S(1)} %collective-permute-done.13.refs_1_), channel_id=1, source_target_pairs={{0,1},{1,0},{2,3},{3,2},{4,5},{5,4},{6,7},{7,6},{8,9},{9,8},{10,11... | collective-permute-start | bytes 1622024 | tf_op jit(solution)/shard_map/ppermute | solution.py:178
  68.4 18.9 %collective-permute-start.21 = (bf16[64,4096]{1,0:T(8,128)(2,1)}, bf16[64,4096]{1,0:T(8,128)(2,1)S(1)}, u32[]{:S(2)}, u32[]{:S(2)}) collective-permute-start(bf16[64,4096]{1,0:T(8,128)(2,1)} %get-tuple-element.24), channel_id=1, source_target_pairs={{0,1},{1,0},{2,3},{3,2},{4,5},{5,4},{6,7},{7,6},{8,9},{9,8},{10,11... | collective-permute-start | bytes 1572872 | tf_op jit(solution)/shard_map/ppermute | solution.py:181
  68.6 41.8 %collective-permute-start.4 = (bf16[64,4224]{1,0:T(8,128)(2,1)S(1)}, bf16[64,4224]{1,0:T(8,128)(2,1)S(1)}, u32[]{:S(2)}, u32[]{:S(2)}) collective-permute-start(bf16[64,4224]{1,0:T(8,128)(2,1)S(1)} %collective-permute-done.2.refs_0_), channel_id=1, source_target_pairs={{0,1},{1,0},{2,3},{3,2},{4,5},{5,4},{6,7},{7,6},{8,9},{9,8},{10,11... | collective-permute-start | bytes 1622024 | tf_op jit(solution)/shard_map/ppermute | solution.py:178
  69.0 41.4 %collective-permute-start.5 = (bf16[64,4224]{1,0:T(8,128)(2,1)S(1)}, bf16[64,4224]{1,0:T(8,128)(2,1)S(1)}, u32[]{:S(2)}, u32[]{:S(2)}) collective-permute-start(bf16[64,4224]{1,0:T(8,128)(2,1)S(1)} %collective-permute-done.3.refs_1_), channel_id=1, source_target_pairs={{0,1},{1,0},{2,3},{3,2},{4,5},{5,4},{6,7},{7,6},{8,9},{9,8},{10,11... | collective-permute-start | bytes 1622024 | tf_op jit(solution)/shard_map/ppermute | solution.py:178
  69.1 18.7 %collective-permute-start.9 = (bf16[64,4224]{1,0:T(8,128)(2,1)S(1)}, bf16[64,4224]{1,0:T(8,128)(2,1)S(1)}, u32[]{:S(2)}, u32[]{:S(2)}) collective-permute-start(bf16[64,4224]{1,0:T(8,128)(2,1)S(1)} %collective-permute-done.7.refs_0_), channel_id=1, source_target_pairs={{0,1},{1,0},{2,3},{3,2},{4,5},{5,4},{6,7},{7,6},{8,9},{9,8},{10,11... | collective-permute-start | bytes 1622024 | tf_op jit(solution)/shard_map/ppermute | solution.py:178
  69.5 20.0 %collective-permute-start.10 = (bf16[64,4224]{1,0:T(8,128)(2,1)S(1)}, bf16[64,4224]{1,0:T(8,128)(2,1)S(1)}, u32[]{:S(2)}, u32[]{:S(2)}) collective-permute-start(bf16[64,4224]{1,0:T(8,128)(2,1)S(1)} %copy-done.1), channel_id=1, source_target_pairs={{0,1},{1,0},{2,3},{3,2},{4,5},{5,4},{6,7},{7,6},{8,9},{9,8},{10,11... | collective-permute-start | bytes 1622024 | tf_op jit(solution)/shard_map/ppermute | solution.py:178
  87.3 20.7 %copy-start.4 = (bf16[128,4096]{1,0:T(8,128)(2,1)S(1)}, bf16[128,4096]{1,0:T(8,128)(2,1)}, u32[]{:S(2)}) copy-start(bf16[128,4096]{1,0:T(8,128)(2,1)} %get-tuple-element.21) | copy-start | bytes 3145732
  87.3 20.7 %collective-permute-start.16 = (bf16[128,4096]{1,0:T(8,128)(2,1)}, bf16[128,4096]{1,0:T(8,128)(2,1)S(1)}, u32[]{:S(2)}, u32[]{:S(2)}) collective-permute-start(bf16[128,4096]{1,0:T(8,128)(2,1)} %get-tuple-element.22), channel_id=1, source_target_pairs={{0,1},{1,0},{2,3},{3,2},{4,5},{5,4},{6,7},{7,6},{8,9},{9,8},{10,11... | collective-permute-start | bytes 3145736 | tf_op jit(solution)/shard_map/ppermute | solution.py:181
  87.9 20.0 %collective-permute-start.22 = (bf16[32,4096]{1,0:T(8,128)(2,1)S(1)}, bf16[32,4096]{1,0:T(8,128)(2,1)S(1)}, u32[]{:S(2)}, u32[]{:S(2)}) collective-permute-start(bf16[32,4096]{1,0:T(8,128)(2,1)S(1)} %get-tuple-element.31), channel_id=1, source_target_pairs={{0,4},{1,5},{4,8},{5,9},{8,12},{9,13},{12,14},{13,15},{14,10},{15,... | collective-permute-start | bytes 786440 | tf_op jit(solution)/shard_map/ppermute | solution.py:193
  89.5 18.4 %collective-permute-start.26 = (bf16[32,4096]{1,0:T(8,128)(2,1)S(1)}, bf16[32,4096]{1,0:T(8,128)(2,1)S(1)}, u32[]{:S(2)}, u32[]{:S(2)}) collective-permute-start(bf16[32,4096]{1,0:T(8,128)(2,1)S(1)} %get-tuple-element.32), channel_id=1, source_target_pairs={{0,2},{1,3},{4,0},{5,1},{8,4},{9,5},{12,8},{13,9},{14,12},{15,13},... | collective-permute-start | bytes 786440 | tf_op jit(solution)/shard_map/ppermute | solution.py:194
  107.8 21.5 %copy-start.5 = (bf16[128,4096]{1,0:T(8,128)(2,1)S(1)}, bf16[128,4096]{1,0:T(8,128)(2,1)}, u32[]{:S(2)}) copy-start(bf16[128,4096]{1,0:T(8,128)(2,1)} %get-tuple-element.19) | copy-start | bytes 3145732
  107.9 21.5 %collective-permute-start.11 = (bf16[128,4096]{1,0:T(8,128)(2,1)}, bf16[128,4096]{1,0:T(8,128)(2,1)S(1)}, u32[]{:S(2)}, u32[]{:S(2)}) collective-permute-start(bf16[128,4096]{1,0:T(8,128)(2,1)} %get-tuple-element.20), channel_id=1, source_target_pairs={{0,1},{1,0},{2,3},{3,2},{4,5},{5,4},{6,7},{7,6},{8,9},{9,8},{10,11... | collective-permute-start | bytes 3145736 | tf_op jit(solution)/shard_map/ppermute | solution.py:181
  108.3 21.0 %collective-permute-start.23 = (bf16[64,4096]{1,0:T(8,128)(2,1)S(1)}, bf16[64,4096]{1,0:T(8,128)(2,1)S(1)}, u32[]{:S(2)}, u32[]{:S(2)}) collective-permute-start(bf16[64,4096]{1,0:T(8,128)(2,1)S(1)} %get-tuple-element.29), channel_id=1, source_target_pairs={{0,4},{1,5},{4,8},{5,9},{8,12},{9,13},{12,14},{13,15},{14,10},{15,... | collective-permute-start | bytes 1572872 | tf_op jit(solution)/shard_map/ppermute | solution.py:201
  110.0 19.4 %collective-permute-start.27 = (bf16[64,4096]{1,0:T(8,128)(2,1)S(1)}, bf16[64,4096]{1,0:T(8,128)(2,1)S(1)}, u32[]{:S(2)}, u32[]{:S(2)}) collective-permute-start(bf16[64,4096]{1,0:T(8,128)(2,1)S(1)} %get-tuple-element.30), channel_id=1, source_target_pairs={{0,2},{1,3},{4,0},{5,1},{8,4},{9,5},{12,8},{13,9},{14,12},{15,13},... | collective-permute-start | bytes 1572872 | tf_op jit(solution)/shard_map/ppermute | solution.py:202
  110.4 21.5 %collective-permute-start = (bf16[64,4224]{1,0:T(8,128)(2,1)S(1)}, bf16[64,4224]{1,0:T(8,128)(2,1)S(1)}, u32[]{:S(2)}, u32[]{:S(2)}) collective-permute-start(bf16[64,4224]{1,0:T(8,128)(2,1)S(1)} %concatenate.3.refs_0_), channel_id=1, source_target_pairs={{0,1},{1,0},{2,3},{3,2},{4,5},{5,4},{6,7},{7,6},{8,9},{9,8},{10,11... | collective-permute-start | bytes 1622024 | tf_op jit(solution)/shard_map/ppermute | solution.py:178
  128.8 16.9 %collective-permute-start.6 = (bf16[128,4096]{1,0:T(8,128)(2,1)}, bf16[128,4096]{1,0:T(8,128)(2,1)S(1)}, u32[]{:S(2)}, u32[]{:S(2)}) collective-permute-start(bf16[128,4096]{1,0:T(8,128)(2,1)} %get-tuple-element.18), channel_id=1, source_target_pairs={{0,1},{1,0},{2,3},{3,2},{4,5},{5,4},{6,7},{7,6},{8,9},{9,8},{10,11... | collective-permute-start | bytes 3145736 | tf_op jit(solution)/shard_map/ppermute | solution.py:181
  129.9 15.9 %collective-permute-start.24 = (bf16[64,4096]{1,0:T(8,128)(2,1)S(1)}, bf16[64,4096]{1,0:T(8,128)(2,1)S(1)}, u32[]{:S(2)}, u32[]{:S(2)}) collective-permute-start(bf16[64,4096]{1,0:T(8,128)(2,1)S(1)} %get-tuple-element.27), channel_id=1, source_target_pairs={{0,4},{1,5},{4,8},{5,9},{8,12},{9,13},{12,14},{13,15},{14,10},{15,... | collective-permute-start | bytes 1572872 | tf_op jit(solution)/shard_map/ppermute | solution.py:201
  131.5 14.3 %collective-permute-start.28 = (bf16[64,4096]{1,0:T(8,128)(2,1)S(1)}, bf16[64,4096]{1,0:T(8,128)(2,1)S(1)}, u32[]{:S(2)}, u32[]{:S(2)}) collective-permute-start(bf16[64,4096]{1,0:T(8,128)(2,1)S(1)} %get-tuple-element.28), channel_id=1, source_target_pairs={{0,2},{1,3},{4,0},{5,1},{8,4},{9,5},{12,8},{13,9},{14,12},{15,13},... | collective-permute-start | bytes 1572872 | tf_op jit(solution)/shard_map/ppermute | solution.py:202
  145.6 2.7 %collective-permute-start.1 = (bf16[64,4096]{1,0:T(8,128)(2,1)S(1)}, bf16[64,4096]{1,0:T(8,128)(2,1)S(1)}, u32[]{:S(2)}, u32[]{:S(2)}) collective-permute-start(bf16[64,4096]{1,0:T(8,128)(2,1)S(1)} %get-tuple-element.16), channel_id=1, source_target_pairs={{0,1},{1,0},{2,3},{3,2},{4,5},{5,4},{6,7},{7,6},{8,9},{9,8},{10,11... | collective-permute-start | bytes 1572872 | tf_op jit(solution)/shard_map/ppermute | solution.py:181
  146.2 14.4 %collective-permute-start.29 = (bf16[64,4096]{1,0:T(8,128)(2,1)S(1)}, bf16[64,4096]{1,0:T(8,128)(2,1)S(1)}, u32[]{:S(2)}, u32[]{:S(2)}) collective-permute-start(bf16[64,4096]{1,0:T(8,128)(2,1)S(1)} %get-tuple-element.26), channel_id=1, source_target_pairs={{0,2},{1,3},{4,0},{5,1},{8,4},{9,5},{12,8},{13,9},{14,12},{15,13},... | collective-permute-start | bytes 1572872 | tf_op jit(solution)/shard_map/ppermute | solution.py:202
  146.7 14.0 %collective-permute-start.25 = (bf16[64,4096]{1,0:T(8,128)(2,1)S(1)}, bf16[64,4096]{1,0:T(8,128)(2,1)S(1)}, u32[]{:S(2)}, u32[]{:S(2)}) collective-permute-start(bf16[64,4096]{1,0:T(8,128)(2,1)S(1)} %get-tuple-element.25), channel_id=1, source_target_pairs={{0,4},{1,5},{4,8},{5,9},{8,12},{9,13},{12,14},{13,15},{14,10},{15,... | collective-permute-start | bytes 1572872 | tf_op jit(solution)/shard_map/ppermute | solution.py:201
  (8 other events, 57.6 us)

commit v4 on v3

--- a/solution.py
+++ b/solution.py
@@ -30,12 +30,40 @@
     return jnp.concatenate([tokens, high, low, blank], axis=1)
 
 
+def keep_kernel(gate_up, down, gate_up_here, down_here, sem):
+    copies = [
+        pltpu.make_async_copy(gate_up, gate_up_here, sem.at[0]),
+        pltpu.make_async_copy(down, down_here, sem.at[1]),
+    ]
+    for copy in copies:
+        copy.start()
+    for copy in copies:
+        copy.wait()
+
+
+def keep(gate_up_w, down_w):
+    anywhere, vmem = pl.BlockSpec(memory_space=pl.ANY), pl.BlockSpec(memory_space=pltpu.VMEM)
+    kept = pl.pallas_call(
+        keep_kernel,
+        in_specs=[anywhere] * 2,
+        out_specs=[vmem] * 2,
+        out_shape=[pltpu.VMEM(w.shape, w.dtype) for w in (gate_up_w, down_w)],
+        scratch_shapes=[pltpu.SemaphoreType.DMA((2,))],
+        compiler_params=pltpu.CompilerParams(vmem_limit_bytes=1 << 20),
+        cost_estimate=pl.CostEstimate(
+            flops=0, bytes_accessed=2 * (gate_up_w.size + down_w.size), transcendentals=0
+        ),
+        name="keep",
+    )(*(pltpu.with_memory_space_constraint(w, pltpu.HBM) for w in (gate_up_w, down_w)))
+    return kept
+
+
 def expert_kernel(sizes, *refs):
     count = len(sizes)
     xs = refs[:count]
     pick, gate_up_s, down_s, gate_up, down = refs[count : count + 5]
     outs = refs[count + 5 : count + 7]
-    x, gate_up_here, down_here, hidden, out, x_sem, gate_up_sem, down_sem, out_sem = refs[count + 7 :]
+    x, hidden, out, x_sem, out_sem = refs[count + 7 :]
     units, width = down.shape
 
     starts = [sum(sizes[:i]) for i in range(count)]
@@ -43,16 +71,6 @@
         pltpu.make_async_copy(ref, x.at[pl.ds(start, size)], x_sem.at[i])
         for i, (ref, start, size) in enumerate(zip(xs, starts, sizes))
     ]
-
-    def gate_up_copy(chunk, side):
-        columns = pl.ds(pl.multiple_of(side * units + chunk * UNIT_CHUNK, UNIT_CHUNK), UNIT_CHUNK)
-        return pltpu.make_async_copy(
-            gate_up.at[:, columns], gate_up_here.at[:, columns], gate_up_sem.at[chunk, side]
-        )
-
-    def down_copy(chunk):
-        columns = pl.ds(pl.multiple_of(chunk * WIDTH_CHUNK, WIDTH_CHUNK), WIDTH_CHUNK)
-        return pltpu.make_async_copy(down.at[:, columns], down_here.at[:, columns], down_sem.at[chunk])
 
     def out_copies(chunk):
         columns = pl.ds(pl.multiple_of(chunk * WIDTH_CHUNK, WIDTH_CHUNK), WIDTH_CHUNK)
@@ -69,11 +87,6 @@
 
     for copy in x_copies:
         copy.start()
-    for chunk in range(units // UNIT_CHUNK):
-        gate_up_copy(chunk, 0).start()
-        gate_up_copy(chunk, 1).start()
-    for chunk in range(width // WIDTH_CHUNK):
-        down_copy(chunk).start()
     for copy in x_copies:
         copy.wait()
 
@@ -83,9 +96,8 @@
     def unit_step(chunk, carry):
         sides = []
         for side in range(2):
-            gate_up_copy(chunk, side).wait()
             columns = pl.ds(pl.multiple_of(side * units + chunk * UNIT_CHUNK, UNIT_CHUNK), UNIT_CHUNK)
-            part = jnp.dot(x[:, :width], gate_up_here[:, columns], preferred_element_type=jnp.float32)
+            part = jnp.dot(x[:, :width], gate_up[:, columns], preferred_element_type=jnp.float32)
             sides.append(part * gate_up_s[:, columns])
         here = pl.ds(pl.multiple_of(chunk * UNIT_CHUNK, UNIT_CHUNK), UNIT_CHUNK)
         hidden[:, here] = (jax.nn.silu(sides[0]) * sides[1]).astype(jnp.bfloat16)
@@ -94,9 +106,8 @@
     lax.fori_loop(0, units // UNIT_CHUNK, unit_step, 0)
 
     def width_step(chunk, carry):
-        down_copy(chunk).wait()
         columns = pl.ds(pl.multiple_of(chunk * WIDTH_CHUNK, WIDTH_CHUNK), WIDTH_CHUNK)
-        part = jnp.dot(hidden[...], down_here[:, columns], preferred_element_type=jnp.float32)
+        part = jnp.dot(hidden[...], down[:, columns], preferred_element_type=jnp.float32)
         out[:, columns] = (part * down_s[:, columns] * weight).astype(jnp.bfloat16)
         for copy in out_copies(chunk):
             copy.start()
@@ -116,27 +127,31 @@
     out_rows = [sum(sizes[:split]), sum(sizes[split:])]
     anywhere, vmem = pl.BlockSpec(memory_space=pl.ANY), pl.BlockSpec(memory_space=pltpu.VMEM)
     flops = 2 * rows * width * (units2 + units)
-    moved = 2 * width * (units2 + units) + 4 * rows * width
     return pl.pallas_call(
         functools.partial(expert_kernel, sizes),
-        in_specs=[anywhere] * len(blocks) + [vmem] * 3 + [anywhere] * 2,
+        in_specs=[anywhere] * len(blocks) + [vmem] * 5,
         out_specs=[anywhere] * 2,
         out_shape=[jax.ShapeDtypeStruct((size, width), jnp.bfloat16) for size in out_rows],
         scratch_shapes=[
             pltpu.VMEM((rows, packed_width), jnp.bfloat16),
-            pltpu.VMEM((width, units2), jnp.bfloat16),
-            pltpu.VMEM((units, width), jnp.bfloat16),
             pltpu.VMEM((rows, units), jnp.bfloat16),
             pltpu.VMEM((rows, width), jnp.bfloat16),
             pltpu.SemaphoreType.DMA((len(blocks),)),
-            pltpu.SemaphoreType.DMA((units // UNIT_CHUNK, 2)),
-            pltpu.SemaphoreType.DMA((width // WIDTH_CHUNK,)),
             pltpu.SemaphoreType.DMA((width // WIDTH_CHUNK, 2)),
         ],
-        compiler_params=pltpu.CompilerParams(vmem_limit_bytes=52 << 20),
-        cost_estimate=pl.CostEstimate(flops=flops, bytes_accessed=moved, transcendentals=rows * units),
+        compiler_params=pltpu.CompilerParams(vmem_limit_bytes=16 << 20),
+        cost_estimate=pl.CostEstimate(
+            flops=2 * flops, bytes_accessed=4 * rows * width, transcendentals=rows * units
+        ),
         name="expert",
-    )(*blocks, pick, gate_up_s, down_s, gate_up_w, down_w)
+    )(
+        *blocks,
+        pick,
+        gate_up_s,
+        down_s,
+        pltpu.with_memory_space_constraint(gate_up_w, pltpu.VMEM),
+        pltpu.with_memory_space_constraint(down_w, pltpu.VMEM),
+    )
 
 
 def add(*terms):
@@ -144,6 +159,10 @@
     for term in terms[1:]:
         total = total + term.astype(jnp.float32)
     return total.astype(jnp.bfloat16)
+
+
+def after(value, *others):
+    return lax.optimization_barrier((value, *others))[0]
 
 
 def body(tokens, routes, gate_num, gate_up_q, gate_up_scale, down_q, down_scale):
@@ -169,7 +188,8 @@
     lane = jnp.arange(LANES, dtype=jnp.int32)
     pick = jnp.where(lane == expert, 256.0, jnp.where(lane == devices + expert, 1.0, 0.0))
     pick = pick.astype(jnp.float32)[None, :]
-    weights = (pick, gate_up_q[0], gate_up_scale, down_q[0], down_scale)
+    gate_up_w, down_w = keep(gate_up_q[0], down_q[0])
+    weights = (pick, gate_up_w, gate_up_scale, down_w, down_scale)
 
     packed = pack(tokens, routes, gate_num, devices)
     mine, theirs = {}, {}
@@ -183,11 +203,18 @@
     from_below, from_above = packed, packed
     run(0, [packed])
     for distance in range(1, reach):
+        if distance > 1:
+            from_below = after(from_below, mine[distance - 2])
+            from_above = after(from_above, mine[distance - 2])
         from_below = send(from_below, perm=upward)
         from_above = send(from_above, perm=downward)
         run(distance, [from_below, from_above])
+    from_below = after(from_below, mine[reach - 2])
+    from_above = after(from_above, mine[reach - 2])
     last_below = send(from_below[:half], perm=upward)
     last_above = send(from_above[half:], perm=downward)
+    last_below = after(last_below, mine[reach - 1])
+    last_above = after(last_above, mine[reach - 1])
     run(reach, [last_below, last_above])
 
     to_above = send(add(mine[reach][:half], theirs[reach][:half]), perm=upward)

time: 162 us -> 131 us (0.81)
  Pallas kernels: 79 us -> 39.9 us
  waiting for transfers between devices: 54.2 us -> 66.3 us
  local copies, waits for them, and re-layouts: 4.66 us -> 1.28 us
    pallas_call x5, Pallas kernels: 79 us -> 33.5 us  [expert_part(): pl.pallas_call(functools.partial(expert_kernel, sizes), in_specs=[anywher...]
    ppermute x3, waiting for transfers between devices: 0.17 us -> 28.8 us  [body(): to_above = send(above, perm=upward)]
    ppermute x3, waiting for transfers between devices: 34.1 us -> 5.82 us  [body(): from_below = send(from_below, perm=upward)]
    ppermute x3, waiting for transfers between devices: 0.01 us -> 17.7 us  [body(): from_above = send(from_above, perm=downward)]
    ppermute x3, waiting for transfers between devices: 12.3 us -> 3.51 us  [body(): to_below = send(below, perm=downward)]
    pallas_call x0 -> x1, Pallas kernels: none -> 6.38 us  [keep(): pl.pallas_call(keep_kernel, in_specs=[anywhere] * 2, out_specs=[vmem] * 2...]
    ppermute x1, waiting for transfers between devices: 0.01 us -> 6.31 us  [body(): to_above = send(add(mine[reach][:half], theirs[reach][:half]), perm=upward)]
    ppermute x1, waiting for transfers between devices: 4.35 us -> 0.01 us  [body(): last_below = send(from_below[:half], perm=upward)]
  transfers between devices with their start and end apart: 30 -> 30, of which waited for: 8 -> 15; matrix products, arithmetic and copies ran while one was open for 1% -> 1% of each run, Pallas kernels for 49% -> 27%
where the time goes in v4:
time: 131 us
  waiting for transfers between devices  66.3 us (51%)
  Pallas kernels  39.9 us (30%)
  starting transfers between devices  19.8 us (15%)
  other arithmetic  3.27 us (2%)
    pallas_call x5, Pallas kernels, expert_part(): pl.pallas_call(functools.partial(expert_kernel, sizes), in_specs=[anywher...  33.5 us
    ppermute x3, waiting for transfers between devices, body(): to_above = send(above, perm=upward)  28.8 us
    ppermute x3, waiting for transfers between devices, body(): from_above = send(from_above, perm=downward)  17.7 us
    pallas_call x1, Pallas kernels, keep(): pl.pallas_call(keep_kernel, in_specs=[anywhere] * 2, out_specs=[vmem] * 2...  6.38 us
    ppermute x1, waiting for transfers between devices, body(): to_above = send(add(mine[reach][:half], theirs[reach][:half]), perm=upward)  6.31 us
    ppermute x3, starting transfers between devices, body(): from_below = send(from_below, perm=upward)  6.12 us
    ppermute x3, waiting for transfers between devices, body(): from_below = send(from_below, perm=upward)  5.82 us
    ppermute x3, starting transfers between devices, body(): to_above = send(above, perm=upward)  4.51 us
  transfers between devices with their start and end apart: 30, of which 15 were waited for; matrix products, arithmetic and copies ran while one was open for 1% of the time, Pallas kernels for 27%

profile of v4, /device:TPU:0, one launch (start us, length us, event | category | flops | bytes accessed | tf_op | source)
XLA Modules:
  0.0 130.7 jit_solution(17151077279726647805)
XLA Ops:
  0.9 1.1 concatenate.3.refs_0_
  2.0 3.1 %collective-permute-start.2 = (bf16[64,4224]{1,0:T(8,128)(2,1)S(1)}, bf16[64,4224]{1,0:T(8,128)(2,1)S(1)}, u32[]{:S(2)}, u32[]{:S(2)}) collective-permute-start(bf16[64,4224]{1,0:T(8,128)(2,1)S(1)} %concatenate.3.refs_0_), channel_id=1, source_target_pairs={{0,4},{1,5},{4,8},{5,9},{8,12},{9,13},{12,14},{13,15},{14,10},{15,... | collective-permute-start | bytes 1622024 | tf_op jit(solution)/shard_map/ppermute | solution.py:209
  5.1 6.4 %keep.1 = (bf16[4096,1536]{1,0:T(8,128)(2,1)S(1)}, bf16[768,4096]{1,0:T(8,128)(2,1)S(1)}) custom-call(bf16[4096,1536]{1,0:T(8,128)(2,1)} %bitcast.2, bf16[768,4096]{1,0:T(8,128)(2,1)} %bitcast.3), custom_call_target="tpu_custom_call" | custom-call | bytes 18874368 | tf_op jit(solution)/shard_map/keep/pallas_call | solution.py:46
  11.5 5.8 %collective-permute-done.2.refs_0_ = bf16[64,4224]{1,0:T(8,128)(2,1)S(1)} collective-permute-done((bf16[64,4224]{1,0:T(8,128)(2,1)S(1)}, bf16[64,4224]{1,0:T(8,128)(2,1)S(1)}, u32[]{:S(2)}, u32[]{:S(2)}) %collective-permute-start.2) | collective-permute-done | bytes 540704 | tf_op jit(solution)/shard_map/ppermute | solution.py:209
  17.3 1.5 %collective-permute-done.3.refs_1_ = bf16[64,4224]{1,0:T(8,128)(2,1)S(1)} collective-permute-done((bf16[64,4224]{1,0:T(8,128)(2,1)S(1)}, bf16[64,4224]{1,0:T(8,128)(2,1)S(1)}, u32[]{:S(2)}, u32[]{:S(2)}) %collective-permute-start.3) | collective-permute-done | bytes 540704 | tf_op jit(solution)/shard_map/ppermute | solution.py:210
  18.9 5.1 %expert.5 = (bf16[64,4096]{1,0:T(8,128)(2,1)S(1)}, bf16[64,4096]{1,0:T(8,128)(2,1)S(1)}) custom-call(bf16[64,4224]{1,0:T(8,128)(2,1)S(1)} %concatenate.3.refs_0_, bf16[64,4224]{1,0:T(8,128)(2,1)S(1)} %collective-permute-done.refs_1_, f32[1,128]{1,0:T(1,128)S(1)} %compare_select_fusion.1.refs_2_.refs_4_, f32[1,1536]{1,0:T(1,128)S(1)} %copy-done.1, ...), custom_call_target="tpu_custom_call" | custom-call | flops 4831838208 | bytes 2097152 | tf_op jit(solution)/shard_map/expert/pallas_call | solution.py:130
  24.7 1.3 %collective-permute-start.7 = (bf16[64,4224]{1,0:T(8,128)(2,1)S(1)}, bf16[64,4224]{1,0:T(8,128)(2,1)S(1)}, u32[]{:S(2)}, u32[]{:S(2)}) collective-permute-start(bf16[64,4224]{1,0:T(8,128)(2,1)S(1)} %collective-permute-done.2.refs_0_), channel_id=1, source_target_pairs={{0,4},{1,5},{4,8},{5,9},{8,12},{9,13},{12,14},{13,15},{14,10},{15,... | collective-permute-start | bytes 1622024 | tf_op jit(solution)/shard_map/ppermute | solution.py:209
  26.1 7.8 %expert.6 = (bf16[128,4096]{1,0:T(8,128)(2,1)S(1)}, bf16[128,4096]{1,0:T(8,128)(2,1)S(1)}) custom-call(bf16[64,4224]{1,0:T(8,128)(2,1)S(1)} %collective-permute-done.2.refs_0_, bf16[64,4224]{1,0:T(8,128)(2,1)S(1)} %collective-permute-done.3.refs_1_, bf16[64,4224]{1,0:T(8,128)(2,1)S(1)} %collective-permute-done.4.refs_2_, ...), custom_call_target="tpu_custom_call" | custom-call | flops 9663676416 | bytes 4194304 | tf_op jit(solution)/shard_map/expert/pallas_call | solution.py:130
  33.9 4.9 %collective-permute-done.8.refs_1_ = bf16[64,4224]{1,0:T(8,128)(2,1)S(1)} collective-permute-done((bf16[64,4224]{1,0:T(8,128)(2,1)S(1)}, bf16[64,4224]{1,0:T(8,128)(2,1)S(1)}, u32[]{:S(2)}, u32[]{:S(2)}) %collective-permute-start.8) | collective-permute-done | bytes 540704 | tf_op jit(solution)/shard_map/ppermute | solution.py:210
  39.0 1.7 %collective-permute-start.12 = (bf16[64,4224]{1,0:T(8,128)(2,1)S(1)}, bf16[64,4224]{1,0:T(8,128)(2,1)S(1)}, u32[]{:S(2)}, u32[]{:S(2)}) collective-permute-start(bf16[64,4224]{1,0:T(8,128)(2,1)S(1)} %collective-permute-done.7.refs_0_), channel_id=1, source_target_pairs={{0,4},{1,5},{4,8},{5,9},{8,12},{9,13},{12,14},{13,15},{14,10},{15,... | collective-permute-start | bytes 1622024 | tf_op jit(solution)/shard_map/ppermute | solution.py:209
  41.2 11.4 %collective-permute-done.13.refs_1_ = bf16[64,4224]{1,0:T(8,128)(2,1)S(1)} collective-permute-done((bf16[64,4224]{1,0:T(8,128)(2,1)S(1)}, bf16[64,4224]{1,0:T(8,128)(2,1)S(1)}, u32[]{:S(2)}, u32[]{:S(2)}) %collective-permute-start.13) | collective-permute-done | bytes 540704 | tf_op jit(solution)/shard_map/ppermute | solution.py:210
  53.1 7.8 %expert.7 = (bf16[128,4096]{1,0:T(8,128)(2,1)S(1)}, bf16[128,4096]{1,0:T(8,128)(2,1)S(1)}) custom-call(bf16[64,4224]{1,0:T(8,128)(2,1)S(1)} %collective-permute-done.7.refs_0_, bf16[64,4224]{1,0:T(8,128)(2,1)S(1)} %collective-permute-done.8.refs_1_, bf16[64,4224]{1,0:T(8,128)(2,1)S(1)} %collective-permute-done.9.refs_2_, ...), custom_call_target="tpu_custom_call" | custom-call | flops 9663676416 | bytes 4194304 | tf_op jit(solution)/shard_map/expert/pallas_call | solution.py:130
  60.9 0.9 collective-permute-start.18
  61.8 1.3 collective-permute-start.17
  63.1 7.8 %expert.8 = (bf16[128,4096]{1,0:T(8,128)(2,1)S(1)}, bf16[128,4096]{1,0:T(8,128)(2,1)S(1)}) custom-call(bf16[64,4224]{1,0:T(8,128)(2,1)S(1)} %collective-permute-done.12.refs_0_, bf16[64,4224]{1,0:T(8,128)(2,1)S(1)} %collective-permute-done.13.refs_1_, bf16[64,4224]{1,0:T(8,128)(2,1)S(1)} %collective-permute-done.14.refs_2_, ...), custom_call_target="tpu_custom_call" | custom-call | flops 9663676416 | bytes 4194304 | tf_op jit(solution)/shard_map/expert/pallas_call | solution.py:130
  71.5 1.0 collective-permute-done.20.refs_3_
  72.9 5.1 %expert.9 = (bf16[64,4096]{1,0:T(8,128)(2,1)S(1)}, bf16[64,4096]{1,0:T(8,128)(2,1)S(1)}) custom-call(bf16[32,4224]{1,0:T(8,128)(2,1)S(1)} %collective-permute-done.17.refs_0_, bf16[32,4224]{1,0:T(8,128)(2,1)S(1)} %collective-permute-done.18.refs_1_, bf16[32,4224]{1,0:T(8,128)(2,1)S(1)} %collective-permute-done.19.refs_2_, ...), custom_call_target="tpu_custom_call" | custom-call | flops 4831838208 | bytes 2097152 | tf_op jit(solution)/shard_map/expert/pallas_call | solution.py:130
  78.6 1.4 %collective-permute-done.21 = bf16[64,4096]{1,0:T(8,128)(2,1)S(1)} collective-permute-done((bf16[64,4096]{1,0:T(8,128)(2,1)S(1)}, bf16[64,4096]{1,0:T(8,128)(2,1)S(1)}, u32[]{:S(2)}, u32[]{:S(2)}) %collective-permute-start.21) | collective-permute-done | bytes 524320 | tf_op jit(solution)/shard_map/ppermute | solution.py:201
  80.1 1.6 %collective-permute-start.22 = (bf16[32,4096]{1,0:T(8,128)(2,1)S(1)}, bf16[32,4096]{1,0:T(8,128)(2,1)S(1)}, u32[]{:S(2)}, u32[]{:S(2)}) collective-permute-start(bf16[32,4096]{1,0:T(8,128)(2,1)S(1)} %get-tuple-element.51), channel_id=1, source_target_pairs={{0,4},{1,5},{4,8},{5,9},{8,12},{9,13},{12,14},{13,15},{14,10},{15,... | collective-permute-start | bytes 786440 | tf_op jit(solution)/shard_map/ppermute | solution.py:220
  82.2 6.3 %collective-permute-done.22 = bf16[32,4096]{1,0:T(8,128)(2,1)S(1)} collective-permute-done((bf16[32,4096]{1,0:T(8,128)(2,1)S(1)}, bf16[32,4096]{1,0:T(8,128)(2,1)S(1)}, u32[]{:S(2)}, u32[]{:S(2)}) %collective-permute-start.22) | collective-permute-done | bytes 262176 | tf_op jit(solution)/shard_map/ppermute | solution.py:220
  88.5 1.3 collective-permute-done.26
  90.1 1.6 %collective-permute-start.23 = (bf16[64,4096]{1,0:T(8,128)(2,1)S(1)}, bf16[64,4096]{1,0:T(8,128)(2,1)S(1)}, u32[]{:S(2)}, u32[]{:S(2)}) collective-permute-start(bf16[64,4096]{1,0:T(8,128)(2,1)S(1)} %get-tuple-element.49), channel_id=1, source_target_pairs={{0,4},{1,5},{4,8},{5,9},{8,12},{9,13},{12,14},{13,15},{14,10},{15,... | collective-permute-start | bytes 1572872 | tf_op jit(solution)/shard_map/ppermute | solution.py:228
  92.2 10.8 %collective-permute-done.23 = bf16[64,4096]{1,0:T(8,128)(2,1)S(1)} collective-permute-done((bf16[64,4096]{1,0:T(8,128)(2,1)S(1)}, bf16[64,4096]{1,0:T(8,128)(2,1)S(1)}, u32[]{:S(2)}, u32[]{:S(2)}) %collective-permute-start.23) | collective-permute-done | bytes 524320 | tf_op jit(solution)/shard_map/ppermute | solution.py:228
  103.0 1.3 collective-permute-done.27
  104.8 1.6 %collective-permute-start.24 = (bf16[64,4096]{1,0:T(8,128)(2,1)S(1)}, bf16[64,4096]{1,0:T(8,128)(2,1)S(1)}, u32[]{:S(2)}, u32[]{:S(2)}) collective-permute-start(bf16[64,4096]{1,0:T(8,128)(2,1)S(1)} %get-tuple-element.47), channel_id=1, source_target_pairs={{0,4},{1,5},{4,8},{5,9},{8,12},{9,13},{12,14},{13,15},{14,10},{15,... | collective-permute-start | bytes 1572872 | tf_op jit(solution)/shard_map/ppermute | solution.py:228
  106.9 9.6 %collective-permute-done.24 = bf16[64,4096]{1,0:T(8,128)(2,1)S(1)} collective-permute-done((bf16[64,4096]{1,0:T(8,128)(2,1)S(1)}, bf16[64,4096]{1,0:T(8,128)(2,1)S(1)}, u32[]{:S(2)}, u32[]{:S(2)}) %collective-permute-start.24) | collective-permute-done | bytes 524320 | tf_op jit(solution)/shard_map/ppermute | solution.py:228
  116.5 1.3 collective-permute-done.28
  118.2 1.3 collective-permute-start.25
  119.5 0.8 collective-permute-start.29
  120.3 8.4 %collective-permute-done.25 = bf16[64,4096]{1,0:T(8,128)(2,1)S(1)} collective-permute-done((bf16[64,4096]{1,0:T(8,128)(2,1)S(1)}, bf16[64,4096]{1,0:T(8,128)(2,1)S(1)}, u32[]{:S(2)}, u32[]{:S(2)}) %collective-permute-start.25) | collective-permute-done | bytes 524320 | tf_op jit(solution)/shard_map/ppermute | solution.py:228
  128.7 1.0 collective-permute-done.29
  129.7 1.1 add_convert_fusion
  (51 shorter events, 7.4 us)
Async XLA Ops:
  0.0 18.9 %copy-start.1 = (f32[1,1536]{1,0:T(1,128)S(1)}, f32[1,1536]{1,0:T(1,128)}, u32[]{:S(2)}) copy-start(f32[1,1536]{1,0:T(1,128)} %refs_5_.7) | copy-start | bytes 18436
  0.0 18.9 %copy-start = (f32[1,4096]{1,0:T(1,128)S(1)}, f32[1,4096]{1,0:T(1,128)}, u32[]{:S(2)}) copy-start(f32[1,4096]{1,0:T(1,128)} %refs_6_.7) | copy-start | bytes 49156
  2.0 15.3 %collective-permute-start.2 = (bf16[64,4224]{1,0:T(8,128)(2,1)S(1)}, bf16[64,4224]{1,0:T(8,128)(2,1)S(1)}, u32[]{:S(2)}, u32[]{:S(2)}) collective-permute-start(bf16[64,4224]{1,0:T(8,128)(2,1)S(1)} %concatenate.3.refs_0_), channel_id=1, source_target_pairs={{0,4},{1,5},{4,8},{5,9},{8,12},{9,13},{12,14},{13,15},{14,10},{15,... | collective-permute-start | bytes 1622024 | tf_op jit(solution)/shard_map/ppermute | solution.py:209
  5.1 13.7 %collective-permute-start.3 = (bf16[64,4224]{1,0:T(8,128)(2,1)S(1)}, bf16[64,4224]{1,0:T(8,128)(2,1)S(1)}, u32[]{:S(2)}, u32[]{:S(2)}) collective-permute-start(bf16[64,4224]{1,0:T(8,128)(2,1)S(1)} %concatenate.3.refs_0_), channel_id=1, source_target_pairs={{0,2},{1,3},{4,0},{5,1},{8,4},{9,5},{12,8},{13,9},{14,12},{15,13},... | collective-permute-start | bytes 1622024 | tf_op jit(solution)/shard_map/ppermute | solution.py:210
  5.1 13.7 %collective-permute-start = (bf16[64,4224]{1,0:T(8,128)(2,1)S(1)}, bf16[64,4224]{1,0:T(8,128)(2,1)S(1)}, u32[]{:S(2)}, u32[]{:S(2)}) collective-permute-start(bf16[64,4224]{1,0:T(8,128)(2,1)S(1)} %concatenate.3.refs_0_), channel_id=1, source_target_pairs={{0,1},{1,0},{2,3},{3,2},{4,5},{5,4},{6,7},{7,6},{8,9},{9,8},{10,11... | collective-permute-start | bytes 1622024 | tf_op jit(solution)/shard_map/ppermute | solution.py:198
  17.3 8.7 %collective-permute-start.4 = (bf16[64,4224]{1,0:T(8,128)(2,1)S(1)}, bf16[64,4224]{1,0:T(8,128)(2,1)S(1)}, u32[]{:S(2)}, u32[]{:S(2)}) collective-permute-start(bf16[64,4224]{1,0:T(8,128)(2,1)S(1)} %collective-permute-done.2.refs_0_), channel_id=1, source_target_pairs={{0,1},{1,0},{2,3},{3,2},{4,5},{5,4},{6,7},{7,6},{8,9},{9,8},{10,11... | collective-permute-start | bytes 1622024 | tf_op jit(solution)/shard_map/ppermute | solution.py:198
  18.8 7.2 %collective-permute-start.5 = (bf16[64,4224]{1,0:T(8,128)(2,1)S(1)}, bf16[64,4224]{1,0:T(8,128)(2,1)S(1)}, u32[]{:S(2)}, u32[]{:S(2)}) collective-permute-start(bf16[64,4224]{1,0:T(8,128)(2,1)S(1)} %collective-permute-done.3.refs_1_), channel_id=1, source_target_pairs={{0,1},{1,0},{2,3},{3,2},{4,5},{5,4},{6,7},{7,6},{8,9},{9,8},{10,11... | collective-permute-start | bytes 1622024 | tf_op jit(solution)/shard_map/ppermute | solution.py:198
  24.0 14.7 %collective-permute-start.8 = (bf16[64,4224]{1,0:T(8,128)(2,1)S(1)}, bf16[64,4224]{1,0:T(8,128)(2,1)S(1)}, u32[]{:S(2)}, u32[]{:S(2)}) collective-permute-start(bf16[64,4224]{1,0:T(8,128)(2,1)S(1)} %collective-permute-done.3.refs_1_), channel_id=1, source_target_pairs={{0,2},{1,3},{4,0},{5,1},{8,4},{9,5},{12,8},{13,9},{14,12},{15,13},... | collective-permute-start | bytes 1622024 | tf_op jit(solution)/shard_map/ppermute | solution.py:210
  24.7 14.2 %collective-permute-start.7 = (bf16[64,4224]{1,0:T(8,128)(2,1)S(1)}, bf16[64,4224]{1,0:T(8,128)(2,1)S(1)}, u32[]{:S(2)}, u32[]{:S(2)}) collective-permute-start(bf16[64,4224]{1,0:T(8,128)(2,1)S(1)} %collective-permute-done.2.refs_0_), channel_id=1, source_target_pairs={{0,4},{1,5},{4,8},{5,9},{8,12},{9,13},{12,14},{13,15},{14,10},{15,... | collective-permute-start | bytes 1622024 | tf_op jit(solution)/shard_map/ppermute | solution.py:209
  38.7 13.9 %collective-permute-start.13 = (bf16[64,4224]{1,0:T(8,128)(2,1)S(1)}, bf16[64,4224]{1,0:T(8,128)(2,1)S(1)}, u32[]{:S(2)}, u32[]{:S(2)}) collective-permute-start(bf16[64,4224]{1,0:T(8,128)(2,1)S(1)} %collective-permute-done.8.refs_1_), channel_id=1, source_target_pairs={{0,2},{1,3},{4,0},{5,1},{8,4},{9,5},{12,8},{13,9},{14,12},{15,13},... | collective-permute-start | bytes 1622024 | tf_op jit(solution)/shard_map/ppermute | solution.py:210
  39.0 13.6 %collective-permute-start.12 = (bf16[64,4224]{1,0:T(8,128)(2,1)S(1)}, bf16[64,4224]{1,0:T(8,128)(2,1)S(1)}, u32[]{:S(2)}, u32[]{:S(2)}) collective-permute-start(bf16[64,4224]{1,0:T(8,128)(2,1)S(1)} %collective-permute-done.7.refs_0_), channel_id=1, source_target_pairs={{0,4},{1,5},{4,8},{5,9},{8,12},{9,13},{12,14},{13,15},{14,10},{15,... | collective-permute-start | bytes 1622024 | tf_op jit(solution)/shard_map/ppermute | solution.py:209
  40.7 12.4 %collective-permute-start.10 = (bf16[64,4224]{1,0:T(8,128)(2,1)S(1)}, bf16[64,4224]{1,0:T(8,128)(2,1)S(1)}, u32[]{:S(2)}, u32[]{:S(2)}) collective-permute-start(bf16[64,4224]{1,0:T(8,128)(2,1)S(1)} %collective-permute-done.8.refs_1_), channel_id=1, source_target_pairs={{0,1},{1,0},{2,3},{3,2},{4,5},{5,4},{6,7},{7,6},{8,9},{9,8},{10,11... | collective-permute-start | bytes 1622024 | tf_op jit(solution)/shard_map/ppermute | solution.py:198
  40.7 12.4 %collective-permute-start.9 = (bf16[64,4224]{1,0:T(8,128)(2,1)S(1)}, bf16[64,4224]{1,0:T(8,128)(2,1)S(1)}, u32[]{:S(2)}, u32[]{:S(2)}) collective-permute-start(bf16[64,4224]{1,0:T(8,128)(2,1)S(1)} %collective-permute-done.7.refs_0_), channel_id=1, source_target_pairs={{0,1},{1,0},{2,3},{3,2},{4,5},{5,4},{6,7},{7,6},{8,9},{9,8},{10,11... | collective-permute-start | bytes 1622024 | tf_op jit(solution)/shard_map/ppermute | solution.py:198
  52.6 10.5 %collective-permute-start.15 = (bf16[64,4224]{1,0:T(8,128)(2,1)S(1)}, bf16[64,4224]{1,0:T(8,128)(2,1)S(1)}, u32[]{:S(2)}, u32[]{:S(2)}) collective-permute-start(bf16[64,4224]{1,0:T(8,128)(2,1)S(1)} %collective-permute-done.13.refs_1_), channel_id=1, source_target_pairs={{0,1},{1,0},{2,3},{3,2},{4,5},{5,4},{6,7},{7,6},{8,9},{9,8},{10,11... | collective-permute-start | bytes 1622024 | tf_op jit(solution)/shard_map/ppermute | solution.py:198
  52.6 10.5 %collective-permute-start.14 = (bf16[64,4224]{1,0:T(8,128)(2,1)S(1)}, bf16[64,4224]{1,0:T(8,128)(2,1)S(1)}, u32[]{:S(2)}, u32[]{:S(2)}) collective-permute-start(bf16[64,4224]{1,0:T(8,128)(2,1)S(1)} %collective-permute-done.12.refs_0_), channel_id=1, source_target_pairs={{0,1},{1,0},{2,3},{3,2},{4,5},{5,4},{6,7},{7,6},{8,9},{9,8},{10,11... | collective-permute-start | bytes 1622024 | tf_op jit(solution)/shard_map/ppermute | solution.py:198
  60.9 9.9 %collective-permute-start.18 = (bf16[32,4224]{1,0:T(8,128)(2,1)S(1)}, bf16[32,4224]{1,0:T(8,128)(2,1)S(1)}, u32[]{:S(2)}, u32[]{:S(2)}) collective-permute-start(bf16[32,4224]{1,0:T(8,128)(2,1)S(1)} %slice.61), channel_id=1, source_target_pairs={{0,2},{1,3},{4,0},{5,1},{8,4},{9,5},{12,8},{13,9},{14,12},{15,13},... | collective-permute-start | bytes 811016 | tf_op jit(solution)/shard_map/ppermute | solution.py:215
  61.8 9.1 %collective-permute-start.17 = (bf16[32,4224]{1,0:T(8,128)(2,1)S(1)}, bf16[32,4224]{1,0:T(8,128)(2,1)S(1)}, u32[]{:S(2)}, u32[]{:S(2)}) collective-permute-start(bf16[32,4224]{1,0:T(8,128)(2,1)S(1)} %slice.60), channel_id=1, source_target_pairs={{0,4},{1,5},{4,8},{5,9},{8,12},{9,13},{12,14},{13,15},{14,10},{15,... | collective-permute-start | bytes 811016 | tf_op jit(solution)/shard_map/ppermute | solution.py:214
  70.9 1.6 %collective-permute-start.20 = (bf16[32,4224]{1,0:T(8,128)(2,1)S(1)}, bf16[32,4224]{1,0:T(8,128)(2,1)S(1)}, u32[]{:S(2)}, u32[]{:S(2)}) collective-permute-start(bf16[32,4224]{1,0:T(8,128)(2,1)S(1)} %collective-permute-done.18.refs_1_), channel_id=1, source_target_pairs={{0,1},{1,0},{2,3},{3,2},{4,5},{5,4},{6,7},{7,6},{8,9},{9,8},{10,11... | collective-permute-start | bytes 811016 | tf_op jit(solution)/shard_map/ppermute | solution.py:198
  71.0 1.9 %collective-permute-start.19 = (bf16[32,4224]{1,0:T(8,128)(2,1)S(1)}, bf16[32,4224]{1,0:T(8,128)(2,1)S(1)}, u32[]{:S(2)}, u32[]{:S(2)}) collective-permute-start(bf16[32,4224]{1,0:T(8,128)(2,1)S(1)} %collective-permute-done.17.refs_0_), channel_id=1, source_target_pairs={{0,1},{1,0},{2,3},{3,2},{4,5},{5,4},{6,7},{7,6},{8,9},{9,8},{10,11... | collective-permute-start | bytes 811016 | tf_op jit(solution)/shard_map/ppermute | solution.py:198
  78.0 2.0 %collective-permute-start.21 = (bf16[64,4096]{1,0:T(8,128)(2,1)S(1)}, bf16[64,4096]{1,0:T(8,128)(2,1)S(1)}, u32[]{:S(2)}, u32[]{:S(2)}) collective-permute-start(bf16[64,4096]{1,0:T(8,128)(2,1)S(1)} %get-tuple-element.44), channel_id=1, source_target_pairs={{0,1},{1,0},{2,3},{3,2},{4,5},{5,4},{6,7},{7,6},{8,9},{9,8},{10,11... | collective-permute-start | bytes 1572872 | tf_op jit(solution)/shard_map/ppermute | solution.py:201
  78.2 4.0 %collective-permute-start.16 = (bf16[128,4096]{1,0:T(8,128)(2,1)S(1)}, bf16[128,4096]{1,0:T(8,128)(2,1)S(1)}, u32[]{:S(2)}, u32[]{:S(2)}) collective-permute-start(bf16[128,4096]{1,0:T(8,128)(2,1)S(1)} %get-tuple-element.38), channel_id=1, source_target_pairs={{0,1},{1,0},{2,3},{3,2},{4,5},{5,4},{6,7},{7,6},{8,9},{9,8},{10,11... | collective-permute-start | bytes 3145736 | tf_op jit(solution)/shard_map/ppermute | solution.py:201
  80.1 8.4 %collective-permute-start.22 = (bf16[32,4096]{1,0:T(8,128)(2,1)S(1)}, bf16[32,4096]{1,0:T(8,128)(2,1)S(1)}, u32[]{:S(2)}, u32[]{:S(2)}) collective-permute-start(bf16[32,4096]{1,0:T(8,128)(2,1)S(1)} %get-tuple-element.51), channel_id=1, source_target_pairs={{0,4},{1,5},{4,8},{5,9},{8,12},{9,13},{12,14},{13,15},{14,10},{15,... | collective-permute-start | bytes 786440 | tf_op jit(solution)/shard_map/ppermute | solution.py:220
  81.7 8.1 %collective-permute-start.26 = (bf16[32,4096]{1,0:T(8,128)(2,1)S(1)}, bf16[32,4096]{1,0:T(8,128)(2,1)S(1)}, u32[]{:S(2)}, u32[]{:S(2)}) collective-permute-start(bf16[32,4096]{1,0:T(8,128)(2,1)S(1)} %get-tuple-element.52), channel_id=1, source_target_pairs={{0,2},{1,3},{4,0},{5,1},{8,4},{9,5},{12,8},{13,9},{14,12},{15,13},... | collective-permute-start | bytes 786440 | tf_op jit(solution)/shard_map/ppermute | solution.py:221
  82.2 10.1 %collective-permute-start.11 = (bf16[128,4096]{1,0:T(8,128)(2,1)S(1)}, bf16[128,4096]{1,0:T(8,128)(2,1)S(1)}, u32[]{:S(2)}, u32[]{:S(2)}) collective-permute-start(bf16[128,4096]{1,0:T(8,128)(2,1)S(1)} %get-tuple-element.34), channel_id=1, source_target_pairs={{0,1},{1,0},{2,3},{3,2},{4,5},{5,4},{6,7},{7,6},{8,9},{9,8},{10,11... | collective-permute-start | bytes 3145736 | tf_op jit(solution)/shard_map/ppermute | solution.py:201
  90.1 12.9 %collective-permute-start.23 = (bf16[64,4096]{1,0:T(8,128)(2,1)S(1)}, bf16[64,4096]{1,0:T(8,128)(2,1)S(1)}, u32[]{:S(2)}, u32[]{:S(2)}) collective-permute-start(bf16[64,4096]{1,0:T(8,128)(2,1)S(1)} %get-tuple-element.49), channel_id=1, source_target_pairs={{0,4},{1,5},{4,8},{5,9},{8,12},{9,13},{12,14},{13,15},{14,10},{15,... | collective-permute-start | bytes 1572872 | tf_op jit(solution)/shard_map/ppermute | solution.py:228
  91.8 12.5 %collective-permute-start.27 = (bf16[64,4096]{1,0:T(8,128)(2,1)S(1)}, bf16[64,4096]{1,0:T(8,128)(2,1)S(1)}, u32[]{:S(2)}, u32[]{:S(2)}) collective-permute-start(bf16[64,4096]{1,0:T(8,128)(2,1)S(1)} %get-tuple-element.50), channel_id=1, source_target_pairs={{0,2},{1,3},{4,0},{5,1},{8,4},{9,5},{12,8},{13,9},{14,12},{15,13},... | collective-permute-start | bytes 1572872 | tf_op jit(solution)/shard_map/ppermute | solution.py:229
  92.2 14.7 %collective-permute-start.6 = (bf16[128,4096]{1,0:T(8,128)(2,1)S(1)}, bf16[128,4096]{1,0:T(8,128)(2,1)S(1)}, u32[]{:S(2)}, u32[]{:S(2)}) collective-permute-start(bf16[128,4096]{1,0:T(8,128)(2,1)S(1)} %get-tuple-element.30), channel_id=1, source_target_pairs={{0,1},{1,0},{2,3},{3,2},{4,5},{5,4},{6,7},{7,6},{8,9},{9,8},{10,11... | collective-permute-start | bytes 3145736 | tf_op jit(solution)/shard_map/ppermute | solution.py:201
  104.8 11.7 %collective-permute-start.24 = (bf16[64,4096]{1,0:T(8,128)(2,1)S(1)}, bf16[64,4096]{1,0:T(8,128)(2,1)S(1)}, u32[]{:S(2)}, u32[]{:S(2)}) collective-permute-start(bf16[64,4096]{1,0:T(8,128)(2,1)S(1)} %get-tuple-element.47), channel_id=1, source_target_pairs={{0,4},{1,5},{4,8},{5,9},{8,12},{9,13},{12,14},{13,15},{14,10},{15,... | collective-permute-start | bytes 1572872 | tf_op jit(solution)/shard_map/ppermute | solution.py:228
  106.4 11.3 %collective-permute-start.28 = (bf16[64,4096]{1,0:T(8,128)(2,1)S(1)}, bf16[64,4096]{1,0:T(8,128)(2,1)S(1)}, u32[]{:S(2)}, u32[]{:S(2)}) collective-permute-start(bf16[64,4096]{1,0:T(8,128)(2,1)S(1)} %get-tuple-element.48), channel_id=1, source_target_pairs={{0,2},{1,3},{4,0},{5,1},{8,4},{9,5},{12,8},{13,9},{14,12},{15,13},... | collective-permute-start | bytes 1572872 | tf_op jit(solution)/shard_map/ppermute | solution.py:229
  106.9 13.4 %collective-permute-start.1 = (bf16[64,4096]{1,0:T(8,128)(2,1)S(1)}, bf16[64,4096]{1,0:T(8,128)(2,1)S(1)}, u32[]{:S(2)}, u32[]{:S(2)}) collective-permute-start(bf16[64,4096]{1,0:T(8,128)(2,1)S(1)} %get-tuple-element.28), channel_id=1, source_target_pairs={{0,1},{1,0},{2,3},{3,2},{4,5},{5,4},{6,7},{7,6},{8,9},{9,8},{10,11... | collective-permute-start | bytes 1572872 | tf_op jit(solution)/shard_map/ppermute | solution.py:201
  118.2 10.5 %collective-permute-start.25 = (bf16[64,4096]{1,0:T(8,128)(2,1)S(1)}, bf16[64,4096]{1,0:T(8,128)(2,1)S(1)}, u32[]{:S(2)}, u32[]{:S(2)}) collective-permute-start(bf16[64,4096]{1,0:T(8,128)(2,1)S(1)} %get-tuple-element.45), channel_id=1, source_target_pairs={{0,4},{1,5},{4,8},{5,9},{8,12},{9,13},{12,14},{13,15},{14,10},{15,... | collective-permute-start | bytes 1572872 | tf_op jit(solution)/shard_map/ppermute | solution.py:228
  119.5 10.1 %collective-permute-start.29 = (bf16[64,4096]{1,0:T(8,128)(2,1)S(1)}, bf16[64,4096]{1,0:T(8,128)(2,1)S(1)}, u32[]{:S(2)}, u32[]{:S(2)}) collective-permute-start(bf16[64,4096]{1,0:T(8,128)(2,1)S(1)} %get-tuple-element.46), channel_id=1, source_target_pairs={{0,2},{1,3},{4,0},{5,1},{8,4},{9,5},{12,8},{13,9},{14,12},{15,13},... | collective-permute-start | bytes 1572872 | tf_op jit(solution)/shard_map/ppermute | solution.py:229

commit v5 on v4

--- a/solution.py
+++ b/solution.py
@@ -62,8 +62,8 @@
     count = len(sizes)
     xs = refs[:count]
     pick, gate_up_s, down_s, gate_up, down = refs[count : count + 5]
-    outs = refs[count + 5 : count + 7]
-    x, hidden, out, x_sem, out_sem = refs[count + 7 :]
+    outs = refs[count + 5 : -5]
+    x, hidden, out, x_sem, out_sem = refs[-5:]
     units, width = down.shape
 
     starts = [sum(sizes[:i]) for i in range(count)]
@@ -119,29 +119,28 @@
             copy.wait()
 
 
-def expert_part(blocks, split, pick, gate_up_w, gate_up_s, down_w, down_s):
+def expert_part(blocks, out_rows, hint, pick, gate_up_w, gate_up_s, down_w, down_s):
     width, units2 = gate_up_w.shape
     units = down_w.shape[0]
     sizes = [block.shape[0] for block in blocks]
     rows, packed_width = sum(sizes), blocks[0].shape[1]
-    out_rows = [sum(sizes[:split]), sum(sizes[split:])]
     anywhere, vmem = pl.BlockSpec(memory_space=pl.ANY), pl.BlockSpec(memory_space=pltpu.VMEM)
-    flops = 2 * rows * width * (units2 + units)
+    flops = int(hint * 2 * rows * width * (units2 + units))
     return pl.pallas_call(
         functools.partial(expert_kernel, sizes),
         in_specs=[anywhere] * len(blocks) + [vmem] * 5,
-        out_specs=[anywhere] * 2,
+        out_specs=[anywhere] * len(out_rows),
         out_shape=[jax.ShapeDtypeStruct((size, width), jnp.bfloat16) for size in out_rows],
         scratch_shapes=[
             pltpu.VMEM((rows, packed_width), jnp.bfloat16),
             pltpu.VMEM((rows, units), jnp.bfloat16),
             pltpu.VMEM((rows, width), jnp.bfloat16),
             pltpu.SemaphoreType.DMA((len(blocks),)),
-            pltpu.SemaphoreType.DMA((width // WIDTH_CHUNK, 2)),
+            pltpu.SemaphoreType.DMA((width // WIDTH_CHUNK, len(out_rows))),
         ],
         compiler_params=pltpu.CompilerParams(vmem_limit_bytes=16 << 20),
         cost_estimate=pl.CostEstimate(
-            flops=2 * flops, bytes_accessed=4 * rows * width, transcendentals=rows * units
+            flops=flops, bytes_accessed=int(hint * 4 * rows * width), transcendentals=0
         ),
         name="expert",
     )(
@@ -161,8 +160,12 @@
     return total.astype(jnp.bfloat16)
 
 
+def together(*values):
+    return lax.optimization_barrier(values)
+
+
 def after(value, *others):
-    return lax.optimization_barrier((value, *others))[0]
+    return together(value, *others)[0]
 
 
 def body(tokens, routes, gate_num, gate_up_q, gate_up_scale, down_q, down_scale):
@@ -194,40 +197,54 @@
     packed = pack(tokens, routes, gate_num, devices)
     mine, theirs = {}, {}
 
-    def run(distance, blocks):
-        others = [send(block, perm=swap) for block in blocks]
-        kept, given = expert_part(blocks + others, len(blocks), *weights)
-        mine[distance] = kept
-        theirs[distance] = send(given, perm=swap)
+    def run(distance, blocks, cuts=()):
+        others = [send(after(block, *mine.get(distance - 1, ())), perm=swap) for block in blocks]
+        count = sum(block.shape[0] for block in blocks)
+        kept, *given = expert_part(blocks + others, (count, *(cuts or (count,))), 2, *weights)
+        mine[distance] = (kept,)
+        theirs[distance] = [send(piece, perm=swap) for piece in given]
 
     from_below, from_above = packed, packed
     run(0, [packed])
     for distance in range(1, reach):
         if distance > 1:
-            from_below = after(from_below, mine[distance - 2])
-            from_above = after(from_above, mine[distance - 2])
+            from_below = after(from_below, *mine[distance - 2])
+            from_above = after(from_above, *mine[distance - 2])
         from_below = send(from_below, perm=upward)
         from_above = send(from_above, perm=downward)
-        run(distance, [from_below, from_above])
-    from_below = after(from_below, mine[reach - 2])
-    from_above = after(from_above, mine[reach - 2])
+        run(distance, [from_below, from_above], (half, rows, half) if distance == reach - 1 else ())
+    from_below = after(from_below, *mine[reach - 2])
+    from_above = after(from_above, *mine[reach - 2])
     last_below = send(from_below[:half], perm=upward)
     last_above = send(from_above[half:], perm=downward)
-    last_below = after(last_below, mine[reach - 1])
-    last_above = after(last_above, mine[reach - 1])
+
+    def part(distance, start):
+        found = []
+        for arrays in (mine[distance], theirs[distance]):
+            at = start
+            for array in arrays:
+                if 0 <= at < array.shape[0]:
+                    found.append(array[at : at + half])
+                at -= array.shape[0]
+        return found
+
+    def forward(distance, is_long, carried):
+        up_start = rows + (0 if is_long else half)
+        down_start = half if is_long else 0
+        up = add(*part(distance, 0 if distance == reach else up_start), *carried[:1])
+        down = add(*part(distance, down_start), *carried[1:])
+        return (up, down), (send(up, perm=upward), send(down, perm=downward))
+
+    sent, short = forward(reach - 1, False, ())
     run(reach, [last_below, last_above])
-
-    to_above = send(add(mine[reach][:half], theirs[reach][:half]), perm=upward)
-    to_below = send(add(mine[reach][half:], theirs[reach][half:]), perm=downward)
-    for distance in range(reach - 1, 0, -1):
-        if distance == reach - 1:
-            to_above = jnp.pad(to_above, ((0, half), (0, 0)))
-            to_below = jnp.pad(to_below, ((half, 0), (0, 0)))
-        above = add(mine[distance][rows:], theirs[distance][rows:], to_above)
-        below = add(mine[distance][:rows], theirs[distance][:rows], to_below)
-        to_above = send(above, perm=upward)
-        to_below = send(below, perm=downward)
-    return add(mine[0], theirs[0], to_above, to_below)
+    sent, long = forward(reach, True, ())
+    for distance in range(reach - 2, -1, -1):
+        if distance > 0:
+            sent, short = forward(distance, False, together(*short, *sent)[:2])
+        sent, long = forward(distance + 1, True, together(*long, *sent)[:2])
+    top = add(*part(0, 0), long[0], short[1])
+    bottom = add(*part(0, half), short[0], long[1])
+    return jnp.concatenate([top, bottom], axis=0)
 
 
 def solution(mesh):

time: 131 us -> 118 us (0.901)
  waiting for transfers between devices: 66.3 us -> 47.7 us
  starting transfers between devices: 19.8 us -> 25.7 us
    ppermute x22 -> x30, waiting for transfers between devices: 42.7 us -> 32.8 us  [the longest x14 31.1 us: forward(): return ((up, down), (send(up, perm=upward), send(down, perm=downward)))]
    ppermute x3, waiting for transfers between devices: 17.7 us -> 11 us  [body(): from_above = send(from_above, perm=downward)]
    ppermute x22 -> x30, starting transfers between devices: 10.5 us -> 16.8 us  [the longest x14 14.4 us: forward(): return ((up, down), (send(up, perm=upward), send(down, perm=downward)))]
    ppermute x3, starting transfers between devices: 6.12 us -> 1.04 us  [body(): from_below = send(from_below, perm=upward)]
    ppermute x3, starting transfers between devices: 1.06 us -> 5.73 us  [body(): from_above = send(from_above, perm=downward)]
    ppermute x3, waiting for transfers between devices: 5.82 us -> 3.99 us  [body(): from_below = send(from_below, perm=upward)]
  transfers between devices with their start and end apart: 30 -> 38, of which waited for: 15 -> 21; matrix products, arithmetic and copies ran while one was open for 1% -> 1% of each run, Pallas kernels for 27% -> 34%
where the time goes in v5:
time: 118 us
  waiting for transfers between devices  47.7 us (40%)
  Pallas kernels  40.2 us (34%)
  starting transfers between devices  25.7 us (22%)
  other arithmetic  3.08 us (3%)
  local copies, waits for them, and re-layouts  1.28 us (1%)
    pallas_call x5, Pallas kernels, expert_part(): pl.pallas_call(functools.partial(expert_kernel, sizes), in_specs=[anywher...  33.8 us
    ppermute x14, waiting for transfers between devices, forward(): return ((up, down), (send(up, perm=upward), send(down, perm=downward)))  31.1 us
    ppermute x14, starting transfers between devices, forward(): return ((up, down), (send(up, perm=upward), send(down, perm=downward)))  14.4 us
    ppermute x3, waiting for transfers between devices, body(): from_above = send(from_above, perm=downward)  11 us
    pallas_call x1, Pallas kernels, keep(): pl.pallas_call(keep_kernel, in_specs=[anywhere] * 2, out_specs=[vmem] * 2...  6.38 us
    ppermute x3, starting transfers between devices, body(): from_above = send(from_above, perm=downward)  5.73 us
    ppermute x3, waiting for transfers between devices, body(): from_below = send(from_below, perm=upward)  3.99 us
  transfers between devices with their start and end apart: 38, of which 21 were waited for; matrix products, arithmetic and copies ran while one was open for 1% of the time, Pallas kernels for 34%

profile of v5, /device:TPU:0, one launch (start us, length us, event | category | flops | bytes accessed | tf_op | source)
XLA Modules:
  0.0 118.2 jit_solution(17260365004792102863)
XLA Ops:
  2.5 2.6 %collective-permute-start.3 = (bf16[64,4224]{1,0:T(8,128)(2,1)S(1)}, bf16[64,4224]{1,0:T(8,128)(2,1)S(1)}, u32[]{:S(2)}, u32[]{:S(2)}) collective-permute-start(bf16[64,4224]{1,0:T(8,128)(2,1)S(1)} %concatenate.6.refs_0_), channel_id=1, source_target_pairs={{0,2},{1,3},{4,0},{5,1},{8,4},{9,5},{12,8},{13,9},{14,12},{15,13},... | collective-permute-start | bytes 1622024 | tf_op jit(solution)/shard_map/ppermute | solution.py:214
  5.3 6.4 %keep.1 = (bf16[4096,1536]{1,0:T(8,128)(2,1)S(1)}, bf16[768,4096]{1,0:T(8,128)(2,1)S(1)}) custom-call(bf16[4096,1536]{1,0:T(8,128)(2,1)} %bitcast.2, bf16[768,4096]{1,0:T(8,128)(2,1)} %bitcast.3), custom_call_target="tpu_custom_call" | custom-call | bytes 18874368 | tf_op jit(solution)/shard_map/keep/pallas_call | solution.py:46
  11.7 5.1 %expert.5 = (bf16[64,4096]{1,0:T(8,128)(2,1)S(1)}, bf16[64,4096]{1,0:T(8,128)(2,1)S(1)}) custom-call(bf16[64,4224]{1,0:T(8,128)(2,1)S(1)} %concatenate.6.refs_0_, bf16[64,4224]{1,0:T(8,128)(2,1)S(1)} %collective-permute-done.refs_1_, f32[1,128]{1,0:T(1,128)S(1)} %compare_select_fusion.1.refs_2_.refs_4_, f32[1,1536]{1,0:T(1,128)S(1)} %copy-done.1, ...), custom_call_target="tpu_custom_call" | custom-call | flops 4831838208 | bytes 4194304 | tf_op jit(solution)/shard_map/expert/pallas_call | solution.py:129
  16.8 1.3 %collective-permute-done.3.refs_1_ = bf16[64,4224]{1,0:T(8,128)(2,1)S(1)} collective-permute-done((bf16[64,4224]{1,0:T(8,128)(2,1)S(1)}, bf16[64,4224]{1,0:T(8,128)(2,1)S(1)}, u32[]{:S(2)}, u32[]{:S(2)}) %collective-permute-start.3) | collective-permute-done | bytes 540704 | tf_op jit(solution)/shard_map/ppermute | solution.py:214
  18.1 1.4 %collective-permute-done.2.refs_0_ = bf16[64,4224]{1,0:T(8,128)(2,1)S(1)} collective-permute-done((bf16[64,4224]{1,0:T(8,128)(2,1)S(1)}, bf16[64,4224]{1,0:T(8,128)(2,1)S(1)}, u32[]{:S(2)}, u32[]{:S(2)}) %collective-permute-start.2) | collective-permute-done | bytes 540704 | tf_op jit(solution)/shard_map/ppermute | solution.py:213
  19.5 1.6 %collective-permute-start.8 = (bf16[64,4224]{1,0:T(8,128)(2,1)S(1)}, bf16[64,4224]{1,0:T(8,128)(2,1)S(1)}, u32[]{:S(2)}, u32[]{:S(2)}) collective-permute-start(bf16[64,4224]{1,0:T(8,128)(2,1)S(1)} %collective-permute-done.3.refs_1_), channel_id=1, source_target_pairs={{0,2},{1,3},{4,0},{5,1},{8,4},{9,5},{12,8},{13,9},{14,12},{15,13},... | collective-permute-start | bytes 1622024 | tf_op jit(solution)/shard_map/ppermute | solution.py:214
  21.5 7.8 %expert.6 = (bf16[128,4096]{1,0:T(8,128)(2,1)S(1)}, bf16[128,4096]{1,0:T(8,128)(2,1)S(1)}) custom-call(bf16[64,4224]{1,0:T(8,128)(2,1)S(1)} %collective-permute-done.2.refs_0_, bf16[64,4224]{1,0:T(8,128)(2,1)S(1)} %collective-permute-done.3.refs_1_, bf16[64,4224]{1,0:T(8,128)(2,1)S(1)} %collective-permute-done.4.refs_2_, ...), custom_call_target="tpu_custom_call" | custom-call | flops 9663676416 | bytes 8388608 | tf_op jit(solution)/shard_map/expert/pallas_call | solution.py:129
  29.3 4.9 %collective-permute-done.8.refs_1_ = bf16[64,4224]{1,0:T(8,128)(2,1)S(1)} collective-permute-done((bf16[64,4224]{1,0:T(8,128)(2,1)S(1)}, bf16[64,4224]{1,0:T(8,128)(2,1)S(1)}, u32[]{:S(2)}, u32[]{:S(2)}) %collective-permute-start.8) | collective-permute-done | bytes 540704 | tf_op jit(solution)/shard_map/ppermute | solution.py:214
  34.2 1.3 %collective-permute-done.7.refs_0_ = bf16[64,4224]{1,0:T(8,128)(2,1)S(1)} collective-permute-done((bf16[64,4224]{1,0:T(8,128)(2,1)S(1)}, bf16[64,4224]{1,0:T(8,128)(2,1)S(1)}, u32[]{:S(2)}, u32[]{:S(2)}) %collective-permute-start.7) | collective-permute-done | bytes 540704 | tf_op jit(solution)/shard_map/ppermute | solution.py:213
  35.5 1.6 %collective-permute-start.13 = (bf16[64,4224]{1,0:T(8,128)(2,1)S(1)}, bf16[64,4224]{1,0:T(8,128)(2,1)S(1)}, u32[]{:S(2)}, u32[]{:S(2)}) collective-permute-start(bf16[64,4224]{1,0:T(8,128)(2,1)S(1)} %collective-permute-done.8.refs_1_), channel_id=1, source_target_pairs={{0,2},{1,3},{4,0},{5,1},{8,4},{9,5},{12,8},{13,9},{14,12},{15,13},... | collective-permute-start | bytes 1622024 | tf_op jit(solution)/shard_map/ppermute | solution.py:214
  37.5 7.8 %expert.7 = (bf16[128,4096]{1,0:T(8,128)(2,1)S(1)}, bf16[128,4096]{1,0:T(8,128)(2,1)S(1)}) custom-call(bf16[64,4224]{1,0:T(8,128)(2,1)S(1)} %collective-permute-done.7.refs_0_, bf16[64,4224]{1,0:T(8,128)(2,1)S(1)} %collective-permute-done.8.refs_1_, bf16[64,4224]{1,0:T(8,128)(2,1)S(1)} %collective-permute-done.9.refs_2_, ...), custom_call_target="tpu_custom_call" | custom-call | flops 9663676416 | bytes 8388608 | tf_op jit(solution)/shard_map/expert/pallas_call | solution.py:129
  45.3 4.9 %collective-permute-done.13.refs_1_ = bf16[64,4224]{1,0:T(8,128)(2,1)S(1)} collective-permute-done((bf16[64,4224]{1,0:T(8,128)(2,1)S(1)}, bf16[64,4224]{1,0:T(8,128)(2,1)S(1)}, u32[]{:S(2)}, u32[]{:S(2)}) %collective-permute-start.13) | collective-permute-done | bytes 540704 | tf_op jit(solution)/shard_map/ppermute | solution.py:214
  50.1 1.3 %collective-permute-done.12.refs_0_ = bf16[64,4224]{1,0:T(8,128)(2,1)S(1)} collective-permute-done((bf16[64,4224]{1,0:T(8,128)(2,1)S(1)}, bf16[64,4224]{1,0:T(8,128)(2,1)S(1)}, u32[]{:S(2)}, u32[]{:S(2)}) %collective-permute-start.12) | collective-permute-done | bytes 540704 | tf_op jit(solution)/shard_map/ppermute | solution.py:213
  51.5 1.6 %collective-permute-start.18 = (bf16[32,4224]{1,0:T(8,128)(2,1)S(1)}, bf16[32,4224]{1,0:T(8,128)(2,1)S(1)}, u32[]{:S(2)}, u32[]{:S(2)}) collective-permute-start(bf16[32,4224]{1,0:T(8,128)(2,1)S(1)} %slice.105), channel_id=1, source_target_pairs={{0,2},{1,3},{4,0},{5,1},{8,4},{9,5},{12,8},{13,9},{14,12},{15,13},... | collective-permute-start | bytes 811016 | tf_op jit(solution)/shard_map/ppermute | solution.py:219
  53.6 8.0 %expert.8 = (bf16[128,4096]{1,0:T(8,128)(2,1)S(1)}, bf16[32,4096]{1,0:T(8,128)(2,1)S(1)}, bf16[64,4096]{1,0:T(8,128)(2,1)S(1)}, bf16[32,4096]{1,0:T(8,128)(2,1)S(1)}) custom-call(bf16[64,4224]{1,0:T(8,128)(2,1)S(1)} %collective-permute-done.12.refs_0_, bf16[64,4224]{1,0:T(8,128)(2,1)S(1)} %collective-permute-done.13.refs_1_, ...), custom_call_target="tpu_custom_call" | custom-call | flops 9663676416 | bytes 8388608 | tf_op jit(solution)/shard_map/expert/pallas_call | solution.py:129
  63.8 5.1 %expert.9 = (bf16[64,4096]{1,0:T(8,128)(2,1)S(1)}, bf16[64,4096]{1,0:T(8,128)(2,1)S(1)}) custom-call(bf16[32,4224]{1,0:T(8,128)(2,1)S(1)} %collective-permute-done.17.refs_0_, bf16[32,4224]{1,0:T(8,128)(2,1)S(1)} %collective-permute-done.18.refs_1_, bf16[32,4224]{1,0:T(8,128)(2,1)S(1)} %collective-permute-done.19.refs_2_, ...), custom_call_target="tpu_custom_call" | custom-call | flops 4831838208 | bytes 4194304 | tf_op jit(solution)/shard_map/expert/pallas_call | solution.py:129
  70.9 1.6 %collective-permute-start.27 = (bf16[32,4096]{1,0:T(8,128)(2,1)S(1)}, bf16[32,4096]{1,0:T(8,128)(2,1)S(1)}, u32[]{:S(2)}, u32[]{:S(2)}) collective-permute-start(bf16[32,4096]{1,0:T(8,128)(2,1)S(1)} %get-tuple-element.81), channel_id=1, source_target_pairs={{0,2},{1,3},{4,0},{5,1},{8,4},{9,5},{12,8},{13,9},{14,12},{15,13},... | collective-permute-start | bytes 786440 | tf_op jit(solution)/shard_map/ppermute | solution.py:236
  72.6 5.3 %collective-permute-done.25 = bf16[32,4096]{1,0:T(8,128)(2,1)S(1)} collective-permute-done((bf16[32,4096]{1,0:T(8,128)(2,1)S(1)}, bf16[32,4096]{1,0:T(8,128)(2,1)S(1)}, u32[]{:S(2)}, u32[]{:S(2)}) %collective-permute-start.25) | collective-permute-done | bytes 262176 | tf_op jit(solution)/shard_map/ppermute | solution.py:236
  79.5 1.6 %collective-permute-start.23 = (bf16[32,4096]{1,0:T(8,128)(2,1)S(1)}, bf16[32,4096]{1,0:T(8,128)(2,1)S(1)}, u32[]{:S(2)}, u32[]{:S(2)}) collective-permute-start(bf16[32,4096]{1,0:T(8,128)(2,1)S(1)} %get-tuple-element.83), channel_id=1, source_target_pairs={{0,2},{1,3},{4,0},{5,1},{8,4},{9,5},{12,8},{13,9},{14,12},{15,13},... | collective-permute-start | bytes 786440 | tf_op jit(solution)/shard_map/ppermute | solution.py:236
  81.8 5.4 %collective-permute-done.22 = bf16[32,4096]{1,0:T(8,128)(2,1)S(1)} collective-permute-done((bf16[32,4096]{1,0:T(8,128)(2,1)S(1)}, bf16[32,4096]{1,0:T(8,128)(2,1)S(1)}, u32[]{:S(2)}, u32[]{:S(2)}) %collective-permute-start.22) | collective-permute-done | bytes 262176 | tf_op jit(solution)/shard_map/ppermute | solution.py:236
  87.1 1.6 %collective-permute-start.31 = (bf16[32,4096]{1,0:T(8,128)(2,1)S(1)}, bf16[32,4096]{1,0:T(8,128)(2,1)S(1)}, u32[]{:S(2)}, u32[]{:S(2)}) collective-permute-start(bf16[32,4096]{1,0:T(8,128)(2,1)S(1)} %get-tuple-element.75), channel_id=1, source_target_pairs={{0,2},{1,3},{4,0},{5,1},{8,4},{9,5},{12,8},{13,9},{14,12},{15,13},... | collective-permute-start | bytes 786440 | tf_op jit(solution)/shard_map/ppermute | solution.py:236
  89.4 1.6 %collective-permute-start.29 = (bf16[32,4096]{1,0:T(8,128)(2,1)S(1)}, bf16[32,4096]{1,0:T(8,128)(2,1)S(1)}, u32[]{:S(2)}, u32[]{:S(2)}) collective-permute-start(bf16[32,4096]{1,0:T(8,128)(2,1)S(1)} %get-tuple-element.77), channel_id=1, source_target_pairs={{0,2},{1,3},{4,0},{5,1},{8,4},{9,5},{12,8},{13,9},{14,12},{15,13},... | collective-permute-start | bytes 786440 | tf_op jit(solution)/shard_map/ppermute | solution.py:236
  91.0 1.8 %collective-permute-done.30 = bf16[32,4096]{1,0:T(8,128)(2,1)S(1)} collective-permute-done((bf16[32,4096]{1,0:T(8,128)(2,1)S(1)}, bf16[32,4096]{1,0:T(8,128)(2,1)S(1)}, u32[]{:S(2)}, u32[]{:S(2)}) %collective-permute-start.30) | collective-permute-done | bytes 262176 | tf_op jit(solution)/shard_map/ppermute | solution.py:236
  92.8 2.9 %collective-permute-done.31 = bf16[32,4096]{1,0:T(8,128)(2,1)S(1)} collective-permute-done((bf16[32,4096]{1,0:T(8,128)(2,1)S(1)}, bf16[32,4096]{1,0:T(8,128)(2,1)S(1)}, u32[]{:S(2)}, u32[]{:S(2)}) %collective-permute-start.31) | collective-permute-done | bytes 262176 | tf_op jit(solution)/shard_map/ppermute | solution.py:236
  96.7 2.2 %collective-permute-done.29 = bf16[32,4096]{1,0:T(8,128)(2,1)S(1)} collective-permute-done((bf16[32,4096]{1,0:T(8,128)(2,1)S(1)}, bf16[32,4096]{1,0:T(8,128)(2,1)S(1)}, u32[]{:S(2)}, u32[]{:S(2)}) %collective-permute-start.29) | collective-permute-done | bytes 262176 | tf_op jit(solution)/shard_map/ppermute | solution.py:236
  99.5 1.6 %collective-permute-start.33 = (bf16[32,4096]{1,0:T(8,128)(2,1)S(1)}, bf16[32,4096]{1,0:T(8,128)(2,1)S(1)}, u32[]{:S(2)}, u32[]{:S(2)}) collective-permute-start(bf16[32,4096]{1,0:T(8,128)(2,1)S(1)} %get-tuple-element.71), channel_id=1, source_target_pairs={{0,2},{1,3},{4,0},{5,1},{8,4},{9,5},{12,8},{13,9},{14,12},{15,13},... | collective-permute-start | bytes 786440 | tf_op jit(solution)/shard_map/ppermute | solution.py:236
  101.1 1.6 %collective-permute-start.35 = (bf16[32,4096]{1,0:T(8,128)(2,1)S(1)}, bf16[32,4096]{1,0:T(8,128)(2,1)S(1)}, u32[]{:S(2)}, u32[]{:S(2)}) collective-permute-start(bf16[32,4096]{1,0:T(8,128)(2,1)S(1)} %get-tuple-element.73), channel_id=1, source_target_pairs={{0,2},{1,3},{4,0},{5,1},{8,4},{9,5},{12,8},{13,9},{14,12},{15,13},... | collective-permute-start | bytes 786440 | tf_op jit(solution)/shard_map/ppermute | solution.py:236
  103.1 2.3 %collective-permute-done.32 = bf16[32,4096]{1,0:T(8,128)(2,1)S(1)} collective-permute-done((bf16[32,4096]{1,0:T(8,128)(2,1)S(1)}, bf16[32,4096]{1,0:T(8,128)(2,1)S(1)}, u32[]{:S(2)}, u32[]{:S(2)}) %collective-permute-start.32) | collective-permute-done | bytes 262176 | tf_op jit(solution)/shard_map/ppermute | solution.py:236
  105.4 2.1 %collective-permute-done.33 = bf16[32,4096]{1,0:T(8,128)(2,1)S(1)} collective-permute-done((bf16[32,4096]{1,0:T(8,128)(2,1)S(1)}, bf16[32,4096]{1,0:T(8,128)(2,1)S(1)}, u32[]{:S(2)}, u32[]{:S(2)}) %collective-permute-start.33) | collective-permute-done | bytes 262176 | tf_op jit(solution)/shard_map/ppermute | solution.py:236
  107.8 2.0 %collective-permute-start.37 = (bf16[32,4096]{1,0:T(8,128)(2,1)S(1)}, bf16[32,4096]{1,0:T(8,128)(2,1)S(1)}, u32[]{:S(2)}, u32[]{:S(2)}) collective-permute-start(bf16[32,4096]{1,0:T(8,128)(2,1)S(1)} %get-tuple-element.70), channel_id=1, source_target_pairs={{0,2},{1,3},{4,0},{5,1},{8,4},{9,5},{12,8},{13,9},{14,12},{15,13},... | collective-permute-start | bytes 786440 | tf_op jit(solution)/shard_map/ppermute | solution.py:236
  109.8 3.3 %collective-permute-done.35 = bf16[32,4096]{1,0:T(8,128)(2,1)S(1)} collective-permute-done((bf16[32,4096]{1,0:T(8,128)(2,1)S(1)}, bf16[32,4096]{1,0:T(8,128)(2,1)S(1)}, u32[]{:S(2)}, u32[]{:S(2)}) %collective-permute-start.35) | collective-permute-done | bytes 262176 | tf_op jit(solution)/shard_map/ppermute | solution.py:236
  113.2 3.6 %collective-permute-done.34 = bf16[32,4096]{1,0:T(8,128)(2,1)S(1)} collective-permute-done((bf16[32,4096]{1,0:T(8,128)(2,1)S(1)}, bf16[32,4096]{1,0:T(8,128)(2,1)S(1)}, u32[]{:S(2)}, u32[]{:S(2)}) %collective-permute-start.34) | collective-permute-done | bytes 262176 | tf_op jit(solution)/shard_map/ppermute | solution.py:236
  (71 shorter events, 15.1 us)
Async XLA Ops:
  2.0 9.6 %collective-permute-start = (bf16[64,4224]{1,0:T(8,128)(2,1)S(1)}, bf16[64,4224]{1,0:T(8,128)(2,1)S(1)}, u32[]{:S(2)}, u32[]{:S(2)}) collective-permute-start(bf16[64,4224]{1,0:T(8,128)(2,1)S(1)} %concatenate.6.refs_0_), channel_id=1, source_target_pairs={{0,1},{1,0},{2,3},{3,2},{4,5},{5,4},{6,7},{7,6},{8,9},{9,8},{10,11... | collective-permute-start | bytes 1622024 | tf_op jit(solution)/shard_map/ppermute | solution.py:201
  2.5 15.5 %collective-permute-start.3 = (bf16[64,4224]{1,0:T(8,128)(2,1)S(1)}, bf16[64,4224]{1,0:T(8,128)(2,1)S(1)}, u32[]{:S(2)}, u32[]{:S(2)}) collective-permute-start(bf16[64,4224]{1,0:T(8,128)(2,1)S(1)} %concatenate.6.refs_0_), channel_id=1, source_target_pairs={{0,2},{1,3},{4,0},{5,1},{8,4},{9,5},{12,8},{13,9},{14,12},{15,13},... | collective-permute-start | bytes 1622024 | tf_op jit(solution)/shard_map/ppermute | solution.py:214
  5.1 14.3 %collective-permute-start.2 = (bf16[64,4224]{1,0:T(8,128)(2,1)S(1)}, bf16[64,4224]{1,0:T(8,128)(2,1)S(1)}, u32[]{:S(2)}, u32[]{:S(2)}) collective-permute-start(bf16[64,4224]{1,0:T(8,128)(2,1)S(1)} %concatenate.6.refs_0_), channel_id=1, source_target_pairs={{0,4},{1,5},{4,8},{5,9},{8,12},{9,13},{12,14},{13,15},{14,10},{15,... | collective-permute-start | bytes 1622024 | tf_op jit(solution)/shard_map/ppermute | solution.py:213
  18.1 3.4 %collective-permute-start.5 = (bf16[64,4224]{1,0:T(8,128)(2,1)S(1)}, bf16[64,4224]{1,0:T(8,128)(2,1)S(1)}, u32[]{:S(2)}, u32[]{:S(2)}) collective-permute-start(bf16[64,4224]{1,0:T(8,128)(2,1)S(1)} %collective-permute-done.3.refs_1_), channel_id=1, source_target_pairs={{0,1},{1,0},{2,3},{3,2},{4,5},{5,4},{6,7},{7,6},{8,9},{9,8},{10,11... | collective-permute-start | bytes 1622024 | tf_op jit(solution)/shard_map/ppermute | solution.py:201
  19.5 14.7 %collective-permute-start.8 = (bf16[64,4224]{1,0:T(8,128)(2,1)S(1)}, bf16[64,4224]{1,0:T(8,128)(2,1)S(1)}, u32[]{:S(2)}, u32[]{:S(2)}) collective-permute-start(bf16[64,4224]{1,0:T(8,128)(2,1)S(1)} %collective-permute-done.3.refs_1_), channel_id=1, source_target_pairs={{0,2},{1,3},{4,0},{5,1},{8,4},{9,5},{12,8},{13,9},{14,12},{15,13},... | collective-permute-start | bytes 1622024 | tf_op jit(solution)/shard_map/ppermute | solution.py:214
  21.0 14.4 %collective-permute-start.7 = (bf16[64,4224]{1,0:T(8,128)(2,1)S(1)}, bf16[64,4224]{1,0:T(8,128)(2,1)S(1)}, u32[]{:S(2)}, u32[]{:S(2)}) collective-permute-start(bf16[64,4224]{1,0:T(8,128)(2,1)S(1)} %collective-permute-done.2.refs_0_), channel_id=1, source_target_pairs={{0,4},{1,5},{4,8},{5,9},{8,12},{9,13},{12,14},{13,15},{14,10},{15,... | collective-permute-start | bytes 1622024 | tf_op jit(solution)/shard_map/ppermute | solution.py:213
  34.2 3.3 %collective-permute-start.10 = (bf16[64,4224]{1,0:T(8,128)(2,1)S(1)}, bf16[64,4224]{1,0:T(8,128)(2,1)S(1)}, u32[]{:S(2)}, u32[]{:S(2)}) collective-permute-start(bf16[64,4224]{1,0:T(8,128)(2,1)S(1)} %collective-permute-done.8.refs_1_), channel_id=1, source_target_pairs={{0,1},{1,0},{2,3},{3,2},{4,5},{5,4},{6,7},{7,6},{8,9},{9,8},{10,11... | collective-permute-start | bytes 1622024 | tf_op jit(solution)/shard_map/ppermute | solution.py:201
  35.5 14.7 %collective-permute-start.13 = (bf16[64,4224]{1,0:T(8,128)(2,1)S(1)}, bf16[64,4224]{1,0:T(8,128)(2,1)S(1)}, u32[]{:S(2)}, u32[]{:S(2)}) collective-permute-start(bf16[64,4224]{1,0:T(8,128)(2,1)S(1)} %collective-permute-done.8.refs_1_), channel_id=1, source_target_pairs={{0,2},{1,3},{4,0},{5,1},{8,4},{9,5},{12,8},{13,9},{14,12},{15,13},... | collective-permute-start | bytes 1622024 | tf_op jit(solution)/shard_map/ppermute | solution.py:214
  37.0 14.4 %collective-permute-start.12 = (bf16[64,4224]{1,0:T(8,128)(2,1)S(1)}, bf16[64,4224]{1,0:T(8,128)(2,1)S(1)}, u32[]{:S(2)}, u32[]{:S(2)}) collective-permute-start(bf16[64,4224]{1,0:T(8,128)(2,1)S(1)} %collective-permute-done.7.refs_0_), channel_id=1, source_target_pairs={{0,4},{1,5},{4,8},{5,9},{8,12},{9,13},{12,14},{13,15},{14,10},{15,... | collective-permute-start | bytes 1622024 | tf_op jit(solution)/shard_map/ppermute | solution.py:213
  50.1 3.4 %collective-permute-start.15 = (bf16[64,4224]{1,0:T(8,128)(2,1)S(1)}, bf16[64,4224]{1,0:T(8,128)(2,1)S(1)}, u32[]{:S(2)}, u32[]{:S(2)}) collective-permute-start(bf16[64,4224]{1,0:T(8,128)(2,1)S(1)} %collective-permute-done.13.refs_1_), channel_id=1, source_target_pairs={{0,1},{1,0},{2,3},{3,2},{4,5},{5,4},{6,7},{7,6},{8,9},{9,8},{10,11... | collective-permute-start | bytes 1622024 | tf_op jit(solution)/shard_map/ppermute | solution.py:201
  51.5 10.1 %collective-permute-start.18 = (bf16[32,4224]{1,0:T(8,128)(2,1)S(1)}, bf16[32,4224]{1,0:T(8,128)(2,1)S(1)}, u32[]{:S(2)}, u32[]{:S(2)}) collective-permute-start(bf16[32,4224]{1,0:T(8,128)(2,1)S(1)} %slice.105), channel_id=1, source_target_pairs={{0,2},{1,3},{4,0},{5,1},{8,4},{9,5},{12,8},{13,9},{14,12},{15,13},... | collective-permute-start | bytes 811016 | tf_op jit(solution)/shard_map/ppermute | solution.py:219
  53.1 8.6 %collective-permute-start.17 = (bf16[32,4224]{1,0:T(8,128)(2,1)S(1)}, bf16[32,4224]{1,0:T(8,128)(2,1)S(1)}, u32[]{:S(2)}, u32[]{:S(2)}) collective-permute-start(bf16[32,4224]{1,0:T(8,128)(2,1)S(1)} %slice.104), channel_id=1, source_target_pairs={{0,4},{1,5},{4,8},{5,9},{8,12},{9,13},{12,14},{13,15},{14,10},{15,... | collective-permute-start | bytes 811016 | tf_op jit(solution)/shard_map/ppermute | solution.py:218
  62.2 33.4 %collective-permute-start.6 = (bf16[128,4096]{1,0:T(8,128)(2,1)S(1)}, bf16[128,4096]{1,0:T(8,128)(2,1)S(1)}, u32[]{:S(2)}, u32[]{:S(2)}) collective-permute-start(bf16[128,4096]{1,0:T(8,128)(2,1)S(1)} %get-tuple-element.44), channel_id=1, source_target_pairs={{0,1},{1,0},{2,3},{3,2},{4,5},{5,4},{6,7},{7,6},{8,9},{9,8},{10,11... | collective-permute-start | bytes 3145736 | tf_op jit(solution)/shard_map/ppermute | solution.py:205
  62.3 18.7 %collective-permute-start.11 = (bf16[128,4096]{1,0:T(8,128)(2,1)S(1)}, bf16[128,4096]{1,0:T(8,128)(2,1)S(1)}, u32[]{:S(2)}, u32[]{:S(2)}) collective-permute-start(bf16[128,4096]{1,0:T(8,128)(2,1)S(1)} %get-tuple-element.48), channel_id=1, source_target_pairs={{0,1},{1,0},{2,3},{3,2},{4,5},{5,4},{6,7},{7,6},{8,9},{9,8},{10,11... | collective-permute-start | bytes 3145736 | tf_op jit(solution)/shard_map/ppermute | solution.py:205
  62.7 6.2 %collective-permute-start.24 = (bf16[32,4096]{1,0:T(8,128)(2,1)S(1)}, bf16[32,4096]{1,0:T(8,128)(2,1)S(1)}, u32[]{:S(2)}, u32[]{:S(2)}) collective-permute-start(bf16[32,4096]{1,0:T(8,128)(2,1)S(1)} %get-tuple-element.57), channel_id=1, source_target_pairs={{0,1},{1,0},{2,3},{3,2},{4,5},{5,4},{6,7},{7,6},{8,9},{9,8},{10,11... | collective-permute-start | bytes 786440 | tf_op jit(solution)/shard_map/ppermute | solution.py:205
  63.3 6.1 %collective-permute-start.26 = (bf16[32,4096]{1,0:T(8,128)(2,1)S(1)}, bf16[32,4096]{1,0:T(8,128)(2,1)S(1)}, u32[]{:S(2)}, u32[]{:S(2)}) collective-permute-start(bf16[32,4096]{1,0:T(8,128)(2,1)S(1)} %get-tuple-element.58), channel_id=1, source_target_pairs={{0,1},{1,0},{2,3},{3,2},{4,5},{5,4},{6,7},{7,6},{8,9},{9,8},{10,11... | collective-permute-start | bytes 786440 | tf_op jit(solution)/shard_map/ppermute | solution.py:205
  63.6 25.1 %collective-permute-start.16 = (bf16[64,4096]{1,0:T(8,128)(2,1)S(1)}, bf16[64,4096]{1,0:T(8,128)(2,1)S(1)}, u32[]{:S(2)}, u32[]{:S(2)}) collective-permute-start(bf16[64,4096]{1,0:T(8,128)(2,1)S(1)} %get-tuple-element.52), channel_id=1, source_target_pairs={{0,1},{1,0},{2,3},{3,2},{4,5},{5,4},{6,7},{7,6},{8,9},{9,8},{10,11... | collective-permute-start | bytes 1572872 | tf_op jit(solution)/shard_map/ppermute | solution.py:205
  69.5 8.4 %collective-permute-start.25 = (bf16[32,4096]{1,0:T(8,128)(2,1)S(1)}, bf16[32,4096]{1,0:T(8,128)(2,1)S(1)}, u32[]{:S(2)}, u32[]{:S(2)}) collective-permute-start(bf16[32,4096]{1,0:T(8,128)(2,1)S(1)} %get-tuple-element.82), channel_id=1, source_target_pairs={{0,4},{1,5},{4,8},{5,9},{8,12},{9,13},{12,14},{13,15},{14,10},{15,... | collective-permute-start | bytes 786440 | tf_op jit(solution)/shard_map/ppermute | solution.py:236
  70.9 8.6 %collective-permute-start.27 = (bf16[32,4096]{1,0:T(8,128)(2,1)S(1)}, bf16[32,4096]{1,0:T(8,128)(2,1)S(1)}, u32[]{:S(2)}, u32[]{:S(2)}) collective-permute-start(bf16[32,4096]{1,0:T(8,128)(2,1)S(1)} %get-tuple-element.81), channel_id=1, source_target_pairs={{0,2},{1,3},{4,0},{5,1},{8,4},{9,5},{12,8},{13,9},{14,12},{15,13},... | collective-permute-start | bytes 786440 | tf_op jit(solution)/shard_map/ppermute | solution.py:236
  77.9 9.2 %collective-permute-start.22 = (bf16[32,4096]{1,0:T(8,128)(2,1)S(1)}, bf16[32,4096]{1,0:T(8,128)(2,1)S(1)}, u32[]{:S(2)}, u32[]{:S(2)}) collective-permute-start(bf16[32,4096]{1,0:T(8,128)(2,1)S(1)} %get-tuple-element.84), channel_id=1, source_target_pairs={{0,4},{1,5},{4,8},{5,9},{8,12},{9,13},{12,14},{13,15},{14,10},{15,... | collective-permute-start | bytes 786440 | tf_op jit(solution)/shard_map/ppermute | solution.py:236
  79.5 9.2 %collective-permute-start.23 = (bf16[32,4096]{1,0:T(8,128)(2,1)S(1)}, bf16[32,4096]{1,0:T(8,128)(2,1)S(1)}, u32[]{:S(2)}, u32[]{:S(2)}) collective-permute-start(bf16[32,4096]{1,0:T(8,128)(2,1)S(1)} %get-tuple-element.83), channel_id=1, source_target_pairs={{0,2},{1,3},{4,0},{5,1},{8,4},{9,5},{12,8},{13,9},{14,12},{15,13},... | collective-permute-start | bytes 786440 | tf_op jit(solution)/shard_map/ppermute | solution.py:236
  81.2 11.5 %collective-permute-start.30 = (bf16[32,4096]{1,0:T(8,128)(2,1)S(1)}, bf16[32,4096]{1,0:T(8,128)(2,1)S(1)}, u32[]{:S(2)}, u32[]{:S(2)}) collective-permute-start(bf16[32,4096]{1,0:T(8,128)(2,1)S(1)} %get-tuple-element.76), channel_id=1, source_target_pairs={{0,4},{1,5},{4,8},{5,9},{8,12},{9,13},{12,14},{13,15},{14,10},{15,... | collective-permute-start | bytes 786440 | tf_op jit(solution)/shard_map/ppermute | solution.py:236
  87.1 8.5 %collective-permute-start.31 = (bf16[32,4096]{1,0:T(8,128)(2,1)S(1)}, bf16[32,4096]{1,0:T(8,128)(2,1)S(1)}, u32[]{:S(2)}, u32[]{:S(2)}) collective-permute-start(bf16[32,4096]{1,0:T(8,128)(2,1)S(1)} %get-tuple-element.75), channel_id=1, source_target_pairs={{0,2},{1,3},{4,0},{5,1},{8,4},{9,5},{12,8},{13,9},{14,12},{15,13},... | collective-permute-start | bytes 786440 | tf_op jit(solution)/shard_map/ppermute | solution.py:236
  88.9 7.7 %collective-permute-start.28 = (bf16[32,4096]{1,0:T(8,128)(2,1)S(1)}, bf16[32,4096]{1,0:T(8,128)(2,1)S(1)}, u32[]{:S(2)}, u32[]{:S(2)}) collective-permute-start(bf16[32,4096]{1,0:T(8,128)(2,1)S(1)} %get-tuple-element.78), channel_id=1, source_target_pairs={{0,4},{1,5},{4,8},{5,9},{8,12},{9,13},{12,14},{13,15},{14,10},{15,... | collective-permute-start | bytes 786440 | tf_op jit(solution)/shard_map/ppermute | solution.py:236
  89.4 9.4 %collective-permute-start.29 = (bf16[32,4096]{1,0:T(8,128)(2,1)S(1)}, bf16[32,4096]{1,0:T(8,128)(2,1)S(1)}, u32[]{:S(2)}, u32[]{:S(2)}) collective-permute-start(bf16[32,4096]{1,0:T(8,128)(2,1)S(1)} %get-tuple-element.77), channel_id=1, source_target_pairs={{0,2},{1,3},{4,0},{5,1},{8,4},{9,5},{12,8},{13,9},{14,12},{15,13},... | collective-permute-start | bytes 786440 | tf_op jit(solution)/shard_map/ppermute | solution.py:236
  99.0 6.4 %collective-permute-start.32 = (bf16[32,4096]{1,0:T(8,128)(2,1)S(1)}, bf16[32,4096]{1,0:T(8,128)(2,1)S(1)}, u32[]{:S(2)}, u32[]{:S(2)}) collective-permute-start(bf16[32,4096]{1,0:T(8,128)(2,1)S(1)} %get-tuple-element.72), channel_id=1, source_target_pairs={{0,4},{1,5},{4,8},{5,9},{8,12},{9,13},{12,14},{13,15},{14,10},{15,... | collective-permute-start | bytes 786440 | tf_op jit(solution)/shard_map/ppermute | solution.py:236
  99.5 8.0 %collective-permute-start.33 = (bf16[32,4096]{1,0:T(8,128)(2,1)S(1)}, bf16[32,4096]{1,0:T(8,128)(2,1)S(1)}, u32[]{:S(2)}, u32[]{:S(2)}) collective-permute-start(bf16[32,4096]{1,0:T(8,128)(2,1)S(1)} %get-tuple-element.71), channel_id=1, source_target_pairs={{0,2},{1,3},{4,0},{5,1},{8,4},{9,5},{12,8},{13,9},{14,12},{15,13},... | collective-permute-start | bytes 786440 | tf_op jit(solution)/shard_map/ppermute | solution.py:236
  101.1 8.7 %collective-permute-start.1 = (bf16[64,4096]{1,0:T(8,128)(2,1)S(1)}, bf16[64,4096]{1,0:T(8,128)(2,1)S(1)}, u32[]{:S(2)}, u32[]{:S(2)}) collective-permute-start(bf16[64,4096]{1,0:T(8,128)(2,1)S(1)} %get-tuple-element.40), channel_id=1, source_target_pairs={{0,1},{1,0},{2,3},{3,2},{4,5},{5,4},{6,7},{7,6},{8,9},{9,8},{10,11... | collective-permute-start | bytes 1572872 | tf_op jit(solution)/shard_map/ppermute | solution.py:205
  101.1 12.1 %collective-permute-start.35 = (bf16[32,4096]{1,0:T(8,128)(2,1)S(1)}, bf16[32,4096]{1,0:T(8,128)(2,1)S(1)}, u32[]{:S(2)}, u32[]{:S(2)}) collective-permute-start(bf16[32,4096]{1,0:T(8,128)(2,1)S(1)} %get-tuple-element.73), channel_id=1, source_target_pairs={{0,2},{1,3},{4,0},{5,1},{8,4},{9,5},{12,8},{13,9},{14,12},{15,13},... | collective-permute-start | bytes 786440 | tf_op jit(solution)/shard_map/ppermute | solution.py:236
  102.7 10.5 %collective-permute-start.36 = (bf16[32,4096]{1,0:T(8,128)(2,1)S(1)}, bf16[32,4096]{1,0:T(8,128)(2,1)S(1)}, u32[]{:S(2)}, u32[]{:S(2)}) collective-permute-start(bf16[32,4096]{1,0:T(8,128)(2,1)S(1)} %get-tuple-element.74), channel_id=1, source_target_pairs={{0,4},{1,5},{4,8},{5,9},{8,12},{9,13},{12,14},{13,15},{14,10},{15,... | collective-permute-start | bytes 786440 | tf_op jit(solution)/shard_map/ppermute | solution.py:236
  107.7 9.0 %collective-permute-start.34 = (bf16[32,4096]{1,0:T(8,128)(2,1)S(1)}, bf16[32,4096]{1,0:T(8,128)(2,1)S(1)}, u32[]{:S(2)}, u32[]{:S(2)}) collective-permute-start(bf16[32,4096]{1,0:T(8,128)(2,1)S(1)} %get-tuple-element.69), channel_id=1, source_target_pairs={{0,4},{1,5},{4,8},{5,9},{8,12},{9,13},{12,14},{13,15},{14,10},{15,... | collective-permute-start | bytes 786440 | tf_op jit(solution)/shard_map/ppermute | solution.py:236
  107.8 9.3 %collective-permute-start.37 = (bf16[32,4096]{1,0:T(8,128)(2,1)S(1)}, bf16[32,4096]{1,0:T(8,128)(2,1)S(1)}, u32[]{:S(2)}, u32[]{:S(2)}) collective-permute-start(bf16[32,4096]{1,0:T(8,128)(2,1)S(1)} %get-tuple-element.70), channel_id=1, source_target_pairs={{0,2},{1,3},{4,0},{5,1},{8,4},{9,5},{12,8},{13,9},{14,12},{15,13},... | collective-permute-start | bytes 786440 | tf_op jit(solution)/shard_map/ppermute | solution.py:236
  (8 other events, 35.1 us)

commit v6 on v4

v6 whole, which is shorter than its diff:
```python
import functools

import jax
import jax.numpy as jnp
from jax import lax
from jax.experimental import pallas as pl
from jax.experimental.pallas import tpu as pltpu
from jax.sharding import PartitionSpec as P

DENOMINATOR = 32768.0
LANES = 128
UNIT_CHUNK = 256
WIDTH_CHUNK = 1024
ANYWHERE = pl.BlockSpec(memory_space=pl.ANY)
VMEM = pl.BlockSpec(memory_space=pltpu.VMEM)
SMEM = pl.BlockSpec(memory_space=pltpu.SMEM)


def ring_of(chips):
    if chips == 8:
        return [0, 2, 4, 6, 7, 5, 3, 1]
    return list(range(chips))


def limits(mebibytes):
    return pltpu.CompilerParams(vmem_limit_bytes=mebibytes << 20)


def pack_kernel(experts, core, tokens, routes, gate_num, first, second, digits):
    rows, width = tokens.shape
    half = rows // 2
    lane = lax.broadcasted_iota(jnp.int32, (rows, LANES), 1)
    expert = jnp.where(lane < experts, lane, lane - experts)
    dense = jnp.zeros((rows, LANES), jnp.int32)
    for pick in range(routes.shape[1]):
        column = slice(pick, pick + 1)
        dense += jnp.where(routes[:, column] == expert, gate_num[:, column], 0)
    digit = jnp.where(lane < experts, dense >> 8, dense & 255)
    digit = jnp.where(lane < 2 * experts, digit, 0)
    digits[...] = digit.astype(jnp.float32).astype(jnp.bfloat16)
    for packed, place in ((first, core[0]), (second, 1 - core[0])):
        here = pl.ds(pl.multiple_of(place * half, half), half)
        packed[:, :width] = tokens[here]
        packed[:, width:] = digits[here]


def pack(core, tokens, routes, gate_num, experts):
    rows, width = tokens.shape
    return pl.pallas_call(
        functools.partial(pack_kernel, experts),
        in_specs=[SMEM] + [VMEM] * 3,
        out_specs=[VMEM] * 2,
        out_shape=[jax.ShapeDtypeStruct((rows // 2, width + LANES), jnp.bfloat16)] * 2,
        scratch_shapes=[pltpu.VMEM((rows, LANES), jnp.bfloat16)],
        compiler_params=limits(4),
        name="pack",
    )(core, tokens, routes, gate_num)


def keep_kernel(gate_up, down, gate_up_here, down_here, sem):
    copies = [
        pltpu.make_async_copy(gate_up, gate_up_here, sem.at[0]),
        pltpu.make_async_copy(down, down_here, sem.at[1]),
    ]
    for copy in copies:
        copy.start()
    for copy in copies:
        copy.wait()


def keep(gate_up_w, down_w):
    return pl.pallas_call(
        keep_kernel,
        in_specs=[ANYWHERE] * 2,
        out_specs=[VMEM] * 2,
        out_shape=[pltpu.VMEM(w.shape, w.dtype) for w in (gate_up_w, down_w)],
        scratch_shapes=[pltpu.SemaphoreType.DMA((2,))],
        compiler_params=limits(1),
        cost_estimate=pl.CostEstimate(
            flops=0, bytes_accessed=2 * (gate_up_w.size + down_w.size), transcendentals=0
        ),
        name="keep",
    )(*(pltpu.with_memory_space_constraint(w, pltpu.HBM) for w in (gate_up_w, down_w)))


def expert_kernel(count, *refs):
    xs = refs[:count]
    pick, gate_up_s, down_s, gate_up, down = refs[count : count + 5]
    outs = refs[count + 5 : -2]
    x, hidden = refs[-2:]
    units, width = down.shape

    at = 0
    for ref in xs:
        x[at : at + ref.shape[0]] = ref[...]
        at += ref.shape[0]
    digits = x[:, width:].astype(jnp.float32)
    weight = jnp.sum(digits * pick[...], axis=1, keepdims=True) / DENOMINATOR

    def unit_step(chunk, carry):
        sides = []
        for side in range(2):
            columns = pl.ds(pl.multiple_of(side * units + chunk * UNIT_CHUNK, UNIT_CHUNK), UNIT_CHUNK)
            part = jnp.dot(x[:, :width], gate_up[:, columns], preferred_element_type=jnp.float32)
            sides.append(part * gate_up_s[:, columns])
        here = pl.ds(pl.multiple_of(chunk * UNIT_CHUNK, UNIT_CHUNK), UNIT_CHUNK)
        hidden[:, here] = (jax.nn.silu(sides[0]) * sides[1]).astype(jnp.bfloat16)
        return carry

    lax.fori_loop(0, units // UNIT_CHUNK, unit_step, 0)

    def width_step(chunk, carry):
        columns = pl.ds(pl.multiple_of(chunk * WIDTH_CHUNK, WIDTH_CHUNK), WIDTH_CHUNK)
        part = jnp.dot(hidden[...], down[:, columns], preferred_element_type=jnp.float32)
        part = (part * down_s[:, columns] * weight).astype(jnp.bfloat16)
        at = 0
        for ref in outs:
            ref[:, columns] = part[at : at + ref.shape[0]]
            at += ref.shape[0]
        return carry

    lax.fori_loop(0, width // WIDTH_CHUNK, width_step, 0)


def expert_part(blocks, out_rows, hint, pick, gate_up_w, gate_up_s, down_w, down_s):
    width, units2 = gate_up_w.shape
    units = down_w.shape[0]
    rows, packed_width = sum(block.shape[0] for block in blocks), blocks[0].shape[1]
    flops = int(hint * 2 * rows * width * (units2 + units))
    return pl.pallas_call(
        functools.partial(expert_kernel, len(blocks)),
        in_specs=[VMEM] * (len(blocks) + 5),
        out_specs=[VMEM] * len(out_rows),
        out_shape=[jax.ShapeDtypeStruct((size, width), jnp.bfloat16) for size in out_rows],
        scratch_shapes=[
            pltpu.VMEM((rows, packed_width), jnp.bfloat16),
            pltpu.VMEM((rows, units), jnp.bfloat16),
        ],
        compiler_params=limits(14),
        cost_estimate=pl.CostEstimate(flops=flops, bytes_accessed=0, transcendentals=0),
        name="expert",
    )(
        *blocks,
        pick,
        gate_up_s,
        down_s,
        pltpu.with_memory_space_constraint(gate_up_w, pltpu.VMEM),
        pltpu.with_memory_space_constraint(down_w, pltpu.VMEM),
    )


def step_kernel(starts, rows, *refs):
    *terms, out = refs
    for column in range(0, out.shape[1], WIDTH_CHUNK):
        columns = slice(column, column + WIDTH_CHUNK)
        total = 0.0
        for ref, start in zip(terms, starts):
            total += ref[start : start + rows, columns].astype(jnp.float32)
        out[:, columns] = total.astype(jnp.bfloat16)


def step_sum(terms, rows):
    arrays, starts = zip(*terms)
    return pl.pallas_call(
        functools.partial(step_kernel, starts, rows),
        in_specs=[VMEM] * len(arrays),
        out_specs=VMEM,
        out_shape=jax.ShapeDtypeStruct((rows, arrays[0].shape[1]), jnp.bfloat16),
        compiler_params=limits(4),
        name="step_sum",
    )(*arrays)


def last_kernel(core, mine, theirs, *refs):
    *arrived, out = refs
    half = out.shape[0] // 2
    for which, place in ((0, core[0]), (1, 1 - core[0])):
        there = pl.ds(pl.multiple_of(place * half, half), half)
        here = slice(which * half, (which + 1) * half)
        for column in range(0, out.shape[1], WIDTH_CHUNK):
            columns = slice(column, column + WIDTH_CHUNK)
            total = mine[here, columns].astype(jnp.float32) + theirs[here, columns].astype(jnp.float32)
            for ref in arrived[2 * which : 2 * which + 2]:
                total += ref[:, columns].astype(jnp.float32)
            out[there, columns] = total.astype(jnp.bfloat16)


def last_sum(core, mine, theirs, *arrived):
    return pl.pallas_call(
        last_kernel,
        in_specs=[SMEM] + [VMEM] * (2 + len(arrived)),
        out_specs=VMEM,
        out_shape=jax.ShapeDtypeStruct(mine.shape, jnp.bfloat16),
        compiler_params=limits(4),
        name="last_sum",
    )(core, mine, theirs, *arrived)


def together(*values):
    return lax.optimization_barrier(values)


def after(value, *others):
    return together(value, *others)[0] if others else value


def body(tokens, routes, gate_num, gate_up_q, gate_up_scale, down_q, down_scale):
    devices = lax.axis_size("expert")
    expert = lax.axis_index("expert")
    chips = devices // 2
    reach = chips // 2
    rows, width = tokens.shape
    half = rows // 2
    ring = ring_of(chips)

    def hop(shift, cross):
        pairs = []
        for place in range(chips):
            for core, way in ((0, shift), (1, -shift)):
                to = ring[(place + way) % chips]
                pairs.append((2 * ring[place] + core, 2 * to + (core ^ cross)))
        return pairs

    on, to_other, back_to_other = hop(1, 0), hop(-1, 1), hop(1, 1)
    swap = [(i, i ^ 1) for i in range(devices)]
    send = functools.partial(lax.ppermute, axis_name="expert")

    lane = jnp.arange(LANES, dtype=jnp.int32)
    pick = jnp.where(lane == expert, 256.0, jnp.where(lane == devices + expert, 1.0, 0.0))
    pick = pick.astype(jnp.float32)[None, :]
    core = (expert & 1).astype(jnp.int32)[None]
    gate_up_w, down_w = keep(gate_up_q[0], down_q[0])
    weights = (pick, gate_up_w, gate_up_scale, down_w, down_scale)

    kept, given = {}, {}

    def run(distance, blocks, hint):
        tie = kept.get(distance - 1)
        others = [send(after(block, tie), perm=swap) for block in blocks]
        heights = [block.shape[0] for block in blocks]
        kept[distance], *cuts = expert_part(others + blocks, (sum(heights), *heights), hint, *weights)
        given[distance] = [send(cut, perm=swap) for cut in cuts]

    first, second = pack(core, tokens, routes, gate_num, devices)
    others = [send(block, perm=swap) for block in (first, second)]
    kept[0], cut = expert_part([first, second] + others, (rows, rows), 2, *weights)
    given[0] = send(cut, perm=swap)
    long = jnp.concatenate([send(first, perm=on), send(second, perm=to_other)], axis=0)
    short = jnp.concatenate([send(second, perm=on), send(first, perm=to_other)], axis=0)
    run(1, [long, short], 2)
    for distance in range(2, reach):
        tie = kept[distance - 2]
        long, short = send(after(long, tie), perm=on), send(after(short, tie), perm=on)
        run(distance, [long, short], 2)
    long = send(after(long, kept[reach - 2]), perm=on)
    run(reach, [long], 2)

    def terms(distance, number):
        return [(kept[distance], number * rows), (given[distance][number], 0)]

    short = send(step_sum(terms(reach - 1, 1), rows), perm=on)
    long = send(step_sum(terms(reach, 0), rows), perm=on)
    for distance in range(reach - 1, 1, -1):
        if distance < reach - 1:
            short = send(step_sum(terms(distance, 1) + [(short, 0)], rows), perm=on)
        long = send(step_sum(terms(distance, 0) + [(long, 0)], rows), perm=on)

    def arrive(carried, number):
        pieces = []
        for start, perm in ((0, back_to_other), (half, on)):
            (kept_1, at), (given_1, _) = terms(1, number)
            pieces.append(send(step_sum([(kept_1, at + start), (given_1, start), (carried, start)], half), perm=perm))
        return pieces

    short_cross, short_same = arrive(short, 1)
    long_cross, long_same = arrive(long, 0)
    return last_sum(core, kept[0], given[0], short_same, long_cross, long_same, short_cross)


def solution(mesh):
    in_specs = (
        P(("groups", "expert"), None),
        P(("groups", "expert"), None),
        P(("groups", "expert"), None),
        P("expert", None, None),
        P("expert", None),
        P("expert", None, None),
        P("expert", None),
    )
    out_specs = P(("groups", "expert"), None)
    return jax.shard_map(body, mesh=mesh, in_specs=in_specs, out_specs=out_specs, check_vma=False)
```

time: 131 us -> 113 us (0.86)
  waiting for transfers between devices: 66.3 us -> 45.6 us
  starting transfers between devices: 19.8 us -> 27.8 us
  Pallas kernels: 39.9 us -> 36.1 us
  other arithmetic: 3.27 us -> 0.01 us
  local copies, waits for them, and re-layouts: 1.28 us -> 2.7 us
    ppermute x30 -> x35, waiting for transfers between devices: 66.3 us -> 45.6 us  [the longest x2 10.9 us: body(): send(after(short, tie), perm=on)]
    ppermute x30 -> x35, starting transfers between devices: 19.8 us -> 27.8 us  [the longest x4 3.86 us: arrive(): send(step_sum([(kept_1, at + start), (given_1, start), (carried, start)],...]
    pallas_call x6 -> x17, Pallas kernels: 39.9 us -> 36.1 us  [the longest x5 27.2 us: expert_part(): pl.pallas_call(functools.partial(expert_kernel, len(blocks)), in_specs=[V...]
    unnamed x4 -> x10, local copies, waits for them, and re-layouts: 0.01 us -> 2.65 us
    convert_element_type x6 -> x0, other arithmetic: 2.52 us -> none  [the longest x5 2.5 us: add(): return total.astype(jnp.bfloat16)]
  transfers between devices with their start and end apart: 30 -> 35, of which waited for: 15 -> 16; matrix products, arithmetic and copies ran while one was open for 1% -> 0% of each run, Pallas kernels for 27% -> 27%
where the time goes in v6:
time: 113 us; the launch traced here: 112 us
  waiting for transfers between devices  45.6 us (40%)
  Pallas kernels  36.1 us (32%)
  starting transfers between devices  27.8 us (25%)
  local copies, waits for them, and re-layouts  2.7 us (2%)
    pallas_call x5, Pallas kernels, expert_part(): pl.pallas_call(functools.partial(expert_kernel, len(blocks)), in_specs=[V...  27.2 us
    ppermute x2, waiting for transfers between devices, body(): send(after(short, tie), perm=on)  10.9 us
    ppermute x4, waiting for transfers between devices, arrive(): send(step_sum([(kept_1, at + start), (given_1, start), (carried, start)],...  8.87 us
    ppermute x2, waiting for transfers between devices, body(): long = send(step_sum(terms(distance, 0) + [(long, 0)], rows), perm=on)  7.49 us
    pallas_call x1, Pallas kernels, keep(): pl.pallas_call(keep_kernel, in_specs=[ANYWHERE] * 2, out_specs=[VMEM] * 2...  6.38 us
    ppermute x1, waiting for transfers between devices, body(): long = send(step_sum(terms(reach, 0), rows), perm=on)  5.82 us
    ppermute x4, starting transfers between devices, arrive(): send(step_sum([(kept_1, at + start), (given_1, start), (carried, start)],...  3.86 us
    ppermute x1, waiting for transfers between devices, body(): short = send(step_sum(terms(distance, 1) + [(short, 0)], rows), perm=on)  3.79 us
  transfers between devices with their start and end apart: 35, of which 16 were waited for; matrix products, arithmetic and copies ran while one was open for 0% of the time, Pallas kernels for 27%

profile of v6, /device:TPU:0, one launch (start us, length us, event | category | flops | bytes accessed | tf_op | source)
XLA Modules:
  0.0 112.4 jit_solution(6069430699174243810)
XLA Ops:
  2.8 3.1 %collective-permute-start.3 = (bf16[32,4224]{1,0:T(8,128)(2,1)S(1)}, bf16[32,4224]{1,0:T(8,128)(2,1)S(1)}, u32[]{:S(2)}, u32[]{:S(2)}) collective-permute-start(bf16[32,4224]{1,0:T(8,128)(2,1)S(1)} %get-tuple-element.29.refs_0_), channel_id=1, source_target_pairs={{0,4},{1,3},{4,8},{5,1},{8,12},{9,5},{12,14},{13,9},{14,10},{15,13... | collective-permute-start | bytes 811016 | tf_op jit(solution)/shard_map/ppermute | solution.py:248
  8.1 6.4 %keep.1 = (bf16[4096,1536]{1,0:T(8,128)(2,1)S(1)}, bf16[768,4096]{1,0:T(8,128)(2,1)S(1)}) custom-call(bf16[4096,1536]{1,0:T(8,128)(2,1)} %bitcast.3, bf16[768,4096]{1,0:T(8,128)(2,1)} %bitcast.4), custom_call_target="tpu_custom_call" | custom-call | bytes 18874368 | tf_op jit(solution)/shard_map/keep/pallas_call | solution.py:72
  15.3 4.0 %expert.5 = (bf16[64,4096]{1,0:T(8,128)(2,1)S(1)}, bf16[64,4096]{1,0:T(8,128)(2,1)S(1)}) custom-call(bf16[32,4224]{1,0:T(8,128)(2,1)S(1)} %get-tuple-element.29.refs_0_, bf16[32,4224]{1,0:T(8,128)(2,1)S(1)} %get-tuple-element.30.refs_1_, bf16[32,4224]{1,0:T(8,128)(2,1)S(1)} %collective-permute-done.refs_2_, ...), custom_call_target="tpu_custom_call" | custom-call | flops 4831838208 | tf_op jit(solution)/shard_map/expert/pallas_call | solution.py:130
  19.3 1.1 collective-permute-start.5
  20.7 1.6 %collective-permute-start.10 = (bf16[64,4224]{1,0:T(8,128)(2,1)S(1)}, bf16[64,4224]{1,0:T(8,128)(2,1)S(1)}, u32[]{:S(2)}, u32[]{:S(2)}) collective-permute-start(bf16[64,4224]{1,0:T(8,128)(2,1)S(1)} %constant_dynamic-update-slice_fusion.refs_2_), channel_id=1, source_target_pairs={{0,4},{1,3},{4,8},{5,1},{8,12},{9,5},{12,14},{13,9},{14,10},{15,13... | collective-permute-start | bytes 1622024 | tf_op jit(solution)/shard_map/ppermute | solution.py:253
  22.3 1.6 %collective-permute-start.12 = (bf16[64,4224]{1,0:T(8,128)(2,1)S(1)}, bf16[64,4224]{1,0:T(8,128)(2,1)S(1)}, u32[]{:S(2)}, u32[]{:S(2)}) collective-permute-start(bf16[64,4224]{1,0:T(8,128)(2,1)S(1)} %constant_dynamic-update-slice_fusion.2.refs_3_), channel_id=1, source_target_pairs={{0,4},{1,3},{4,8},{5,1},{8,12},{9,5},{12,14},{13,9},{14,10},{15,13... | collective-permute-start | bytes 1622024 | tf_op jit(solution)/shard_map/ppermute | solution.py:253
  23.9 6.4 %expert.6 = (bf16[128,4096]{1,0:T(8,128)(2,1)S(1)}, bf16[64,4096]{1,0:T(8,128)(2,1)S(1)}, bf16[64,4096]{1,0:T(8,128)(2,1)S(1)}) custom-call(bf16[64,4224]{1,0:T(8,128)(2,1)S(1)} %collective-permute-done.5.refs_0_, bf16[64,4224]{1,0:T(8,128)(2,1)S(1)} %collective-permute-done.8.refs_1_, bf16[64,4224]{1,0:T(8,128)(2,1)S(1)} %constant_dynamic-update-slice_fusion.refs_2_, ...), custom_call_target="tpu_custom_call" | custom-call | flops 9663676416 | tf_op jit(solution)/shard_map/expert/pallas_call | solution.py:130
  30.4 5.5 %collective-permute-done.12.refs_3_ = bf16[64,4224]{1,0:T(8,128)(2,1)S(1)} collective-permute-done((bf16[64,4224]{1,0:T(8,128)(2,1)S(1)}, bf16[64,4224]{1,0:T(8,128)(2,1)S(1)}, u32[]{:S(2)}, u32[]{:S(2)}) %collective-permute-start.12) | collective-permute-done | bytes 540704 | tf_op jit(solution)/shard_map/ppermute | solution.py:253
  35.9 1.6 %collective-permute-start.15 = (bf16[64,4224]{1,0:T(8,128)(2,1)S(1)}, bf16[64,4224]{1,0:T(8,128)(2,1)S(1)}, u32[]{:S(2)}, u32[]{:S(2)}) collective-permute-start(bf16[64,4224]{1,0:T(8,128)(2,1)S(1)} %collective-permute-done.10.refs_2_), channel_id=1, source_target_pairs={{0,4},{1,3},{4,8},{5,1},{8,12},{9,5},{12,14},{13,9},{14,10},{15,13... | collective-permute-start | bytes 1622024 | tf_op jit(solution)/shard_map/ppermute | solution.py:253
  37.5 1.6 %collective-permute-start.17 = (bf16[64,4224]{1,0:T(8,128)(2,1)S(1)}, bf16[64,4224]{1,0:T(8,128)(2,1)S(1)}, u32[]{:S(2)}, u32[]{:S(2)}) collective-permute-start(bf16[64,4224]{1,0:T(8,128)(2,1)S(1)} %collective-permute-done.12.refs_3_), channel_id=1, source_target_pairs={{0,4},{1,3},{4,8},{5,1},{8,12},{9,5},{12,14},{13,9},{14,10},{15,13... | collective-permute-start | bytes 1622024 | tf_op jit(solution)/shard_map/ppermute | solution.py:253
  39.1 6.4 %expert.7 = (bf16[128,4096]{1,0:T(8,128)(2,1)S(1)}, bf16[64,4096]{1,0:T(8,128)(2,1)S(1)}, bf16[64,4096]{1,0:T(8,128)(2,1)S(1)}) custom-call(bf16[64,4224]{1,0:T(8,128)(2,1)S(1)} %collective-permute-done.11.refs_0_, bf16[64,4224]{1,0:T(8,128)(2,1)S(1)} %collective-permute-done.13.refs_1_, bf16[64,4224]{1,0:T(8,128)(2,1)S(1)} %collective-permute-done.10.refs_2_, ...), custom_call_target="tpu_custom_call" | custom-call | flops 9663676416 | tf_op jit(solution)/shard_map/expert/pallas_call | solution.py:130
  45.6 5.5 %collective-permute-done.17.refs_3_ = bf16[64,4224]{1,0:T(8,128)(2,1)S(1)} collective-permute-done((bf16[64,4224]{1,0:T(8,128)(2,1)S(1)}, bf16[64,4224]{1,0:T(8,128)(2,1)S(1)}, u32[]{:S(2)}, u32[]{:S(2)}) %collective-permute-start.17) | collective-permute-done | bytes 540704 | tf_op jit(solution)/shard_map/ppermute | solution.py:253
  51.0 1.6 %collective-permute-start.26 = (bf16[64,4224]{1,0:T(8,128)(2,1)S(1)}, bf16[64,4224]{1,0:T(8,128)(2,1)S(1)}, u32[]{:S(2)}, u32[]{:S(2)}) collective-permute-start(bf16[64,4224]{1,0:T(8,128)(2,1)S(1)} %collective-permute-done.15.refs_2_), channel_id=1, source_target_pairs={{0,4},{1,3},{4,8},{5,1},{8,12},{9,5},{12,14},{13,9},{14,10},{15,13... | collective-permute-start | bytes 1622024 | tf_op jit(solution)/shard_map/ppermute | solution.py:255
  53.0 6.4 %expert.8 = (bf16[128,4096]{1,0:T(8,128)(2,1)S(1)}, bf16[64,4096]{1,0:T(8,128)(2,1)S(1)}, bf16[64,4096]{1,0:T(8,128)(2,1)S(1)}) custom-call(bf16[64,4224]{1,0:T(8,128)(2,1)S(1)} %collective-permute-done.16.refs_0_, bf16[64,4224]{1,0:T(8,128)(2,1)S(1)} %collective-permute-done.18.refs_1_, bf16[64,4224]{1,0:T(8,128)(2,1)S(1)} %collective-permute-done.15.refs_2_, ...), custom_call_target="tpu_custom_call" | custom-call | flops 9663676416 | tf_op jit(solution)/shard_map/expert/pallas_call | solution.py:130
  60.4 1.9 %collective-permute-done.27.refs_0_ = bf16[64,4224]{1,0:T(8,128)(2,1)S(1)} collective-permute-done((bf16[64,4224]{1,0:T(8,128)(2,1)S(1)}, bf16[64,4224]{1,0:T(8,128)(2,1)S(1)}, u32[]{:S(2)}, u32[]{:S(2)}) %collective-permute-start.27) | collective-permute-done | bytes 540704 | tf_op jit(solution)/shard_map/ppermute | solution.py:239
  62.3 3.9 %expert.9 = (bf16[64,4096]{1,0:T(8,128)(2,1)S(1)}, bf16[64,4096]{1,0:T(8,128)(2,1)S(1)}) custom-call(bf16[64,4224]{1,0:T(8,128)(2,1)S(1)} %collective-permute-done.27.refs_0_, bf16[64,4224]{1,0:T(8,128)(2,1)S(1)} %collective-permute-done.26.refs_1_, f32[1,128]{1,0:T(1,128)S(1)} %compare_select_fusion.1.refs_4_.refs_2_, f32[1,1536]{1,0:T(1,128)S(1)} %copy-done.2, ...), custom_call_target="tpu_custom_call" | custom-call | flops 4831838208 | tf_op jit(solution)/shard_map/expert/pallas_call | solution.py:130
  67.0 1.3 %collective-permute-done.28.refs_1_ = bf16[64,4096]{1,0:T(8,128)(2,1)S(1)} collective-permute-done((bf16[64,4096]{1,0:T(8,128)(2,1)S(1)}, bf16[64,4096]{1,0:T(8,128)(2,1)S(1)}, u32[]{:S(2)}, u32[]{:S(2)}) %collective-permute-start.28) | collective-permute-done | bytes 524320 | tf_op jit(solution)/shard_map/ppermute | solution.py:242
  68.4 1.6 %collective-permute-start.29 = (bf16[64,4096]{1,0:T(8,128)(2,1)S(1)}, bf16[64,4096]{1,0:T(8,128)(2,1)S(1)}, u32[]{:S(2)}, u32[]{:S(2)}) collective-permute-start(bf16[64,4096]{1,0:T(8,128)(2,1)S(1)} %step_sum.12), channel_id=1, source_target_pairs={{0,4},{1,3},{4,8},{5,1},{8,12},{9,5},{12,14},{13,9},{14,10},{15,13... | collective-permute-start | bytes 1572872 | tf_op jit(solution)/shard_map/ppermute | solution.py:262
  70.2 1.6 %collective-permute-start.20 = (bf16[64,4096]{1,0:T(8,128)(2,1)S(1)}, bf16[64,4096]{1,0:T(8,128)(2,1)S(1)}, u32[]{:S(2)}, u32[]{:S(2)}) collective-permute-start(bf16[64,4096]{1,0:T(8,128)(2,1)S(1)} %step_sum.9), channel_id=1, source_target_pairs={{0,4},{1,3},{4,8},{5,1},{8,12},{9,5},{12,14},{13,9},{14,10},{15,13... | collective-permute-start | bytes 1572872 | tf_op jit(solution)/shard_map/ppermute | solution.py:261
  71.8 5.8 %collective-permute-done.29.refs_2_ = bf16[64,4096]{1,0:T(8,128)(2,1)S(1)} collective-permute-done((bf16[64,4096]{1,0:T(8,128)(2,1)S(1)}, bf16[64,4096]{1,0:T(8,128)(2,1)S(1)}, u32[]{:S(2)}, u32[]{:S(2)}) %collective-permute-start.29) | collective-permute-done | bytes 524320 | tf_op jit(solution)/shard_map/ppermute | solution.py:262
  77.8 1.6 %collective-permute-start.30 = (bf16[64,4096]{1,0:T(8,128)(2,1)S(1)}, bf16[64,4096]{1,0:T(8,128)(2,1)S(1)}, u32[]{:S(2)}, u32[]{:S(2)}) collective-permute-start(bf16[64,4096]{1,0:T(8,128)(2,1)S(1)} %step_sum.13), channel_id=1, source_target_pairs={{0,4},{1,3},{4,8},{5,1},{8,12},{9,5},{12,14},{13,9},{14,10},{15,13... | collective-permute-start | bytes 1572872 | tf_op jit(solution)/shard_map/ppermute | solution.py:266
  79.5 3.8 %collective-permute-done.20.refs_2_ = bf16[64,4096]{1,0:T(8,128)(2,1)S(1)} collective-permute-done((bf16[64,4096]{1,0:T(8,128)(2,1)S(1)}, bf16[64,4096]{1,0:T(8,128)(2,1)S(1)}, u32[]{:S(2)}, u32[]{:S(2)}) %collective-permute-start.20) | collective-permute-done | bytes 524320 | tf_op jit(solution)/shard_map/ppermute | solution.py:261
  83.4 1.6 %collective-permute-start.21 = (bf16[64,4096]{1,0:T(8,128)(2,1)S(1)}, bf16[64,4096]{1,0:T(8,128)(2,1)S(1)}, u32[]{:S(2)}, u32[]{:S(2)}) collective-permute-start(bf16[64,4096]{1,0:T(8,128)(2,1)S(1)} %step_sum.10), channel_id=1, source_target_pairs={{0,4},{1,3},{4,8},{5,1},{8,12},{9,5},{12,14},{13,9},{14,10},{15,13... | collective-permute-start | bytes 1572872 | tf_op jit(solution)/shard_map/ppermute | solution.py:265
  85.1 3.8 %collective-permute-done.30.refs_2_ = bf16[64,4096]{1,0:T(8,128)(2,1)S(1)} collective-permute-done((bf16[64,4096]{1,0:T(8,128)(2,1)S(1)}, bf16[64,4096]{1,0:T(8,128)(2,1)S(1)}, u32[]{:S(2)}, u32[]{:S(2)}) %collective-permute-start.30) | collective-permute-done | bytes 524320 | tf_op jit(solution)/shard_map/ppermute | solution.py:266
  89.1 1.6 %collective-permute-start.31 = (bf16[64,4096]{1,0:T(8,128)(2,1)S(1)}, bf16[64,4096]{1,0:T(8,128)(2,1)S(1)}, u32[]{:S(2)}, u32[]{:S(2)}) collective-permute-start(bf16[64,4096]{1,0:T(8,128)(2,1)S(1)} %step_sum.14), channel_id=1, source_target_pairs={{0,4},{1,3},{4,8},{5,1},{8,12},{9,5},{12,14},{13,9},{14,10},{15,13... | collective-permute-start | bytes 1572872 | tf_op jit(solution)/shard_map/ppermute | solution.py:266
  90.7 3.8 %collective-permute-done.21.refs_2_ = bf16[64,4096]{1,0:T(8,128)(2,1)S(1)} collective-permute-done((bf16[64,4096]{1,0:T(8,128)(2,1)S(1)}, bf16[64,4096]{1,0:T(8,128)(2,1)S(1)}, u32[]{:S(2)}, u32[]{:S(2)}) %collective-permute-start.21) | collective-permute-done | bytes 524320 | tf_op jit(solution)/shard_map/ppermute | solution.py:265
  94.6 1.6 %collective-permute-start.22 = (bf16[32,4096]{1,0:T(8,128)(2,1)S(1)}, bf16[32,4096]{1,0:T(8,128)(2,1)S(1)}, u32[]{:S(2)}, u32[]{:S(2)}) collective-permute-start(bf16[32,4096]{1,0:T(8,128)(2,1)S(1)} %step_sum.11), channel_id=1, source_target_pairs={{0,4},{1,3},{4,8},{5,1},{8,12},{9,5},{12,14},{13,9},{14,10},{15,13... | collective-permute-start | bytes 786440 | tf_op jit(solution)/shard_map/ppermute | solution.py:272
  96.4 3.7 %collective-permute-done.31.refs_2_ = bf16[64,4096]{1,0:T(8,128)(2,1)S(1)} collective-permute-done((bf16[64,4096]{1,0:T(8,128)(2,1)S(1)}, bf16[64,4096]{1,0:T(8,128)(2,1)S(1)}, u32[]{:S(2)}, u32[]{:S(2)}) %collective-permute-start.31) | collective-permute-done | bytes 524320 | tf_op jit(solution)/shard_map/ppermute | solution.py:266
  100.8 1.6 %collective-permute-start.33 = (bf16[32,4096]{1,0:T(8,128)(2,1)S(1)}, bf16[32,4096]{1,0:T(8,128)(2,1)S(1)}, u32[]{:S(2)}, u32[]{:S(2)}) collective-permute-start(bf16[32,4096]{1,0:T(8,128)(2,1)S(1)} %step_sum.16), channel_id=1, source_target_pairs={{0,4},{1,3},{4,8},{5,1},{8,12},{9,5},{12,14},{13,9},{14,10},{15,13... | collective-permute-start | bytes 786440 | tf_op jit(solution)/shard_map/ppermute | solution.py:272
  102.9 2.0 %collective-permute-done.34.refs_3_ = bf16[32,4096]{1,0:T(8,128)(2,1)S(1)} collective-permute-done((bf16[32,4096]{1,0:T(8,128)(2,1)S(1)}, bf16[32,4096]{1,0:T(8,128)(2,1)S(1)}, u32[]{:S(2)}, u32[]{:S(2)}) %collective-permute-start.34) | collective-permute-done | bytes 262176 | tf_op jit(solution)/shard_map/ppermute | solution.py:272
  104.9 2.8 %collective-permute-done.32.refs_1_ = bf16[32,4096]{1,0:T(8,128)(2,1)S(1)} collective-permute-done((bf16[32,4096]{1,0:T(8,128)(2,1)S(1)}, bf16[32,4096]{1,0:T(8,128)(2,1)S(1)}, u32[]{:S(2)}, u32[]{:S(2)}) %collective-permute-start.32) | collective-permute-done | bytes 262176 | tf_op jit(solution)/shard_map/ppermute | solution.py:272
  107.7 3.6 %collective-permute-done.33.refs_2_ = bf16[32,4096]{1,0:T(8,128)(2,1)S(1)} collective-permute-done((bf16[32,4096]{1,0:T(8,128)(2,1)S(1)}, bf16[32,4096]{1,0:T(8,128)(2,1)S(1)}, u32[]{:S(2)}, u32[]{:S(2)}) %collective-permute-start.33) | collective-permute-done | bytes 262176 | tf_op jit(solution)/shard_map/ppermute | solution.py:272
  (68 shorter events, 11.8 us)
Async XLA Ops:
  2.8 11.6 %collective-permute-start.3 = (bf16[32,4224]{1,0:T(8,128)(2,1)S(1)}, bf16[32,4224]{1,0:T(8,128)(2,1)S(1)}, u32[]{:S(2)}, u32[]{:S(2)}) collective-permute-start(bf16[32,4224]{1,0:T(8,128)(2,1)S(1)} %get-tuple-element.29.refs_0_), channel_id=1, source_target_pairs={{0,4},{1,3},{4,8},{5,1},{8,12},{9,5},{12,14},{13,9},{14,10},{15,13... | collective-permute-start | bytes 811016 | tf_op jit(solution)/shard_map/ppermute | solution.py:248
  5.9 9.4 %collective-permute-start = (bf16[32,4224]{1,0:T(8,128)(2,1)S(1)}, bf16[32,4224]{1,0:T(8,128)(2,1)S(1)}, u32[]{:S(2)}, u32[]{:S(2)}) collective-permute-start(bf16[32,4224]{1,0:T(8,128)(2,1)S(1)} %get-tuple-element.29.refs_0_), channel_id=1, source_target_pairs={{0,1},{1,0},{2,3},{3,2},{4,5},{5,4},{6,7},{7,6},{8,9},{9,8},{10,11... | collective-permute-start | bytes 811016 | tf_op jit(solution)/shard_map/ppermute | solution.py:245
  5.9 9.4 %collective-permute-start.1 = (bf16[32,4224]{1,0:T(8,128)(2,1)S(1)}, bf16[32,4224]{1,0:T(8,128)(2,1)S(1)}, u32[]{:S(2)}, u32[]{:S(2)}) collective-permute-start(bf16[32,4224]{1,0:T(8,128)(2,1)S(1)} %get-tuple-element.30.refs_1_), channel_id=1, source_target_pairs={{0,1},{1,0},{2,3},{3,2},{4,5},{5,4},{6,7},{7,6},{8,9},{9,8},{10,11... | collective-permute-start | bytes 811016 | tf_op jit(solution)/shard_map/ppermute | solution.py:245
  6.4 8.8 %collective-permute-start.4 = (bf16[32,4224]{1,0:T(8,128)(2,1)S(1)}, bf16[32,4224]{1,0:T(8,128)(2,1)S(1)}, u32[]{:S(2)}, u32[]{:S(2)}) collective-permute-start(bf16[32,4224]{1,0:T(8,128)(2,1)S(1)} %get-tuple-element.30.refs_1_), channel_id=1, source_target_pairs={{0,3},{1,4},{4,1},{5,8},{8,5},{9,12},{12,9},{13,14},{14,13},{15,10... | collective-permute-start | bytes 811016 | tf_op jit(solution)/shard_map/ppermute | solution.py:248
  7.1 13.3 %collective-permute-start.6 = (bf16[32,4224]{1,0:T(8,128)(2,1)S(1)}, bf16[32,4224]{1,0:T(8,128)(2,1)S(1)}, u32[]{:S(2)}, u32[]{:S(2)}) collective-permute-start(bf16[32,4224]{1,0:T(8,128)(2,1)S(1)} %get-tuple-element.30.refs_1_), channel_id=1, source_target_pairs={{0,4},{1,3},{4,8},{5,1},{8,12},{9,5},{12,14},{13,9},{14,10},{15,13... | collective-permute-start | bytes 811016 | tf_op jit(solution)/shard_map/ppermute | solution.py:249
  14.5 6.0 %collective-permute-start.7 = (bf16[32,4224]{1,0:T(8,128)(2,1)S(1)}, bf16[32,4224]{1,0:T(8,128)(2,1)S(1)}, u32[]{:S(2)}, u32[]{:S(2)}) collective-permute-start(bf16[32,4224]{1,0:T(8,128)(2,1)S(1)} %get-tuple-element.29.refs_0_), channel_id=1, source_target_pairs={{0,3},{1,4},{4,1},{5,8},{8,5},{9,12},{12,9},{13,14},{14,13},{15,10... | collective-permute-start | bytes 811016 | tf_op jit(solution)/shard_map/ppermute | solution.py:249
  19.3 4.6 %collective-permute-start.5 = (bf16[64,4224]{1,0:T(8,128)(2,1)S(1)}, bf16[64,4224]{1,0:T(8,128)(2,1)S(1)}, u32[]{:S(2)}, u32[]{:S(2)}) collective-permute-start(bf16[64,4224]{1,0:T(8,128)(2,1)S(1)} %constant_dynamic-update-slice_fusion.refs_2_), channel_id=1, source_target_pairs={{0,1},{1,0},{2,3},{3,2},{4,5},{5,4},{6,7},{7,6},{8,9},{9,8},{10,11... | collective-permute-start | bytes 1622024 | tf_op jit(solution)/shard_map/ppermute | solution.py:239
  20.4 3.5 %collective-permute-start.8 = (bf16[64,4224]{1,0:T(8,128)(2,1)S(1)}, bf16[64,4224]{1,0:T(8,128)(2,1)S(1)}, u32[]{:S(2)}, u32[]{:S(2)}) collective-permute-start(bf16[64,4224]{1,0:T(8,128)(2,1)S(1)} %constant_dynamic-update-slice_fusion.2.refs_3_), channel_id=1, source_target_pairs={{0,1},{1,0},{2,3},{3,2},{4,5},{5,4},{6,7},{7,6},{8,9},{9,8},{10,11... | collective-permute-start | bytes 1622024 | tf_op jit(solution)/shard_map/ppermute | solution.py:239
  20.7 9.6 %collective-permute-start.10 = (bf16[64,4224]{1,0:T(8,128)(2,1)S(1)}, bf16[64,4224]{1,0:T(8,128)(2,1)S(1)}, u32[]{:S(2)}, u32[]{:S(2)}) collective-permute-start(bf16[64,4224]{1,0:T(8,128)(2,1)S(1)} %constant_dynamic-update-slice_fusion.refs_2_), channel_id=1, source_target_pairs={{0,4},{1,3},{4,8},{5,1},{8,12},{9,5},{12,14},{13,9},{14,10},{15,13... | collective-permute-start | bytes 1622024 | tf_op jit(solution)/shard_map/ppermute | solution.py:253
  22.3 13.6 %collective-permute-start.12 = (bf16[64,4224]{1,0:T(8,128)(2,1)S(1)}, bf16[64,4224]{1,0:T(8,128)(2,1)S(1)}, u32[]{:S(2)}, u32[]{:S(2)}) collective-permute-start(bf16[64,4224]{1,0:T(8,128)(2,1)S(1)} %constant_dynamic-update-slice_fusion.2.refs_3_), channel_id=1, source_target_pairs={{0,4},{1,3},{4,8},{5,1},{8,12},{9,5},{12,14},{13,9},{14,10},{15,13... | collective-permute-start | bytes 1622024 | tf_op jit(solution)/shard_map/ppermute | solution.py:253
  30.3 8.7 %collective-permute-start.11 = (bf16[64,4224]{1,0:T(8,128)(2,1)S(1)}, bf16[64,4224]{1,0:T(8,128)(2,1)S(1)}, u32[]{:S(2)}, u32[]{:S(2)}) collective-permute-start(bf16[64,4224]{1,0:T(8,128)(2,1)S(1)} %collective-permute-done.10.refs_2_), channel_id=1, source_target_pairs={{0,1},{1,0},{2,3},{3,2},{4,5},{5,4},{6,7},{7,6},{8,9},{9,8},{10,11... | collective-permute-start | bytes 1622024 | tf_op jit(solution)/shard_map/ppermute | solution.py:239
  35.9 3.2 %collective-permute-start.13 = (bf16[64,4224]{1,0:T(8,128)(2,1)S(1)}, bf16[64,4224]{1,0:T(8,128)(2,1)S(1)}, u32[]{:S(2)}, u32[]{:S(2)}) collective-permute-start(bf16[64,4224]{1,0:T(8,128)(2,1)S(1)} %collective-permute-done.12.refs_3_), channel_id=1, source_target_pairs={{0,1},{1,0},{2,3},{3,2},{4,5},{5,4},{6,7},{7,6},{8,9},{9,8},{10,11... | collective-permute-start | bytes 1622024 | tf_op jit(solution)/shard_map/ppermute | solution.py:239
  35.9 9.6 %collective-permute-start.15 = (bf16[64,4224]{1,0:T(8,128)(2,1)S(1)}, bf16[64,4224]{1,0:T(8,128)(2,1)S(1)}, u32[]{:S(2)}, u32[]{:S(2)}) collective-permute-start(bf16[64,4224]{1,0:T(8,128)(2,1)S(1)} %collective-permute-done.10.refs_2_), channel_id=1, source_target_pairs={{0,4},{1,3},{4,8},{5,1},{8,12},{9,5},{12,14},{13,9},{14,10},{15,13... | collective-permute-start | bytes 1622024 | tf_op jit(solution)/shard_map/ppermute | solution.py:253
  37.5 13.6 %collective-permute-start.17 = (bf16[64,4224]{1,0:T(8,128)(2,1)S(1)}, bf16[64,4224]{1,0:T(8,128)(2,1)S(1)}, u32[]{:S(2)}, u32[]{:S(2)}) collective-permute-start(bf16[64,4224]{1,0:T(8,128)(2,1)S(1)} %collective-permute-done.12.refs_3_), channel_id=1, source_target_pairs={{0,4},{1,3},{4,8},{5,1},{8,12},{9,5},{12,14},{13,9},{14,10},{15,13... | collective-permute-start | bytes 1622024 | tf_op jit(solution)/shard_map/ppermute | solution.py:253
  45.5 7.1 %collective-permute-start.16 = (bf16[64,4224]{1,0:T(8,128)(2,1)S(1)}, bf16[64,4224]{1,0:T(8,128)(2,1)S(1)}, u32[]{:S(2)}, u32[]{:S(2)}) collective-permute-start(bf16[64,4224]{1,0:T(8,128)(2,1)S(1)} %collective-permute-done.15.refs_2_), channel_id=1, source_target_pairs={{0,1},{1,0},{2,3},{3,2},{4,5},{5,4},{6,7},{7,6},{8,9},{9,8},{10,11... | collective-permute-start | bytes 1622024 | tf_op jit(solution)/shard_map/ppermute | solution.py:239
  51.0 9.4 %collective-permute-start.26 = (bf16[64,4224]{1,0:T(8,128)(2,1)S(1)}, bf16[64,4224]{1,0:T(8,128)(2,1)S(1)}, u32[]{:S(2)}, u32[]{:S(2)}) collective-permute-start(bf16[64,4224]{1,0:T(8,128)(2,1)S(1)} %collective-permute-done.15.refs_2_), channel_id=1, source_target_pairs={{0,4},{1,3},{4,8},{5,1},{8,12},{9,5},{12,14},{13,9},{14,10},{15,13... | collective-permute-start | bytes 1622024 | tf_op jit(solution)/shard_map/ppermute | solution.py:255
  66.5 3.5 %collective-permute-start.19 = (bf16[64,4096]{1,0:T(8,128)(2,1)S(1)}, bf16[64,4096]{1,0:T(8,128)(2,1)S(1)}, u32[]{:S(2)}, u32[]{:S(2)}) collective-permute-start(bf16[64,4096]{1,0:T(8,128)(2,1)S(1)} %get-tuple-element.46), channel_id=1, source_target_pairs={{0,1},{1,0},{2,3},{3,2},{4,5},{5,4},{6,7},{7,6},{8,9},{9,8},{10,11... | collective-permute-start | bytes 1572872 | tf_op jit(solution)/shard_map/ppermute | solution.py:242
  66.9 4.9 %collective-permute-start.25 = (bf16[64,4096]{1,0:T(8,128)(2,1)S(1)}, bf16[64,4096]{1,0:T(8,128)(2,1)S(1)}, u32[]{:S(2)}, u32[]{:S(2)}) collective-permute-start(bf16[64,4096]{1,0:T(8,128)(2,1)S(1)} %get-tuple-element.49), channel_id=1, source_target_pairs={{0,1},{1,0},{2,3},{3,2},{4,5},{5,4},{6,7},{7,6},{8,9},{9,8},{10,11... | collective-permute-start | bytes 1572872 | tf_op jit(solution)/shard_map/ppermute | solution.py:242
  68.4 9.2 %collective-permute-start.29 = (bf16[64,4096]{1,0:T(8,128)(2,1)S(1)}, bf16[64,4096]{1,0:T(8,128)(2,1)S(1)}, u32[]{:S(2)}, u32[]{:S(2)}) collective-permute-start(bf16[64,4096]{1,0:T(8,128)(2,1)S(1)} %step_sum.12), channel_id=1, source_target_pairs={{0,4},{1,3},{4,8},{5,1},{8,12},{9,5},{12,14},{13,9},{14,10},{15,13... | collective-permute-start | bytes 1572872 | tf_op jit(solution)/shard_map/ppermute | solution.py:262
  70.0 9.4 %collective-permute-start.14 = (bf16[64,4096]{1,0:T(8,128)(2,1)S(1)}, bf16[64,4096]{1,0:T(8,128)(2,1)S(1)}, u32[]{:S(2)}, u32[]{:S(2)}) collective-permute-start(bf16[64,4096]{1,0:T(8,128)(2,1)S(1)} %get-tuple-element.42), channel_id=1, source_target_pairs={{0,1},{1,0},{2,3},{3,2},{4,5},{5,4},{6,7},{7,6},{8,9},{9,8},{10,11... | collective-permute-start | bytes 1572872 | tf_op jit(solution)/shard_map/ppermute | solution.py:242
  70.2 13.1 %collective-permute-start.20 = (bf16[64,4096]{1,0:T(8,128)(2,1)S(1)}, bf16[64,4096]{1,0:T(8,128)(2,1)S(1)}, u32[]{:S(2)}, u32[]{:S(2)}) collective-permute-start(bf16[64,4096]{1,0:T(8,128)(2,1)S(1)} %step_sum.9), channel_id=1, source_target_pairs={{0,4},{1,3},{4,8},{5,1},{8,12},{9,5},{12,14},{13,9},{14,10},{15,13... | collective-permute-start | bytes 1572872 | tf_op jit(solution)/shard_map/ppermute | solution.py:261
  71.8 13.3 %collective-permute-start.24 = (bf16[64,4096]{1,0:T(8,128)(2,1)S(1)}, bf16[64,4096]{1,0:T(8,128)(2,1)S(1)}, u32[]{:S(2)}, u32[]{:S(2)}) collective-permute-start(bf16[64,4096]{1,0:T(8,128)(2,1)S(1)} %get-tuple-element.48), channel_id=1, source_target_pairs={{0,1},{1,0},{2,3},{3,2},{4,5},{5,4},{6,7},{7,6},{8,9},{9,8},{10,11... | collective-permute-start | bytes 1572872 | tf_op jit(solution)/shard_map/ppermute | solution.py:242
  77.8 11.0 %collective-permute-start.30 = (bf16[64,4096]{1,0:T(8,128)(2,1)S(1)}, bf16[64,4096]{1,0:T(8,128)(2,1)S(1)}, u32[]{:S(2)}, u32[]{:S(2)}) collective-permute-start(bf16[64,4096]{1,0:T(8,128)(2,1)S(1)} %step_sum.13), channel_id=1, source_target_pairs={{0,4},{1,3},{4,8},{5,1},{8,12},{9,5},{12,14},{13,9},{14,10},{15,13... | collective-permute-start | bytes 1572872 | tf_op jit(solution)/shard_map/ppermute | solution.py:266
  79.5 11.2 %collective-permute-start.9 = (bf16[64,4096]{1,0:T(8,128)(2,1)S(1)}, bf16[64,4096]{1,0:T(8,128)(2,1)S(1)}, u32[]{:S(2)}, u32[]{:S(2)}) collective-permute-start(bf16[64,4096]{1,0:T(8,128)(2,1)S(1)} %get-tuple-element.38), channel_id=1, source_target_pairs={{0,1},{1,0},{2,3},{3,2},{4,5},{5,4},{6,7},{7,6},{8,9},{9,8},{10,11... | collective-permute-start | bytes 1572872 | tf_op jit(solution)/shard_map/ppermute | solution.py:242
  83.4 11.0 %collective-permute-start.21 = (bf16[64,4096]{1,0:T(8,128)(2,1)S(1)}, bf16[64,4096]{1,0:T(8,128)(2,1)S(1)}, u32[]{:S(2)}, u32[]{:S(2)}) collective-permute-start(bf16[64,4096]{1,0:T(8,128)(2,1)S(1)} %step_sum.10), channel_id=1, source_target_pairs={{0,4},{1,3},{4,8},{5,1},{8,12},{9,5},{12,14},{13,9},{14,10},{15,13... | collective-permute-start | bytes 1572872 | tf_op jit(solution)/shard_map/ppermute | solution.py:265
  85.1 11.3 %collective-permute-start.23 = (bf16[64,4096]{1,0:T(8,128)(2,1)S(1)}, bf16[64,4096]{1,0:T(8,128)(2,1)S(1)}, u32[]{:S(2)}, u32[]{:S(2)}) collective-permute-start(bf16[64,4096]{1,0:T(8,128)(2,1)S(1)} %get-tuple-element.47), channel_id=1, source_target_pairs={{0,1},{1,0},{2,3},{3,2},{4,5},{5,4},{6,7},{7,6},{8,9},{9,8},{10,11... | collective-permute-start | bytes 1572872 | tf_op jit(solution)/shard_map/ppermute | solution.py:242
  89.1 11.0 %collective-permute-start.31 = (bf16[64,4096]{1,0:T(8,128)(2,1)S(1)}, bf16[64,4096]{1,0:T(8,128)(2,1)S(1)}, u32[]{:S(2)}, u32[]{:S(2)}) collective-permute-start(bf16[64,4096]{1,0:T(8,128)(2,1)S(1)} %step_sum.14), channel_id=1, source_target_pairs={{0,4},{1,3},{4,8},{5,1},{8,12},{9,5},{12,14},{13,9},{14,10},{15,13... | collective-permute-start | bytes 1572872 | tf_op jit(solution)/shard_map/ppermute | solution.py:266
  90.7 11.8 %collective-permute-start.2 = (bf16[64,4096]{1,0:T(8,128)(2,1)S(1)}, bf16[64,4096]{1,0:T(8,128)(2,1)S(1)}, u32[]{:S(2)}, u32[]{:S(2)}) collective-permute-start(bf16[64,4096]{1,0:T(8,128)(2,1)S(1)} %get-tuple-element.34), channel_id=1, source_target_pairs={{0,1},{1,0},{2,3},{3,2},{4,5},{5,4},{6,7},{7,6},{8,9},{9,8},{10,11... | collective-permute-start | bytes 1572872 | tf_op jit(solution)/shard_map/ppermute | solution.py:247
  94.6 8.3 %collective-permute-start.22 = (bf16[32,4096]{1,0:T(8,128)(2,1)S(1)}, bf16[32,4096]{1,0:T(8,128)(2,1)S(1)}, u32[]{:S(2)}, u32[]{:S(2)}) collective-permute-start(bf16[32,4096]{1,0:T(8,128)(2,1)S(1)} %step_sum.11), channel_id=1, source_target_pairs={{0,4},{1,3},{4,8},{5,1},{8,12},{9,5},{12,14},{13,9},{14,10},{15,13... | collective-permute-start | bytes 786440 | tf_op jit(solution)/shard_map/ppermute | solution.py:272
  96.3 8.6 %collective-permute-start.34 = (bf16[32,4096]{1,0:T(8,128)(2,1)S(1)}, bf16[32,4096]{1,0:T(8,128)(2,1)S(1)}, u32[]{:S(2)}, u32[]{:S(2)}) collective-permute-start(bf16[32,4096]{1,0:T(8,128)(2,1)S(1)} %step_sum.17), channel_id=1, source_target_pairs={{0,5},{1,2},{4,9},{5,0},{8,13},{9,4},{12,15},{13,8},{14,11},{15,12... | collective-permute-start | bytes 786440 | tf_op jit(solution)/shard_map/ppermute | solution.py:272
  100.2 7.5 %collective-permute-start.32 = (bf16[32,4096]{1,0:T(8,128)(2,1)S(1)}, bf16[32,4096]{1,0:T(8,128)(2,1)S(1)}, u32[]{:S(2)}, u32[]{:S(2)}) collective-permute-start(bf16[32,4096]{1,0:T(8,128)(2,1)S(1)} %step_sum.15), channel_id=1, source_target_pairs={{0,5},{1,2},{4,9},{5,0},{8,13},{9,4},{12,15},{13,8},{14,11},{15,12... | collective-permute-start | bytes 786440 | tf_op jit(solution)/shard_map/ppermute | solution.py:272
  100.8 10.5 %collective-permute-start.33 = (bf16[32,4096]{1,0:T(8,128)(2,1)S(1)}, bf16[32,4096]{1,0:T(8,128)(2,1)S(1)}, u32[]{:S(2)}, u32[]{:S(2)}) collective-permute-start(bf16[32,4096]{1,0:T(8,128)(2,1)S(1)} %step_sum.16), channel_id=1, source_target_pairs={{0,4},{1,3},{4,8},{5,1},{8,12},{9,5},{12,14},{13,9},{14,10},{15,13... | collective-permute-start | bytes 786440 | tf_op jit(solution)/shard_map/ppermute | solution.py:272
  (6 other events, 37.5 us)

commit v7 on v6

--- a/solution.py
+++ b/solution.py
@@ -26,7 +26,7 @@
     return pltpu.CompilerParams(vmem_limit_bytes=mebibytes << 20)
 
 
-def pack_kernel(experts, core, tokens, routes, gate_num, first, second, digits):
+def pack_kernel(experts, core, tokens, routes, gate_num, own, other, digits):
     rows, width = tokens.shape
     half = rows // 2
     lane = lax.broadcasted_iota(jnp.int32, (rows, LANES), 1)
@@ -38,10 +38,11 @@
     digit = jnp.where(lane < experts, dense >> 8, dense & 255)
     digit = jnp.where(lane < 2 * experts, digit, 0)
     digits[...] = digit.astype(jnp.float32).astype(jnp.bfloat16)
-    for packed, place in ((first, core[0]), (second, 1 - core[0])):
-        here = pl.ds(pl.multiple_of(place * half, half), half)
-        packed[:, :width] = tokens[here]
-        packed[:, width:] = digits[here]
+    for packed, place in ((own, core[0]), (other, 1 - core[0])):
+        for there, place_here in ((0, place), (half, 1 - place)):
+            here = pl.ds(pl.multiple_of(place_here * half, half), half)
+            packed[there : there + half, :width] = tokens[here]
+            packed[there : there + half, width:] = digits[here]
 
 
 def pack(core, tokens, routes, gate_num, experts):
@@ -50,7 +51,7 @@
         functools.partial(pack_kernel, experts),
         in_specs=[SMEM] + [VMEM] * 3,
         out_specs=[VMEM] * 2,
-        out_shape=[jax.ShapeDtypeStruct((rows // 2, width + LANES), jnp.bfloat16)] * 2,
+        out_shape=[jax.ShapeDtypeStruct((rows, width + LANES), jnp.bfloat16)] * 2,
         scratch_shapes=[pltpu.VMEM((rows, LANES), jnp.bfloat16)],
         compiler_params=limits(4),
         name="pack",
@@ -149,26 +150,54 @@
     )
 
 
-def step_kernel(starts, rows, *refs):
+def step_kernel(plan, *refs):
     *terms, out = refs
-    for column in range(0, out.shape[1], WIDTH_CHUNK):
-        columns = slice(column, column + WIDTH_CHUNK)
-        total = 0.0
-        for ref, start in zip(terms, starts):
-            total += ref[start : start + rows, columns].astype(jnp.float32)
-        out[:, columns] = total.astype(jnp.bfloat16)
-
-
-def step_sum(terms, rows):
-    arrays, starts = zip(*terms)
-    return pl.pallas_call(
-        functools.partial(step_kernel, starts, rows),
+    for first, rows, places in plan:
+        for column in range(0, out.shape[1], WIDTH_CHUNK):
+            columns = slice(column, column + WIDTH_CHUNK)
+            total = 0.0
+            for number, start in places:
+                total += terms[number][start : start + rows, columns].astype(jnp.float32)
+            out[first : first + rows, columns] = total.astype(jnp.bfloat16)
+
+
+def step_sum(*segments):
+    arrays, plan, height = [], [], 0
+    for rows, terms in segments:
+        places = []
+        for array, start in terms:
+            number = next((i for i, known in enumerate(arrays) if known is array), len(arrays))
+            if number == len(arrays):
+                arrays.append(array)
+            places.append((number, start))
+        plan.append((height, rows, tuple(places)))
+        height += rows
+    return pl.pallas_call(
+        functools.partial(step_kernel, tuple(plan)),
         in_specs=[VMEM] * len(arrays),
         out_specs=VMEM,
-        out_shape=jax.ShapeDtypeStruct((rows, arrays[0].shape[1]), jnp.bfloat16),
+        out_shape=jax.ShapeDtypeStruct((height, arrays[0].shape[1]), jnp.bfloat16),
         compiler_params=limits(4),
         name="step_sum",
     )(*arrays)
+
+
+def join_kernel(same, cross, block):
+    half = same.shape[0] // 2
+    for number in range(4):
+        place = slice((number // 2) * half, (number // 2 + 1) * half)
+        block[number * half : (number + 1) * half] = (same, cross)[number % 2][place]
+
+
+def join(same, cross):
+    return pl.pallas_call(
+        join_kernel,
+        in_specs=[VMEM] * 2,
+        out_specs=VMEM,
+        out_shape=jax.ShapeDtypeStruct((2 * same.shape[0], same.shape[1]), same.dtype),
+        compiler_params=limits(4),
+        name="join",
+    )(same, cross)
 
 
 def last_kernel(core, mine, theirs, *refs):
@@ -223,7 +252,10 @@
 
     on, to_other, back_to_other = hop(1, 0), hop(-1, 1), hop(1, 1)
     swap = [(i, i ^ 1) for i in range(devices)]
-    send = functools.partial(lax.ppermute, axis_name="expert")
+
+    def send(x, perm, name):
+        with jax.named_scope(name):
+            return lax.ppermute(x, "expert", perm)
 
     lane = jnp.arange(LANES, dtype=jnp.int32)
     pick = jnp.where(lane == expert, 256.0, jnp.where(lane == devices + expert, 1.0, 0.0))
@@ -234,46 +266,57 @@
 
     kept, given = {}, {}
 
-    def run(distance, blocks, hint):
-        tie = kept.get(distance - 1)
-        others = [send(after(block, tie), perm=swap) for block in blocks]
-        heights = [block.shape[0] for block in blocks]
-        kept[distance], *cuts = expert_part(others + blocks, (sum(heights), *heights), hint, *weights)
-        given[distance] = [send(cut, perm=swap) for cut in cuts]
-
-    first, second = pack(core, tokens, routes, gate_num, devices)
-    others = [send(block, perm=swap) for block in (first, second)]
-    kept[0], cut = expert_part([first, second] + others, (rows, rows), 2, *weights)
-    given[0] = send(cut, perm=swap)
-    long = jnp.concatenate([send(first, perm=on), send(second, perm=to_other)], axis=0)
-    short = jnp.concatenate([send(second, perm=on), send(first, perm=to_other)], axis=0)
-    run(1, [long, short], 2)
+    def run(distance, block, cuts, hint):
+        other = send(after(block, kept[distance - 1]), swap, f"swap_in_{distance}")
+        kept[distance], *given_here = expert_part([other, block], (block.shape[0], *cuts), hint, *weights)
+        given[distance] = [send(cut, swap, f"swap_out_{distance}") for cut in given_here]
+
+    own, own_for_other = pack(core, tokens, routes, gate_num, devices)
+    other = send(own, swap, "swap_in_0")
+    kept[0], cut = expert_part([own, other], (rows, rows), 2, *weights)
+    given[0] = send(cut, swap, "swap_out_0")
+    same, cross = send(own, on, "gather_1"), send(own_for_other, to_other, "gather_1")
+    block = join(after(same, kept[0]), cross)
+    run(1, block, (rows, rows), 2)
     for distance in range(2, reach):
-        tie = kept[distance - 2]
-        long, short = send(after(long, tie), perm=on), send(after(short, tie), perm=on)
-        run(distance, [long, short], 2)
-    long = send(after(long, kept[reach - 2]), perm=on)
-    run(reach, [long], 2)
+        block = send(after(block, kept[distance - 2]), on, f"gather_{distance}")
+        run(distance, block, (rows, rows), 2)
+    block = send(after(block[:rows], kept[reach - 2]), on, f"gather_{reach}")
 
     def terms(distance, number):
         return [(kept[distance], number * rows), (given[distance][number], 0)]
 
-    short = send(step_sum(terms(reach - 1, 1), rows), perm=on)
-    long = send(step_sum(terms(reach, 0), rows), perm=on)
-    for distance in range(reach - 1, 1, -1):
-        if distance < reach - 1:
-            short = send(step_sum(terms(distance, 1) + [(short, 0)], rows), perm=on)
-        long = send(step_sum(terms(distance, 0) + [(long, 0)], rows), perm=on)
-
-    def arrive(carried, number):
-        pieces = []
+    total = step_sum((rows, terms(reach - 1, 1)))
+    short = send(total, on, f"return_short_{reach - 1}")
+    block = after(block, total)
+    run(reach, block, (rows,), 2)
+
+    def arrive(carried, number, name):
+        pieces, totals = [], []
         for start, perm in ((0, back_to_other), (half, on)):
             (kept_1, at), (given_1, _) = terms(1, number)
-            pieces.append(send(step_sum([(kept_1, at + start), (given_1, start), (carried, start)], half), perm=perm))
-        return pieces
-
-    short_cross, short_same = arrive(short, 1)
-    long_cross, long_same = arrive(long, 0)
+            total = step_sum((half, [(kept_1, at + start), (given_1, start), (carried, start)]))
+            pieces.append(send(total, perm, name))
+            totals.append(total)
+        return pieces, totals
+
+    pieces, height = [], rows // len(given[reach])
+    for number, piece in enumerate(given[reach]):
+        pieces.append((height, [(kept[reach], number * height), (after(piece, short), 0)]))
+    long = send(step_sum(*pieces), on, f"return_long_{reach}")
+    for distance in range(reach - 1, 1, -1):
+        if distance > 2:
+            total = step_sum((rows, terms(distance - 1, 1) + [(short, 0)]))
+            short_next = send(total, on, f"return_short_{distance - 1}")
+            totals = [total]
+        else:
+            short_next, totals = arrive(short, 1, "return_short_1")
+        total = step_sum((rows, terms(distance, 0) + [(after(long, *totals), 0)]))
+        long = send(total, on, f"return_long_{distance}")
+        short = short_next
+
+    short_cross, short_same = short
+    long_cross, long_same = arrive(long, 0, "return_long_1")[0]
     return last_sum(core, kept[0], given[0], short_same, long_cross, long_same, short_cross)
 
 

time: 113 us -> 113 us (level)
    ppermute x35 -> x27, waiting for transfers between devices: 45.6 us -> 46.5 us  [send(): return lax.ppermute(x, 'expert', perm)]
    ppermute x35 -> x27, starting transfers between devices: 27.8 us -> 27 us  [send(): return lax.ppermute(x, 'expert', perm)]
    unnamed x10 -> x8, local copies, waits for them, and re-layouts: 2.65 us -> 2.59 us
  transfers between devices with their start and end apart: 35 -> 27, of which waited for: 16 -> 16; matrix products, arithmetic and copies ran while one was open for 0% -> 0% of each run, Pallas kernels for 27% -> 31%
where the time goes in v7:
time: 113 us
  waiting for transfers between devices  46.5 us (41%)
  Pallas kernels  36.2 us (32%)
  starting transfers between devices  27 us (24%)
  local copies, waits for them, and re-layouts  2.62 us (2%)
    ppermute x27, waiting for transfers between devices, send(): return lax.ppermute(x, 'expert', perm)  46.5 us
    pallas_call x5, Pallas kernels, expert_part(): pl.pallas_call(functools.partial(expert_kernel, len(blocks)), in_specs=[V...  27.2 us
    ppermute x27, starting transfers between devices, send(): return lax.ppermute(x, 'expert', perm)  27 us
    pallas_call x1, Pallas kernels, keep(): pl.pallas_call(keep_kernel, in_specs=[ANYWHERE] * 2, out_specs=[VMEM] * 2...  6.4 us
    unnamed x8, local copies, waits for them, and re-layouts  2.59 us
  transfers between devices with their start and end apart: 27, of which 16 were waited for; matrix products, arithmetic and copies ran while one was open for 0% of the time, Pallas kernels for 31%

profile of v7, /device:TPU:0, one launch (start us, length us, event | category | flops | bytes accessed | tf_op | source)
XLA Modules:
  0.0 112.5 jit_solution(8654868816736660488)
XLA Ops:
  1.5 1.0 copy-done
  3.3 2.6 %collective-permute-start.2 = (bf16[64,4224]{1,0:T(8,128)(2,1)S(1)}, bf16[64,4224]{1,0:T(8,128)(2,1)S(1)}, u32[]{:S(2)}, u32[]{:S(2)}) collective-permute-start(bf16[64,4224]{1,0:T(8,128)(2,1)S(1)} %get-tuple-element.32.refs_0_), channel_id=1, source_target_pairs={{0,4},{1,3},{4,8},{5,1},{8,12},{9,5},{12,14},{13,9},{14,10},{15,13... | collective-permute-start | bytes 1622024 | tf_op jit(solution)/shard_map/gather_1/ppermute | solution.py:258
  6.0 1.3 %collective-permute-start.3 = (bf16[64,4224]{1,0:T(8,128)(2,1)S(1)}, bf16[64,4224]{1,0:T(8,128)(2,1)S(1)}, u32[]{:S(2)}, u32[]{:S(2)}) collective-permute-start(bf16[64,4224]{1,0:T(8,128)(2,1)S(1)} %get-tuple-element.38), channel_id=1, source_target_pairs={{0,3},{1,4},{4,1},{5,8},{8,5},{9,12},{12,9},{13,14},{14,13},{15,10... | collective-permute-start | bytes 1622024 | tf_op jit(solution)/shard_map/gather_1/ppermute | solution.py:258
  7.3 6.4 %keep.1 = (bf16[4096,1536]{1,0:T(8,128)(2,1)S(1)}, bf16[768,4096]{1,0:T(8,128)(2,1)S(1)}) custom-call(bf16[4096,1536]{1,0:T(8,128)(2,1)} %bitcast.3, bf16[768,4096]{1,0:T(8,128)(2,1)} %bitcast.4), custom_call_target="tpu_custom_call" | custom-call | bytes 18874368 | tf_op jit(solution)/shard_map/keep/pallas_call | solution.py:73
  13.7 3.9 %expert.5 = (bf16[64,4096]{1,0:T(8,128)(2,1)S(1)}, bf16[64,4096]{1,0:T(8,128)(2,1)S(1)}) custom-call(bf16[64,4224]{1,0:T(8,128)(2,1)S(1)} %get-tuple-element.32.refs_0_, bf16[64,4224]{1,0:T(8,128)(2,1)S(1)} %collective-permute-done.refs_1_, f32[1,128]{1,0:T(1,128)S(1)} %compare_select_fusion.1.refs_2_, f32[1,1536]{1,0:T(1,128)S(1)} %copy-done.2, ...), custom_call_target="tpu_custom_call" | custom-call | flops 4831838208 | tf_op jit(solution)/shard_map/expert/pallas_call | solution.py:131
  17.7 1.4 %collective-permute-done.3.cross = bf16[64,4224]{1,0:T(8,128)(2,1)S(1)} collective-permute-done((bf16[64,4224]{1,0:T(8,128)(2,1)S(1)}, bf16[64,4224]{1,0:T(8,128)(2,1)S(1)}, u32[]{:S(2)}, u32[]{:S(2)}) %collective-permute-start.3) | collective-permute-done | bytes 540704 | tf_op jit(solution)/shard_map/gather_1/ppermute | solution.py:258
  19.2 2.1 %collective-permute-start.6 = (bf16[128,4224]{1,0:T(8,128)(2,1)S(1)}, bf16[128,4224]{1,0:T(8,128)(2,1)S(1)}, u32[]{:S(2)}, u32[]{:S(2)}) collective-permute-start(bf16[128,4224]{1,0:T(8,128)(2,1)S(1)} %join.1.refs_1_), channel_id=1, source_target_pairs={{0,4},{1,3},{4,8},{5,1},{8,12},{9,5},{12,14},{13,9},{14,10},{15,13... | collective-permute-start | bytes 3244040 | tf_op jit(solution)/shard_map/gather_2/ppermute | solution.py:258
  21.9 6.4 %expert.6 = (bf16[128,4096]{1,0:T(8,128)(2,1)S(1)}, bf16[64,4096]{1,0:T(8,128)(2,1)S(1)}, bf16[64,4096]{1,0:T(8,128)(2,1)S(1)}) custom-call(bf16[128,4224]{1,0:T(8,128)(2,1)S(1)} %collective-permute-done.4.refs_0_, bf16[128,4224]{1,0:T(8,128)(2,1)S(1)} %join.1.refs_1_, f32[1,128]{1,0:T(1,128)S(1)} %compare_select_fusion.1.refs_2_, f32[1,1536]{1,0:T(1,128)S(1)} %copy-done.2, ...), custom_call_target="tpu_custom_call" | custom-call | flops 9663676416 | tf_op jit(solution)/shard_map/expert/pallas_call | solution.py:131
  28.3 6.1 %collective-permute-done.6.refs_1_ = bf16[128,4224]{1,0:T(8,128)(2,1)S(1)} collective-permute-done((bf16[128,4224]{1,0:T(8,128)(2,1)S(1)}, bf16[128,4224]{1,0:T(8,128)(2,1)S(1)}, u32[]{:S(2)}, u32[]{:S(2)}) %collective-permute-start.6) | collective-permute-done | bytes 1081376 | tf_op jit(solution)/shard_map/gather_2/ppermute | solution.py:258
  34.4 2.1 %collective-permute-start.9 = (bf16[128,4224]{1,0:T(8,128)(2,1)S(1)}, bf16[128,4224]{1,0:T(8,128)(2,1)S(1)}, u32[]{:S(2)}, u32[]{:S(2)}) collective-permute-start(bf16[128,4224]{1,0:T(8,128)(2,1)S(1)} %collective-permute-done.6.refs_1_), channel_id=1, source_target_pairs={{0,4},{1,3},{4,8},{5,1},{8,12},{9,5},{12,14},{13,9},{14,10},{15,13... | collective-permute-start | bytes 3244040 | tf_op jit(solution)/shard_map/gather_3/ppermute | solution.py:258
  37.1 6.4 %expert.7 = (bf16[128,4096]{1,0:T(8,128)(2,1)S(1)}, bf16[64,4096]{1,0:T(8,128)(2,1)S(1)}, bf16[64,4096]{1,0:T(8,128)(2,1)S(1)}) custom-call(bf16[128,4224]{1,0:T(8,128)(2,1)S(1)} %collective-permute-done.7.refs_0_, bf16[128,4224]{1,0:T(8,128)(2,1)S(1)} %collective-permute-done.6.refs_1_, f32[1,128]{1,0:T(1,128)S(1)} %compare_select_fusion.1.refs_2_, ...), custom_call_target="tpu_custom_call" | custom-call | flops 9663676416 | tf_op jit(solution)/shard_map/expert/pallas_call | solution.py:131
  43.5 6.0 %collective-permute-done.9.refs_1_ = bf16[128,4224]{1,0:T(8,128)(2,1)S(1)} collective-permute-done((bf16[128,4224]{1,0:T(8,128)(2,1)S(1)}, bf16[128,4224]{1,0:T(8,128)(2,1)S(1)}, u32[]{:S(2)}, u32[]{:S(2)}) %collective-permute-start.9) | collective-permute-done | bytes 1081376 | tf_op jit(solution)/shard_map/gather_3/ppermute | solution.py:258
  49.6 2.1 %collective-permute-start.18 = (bf16[64,4224]{1,0:T(8,128)(2,1)S(1)}, bf16[64,4224]{1,0:T(8,128)(2,1)S(1)}, u32[]{:S(2)}, u32[]{:S(2)}) collective-permute-start(bf16[64,4224]{1,0:T(8,128)(2,1)S(1)} %slice.4), channel_id=1, source_target_pairs={{0,4},{1,3},{4,8},{5,1},{8,12},{9,5},{12,14},{13,9},{14,10},{15,13... | collective-permute-start | bytes 1622024 | tf_op jit(solution)/shard_map/gather_4/ppermute | solution.py:258
  52.3 6.4 %expert.8 = (bf16[128,4096]{1,0:T(8,128)(2,1)S(1)}, bf16[64,4096]{1,0:T(8,128)(2,1)S(1)}, bf16[64,4096]{1,0:T(8,128)(2,1)S(1)}) custom-call(bf16[128,4224]{1,0:T(8,128)(2,1)S(1)} %collective-permute-done.10.refs_0_, bf16[128,4224]{1,0:T(8,128)(2,1)S(1)} %collective-permute-done.9.refs_1_, f32[1,128]{1,0:T(1,128)S(1)} %compare_select_fusion.1.refs_2_, ...), custom_call_target="tpu_custom_call" | custom-call | flops 9663676416 | tf_op jit(solution)/shard_map/expert/pallas_call | solution.py:131
  58.9 1.8 %collective-permute-done.11.refs_1_ = bf16[64,4096]{1,0:T(8,128)(2,1)S(1)} collective-permute-done((bf16[64,4096]{1,0:T(8,128)(2,1)S(1)}, bf16[64,4096]{1,0:T(8,128)(2,1)S(1)}, u32[]{:S(2)}, u32[]{:S(2)}) %collective-permute-start.11) | collective-permute-done | bytes 524320 | tf_op jit(solution)/shard_map/swap_out_3/ppermute | solution.py:258
  61.0 2.1 %collective-permute-start.12 = (bf16[64,4096]{1,0:T(8,128)(2,1)S(1)}, bf16[64,4096]{1,0:T(8,128)(2,1)S(1)}, u32[]{:S(2)}, u32[]{:S(2)}) collective-permute-start(bf16[64,4096]{1,0:T(8,128)(2,1)S(1)} %step_sum.9), channel_id=1, source_target_pairs={{0,4},{1,3},{4,8},{5,1},{8,12},{9,5},{12,14},{13,9},{14,10},{15,13... | collective-permute-start | bytes 1572872 | tf_op jit(solution)/shard_map/return_short_3/ppermute | solution.py:258
  63.1 3.9 %expert.9 = (bf16[64,4096]{1,0:T(8,128)(2,1)S(1)}, bf16[64,4096]{1,0:T(8,128)(2,1)S(1)}) custom-call(bf16[64,4224]{1,0:T(8,128)(2,1)S(1)} %collective-permute-done.19.refs_0_, bf16[64,4224]{1,0:T(8,128)(2,1)S(1)} %collective-permute-done.18.refs_1_, f32[1,128]{1,0:T(1,128)S(1)} %compare_select_fusion.1.refs_2_, f32[1,1536]{1,0:T(1,128)S(1)} %copy-done.2, ...), custom_call_target="tpu_custom_call" | custom-call | flops 4831838208 | tf_op jit(solution)/shard_map/expert/pallas_call | solution.py:131
  67.6 2.6 %collective-permute-done.12.refs_2_ = bf16[64,4096]{1,0:T(8,128)(2,1)S(1)} collective-permute-done((bf16[64,4096]{1,0:T(8,128)(2,1)S(1)}, bf16[64,4096]{1,0:T(8,128)(2,1)S(1)}, u32[]{:S(2)}, u32[]{:S(2)}) %collective-permute-start.12) | collective-permute-done | bytes 524320 | tf_op jit(solution)/shard_map/return_short_3/ppermute | solution.py:258
  70.3 2.1 %collective-permute-start.21 = (bf16[64,4096]{1,0:T(8,128)(2,1)S(1)}, bf16[64,4096]{1,0:T(8,128)(2,1)S(1)}, u32[]{:S(2)}, u32[]{:S(2)}) collective-permute-start(bf16[64,4096]{1,0:T(8,128)(2,1)S(1)} %step_sum.12), channel_id=1, source_target_pairs={{0,4},{1,3},{4,8},{5,1},{8,12},{9,5},{12,14},{13,9},{14,10},{15,13... | collective-permute-start | bytes 1572872 | tf_op jit(solution)/shard_map/return_long_4/ppermute | solution.py:258
  73.2 1.6 %collective-permute-start.13 = (bf16[64,4096]{1,0:T(8,128)(2,1)S(1)}, bf16[64,4096]{1,0:T(8,128)(2,1)S(1)}, u32[]{:S(2)}, u32[]{:S(2)}) collective-permute-start(bf16[64,4096]{1,0:T(8,128)(2,1)S(1)} %step_sum.10), channel_id=1, source_target_pairs={{0,4},{1,3},{4,8},{5,1},{8,12},{9,5},{12,14},{13,9},{14,10},{15,13... | collective-permute-start | bytes 1572872 | tf_op jit(solution)/shard_map/return_short_2/ppermute | solution.py:258
  74.8 4.8 %collective-permute-done.21.refs_2_ = bf16[64,4096]{1,0:T(8,128)(2,1)S(1)} collective-permute-done((bf16[64,4096]{1,0:T(8,128)(2,1)S(1)}, bf16[64,4096]{1,0:T(8,128)(2,1)S(1)}, u32[]{:S(2)}, u32[]{:S(2)}) %collective-permute-start.21) | collective-permute-done | bytes 524320 | tf_op jit(solution)/shard_map/return_long_4/ppermute | solution.py:258
  79.8 2.1 %collective-permute-start.22 = (bf16[64,4096]{1,0:T(8,128)(2,1)S(1)}, bf16[64,4096]{1,0:T(8,128)(2,1)S(1)}, u32[]{:S(2)}, u32[]{:S(2)}) collective-permute-start(bf16[64,4096]{1,0:T(8,128)(2,1)S(1)} %step_sum.13), channel_id=1, source_target_pairs={{0,4},{1,3},{4,8},{5,1},{8,12},{9,5},{12,14},{13,9},{14,10},{15,13... | collective-permute-start | bytes 1572872 | tf_op jit(solution)/shard_map/return_long_3/ppermute | solution.py:258
  82.4 2.8 %collective-permute-done.13.refs_2_ = bf16[64,4096]{1,0:T(8,128)(2,1)S(1)} collective-permute-done((bf16[64,4096]{1,0:T(8,128)(2,1)S(1)}, bf16[64,4096]{1,0:T(8,128)(2,1)S(1)}, u32[]{:S(2)}, u32[]{:S(2)}) %collective-permute-start.13) | collective-permute-done | bytes 524320 | tf_op jit(solution)/shard_map/return_short_2/ppermute | solution.py:258
  85.4 5.4 %collective-permute-done.22.refs_2_ = bf16[64,4096]{1,0:T(8,128)(2,1)S(1)} collective-permute-done((bf16[64,4096]{1,0:T(8,128)(2,1)S(1)}, bf16[64,4096]{1,0:T(8,128)(2,1)S(1)}, u32[]{:S(2)}, u32[]{:S(2)}) %collective-permute-start.22) | collective-permute-done | bytes 524320 | tf_op jit(solution)/shard_map/return_long_3/ppermute | solution.py:258
  91.0 2.1 %collective-permute-start.23 = (bf16[64,4096]{1,0:T(8,128)(2,1)S(1)}, bf16[64,4096]{1,0:T(8,128)(2,1)S(1)}, u32[]{:S(2)}, u32[]{:S(2)}) collective-permute-start(bf16[64,4096]{1,0:T(8,128)(2,1)S(1)} %step_sum.15), channel_id=1, source_target_pairs={{0,4},{1,3},{4,8},{5,1},{8,12},{9,5},{12,14},{13,9},{14,10},{15,13... | collective-permute-start | bytes 1572872 | tf_op jit(solution)/shard_map/return_long_2/ppermute | solution.py:258
  93.1 1.6 %collective-permute-start.14 = (bf16[32,4096]{1,0:T(8,128)(2,1)S(1)}, bf16[32,4096]{1,0:T(8,128)(2,1)S(1)}, u32[]{:S(2)}, u32[]{:S(2)}) collective-permute-start(bf16[32,4096]{1,0:T(8,128)(2,1)S(1)} %step_sum.11), channel_id=1, source_target_pairs={{0,4},{1,3},{4,8},{5,1},{8,12},{9,5},{12,14},{13,9},{14,10},{15,13... | collective-permute-start | bytes 786440 | tf_op jit(solution)/shard_map/return_short_1/ppermute | solution.py:258
  95.0 5.2 %collective-permute-done.23.refs_2_ = bf16[64,4096]{1,0:T(8,128)(2,1)S(1)} collective-permute-done((bf16[64,4096]{1,0:T(8,128)(2,1)S(1)}, bf16[64,4096]{1,0:T(8,128)(2,1)S(1)}, u32[]{:S(2)}, u32[]{:S(2)}) %collective-permute-start.23) | collective-permute-done | bytes 524320 | tf_op jit(solution)/shard_map/return_long_2/ppermute | solution.py:258
  100.5 2.1 %collective-permute-start.25 = (bf16[32,4096]{1,0:T(8,128)(2,1)S(1)}, bf16[32,4096]{1,0:T(8,128)(2,1)S(1)}, u32[]{:S(2)}, u32[]{:S(2)}) collective-permute-start(bf16[32,4096]{1,0:T(8,128)(2,1)S(1)} %step_sum.17), channel_id=1, source_target_pairs={{0,4},{1,3},{4,8},{5,1},{8,12},{9,5},{12,14},{13,9},{14,10},{15,13... | collective-permute-start | bytes 786440 | tf_op jit(solution)/shard_map/return_long_1/ppermute | solution.py:258
  103.0 2.4 %collective-permute-done.26.refs_3_ = bf16[32,4096]{1,0:T(8,128)(2,1)S(1)} collective-permute-done((bf16[32,4096]{1,0:T(8,128)(2,1)S(1)}, bf16[32,4096]{1,0:T(8,128)(2,1)S(1)}, u32[]{:S(2)}, u32[]{:S(2)}) %collective-permute-start.26) | collective-permute-done | bytes 262176 | tf_op jit(solution)/shard_map/return_short_1/ppermute | solution.py:258
  105.4 2.8 %collective-permute-done.24.refs_1_ = bf16[32,4096]{1,0:T(8,128)(2,1)S(1)} collective-permute-done((bf16[32,4096]{1,0:T(8,128)(2,1)S(1)}, bf16[32,4096]{1,0:T(8,128)(2,1)S(1)}, u32[]{:S(2)}, u32[]{:S(2)}) %collective-permute-start.24) | collective-permute-done | bytes 262176 | tf_op jit(solution)/shard_map/return_long_1/ppermute | solution.py:258
  108.3 3.2 %collective-permute-done.25.refs_2_ = bf16[32,4096]{1,0:T(8,128)(2,1)S(1)} collective-permute-done((bf16[32,4096]{1,0:T(8,128)(2,1)S(1)}, bf16[32,4096]{1,0:T(8,128)(2,1)S(1)}, u32[]{:S(2)}, u32[]{:S(2)}) %collective-permute-start.25) | collective-permute-done | bytes 262176 | tf_op jit(solution)/shard_map/return_long_1/ppermute | solution.py:258
  111.5 1.0 last_sum.1
  (50 shorter events, 8.2 us)
Async XLA Ops:
  1.5 1.0 copy-start
  2.8 10.9 %collective-permute-start = (bf16[64,4224]{1,0:T(8,128)(2,1)S(1)}, bf16[64,4224]{1,0:T(8,128)(2,1)S(1)}, u32[]{:S(2)}, u32[]{:S(2)}) collective-permute-start(bf16[64,4224]{1,0:T(8,128)(2,1)S(1)} %get-tuple-element.32.refs_0_), channel_id=1, source_target_pairs={{0,1},{1,0},{2,3},{3,2},{4,5},{5,4},{6,7},{7,6},{8,9},{9,8},{10,11... | collective-permute-start | bytes 1622024 | tf_op jit(solution)/shard_map/swap_in_0/ppermute | solution.py:258
  3.3 14.3 %collective-permute-start.2 = (bf16[64,4224]{1,0:T(8,128)(2,1)S(1)}, bf16[64,4224]{1,0:T(8,128)(2,1)S(1)}, u32[]{:S(2)}, u32[]{:S(2)}) collective-permute-start(bf16[64,4224]{1,0:T(8,128)(2,1)S(1)} %get-tuple-element.32.refs_0_), channel_id=1, source_target_pairs={{0,4},{1,3},{4,8},{5,1},{8,12},{9,5},{12,14},{13,9},{14,10},{15,13... | collective-permute-start | bytes 1622024 | tf_op jit(solution)/shard_map/gather_1/ppermute | solution.py:258
  6.0 13.1 %collective-permute-start.3 = (bf16[64,4224]{1,0:T(8,128)(2,1)S(1)}, bf16[64,4224]{1,0:T(8,128)(2,1)S(1)}, u32[]{:S(2)}, u32[]{:S(2)}) collective-permute-start(bf16[64,4224]{1,0:T(8,128)(2,1)S(1)} %get-tuple-element.38), channel_id=1, source_target_pairs={{0,3},{1,4},{4,1},{5,8},{8,5},{9,12},{12,9},{13,14},{14,13},{15,10... | collective-permute-start | bytes 1622024 | tf_op jit(solution)/shard_map/gather_1/ppermute | solution.py:258
  7.3 6.4 %copy-start.1 = (f32[1,4096]{1,0:T(1,128)S(1)}, f32[1,4096]{1,0:T(1,128)}, u32[]{:S(2)}) copy-start(f32[1,4096]{1,0:T(1,128)} %refs_4_.9) | copy-start | bytes 49156
  7.3 6.4 %copy-start.2 = (f32[1,1536]{1,0:T(1,128)S(1)}, f32[1,1536]{1,0:T(1,128)}, u32[]{:S(2)}) copy-start(f32[1,1536]{1,0:T(1,128)} %refs_3_.9) | copy-start | bytes 18436
  19.1 2.8 %collective-permute-start.4 = (bf16[128,4224]{1,0:T(8,128)(2,1)S(1)}, bf16[128,4224]{1,0:T(8,128)(2,1)S(1)}, u32[]{:S(2)}, u32[]{:S(2)}) collective-permute-start(bf16[128,4224]{1,0:T(8,128)(2,1)S(1)} %join.1.refs_1_), channel_id=1, source_target_pairs={{0,1},{1,0},{2,3},{3,2},{4,5},{5,4},{6,7},{7,6},{8,9},{9,8},{10,11... | collective-permute-start | bytes 3244040 | tf_op jit(solution)/shard_map/swap_in_1/ppermute | solution.py:258
  19.2 15.2 %collective-permute-start.6 = (bf16[128,4224]{1,0:T(8,128)(2,1)S(1)}, bf16[128,4224]{1,0:T(8,128)(2,1)S(1)}, u32[]{:S(2)}, u32[]{:S(2)}) collective-permute-start(bf16[128,4224]{1,0:T(8,128)(2,1)S(1)} %join.1.refs_1_), channel_id=1, source_target_pairs={{0,4},{1,3},{4,8},{5,1},{8,12},{9,5},{12,14},{13,9},{14,10},{15,13... | collective-permute-start | bytes 3244040 | tf_op jit(solution)/shard_map/gather_2/ppermute | solution.py:258
  34.4 2.7 %collective-permute-start.7 = (bf16[128,4224]{1,0:T(8,128)(2,1)S(1)}, bf16[128,4224]{1,0:T(8,128)(2,1)S(1)}, u32[]{:S(2)}, u32[]{:S(2)}) collective-permute-start(bf16[128,4224]{1,0:T(8,128)(2,1)S(1)} %collective-permute-done.6.refs_1_), channel_id=1, source_target_pairs={{0,1},{1,0},{2,3},{3,2},{4,5},{5,4},{6,7},{7,6},{8,9},{9,8},{10,11... | collective-permute-start | bytes 3244040 | tf_op jit(solution)/shard_map/swap_in_2/ppermute | solution.py:258
  34.4 15.2 %collective-permute-start.9 = (bf16[128,4224]{1,0:T(8,128)(2,1)S(1)}, bf16[128,4224]{1,0:T(8,128)(2,1)S(1)}, u32[]{:S(2)}, u32[]{:S(2)}) collective-permute-start(bf16[128,4224]{1,0:T(8,128)(2,1)S(1)} %collective-permute-done.6.refs_1_), channel_id=1, source_target_pairs={{0,4},{1,3},{4,8},{5,1},{8,12},{9,5},{12,14},{13,9},{14,10},{15,13... | collective-permute-start | bytes 3244040 | tf_op jit(solution)/shard_map/gather_3/ppermute | solution.py:258
  49.5 2.7 %collective-permute-start.10 = (bf16[128,4224]{1,0:T(8,128)(2,1)S(1)}, bf16[128,4224]{1,0:T(8,128)(2,1)S(1)}, u32[]{:S(2)}, u32[]{:S(2)}) collective-permute-start(bf16[128,4224]{1,0:T(8,128)(2,1)S(1)} %collective-permute-done.9.refs_1_), channel_id=1, source_target_pairs={{0,1},{1,0},{2,3},{3,2},{4,5},{5,4},{6,7},{7,6},{8,9},{9,8},{10,11... | collective-permute-start | bytes 3244040 | tf_op jit(solution)/shard_map/swap_in_3/ppermute | solution.py:258
  49.6 11.2 %collective-permute-start.18 = (bf16[64,4224]{1,0:T(8,128)(2,1)S(1)}, bf16[64,4224]{1,0:T(8,128)(2,1)S(1)}, u32[]{:S(2)}, u32[]{:S(2)}) collective-permute-start(bf16[64,4224]{1,0:T(8,128)(2,1)S(1)} %slice.4), channel_id=1, source_target_pairs={{0,4},{1,3},{4,8},{5,1},{8,12},{9,5},{12,14},{13,9},{14,10},{15,13... | collective-permute-start | bytes 1622024 | tf_op jit(solution)/shard_map/gather_4/ppermute | solution.py:258
  58.7 2.0 %collective-permute-start.11 = (bf16[64,4096]{1,0:T(8,128)(2,1)S(1)}, bf16[64,4096]{1,0:T(8,128)(2,1)S(1)}, u32[]{:S(2)}, u32[]{:S(2)}) collective-permute-start(bf16[64,4096]{1,0:T(8,128)(2,1)S(1)} %get-tuple-element.47), channel_id=1, source_target_pairs={{0,1},{1,0},{2,3},{3,2},{4,5},{5,4},{6,7},{7,6},{8,9},{9,8},{10,11... | collective-permute-start | bytes 1572872 | tf_op jit(solution)/shard_map/swap_out_3/ppermute | solution.py:258
  60.8 2.3 %collective-permute-start.19 = (bf16[64,4224]{1,0:T(8,128)(2,1)S(1)}, bf16[64,4224]{1,0:T(8,128)(2,1)S(1)}, u32[]{:S(2)}, u32[]{:S(2)}) collective-permute-start(bf16[64,4224]{1,0:T(8,128)(2,1)S(1)} %collective-permute-done.18.refs_1_), channel_id=1, source_target_pairs={{0,1},{1,0},{2,3},{3,2},{4,5},{5,4},{6,7},{7,6},{8,9},{9,8},{10,11... | collective-permute-start | bytes 1622024 | tf_op jit(solution)/shard_map/swap_in_4/ppermute | solution.py:258
  61.0 9.2 %collective-permute-start.12 = (bf16[64,4096]{1,0:T(8,128)(2,1)S(1)}, bf16[64,4096]{1,0:T(8,128)(2,1)S(1)}, u32[]{:S(2)}, u32[]{:S(2)}) collective-permute-start(bf16[64,4096]{1,0:T(8,128)(2,1)S(1)} %step_sum.9), channel_id=1, source_target_pairs={{0,4},{1,3},{4,8},{5,1},{8,12},{9,5},{12,14},{13,9},{14,10},{15,13... | collective-permute-start | bytes 1572872 | tf_op jit(solution)/shard_map/return_short_3/ppermute | solution.py:258
  67.0 3.1 %collective-permute-start.20 = (bf16[64,4096]{1,0:T(8,128)(2,1)S(1)}, bf16[64,4096]{1,0:T(8,128)(2,1)S(1)}, u32[]{:S(2)}, u32[]{:S(2)}) collective-permute-start(bf16[64,4096]{1,0:T(8,128)(2,1)S(1)} %get-tuple-element.55), channel_id=1, source_target_pairs={{0,1},{1,0},{2,3},{3,2},{4,5},{5,4},{6,7},{7,6},{8,9},{9,8},{10,11... | collective-permute-start | bytes 1572872 | tf_op jit(solution)/shard_map/swap_out_4/ppermute | solution.py:258
  67.1 5.8 %collective-permute-start.8 = (bf16[64,4096]{1,0:T(8,128)(2,1)S(1)}, bf16[64,4096]{1,0:T(8,128)(2,1)S(1)}, u32[]{:S(2)}, u32[]{:S(2)}) collective-permute-start(bf16[64,4096]{1,0:T(8,128)(2,1)S(1)} %get-tuple-element.44), channel_id=1, source_target_pairs={{0,1},{1,0},{2,3},{3,2},{4,5},{5,4},{6,7},{7,6},{8,9},{9,8},{10,11... | collective-permute-start | bytes 1572872 | tf_op jit(solution)/shard_map/swap_out_2/ppermute | solution.py:258
  70.3 9.2 %collective-permute-start.21 = (bf16[64,4096]{1,0:T(8,128)(2,1)S(1)}, bf16[64,4096]{1,0:T(8,128)(2,1)S(1)}, u32[]{:S(2)}, u32[]{:S(2)}) collective-permute-start(bf16[64,4096]{1,0:T(8,128)(2,1)S(1)} %step_sum.12), channel_id=1, source_target_pairs={{0,4},{1,3},{4,8},{5,1},{8,12},{9,5},{12,14},{13,9},{14,10},{15,13... | collective-permute-start | bytes 1572872 | tf_op jit(solution)/shard_map/return_long_4/ppermute | solution.py:258
  72.5 7.1 %collective-permute-start.17 = (bf16[64,4096]{1,0:T(8,128)(2,1)S(1)}, bf16[64,4096]{1,0:T(8,128)(2,1)S(1)}, u32[]{:S(2)}, u32[]{:S(2)}) collective-permute-start(bf16[64,4096]{1,0:T(8,128)(2,1)S(1)} %get-tuple-element.50), channel_id=1, source_target_pairs={{0,1},{1,0},{2,3},{3,2},{4,5},{5,4},{6,7},{7,6},{8,9},{9,8},{10,11... | collective-permute-start | bytes 1572872 | tf_op jit(solution)/shard_map/swap_out_3/ppermute | solution.py:258
  72.5 10.0 %collective-permute-start.5 = (bf16[64,4096]{1,0:T(8,128)(2,1)S(1)}, bf16[64,4096]{1,0:T(8,128)(2,1)S(1)}, u32[]{:S(2)}, u32[]{:S(2)}) collective-permute-start(bf16[64,4096]{1,0:T(8,128)(2,1)S(1)} %get-tuple-element.41), channel_id=1, source_target_pairs={{0,1},{1,0},{2,3},{3,2},{4,5},{5,4},{6,7},{7,6},{8,9},{9,8},{10,11... | collective-permute-start | bytes 1572872 | tf_op jit(solution)/shard_map/swap_out_1/ppermute | solution.py:258
  73.2 12.0 %collective-permute-start.13 = (bf16[64,4096]{1,0:T(8,128)(2,1)S(1)}, bf16[64,4096]{1,0:T(8,128)(2,1)S(1)}, u32[]{:S(2)}, u32[]{:S(2)}) collective-permute-start(bf16[64,4096]{1,0:T(8,128)(2,1)S(1)} %step_sum.10), channel_id=1, source_target_pairs={{0,4},{1,3},{4,8},{5,1},{8,12},{9,5},{12,14},{13,9},{14,10},{15,13... | collective-permute-start | bytes 1572872 | tf_op jit(solution)/shard_map/return_short_2/ppermute | solution.py:258
  79.8 11.0 %collective-permute-start.22 = (bf16[64,4096]{1,0:T(8,128)(2,1)S(1)}, bf16[64,4096]{1,0:T(8,128)(2,1)S(1)}, u32[]{:S(2)}, u32[]{:S(2)}) collective-permute-start(bf16[64,4096]{1,0:T(8,128)(2,1)S(1)} %step_sum.13), channel_id=1, source_target_pairs={{0,4},{1,3},{4,8},{5,1},{8,12},{9,5},{12,14},{13,9},{14,10},{15,13... | collective-permute-start | bytes 1572872 | tf_op jit(solution)/shard_map/return_long_3/ppermute | solution.py:258
  81.9 8.9 %collective-permute-start.16 = (bf16[64,4096]{1,0:T(8,128)(2,1)S(1)}, bf16[64,4096]{1,0:T(8,128)(2,1)S(1)}, u32[]{:S(2)}, u32[]{:S(2)}) collective-permute-start(bf16[64,4096]{1,0:T(8,128)(2,1)S(1)} %get-tuple-element.49), channel_id=1, source_target_pairs={{0,1},{1,0},{2,3},{3,2},{4,5},{5,4},{6,7},{7,6},{8,9},{9,8},{10,11... | collective-permute-start | bytes 1572872 | tf_op jit(solution)/shard_map/swap_out_2/ppermute | solution.py:258
  81.9 13.1 %collective-permute-start.15 = (bf16[64,4096]{1,0:T(8,128)(2,1)S(1)}, bf16[64,4096]{1,0:T(8,128)(2,1)S(1)}, u32[]{:S(2)}, u32[]{:S(2)}) collective-permute-start(bf16[64,4096]{1,0:T(8,128)(2,1)S(1)} %get-tuple-element.48), channel_id=1, source_target_pairs={{0,1},{1,0},{2,3},{3,2},{4,5},{5,4},{6,7},{7,6},{8,9},{9,8},{10,11... | collective-permute-start | bytes 1572872 | tf_op jit(solution)/shard_map/swap_out_1/ppermute | solution.py:258
  91.0 9.2 %collective-permute-start.23 = (bf16[64,4096]{1,0:T(8,128)(2,1)S(1)}, bf16[64,4096]{1,0:T(8,128)(2,1)S(1)}, u32[]{:S(2)}, u32[]{:S(2)}) collective-permute-start(bf16[64,4096]{1,0:T(8,128)(2,1)S(1)} %step_sum.15), channel_id=1, source_target_pairs={{0,4},{1,3},{4,8},{5,1},{8,12},{9,5},{12,14},{13,9},{14,10},{15,13... | collective-permute-start | bytes 1572872 | tf_op jit(solution)/shard_map/return_long_2/ppermute | solution.py:258
  93.1 9.5 %collective-permute-start.1 = (bf16[64,4096]{1,0:T(8,128)(2,1)S(1)}, bf16[64,4096]{1,0:T(8,128)(2,1)S(1)}, u32[]{:S(2)}, u32[]{:S(2)}) collective-permute-start(bf16[64,4096]{1,0:T(8,128)(2,1)S(1)} %get-tuple-element.36), channel_id=1, source_target_pairs={{0,1},{1,0},{2,3},{3,2},{4,5},{5,4},{6,7},{7,6},{8,9},{9,8},{10,11... | collective-permute-start | bytes 1572872 | tf_op jit(solution)/shard_map/swap_out_0/ppermute | solution.py:258
  93.1 9.9 %collective-permute-start.14 = (bf16[32,4096]{1,0:T(8,128)(2,1)S(1)}, bf16[32,4096]{1,0:T(8,128)(2,1)S(1)}, u32[]{:S(2)}, u32[]{:S(2)}) collective-permute-start(bf16[32,4096]{1,0:T(8,128)(2,1)S(1)} %step_sum.11), channel_id=1, source_target_pairs={{0,4},{1,3},{4,8},{5,1},{8,12},{9,5},{12,14},{13,9},{14,10},{15,13... | collective-permute-start | bytes 786440 | tf_op jit(solution)/shard_map/return_short_1/ppermute | solution.py:258
  94.7 10.7 %collective-permute-start.26 = (bf16[32,4096]{1,0:T(8,128)(2,1)S(1)}, bf16[32,4096]{1,0:T(8,128)(2,1)S(1)}, u32[]{:S(2)}, u32[]{:S(2)}) collective-permute-start(bf16[32,4096]{1,0:T(8,128)(2,1)S(1)} %step_sum.14), channel_id=1, source_target_pairs={{0,5},{1,2},{4,9},{5,0},{8,13},{9,4},{12,15},{13,8},{14,11},{15,12... | collective-permute-start | bytes 786440 | tf_op jit(solution)/shard_map/return_short_1/ppermute | solution.py:258
  100.3 7.9 %collective-permute-start.24 = (bf16[32,4096]{1,0:T(8,128)(2,1)S(1)}, bf16[32,4096]{1,0:T(8,128)(2,1)S(1)}, u32[]{:S(2)}, u32[]{:S(2)}) collective-permute-start(bf16[32,4096]{1,0:T(8,128)(2,1)S(1)} %step_sum.16), channel_id=1, source_target_pairs={{0,5},{1,2},{4,9},{5,0},{8,13},{9,4},{12,15},{13,8},{14,11},{15,12... | collective-permute-start | bytes 786440 | tf_op jit(solution)/shard_map/return_long_1/ppermute | solution.py:258
  100.5 10.9 %collective-permute-start.25 = (bf16[32,4096]{1,0:T(8,128)(2,1)S(1)}, bf16[32,4096]{1,0:T(8,128)(2,1)S(1)}, u32[]{:S(2)}, u32[]{:S(2)}) collective-permute-start(bf16[32,4096]{1,0:T(8,128)(2,1)S(1)} %step_sum.17), channel_id=1, source_target_pairs={{0,4},{1,3},{4,8},{5,1},{8,12},{9,5},{12,14},{13,9},{14,10},{15,13... | collective-permute-start | bytes 786440 | tf_op jit(solution)/shard_map/return_long_1/ppermute | solution.py:258

commit v8 on v7

v8 whole, which is shorter than its diff:
```python
import functools

import jax
import jax.numpy as jnp
from jax import lax
from jax.experimental import pallas as pl
from jax.experimental.pallas import tpu as pltpu
from jax.sharding import PartitionSpec as P

DENOMINATOR = 32768.0
LANES = 128
UNIT_CHUNK = 256
WIDTH_CHUNK = 1024
ANYWHERE = pl.BlockSpec(memory_space=pl.ANY)
VMEM = pl.BlockSpec(memory_space=pltpu.VMEM)
SMEM = pl.BlockSpec(memory_space=pltpu.SMEM)


def ring_of(chips):
    if chips == 8:
        return [0, 2, 4, 6, 7, 5, 3, 1]
    return list(range(chips))


def limits(mebibytes):
    return pltpu.CompilerParams(vmem_limit_bytes=mebibytes << 20)


def pack_kernel(experts, core, tokens, routes, gate_num, own, for_other, digits):
    rows, width = tokens.shape
    half = rows // 2
    lane = lax.broadcasted_iota(jnp.int32, (rows, LANES), 1)
    expert = jnp.where(lane < experts, lane, lane - experts)
    dense = jnp.zeros((rows, LANES), jnp.int32)
    for pick in range(routes.shape[1]):
        column = slice(pick, pick + 1)
        dense += jnp.where(routes[:, column] == expert, gate_num[:, column], 0)
    digit = jnp.where(lane < experts, dense >> 8, dense & 255)
    digit = jnp.where(lane < 2 * experts, digit, 0)
    digits[...] = digit.astype(jnp.float32).astype(jnp.bfloat16)
    for packed, place in ((own, core[0]), (for_other, 1 - core[0])):
        for there, place_here in ((0, place), (half, 1 - place)):
            here = pl.ds(pl.multiple_of(place_here * half, half), half)
            packed[there : there + half, :width] = tokens[here]
            packed[there : there + half, width:] = digits[here]


def pack(core, tokens, routes, gate_num, experts):
    rows, width = tokens.shape
    return pl.pallas_call(
        functools.partial(pack_kernel, experts),
        in_specs=[SMEM] + [VMEM] * 3,
        out_specs=[VMEM] * 2,
        out_shape=[jax.ShapeDtypeStruct((rows, width + LANES), jnp.bfloat16)] * 2,
        scratch_shapes=[pltpu.VMEM((rows, LANES), jnp.bfloat16)],
        compiler_params=limits(2),
        name="pack",
    )(core, tokens, routes, gate_num)


def expert_kernel(count, experts, has_before, fetch, *refs):
    refs = list(refs)
    take = lambda number: [refs.pop(0) for _ in range(number)]
    xs, sets = take(count), [take(5) for _ in range(experts)]
    before = take(count) if has_before else []
    outs, here = take(count), take(2) if fetch else []
    (x,), hiddens, sems = take(1), take(experts), refs
    units, width = sets[0][4].shape

    def unit_columns(chunk, side):
        return pl.ds(pl.multiple_of(side * units + chunk * UNIT_CHUNK, UNIT_CHUNK), UNIT_CHUNK)

    def width_columns(chunk):
        return pl.ds(pl.multiple_of(chunk * WIDTH_CHUNK, WIDTH_CHUNK), WIDTH_CHUNK)

    def unit_copy(chunk, side):
        columns = unit_columns(chunk, side)
        return pltpu.make_async_copy(there[0].at[:, columns], here[0].at[:, columns], sems[0].at[chunk, side])

    def width_copy(chunk):
        columns = width_columns(chunk)
        return pltpu.make_async_copy(there[1].at[:, columns], here[1].at[:, columns], sems[1].at[chunk])

    if fetch:
        there = sets[0][3:]
        sets[0][3:] = here
        for chunk in range(units // UNIT_CHUNK):
            for side in range(2):
                unit_copy(chunk, side).start()
        for chunk in range(width // WIDTH_CHUNK):
            width_copy(chunk).start()

    at = 0
    for ref in xs:
        x[at : at + ref.shape[0]] = ref[...]
        at += ref.shape[0]
    digits = x[:, width:].astype(jnp.float32)
    gates = [jnp.sum(digits * pick[...], axis=1, keepdims=True) / DENOMINATOR for pick, *_ in sets]

    for (_, gate_up_s, _, gate_up, _), hidden in zip(sets, hiddens):

        def unit_step(chunk, carry, gate_up_s=gate_up_s, gate_up=gate_up, hidden=hidden):
            sides = []
            for side in range(2):
                columns = unit_columns(chunk, side)
                if fetch:
                    unit_copy(chunk, side).wait()
                part = jnp.dot(x[:, :width], gate_up[:, columns], preferred_element_type=jnp.float32)
                sides.append(part * gate_up_s[:, columns])
            hidden[:, unit_columns(chunk, 0)] = (jax.nn.silu(sides[0]) * sides[1]).astype(jnp.bfloat16)
            return carry

        lax.fori_loop(0, units // UNIT_CHUNK, unit_step, 0)

    def width_step(chunk, carry):
        columns = width_columns(chunk)
        if fetch:
            width_copy(chunk).wait()
        total = 0.0
        for (_, _, down_s, _, down), hidden, gate in zip(sets, hiddens, gates):
            part = jnp.dot(hidden[...], down[:, columns], preferred_element_type=jnp.float32)
            total += part * down_s[:, columns] * gate
        at = 0
        for number, ref in enumerate(outs):
            part = total[at : at + ref.shape[0]]
            if has_before:
                part += before[number][:, columns].astype(jnp.float32)
            ref[:, columns] = part.astype(jnp.bfloat16)
            at += ref.shape[0]
        return carry

    lax.fori_loop(0, width // WIDTH_CHUNK, width_step, 0)


def expert_part(blocks, sets, before=(), fetch=False):
    units, width = sets[0][4].shape
    rows, packed_width = sum(block.shape[0] for block in blocks), blocks[0].shape[1]
    space = pltpu.HBM if fetch else pltpu.VMEM
    operands, specs = list(blocks), [VMEM] * len(blocks)
    for pick, gate_up_s, down_s, gate_up_w, down_w in sets:
        operands += [pick, gate_up_s, down_s]
        operands += [pltpu.with_memory_space_constraint(w, space) for w in (gate_up_w, down_w)]
        specs += [VMEM] * 3 + [ANYWHERE if fetch else VMEM] * 2
    operands += before
    specs += [VMEM] * len(before)
    out_shape = [jax.ShapeDtypeStruct((block.shape[0], width), jnp.bfloat16) for block in blocks]
    scratch = [pltpu.VMEM((rows, packed_width), jnp.bfloat16)]
    scratch += [pltpu.VMEM((rows, units), jnp.bfloat16)] * len(sets)
    if fetch:
        out_shape += [pltpu.VMEM(w.shape, w.dtype) for w in sets[0][3:]]
        scratch.append(pltpu.SemaphoreType.DMA((units // UNIT_CHUNK, 2)))
        scratch.append(pltpu.SemaphoreType.DMA((width // WIDTH_CHUNK,)))
    return pl.pallas_call(
        functools.partial(expert_kernel, len(blocks), len(sets), bool(before), fetch),
        in_specs=specs,
        out_specs=[VMEM] * len(out_shape),
        out_shape=out_shape,
        scratch_shapes=scratch,
        compiler_params=limits(6),
        cost_estimate=pl.CostEstimate(
            flops=2 * len(sets) * 2 * rows * width * 3 * units, bytes_accessed=0, transcendentals=0
        ),
        name="expert",
    )(*operands)


def step_kernel(plan, *refs):
    *terms, out = refs
    for first, rows, places in plan:
        for column in range(0, out.shape[1], WIDTH_CHUNK):
            columns = slice(column, column + WIDTH_CHUNK)
            total = 0.0
            for number, start in places:
                total += terms[number][start : start + rows, columns].astype(jnp.float32)
            out[first : first + rows, columns] = total.astype(jnp.bfloat16)


def step_sum(*segments):
    arrays, plan, height = [], [], 0
    for rows, terms in segments:
        places = []
        for array, start in terms:
            number = next((i for i, known in enumerate(arrays) if known is array), len(arrays))
            if number == len(arrays):
                arrays.append(array)
            places.append((number, start))
        plan.append((height, rows, tuple(places)))
        height += rows
    return pl.pallas_call(
        functools.partial(step_kernel, tuple(plan)),
        in_specs=[VMEM] * len(arrays),
        out_specs=VMEM,
        out_shape=jax.ShapeDtypeStruct((height, arrays[0].shape[1]), jnp.bfloat16),
        compiler_params=limits(2),
        name="step_sum",
    )(*arrays)


def join_kernel(same, cross, long, short):
    half = same.shape[0] // 2
    for block, first in ((long, 0), (short, half)):
        block[:half] = same[first : first + half]
        block[half:] = cross[first : first + half]


def join(same, cross):
    return pl.pallas_call(
        join_kernel,
        in_specs=[VMEM] * 2,
        out_specs=[VMEM] * 2,
        out_shape=[jax.ShapeDtypeStruct(same.shape, same.dtype)] * 2,
        compiler_params=limits(2),
        name="join",
    )(same, cross)


def last_kernel(core, mine, *refs):
    *arrived, out = refs
    half = out.shape[0] // 2
    for which, place in ((0, core[0]), (1, 1 - core[0])):
        there = pl.ds(pl.multiple_of(place * half, half), half)
        for column in range(0, out.shape[1], WIDTH_CHUNK):
            columns = slice(column, column + WIDTH_CHUNK)
            total = mine[which * half : (which + 1) * half, columns].astype(jnp.float32)
            for ref in arrived[2 * which : 2 * which + 2]:
                total += ref[:, columns].astype(jnp.float32)
            out[there, columns] = total.astype(jnp.bfloat16)


def last_sum(core, mine, *arrived):
    return pl.pallas_call(
        last_kernel,
        in_specs=[SMEM] + [VMEM] * (1 + len(arrived)),
        out_specs=VMEM,
        out_shape=jax.ShapeDtypeStruct(mine.shape, jnp.bfloat16),
        compiler_params=limits(2),
        name="last_sum",
    )(core, mine, *arrived)


def together(*values):
    return lax.optimization_barrier(values)


def after(value, *others):
    return together(value, *others)[0] if others else value


def body(tokens, routes, gate_num, gate_up_q, gate_up_scale, down_q, down_scale):
    devices = lax.axis_size("expert")
    expert = lax.axis_index("expert")
    chips = devices // 2
    reach = chips // 2
    rows, width = tokens.shape
    half = rows // 2
    ring = ring_of(chips)

    def hop(shift, cross):
        pairs = []
        for place in range(chips):
            for core, way in ((0, shift), (1, -shift)):
                to = ring[(place + way) % chips]
                pairs.append((2 * ring[place] + core, 2 * to + (core ^ cross)))
        return pairs

    on, back, back_to_other = hop(1, 0), hop(-1, 0), hop(-1, 1)
    swap = [(i, i ^ 1) for i in range(devices)]

    def send(x, perm, name):
        with jax.named_scope(name):
            return lax.ppermute(x, "expert", perm)

    def pick(expert):
        lane = jnp.arange(LANES, dtype=jnp.int32)
        digits = jnp.where(lane == expert, 256.0, jnp.where(lane == devices + expert, 1.0, 0.0))
        return digits.astype(jnp.float32)[None, :]

    core = (expert & 1).astype(jnp.int32)[None]
    theirs = [send(x, swap, "weights") for x in (gate_up_q[0], down_q[0])]
    scales = send(jnp.concatenate([gate_up_scale, down_scale], axis=1), swap, "weights")
    theirs += [scales[:, : gate_up_scale.shape[1]], scales[:, gate_up_scale.shape[1] :]]
    own_set = (pick(expert), gate_up_scale, down_scale, gate_up_q[0], down_q[0])
    other_set = (pick(expert ^ 1), theirs[2], theirs[3], theirs[0], theirs[1])

    blocks, mine = {}, {}
    own, own_for_other = pack(core, tokens, routes, gate_num, devices)
    blocks[0] = [own]
    *mine[0], gate_up_w, down_w = expert_part(blocks[0], [own_set], fetch=True)
    own_set = (*own_set[:3], gate_up_w, down_w)
    same, cross = send(own, on, "gather_long_1"), send(own_for_other, back_to_other, "gather_long_1")
    long, short = join(after(same, *mine[0]), cross)
    for distance in range(1, reach):
        if distance > 1:
            tie = mine[distance - 2]
            long = send(after(long, *tie), on, f"gather_long_{distance}")
            short = send(after(short, *tie), on, f"gather_short_{distance}")
        blocks[distance] = [long, short]
        if distance < reach - 1:
            mine[distance] = expert_part(blocks[distance], [own_set])
    for start in range(0, reach - 1, 3):
        near = [(distance, number) for distance in range(start, min(start + 3, reach - 1)) for number in range(len(mine[distance]))]
        done = expert_part(
            [blocks[distance][number] for distance, number in near],
            [other_set],
            [mine[distance][number] for distance, number in near],
            fetch=start == 0,
        )
        if start == 0:
            other_set = (*other_set[:3], *done[-2:])
        for (distance, number), part in zip(near, done):
            mine[distance] = [part if i == number else x for i, x in enumerate(mine[distance])]
    farthest = send(after(long, *mine[reach - 3]), on, f"gather_long_{reach}")
    blocks[reach - 1] = [after(block, mine[0][0]) for block in blocks[reach - 1]]
    mine[reach - 1] = expert_part(blocks[reach - 1], [own_set, other_set])
    mine[reach] = expert_part([after(farthest, *mine[reach - 1])], [own_set, other_set])

    def onward(distance, number, carried):
        terms = [(mine[distance][number], 0)] + [(x, 0) for x in carried]
        name = f"return_{('long', 'short')[number]}_{distance}"
        if distance > 1:
            total = step_sum((rows, terms)) if carried else mine[distance][number]
            return [send(total, back, name)], total
        sent, totals = [], []
        for start, perm in ((0, back), (half, back_to_other)):
            totals.append(step_sum((half, [(x, start) for x, _ in terms])))
            sent.append(send(totals[-1], perm, name))
        return sent, totals[0]

    short, _ = onward(reach - 1, 1, [])
    long, total = onward(reach, 0, [])
    for distance in range(reach - 1, 0, -1):
        if distance > 1:
            short, total = onward(distance - 1, 1, [after(x, total) for x in short])
        long, total = onward(distance, 0, [after(x, total) for x in long])
    return last_sum(core, *mine[0], long[0], short[1], short[0], long[1])


def solution(mesh):
    in_specs = (
        P(("groups", "expert"), None),
        P(("groups", "expert"), None),
        P(("groups", "expert"), None),
        P("expert", None, None),
        P("expert", None),
        P("expert", None, None),
        P("expert", None),
    )
    out_specs = P(("groups", "expert"), None)
    return jax.shard_map(body, mesh=mesh, in_specs=in_specs, out_specs=out_specs, check_vma=False)
```

time: 113 us -> 125 us (1.11)
  Pallas kernels: 36.2 us -> 48.5 us
  starting transfers between devices: 27 us -> 15.8 us
  local copies, waits for them, and re-layouts: 2.62 us -> 13.1 us
  waiting for transfers between devices: 46.5 us -> 44.9 us
    pallas_call x8, Pallas kernels: 34.7 us -> 46.8 us  [the longest x6 45.7 us: expert_part(): pl.pallas_call(functools.partial(expert_kernel, len(blocks), len(sets), b...]
    ppermute x27 -> x19, starting transfers between devices: 27 us -> 15.8 us  [send(): return lax.ppermute(x, 'expert', perm)]
    unnamed x8 -> x16, local copies, waits for them, and re-layouts: 2.59 us -> 13.1 us
    ppermute x27 -> x19, waiting for transfers between devices: 46.5 us -> 44.9 us  [send(): return lax.ppermute(x, 'expert', perm)]
  transfers between devices with their start and end apart: 27 -> 19, of which waited for: 16 -> 11; matrix products, arithmetic and copies ran while one was open for 0% -> 2% of each run, Pallas kernels for 31% -> 38%
where the time goes in v8:
time: 125 us; the launch traced here: 123 us
  Pallas kernels  48.5 us (39%)
  waiting for transfers between devices  44.9 us (36%)
  starting transfers between devices  15.8 us (13%)
  local copies, waits for them, and re-layouts  13.1 us (10%)
    pallas_call x6, Pallas kernels, expert_part(): pl.pallas_call(functools.partial(expert_kernel, len(blocks), len(sets), b...  45.7 us
    ppermute x19, waiting for transfers between devices, send(): return lax.ppermute(x, 'expert', perm)  44.9 us
    ppermute x19, starting transfers between devices, send(): return lax.ppermute(x, 'expert', perm)  15.8 us
    unnamed x16, local copies, waits for them, and re-layouts  13.1 us
  transfers between devices with their start and end apart: 19, of which 11 were waited for; matrix products, arithmetic and copies ran while one was open for 2% of the time, Pallas kernels for 38%

profile of v8, /device:TPU:0, one launch (start us, length us, event | category | flops | bytes accessed | tf_op | source)
XLA Modules:
  0.0 123.3 jit_solution(2891845903232606264)
XLA Ops:
  0.5 0.8 copy.8.routes
  1.3 0.8 copy.9.gate_num
  2.1 1.0 copy-done.4
  3.1 1.0 pack.1
  4.2 2.6 %collective-permute-start.1 = (bf16[64,4224]{1,0:T(8,128)(2,1)}, bf16[64,4224]{1,0:T(8,128)(2,1)S(1)}, u32[]{:S(2)}, u32[]{:S(2)}) collective-permute-start(bf16[64,4224]{1,0:T(8,128)(2,1)} %get-tuple-element.42), channel_id=1, source_target_pairs={{0,3},{1,4},{4,1},{5,8},{8,5},{9,12},{12,9},{13,14},{14,13},{15,10... | collective-permute-start | bytes 1622024 | tf_op jit(solution)/shard_map/gather_long_1/ppermute | solution.py:271
  7.2 0.7 pad_maximum_fusion
  8.1 0.7 copy-done.2
  8.8 0.7 copy-done.5
  9.5 8.5 %expert.6 = (bf16[64,4096]{1,0:T(8,128)(2,1)S(1)}, bf16[4096,1536]{1,0:T(8,128)(2,1)S(1)}, bf16[768,4096]{1,0:T(8,128)(2,1)S(1)}) custom-call(bf16[64,4224]{1,0:T(8,128)(2,1)S(1)} %get-tuple-element.39.refs_0_, f32[1,128]{1,0:T(1,128)S(1)} %compare_select_fusion.3.refs_1_.refs_2_, f32[1,1536]{1,0:T(1,128)S(1)} %copy-done.5, f32[1,4096]{1,0:T(1,128)S(1)} %copy-done.2, ...), custom_call_target="tpu_custom_call" | custom-call | flops 2415919104 | tf_op jit(solution)/shard_map/expert/pallas_call | solution.py:153
  18.1 1.8 %collective-permute-done.same = bf16[64,4224]{1,0:T(8,128)(2,1)S(1)} collective-permute-done((bf16[64,4224]{1,0:T(8,128)(2,1)S(1)}, bf16[64,4224]{1,0:T(8,128)(2,1)S(1)}, u32[]{:S(2)}, u32[]{:S(2)}) %collective-permute-start) | collective-permute-done | bytes 540704 | tf_op jit(solution)/shard_map/gather_long_1/ppermute | solution.py:271
  19.9 2.2 %collective-permute-start.3 = (bf16[64,4224]{1,0:T(8,128)(2,1)S(1)}, bf16[64,4224]{1,0:T(8,128)(2,1)S(1)}, u32[]{:S(2)}, u32[]{:S(2)}) collective-permute-start(bf16[64,4224]{1,0:T(8,128)(2,1)S(1)} %get-tuple-element.46.refs_1_.refs_2_), channel_id=1, source_target_pairs={{0,4},{1,3},{4,8},{5,1},{8,12},{9,5},{12,14},{13,9},{14,10},{15,13... | collective-permute-start | bytes 1622024 | tf_op jit(solution)/shard_map/gather_short_2/ppermute | solution.py:271
  22.1 1.6 %collective-permute-start.2 = (bf16[64,4224]{1,0:T(8,128)(2,1)S(1)}, bf16[64,4224]{1,0:T(8,128)(2,1)S(1)}, u32[]{:S(2)}, u32[]{:S(2)}) collective-permute-start(bf16[64,4224]{1,0:T(8,128)(2,1)S(1)} %get-tuple-element.45.refs_0_.refs_1_), channel_id=1, source_target_pairs={{0,4},{1,3},{4,8},{5,1},{8,12},{9,5},{12,14},{13,9},{14,10},{15,13... | collective-permute-start | bytes 1622024 | tf_op jit(solution)/shard_map/gather_long_2/ppermute | solution.py:271
  23.7 4.0 %expert.7 = (bf16[64,4096]{1,0:T(8,128)(2,1)S(1)}, bf16[64,4096]{1,0:T(8,128)(2,1)S(1)}) custom-call(bf16[64,4224]{1,0:T(8,128)(2,1)S(1)} %get-tuple-element.45.refs_0_.refs_1_, bf16[64,4224]{1,0:T(8,128)(2,1)S(1)} %get-tuple-element.46.refs_1_.refs_2_, f32[1,128]{1,0:T(1,128)S(1)} %compare_select_fusion.3.refs_1_.refs_2_, f32[1,1536]{1,0:T(1,128)S(1)} %copy-done.6, ...), custom_call_target="tpu_custom_call" | custom-call | flops 4831838208 | tf_op jit(solution)/shard_map/expert/pallas_call | solution.py:153
  27.7 1.7 %collective-permute-done.3.refs_1_.refs_4_ = bf16[64,4224]{1,0:T(8,128)(2,1)S(1)} collective-permute-done((bf16[64,4224]{1,0:T(8,128)(2,1)S(1)}, bf16[64,4224]{1,0:T(8,128)(2,1)S(1)}, u32[]{:S(2)}, u32[]{:S(2)}) %collective-permute-start.3) | collective-permute-done | bytes 540704 | tf_op jit(solution)/shard_map/gather_short_2/ppermute | solution.py:271
  29.4 5.8 %collective-permute-done.2.refs_0_.refs_3_ = bf16[64,4224]{1,0:T(8,128)(2,1)S(1)} collective-permute-done((bf16[64,4224]{1,0:T(8,128)(2,1)S(1)}, bf16[64,4224]{1,0:T(8,128)(2,1)S(1)}, u32[]{:S(2)}, u32[]{:S(2)}) %collective-permute-start.2) | collective-permute-done | bytes 540704 | tf_op jit(solution)/shard_map/gather_long_2/ppermute | solution.py:271
  35.2 2.1 %collective-permute-start.7 = (bf16[64,4224]{1,0:T(8,128)(2,1)S(1)}, bf16[64,4224]{1,0:T(8,128)(2,1)S(1)}, u32[]{:S(2)}, u32[]{:S(2)}) collective-permute-start(bf16[64,4224]{1,0:T(8,128)(2,1)S(1)} %collective-permute-done.2.refs_0_.refs_3_), channel_id=1, source_target_pairs={{0,4},{1,3},{4,8},{5,1},{8,12},{9,5},{12,14},{13,9},{14,10},{15,13... | collective-permute-start | bytes 1622024 | tf_op jit(solution)/shard_map/gather_long_3/ppermute | solution.py:271
  37.2 1.6 %collective-permute-start.8 = (bf16[64,4224]{1,0:T(8,128)(2,1)S(1)}, bf16[64,4224]{1,0:T(8,128)(2,1)S(1)}, u32[]{:S(2)}, u32[]{:S(2)}) collective-permute-start(bf16[64,4224]{1,0:T(8,128)(2,1)S(1)} %collective-permute-done.3.refs_1_.refs_4_), channel_id=1, source_target_pairs={{0,4},{1,3},{4,8},{5,1},{8,12},{9,5},{12,14},{13,9},{14,10},{15,13... | collective-permute-start | bytes 1622024 | tf_op jit(solution)/shard_map/gather_short_3/ppermute | solution.py:271
  38.8 4.0 %expert.8 = (bf16[64,4096]{1,0:T(8,128)(2,1)S(1)}, bf16[64,4096]{1,0:T(8,128)(2,1)S(1)}) custom-call(bf16[64,4224]{1,0:T(8,128)(2,1)S(1)} %collective-permute-done.2.refs_0_.refs_3_, bf16[64,4224]{1,0:T(8,128)(2,1)S(1)} %collective-permute-done.3.refs_1_.refs_4_, f32[1,128]{1,0:T(1,128)S(1)} %compare_select_fusion.3.refs_1_.refs_2_, ...), custom_call_target="tpu_custom_call" | custom-call | flops 4831838208 | tf_op jit(solution)/shard_map/expert/pallas_call | solution.py:153
  42.8 14.0 %expert.9 = (bf16[64,4096]{1,0:T(8,128)(2,1)S(1)}, bf16[64,4096]{1,0:T(8,128)(2,1)S(1)}, bf16[64,4096]{1,0:T(8,128)(2,1)S(1)}, bf16[64,4096]{1,0:T(8,128)(2,1)S(...) custom-call(bf16[64,4224]{1,0:T(8,128)(2,1)S(1)} %get-tuple-element.39.refs_0_, ...), custom_call_target="tpu_custom_call" | custom-call | flops 12079595520 | tf_op jit(solution)/shard_map/expert/pallas_call | solution.py:153
  56.9 4.5 %copy-done = bf16[4096,1536]{1,0:T(8,128)(2,1)} copy-done((bf16[4096,1536]{1,0:T(8,128)(2,1)}, bf16[4096,1536]{1,0:T(8,128)(2,1)S(1)}, u32[]{:S(2)}) %copy-start) | copy-done | bytes 12582936
  61.4 1.6 %collective-permute-start.9 = (bf16[64,4224]{1,0:T(8,128)(2,1)S(1)}, bf16[64,4224]{1,0:T(8,128)(2,1)S(1)}, u32[]{:S(2)}, u32[]{:S(2)}) collective-permute-start(bf16[64,4224]{1,0:T(8,128)(2,1)S(1)} %collective-permute-done.7.refs_0_), channel_id=1, source_target_pairs={{0,4},{1,3},{4,8},{5,1},{8,12},{9,5},{12,14},{13,9},{14,10},{15,13... | collective-permute-start | bytes 1622024 | tf_op jit(solution)/shard_map/gather_long_4/ppermute | solution.py:271
  63.0 4.6 %copy-done.1 = bf16[4096,1536]{1,0:T(8,128)(2,1)S(1)} copy-done((bf16[4096,1536]{1,0:T(8,128)(2,1)S(1)}, bf16[4096,1536]{1,0:T(8,128)(2,1)}, u32[]{:S(2)}) %copy-start.1) | copy-done | bytes 12582936
  67.5 7.2 %expert.10 = (bf16[64,4096]{1,0:T(8,128)(2,1)S(1)}, bf16[64,4096]{1,0:T(8,128)(2,1)S(1)}) custom-call(bf16[64,4224]{1,0:T(8,128)(2,1)S(1)} %collective-permute-done.7.refs_0_, bf16[64,4224]{1,0:T(8,128)(2,1)S(1)} %collective-permute-done.8.refs_1_, f32[1,128]{1,0:T(1,128)S(1)} %compare_select_fusion.3.refs_1_.refs_2_, f32[1,1536]{1,0:T(1,128)S(1)} %copy-done.6, ...), custom_call_target="tpu_custom_call" | custom-call | flops 9663676416 | tf_op jit(solution)/shard_map/expert/pallas_call | solution.py:153
  75.3 8.0 %expert.11 = bf16[64,4096]{1,0:T(8,128)(2,1)S(1)} custom-call(bf16[64,4224]{1,0:T(8,128)(2,1)S(1)} %collective-permute-done.9.refs_0_, f32[1,128]{1,0:T(1,128)S(1)} %compare_select_fusion.3.refs_1_.refs_2_, f32[1,1536]{1,0:T(1,128)S(1)} %copy-done.6, f32[1,4096]{1,0:T(1,128)S(1)} %copy-done.3, bf16[4096,1536]{1,0:T(8,128)(2,1)S(1)} %get-tuple-element.47.refs_5_.refs_4_, ...), custom_call_target="tpu_custom_call" | custom-call | flops 4831838208 | tf_op jit(solution)/shard_map/expert/pallas_call | solution.py:153
  84.6 7.9 %collective-permute-done.10.refs_1_ = bf16[64,4096]{1,0:T(8,128)(2,1)S(1)} collective-permute-done((bf16[64,4096]{1,0:T(8,128)(2,1)S(1)}, bf16[64,4096]{1,0:T(8,128)(2,1)S(1)}, u32[]{:S(2)}, u32[]{:S(2)}) %collective-permute-start.10) | collective-permute-done | bytes 524320 | tf_op jit(solution)/shard_map/return_long_4/ppermute | solution.py:271
  93.1 5.0 %collective-permute-done.13.refs_1_ = bf16[64,4096]{1,0:T(8,128)(2,1)S(1)} collective-permute-done((bf16[64,4096]{1,0:T(8,128)(2,1)S(1)}, bf16[64,4096]{1,0:T(8,128)(2,1)S(1)}, u32[]{:S(2)}, u32[]{:S(2)}) %collective-permute-start.13) | collective-permute-done | bytes 524320 | tf_op jit(solution)/shard_map/return_short_2/ppermute | solution.py:271
  98.2 5.5 %collective-permute-done.12.refs_1_ = bf16[64,4096]{1,0:T(8,128)(2,1)S(1)} collective-permute-done((bf16[64,4096]{1,0:T(8,128)(2,1)S(1)}, bf16[64,4096]{1,0:T(8,128)(2,1)S(1)}, u32[]{:S(2)}, u32[]{:S(2)}) %collective-permute-start.12) | collective-permute-done | bytes 524320 | tf_op jit(solution)/shard_map/return_long_3/ppermute | solution.py:271
  104.6 8.5 %collective-permute-done.14.refs_1_ = bf16[64,4096]{1,0:T(8,128)(2,1)S(1)} collective-permute-done((bf16[64,4096]{1,0:T(8,128)(2,1)S(1)}, bf16[64,4096]{1,0:T(8,128)(2,1)S(1)}, u32[]{:S(2)}, u32[]{:S(2)}) %collective-permute-start.14) | collective-permute-done | bytes 524320 | tf_op jit(solution)/shard_map/return_long_2/ppermute | solution.py:271
  113.8 2.9 %collective-permute-done.16.refs_1_ = bf16[32,4096]{1,0:T(8,128)(2,1)S(1)} collective-permute-done((bf16[32,4096]{1,0:T(8,128)(2,1)S(1)}, bf16[32,4096]{1,0:T(8,128)(2,1)S(1)}, u32[]{:S(2)}, u32[]{:S(2)}) %collective-permute-start.16) | collective-permute-done | bytes 262176 | tf_op jit(solution)/shard_map/return_short_1/ppermute | solution.py:271
  116.7 4.8 %collective-permute-done.15.refs_0_ = bf16[32,4096]{1,0:T(8,128)(2,1)S(1)} collective-permute-done((bf16[32,4096]{1,0:T(8,128)(2,1)S(1)}, bf16[32,4096]{1,0:T(8,128)(2,1)S(1)}, u32[]{:S(2)}, u32[]{:S(2)}) %collective-permute-start.15) | collective-permute-done | bytes 262176 | tf_op jit(solution)/shard_map/return_long_1/ppermute | solution.py:271
  121.5 0.8 collective-permute-done.18.refs_3_
  122.3 1.0 last_sum.1
  (43 shorter events, 5.2 us)
Async XLA Ops:
  0.0 23.7 %copy-start.3 = (f32[1,4096]{1,0:T(1,128)S(1)}, f32[1,4096]{1,0:T(1,128)}, u32[]{:S(2)}) copy-start(f32[1,4096]{1,0:T(1,128)} %refs_3_.9) | copy-start | bytes 49156
  0.0 23.7 %copy-start.6 = (f32[1,1536]{1,0:T(1,128)S(1)}, f32[1,1536]{1,0:T(1,128)}, u32[]{:S(2)}) copy-start(f32[1,1536]{1,0:T(1,128)} %refs_2_.3) | copy-start | bytes 18436
  0.0 42.8 %collective-permute-start.5 = (bf16[4096,1536]{1,0:T(8,128)(2,1)}, bf16[4096,1536]{1,0:T(8,128)(2,1)}, u32[]{:S(2)}, u32[]{:S(2)}) collective-permute-start(bf16[4096,1536]{1,0:T(8,128)(2,1)} %bitcast.3), channel_id=1, source_target_pairs={{0,1},{1,0},{2,3},{3,2},{4,5},{5,4},{6,7},{7,6},{8,9},{9,8},{10,11... | collective-permute-start | bytes 37748744 | tf_op jit(solution)/shard_map/weights/ppermute | solution.py:271
  0.5 42.3 %collective-permute-start.6 = (bf16[768,4096]{1,0:T(8,128)(2,1)}, bf16[768,4096]{1,0:T(8,128)(2,1)}, u32[]{:S(2)}, u32[]{:S(2)}) collective-permute-start(bf16[768,4096]{1,0:T(8,128)(2,1)} %bitcast.5), channel_id=1, source_target_pairs={{0,1},{1,0},{2,3},{3,2},{4,5},{5,4},{6,7},{7,6},{8,9},{9,8},{10,11... | collective-permute-start | bytes 18874376 | tf_op jit(solution)/shard_map/weights/ppermute | solution.py:271
  2.1 1.0 copy-start.4
  4.2 15.7 %collective-permute-start.1 = (bf16[64,4224]{1,0:T(8,128)(2,1)}, bf16[64,4224]{1,0:T(8,128)(2,1)S(1)}, u32[]{:S(2)}, u32[]{:S(2)}) collective-permute-start(bf16[64,4224]{1,0:T(8,128)(2,1)} %get-tuple-element.42), channel_id=1, source_target_pairs={{0,3},{1,4},{4,1},{5,8},{8,5},{9,12},{12,9},{13,14},{14,13},{15,10... | collective-permute-start | bytes 1622024 | tf_op jit(solution)/shard_map/gather_long_1/ppermute | solution.py:271
  6.8 13.0 %collective-permute-start = (bf16[64,4224]{1,0:T(8,128)(2,1)S(1)}, bf16[64,4224]{1,0:T(8,128)(2,1)S(1)}, u32[]{:S(2)}, u32[]{:S(2)}) collective-permute-start(bf16[64,4224]{1,0:T(8,128)(2,1)S(1)} %get-tuple-element.39.refs_0_), channel_id=1, source_target_pairs={{0,4},{1,3},{4,8},{5,1},{8,12},{9,5},{12,14},{13,9},{14,10},{15,13... | collective-permute-start | bytes 1622024 | tf_op jit(solution)/shard_map/gather_long_1/ppermute | solution.py:271
  7.9 15.7 %collective-permute-start.4 = (f32[1,5632]{1,0:T(1,128)S(1)}, f32[1,5632]{1,0:T(1,128)S(1)}, u32[]{:S(2)}, u32[]{:S(2)}) collective-permute-start(f32[1,5632]{1,0:T(1,128)S(1)} %pad_maximum_fusion), channel_id=1, source_target_pairs={{0,1},{1,0},{2,3},{3,2},{4,5},{5,4},{6,7},{7,6},{8,9},{9,8},{10,11... | collective-permute-start | bytes 67592 | tf_op jit(solution)/shard_map/weights/ppermute | solution.py:271
  8.1 0.7 copy-start.2
  8.8 0.7 copy-start.5
  19.9 9.4 %collective-permute-start.3 = (bf16[64,4224]{1,0:T(8,128)(2,1)S(1)}, bf16[64,4224]{1,0:T(8,128)(2,1)S(1)}, u32[]{:S(2)}, u32[]{:S(2)}) collective-permute-start(bf16[64,4224]{1,0:T(8,128)(2,1)S(1)} %get-tuple-element.46.refs_1_.refs_2_), channel_id=1, source_target_pairs={{0,4},{1,3},{4,8},{5,1},{8,12},{9,5},{12,14},{13,9},{14,10},{15,13... | collective-permute-start | bytes 1622024 | tf_op jit(solution)/shard_map/gather_short_2/ppermute | solution.py:271
  22.1 13.1 %collective-permute-start.2 = (bf16[64,4224]{1,0:T(8,128)(2,1)S(1)}, bf16[64,4224]{1,0:T(8,128)(2,1)S(1)}, u32[]{:S(2)}, u32[]{:S(2)}) collective-permute-start(bf16[64,4224]{1,0:T(8,128)(2,1)S(1)} %get-tuple-element.45.refs_0_.refs_1_), channel_id=1, source_target_pairs={{0,4},{1,3},{4,8},{5,1},{8,12},{9,5},{12,14},{13,9},{14,10},{15,13... | collective-permute-start | bytes 1622024 | tf_op jit(solution)/shard_map/gather_long_2/ppermute | solution.py:271
  35.2 26.2 %collective-permute-start.7 = (bf16[64,4224]{1,0:T(8,128)(2,1)S(1)}, bf16[64,4224]{1,0:T(8,128)(2,1)S(1)}, u32[]{:S(2)}, u32[]{:S(2)}) collective-permute-start(bf16[64,4224]{1,0:T(8,128)(2,1)S(1)} %collective-permute-done.2.refs_0_.refs_3_), channel_id=1, source_target_pairs={{0,4},{1,3},{4,8},{5,1},{8,12},{9,5},{12,14},{13,9},{14,10},{15,13... | collective-permute-start | bytes 1622024 | tf_op jit(solution)/shard_map/gather_long_3/ppermute | solution.py:271
  37.2 25.7 %collective-permute-start.8 = (bf16[64,4224]{1,0:T(8,128)(2,1)S(1)}, bf16[64,4224]{1,0:T(8,128)(2,1)S(1)}, u32[]{:S(2)}, u32[]{:S(2)}) collective-permute-start(bf16[64,4224]{1,0:T(8,128)(2,1)S(1)} %collective-permute-done.3.refs_1_.refs_4_), channel_id=1, source_target_pairs={{0,4},{1,3},{4,8},{5,1},{8,12},{9,5},{12,14},{13,9},{14,10},{15,13... | collective-permute-start | bytes 1622024 | tf_op jit(solution)/shard_map/gather_short_3/ppermute | solution.py:271
  56.8 4.5 %copy-start = (bf16[4096,1536]{1,0:T(8,128)(2,1)}, bf16[4096,1536]{1,0:T(8,128)(2,1)S(1)}, u32[]{:S(2)}) copy-start(bf16[4096,1536]{1,0:T(8,128)(2,1)S(1)} %get-tuple-element.60.refs_10_.refs_9_) | copy-start | bytes 37748740
  61.4 13.9 %collective-permute-start.9 = (bf16[64,4224]{1,0:T(8,128)(2,1)S(1)}, bf16[64,4224]{1,0:T(8,128)(2,1)S(1)}, u32[]{:S(2)}, u32[]{:S(2)}) collective-permute-start(bf16[64,4224]{1,0:T(8,128)(2,1)S(1)} %collective-permute-done.7.refs_0_), channel_id=1, source_target_pairs={{0,4},{1,3},{4,8},{5,1},{8,12},{9,5},{12,14},{13,9},{14,10},{15,13... | collective-permute-start | bytes 1622024 | tf_op jit(solution)/shard_map/gather_long_4/ppermute | solution.py:271
  63.0 4.6 %copy-start.1 = (bf16[4096,1536]{1,0:T(8,128)(2,1)S(1)}, bf16[4096,1536]{1,0:T(8,128)(2,1)}, u32[]{:S(2)}) copy-start(bf16[4096,1536]{1,0:T(8,128)(2,1)} %copy-done) | copy-start | bytes 37748740
  74.8 9.2 %collective-permute-start.11 = (bf16[64,4096]{1,0:T(8,128)(2,1)S(1)}, bf16[64,4096]{1,0:T(8,128)(2,1)S(1)}, u32[]{:S(2)}, u32[]{:S(2)}) collective-permute-start(bf16[64,4096]{1,0:T(8,128)(2,1)S(1)} %get-tuple-element.65), channel_id=1, source_target_pairs={{0,2},{1,5},{4,0},{5,9},{8,4},{9,13},{12,8},{13,15},{14,12},{15,11... | collective-permute-start | bytes 1572872 | tf_op jit(solution)/shard_map/return_short_3/ppermute | solution.py:271
  83.3 9.2 %collective-permute-start.10 = (bf16[64,4096]{1,0:T(8,128)(2,1)S(1)}, bf16[64,4096]{1,0:T(8,128)(2,1)S(1)}, u32[]{:S(2)}, u32[]{:S(2)}) collective-permute-start(bf16[64,4096]{1,0:T(8,128)(2,1)S(1)} %expert.11), channel_id=1, source_target_pairs={{0,2},{1,5},{4,0},{5,9},{8,4},{9,13},{12,8},{13,15},{14,12},{15,11... | collective-permute-start | bytes 1572872 | tf_op jit(solution)/shard_map/return_long_4/ppermute | solution.py:271
  84.1 14.0 %collective-permute-start.13 = (bf16[64,4096]{1,0:T(8,128)(2,1)S(1)}, bf16[64,4096]{1,0:T(8,128)(2,1)S(1)}, u32[]{:S(2)}, u32[]{:S(2)}) collective-permute-start(bf16[64,4096]{1,0:T(8,128)(2,1)S(1)} %step_sum.7), channel_id=1, source_target_pairs={{0,2},{1,5},{4,0},{5,9},{8,4},{9,13},{12,8},{13,15},{14,12},{15,11... | collective-permute-start | bytes 1572872 | tf_op jit(solution)/shard_map/return_short_2/ppermute | solution.py:271
  92.6 11.1 %collective-permute-start.12 = (bf16[64,4096]{1,0:T(8,128)(2,1)S(1)}, bf16[64,4096]{1,0:T(8,128)(2,1)S(1)}, u32[]{:S(2)}, u32[]{:S(2)}) collective-permute-start(bf16[64,4096]{1,0:T(8,128)(2,1)S(1)} %step_sum.8), channel_id=1, source_target_pairs={{0,2},{1,5},{4,0},{5,9},{8,4},{9,13},{12,8},{13,15},{14,12},{15,11... | collective-permute-start | bytes 1572872 | tf_op jit(solution)/shard_map/return_long_3/ppermute | solution.py:271
  103.9 9.2 %collective-permute-start.14 = (bf16[64,4096]{1,0:T(8,128)(2,1)S(1)}, bf16[64,4096]{1,0:T(8,128)(2,1)S(1)}, u32[]{:S(2)}, u32[]{:S(2)}) collective-permute-start(bf16[64,4096]{1,0:T(8,128)(2,1)S(1)} %step_sum.10), channel_id=1, source_target_pairs={{0,2},{1,5},{4,0},{5,9},{8,4},{9,13},{12,8},{13,15},{14,12},{15,11... | collective-permute-start | bytes 1572872 | tf_op jit(solution)/shard_map/return_long_2/ppermute | solution.py:271
  104.4 12.2 %collective-permute-start.17 = (bf16[32,4096]{1,0:T(8,128)(2,1)S(1)}, bf16[32,4096]{1,0:T(8,128)(2,1)S(1)}, u32[]{:S(2)}, u32[]{:S(2)}) collective-permute-start(bf16[32,4096]{1,0:T(8,128)(2,1)S(1)} %step_sum.9), channel_id=1, source_target_pairs={{0,2},{1,5},{4,0},{5,9},{8,4},{9,13},{12,8},{13,15},{14,12},{15,11... | collective-permute-start | bytes 786440 | tf_op jit(solution)/shard_map/return_short_1/ppermute | solution.py:271
  104.5 12.2 %collective-permute-start.16 = (bf16[32,4096]{1,0:T(8,128)(2,1)S(1)}, bf16[32,4096]{1,0:T(8,128)(2,1)S(1)}, u32[]{:S(2)}, u32[]{:S(2)}) collective-permute-start(bf16[32,4096]{1,0:T(8,128)(2,1)S(1)} %step_sum.12), channel_id=1, source_target_pairs={{0,3},{1,4},{4,1},{5,8},{8,5},{9,12},{12,9},{13,14},{14,13},{15,10... | collective-permute-start | bytes 786440 | tf_op jit(solution)/shard_map/return_short_1/ppermute | solution.py:271
  113.2 8.3 %collective-permute-start.15 = (bf16[32,4096]{1,0:T(8,128)(2,1)S(1)}, bf16[32,4096]{1,0:T(8,128)(2,1)S(1)}, u32[]{:S(2)}, u32[]{:S(2)}) collective-permute-start(bf16[32,4096]{1,0:T(8,128)(2,1)S(1)} %step_sum.11), channel_id=1, source_target_pairs={{0,2},{1,5},{4,0},{5,9},{8,4},{9,13},{12,8},{13,15},{14,12},{15,11... | collective-permute-start | bytes 786440 | tf_op jit(solution)/shard_map/return_long_1/ppermute | solution.py:271
  113.7 8.6 %collective-permute-start.18 = (bf16[32,4096]{1,0:T(8,128)(2,1)S(1)}, bf16[32,4096]{1,0:T(8,128)(2,1)S(1)}, u32[]{:S(2)}, u32[]{:S(2)}) collective-permute-start(bf16[32,4096]{1,0:T(8,128)(2,1)S(1)} %step_sum.13), channel_id=1, source_target_pairs={{0,3},{1,4},{4,1},{5,8},{8,5},{9,12},{12,9},{13,14},{14,13},{15,10... | collective-permute-start | bytes 786440 | tf_op jit(solution)/shard_map/return_long_1/ppermute | solution.py:271

commit v9 on v7

--- a/solution.py
+++ b/solution.py
@@ -182,20 +182,20 @@
     )(*arrays)
 
 
-def join_kernel(same, cross, block):
+def join_kernel(same, cross, long, short):
     half = same.shape[0] // 2
-    for number in range(4):
-        place = slice((number // 2) * half, (number // 2 + 1) * half)
-        block[number * half : (number + 1) * half] = (same, cross)[number % 2][place]
+    for block, first in ((long, 0), (short, half)):
+        block[:half] = same[first : first + half]
+        block[half:] = cross[first : first + half]
 
 
 def join(same, cross):
     return pl.pallas_call(
         join_kernel,
         in_specs=[VMEM] * 2,
-        out_specs=VMEM,
-        out_shape=jax.ShapeDtypeStruct((2 * same.shape[0], same.shape[1]), same.dtype),
-        compiler_params=limits(4),
+        out_specs=[VMEM] * 2,
+        out_shape=[jax.ShapeDtypeStruct(same.shape, same.dtype)] * 2,
+        compiler_params=limits(2),
         name="join",
     )(same, cross)
 
@@ -266,57 +266,61 @@
 
     kept, given = {}, {}
 
-    def run(distance, block, cuts, hint):
-        other = send(after(block, kept[distance - 1]), swap, f"swap_in_{distance}")
-        kept[distance], *given_here = expert_part([other, block], (block.shape[0], *cuts), hint, *weights)
-        given[distance] = [send(cut, swap, f"swap_out_{distance}") for cut in given_here]
+    def run(items, tie, hint=2):
+        halves = [after(blocks[item], *tie) for item in items]
+        others = [send(x, swap, f"swap_in_{item[0]}") for x, item in zip(halves, items)]
+        outs = expert_part([*others, *halves], [x.shape[0] for x in halves] * 2, hint, *weights)
+        for number, (distance, name) in enumerate(items):
+            kept[distance, name] = outs[number]
+            given[distance, name] = send(outs[len(items) + number], swap, f"swap_out_{distance}")
+        return outs[:1]
 
     own, own_for_other = pack(core, tokens, routes, gate_num, devices)
     other = send(own, swap, "swap_in_0")
     kept[0], cut = expert_part([own, other], (rows, rows), 2, *weights)
     given[0] = send(cut, swap, "swap_out_0")
-    same, cross = send(own, on, "gather_1"), send(own_for_other, to_other, "gather_1")
-    block = join(after(same, kept[0]), cross)
-    run(1, block, (rows, rows), 2)
+    same, cross = send(own, on, "gather_long_1"), send(own_for_other, to_other, "gather_long_1")
+    long, short = join(after(same, kept[0]), cross)
+    blocks = {(1, "long"): long, (1, "short"): short}
+    last = run([(1, "long"), (1, "short")], [kept[0]])
     for distance in range(2, reach):
-        block = send(after(block, kept[distance - 2]), on, f"gather_{distance}")
-        run(distance, block, (rows, rows), 2)
-    block = send(after(block[:rows], kept[reach - 2]), on, f"gather_{reach}")
-
-    def terms(distance, number):
-        return [(kept[distance], number * rows), (given[distance][number], 0)]
-
-    total = step_sum((rows, terms(reach - 1, 1)))
-    short = send(total, on, f"return_short_{reach - 1}")
-    block = after(block, total)
-    run(reach, block, (rows,), 2)
-
-    def arrive(carried, number, name):
-        pieces, totals = [], []
+        tie = last if distance > 2 else []
+        long = send(after(long, *tie), on, f"gather_long_{distance}")
+        short = send(after(short, *tie), on, f"gather_short_{distance}")
+        blocks[distance, "long"], blocks[distance, "short"] = long, short
+    blocks[reach, "long"] = send(long, on, f"gather_long_{reach}")
+
+    def step(distance, name, carried):
+        terms = [(x, 0) for x in (kept[distance, name], given[distance, name], *carried)]
+        total = step_sum((rows, terms))
+        return [send(total, on, f"return_{name}_{distance}")], [total]
+
+    def arrive(name, carried):
+        sent, totals = [], []
         for start, perm in ((0, back_to_other), (half, on)):
-            (kept_1, at), (given_1, _) = terms(1, number)
-            total = step_sum((half, [(kept_1, at + start), (given_1, start), (carried, start)]))
-            pieces.append(send(total, perm, name))
-            totals.append(total)
-        return pieces, totals
-
-    pieces, height = [], rows // len(given[reach])
-    for number, piece in enumerate(given[reach]):
-        pieces.append((height, [(kept[reach], number * height), (after(piece, short), 0)]))
-    long = send(step_sum(*pieces), on, f"return_long_{reach}")
-    for distance in range(reach - 1, 1, -1):
+            terms = [(x, start) for x in (kept[1, name], given[1, name], *carried)]
+            totals.append(step_sum((half, terms)))
+            sent.append(send(totals[-1], perm, f"return_{name}_1"))
+        return sent, totals
+
+    run([(distance, "short") for distance in (reach - 1, reach - 2) if distance > 1], [])
+    short, totals = step(reach - 1, "short", ())
+    run([(reach, "long")], totals, 2)
+    given[reach, "long"] = after(given[reach, "long"], *short)
+    long, totals = step(reach, "long", ())
+    for distance in range(reach - 1, 0, -1):
+        if distance > 1:
+            run([(distance, "long")] + [(distance - 2, "short")] * (distance > 3), [], 2)
         if distance > 2:
-            total = step_sum((rows, terms(distance - 1, 1) + [(short, 0)]))
-            short_next = send(total, on, f"return_short_{distance - 1}")
-            totals = [total]
+            short, totals = step(distance - 1, "short", [after(x, *totals) for x in short])
+        elif distance == 2:
+            short, totals = arrive("short", [after(x, *totals) for x in short])
+        if distance > 1:
+            long, totals = step(distance, "long", [after(x, *totals) for x in long])
         else:
-            short_next, totals = arrive(short, 1, "return_short_1")
-        total = step_sum((rows, terms(distance, 0) + [(after(long, *totals), 0)]))
-        long = send(total, on, f"return_long_{distance}")
-        short = short_next
-
+            long, totals = arrive("long", long)
     short_cross, short_same = short
-    long_cross, long_same = arrive(long, 0, "return_long_1")[0]
+    long_cross, long_same = long
     return last_sum(core, kept[0], given[0], short_same, long_cross, long_same, short_cross)
 
 

time: 113 us -> 110 us (0.973)
  waiting for transfers between devices: 46.5 us -> 40.9 us
  starting transfers between devices: 27 us -> 28.5 us
  Pallas kernels: 36.2 us -> 37.6 us
    ppermute x27 -> x32, waiting for transfers between devices: 46.5 us -> 40.9 us  [send(): return lax.ppermute(x, 'expert', perm)]
    ppermute x27 -> x32, starting transfers between devices: 27 us -> 28.5 us  [send(): return lax.ppermute(x, 'expert', perm)]
    pallas_call x5 -> x6, Pallas kernels: 27.2 us -> 28.7 us  [expert_part(): pl.pallas_call(functools.partial(expert_kernel, len(blocks)), in_specs=[V...]
  transfers between devices with their start and end apart: 27 -> 32, of which waited for: 16 -> 13; matrix products, arithmetic and copies ran while one was open for 0% -> 0% of each run, Pallas kernels for 31% -> 33%
where the time goes in v9:
time: 110 us
  waiting for transfers between devices  40.9 us (37%)
  Pallas kernels  37.6 us (34%)
  starting transfers between devices  28.5 us (26%)
  local copies, waits for them, and re-layouts  2.61 us (2%)
    ppermute x32, waiting for transfers between devices, send(): return lax.ppermute(x, 'expert', perm)  40.9 us
    pallas_call x6, Pallas kernels, expert_part(): pl.pallas_call(functools.partial(expert_kernel, len(blocks)), in_specs=[V...  28.7 us
    ppermute x32, starting transfers between devices, send(): return lax.ppermute(x, 'expert', perm)  28.5 us
    pallas_call x1, Pallas kernels, keep(): pl.pallas_call(keep_kernel, in_specs=[ANYWHERE] * 2, out_specs=[VMEM] * 2...  6.38 us
    unnamed x8, local copies, waits for them, and re-layouts  2.61 us
  transfers between devices with their start and end apart: 32, of which 13 were waited for; matrix products, arithmetic and copies ran while one was open for 0% of the time, Pallas kernels for 33%

profile of v9, /device:TPU:0, one launch (start us, length us, event | category | flops | bytes accessed | tf_op | source)
XLA Modules:
  0.0 109.9 jit_solution(16219471768365159994)
XLA Ops:
  3.4 2.6 %collective-permute-start.2 = (bf16[64,4224]{1,0:T(8,128)(2,1)S(1)}, bf16[64,4224]{1,0:T(8,128)(2,1)S(1)}, u32[]{:S(2)}, u32[]{:S(2)}) collective-permute-start(bf16[64,4224]{1,0:T(8,128)(2,1)S(1)} %get-tuple-element.38.refs_0_), channel_id=1, source_target_pairs={{0,4},{1,3},{4,8},{5,1},{8,12},{9,5},{12,14},{13,9},{14,10},{15,13... | collective-permute-start | bytes 1622024 | tf_op jit(solution)/shard_map/gather_long_1/ppermute | solution.py:258
  6.0 1.3 %collective-permute-start.3 = (bf16[64,4224]{1,0:T(8,128)(2,1)S(1)}, bf16[64,4224]{1,0:T(8,128)(2,1)S(1)}, u32[]{:S(2)}, u32[]{:S(2)}) collective-permute-start(bf16[64,4224]{1,0:T(8,128)(2,1)S(1)} %get-tuple-element.44), channel_id=1, source_target_pairs={{0,3},{1,4},{4,1},{5,8},{8,5},{9,12},{12,9},{13,14},{14,13},{15,10... | collective-permute-start | bytes 1622024 | tf_op jit(solution)/shard_map/gather_long_1/ppermute | solution.py:258
  7.3 6.4 %keep.1 = (bf16[4096,1536]{1,0:T(8,128)(2,1)S(1)}, bf16[768,4096]{1,0:T(8,128)(2,1)S(1)}) custom-call(bf16[4096,1536]{1,0:T(8,128)(2,1)} %bitcast.3, bf16[768,4096]{1,0:T(8,128)(2,1)} %bitcast.4), custom_call_target="tpu_custom_call" | custom-call | bytes 18874368 | tf_op jit(solution)/shard_map/keep/pallas_call | solution.py:73
  13.7 4.0 %expert.6 = (bf16[64,4096]{1,0:T(8,128)(2,1)S(1)}, bf16[64,4096]{1,0:T(8,128)(2,1)S(1)}) custom-call(bf16[64,4224]{1,0:T(8,128)(2,1)S(1)} %get-tuple-element.38.refs_0_, bf16[64,4224]{1,0:T(8,128)(2,1)S(1)} %collective-permute-done.refs_1_, f32[1,128]{1,0:T(1,128)S(1)} %compare_select_fusion.1.refs_2_.refs_4_, f32[1,1536]{1,0:T(1,128)S(1)} %copy-done.2, ...), custom_call_target="tpu_custom_call" | custom-call | flops 4831838208 | tf_op jit(solution)/shard_map/expert/pallas_call | solution.py:131
  17.7 1.4 %collective-permute-done.3.cross = bf16[64,4224]{1,0:T(8,128)(2,1)S(1)} collective-permute-done((bf16[64,4224]{1,0:T(8,128)(2,1)S(1)}, bf16[64,4224]{1,0:T(8,128)(2,1)S(1)}, u32[]{:S(2)}, u32[]{:S(2)}) %collective-permute-start.3) | collective-permute-done | bytes 540704 | tf_op jit(solution)/shard_map/gather_long_1/ppermute | solution.py:258
  19.7 2.1 %collective-permute-start.7 = (bf16[64,4224]{1,0:T(8,128)(2,1)S(1)}, bf16[64,4224]{1,0:T(8,128)(2,1)S(1)}, u32[]{:S(2)}, u32[]{:S(2)}) collective-permute-start(bf16[64,4224]{1,0:T(8,128)(2,1)S(1)} %get-tuple-element.48.refs_3_), channel_id=1, source_target_pairs={{0,4},{1,3},{4,8},{5,1},{8,12},{9,5},{12,14},{13,9},{14,10},{15,13... | collective-permute-start | bytes 1622024 | tf_op jit(solution)/shard_map/gather_short_2/ppermute | solution.py:258
  21.8 1.6 %collective-permute-start.14 = (bf16[64,4224]{1,0:T(8,128)(2,1)S(1)}, bf16[64,4224]{1,0:T(8,128)(2,1)S(1)}, u32[]{:S(2)}, u32[]{:S(2)}) collective-permute-start(bf16[64,4224]{1,0:T(8,128)(2,1)S(1)} %get-tuple-element.46.refs_2_), channel_id=1, source_target_pairs={{0,4},{1,3},{4,8},{5,1},{8,12},{9,5},{12,14},{13,9},{14,10},{15,13... | collective-permute-start | bytes 1622024 | tf_op jit(solution)/shard_map/gather_long_2/ppermute | solution.py:258
  23.4 6.4 %expert.7 = (bf16[64,4096]{1,0:T(8,128)(2,1)S(1)}, bf16[64,4096]{1,0:T(8,128)(2,1)S(1)}, bf16[64,4096]{1,0:T(8,128)(2,1)S(1)}, bf16[64,4096]{1,0:T(8,128)(2,1)S(1)}) custom-call(bf16[64,4224]{1,0:T(8,128)(2,1)S(1)} %collective-permute-done.4.refs_0_, bf16[64,4224]{1,0:T(8,128)(2,1)S(1)} %collective-permute-done.5.refs_1_, ...), custom_call_target="tpu_custom_call" | custom-call | flops 9663676416 | tf_op jit(solution)/shard_map/expert/pallas_call | solution.py:131
  29.8 1.6 %collective-permute-start.8 = (bf16[64,4224]{1,0:T(8,128)(2,1)S(1)}, bf16[64,4224]{1,0:T(8,128)(2,1)S(1)}, u32[]{:S(2)}, u32[]{:S(2)}) collective-permute-start(bf16[64,4224]{1,0:T(8,128)(2,1)S(1)} %collective-permute-done.7.refs_3_), channel_id=1, source_target_pairs={{0,4},{1,3},{4,8},{5,1},{8,12},{9,5},{12,14},{13,9},{14,10},{15,13... | collective-permute-start | bytes 1622024 | tf_op jit(solution)/shard_map/gather_short_3/ppermute | solution.py:258
  31.4 3.4 %collective-permute-done.14.refs_1_ = bf16[64,4224]{1,0:T(8,128)(2,1)S(1)} collective-permute-done((bf16[64,4224]{1,0:T(8,128)(2,1)S(1)}, bf16[64,4224]{1,0:T(8,128)(2,1)S(1)}, u32[]{:S(2)}, u32[]{:S(2)}) %collective-permute-start.14) | collective-permute-done | bytes 540704 | tf_op jit(solution)/shard_map/gather_long_2/ppermute | solution.py:258
  34.9 2.1 %collective-permute-start.15 = (bf16[64,4224]{1,0:T(8,128)(2,1)S(1)}, bf16[64,4224]{1,0:T(8,128)(2,1)S(1)}, u32[]{:S(2)}, u32[]{:S(2)}) collective-permute-start(bf16[64,4224]{1,0:T(8,128)(2,1)S(1)} %collective-permute-done.14.refs_1_), channel_id=1, source_target_pairs={{0,4},{1,3},{4,8},{5,1},{8,12},{9,5},{12,14},{13,9},{14,10},{15,13... | collective-permute-start | bytes 1622024 | tf_op jit(solution)/shard_map/gather_long_3/ppermute | solution.py:258
  36.9 3.7 %collective-permute-done.8.refs_2_ = bf16[64,4224]{1,0:T(8,128)(2,1)S(1)} collective-permute-done((bf16[64,4224]{1,0:T(8,128)(2,1)S(1)}, bf16[64,4224]{1,0:T(8,128)(2,1)S(1)}, u32[]{:S(2)}, u32[]{:S(2)}) %collective-permute-start.8) | collective-permute-done | bytes 540704 | tf_op jit(solution)/shard_map/gather_short_3/ppermute | solution.py:258
  40.7 5.8 %collective-permute-done.15.refs_1_ = bf16[64,4224]{1,0:T(8,128)(2,1)S(1)} collective-permute-done((bf16[64,4224]{1,0:T(8,128)(2,1)S(1)}, bf16[64,4224]{1,0:T(8,128)(2,1)S(1)}, u32[]{:S(2)}, u32[]{:S(2)}) %collective-permute-start.15) | collective-permute-done | bytes 540704 | tf_op jit(solution)/shard_map/gather_long_3/ppermute | solution.py:258
  46.5 2.1 %collective-permute-start.16 = (bf16[64,4224]{1,0:T(8,128)(2,1)S(1)}, bf16[64,4224]{1,0:T(8,128)(2,1)S(1)}, u32[]{:S(2)}, u32[]{:S(2)}) collective-permute-start(bf16[64,4224]{1,0:T(8,128)(2,1)S(1)} %collective-permute-done.15.refs_1_), channel_id=1, source_target_pairs={{0,4},{1,3},{4,8},{5,1},{8,12},{9,5},{12,14},{13,9},{14,10},{15,13... | collective-permute-start | bytes 1622024 | tf_op jit(solution)/shard_map/gather_long_4/ppermute | solution.py:258
  48.5 6.4 %expert.8 = (bf16[64,4096]{1,0:T(8,128)(2,1)S(1)}, bf16[64,4096]{1,0:T(8,128)(2,1)S(1)}, bf16[64,4096]{1,0:T(8,128)(2,1)S(1)}, bf16[64,4096]{1,0:T(8,128)(2,1)S(1)}) custom-call(bf16[64,4224]{1,0:T(8,128)(2,1)S(1)} %collective-permute-done.9.refs_0_, bf16[64,4224]{1,0:T(8,128)(2,1)S(1)} %collective-permute-done.10.refs_1_, ...), custom_call_target="tpu_custom_call" | custom-call | flops 9663676416 | tf_op jit(solution)/shard_map/expert/pallas_call | solution.py:131
  55.0 1.9 %collective-permute-done.12.refs_1_ = bf16[64,4096]{1,0:T(8,128)(2,1)S(1)} collective-permute-done((bf16[64,4096]{1,0:T(8,128)(2,1)S(1)}, bf16[64,4096]{1,0:T(8,128)(2,1)S(1)}, u32[]{:S(2)}, u32[]{:S(2)}) %collective-permute-start.12) | collective-permute-done | bytes 524320 | tf_op jit(solution)/shard_map/swap_out_3/ppermute | solution.py:258
  57.7 1.6 %collective-permute-start.13 = (bf16[64,4096]{1,0:T(8,128)(2,1)S(1)}, bf16[64,4096]{1,0:T(8,128)(2,1)S(1)}, u32[]{:S(2)}, u32[]{:S(2)}) collective-permute-start(bf16[64,4096]{1,0:T(8,128)(2,1)S(1)} %step_sum.9), channel_id=1, source_target_pairs={{0,4},{1,3},{4,8},{5,1},{8,12},{9,5},{12,14},{13,9},{14,10},{15,13... | collective-permute-start | bytes 1572872 | tf_op jit(solution)/shard_map/return_short_3/ppermute | solution.py:258
  59.2 4.0 %expert.9 = (bf16[64,4096]{1,0:T(8,128)(2,1)S(1)}, bf16[64,4096]{1,0:T(8,128)(2,1)S(1)}) custom-call(bf16[64,4224]{1,0:T(8,128)(2,1)S(1)} %collective-permute-done.17.refs_0_, bf16[64,4224]{1,0:T(8,128)(2,1)S(1)} %collective-permute-done.16.refs_1_, f32[1,128]{1,0:T(1,128)S(1)} %compare_select_fusion.1.refs_2_.refs_4_, f32[1,1536]{1,0:T(1,128)S(1)} %copy-done.2, ...), custom_call_target="tpu_custom_call" | custom-call | flops 4831838208 | tf_op jit(solution)/shard_map/expert/pallas_call | solution.py:131
  63.9 3.0 %collective-permute-done.13.refs_2_ = bf16[64,4096]{1,0:T(8,128)(2,1)S(1)} collective-permute-done((bf16[64,4096]{1,0:T(8,128)(2,1)S(1)}, bf16[64,4096]{1,0:T(8,128)(2,1)S(1)}, u32[]{:S(2)}, u32[]{:S(2)}) %collective-permute-start.13) | collective-permute-done | bytes 524320 | tf_op jit(solution)/shard_map/return_short_3/ppermute | solution.py:258
  67.0 1.6 %collective-permute-start.22 = (bf16[64,4096]{1,0:T(8,128)(2,1)S(1)}, bf16[64,4096]{1,0:T(8,128)(2,1)S(1)}, u32[]{:S(2)}, u32[]{:S(2)}) collective-permute-start(bf16[64,4096]{1,0:T(8,128)(2,1)S(1)} %step_sum.10), channel_id=1, source_target_pairs={{0,4},{1,3},{4,8},{5,1},{8,12},{9,5},{12,14},{13,9},{14,10},{15,13... | collective-permute-start | bytes 1572872 | tf_op jit(solution)/shard_map/return_long_4/ppermute | solution.py:258
  68.6 4.0 %expert.10 = (bf16[64,4096]{1,0:T(8,128)(2,1)S(1)}, bf16[64,4096]{1,0:T(8,128)(2,1)S(1)}) custom-call(bf16[64,4224]{1,0:T(8,128)(2,1)S(1)} %collective-permute-done.20.refs_0_, bf16[64,4224]{1,0:T(8,128)(2,1)S(1)} %collective-permute-done.15.refs_1_, f32[1,128]{1,0:T(1,128)S(1)} %compare_select_fusion.1.refs_2_.refs_4_, f32[1,1536]{1,0:T(1,128)S(1)} %copy-done.2, ...), custom_call_target="tpu_custom_call" | custom-call | flops 4831838208 | tf_op jit(solution)/shard_map/expert/pallas_call | solution.py:131
  73.4 1.6 %collective-permute-start.19 = (bf16[64,4096]{1,0:T(8,128)(2,1)S(1)}, bf16[64,4096]{1,0:T(8,128)(2,1)S(1)}, u32[]{:S(2)}, u32[]{:S(2)}) collective-permute-start(bf16[64,4096]{1,0:T(8,128)(2,1)S(1)} %step_sum.11), channel_id=1, source_target_pairs={{0,4},{1,3},{4,8},{5,1},{8,12},{9,5},{12,14},{13,9},{14,10},{15,13... | collective-permute-start | bytes 1572872 | tf_op jit(solution)/shard_map/return_short_2/ppermute | solution.py:258
  76.4 1.6 %collective-permute-start.27 = (bf16[64,4096]{1,0:T(8,128)(2,1)S(1)}, bf16[64,4096]{1,0:T(8,128)(2,1)S(1)}, u32[]{:S(2)}, u32[]{:S(2)}) collective-permute-start(bf16[64,4096]{1,0:T(8,128)(2,1)S(1)} %step_sum.12), channel_id=1, source_target_pairs={{0,4},{1,3},{4,8},{5,1},{8,12},{9,5},{12,14},{13,9},{14,10},{15,13... | collective-permute-start | bytes 1572872 | tf_op jit(solution)/shard_map/return_long_3/ppermute | solution.py:258
  78.1 4.0 %expert.11 = (bf16[64,4096]{1,0:T(8,128)(2,1)S(1)}, bf16[64,4096]{1,0:T(8,128)(2,1)S(1)}) custom-call(bf16[64,4224]{1,0:T(8,128)(2,1)S(1)} %collective-permute-done.25.refs_0_, bf16[64,4224]{1,0:T(8,128)(2,1)S(1)} %collective-permute-done.14.refs_1_, f32[1,128]{1,0:T(1,128)S(1)} %compare_select_fusion.1.refs_2_.refs_4_, f32[1,1536]{1,0:T(1,128)S(1)} %copy-done.2, ...), custom_call_target="tpu_custom_call" | custom-call | flops 4831838208 | tf_op jit(solution)/shard_map/expert/pallas_call | solution.py:131
  82.8 5.4 %collective-permute-done.27.refs_2_ = bf16[64,4096]{1,0:T(8,128)(2,1)S(1)} collective-permute-done((bf16[64,4096]{1,0:T(8,128)(2,1)S(1)}, bf16[64,4096]{1,0:T(8,128)(2,1)S(1)}, u32[]{:S(2)}, u32[]{:S(2)}) %collective-permute-start.27) | collective-permute-done | bytes 524320 | tf_op jit(solution)/shard_map/return_long_3/ppermute | solution.py:258
  88.4 1.6 %collective-permute-start.28 = (bf16[64,4096]{1,0:T(8,128)(2,1)S(1)}, bf16[64,4096]{1,0:T(8,128)(2,1)S(1)}, u32[]{:S(2)}, u32[]{:S(2)}) collective-permute-start(bf16[64,4096]{1,0:T(8,128)(2,1)S(1)} %step_sum.15), channel_id=1, source_target_pairs={{0,4},{1,3},{4,8},{5,1},{8,12},{9,5},{12,14},{13,9},{14,10},{15,13... | collective-permute-start | bytes 1572872 | tf_op jit(solution)/shard_map/return_long_2/ppermute | solution.py:258
  90.0 1.4 %collective-permute-start.23 = (bf16[32,4096]{1,0:T(8,128)(2,1)S(1)}, bf16[32,4096]{1,0:T(8,128)(2,1)S(1)}, u32[]{:S(2)}, u32[]{:S(2)}) collective-permute-start(bf16[32,4096]{1,0:T(8,128)(2,1)S(1)} %step_sum.13), channel_id=1, source_target_pairs={{0,4},{1,3},{4,8},{5,1},{8,12},{9,5},{12,14},{13,9},{14,10},{15,13... | collective-permute-start | bytes 786440 | tf_op jit(solution)/shard_map/return_short_1/ppermute | solution.py:258
  91.9 5.8 %collective-permute-done.28.refs_2_ = bf16[64,4096]{1,0:T(8,128)(2,1)S(1)} collective-permute-done((bf16[64,4096]{1,0:T(8,128)(2,1)S(1)}, bf16[64,4096]{1,0:T(8,128)(2,1)S(1)}, u32[]{:S(2)}, u32[]{:S(2)}) %collective-permute-start.28) | collective-permute-done | bytes 524320 | tf_op jit(solution)/shard_map/return_long_2/ppermute | solution.py:258
  97.9 1.6 %collective-permute-start.30 = (bf16[32,4096]{1,0:T(8,128)(2,1)S(1)}, bf16[32,4096]{1,0:T(8,128)(2,1)S(1)}, u32[]{:S(2)}, u32[]{:S(2)}) collective-permute-start(bf16[32,4096]{1,0:T(8,128)(2,1)S(1)} %step_sum.17), channel_id=1, source_target_pairs={{0,4},{1,3},{4,8},{5,1},{8,12},{9,5},{12,14},{13,9},{14,10},{15,13... | collective-permute-start | bytes 786440 | tf_op jit(solution)/shard_map/return_long_1/ppermute | solution.py:258
  100.4 1.9 %collective-permute-done.31.refs_3_ = bf16[32,4096]{1,0:T(8,128)(2,1)S(1)} collective-permute-done((bf16[32,4096]{1,0:T(8,128)(2,1)S(1)}, bf16[32,4096]{1,0:T(8,128)(2,1)S(1)}, u32[]{:S(2)}, u32[]{:S(2)}) %collective-permute-start.31) | collective-permute-done | bytes 262176 | tf_op jit(solution)/shard_map/return_short_1/ppermute | solution.py:258
  102.3 2.8 %collective-permute-done.29.refs_1_ = bf16[32,4096]{1,0:T(8,128)(2,1)S(1)} collective-permute-done((bf16[32,4096]{1,0:T(8,128)(2,1)S(1)}, bf16[32,4096]{1,0:T(8,128)(2,1)S(1)}, u32[]{:S(2)}, u32[]{:S(2)}) %collective-permute-start.29) | collective-permute-done | bytes 262176 | tf_op jit(solution)/shard_map/return_long_1/ppermute | solution.py:258
  105.1 3.7 %collective-permute-done.30.refs_2_ = bf16[32,4096]{1,0:T(8,128)(2,1)S(1)} collective-permute-done((bf16[32,4096]{1,0:T(8,128)(2,1)S(1)}, bf16[32,4096]{1,0:T(8,128)(2,1)S(1)}, u32[]{:S(2)}, u32[]{:S(2)}) %collective-permute-start.30) | collective-permute-done | bytes 262176 | tf_op jit(solution)/shard_map/return_long_1/ppermute | solution.py:258
  (60 shorter events, 11.5 us)
Async XLA Ops:
  2.8 10.9 %collective-permute-start = (bf16[64,4224]{1,0:T(8,128)(2,1)S(1)}, bf16[64,4224]{1,0:T(8,128)(2,1)S(1)}, u32[]{:S(2)}, u32[]{:S(2)}) collective-permute-start(bf16[64,4224]{1,0:T(8,128)(2,1)S(1)} %get-tuple-element.38.refs_0_), channel_id=1, source_target_pairs={{0,1},{1,0},{2,3},{3,2},{4,5},{5,4},{6,7},{7,6},{8,9},{9,8},{10,11... | collective-permute-start | bytes 1622024 | tf_op jit(solution)/shard_map/swap_in_0/ppermute | solution.py:258
  3.4 14.3 %collective-permute-start.2 = (bf16[64,4224]{1,0:T(8,128)(2,1)S(1)}, bf16[64,4224]{1,0:T(8,128)(2,1)S(1)}, u32[]{:S(2)}, u32[]{:S(2)}) collective-permute-start(bf16[64,4224]{1,0:T(8,128)(2,1)S(1)} %get-tuple-element.38.refs_0_), channel_id=1, source_target_pairs={{0,4},{1,3},{4,8},{5,1},{8,12},{9,5},{12,14},{13,9},{14,10},{15,13... | collective-permute-start | bytes 1622024 | tf_op jit(solution)/shard_map/gather_long_1/ppermute | solution.py:258
  6.0 13.1 %collective-permute-start.3 = (bf16[64,4224]{1,0:T(8,128)(2,1)S(1)}, bf16[64,4224]{1,0:T(8,128)(2,1)S(1)}, u32[]{:S(2)}, u32[]{:S(2)}) collective-permute-start(bf16[64,4224]{1,0:T(8,128)(2,1)S(1)} %get-tuple-element.44), channel_id=1, source_target_pairs={{0,3},{1,4},{4,1},{5,8},{8,5},{9,12},{12,9},{13,14},{14,13},{15,10... | collective-permute-start | bytes 1622024 | tf_op jit(solution)/shard_map/gather_long_1/ppermute | solution.py:258
  19.1 4.2 %collective-permute-start.4 = (bf16[64,4224]{1,0:T(8,128)(2,1)S(1)}, bf16[64,4224]{1,0:T(8,128)(2,1)S(1)}, u32[]{:S(2)}, u32[]{:S(2)}) collective-permute-start(bf16[64,4224]{1,0:T(8,128)(2,1)S(1)} %get-tuple-element.46.refs_2_), channel_id=1, source_target_pairs={{0,1},{1,0},{2,3},{3,2},{4,5},{5,4},{6,7},{7,6},{8,9},{9,8},{10,11... | collective-permute-start | bytes 1622024 | tf_op jit(solution)/shard_map/swap_in_1/ppermute | solution.py:258
  19.2 4.2 %collective-permute-start.5 = (bf16[64,4224]{1,0:T(8,128)(2,1)S(1)}, bf16[64,4224]{1,0:T(8,128)(2,1)S(1)}, u32[]{:S(2)}, u32[]{:S(2)}) collective-permute-start(bf16[64,4224]{1,0:T(8,128)(2,1)S(1)} %get-tuple-element.48.refs_3_), channel_id=1, source_target_pairs={{0,1},{1,0},{2,3},{3,2},{4,5},{5,4},{6,7},{7,6},{8,9},{9,8},{10,11... | collective-permute-start | bytes 1622024 | tf_op jit(solution)/shard_map/swap_in_1/ppermute | solution.py:258
  19.7 10.1 %collective-permute-start.7 = (bf16[64,4224]{1,0:T(8,128)(2,1)S(1)}, bf16[64,4224]{1,0:T(8,128)(2,1)S(1)}, u32[]{:S(2)}, u32[]{:S(2)}) collective-permute-start(bf16[64,4224]{1,0:T(8,128)(2,1)S(1)} %get-tuple-element.48.refs_3_), channel_id=1, source_target_pairs={{0,4},{1,3},{4,8},{5,1},{8,12},{9,5},{12,14},{13,9},{14,10},{15,13... | collective-permute-start | bytes 1622024 | tf_op jit(solution)/shard_map/gather_short_2/ppermute | solution.py:258
  21.8 13.1 %collective-permute-start.14 = (bf16[64,4224]{1,0:T(8,128)(2,1)S(1)}, bf16[64,4224]{1,0:T(8,128)(2,1)S(1)}, u32[]{:S(2)}, u32[]{:S(2)}) collective-permute-start(bf16[64,4224]{1,0:T(8,128)(2,1)S(1)} %get-tuple-element.46.refs_2_), channel_id=1, source_target_pairs={{0,4},{1,3},{4,8},{5,1},{8,12},{9,5},{12,14},{13,9},{14,10},{15,13... | collective-permute-start | bytes 1622024 | tf_op jit(solution)/shard_map/gather_long_2/ppermute | solution.py:258
  29.8 10.8 %collective-permute-start.8 = (bf16[64,4224]{1,0:T(8,128)(2,1)S(1)}, bf16[64,4224]{1,0:T(8,128)(2,1)S(1)}, u32[]{:S(2)}, u32[]{:S(2)}) collective-permute-start(bf16[64,4224]{1,0:T(8,128)(2,1)S(1)} %collective-permute-done.7.refs_3_), channel_id=1, source_target_pairs={{0,4},{1,3},{4,8},{5,1},{8,12},{9,5},{12,14},{13,9},{14,10},{15,13... | collective-permute-start | bytes 1622024 | tf_op jit(solution)/shard_map/gather_short_3/ppermute | solution.py:258
  34.9 11.6 %collective-permute-start.15 = (bf16[64,4224]{1,0:T(8,128)(2,1)S(1)}, bf16[64,4224]{1,0:T(8,128)(2,1)S(1)}, u32[]{:S(2)}, u32[]{:S(2)}) collective-permute-start(bf16[64,4224]{1,0:T(8,128)(2,1)S(1)} %collective-permute-done.14.refs_1_), channel_id=1, source_target_pairs={{0,4},{1,3},{4,8},{5,1},{8,12},{9,5},{12,14},{13,9},{14,10},{15,13... | collective-permute-start | bytes 1622024 | tf_op jit(solution)/shard_map/gather_long_3/ppermute | solution.py:258
  36.9 11.6 %collective-permute-start.10 = (bf16[64,4224]{1,0:T(8,128)(2,1)S(1)}, bf16[64,4224]{1,0:T(8,128)(2,1)S(1)}, u32[]{:S(2)}, u32[]{:S(2)}) collective-permute-start(bf16[64,4224]{1,0:T(8,128)(2,1)S(1)} %collective-permute-done.7.refs_3_), channel_id=1, source_target_pairs={{0,1},{1,0},{2,3},{3,2},{4,5},{5,4},{6,7},{7,6},{8,9},{9,8},{10,11... | collective-permute-start | bytes 1622024 | tf_op jit(solution)/shard_map/swap_in_2/ppermute | solution.py:258
  40.7 7.9 %collective-permute-start.9 = (bf16[64,4224]{1,0:T(8,128)(2,1)S(1)}, bf16[64,4224]{1,0:T(8,128)(2,1)S(1)}, u32[]{:S(2)}, u32[]{:S(2)}) collective-permute-start(bf16[64,4224]{1,0:T(8,128)(2,1)S(1)} %collective-permute-done.8.refs_2_), channel_id=1, source_target_pairs={{0,1},{1,0},{2,3},{3,2},{4,5},{5,4},{6,7},{7,6},{8,9},{9,8},{10,11... | collective-permute-start | bytes 1622024 | tf_op jit(solution)/shard_map/swap_in_3/ppermute | solution.py:258
  46.5 10.6 %collective-permute-start.16 = (bf16[64,4224]{1,0:T(8,128)(2,1)S(1)}, bf16[64,4224]{1,0:T(8,128)(2,1)S(1)}, u32[]{:S(2)}, u32[]{:S(2)}) collective-permute-start(bf16[64,4224]{1,0:T(8,128)(2,1)S(1)} %collective-permute-done.15.refs_1_), channel_id=1, source_target_pairs={{0,4},{1,3},{4,8},{5,1},{8,12},{9,5},{12,14},{13,9},{14,10},{15,13... | collective-permute-start | bytes 1622024 | tf_op jit(solution)/shard_map/gather_long_4/ppermute | solution.py:258
  55.0 2.0 %collective-permute-start.12 = (bf16[64,4096]{1,0:T(8,128)(2,1)S(1)}, bf16[64,4096]{1,0:T(8,128)(2,1)S(1)}, u32[]{:S(2)}, u32[]{:S(2)}) collective-permute-start(bf16[64,4096]{1,0:T(8,128)(2,1)S(1)} %get-tuple-element.56), channel_id=1, source_target_pairs={{0,1},{1,0},{2,3},{3,2},{4,5},{5,4},{6,7},{7,6},{8,9},{9,8},{10,11... | collective-permute-start | bytes 1572872 | tf_op jit(solution)/shard_map/swap_out_3/ppermute | solution.py:258
  57.1 2.2 %collective-permute-start.17 = (bf16[64,4224]{1,0:T(8,128)(2,1)S(1)}, bf16[64,4224]{1,0:T(8,128)(2,1)S(1)}, u32[]{:S(2)}, u32[]{:S(2)}) collective-permute-start(bf16[64,4224]{1,0:T(8,128)(2,1)S(1)} %collective-permute-done.16.refs_1_), channel_id=1, source_target_pairs={{0,1},{1,0},{2,3},{3,2},{4,5},{5,4},{6,7},{7,6},{8,9},{9,8},{10,11... | collective-permute-start | bytes 1622024 | tf_op jit(solution)/shard_map/swap_in_4/ppermute | solution.py:258
  57.3 11.3 %collective-permute-start.20 = (bf16[64,4224]{1,0:T(8,128)(2,1)S(1)}, bf16[64,4224]{1,0:T(8,128)(2,1)S(1)}, u32[]{:S(2)}, u32[]{:S(2)}) collective-permute-start(bf16[64,4224]{1,0:T(8,128)(2,1)S(1)} %collective-permute-done.15.refs_1_), channel_id=1, source_target_pairs={{0,1},{1,0},{2,3},{3,2},{4,5},{5,4},{6,7},{7,6},{8,9},{9,8},{10,11... | collective-permute-start | bytes 1622024 | tf_op jit(solution)/shard_map/swap_in_3/ppermute | solution.py:258
  57.7 9.2 %collective-permute-start.13 = (bf16[64,4096]{1,0:T(8,128)(2,1)S(1)}, bf16[64,4096]{1,0:T(8,128)(2,1)S(1)}, u32[]{:S(2)}, u32[]{:S(2)}) collective-permute-start(bf16[64,4096]{1,0:T(8,128)(2,1)S(1)} %step_sum.9), channel_id=1, source_target_pairs={{0,4},{1,3},{4,8},{5,1},{8,12},{9,5},{12,14},{13,9},{14,10},{15,13... | collective-permute-start | bytes 1572872 | tf_op jit(solution)/shard_map/return_short_3/ppermute | solution.py:258
  63.2 3.6 %collective-permute-start.18 = (bf16[64,4096]{1,0:T(8,128)(2,1)S(1)}, bf16[64,4096]{1,0:T(8,128)(2,1)S(1)}, u32[]{:S(2)}, u32[]{:S(2)}) collective-permute-start(bf16[64,4096]{1,0:T(8,128)(2,1)S(1)} %get-tuple-element.60), channel_id=1, source_target_pairs={{0,1},{1,0},{2,3},{3,2},{4,5},{5,4},{6,7},{7,6},{8,9},{9,8},{10,11... | collective-permute-start | bytes 1572872 | tf_op jit(solution)/shard_map/swap_out_4/ppermute | solution.py:258
  63.3 14.8 %collective-permute-start.25 = (bf16[64,4224]{1,0:T(8,128)(2,1)S(1)}, bf16[64,4224]{1,0:T(8,128)(2,1)S(1)}, u32[]{:S(2)}, u32[]{:S(2)}) collective-permute-start(bf16[64,4224]{1,0:T(8,128)(2,1)S(1)} %collective-permute-done.14.refs_1_), channel_id=1, source_target_pairs={{0,1},{1,0},{2,3},{3,2},{4,5},{5,4},{6,7},{7,6},{8,9},{9,8},{10,11... | collective-permute-start | bytes 1622024 | tf_op jit(solution)/shard_map/swap_in_2/ppermute | solution.py:258
  63.8 9.4 %collective-permute-start.11 = (bf16[64,4096]{1,0:T(8,128)(2,1)S(1)}, bf16[64,4096]{1,0:T(8,128)(2,1)S(1)}, u32[]{:S(2)}, u32[]{:S(2)}) collective-permute-start(bf16[64,4096]{1,0:T(8,128)(2,1)S(1)} %get-tuple-element.54), channel_id=1, source_target_pairs={{0,1},{1,0},{2,3},{3,2},{4,5},{5,4},{6,7},{7,6},{8,9},{9,8},{10,11... | collective-permute-start | bytes 1572872 | tf_op jit(solution)/shard_map/swap_out_2/ppermute | solution.py:258
  67.0 9.2 %collective-permute-start.22 = (bf16[64,4096]{1,0:T(8,128)(2,1)S(1)}, bf16[64,4096]{1,0:T(8,128)(2,1)S(1)}, u32[]{:S(2)}, u32[]{:S(2)}) collective-permute-start(bf16[64,4096]{1,0:T(8,128)(2,1)S(1)} %step_sum.10), channel_id=1, source_target_pairs={{0,4},{1,3},{4,8},{5,1},{8,12},{9,5},{12,14},{13,9},{14,10},{15,13... | collective-permute-start | bytes 1572872 | tf_op jit(solution)/shard_map/return_long_4/ppermute | solution.py:258
  72.6 3.6 %collective-permute-start.21 = (bf16[64,4096]{1,0:T(8,128)(2,1)S(1)}, bf16[64,4096]{1,0:T(8,128)(2,1)S(1)}, u32[]{:S(2)}, u32[]{:S(2)}) collective-permute-start(bf16[64,4096]{1,0:T(8,128)(2,1)S(1)} %get-tuple-element.64), channel_id=1, source_target_pairs={{0,1},{1,0},{2,3},{3,2},{4,5},{5,4},{6,7},{7,6},{8,9},{9,8},{10,11... | collective-permute-start | bytes 1572872 | tf_op jit(solution)/shard_map/swap_out_3/ppermute | solution.py:258
  72.7 10.0 %collective-permute-start.6 = (bf16[64,4096]{1,0:T(8,128)(2,1)S(1)}, bf16[64,4096]{1,0:T(8,128)(2,1)S(1)}, u32[]{:S(2)}, u32[]{:S(2)}) collective-permute-start(bf16[64,4096]{1,0:T(8,128)(2,1)S(1)} %get-tuple-element.50), channel_id=1, source_target_pairs={{0,1},{1,0},{2,3},{3,2},{4,5},{5,4},{6,7},{7,6},{8,9},{9,8},{10,11... | collective-permute-start | bytes 1572872 | tf_op jit(solution)/shard_map/swap_out_1/ppermute | solution.py:258
  73.4 9.3 %collective-permute-start.19 = (bf16[64,4096]{1,0:T(8,128)(2,1)S(1)}, bf16[64,4096]{1,0:T(8,128)(2,1)S(1)}, u32[]{:S(2)}, u32[]{:S(2)}) collective-permute-start(bf16[64,4096]{1,0:T(8,128)(2,1)S(1)} %step_sum.11), channel_id=1, source_target_pairs={{0,4},{1,3},{4,8},{5,1},{8,12},{9,5},{12,14},{13,9},{14,10},{15,13... | collective-permute-start | bytes 1572872 | tf_op jit(solution)/shard_map/return_short_2/ppermute | solution.py:258
  76.4 11.8 %collective-permute-start.27 = (bf16[64,4096]{1,0:T(8,128)(2,1)S(1)}, bf16[64,4096]{1,0:T(8,128)(2,1)S(1)}, u32[]{:S(2)}, u32[]{:S(2)}) collective-permute-start(bf16[64,4096]{1,0:T(8,128)(2,1)S(1)} %step_sum.12), channel_id=1, source_target_pairs={{0,4},{1,3},{4,8},{5,1},{8,12},{9,5},{12,14},{13,9},{14,10},{15,13... | collective-permute-start | bytes 1572872 | tf_op jit(solution)/shard_map/return_long_3/ppermute | solution.py:258
  82.0 6.2 %collective-permute-start.26 = (bf16[64,4096]{1,0:T(8,128)(2,1)S(1)}, bf16[64,4096]{1,0:T(8,128)(2,1)S(1)}, u32[]{:S(2)}, u32[]{:S(2)}) collective-permute-start(bf16[64,4096]{1,0:T(8,128)(2,1)S(1)} %get-tuple-element.69), channel_id=1, source_target_pairs={{0,1},{1,0},{2,3},{3,2},{4,5},{5,4},{6,7},{7,6},{8,9},{9,8},{10,11... | collective-permute-start | bytes 1572872 | tf_op jit(solution)/shard_map/swap_out_2/ppermute | solution.py:258
  82.1 9.8 %collective-permute-start.24 = (bf16[64,4096]{1,0:T(8,128)(2,1)S(1)}, bf16[64,4096]{1,0:T(8,128)(2,1)S(1)}, u32[]{:S(2)}, u32[]{:S(2)}) collective-permute-start(bf16[64,4096]{1,0:T(8,128)(2,1)S(1)} %get-tuple-element.67), channel_id=1, source_target_pairs={{0,1},{1,0},{2,3},{3,2},{4,5},{5,4},{6,7},{7,6},{8,9},{9,8},{10,11... | collective-permute-start | bytes 1572872 | tf_op jit(solution)/shard_map/swap_out_1/ppermute | solution.py:258
  88.4 9.2 %collective-permute-start.28 = (bf16[64,4096]{1,0:T(8,128)(2,1)S(1)}, bf16[64,4096]{1,0:T(8,128)(2,1)S(1)}, u32[]{:S(2)}, u32[]{:S(2)}) collective-permute-start(bf16[64,4096]{1,0:T(8,128)(2,1)S(1)} %step_sum.15), channel_id=1, source_target_pairs={{0,4},{1,3},{4,8},{5,1},{8,12},{9,5},{12,14},{13,9},{14,10},{15,13... | collective-permute-start | bytes 1572872 | tf_op jit(solution)/shard_map/return_long_2/ppermute | solution.py:258
  90.0 9.5 %collective-permute-start.1 = (bf16[64,4096]{1,0:T(8,128)(2,1)S(1)}, bf16[64,4096]{1,0:T(8,128)(2,1)S(1)}, u32[]{:S(2)}, u32[]{:S(2)}) collective-permute-start(bf16[64,4096]{1,0:T(8,128)(2,1)S(1)} %get-tuple-element.42), channel_id=1, source_target_pairs={{0,1},{1,0},{2,3},{3,2},{4,5},{5,4},{6,7},{7,6},{8,9},{9,8},{10,11... | collective-permute-start | bytes 1572872 | tf_op jit(solution)/shard_map/swap_out_0/ppermute | solution.py:258
  90.0 10.4 %collective-permute-start.23 = (bf16[32,4096]{1,0:T(8,128)(2,1)S(1)}, bf16[32,4096]{1,0:T(8,128)(2,1)S(1)}, u32[]{:S(2)}, u32[]{:S(2)}) collective-permute-start(bf16[32,4096]{1,0:T(8,128)(2,1)S(1)} %step_sum.13), channel_id=1, source_target_pairs={{0,4},{1,3},{4,8},{5,1},{8,12},{9,5},{12,14},{13,9},{14,10},{15,13... | collective-permute-start | bytes 786440 | tf_op jit(solution)/shard_map/return_short_1/ppermute | solution.py:258
  91.4 10.9 %collective-permute-start.31 = (bf16[32,4096]{1,0:T(8,128)(2,1)S(1)}, bf16[32,4096]{1,0:T(8,128)(2,1)S(1)}, u32[]{:S(2)}, u32[]{:S(2)}) collective-permute-start(bf16[32,4096]{1,0:T(8,128)(2,1)S(1)} %step_sum.14), channel_id=1, source_target_pairs={{0,5},{1,2},{4,9},{5,0},{8,13},{9,4},{12,15},{13,8},{14,11},{15,12... | collective-permute-start | bytes 786440 | tf_op jit(solution)/shard_map/return_short_1/ppermute | solution.py:258
  97.7 7.4 %collective-permute-start.29 = (bf16[32,4096]{1,0:T(8,128)(2,1)S(1)}, bf16[32,4096]{1,0:T(8,128)(2,1)S(1)}, u32[]{:S(2)}, u32[]{:S(2)}) collective-permute-start(bf16[32,4096]{1,0:T(8,128)(2,1)S(1)} %step_sum.16), channel_id=1, source_target_pairs={{0,5},{1,2},{4,9},{5,0},{8,13},{9,4},{12,15},{13,8},{14,11},{15,12... | collective-permute-start | bytes 786440 | tf_op jit(solution)/shard_map/return_long_1/ppermute | solution.py:258
  97.9 10.9 %collective-permute-start.30 = (bf16[32,4096]{1,0:T(8,128)(2,1)S(1)}, bf16[32,4096]{1,0:T(8,128)(2,1)S(1)}, u32[]{:S(2)}, u32[]{:S(2)}) collective-permute-start(bf16[32,4096]{1,0:T(8,128)(2,1)S(1)} %step_sum.17), channel_id=1, source_target_pairs={{0,4},{1,3},{4,8},{5,1},{8,12},{9,5},{12,14},{13,9},{14,10},{15,13... | collective-permute-start | bytes 786440 | tf_op jit(solution)/shard_map/return_long_1/ppermute | solution.py:258
  (3 other events, 28.4 us)

commit v10 on v6

v10 whole, which is shorter than its diff:
```python
import functools

import jax
import jax.numpy as jnp
from jax import lax
from jax.experimental import pallas as pl
from jax.experimental.pallas import tpu as pltpu
from jax.sharding import PartitionSpec as P

DENOMINATOR = 32768.0
LANES = 128
UNIT_CHUNK = 256
WIDTH_CHUNK = 1024
ANYWHERE = pl.BlockSpec(memory_space=pl.ANY)
VMEM = pl.BlockSpec(memory_space=pltpu.VMEM)
SMEM = pl.BlockSpec(memory_space=pltpu.SMEM)


def ring_of(chips):
    if chips == 8:
        return [0, 2, 4, 6, 7, 5, 3, 1]
    return list(range(chips))


def limits(mebibytes):
    return pltpu.CompilerParams(vmem_limit_bytes=mebibytes << 20)


def pack_kernel(experts, tokens, routes, gate_num, packed):
    rows, width = tokens.shape
    lane = lax.broadcasted_iota(jnp.int32, (rows, LANES), 1)
    expert = jnp.where(lane < experts, lane, lane - experts)
    dense = jnp.zeros((rows, LANES), jnp.int32)
    for pick in range(routes.shape[1]):
        column = slice(pick, pick + 1)
        dense += jnp.where(routes[:, column] == expert, gate_num[:, column], 0)
    digit = jnp.where(lane < experts, dense >> 8, dense & 255)
    digit = jnp.where(lane < 2 * experts, digit, 0)
    packed[:, :width] = tokens[...]
    packed[:, width:] = digit.astype(jnp.float32).astype(jnp.bfloat16)


def pack(tokens, routes, gate_num, experts):
    rows, width = tokens.shape
    return pl.pallas_call(
        functools.partial(pack_kernel, experts),
        in_specs=[VMEM] * 3,
        out_specs=VMEM,
        out_shape=jax.ShapeDtypeStruct((rows, width + LANES), jnp.bfloat16),
        compiler_params=limits(4),
        name="pack",
    )(tokens, routes, gate_num)


def keep_kernel(gate_up, down, gate_up_here, down_here, sem):
    copies = [
        pltpu.make_async_copy(gate_up, gate_up_here, sem.at[0]),
        pltpu.make_async_copy(down, down_here, sem.at[1]),
    ]
    for copy in copies:
        copy.start()
    for copy in copies:
        copy.wait()


def keep(gate_up_w, down_w):
    return pl.pallas_call(
        keep_kernel,
        in_specs=[ANYWHERE] * 2,
        out_specs=[VMEM] * 2,
        out_shape=[pltpu.VMEM(w.shape, w.dtype) for w in (gate_up_w, down_w)],
        scratch_shapes=[pltpu.SemaphoreType.DMA((2,))],
        compiler_params=limits(1),
        cost_estimate=pl.CostEstimate(
            flops=0, bytes_accessed=2 * (gate_up_w.size + down_w.size), transcendentals=0
        ),
        name="keep",
    )(*(pltpu.with_memory_space_constraint(w, pltpu.HBM) for w in (gate_up_w, down_w)))


def expert_kernel(count, *refs):
    xs = refs[:count]
    pick, gate_up_s, down_s, gate_up, down = refs[count : count + 5]
    outs = refs[count + 5 : -2]
    x, hidden = refs[-2:]
    units, width = down.shape

    at = 0
    for ref in xs:
        x[at : at + ref.shape[0]] = ref[...]
        at += ref.shape[0]
    digits = x[:, width:].astype(jnp.float32)
    weight = jnp.sum(digits * pick[...], axis=1, keepdims=True) / DENOMINATOR

    def unit_step(chunk, carry):
        sides = []
        for side in range(2):
            columns = pl.ds(pl.multiple_of(side * units + chunk * UNIT_CHUNK, UNIT_CHUNK), UNIT_CHUNK)
            part = jnp.dot(x[:, :width], gate_up[:, columns], preferred_element_type=jnp.float32)
            sides.append(part * gate_up_s[:, columns])
        here = pl.ds(pl.multiple_of(chunk * UNIT_CHUNK, UNIT_CHUNK), UNIT_CHUNK)
        hidden[:, here] = (jax.nn.silu(sides[0]) * sides[1]).astype(jnp.bfloat16)
        return carry

    lax.fori_loop(0, units // UNIT_CHUNK, unit_step, 0)

    def width_step(chunk, carry):
        columns = pl.ds(pl.multiple_of(chunk * WIDTH_CHUNK, WIDTH_CHUNK), WIDTH_CHUNK)
        part = jnp.dot(hidden[...], down[:, columns], preferred_element_type=jnp.float32)
        part = (part * down_s[:, columns] * weight).astype(jnp.bfloat16)
        at = 0
        for ref in outs:
            ref[:, columns] = part[at : at + ref.shape[0]]
            at += ref.shape[0]
        return carry

    lax.fori_loop(0, width // WIDTH_CHUNK, width_step, 0)


def expert_part(blocks, out_rows, hint, pick, gate_up_w, gate_up_s, down_w, down_s):
    width, units2 = gate_up_w.shape
    units = down_w.shape[0]
    rows, packed_width = sum(block.shape[0] for block in blocks), blocks[0].shape[1]
    flops = int(hint * 2 * rows * width * (units2 + units))
    return pl.pallas_call(
        functools.partial(expert_kernel, len(blocks)),
        in_specs=[VMEM] * (len(blocks) + 5),
        out_specs=[VMEM] * len(out_rows),
        out_shape=[jax.ShapeDtypeStruct((size, width), jnp.bfloat16) for size in out_rows],
        scratch_shapes=[
            pltpu.VMEM((rows, packed_width), jnp.bfloat16),
            pltpu.VMEM((rows, units), jnp.bfloat16),
        ],
        compiler_params=limits(14),
        cost_estimate=pl.CostEstimate(flops=flops, bytes_accessed=0, transcendentals=0),
        name="expert",
    )(
        *blocks,
        pick,
        gate_up_s,
        down_s,
        pltpu.with_memory_space_constraint(gate_up_w, pltpu.VMEM),
        pltpu.with_memory_space_constraint(down_w, pltpu.VMEM),
    )


def sums_kernel(plan, *refs):
    outs = refs[-1 - max(out for _, out, _, _ in plan) :]
    for terms, out, first, rows in plan:
        for column in range(0, outs[out].shape[1], WIDTH_CHUNK):
            columns = slice(column, column + WIDTH_CHUNK)
            total = 0.0
            for number, start in terms:
                total += refs[number][start : start + rows, columns].astype(jnp.float32)
            outs[out][first : first + rows, columns] = total.astype(jnp.bfloat16)


def sums(wanted, shapes, name):
    arrays, plan = [], []
    for terms, *place in wanted:
        numbers = []
        for array, start in terms:
            number = next((i for i, known in enumerate(arrays) if known is array), len(arrays))
            if number == len(arrays):
                arrays.append(array)
            numbers.append((number, start))
        plan.append((tuple(numbers), *place))
    return pl.pallas_call(
        functools.partial(sums_kernel, tuple(plan)),
        in_specs=[VMEM] * len(arrays),
        out_specs=[VMEM] * len(shapes),
        out_shape=[jax.ShapeDtypeStruct(shape, jnp.bfloat16) for shape in shapes],
        compiler_params=limits(4),
        name=name,
    )(*arrays)


def together(*values):
    return lax.optimization_barrier(values)


def after(value, *others):
    return together(value, *others)[0] if others else value


def body(tokens, routes, gate_num, gate_up_q, gate_up_scale, down_q, down_scale):
    devices = lax.axis_size("expert")
    expert = lax.axis_index("expert")
    chips = devices // 2
    reach = chips // 2
    rows, width = tokens.shape
    half = rows // 2
    ring = ring_of(chips)

    def hop(way):
        pairs = []
        for place in range(chips):
            for core in range(2):
                pairs.append((2 * ring[place] + core, 2 * ring[(place + way) % chips] + core))
        return pairs

    ways = (hop(1), hop(-1))
    swap = [(i, i ^ 1) for i in range(devices)]

    def send(x, perm, name):
        with jax.named_scope(name):
            return lax.ppermute(x, "expert", perm)

    def send_both(pair, name):
        return [send(x, way, name) for x, way in zip(pair, ways)]

    lane = jnp.arange(LANES, dtype=jnp.int32)
    pick = jnp.where(lane == expert, 256.0, jnp.where(lane == devices + expert, 1.0, 0.0))
    pick = pick.astype(jnp.float32)[None, :]
    gate_up_w, down_w = keep(gate_up_q[0], down_q[0])
    weights = (pick, gate_up_w, gate_up_scale, down_w, down_scale)

    kept, given = {}, {}

    def run(arrays, items, tie, hint=2):
        arrays = together(*arrays, *tie)[: len(arrays)]
        name = items[0][0]
        others = together(*[send(x, swap, f"swap_in_{name}") for x in arrays])
        outs = expert_part([*arrays, *others], [half] * (2 * len(items)), hint, *weights)
        for number, item in enumerate(items):
            kept[item] = outs[number]
            given[item] = send(outs[len(items) + number], swap, f"swap_out_{name}")
        return outs[:1]

    def run_late(keys, tie, hint=2):
        return run([x for key in keys for x in blocks[key]], [(*key, way) for key in keys for way in range(2)], tie, hint)

    own = pack(tokens, routes, gate_num, devices)
    start = run([own], [(0, "own", 0), (0, "own", 1)], [])
    below, above = send_both((own, own), "gather_long_1")
    below, above = together(below, above, *start)[:2]
    items = [(1, "long", 0), (1, "short", 0), (1, "short", 1), (1, "long", 1)]
    last = run([below, above], items, start)
    long, short = (below[:half], above[half:]), (below[half:], above[:half])
    blocks = {}
    for distance in range(2, reach):
        tie = last if distance > 2 else []
        long = send_both(together(*long, *tie)[:2], f"gather_long_{distance}")
        short = send_both(together(*short, *tie)[:2], f"gather_short_{distance}")
        blocks[distance, "long"], blocks[distance, "short"] = long, short
    blocks[reach, "long"] = send_both(together(*long), f"gather_long_{reach}")

    def step(distance, name, carried):
        wanted = []
        for way in range(2):
            item = (distance, name, 1 - way)
            terms = [(x, 0) for x in (kept[item], given[item], *carried[way : way + 1])]
            wanted.append((terms, way, 0, half))
        totals = sums(wanted, [(half, width)] * 2, "step_sums")
        return send_both(totals, f"return_{name}_{distance}"), totals

    run_late([(distance, "short") for distance in (reach - 1, reach - 2) if distance > 1], [])
    short, totals = step(reach - 1, "short", ())
    run_late([(reach, "long")], totals)
    for way in range(2):
        item = (reach, "long", way)
        given[item] = after(given[item], *short)
    long, totals = step(reach, "long", ())
    for distance in range(reach - 1, 0, -1):
        if distance > 1:
            late = [(d, "long") for d in (distance, distance - 1) if d > 1 and (d, "long", 0) not in kept]
            late += [(d, "short") for d in (distance - 2,) if d > 1]
            if late:
                run_late(late, totals)
            short, totals = step(distance - 1, "short", together(*short, *totals)[:2])
        tie = short if distance == 1 else totals
        long, totals = step(distance, "long", together(*long, *tie)[:2])
    wanted = []
    for which, arrived in enumerate(((short[0], long[1]), (long[0], short[1]))):
        item = (0, "own", which)
        wanted.append(([(x, 0) for x in (kept[item], given[item], *arrived)], 0, which * half, half))
    return sums(wanted, [(rows, width)], "last_sums")[0]


def solution(mesh):
    in_specs = (
        P(("groups", "expert"), None),
        P(("groups", "expert"), None),
        P(("groups", "expert"), None),
        P("expert", None, None),
        P("expert", None),
        P("expert", None, None),
        P("expert", None),
    )
    out_specs = P(("groups", "expert"), None)
    return jax.shard_map(body, mesh=mesh, in_specs=in_specs, out_specs=out_specs, check_vma=False)
```

time: 113 us -> 116 us (1.027)
  starting transfers between devices: 27.8 us -> 32.4 us
  waiting for transfers between devices: 45.6 us -> 44 us
    ppermute x35 -> x55, starting transfers between devices: 27.8 us -> 32.4 us  [send(): return lax.ppermute(x, 'expert', perm)]
    ppermute x35 -> x55, waiting for transfers between devices: 45.6 us -> 44 us  [send(): return lax.ppermute(x, 'expert', perm)]
    unnamed x10 -> x8, local copies, waits for them, and re-layouts: 2.65 us -> 2.61 us
    pallas_call x11 -> x9, Pallas kernels: 2.5 us -> 2.52 us  [the longest x8 2.31 us: sums(): pl.pallas_call(functools.partial(sums_kernel, tuple(plan)), in_specs=[VME...]
  transfers between devices with their start and end apart: 35 -> 55, of which waited for: 16 -> 24; matrix products, arithmetic and copies ran while one was open for 0% -> 0% of each run, Pallas kernels for 27% -> 30%
where the time goes in v10:
time: 116 us; the launch traced here: 115 us
  waiting for transfers between devices  44 us (38%)
  Pallas kernels  36.1 us (31%)
  starting transfers between devices  32.4 us (28%)
  local copies, waits for them, and re-layouts  2.68 us (2%)
    ppermute x55, waiting for transfers between devices, send(): return lax.ppermute(x, 'expert', perm)  44 us
    ppermute x55, starting transfers between devices, send(): return lax.ppermute(x, 'expert', perm)  32.4 us
    pallas_call x5, Pallas kernels, expert_part(): pl.pallas_call(functools.partial(expert_kernel, len(blocks)), in_specs=[V...  27.2 us
    pallas_call x1, Pallas kernels, keep(): pl.pallas_call(keep_kernel, in_specs=[ANYWHERE] * 2, out_specs=[VMEM] * 2...  6.38 us
    unnamed x8, local copies, waits for them, and re-layouts  2.61 us
  transfers between devices with their start and end apart: 55, of which 24 were waited for; matrix products, arithmetic and copies ran while one was open for 0% of the time, Pallas kernels for 30%

profile of v10, /device:TPU:0, one launch (start us, length us, event | category | flops | bytes accessed | tf_op | source)
XLA Modules:
  0.0 115.4 jit_solution(2444962992465749085)
XLA Ops:
  3.3 2.6 %collective-permute-start.3 = (bf16[64,4224]{1,0:T(8,128)(2,1)S(1)}, bf16[64,4224]{1,0:T(8,128)(2,1)S(1)}, u32[]{:S(2)}, u32[]{:S(2)}) collective-permute-start(bf16[64,4224]{1,0:T(8,128)(2,1)S(1)} %pack.1.refs_0_), channel_id=1, source_target_pairs={{0,2},{1,3},{4,0},{5,1},{8,4},{9,5},{12,8},{13,9},{14,12},{15,13},... | collective-permute-start | bytes 1622024 | tf_op jit(solution)/shard_map/gather_long_1/ppermute | solution.py:207
  6.1 6.4 %keep.1 = (bf16[4096,1536]{1,0:T(8,128)(2,1)S(1)}, bf16[768,4096]{1,0:T(8,128)(2,1)S(1)}) custom-call(bf16[4096,1536]{1,0:T(8,128)(2,1)} %bitcast.2, bf16[768,4096]{1,0:T(8,128)(2,1)} %bitcast.3), custom_call_target="tpu_custom_call" | custom-call | bytes 18874368 | tf_op jit(solution)/shard_map/keep/pallas_call | solution.py:67
  12.5 4.0 %expert.5 = (bf16[32,4096]{1,0:T(8,128)(2,1)S(1)}, bf16[32,4096]{1,0:T(8,128)(2,1)S(1)}, bf16[32,4096]{1,0:T(8,128)(2,1)S(1)}, bf16[32,4096]{1,0:T(8,128)(2,1)S(1)}) custom-call(bf16[64,4224]{1,0:T(8,128)(2,1)S(1)} %pack.1.refs_0_, bf16[64,4224]{1,0:T(8,128)(2,1)S(1)} %collective-permute-done.refs_1_, ...), custom_call_target="tpu_custom_call" | custom-call | flops 4831838208 | tf_op jit(solution)/shard_map/expert/pallas_call | solution.py:125
  16.5 2.4 %collective-permute-done.3.refs_1_ = bf16[64,4224]{1,0:T(8,128)(2,1)S(1)} collective-permute-done((bf16[64,4224]{1,0:T(8,128)(2,1)S(1)}, bf16[64,4224]{1,0:T(8,128)(2,1)S(1)}, u32[]{:S(2)}, u32[]{:S(2)}) %collective-permute-start.3) | collective-permute-done | bytes 540704 | tf_op jit(solution)/shard_map/gather_long_1/ppermute | solution.py:207
  21.3 1.7 %collective-permute-start.8 = (bf16[32,4224]{1,0:T(8,128)(2,1)S(1)}, bf16[32,4224]{1,0:T(8,128)(2,1)S(1)}, u32[]{:S(2)}, u32[]{:S(2)}) collective-permute-start(bf16[32,4224]{1,0:T(8,128)(2,1)S(1)} %get-tuple-element.114), channel_id=1, source_target_pairs={{0,2},{1,3},{4,0},{5,1},{8,4},{9,5},{12,8},{13,9},{14,12},{15,13},... | collective-permute-start | bytes 811016 | tf_op jit(solution)/shard_map/gather_short_2/ppermute | solution.py:207
  23.3 1.7 %collective-permute-start.21 = (bf16[32,4224]{1,0:T(8,128)(2,1)S(1)}, bf16[32,4224]{1,0:T(8,128)(2,1)S(1)}, u32[]{:S(2)}, u32[]{:S(2)}) collective-permute-start(bf16[32,4224]{1,0:T(8,128)(2,1)S(1)} %get-tuple-element.135), channel_id=1, source_target_pairs={{0,2},{1,3},{4,0},{5,1},{8,4},{9,5},{12,8},{13,9},{14,12},{15,13},... | collective-permute-start | bytes 811016 | tf_op jit(solution)/shard_map/gather_long_2/ppermute | solution.py:207
  25.0 6.4 %expert.6 = (bf16[32,4096]{1,0:T(8,128)(2,1)S(1)}, bf16[32,4096]{1,0:T(8,128)(2,1)S(1)}, bf16[32,4096]{1,0:T(8,128)(2,1)S(1)}, bf16[32,4096]{1,0:T(8,128)(2,1)S(...) custom-call(bf16[64,4224]{1,0:T(8,128)(2,1)S(1)} %collective-permute, ...), custom_call_target="tpu_custom_call" | custom-call | flops 9663676416 | tf_op jit(solution)/shard_map/expert/pallas_call | solution.py:125
  33.5 2.6 %collective-permute-done.20.refs_2_ = bf16[32,4224]{1,0:T(8,128)(2,1)S(1)} collective-permute-done((bf16[32,4224]{1,0:T(8,128)(2,1)S(1)}, bf16[32,4224]{1,0:T(8,128)(2,1)S(1)}, u32[]{:S(2)}, u32[]{:S(2)}) %collective-permute-start.20) | collective-permute-done | bytes 270368 | tf_op jit(solution)/shard_map/gather_long_2/ppermute | solution.py:207
  36.4 1.7 %collective-permute-start.22 = (bf16[32,4224]{1,0:T(8,128)(2,1)S(1)}, bf16[32,4224]{1,0:T(8,128)(2,1)S(1)}, u32[]{:S(2)}, u32[]{:S(2)}) collective-permute-start(bf16[32,4224]{1,0:T(8,128)(2,1)S(1)} %collective-permute-done.20.refs_2_), channel_id=1, source_target_pairs={{0,4},{1,5},{4,8},{5,9},{8,12},{9,13},{12,14},{13,15},{14,10},{15,... | collective-permute-start | bytes 811016 | tf_op jit(solution)/shard_map/gather_long_3/ppermute | solution.py:207
  38.5 3.4 %collective-permute-done.9.refs_0_ = bf16[32,4224]{1,0:T(8,128)(2,1)S(1)} collective-permute-done((bf16[32,4224]{1,0:T(8,128)(2,1)S(1)}, bf16[32,4224]{1,0:T(8,128)(2,1)S(1)}, u32[]{:S(2)}, u32[]{:S(2)}) %collective-permute-start.9) | collective-permute-done | bytes 270368 | tf_op jit(solution)/shard_map/gather_short_3/ppermute | solution.py:207
  42.7 3.9 %collective-permute-done.22.refs_0_ = bf16[32,4224]{1,0:T(8,128)(2,1)S(1)} collective-permute-done((bf16[32,4224]{1,0:T(8,128)(2,1)S(1)}, bf16[32,4224]{1,0:T(8,128)(2,1)S(1)}, u32[]{:S(2)}, u32[]{:S(2)}) %collective-permute-start.22) | collective-permute-done | bytes 270368 | tf_op jit(solution)/shard_map/gather_long_3/ppermute | solution.py:207
  46.8 1.7 %collective-permute-start.24 = (bf16[32,4224]{1,0:T(8,128)(2,1)S(1)}, bf16[32,4224]{1,0:T(8,128)(2,1)S(1)}, u32[]{:S(2)}, u32[]{:S(2)}) collective-permute-start(bf16[32,4224]{1,0:T(8,128)(2,1)S(1)} %collective-permute-done.22.refs_0_), channel_id=1, source_target_pairs={{0,4},{1,5},{4,8},{5,9},{8,12},{9,13},{12,14},{13,15},{14,10},{15,... | collective-permute-start | bytes 811016 | tf_op jit(solution)/shard_map/gather_long_4/ppermute | solution.py:207
  48.8 6.4 %expert.7 = (bf16[32,4096]{1,0:T(8,128)(2,1)S(1)}, bf16[32,4096]{1,0:T(8,128)(2,1)S(1)}, bf16[32,4096]{1,0:T(8,128)(2,1)S(1)}, bf16[32,4096]{1,0:T(8,128)(2,1)S(...) custom-call(bf16[32,4224]{1,0:T(8,128)(2,1)S(1)} %collective-permute, ...), custom_call_target="tpu_custom_call" | custom-call | flops 9663676416 | tf_op jit(solution)/shard_map/expert/pallas_call | solution.py:125
  58.0 1.7 %collective-permute-start.18 = (bf16[32,4096]{1,0:T(8,128)(2,1)S(1)}, bf16[32,4096]{1,0:T(8,128)(2,1)S(1)}, u32[]{:S(2)}, u32[]{:S(2)}) collective-permute-start(bf16[32,4096]{1,0:T(8,128)(2,1)S(1)} %get-tuple-element.132), channel_id=1, source_target_pairs={{0,4},{1,5},{4,8},{5,9},{8,12},{9,13},{12,14},{13,15},{14,10},{15,... | collective-permute-start | bytes 786440 | tf_op jit(solution)/shard_map/return_short_3/ppermute | solution.py:207
  60.0 3.9 %expert.8 = (bf16[32,4096]{1,0:T(8,128)(2,1)S(1)}, bf16[32,4096]{1,0:T(8,128)(2,1)S(1)}, bf16[32,4096]{1,0:T(8,128)(2,1)S(1)}, bf16[32,4096]{1,0:T(8,128)(2,1)S(1)}) custom-call(bf16[32,4224]{1,0:T(8,128)(2,1)S(1)} %collective-permute-done.24.refs_0_, bf16[32,4224]{1,0:T(8,128)(2,1)S(1)} %collective-permute-done.25.refs_1_, ...), custom_call_target="tpu_custom_call" | custom-call | flops 4831838208 | tf_op jit(solution)/shard_map/expert/pallas_call | solution.py:125
  64.5 1.8 %collective-permute-done.18.refs_2_ = bf16[32,4096]{1,0:T(8,128)(2,1)S(1)} collective-permute-done((bf16[32,4096]{1,0:T(8,128)(2,1)S(1)}, bf16[32,4096]{1,0:T(8,128)(2,1)S(1)}, u32[]{:S(2)}, u32[]{:S(2)}) %collective-permute-start.18) | collective-permute-done | bytes 262176 | tf_op jit(solution)/shard_map/return_short_3/ppermute | solution.py:207
  66.3 1.5 %collective-permute-done.19.refs_5_ = bf16[32,4096]{1,0:T(8,128)(2,1)S(1)} collective-permute-done((bf16[32,4096]{1,0:T(8,128)(2,1)S(1)}, bf16[32,4096]{1,0:T(8,128)(2,1)S(1)}, u32[]{:S(2)}, u32[]{:S(2)}) %collective-permute-start.19) | collective-permute-done | bytes 262176 | tf_op jit(solution)/shard_map/return_short_3/ppermute | solution.py:207
  69.9 1.6 %collective-permute-start.38 = (bf16[32,4096]{1,0:T(8,128)(2,1)S(1)}, bf16[32,4096]{1,0:T(8,128)(2,1)S(1)}, u32[]{:S(2)}, u32[]{:S(2)}) collective-permute-start(bf16[32,4096]{1,0:T(8,128)(2,1)S(1)} %get-tuple-element.150), channel_id=1, source_target_pairs={{0,4},{1,5},{4,8},{5,9},{8,12},{9,13},{12,14},{13,15},{14,10},{15,... | collective-permute-start | bytes 786440 | tf_op jit(solution)/shard_map/return_long_4/ppermute | solution.py:207
  71.9 6.4 %expert.9 = (bf16[32,4096]{1,0:T(8,128)(2,1)S(1)}, bf16[32,4096]{1,0:T(8,128)(2,1)S(1)}, bf16[32,4096]{1,0:T(8,128)(2,1)S(1)}, bf16[32,4096]{1,0:T(8,128)(2,1)S(...) custom-call(bf16[32,4224]{1,0:T(8,128)(2,1)S(1)} %collective-permute, ...), custom_call_target="tpu_custom_call" | custom-call | flops 9663676416 | tf_op jit(solution)/shard_map/expert/pallas_call | solution.py:125
  79.3 1.6 %collective-permute-start.31 = (bf16[32,4096]{1,0:T(8,128)(2,1)S(1)}, bf16[32,4096]{1,0:T(8,128)(2,1)S(1)}, u32[]{:S(2)}, u32[]{:S(2)}) collective-permute-start(bf16[32,4096]{1,0:T(8,128)(2,1)S(1)} %get-tuple-element.156), channel_id=1, source_target_pairs={{0,4},{1,5},{4,8},{5,9},{8,12},{9,13},{12,14},{13,15},{14,10},{15,... | collective-permute-start | bytes 786440 | tf_op jit(solution)/shard_map/return_short_2/ppermute | solution.py:207
  81.6 1.6 %collective-permute-start.45 = (bf16[32,4096]{1,0:T(8,128)(2,1)S(1)}, bf16[32,4096]{1,0:T(8,128)(2,1)S(1)}, u32[]{:S(2)}, u32[]{:S(2)}) collective-permute-start(bf16[32,4096]{1,0:T(8,128)(2,1)S(1)} %get-tuple-element.172), channel_id=1, source_target_pairs={{0,4},{1,5},{4,8},{5,9},{8,12},{9,13},{12,14},{13,15},{14,10},{15,... | collective-permute-start | bytes 786440 | tf_op jit(solution)/shard_map/return_long_3/ppermute | solution.py:207
  83.6 4.8 %collective-permute-done.31.refs_2_ = bf16[32,4096]{1,0:T(8,128)(2,1)S(1)} collective-permute-done((bf16[32,4096]{1,0:T(8,128)(2,1)S(1)}, bf16[32,4096]{1,0:T(8,128)(2,1)S(1)}, u32[]{:S(2)}, u32[]{:S(2)}) %collective-permute-start.31) | collective-permute-done | bytes 262176 | tf_op jit(solution)/shard_map/return_short_2/ppermute | solution.py:207
  88.4 1.6 %collective-permute-done.32.refs_5_ = bf16[32,4096]{1,0:T(8,128)(2,1)S(1)} collective-permute-done((bf16[32,4096]{1,0:T(8,128)(2,1)S(1)}, bf16[32,4096]{1,0:T(8,128)(2,1)S(1)}, u32[]{:S(2)}, u32[]{:S(2)}) %collective-permute-start.32) | collective-permute-done | bytes 262176 | tf_op jit(solution)/shard_map/return_short_2/ppermute | solution.py:207
  90.2 1.6 %collective-permute-start.42 = (bf16[32,4096]{1,0:T(8,128)(2,1)S(1)}, bf16[32,4096]{1,0:T(8,128)(2,1)S(1)}, u32[]{:S(2)}, u32[]{:S(2)}) collective-permute-start(bf16[32,4096]{1,0:T(8,128)(2,1)S(1)} %get-tuple-element.178), channel_id=1, source_target_pairs={{0,4},{1,5},{4,8},{5,9},{8,12},{9,13},{12,14},{13,15},{14,10},{15,... | collective-permute-start | bytes 786440 | tf_op jit(solution)/shard_map/return_short_1/ppermute | solution.py:207
  91.9 1.8 %collective-permute-done.45.refs_2_ = bf16[32,4096]{1,0:T(8,128)(2,1)S(1)} collective-permute-done((bf16[32,4096]{1,0:T(8,128)(2,1)S(1)}, bf16[32,4096]{1,0:T(8,128)(2,1)S(1)}, u32[]{:S(2)}, u32[]{:S(2)}) %collective-permute-start.45) | collective-permute-done | bytes 262176 | tf_op jit(solution)/shard_map/return_long_3/ppermute | solution.py:207
  95.1 1.6 %collective-permute-start.48 = (bf16[32,4096]{1,0:T(8,128)(2,1)S(1)}, bf16[32,4096]{1,0:T(8,128)(2,1)S(1)}, u32[]{:S(2)}, u32[]{:S(2)}) collective-permute-start(bf16[32,4096]{1,0:T(8,128)(2,1)S(1)} %get-tuple-element.188), channel_id=1, source_target_pairs={{0,4},{1,5},{4,8},{5,9},{8,12},{9,13},{12,14},{13,15},{14,10},{15,... | collective-permute-start | bytes 786440 | tf_op jit(solution)/shard_map/return_long_2/ppermute | solution.py:207
  97.2 2.3 %collective-permute-done.42.refs_2_ = bf16[32,4096]{1,0:T(8,128)(2,1)S(1)} collective-permute-done((bf16[32,4096]{1,0:T(8,128)(2,1)S(1)}, bf16[32,4096]{1,0:T(8,128)(2,1)S(1)}, u32[]{:S(2)}, u32[]{:S(2)}) %collective-permute-start.42) | collective-permute-done | bytes 262176 | tf_op jit(solution)/shard_map/return_short_1/ppermute | solution.py:207
  99.5 3.5 %collective-permute-done.50.refs_7_ = bf16[32,4096]{1,0:T(8,128)(2,1)S(1)} collective-permute-done((bf16[32,4096]{1,0:T(8,128)(2,1)S(1)}, bf16[32,4096]{1,0:T(8,128)(2,1)S(1)}, u32[]{:S(2)}, u32[]{:S(2)}) %collective-permute-start.50) | collective-permute-done | bytes 262176 | tf_op jit(solution)/shard_map/return_short_1/ppermute | solution.py:207
  102.9 1.9 %collective-permute-done.48.refs_2_ = bf16[32,4096]{1,0:T(8,128)(2,1)S(1)} collective-permute-done((bf16[32,4096]{1,0:T(8,128)(2,1)S(1)}, bf16[32,4096]{1,0:T(8,128)(2,1)S(1)}, u32[]{:S(2)}, u32[]{:S(2)}) %collective-permute-start.48) | collective-permute-done | bytes 262176 | tf_op jit(solution)/shard_map/return_long_2/ppermute | solution.py:207
  104.8 2.2 %collective-permute-done.49.refs_5_ = bf16[32,4096]{1,0:T(8,128)(2,1)S(1)} collective-permute-done((bf16[32,4096]{1,0:T(8,128)(2,1)S(1)}, bf16[32,4096]{1,0:T(8,128)(2,1)S(1)}, u32[]{:S(2)}, u32[]{:S(2)}) %collective-permute-start.49) | collective-permute-done | bytes 262176 | tf_op jit(solution)/shard_map/return_long_2/ppermute | solution.py:207
  107.6 1.7 %collective-permute-start.54 = (bf16[32,4096]{1,0:T(8,128)(2,1)S(1)}, bf16[32,4096]{1,0:T(8,128)(2,1)S(1)}, u32[]{:S(2)}, u32[]{:S(2)}) collective-permute-start(bf16[32,4096]{1,0:T(8,128)(2,1)S(1)} %get-tuple-element.196), channel_id=1, source_target_pairs={{0,4},{1,5},{4,8},{5,9},{8,12},{9,13},{12,14},{13,15},{14,10},{15,... | collective-permute-start | bytes 786440 | tf_op jit(solution)/shard_map/return_long_1/ppermute | solution.py:207
  109.3 4.8 %collective-permute-done.52.refs_3_ = bf16[32,4096]{1,0:T(8,128)(2,1)S(1)} collective-permute-done((bf16[32,4096]{1,0:T(8,128)(2,1)S(1)}, bf16[32,4096]{1,0:T(8,128)(2,1)S(1)}, u32[]{:S(2)}, u32[]{:S(2)}) %collective-permute-start.52) | collective-permute-done | bytes 262176 | tf_op jit(solution)/shard_map/return_long_1/ppermute | solution.py:207
  (103 shorter events, 22.2 us)
Async XLA Ops:
  2.8 9.6 %collective-permute-start = (bf16[64,4224]{1,0:T(8,128)(2,1)S(1)}, bf16[64,4224]{1,0:T(8,128)(2,1)S(1)}, u32[]{:S(2)}, u32[]{:S(2)}) collective-permute-start(bf16[64,4224]{1,0:T(8,128)(2,1)S(1)} %pack.1.refs_0_), channel_id=1, source_target_pairs={{0,1},{1,0},{2,3},{3,2},{4,5},{5,4},{6,7},{7,6},{8,9},{9,8},{10,11... | collective-permute-start | bytes 1622024 | tf_op jit(solution)/shard_map/swap_in_0/ppermute | solution.py:207
  3.3 15.5 %collective-permute-start.3 = (bf16[64,4224]{1,0:T(8,128)(2,1)S(1)}, bf16[64,4224]{1,0:T(8,128)(2,1)S(1)}, u32[]{:S(2)}, u32[]{:S(2)}) collective-permute-start(bf16[64,4224]{1,0:T(8,128)(2,1)S(1)} %pack.1.refs_0_), channel_id=1, source_target_pairs={{0,2},{1,3},{4,0},{5,1},{8,4},{9,5},{12,8},{13,9},{14,12},{15,13},... | collective-permute-start | bytes 1622024 | tf_op jit(solution)/shard_map/gather_long_1/ppermute | solution.py:207
  5.9 14.3 %collective-permute-start.2 = (bf16[64,4224]{1,0:T(8,128)(2,1)S(1)}, bf16[64,4224]{1,0:T(8,128)(2,1)S(1)}, u32[]{:S(2)}, u32[]{:S(2)}) collective-permute-start(bf16[64,4224]{1,0:T(8,128)(2,1)S(1)} %pack.1.refs_0_), channel_id=1, source_target_pairs={{0,4},{1,5},{4,8},{5,9},{8,12},{9,13},{12,14},{13,15},{14,10},{15,... | collective-permute-start | bytes 1622024 | tf_op jit(solution)/shard_map/gather_long_1/ppermute | solution.py:207
  20.9 10.5 %collective-permute-start.7 = (bf16[32,4224]{1,0:T(8,128)(2,1)S(1)}, bf16[32,4224]{1,0:T(8,128)(2,1)S(1)}, u32[]{:S(2)}, u32[]{:S(2)}) collective-permute-start(bf16[32,4224]{1,0:T(8,128)(2,1)S(1)} %get-tuple-element.113), channel_id=1, source_target_pairs={{0,4},{1,5},{4,8},{5,9},{8,12},{9,13},{12,14},{13,15},{14,10},{15,... | collective-permute-start | bytes 811016 | tf_op jit(solution)/shard_map/gather_short_2/ppermute | solution.py:207
  21.3 10.2 %collective-permute-start.8 = (bf16[32,4224]{1,0:T(8,128)(2,1)S(1)}, bf16[32,4224]{1,0:T(8,128)(2,1)S(1)}, u32[]{:S(2)}, u32[]{:S(2)}) collective-permute-start(bf16[32,4224]{1,0:T(8,128)(2,1)S(1)} %get-tuple-element.114), channel_id=1, source_target_pairs={{0,2},{1,3},{4,0},{5,1},{8,4},{9,5},{12,8},{13,9},{14,12},{15,13},... | collective-permute-start | bytes 811016 | tf_op jit(solution)/shard_map/gather_short_2/ppermute | solution.py:207
  22.9 13.1 %collective-permute-start.20 = (bf16[32,4224]{1,0:T(8,128)(2,1)S(1)}, bf16[32,4224]{1,0:T(8,128)(2,1)S(1)}, u32[]{:S(2)}, u32[]{:S(2)}) collective-permute-start(bf16[32,4224]{1,0:T(8,128)(2,1)S(1)} %get-tuple-element.134), channel_id=1, source_target_pairs={{0,4},{1,5},{4,8},{5,9},{8,12},{9,13},{12,14},{13,15},{14,10},{15,... | collective-permute-start | bytes 811016 | tf_op jit(solution)/shard_map/gather_long_2/ppermute | solution.py:207
  23.3 13.2 %collective-permute-start.21 = (bf16[32,4224]{1,0:T(8,128)(2,1)S(1)}, bf16[32,4224]{1,0:T(8,128)(2,1)S(1)}, u32[]{:S(2)}, u32[]{:S(2)}) collective-permute-start(bf16[32,4224]{1,0:T(8,128)(2,1)S(1)} %get-tuple-element.135), channel_id=1, source_target_pairs={{0,2},{1,3},{4,0},{5,1},{8,4},{9,5},{12,8},{13,9},{14,12},{15,13},... | collective-permute-start | bytes 811016 | tf_op jit(solution)/shard_map/gather_long_2/ppermute | solution.py:207
  31.4 10.4 %collective-permute-start.9 = (bf16[32,4224]{1,0:T(8,128)(2,1)S(1)}, bf16[32,4224]{1,0:T(8,128)(2,1)S(1)}, u32[]{:S(2)}, u32[]{:S(2)}) collective-permute-start(bf16[32,4224]{1,0:T(8,128)(2,1)S(1)} %collective-permute-done.7.refs_2_), channel_id=1, source_target_pairs={{0,4},{1,5},{4,8},{5,9},{8,12},{9,13},{12,14},{13,15},{14,10},{15,... | collective-permute-start | bytes 811016 | tf_op jit(solution)/shard_map/gather_short_3/ppermute | solution.py:207
  32.4 9.8 %collective-permute-start.10 = (bf16[32,4224]{1,0:T(8,128)(2,1)S(1)}, bf16[32,4224]{1,0:T(8,128)(2,1)S(1)}, u32[]{:S(2)}, u32[]{:S(2)}) collective-permute-start(bf16[32,4224]{1,0:T(8,128)(2,1)S(1)} %collective-permute-done.8.refs_3_), channel_id=1, source_target_pairs={{0,2},{1,3},{4,0},{5,1},{8,4},{9,5},{12,8},{13,9},{14,12},{15,13},... | collective-permute-start | bytes 811016 | tf_op jit(solution)/shard_map/gather_short_3/ppermute | solution.py:207
  36.4 10.2 %collective-permute-start.22 = (bf16[32,4224]{1,0:T(8,128)(2,1)S(1)}, bf16[32,4224]{1,0:T(8,128)(2,1)S(1)}, u32[]{:S(2)}, u32[]{:S(2)}) collective-permute-start(bf16[32,4224]{1,0:T(8,128)(2,1)S(1)} %collective-permute-done.20.refs_2_), channel_id=1, source_target_pairs={{0,4},{1,5},{4,8},{5,9},{8,12},{9,13},{12,14},{13,15},{14,10},{15,... | collective-permute-start | bytes 811016 | tf_op jit(solution)/shard_map/gather_long_3/ppermute | solution.py:207
  38.2 8.6 %collective-permute-start.23 = (bf16[32,4224]{1,0:T(8,128)(2,1)S(1)}, bf16[32,4224]{1,0:T(8,128)(2,1)S(1)}, u32[]{:S(2)}, u32[]{:S(2)}) collective-permute-start(bf16[32,4224]{1,0:T(8,128)(2,1)S(1)} %collective-permute-done.21.refs_3_), channel_id=1, source_target_pairs={{0,2},{1,3},{4,0},{5,1},{8,4},{9,5},{12,8},{13,9},{14,12},{15,13},... | collective-permute-start | bytes 811016 | tf_op jit(solution)/shard_map/gather_long_3/ppermute | solution.py:207
  46.8 10.6 %collective-permute-start.24 = (bf16[32,4224]{1,0:T(8,128)(2,1)S(1)}, bf16[32,4224]{1,0:T(8,128)(2,1)S(1)}, u32[]{:S(2)}, u32[]{:S(2)}) collective-permute-start(bf16[32,4224]{1,0:T(8,128)(2,1)S(1)} %collective-permute-done.22.refs_0_), channel_id=1, source_target_pairs={{0,4},{1,5},{4,8},{5,9},{8,12},{9,13},{12,14},{13,15},{14,10},{15,... | collective-permute-start | bytes 811016 | tf_op jit(solution)/shard_map/gather_long_4/ppermute | solution.py:207
  48.5 8.9 %collective-permute-start.25 = (bf16[32,4224]{1,0:T(8,128)(2,1)S(1)}, bf16[32,4224]{1,0:T(8,128)(2,1)S(1)}, u32[]{:S(2)}, u32[]{:S(2)}) collective-permute-start(bf16[32,4224]{1,0:T(8,128)(2,1)S(1)} %collective-permute-done.23.refs_1_), channel_id=1, source_target_pairs={{0,2},{1,3},{4,0},{5,1},{8,4},{9,5},{12,8},{13,9},{14,12},{15,13},... | collective-permute-start | bytes 811016 | tf_op jit(solution)/shard_map/gather_long_4/ppermute | solution.py:207
  58.0 8.3 %collective-permute-start.18 = (bf16[32,4096]{1,0:T(8,128)(2,1)S(1)}, bf16[32,4096]{1,0:T(8,128)(2,1)S(1)}, u32[]{:S(2)}, u32[]{:S(2)}) collective-permute-start(bf16[32,4096]{1,0:T(8,128)(2,1)S(1)} %get-tuple-element.132), channel_id=1, source_target_pairs={{0,4},{1,5},{4,8},{5,9},{8,12},{9,13},{12,14},{13,15},{14,10},{15,... | collective-permute-start | bytes 786440 | tf_op jit(solution)/shard_map/return_short_3/ppermute | solution.py:207
  59.7 8.1 %collective-permute-start.19 = (bf16[32,4096]{1,0:T(8,128)(2,1)S(1)}, bf16[32,4096]{1,0:T(8,128)(2,1)S(1)}, u32[]{:S(2)}, u32[]{:S(2)}) collective-permute-start(bf16[32,4096]{1,0:T(8,128)(2,1)S(1)} %get-tuple-element.133), channel_id=1, source_target_pairs={{0,2},{1,3},{4,0},{5,1},{8,4},{9,5},{12,8},{13,9},{14,12},{15,13},... | collective-permute-start | bytes 786440 | tf_op jit(solution)/shard_map/return_short_3/ppermute | solution.py:207
  69.0 9.5 %collective-permute-start.15 = (bf16[32,4096]{1,0:T(8,128)(2,1)S(1)}, bf16[32,4096]{1,0:T(8,128)(2,1)S(1)}, u32[]{:S(2)}, u32[]{:S(2)}) collective-permute-start(bf16[32,4096]{1,0:T(8,128)(2,1)S(1)} %get-tuple-element.127), channel_id=1, source_target_pairs={{0,1},{1,0},{2,3},{3,2},{4,5},{5,4},{6,7},{7,6},{8,9},{9,8},{10,11... | collective-permute-start | bytes 786440 | tf_op jit(solution)/shard_map/swap_out_3/ppermute | solution.py:207
  69.5 9.4 %collective-permute-start.30 = (bf16[32,4096]{1,0:T(8,128)(2,1)S(1)}, bf16[32,4096]{1,0:T(8,128)(2,1)S(1)}, u32[]{:S(2)}, u32[]{:S(2)}) collective-permute-start(bf16[32,4096]{1,0:T(8,128)(2,1)S(1)} %get-tuple-element.154), channel_id=1, source_target_pairs={{0,1},{1,0},{2,3},{3,2},{4,5},{5,4},{6,7},{7,6},{8,9},{9,8},{10,11... | collective-permute-start | bytes 786440 | tf_op jit(solution)/shard_map/swap_out_3/ppermute | solution.py:207
  69.9 9.3 %collective-permute-start.38 = (bf16[32,4096]{1,0:T(8,128)(2,1)S(1)}, bf16[32,4096]{1,0:T(8,128)(2,1)S(1)}, u32[]{:S(2)}, u32[]{:S(2)}) collective-permute-start(bf16[32,4096]{1,0:T(8,128)(2,1)S(1)} %get-tuple-element.150), channel_id=1, source_target_pairs={{0,4},{1,5},{4,8},{5,9},{8,12},{9,13},{12,14},{13,15},{14,10},{15,... | collective-permute-start | bytes 786440 | tf_op jit(solution)/shard_map/return_long_4/ppermute | solution.py:207
  71.5 9.4 %collective-permute-start.39 = (bf16[32,4096]{1,0:T(8,128)(2,1)S(1)}, bf16[32,4096]{1,0:T(8,128)(2,1)S(1)}, u32[]{:S(2)}, u32[]{:S(2)}) collective-permute-start(bf16[32,4096]{1,0:T(8,128)(2,1)S(1)} %get-tuple-element.151), channel_id=1, source_target_pairs={{0,2},{1,3},{4,0},{5,1},{8,4},{9,5},{12,8},{13,9},{14,12},{15,13},... | collective-permute-start | bytes 786440 | tf_op jit(solution)/shard_map/return_long_4/ppermute | solution.py:207
  79.3 9.2 %collective-permute-start.31 = (bf16[32,4096]{1,0:T(8,128)(2,1)S(1)}, bf16[32,4096]{1,0:T(8,128)(2,1)S(1)}, u32[]{:S(2)}, u32[]{:S(2)}) collective-permute-start(bf16[32,4096]{1,0:T(8,128)(2,1)S(1)} %get-tuple-element.156), channel_id=1, source_target_pairs={{0,4},{1,5},{4,8},{5,9},{8,12},{9,13},{12,14},{13,15},{14,10},{15,... | collective-permute-start | bytes 786440 | tf_op jit(solution)/shard_map/return_short_2/ppermute | solution.py:207
  80.9 9.1 %collective-permute-start.32 = (bf16[32,4096]{1,0:T(8,128)(2,1)S(1)}, bf16[32,4096]{1,0:T(8,128)(2,1)S(1)}, u32[]{:S(2)}, u32[]{:S(2)}) collective-permute-start(bf16[32,4096]{1,0:T(8,128)(2,1)S(1)} %get-tuple-element.157), channel_id=1, source_target_pairs={{0,2},{1,3},{4,0},{5,1},{8,4},{9,5},{12,8},{13,9},{14,12},{15,13},... | collective-permute-start | bytes 786440 | tf_op jit(solution)/shard_map/return_short_2/ppermute | solution.py:207
  81.3 8.7 %collective-permute-start.41 = (bf16[32,4096]{1,0:T(8,128)(2,1)S(1)}, bf16[32,4096]{1,0:T(8,128)(2,1)S(1)}, u32[]{:S(2)}, u32[]{:S(2)}) collective-permute-start(bf16[32,4096]{1,0:T(8,128)(2,1)S(1)} %get-tuple-element.176), channel_id=1, source_target_pairs={{0,1},{1,0},{2,3},{3,2},{4,5},{5,4},{6,7},{7,6},{8,9},{9,8},{10,11... | collective-permute-start | bytes 786440 | tf_op jit(solution)/shard_map/swap_out_1/ppermute | solution.py:207
  81.6 12.1 %collective-permute-start.45 = (bf16[32,4096]{1,0:T(8,128)(2,1)S(1)}, bf16[32,4096]{1,0:T(8,128)(2,1)S(1)}, u32[]{:S(2)}, u32[]{:S(2)}) collective-permute-start(bf16[32,4096]{1,0:T(8,128)(2,1)S(1)} %get-tuple-element.172), channel_id=1, source_target_pairs={{0,4},{1,5},{4,8},{5,9},{8,12},{9,13},{12,14},{13,15},{14,10},{15,... | collective-permute-start | bytes 786440 | tf_op jit(solution)/shard_map/return_long_3/ppermute | solution.py:207
  83.2 11.7 %collective-permute-start.46 = (bf16[32,4096]{1,0:T(8,128)(2,1)S(1)}, bf16[32,4096]{1,0:T(8,128)(2,1)S(1)}, u32[]{:S(2)}, u32[]{:S(2)}) collective-permute-start(bf16[32,4096]{1,0:T(8,128)(2,1)S(1)} %get-tuple-element.173), channel_id=1, source_target_pairs={{0,2},{1,3},{4,0},{5,1},{8,4},{9,5},{12,8},{13,9},{14,12},{15,13},... | collective-permute-start | bytes 786440 | tf_op jit(solution)/shard_map/return_long_3/ppermute | solution.py:207
  90.2 9.2 %collective-permute-start.42 = (bf16[32,4096]{1,0:T(8,128)(2,1)S(1)}, bf16[32,4096]{1,0:T(8,128)(2,1)S(1)}, u32[]{:S(2)}, u32[]{:S(2)}) collective-permute-start(bf16[32,4096]{1,0:T(8,128)(2,1)S(1)} %get-tuple-element.178), channel_id=1, source_target_pairs={{0,4},{1,5},{4,8},{5,9},{8,12},{9,13},{12,14},{13,15},{14,10},{15,... | collective-permute-start | bytes 786440 | tf_op jit(solution)/shard_map/return_short_1/ppermute | solution.py:207
  93.7 9.2 %collective-permute-start.50 = (bf16[32,4096]{1,0:T(8,128)(2,1)S(1)}, bf16[32,4096]{1,0:T(8,128)(2,1)S(1)}, u32[]{:S(2)}, u32[]{:S(2)}) collective-permute-start(bf16[32,4096]{1,0:T(8,128)(2,1)S(1)} %get-tuple-element.183), channel_id=1, source_target_pairs={{0,2},{1,3},{4,0},{5,1},{8,4},{9,5},{12,8},{13,9},{14,12},{15,13},... | collective-permute-start | bytes 786440 | tf_op jit(solution)/shard_map/return_short_1/ppermute | solution.py:207
  95.1 9.7 %collective-permute-start.48 = (bf16[32,4096]{1,0:T(8,128)(2,1)S(1)}, bf16[32,4096]{1,0:T(8,128)(2,1)S(1)}, u32[]{:S(2)}, u32[]{:S(2)}) collective-permute-start(bf16[32,4096]{1,0:T(8,128)(2,1)S(1)} %get-tuple-element.188), channel_id=1, source_target_pairs={{0,4},{1,5},{4,8},{5,9},{8,12},{9,13},{12,14},{13,15},{14,10},{15,... | collective-permute-start | bytes 786440 | tf_op jit(solution)/shard_map/return_long_2/ppermute | solution.py:207
  96.7 10.3 %collective-permute-start.49 = (bf16[32,4096]{1,0:T(8,128)(2,1)S(1)}, bf16[32,4096]{1,0:T(8,128)(2,1)S(1)}, u32[]{:S(2)}, u32[]{:S(2)}) collective-permute-start(bf16[32,4096]{1,0:T(8,128)(2,1)S(1)} %get-tuple-element.189), channel_id=1, source_target_pairs={{0,2},{1,3},{4,0},{5,1},{8,4},{9,5},{12,8},{13,9},{14,12},{15,13},... | collective-permute-start | bytes 786440 | tf_op jit(solution)/shard_map/return_long_2/ppermute | solution.py:207
  97.2 9.9 %collective-permute-start.43 = (bf16[32,4096]{1,0:T(8,128)(2,1)S(1)}, bf16[32,4096]{1,0:T(8,128)(2,1)S(1)}, u32[]{:S(2)}, u32[]{:S(2)}) collective-permute-start(bf16[32,4096]{1,0:T(8,128)(2,1)S(1)} %get-tuple-element.180), channel_id=1, source_target_pairs={{0,1},{1,0},{2,3},{3,2},{4,5},{5,4},{6,7},{7,6},{8,9},{9,8},{10,11... | collective-permute-start | bytes 786440 | tf_op jit(solution)/shard_map/swap_out_1/ppermute | solution.py:207
  99.5 7.6 %collective-permute-start.51 = (bf16[32,4096]{1,0:T(8,128)(2,1)S(1)}, bf16[32,4096]{1,0:T(8,128)(2,1)S(1)}, u32[]{:S(2)}, u32[]{:S(2)}) collective-permute-start(bf16[32,4096]{1,0:T(8,128)(2,1)S(1)} %get-tuple-element.191), channel_id=1, source_target_pairs={{0,1},{1,0},{2,3},{3,2},{4,5},{5,4},{6,7},{7,6},{8,9},{9,8},{10,11... | collective-permute-start | bytes 786440 | tf_op jit(solution)/shard_map/swap_out_1/ppermute | solution.py:207
  107.3 6.9 %collective-permute-start.52 = (bf16[32,4096]{1,0:T(8,128)(2,1)S(1)}, bf16[32,4096]{1,0:T(8,128)(2,1)S(1)}, u32[]{:S(2)}, u32[]{:S(2)}) collective-permute-start(bf16[32,4096]{1,0:T(8,128)(2,1)S(1)} %get-tuple-element.193), channel_id=1, source_target_pairs={{0,2},{1,3},{4,0},{5,1},{8,4},{9,5},{12,8},{13,9},{14,12},{15,13},... | collective-permute-start | bytes 786440 | tf_op jit(solution)/shard_map/return_long_1/ppermute | solution.py:207
  107.6 6.7 %collective-permute-start.54 = (bf16[32,4096]{1,0:T(8,128)(2,1)S(1)}, bf16[32,4096]{1,0:T(8,128)(2,1)S(1)}, u32[]{:S(2)}, u32[]{:S(2)}) collective-permute-start(bf16[32,4096]{1,0:T(8,128)(2,1)S(1)} %get-tuple-element.196), channel_id=1, source_target_pairs={{0,4},{1,5},{4,8},{5,9},{8,12},{9,13},{12,14},{13,15},{14,10},{15,... | collective-permute-start | bytes 786440 | tf_op jit(solution)/shard_map/return_long_1/ppermute | solution.py:207
  (26 other events, 113.0 us)

commit v11 on v9

--- a/solution.py
+++ b/solution.py
@@ -26,36 +26,51 @@
     return pltpu.CompilerParams(vmem_limit_bytes=mebibytes << 20)
 
 
-def pack_kernel(experts, core, tokens, routes, gate_num, own, other, digits):
+def pack_kernel(experts, core, tokens, routes, gate_num, own, for_other, routes_here, gate_num_here, digits, sem):
     rows, width = tokens.shape
     half = rows // 2
-    lane = lax.broadcasted_iota(jnp.int32, (rows, LANES), 1)
-    expert = jnp.where(lane < experts, lane, lane - experts)
-    dense = jnp.zeros((rows, LANES), jnp.int32)
-    for pick in range(routes.shape[1]):
-        column = slice(pick, pick + 1)
-        dense += jnp.where(routes[:, column] == expert, gate_num[:, column], 0)
-    digit = jnp.where(lane < experts, dense >> 8, dense & 255)
-    digit = jnp.where(lane < 2 * experts, digit, 0)
-    digits[...] = digit.astype(jnp.float32).astype(jnp.bfloat16)
-    for packed, place in ((own, core[0]), (other, 1 - core[0])):
-        for there, place_here in ((0, place), (half, 1 - place)):
-            here = pl.ds(pl.multiple_of(place_here * half, half), half)
-            packed[there : there + half, :width] = tokens[here]
-            packed[there : there + half, width:] = digits[here]
+    halves = []
+    for packed, place in ((own, core[0]), (for_other, 1 - core[0])):
+        for there, from_place in ((0, place), (half, 1 - place)):
+            halves.append((packed, there, pl.ds(pl.multiple_of(from_place * half, half), half)))
+    copies = [pltpu.make_async_copy(routes, routes_here, sem.at[0])]
+    copies.append(pltpu.make_async_copy(gate_num, gate_num_here, sem.at[1]))
+    for number, (packed, there, here) in enumerate(halves):
+        target = packed.at[pl.ds(there, half), pl.ds(0, width)]
+        copies.append(pltpu.make_async_copy(tokens.at[here], target, sem.at[2 + number]))
+    for copy in copies:
+        copy.start()
+    for copy in copies[:2]:
+        copy.wait()
+
+    place = lax.broadcasted_iota(jnp.int32, (LANES, rows), 0)
+    expert = jnp.where(place < experts, place, place - experts)
+    dense = jnp.zeros((LANES, rows), jnp.int32)
+    for pick in range(routes_here.shape[0]):
+        choice = slice(pick, pick + 1)
+        dense += jnp.where(routes_here[choice] == expert, gate_num_here[choice], 0)
+    digit = jnp.where(place < experts, dense >> 8, dense & 255)
+    digit = jnp.where(place < 2 * experts, digit, 0)
+    digits[...] = digit.astype(jnp.float32).T.astype(jnp.bfloat16)
+    for packed, there, here in halves:
+        packed[there : there + half, width:] = digits[here]
+    for copy in copies[2:]:
+        copy.wait()
 
 
 def pack(core, tokens, routes, gate_num, experts):
     rows, width = tokens.shape
+    operands = [pltpu.with_memory_space_constraint(x, pltpu.HBM) for x in (tokens, routes.T, gate_num.T)]
     return pl.pallas_call(
         functools.partial(pack_kernel, experts),
-        in_specs=[SMEM] + [VMEM] * 3,
+        in_specs=[SMEM] + [ANYWHERE] * 3,
         out_specs=[VMEM] * 2,
         out_shape=[jax.ShapeDtypeStruct((rows, width + LANES), jnp.bfloat16)] * 2,
-        scratch_shapes=[pltpu.VMEM((rows, LANES), jnp.bfloat16)],
+        scratch_shapes=[pltpu.VMEM(routes.T.shape, jnp.int32)] * 2
+        + [pltpu.VMEM((rows, LANES), jnp.bfloat16), pltpu.SemaphoreType.DMA((6,))],
         compiler_params=limits(4),
         name="pack",
-    )(core, tokens, routes, gate_num)
+    )(core, *operands)
 
 
 def keep_kernel(gate_up, down, gate_up_here, down_here, sem):
@@ -182,6 +197,30 @@
     )(*arrays)
 
 
+def split_kernel(*refs):
+    *terms, first, second = refs
+    half = first.shape[0]
+    for out, start in ((first, 0), (second, half)):
+        for column in range(0, out.shape[1], WIDTH_CHUNK):
+            columns = slice(column, column + WIDTH_CHUNK)
+            total = 0.0
+            for term in terms:
+                total += term[start : start + half, columns].astype(jnp.float32)
+            out[:, columns] = total.astype(jnp.bfloat16)
+
+
+def split_sum(*terms):
+    rows, width = terms[0].shape
+    return pl.pallas_call(
+        split_kernel,
+        in_specs=[VMEM] * len(terms),
+        out_specs=[VMEM] * 2,
+        out_shape=[jax.ShapeDtypeStruct((rows // 2, width), jnp.bfloat16)] * 2,
+        compiler_params=limits(4),
+        name="split_sum",
+    )(*terms)
+
+
 def join_kernel(same, cross, long, short):
     half = same.shape[0] // 2
     for block, first in ((long, 0), (short, half)):
@@ -296,14 +335,13 @@
         return [send(total, on, f"return_{name}_{distance}")], [total]
 
     def arrive(name, carried):
-        sent, totals = [], []
-        for start, perm in ((0, back_to_other), (half, on)):
-            terms = [(x, start) for x in (kept[1, name], given[1, name], *carried)]
-            totals.append(step_sum((half, terms)))
-            sent.append(send(totals[-1], perm, f"return_{name}_1"))
-        return sent, totals
-
-    run([(distance, "short") for distance in (reach - 1, reach - 2) if distance > 1], [])
+        terms = (kept[1, name], given[1, name], *carried)
+        totals = split_sum(*terms)
+        return [send(x, perm, f"return_{name}_1") for x, perm in zip(totals, (back_to_other, on))], totals
+
+    if reach > 3:
+        last = run([(reach - 2, "short")], last)
+    run([(reach - 1, "short")], last)
     short, totals = step(reach - 1, "short", ())
     run([(reach, "long")], totals, 2)
     given[reach, "long"] = after(given[reach, "long"], *short)
@@ -318,7 +356,7 @@
         if distance > 1:
             long, totals = step(distance, "long", [after(x, *totals) for x in long])
         else:
-            long, totals = arrive("long", long)
+            long, totals = arrive("long", [after(x, *short) for x in long])
     short_cross, short_same = short
     long_cross, long_same = long
     return last_sum(core, kept[0], given[0], short_same, long_cross, long_same, short_cross)

time: 110 us -> 111 us (level)
  starting transfers between devices: 28.5 us -> 31.8 us
  local copies, waits for them, and re-layouts: 2.61 us -> 0.01 us
  Pallas kernels: 37.6 us -> 40.1 us
  waiting for transfers between devices: 40.9 us -> 38.7 us
    ppermute x32, starting transfers between devices: 28.5 us -> 31.8 us  [send(): return lax.ppermute(x, 'expert', perm)]
    unnamed x8 -> x4, local copies, waits for them, and re-layouts: 2.61 us -> 0.01 us
    ppermute x32, waiting for transfers between devices: 40.9 us -> 38.7 us  [send(): return lax.ppermute(x, 'expert', perm)]
    pallas_call x6 -> x7, Pallas kernels: 28.7 us -> 30.1 us  [expert_part(): pl.pallas_call(functools.partial(expert_kernel, len(blocks)), in_specs=[V...]
  transfers between devices with their start and end apart: 32 -> 32, of which waited for: 13 -> 13; matrix products, arithmetic and copies ran while one was open for 0% -> 0% of each run, Pallas kernels for 33% -> 34%
where the time goes in v11:
time: 111 us
  Pallas kernels  40.1 us (36%)
  waiting for transfers between devices  38.7 us (35%)
  starting transfers between devices  31.8 us (29%)
    ppermute x32, waiting for transfers between devices, send(): return lax.ppermute(x, 'expert', perm)  38.7 us
    ppermute x32, starting transfers between devices, send(): return lax.ppermute(x, 'expert', perm)  31.8 us
    pallas_call x7, Pallas kernels, expert_part(): pl.pallas_call(functools.partial(expert_kernel, len(blocks)), in_specs=[V...  30.1 us
    pallas_call x1, Pallas kernels, keep(): pl.pallas_call(keep_kernel, in_specs=[ANYWHERE] * 2, out_specs=[VMEM] * 2...  6.38 us
  transfers between devices with their start and end apart: 32, of which 13 were waited for; matrix products, arithmetic and copies ran while one was open for 0% of the time, Pallas kernels for 34%

profile of v11, /device:TPU:0, one launch (start us, length us, event | category | flops | bytes accessed | tf_op | source)
XLA Modules:
  0.0 110.8 jit_solution(5620384311329063415)
XLA Ops:
  1.8 2.6 %collective-permute-start.2 = (bf16[64,4224]{1,0:T(8,128)(2,1)S(1)}, bf16[64,4224]{1,0:T(8,128)(2,1)S(1)}, u32[]{:S(2)}, u32[]{:S(2)}) collective-permute-start(bf16[64,4224]{1,0:T(8,128)(2,1)S(1)} %get-tuple-element.44.refs_0_), channel_id=1, source_target_pairs={{0,4},{1,3},{4,8},{5,1},{8,12},{9,5},{12,14},{13,9},{14,10},{15,13... | collective-permute-start | bytes 1622024 | tf_op jit(solution)/shard_map/gather_long_1/ppermute | solution.py:297
  5.7 6.4 %keep.1 = (bf16[4096,1536]{1,0:T(8,128)(2,1)S(1)}, bf16[768,4096]{1,0:T(8,128)(2,1)S(1)}) custom-call(bf16[4096,1536]{1,0:T(8,128)(2,1)} %bitcast.5, bf16[768,4096]{1,0:T(8,128)(2,1)} %bitcast.6), custom_call_target="tpu_custom_call" | custom-call | bytes 18874368 | tf_op jit(solution)/shard_map/keep/pallas_call | solution.py:88
  12.2 3.9 %expert.7 = (bf16[64,4096]{1,0:T(8,128)(2,1)S(1)}, bf16[64,4096]{1,0:T(8,128)(2,1)S(1)}) custom-call(bf16[64,4224]{1,0:T(8,128)(2,1)S(1)} %get-tuple-element.44.refs_0_, bf16[64,4224]{1,0:T(8,128)(2,1)S(1)} %collective-permute-done.refs_1_, f32[1,128]{1,0:T(1,128)S(1)} %compare_select_fusion.1.refs_2_.refs_4_, f32[1,1536]{1,0:T(1,128)S(1)} %copy-done.1, ...), custom_call_target="tpu_custom_call" | custom-call | flops 4831838208 | tf_op jit(solution)/shard_map/expert/pallas_call | solution.py:146
  16.1 1.4 %collective-permute-done.3.cross = bf16[64,4224]{1,0:T(8,128)(2,1)S(1)} collective-permute-done((bf16[64,4224]{1,0:T(8,128)(2,1)S(1)}, bf16[64,4224]{1,0:T(8,128)(2,1)S(1)}, u32[]{:S(2)}, u32[]{:S(2)}) %collective-permute-start.3) | collective-permute-done | bytes 540704 | tf_op jit(solution)/shard_map/gather_long_1/ppermute | solution.py:297
  18.2 2.1 %collective-permute-start.7 = (bf16[64,4224]{1,0:T(8,128)(2,1)S(1)}, bf16[64,4224]{1,0:T(8,128)(2,1)S(1)}, u32[]{:S(2)}, u32[]{:S(2)}) collective-permute-start(bf16[64,4224]{1,0:T(8,128)(2,1)S(1)} %get-tuple-element.54.refs_3_), channel_id=1, source_target_pairs={{0,4},{1,3},{4,8},{5,1},{8,12},{9,5},{12,14},{13,9},{14,10},{15,13... | collective-permute-start | bytes 1622024 | tf_op jit(solution)/shard_map/gather_short_2/ppermute | solution.py:297
  20.3 1.6 %collective-permute-start.14 = (bf16[64,4224]{1,0:T(8,128)(2,1)S(1)}, bf16[64,4224]{1,0:T(8,128)(2,1)S(1)}, u32[]{:S(2)}, u32[]{:S(2)}) collective-permute-start(bf16[64,4224]{1,0:T(8,128)(2,1)S(1)} %get-tuple-element.52.refs_2_), channel_id=1, source_target_pairs={{0,4},{1,3},{4,8},{5,1},{8,12},{9,5},{12,14},{13,9},{14,10},{15,13... | collective-permute-start | bytes 1622024 | tf_op jit(solution)/shard_map/gather_long_2/ppermute | solution.py:297
  21.8 6.4 %expert.8 = (bf16[64,4096]{1,0:T(8,128)(2,1)S(1)}, bf16[64,4096]{1,0:T(8,128)(2,1)S(1)}, bf16[64,4096]{1,0:T(8,128)(2,1)S(1)}, bf16[64,4096]{1,0:T(8,128)(2,1)S(1)}) custom-call(bf16[64,4224]{1,0:T(8,128)(2,1)S(1)} %collective-permute-done.4.refs_0_, bf16[64,4224]{1,0:T(8,128)(2,1)S(1)} %collective-permute-done.5.refs_1_, ...), custom_call_target="tpu_custom_call" | custom-call | flops 9663676416 | tf_op jit(solution)/shard_map/expert/pallas_call | solution.py:146
  28.4 1.6 %collective-permute-start.10 = (bf16[64,4224]{1,0:T(8,128)(2,1)S(1)}, bf16[64,4224]{1,0:T(8,128)(2,1)S(1)}, u32[]{:S(2)}, u32[]{:S(2)}) collective-permute-start(bf16[64,4224]{1,0:T(8,128)(2,1)S(1)} %collective-permute-done.7.refs_1_), channel_id=1, source_target_pairs={{0,4},{1,3},{4,8},{5,1},{8,12},{9,5},{12,14},{13,9},{14,10},{15,13... | collective-permute-start | bytes 1622024 | tf_op jit(solution)/shard_map/gather_short_3/ppermute | solution.py:297
  30.0 3.4 %collective-permute-done.14.refs_1_ = bf16[64,4224]{1,0:T(8,128)(2,1)S(1)} collective-permute-done((bf16[64,4224]{1,0:T(8,128)(2,1)S(1)}, bf16[64,4224]{1,0:T(8,128)(2,1)S(1)}, u32[]{:S(2)}, u32[]{:S(2)}) %collective-permute-start.14) | collective-permute-done | bytes 540704 | tf_op jit(solution)/shard_map/gather_long_2/ppermute | solution.py:297
  33.3 2.1 %collective-permute-start.15 = (bf16[64,4224]{1,0:T(8,128)(2,1)S(1)}, bf16[64,4224]{1,0:T(8,128)(2,1)S(1)}, u32[]{:S(2)}, u32[]{:S(2)}) collective-permute-start(bf16[64,4224]{1,0:T(8,128)(2,1)S(1)} %collective-permute-done.14.refs_1_), channel_id=1, source_target_pairs={{0,4},{1,3},{4,8},{5,1},{8,12},{9,5},{12,14},{13,9},{14,10},{15,13... | collective-permute-start | bytes 1622024 | tf_op jit(solution)/shard_map/gather_long_3/ppermute | solution.py:297
  35.4 3.9 %expert.9 = (bf16[64,4096]{1,0:T(8,128)(2,1)S(1)}, bf16[64,4096]{1,0:T(8,128)(2,1)S(1)}) custom-call(bf16[64,4224]{1,0:T(8,128)(2,1)S(1)} %collective-permute-done.8.refs_0_, bf16[64,4224]{1,0:T(8,128)(2,1)S(1)} %collective-permute-done.7.refs_1_, f32[1,128]{1,0:T(1,128)S(1)} %compare_select_fusion.1.refs_2_.refs_4_, f32[1,1536]{1,0:T(1,128)S(1)} %copy-done.1, ...), custom_call_target="tpu_custom_call" | custom-call | flops 4831838208 | tf_op jit(solution)/shard_map/expert/pallas_call | solution.py:146
  39.5 5.5 %collective-permute-done.15.refs_1_ = bf16[64,4224]{1,0:T(8,128)(2,1)S(1)} collective-permute-done((bf16[64,4224]{1,0:T(8,128)(2,1)S(1)}, bf16[64,4224]{1,0:T(8,128)(2,1)S(1)}, u32[]{:S(2)}, u32[]{:S(2)}) %collective-permute-start.15) | collective-permute-done | bytes 540704 | tf_op jit(solution)/shard_map/gather_long_3/ppermute | solution.py:297
  44.9 2.1 %collective-permute-start.16 = (bf16[64,4224]{1,0:T(8,128)(2,1)S(1)}, bf16[64,4224]{1,0:T(8,128)(2,1)S(1)}, u32[]{:S(2)}, u32[]{:S(2)}) collective-permute-start(bf16[64,4224]{1,0:T(8,128)(2,1)S(1)} %collective-permute-done.15.refs_1_), channel_id=1, source_target_pairs={{0,4},{1,3},{4,8},{5,1},{8,12},{9,5},{12,14},{13,9},{14,10},{15,13... | collective-permute-start | bytes 1622024 | tf_op jit(solution)/shard_map/gather_long_4/ppermute | solution.py:297
  47.0 4.0 %expert.10 = (bf16[64,4096]{1,0:T(8,128)(2,1)S(1)}, bf16[64,4096]{1,0:T(8,128)(2,1)S(1)}) custom-call(bf16[64,4224]{1,0:T(8,128)(2,1)S(1)} %collective-permute-done.11.refs_0_, bf16[64,4224]{1,0:T(8,128)(2,1)S(1)} %collective-permute-done.10.refs_1_, f32[1,128]{1,0:T(1,128)S(1)} %compare_select_fusion.1.refs_2_.refs_4_, f32[1,1536]{1,0:T(1,128)S(1)} %copy-done.1, ...), custom_call_target="tpu_custom_call" | custom-call | flops 4831838208 | tf_op jit(solution)/shard_map/expert/pallas_call | solution.py:146
  51.0 1.9 %collective-permute-done.12.refs_1_ = bf16[64,4096]{1,0:T(8,128)(2,1)S(1)} collective-permute-done((bf16[64,4096]{1,0:T(8,128)(2,1)S(1)}, bf16[64,4096]{1,0:T(8,128)(2,1)S(1)}, u32[]{:S(2)}, u32[]{:S(2)}) %collective-permute-start.12) | collective-permute-done | bytes 524320 | tf_op jit(solution)/shard_map/swap_out_3/ppermute | solution.py:297
  54.8 2.1 %collective-permute-start.13 = (bf16[64,4096]{1,0:T(8,128)(2,1)S(1)}, bf16[64,4096]{1,0:T(8,128)(2,1)S(1)}, u32[]{:S(2)}, u32[]{:S(2)}) collective-permute-start(bf16[64,4096]{1,0:T(8,128)(2,1)S(1)} %step_sum.5), channel_id=1, source_target_pairs={{0,4},{1,3},{4,8},{5,1},{8,12},{9,5},{12,14},{13,9},{14,10},{15,13... | collective-permute-start | bytes 1572872 | tf_op jit(solution)/shard_map/return_short_3/ppermute | solution.py:297
  56.9 3.9 %expert.11 = (bf16[64,4096]{1,0:T(8,128)(2,1)S(1)}, bf16[64,4096]{1,0:T(8,128)(2,1)S(1)}) custom-call(bf16[64,4224]{1,0:T(8,128)(2,1)S(1)} %collective-permute-done.17.refs_0_, bf16[64,4224]{1,0:T(8,128)(2,1)S(1)} %collective-permute-done.16.refs_1_, f32[1,128]{1,0:T(1,128)S(1)} %compare_select_fusion.1.refs_2_.refs_4_, f32[1,1536]{1,0:T(1,128)S(1)} %copy-done.1, ...), custom_call_target="tpu_custom_call" | custom-call | flops 4831838208 | tf_op jit(solution)/shard_map/expert/pallas_call | solution.py:146
  61.5 2.5 %collective-permute-done.13.refs_2_ = bf16[64,4096]{1,0:T(8,128)(2,1)S(1)} collective-permute-done((bf16[64,4096]{1,0:T(8,128)(2,1)S(1)}, bf16[64,4096]{1,0:T(8,128)(2,1)S(1)}, u32[]{:S(2)}, u32[]{:S(2)}) %collective-permute-start.13) | collective-permute-done | bytes 524320 | tf_op jit(solution)/shard_map/return_short_3/ppermute | solution.py:297
  64.1 2.1 %collective-permute-start.22 = (bf16[64,4096]{1,0:T(8,128)(2,1)S(1)}, bf16[64,4096]{1,0:T(8,128)(2,1)S(1)}, u32[]{:S(2)}, u32[]{:S(2)}) collective-permute-start(bf16[64,4096]{1,0:T(8,128)(2,1)S(1)} %step_sum.6), channel_id=1, source_target_pairs={{0,4},{1,3},{4,8},{5,1},{8,12},{9,5},{12,14},{13,9},{14,10},{15,13... | collective-permute-start | bytes 1572872 | tf_op jit(solution)/shard_map/return_long_4/ppermute | solution.py:297
  66.2 3.9 %expert.12 = (bf16[64,4096]{1,0:T(8,128)(2,1)S(1)}, bf16[64,4096]{1,0:T(8,128)(2,1)S(1)}) custom-call(bf16[64,4224]{1,0:T(8,128)(2,1)S(1)} %collective-permute-done.20.refs_0_, bf16[64,4224]{1,0:T(8,128)(2,1)S(1)} %collective-permute-done.15.refs_1_, f32[1,128]{1,0:T(1,128)S(1)} %compare_select_fusion.1.refs_2_.refs_4_, f32[1,1536]{1,0:T(1,128)S(1)} %copy-done.1, ...), custom_call_target="tpu_custom_call" | custom-call | flops 4831838208 | tf_op jit(solution)/shard_map/expert/pallas_call | solution.py:146
  71.0 1.6 %collective-permute-start.19 = (bf16[64,4096]{1,0:T(8,128)(2,1)S(1)}, bf16[64,4096]{1,0:T(8,128)(2,1)S(1)}, u32[]{:S(2)}, u32[]{:S(2)}) collective-permute-start(bf16[64,4096]{1,0:T(8,128)(2,1)S(1)} %step_sum.7), channel_id=1, source_target_pairs={{0,4},{1,3},{4,8},{5,1},{8,12},{9,5},{12,14},{13,9},{14,10},{15,13... | collective-permute-start | bytes 1572872 | tf_op jit(solution)/shard_map/return_short_2/ppermute | solution.py:297
  73.6 2.1 %collective-permute-start.27 = (bf16[64,4096]{1,0:T(8,128)(2,1)S(1)}, bf16[64,4096]{1,0:T(8,128)(2,1)S(1)}, u32[]{:S(2)}, u32[]{:S(2)}) collective-permute-start(bf16[64,4096]{1,0:T(8,128)(2,1)S(1)} %step_sum.8), channel_id=1, source_target_pairs={{0,4},{1,3},{4,8},{5,1},{8,12},{9,5},{12,14},{13,9},{14,10},{15,13... | collective-permute-start | bytes 1572872 | tf_op jit(solution)/shard_map/return_long_3/ppermute | solution.py:297
  75.7 3.9 %expert.13 = (bf16[64,4096]{1,0:T(8,128)(2,1)S(1)}, bf16[64,4096]{1,0:T(8,128)(2,1)S(1)}) custom-call(bf16[64,4224]{1,0:T(8,128)(2,1)S(1)} %collective-permute-done.25.refs_0_, bf16[64,4224]{1,0:T(8,128)(2,1)S(1)} %collective-permute-done.14.refs_1_, f32[1,128]{1,0:T(1,128)S(1)} %compare_select_fusion.1.refs_2_.refs_4_, f32[1,1536]{1,0:T(1,128)S(1)} %copy-done.1, ...), custom_call_target="tpu_custom_call" | custom-call | flops 4831838208 | tf_op jit(solution)/shard_map/expert/pallas_call | solution.py:146
  80.4 5.4 %collective-permute-done.27.refs_2_ = bf16[64,4096]{1,0:T(8,128)(2,1)S(1)} collective-permute-done((bf16[64,4096]{1,0:T(8,128)(2,1)S(1)}, bf16[64,4096]{1,0:T(8,128)(2,1)S(1)}, u32[]{:S(2)}, u32[]{:S(2)}) %collective-permute-start.27) | collective-permute-done | bytes 524320 | tf_op jit(solution)/shard_map/return_long_3/ppermute | solution.py:297
  86.0 1.6 %collective-permute-start.28 = (bf16[64,4096]{1,0:T(8,128)(2,1)S(1)}, bf16[64,4096]{1,0:T(8,128)(2,1)S(1)}, u32[]{:S(2)}, u32[]{:S(2)}) collective-permute-start(bf16[64,4096]{1,0:T(8,128)(2,1)S(1)} %step_sum.9), channel_id=1, source_target_pairs={{0,4},{1,3},{4,8},{5,1},{8,12},{9,5},{12,14},{13,9},{14,10},{15,13... | collective-permute-start | bytes 1572872 | tf_op jit(solution)/shard_map/return_long_2/ppermute | solution.py:297
  87.7 1.6 %collective-permute-start.23 = (bf16[32,4096]{1,0:T(8,128)(2,1)S(1)}, bf16[32,4096]{1,0:T(8,128)(2,1)S(1)}, u32[]{:S(2)}, u32[]{:S(2)}) collective-permute-start(bf16[32,4096]{1,0:T(8,128)(2,1)S(1)} %get-tuple-element.74), channel_id=1, source_target_pairs={{0,4},{1,3},{4,8},{5,1},{8,12},{9,5},{12,14},{13,9},{14,10},{15,13... | collective-permute-start | bytes 786440 | tf_op jit(solution)/shard_map/return_short_1/ppermute | solution.py:297
  89.8 8.3 %collective-permute-done.23.refs_0_ = bf16[32,4096]{1,0:T(8,128)(2,1)S(1)} collective-permute-done((bf16[32,4096]{1,0:T(8,128)(2,1)S(1)}, bf16[32,4096]{1,0:T(8,128)(2,1)S(1)}, u32[]{:S(2)}, u32[]{:S(2)}) %collective-permute-start.23) | collective-permute-done | bytes 262176 | tf_op jit(solution)/shard_map/return_short_1/ppermute | solution.py:297
  98.1 1.9 %collective-permute-done.29.refs_3_ = bf16[32,4096]{1,0:T(8,128)(2,1)S(1)} collective-permute-done((bf16[32,4096]{1,0:T(8,128)(2,1)S(1)}, bf16[32,4096]{1,0:T(8,128)(2,1)S(1)}, u32[]{:S(2)}, u32[]{:S(2)}) %collective-permute-start.29) | collective-permute-done | bytes 262176 | tf_op jit(solution)/shard_map/return_short_1/ppermute | solution.py:297
  100.2 2.0 %collective-permute-start.30 = (bf16[32,4096]{1,0:T(8,128)(2,1)S(1)}, bf16[32,4096]{1,0:T(8,128)(2,1)S(1)}, u32[]{:S(2)}, u32[]{:S(2)}) collective-permute-start(bf16[32,4096]{1,0:T(8,128)(2,1)S(1)} %get-tuple-element.81), channel_id=1, source_target_pairs={{0,5},{1,2},{4,9},{5,0},{8,13},{9,4},{12,15},{13,8},{14,11},{15,12... | collective-permute-start | bytes 786440 | tf_op jit(solution)/shard_map/return_long_1/ppermute | solution.py:297
  102.2 1.6 %collective-permute-start.31 = (bf16[32,4096]{1,0:T(8,128)(2,1)S(1)}, bf16[32,4096]{1,0:T(8,128)(2,1)S(1)}, u32[]{:S(2)}, u32[]{:S(2)}) collective-permute-start(bf16[32,4096]{1,0:T(8,128)(2,1)S(1)} %get-tuple-element.82), channel_id=1, source_target_pairs={{0,4},{1,3},{4,8},{5,1},{8,12},{9,5},{12,14},{13,9},{14,10},{15,13... | collective-permute-start | bytes 786440 | tf_op jit(solution)/shard_map/return_long_1/ppermute | solution.py:297
  103.7 2.5 %collective-permute-done.30.refs_1_ = bf16[32,4096]{1,0:T(8,128)(2,1)S(1)} collective-permute-done((bf16[32,4096]{1,0:T(8,128)(2,1)S(1)}, bf16[32,4096]{1,0:T(8,128)(2,1)S(1)}, u32[]{:S(2)}, u32[]{:S(2)}) %collective-permute-start.30) | collective-permute-done | bytes 262176 | tf_op jit(solution)/shard_map/return_long_1/ppermute | solution.py:297
  106.2 3.5 %collective-permute-done.31.refs_2_ = bf16[32,4096]{1,0:T(8,128)(2,1)S(1)} collective-permute-done((bf16[32,4096]{1,0:T(8,128)(2,1)S(1)}, bf16[32,4096]{1,0:T(8,128)(2,1)S(1)}, u32[]{:S(2)}, u32[]{:S(2)}) %collective-permute-start.31) | collective-permute-done | bytes 262176 | tf_op jit(solution)/shard_map/return_long_1/ppermute | solution.py:297
  (55 shorter events, 11.1 us)
Async XLA Ops:
  1.3 10.9 %collective-permute-start = (bf16[64,4224]{1,0:T(8,128)(2,1)S(1)}, bf16[64,4224]{1,0:T(8,128)(2,1)S(1)}, u32[]{:S(2)}, u32[]{:S(2)}) collective-permute-start(bf16[64,4224]{1,0:T(8,128)(2,1)S(1)} %get-tuple-element.44.refs_0_), channel_id=1, source_target_pairs={{0,1},{1,0},{2,3},{3,2},{4,5},{5,4},{6,7},{7,6},{8,9},{9,8},{10,11... | collective-permute-start | bytes 1622024 | tf_op jit(solution)/shard_map/swap_in_0/ppermute | solution.py:297
  1.8 14.3 %collective-permute-start.2 = (bf16[64,4224]{1,0:T(8,128)(2,1)S(1)}, bf16[64,4224]{1,0:T(8,128)(2,1)S(1)}, u32[]{:S(2)}, u32[]{:S(2)}) collective-permute-start(bf16[64,4224]{1,0:T(8,128)(2,1)S(1)} %get-tuple-element.44.refs_0_), channel_id=1, source_target_pairs={{0,4},{1,3},{4,8},{5,1},{8,12},{9,5},{12,14},{13,9},{14,10},{15,13... | collective-permute-start | bytes 1622024 | tf_op jit(solution)/shard_map/gather_long_1/ppermute | solution.py:297
  4.5 13.1 %collective-permute-start.3 = (bf16[64,4224]{1,0:T(8,128)(2,1)S(1)}, bf16[64,4224]{1,0:T(8,128)(2,1)S(1)}, u32[]{:S(2)}, u32[]{:S(2)}) collective-permute-start(bf16[64,4224]{1,0:T(8,128)(2,1)S(1)} %get-tuple-element.50), channel_id=1, source_target_pairs={{0,3},{1,4},{4,1},{5,8},{8,5},{9,12},{12,9},{13,14},{14,13},{15,10... | collective-permute-start | bytes 1622024 | tf_op jit(solution)/shard_map/gather_long_1/ppermute | solution.py:297
  17.6 4.2 %collective-permute-start.4 = (bf16[64,4224]{1,0:T(8,128)(2,1)S(1)}, bf16[64,4224]{1,0:T(8,128)(2,1)S(1)}, u32[]{:S(2)}, u32[]{:S(2)}) collective-permute-start(bf16[64,4224]{1,0:T(8,128)(2,1)S(1)} %get-tuple-element.52.refs_2_), channel_id=1, source_target_pairs={{0,1},{1,0},{2,3},{3,2},{4,5},{5,4},{6,7},{7,6},{8,9},{9,8},{10,11... | collective-permute-start | bytes 1622024 | tf_op jit(solution)/shard_map/swap_in_1/ppermute | solution.py:297
  17.7 4.2 %collective-permute-start.5 = (bf16[64,4224]{1,0:T(8,128)(2,1)S(1)}, bf16[64,4224]{1,0:T(8,128)(2,1)S(1)}, u32[]{:S(2)}, u32[]{:S(2)}) collective-permute-start(bf16[64,4224]{1,0:T(8,128)(2,1)S(1)} %get-tuple-element.54.refs_3_), channel_id=1, source_target_pairs={{0,1},{1,0},{2,3},{3,2},{4,5},{5,4},{6,7},{7,6},{8,9},{9,8},{10,11... | collective-permute-start | bytes 1622024 | tf_op jit(solution)/shard_map/swap_in_1/ppermute | solution.py:297
  18.2 10.1 %collective-permute-start.7 = (bf16[64,4224]{1,0:T(8,128)(2,1)S(1)}, bf16[64,4224]{1,0:T(8,128)(2,1)S(1)}, u32[]{:S(2)}, u32[]{:S(2)}) collective-permute-start(bf16[64,4224]{1,0:T(8,128)(2,1)S(1)} %get-tuple-element.54.refs_3_), channel_id=1, source_target_pairs={{0,4},{1,3},{4,8},{5,1},{8,12},{9,5},{12,14},{13,9},{14,10},{15,13... | collective-permute-start | bytes 1622024 | tf_op jit(solution)/shard_map/gather_short_2/ppermute | solution.py:297
  20.3 13.1 %collective-permute-start.14 = (bf16[64,4224]{1,0:T(8,128)(2,1)S(1)}, bf16[64,4224]{1,0:T(8,128)(2,1)S(1)}, u32[]{:S(2)}, u32[]{:S(2)}) collective-permute-start(bf16[64,4224]{1,0:T(8,128)(2,1)S(1)} %get-tuple-element.52.refs_2_), channel_id=1, source_target_pairs={{0,4},{1,3},{4,8},{5,1},{8,12},{9,5},{12,14},{13,9},{14,10},{15,13... | collective-permute-start | bytes 1622024 | tf_op jit(solution)/shard_map/gather_long_2/ppermute | solution.py:297
  28.3 7.1 %collective-permute-start.8 = (bf16[64,4224]{1,0:T(8,128)(2,1)S(1)}, bf16[64,4224]{1,0:T(8,128)(2,1)S(1)}, u32[]{:S(2)}, u32[]{:S(2)}) collective-permute-start(bf16[64,4224]{1,0:T(8,128)(2,1)S(1)} %collective-permute-done.7.refs_1_), channel_id=1, source_target_pairs={{0,1},{1,0},{2,3},{3,2},{4,5},{5,4},{6,7},{7,6},{8,9},{9,8},{10,11... | collective-permute-start | bytes 1622024 | tf_op jit(solution)/shard_map/swap_in_2/ppermute | solution.py:297
  28.4 11.0 %collective-permute-start.10 = (bf16[64,4224]{1,0:T(8,128)(2,1)S(1)}, bf16[64,4224]{1,0:T(8,128)(2,1)S(1)}, u32[]{:S(2)}, u32[]{:S(2)}) collective-permute-start(bf16[64,4224]{1,0:T(8,128)(2,1)S(1)} %collective-permute-done.7.refs_1_), channel_id=1, source_target_pairs={{0,4},{1,3},{4,8},{5,1},{8,12},{9,5},{12,14},{13,9},{14,10},{15,13... | collective-permute-start | bytes 1622024 | tf_op jit(solution)/shard_map/gather_short_3/ppermute | solution.py:297
  33.3 11.6 %collective-permute-start.15 = (bf16[64,4224]{1,0:T(8,128)(2,1)S(1)}, bf16[64,4224]{1,0:T(8,128)(2,1)S(1)}, u32[]{:S(2)}, u32[]{:S(2)}) collective-permute-start(bf16[64,4224]{1,0:T(8,128)(2,1)S(1)} %collective-permute-done.14.refs_1_), channel_id=1, source_target_pairs={{0,4},{1,3},{4,8},{5,1},{8,12},{9,5},{12,14},{13,9},{14,10},{15,13... | collective-permute-start | bytes 1622024 | tf_op jit(solution)/shard_map/gather_long_3/ppermute | solution.py:297
  39.4 7.6 %collective-permute-start.11 = (bf16[64,4224]{1,0:T(8,128)(2,1)S(1)}, bf16[64,4224]{1,0:T(8,128)(2,1)S(1)}, u32[]{:S(2)}, u32[]{:S(2)}) collective-permute-start(bf16[64,4224]{1,0:T(8,128)(2,1)S(1)} %collective-permute-done.10.refs_1_), channel_id=1, source_target_pairs={{0,1},{1,0},{2,3},{3,2},{4,5},{5,4},{6,7},{7,6},{8,9},{9,8},{10,11... | collective-permute-start | bytes 1622024 | tf_op jit(solution)/shard_map/swap_in_3/ppermute | solution.py:297
  44.9 9.4 %collective-permute-start.16 = (bf16[64,4224]{1,0:T(8,128)(2,1)S(1)}, bf16[64,4224]{1,0:T(8,128)(2,1)S(1)}, u32[]{:S(2)}, u32[]{:S(2)}) collective-permute-start(bf16[64,4224]{1,0:T(8,128)(2,1)S(1)} %collective-permute-done.15.refs_1_), channel_id=1, source_target_pairs={{0,4},{1,3},{4,8},{5,1},{8,12},{9,5},{12,14},{13,9},{14,10},{15,13... | collective-permute-start | bytes 1622024 | tf_op jit(solution)/shard_map/gather_long_4/ppermute | solution.py:297
  51.0 2.0 %collective-permute-start.12 = (bf16[64,4096]{1,0:T(8,128)(2,1)S(1)}, bf16[64,4096]{1,0:T(8,128)(2,1)S(1)}, u32[]{:S(2)}, u32[]{:S(2)}) collective-permute-start(bf16[64,4096]{1,0:T(8,128)(2,1)S(1)} %get-tuple-element.63), channel_id=1, source_target_pairs={{0,1},{1,0},{2,3},{3,2},{4,5},{5,4},{6,7},{7,6},{8,9},{9,8},{10,11... | collective-permute-start | bytes 1572872 | tf_op jit(solution)/shard_map/swap_out_3/ppermute | solution.py:297
  54.3 2.6 %collective-permute-start.17 = (bf16[64,4224]{1,0:T(8,128)(2,1)S(1)}, bf16[64,4224]{1,0:T(8,128)(2,1)S(1)}, u32[]{:S(2)}, u32[]{:S(2)}) collective-permute-start(bf16[64,4224]{1,0:T(8,128)(2,1)S(1)} %collective-permute-done.16.refs_1_), channel_id=1, source_target_pairs={{0,1},{1,0},{2,3},{3,2},{4,5},{5,4},{6,7},{7,6},{8,9},{9,8},{10,11... | collective-permute-start | bytes 1622024 | tf_op jit(solution)/shard_map/swap_in_4/ppermute | solution.py:297
  54.3 12.0 %collective-permute-start.20 = (bf16[64,4224]{1,0:T(8,128)(2,1)S(1)}, bf16[64,4224]{1,0:T(8,128)(2,1)S(1)}, u32[]{:S(2)}, u32[]{:S(2)}) collective-permute-start(bf16[64,4224]{1,0:T(8,128)(2,1)S(1)} %collective-permute-done.15.refs_1_), channel_id=1, source_target_pairs={{0,1},{1,0},{2,3},{3,2},{4,5},{5,4},{6,7},{7,6},{8,9},{9,8},{10,11... | collective-permute-start | bytes 1622024 | tf_op jit(solution)/shard_map/swap_in_3/ppermute | solution.py:297
  54.8 9.2 %collective-permute-start.13 = (bf16[64,4096]{1,0:T(8,128)(2,1)S(1)}, bf16[64,4096]{1,0:T(8,128)(2,1)S(1)}, u32[]{:S(2)}, u32[]{:S(2)}) collective-permute-start(bf16[64,4096]{1,0:T(8,128)(2,1)S(1)} %step_sum.5), channel_id=1, source_target_pairs={{0,4},{1,3},{4,8},{5,1},{8,12},{9,5},{12,14},{13,9},{14,10},{15,13... | collective-permute-start | bytes 1572872 | tf_op jit(solution)/shard_map/return_short_3/ppermute | solution.py:297
  60.8 3.1 %collective-permute-start.18 = (bf16[64,4096]{1,0:T(8,128)(2,1)S(1)}, bf16[64,4096]{1,0:T(8,128)(2,1)S(1)}, u32[]{:S(2)}, u32[]{:S(2)}) collective-permute-start(bf16[64,4096]{1,0:T(8,128)(2,1)S(1)} %get-tuple-element.67), channel_id=1, source_target_pairs={{0,1},{1,0},{2,3},{3,2},{4,5},{5,4},{6,7},{7,6},{8,9},{9,8},{10,11... | collective-permute-start | bytes 1572872 | tf_op jit(solution)/shard_map/swap_out_4/ppermute | solution.py:297
  60.9 14.8 %collective-permute-start.25 = (bf16[64,4224]{1,0:T(8,128)(2,1)S(1)}, bf16[64,4224]{1,0:T(8,128)(2,1)S(1)}, u32[]{:S(2)}, u32[]{:S(2)}) collective-permute-start(bf16[64,4224]{1,0:T(8,128)(2,1)S(1)} %collective-permute-done.14.refs_1_), channel_id=1, source_target_pairs={{0,1},{1,0},{2,3},{3,2},{4,5},{5,4},{6,7},{7,6},{8,9},{9,8},{10,11... | collective-permute-start | bytes 1622024 | tf_op jit(solution)/shard_map/swap_in_2/ppermute | solution.py:297
  61.4 9.4 %collective-permute-start.9 = (bf16[64,4096]{1,0:T(8,128)(2,1)S(1)}, bf16[64,4096]{1,0:T(8,128)(2,1)S(1)}, u32[]{:S(2)}, u32[]{:S(2)}) collective-permute-start(bf16[64,4096]{1,0:T(8,128)(2,1)S(1)} %get-tuple-element.60), channel_id=1, source_target_pairs={{0,1},{1,0},{2,3},{3,2},{4,5},{5,4},{6,7},{7,6},{8,9},{9,8},{10,11... | collective-permute-start | bytes 1572872 | tf_op jit(solution)/shard_map/swap_out_2/ppermute | solution.py:297
  64.1 9.2 %collective-permute-start.22 = (bf16[64,4096]{1,0:T(8,128)(2,1)S(1)}, bf16[64,4096]{1,0:T(8,128)(2,1)S(1)}, u32[]{:S(2)}, u32[]{:S(2)}) collective-permute-start(bf16[64,4096]{1,0:T(8,128)(2,1)S(1)} %step_sum.6), channel_id=1, source_target_pairs={{0,4},{1,3},{4,8},{5,1},{8,12},{9,5},{12,14},{13,9},{14,10},{15,13... | collective-permute-start | bytes 1572872 | tf_op jit(solution)/shard_map/return_long_4/ppermute | solution.py:297
  70.2 3.2 %collective-permute-start.21 = (bf16[64,4096]{1,0:T(8,128)(2,1)S(1)}, bf16[64,4096]{1,0:T(8,128)(2,1)S(1)}, u32[]{:S(2)}, u32[]{:S(2)}) collective-permute-start(bf16[64,4096]{1,0:T(8,128)(2,1)S(1)} %get-tuple-element.71), channel_id=1, source_target_pairs={{0,1},{1,0},{2,3},{3,2},{4,5},{5,4},{6,7},{7,6},{8,9},{9,8},{10,11... | collective-permute-start | bytes 1572872 | tf_op jit(solution)/shard_map/swap_out_3/ppermute | solution.py:297
  70.3 9.9 %collective-permute-start.6 = (bf16[64,4096]{1,0:T(8,128)(2,1)S(1)}, bf16[64,4096]{1,0:T(8,128)(2,1)S(1)}, u32[]{:S(2)}, u32[]{:S(2)}) collective-permute-start(bf16[64,4096]{1,0:T(8,128)(2,1)S(1)} %get-tuple-element.56), channel_id=1, source_target_pairs={{0,1},{1,0},{2,3},{3,2},{4,5},{5,4},{6,7},{7,6},{8,9},{9,8},{10,11... | collective-permute-start | bytes 1572872 | tf_op jit(solution)/shard_map/swap_out_1/ppermute | solution.py:297
  71.0 9.2 %collective-permute-start.19 = (bf16[64,4096]{1,0:T(8,128)(2,1)S(1)}, bf16[64,4096]{1,0:T(8,128)(2,1)S(1)}, u32[]{:S(2)}, u32[]{:S(2)}) collective-permute-start(bf16[64,4096]{1,0:T(8,128)(2,1)S(1)} %step_sum.7), channel_id=1, source_target_pairs={{0,4},{1,3},{4,8},{5,1},{8,12},{9,5},{12,14},{13,9},{14,10},{15,13... | collective-permute-start | bytes 1572872 | tf_op jit(solution)/shard_map/return_short_2/ppermute | solution.py:297
  73.6 12.3 %collective-permute-start.27 = (bf16[64,4096]{1,0:T(8,128)(2,1)S(1)}, bf16[64,4096]{1,0:T(8,128)(2,1)S(1)}, u32[]{:S(2)}, u32[]{:S(2)}) collective-permute-start(bf16[64,4096]{1,0:T(8,128)(2,1)S(1)} %step_sum.8), channel_id=1, source_target_pairs={{0,4},{1,3},{4,8},{5,1},{8,12},{9,5},{12,14},{13,9},{14,10},{15,13... | collective-permute-start | bytes 1572872 | tf_op jit(solution)/shard_map/return_long_3/ppermute | solution.py:297
  79.6 6.2 %collective-permute-start.26 = (bf16[64,4096]{1,0:T(8,128)(2,1)S(1)}, bf16[64,4096]{1,0:T(8,128)(2,1)S(1)}, u32[]{:S(2)}, u32[]{:S(2)}) collective-permute-start(bf16[64,4096]{1,0:T(8,128)(2,1)S(1)} %get-tuple-element.77), channel_id=1, source_target_pairs={{0,1},{1,0},{2,3},{3,2},{4,5},{5,4},{6,7},{7,6},{8,9},{9,8},{10,11... | collective-permute-start | bytes 1572872 | tf_op jit(solution)/shard_map/swap_out_2/ppermute | solution.py:297
  86.0 14.0 %collective-permute-start.28 = (bf16[64,4096]{1,0:T(8,128)(2,1)S(1)}, bf16[64,4096]{1,0:T(8,128)(2,1)S(1)}, u32[]{:S(2)}, u32[]{:S(2)}) collective-permute-start(bf16[64,4096]{1,0:T(8,128)(2,1)S(1)} %step_sum.9), channel_id=1, source_target_pairs={{0,4},{1,3},{4,8},{5,1},{8,12},{9,5},{12,14},{13,9},{14,10},{15,13... | collective-permute-start | bytes 1572872 | tf_op jit(solution)/shard_map/return_long_2/ppermute | solution.py:297
  87.7 12.3 %collective-permute-start.24 = (bf16[64,4096]{1,0:T(8,128)(2,1)S(1)}, bf16[64,4096]{1,0:T(8,128)(2,1)S(1)}, u32[]{:S(2)}, u32[]{:S(2)}) collective-permute-start(bf16[64,4096]{1,0:T(8,128)(2,1)S(1)} %get-tuple-element.75), channel_id=1, source_target_pairs={{0,1},{1,0},{2,3},{3,2},{4,5},{5,4},{6,7},{7,6},{8,9},{9,8},{10,11... | collective-permute-start | bytes 1572872 | tf_op jit(solution)/shard_map/swap_out_1/ppermute | solution.py:297
  87.7 10.4 %collective-permute-start.23 = (bf16[32,4096]{1,0:T(8,128)(2,1)S(1)}, bf16[32,4096]{1,0:T(8,128)(2,1)S(1)}, u32[]{:S(2)}, u32[]{:S(2)}) collective-permute-start(bf16[32,4096]{1,0:T(8,128)(2,1)S(1)} %get-tuple-element.74), channel_id=1, source_target_pairs={{0,4},{1,3},{4,8},{5,1},{8,12},{9,5},{12,14},{13,9},{14,10},{15,13... | collective-permute-start | bytes 786440 | tf_op jit(solution)/shard_map/return_short_1/ppermute | solution.py:297
  89.3 10.7 %collective-permute-start.29 = (bf16[32,4096]{1,0:T(8,128)(2,1)S(1)}, bf16[32,4096]{1,0:T(8,128)(2,1)S(1)}, u32[]{:S(2)}, u32[]{:S(2)}) collective-permute-start(bf16[32,4096]{1,0:T(8,128)(2,1)S(1)} %get-tuple-element.78), channel_id=1, source_target_pairs={{0,5},{1,2},{4,9},{5,0},{8,13},{9,4},{12,15},{13,8},{14,11},{15,12... | collective-permute-start | bytes 786440 | tf_op jit(solution)/shard_map/return_short_1/ppermute | solution.py:297
  89.5 14.2 %collective-permute-start.1 = (bf16[64,4096]{1,0:T(8,128)(2,1)S(1)}, bf16[64,4096]{1,0:T(8,128)(2,1)S(1)}, u32[]{:S(2)}, u32[]{:S(2)}) collective-permute-start(bf16[64,4096]{1,0:T(8,128)(2,1)S(1)} %get-tuple-element.48), channel_id=1, source_target_pairs={{0,1},{1,0},{2,3},{3,2},{4,5},{5,4},{6,7},{7,6},{8,9},{9,8},{10,11... | collective-permute-start | bytes 1572872 | tf_op jit(solution)/shard_map/swap_out_0/ppermute | solution.py:297
  100.2 6.0 %collective-permute-start.30 = (bf16[32,4096]{1,0:T(8,128)(2,1)S(1)}, bf16[32,4096]{1,0:T(8,128)(2,1)S(1)}, u32[]{:S(2)}, u32[]{:S(2)}) collective-permute-start(bf16[32,4096]{1,0:T(8,128)(2,1)S(1)} %get-tuple-element.81), channel_id=1, source_target_pairs={{0,5},{1,2},{4,9},{5,0},{8,13},{9,4},{12,15},{13,8},{14,11},{15,12... | collective-permute-start | bytes 786440 | tf_op jit(solution)/shard_map/return_long_1/ppermute | solution.py:297
  102.2 7.6 %collective-permute-start.31 = (bf16[32,4096]{1,0:T(8,128)(2,1)S(1)}, bf16[32,4096]{1,0:T(8,128)(2,1)S(1)}, u32[]{:S(2)}, u32[]{:S(2)}) collective-permute-start(bf16[32,4096]{1,0:T(8,128)(2,1)S(1)} %get-tuple-element.82), channel_id=1, source_target_pairs={{0,4},{1,3},{4,8},{5,1},{8,12},{9,5},{12,14},{13,9},{14,10},{15,13... | collective-permute-start | bytes 786440 | tf_op jit(solution)/shard_map/return_long_1/ppermute | solution.py:297
  (2 other events, 24.3 us)

commit v12 on v11

--- a/solution.py
+++ b/solution.py
@@ -339,16 +339,16 @@
         totals = split_sum(*terms)
         return [send(x, perm, f"return_{name}_1") for x, perm in zip(totals, (back_to_other, on))], totals
 
-    if reach > 3:
-        last = run([(reach - 2, "short")], last)
-    run([(reach - 1, "short")], last)
+    for distance in range(2, reach - 1):
+        last = run([(distance, "short")], last)
+    run([(reach - 1, "short"), (reach - 1, "long")], last)
     short, totals = step(reach - 1, "short", ())
     run([(reach, "long")], totals, 2)
     given[reach, "long"] = after(given[reach, "long"], *short)
     long, totals = step(reach, "long", ())
     for distance in range(reach - 1, 0, -1):
-        if distance > 1:
-            run([(distance, "long")] + [(distance - 2, "short")] * (distance > 3), [], 2)
+        if 1 < distance < reach - 1:
+            run([(distance, "long")], [])
         if distance > 2:
             short, totals = step(distance - 1, "short", [after(x, *totals) for x in short])
         elif distance == 2:
@@ -356,7 +356,7 @@
         if distance > 1:
             long, totals = step(distance, "long", [after(x, *totals) for x in long])
         else:
-            long, totals = arrive("long", [after(x, *short) for x in long])
+            long, totals = arrive("long", long)
     short_cross, short_same = short
     long_cross, long_same = long
     return last_sum(core, kept[0], given[0], short_same, long_cross, long_same, short_cross)

time: 111 us -> 107 us (0.964)
  starting transfers between devices: 31.8 us -> 30 us
  Pallas kernels: 40.1 us -> 38.7 us
    ppermute x32, starting transfers between devices: 31.8 us -> 30 us  [send(): return lax.ppermute(x, 'expert', perm)]
    pallas_call x7 -> x6, Pallas kernels: 30.1 us -> 28.6 us  [expert_part(): pl.pallas_call(functools.partial(expert_kernel, len(blocks)), in_specs=[V...]
  transfers between devices with their start and end apart: 32 -> 32, of which waited for: 13 -> 12; matrix products, arithmetic and copies ran while one was open for 0% -> 0% of each run, Pallas kernels for 34% -> 34%
where the time goes in v12:
time: 107 us
  Pallas kernels  38.7 us (36%)
  waiting for transfers between devices  38.4 us (36%)
  starting transfers between devices  30 us (28%)
    ppermute x32, waiting for transfers between devices, send(): return lax.ppermute(x, 'expert', perm)  38.4 us
    ppermute x32, starting transfers between devices, send(): return lax.ppermute(x, 'expert', perm)  30 us
    pallas_call x6, Pallas kernels, expert_part(): pl.pallas_call(functools.partial(expert_kernel, len(blocks)), in_specs=[V...  28.6 us
    pallas_call x1, Pallas kernels, keep(): pl.pallas_call(keep_kernel, in_specs=[ANYWHERE] * 2, out_specs=[VMEM] * 2...  6.38 us
  transfers between devices with their start and end apart: 32, of which 12 were waited for; matrix products, arithmetic and copies ran while one was open for 0% of the time, Pallas kernels for 34%

profile of v12, /device:TPU:0, one launch (start us, length us, event | category | flops | bytes accessed | tf_op | source)
XLA Modules:
  0.0 107.3 jit_solution(12396936871012052045)
XLA Ops:
  0.0 1.3 %pack.1 = (bf16[64,4224]{1,0:T(8,128)(2,1)S(1)}, bf16[64,4224]{1,0:T(8,128)(2,1)S(1)}) custom-call(s32[1]{0:T(128)} %bitcast.core, bf16[64,4096]{1,0:T(8,128)(2,1)} %tokens.1, s32[8,64]{1,0:T(8,128)} %bitcast.7, s32[8,64]{1,0:T(8,128)} %bitcast.8), custom_call_target="tpu_custom_call" | custom-call | tf_op jit(solution)/shard_map/pack/pallas_call | solution.py:64
  1.8 2.6 %collective-permute-start.2 = (bf16[64,4224]{1,0:T(8,128)(2,1)S(1)}, bf16[64,4224]{1,0:T(8,128)(2,1)S(1)}, u32[]{:S(2)}, u32[]{:S(2)}) collective-permute-start(bf16[64,4224]{1,0:T(8,128)(2,1)S(1)} %get-tuple-element.44.refs_0_), channel_id=1, source_target_pairs={{0,4},{1,3},{4,8},{5,1},{8,12},{9,5},{12,14},{13,9},{14,10},{15,13... | collective-permute-start | bytes 1622024 | tf_op jit(solution)/shard_map/gather_long_1/ppermute | solution.py:297
  5.7 6.4 %keep.1 = (bf16[4096,1536]{1,0:T(8,128)(2,1)S(1)}, bf16[768,4096]{1,0:T(8,128)(2,1)S(1)}) custom-call(bf16[4096,1536]{1,0:T(8,128)(2,1)} %bitcast.5, bf16[768,4096]{1,0:T(8,128)(2,1)} %bitcast.6), custom_call_target="tpu_custom_call" | custom-call | bytes 18874368 | tf_op jit(solution)/shard_map/keep/pallas_call | solution.py:88
  12.2 4.0 %expert.6 = (bf16[64,4096]{1,0:T(8,128)(2,1)S(1)}, bf16[64,4096]{1,0:T(8,128)(2,1)S(1)}) custom-call(bf16[64,4224]{1,0:T(8,128)(2,1)S(1)} %get-tuple-element.44.refs_0_, bf16[64,4224]{1,0:T(8,128)(2,1)S(1)} %collective-permute-done.refs_1_, f32[1,128]{1,0:T(1,128)S(1)} %compare_select_fusion.1.refs_2_.refs_4_, f32[1,1536]{1,0:T(1,128)S(1)} %copy-done.1, ...), custom_call_target="tpu_custom_call" | custom-call | flops 4831838208 | tf_op jit(solution)/shard_map/expert/pallas_call | solution.py:146
  16.2 1.4 %collective-permute-done.3.cross = bf16[64,4224]{1,0:T(8,128)(2,1)S(1)} collective-permute-done((bf16[64,4224]{1,0:T(8,128)(2,1)S(1)}, bf16[64,4224]{1,0:T(8,128)(2,1)S(1)}, u32[]{:S(2)}, u32[]{:S(2)}) %collective-permute-start.3) | collective-permute-done | bytes 540704 | tf_op jit(solution)/shard_map/gather_long_1/ppermute | solution.py:297
  18.2 2.1 %collective-permute-start.7 = (bf16[64,4224]{1,0:T(8,128)(2,1)S(1)}, bf16[64,4224]{1,0:T(8,128)(2,1)S(1)}, u32[]{:S(2)}, u32[]{:S(2)}) collective-permute-start(bf16[64,4224]{1,0:T(8,128)(2,1)S(1)} %get-tuple-element.54.refs_3_), channel_id=1, source_target_pairs={{0,4},{1,3},{4,8},{5,1},{8,12},{9,5},{12,14},{13,9},{14,10},{15,13... | collective-permute-start | bytes 1622024 | tf_op jit(solution)/shard_map/gather_short_2/ppermute | solution.py:297
  20.3 1.6 %collective-permute-start.12 = (bf16[64,4224]{1,0:T(8,128)(2,1)S(1)}, bf16[64,4224]{1,0:T(8,128)(2,1)S(1)}, u32[]{:S(2)}, u32[]{:S(2)}) collective-permute-start(bf16[64,4224]{1,0:T(8,128)(2,1)S(1)} %get-tuple-element.52.refs_2_), channel_id=1, source_target_pairs={{0,4},{1,3},{4,8},{5,1},{8,12},{9,5},{12,14},{13,9},{14,10},{15,13... | collective-permute-start | bytes 1622024 | tf_op jit(solution)/shard_map/gather_long_2/ppermute | solution.py:297
  21.8 6.4 %expert.7 = (bf16[64,4096]{1,0:T(8,128)(2,1)S(1)}, bf16[64,4096]{1,0:T(8,128)(2,1)S(1)}, bf16[64,4096]{1,0:T(8,128)(2,1)S(1)}, bf16[64,4096]{1,0:T(8,128)(2,1)S(1)}) custom-call(bf16[64,4224]{1,0:T(8,128)(2,1)S(1)} %collective-permute-done.4.refs_0_, bf16[64,4224]{1,0:T(8,128)(2,1)S(1)} %collective-permute-done.5.refs_1_, ...), custom_call_target="tpu_custom_call" | custom-call | flops 9663676416 | tf_op jit(solution)/shard_map/expert/pallas_call | solution.py:146
  28.4 1.6 %collective-permute-start.10 = (bf16[64,4224]{1,0:T(8,128)(2,1)S(1)}, bf16[64,4224]{1,0:T(8,128)(2,1)S(1)}, u32[]{:S(2)}, u32[]{:S(2)}) collective-permute-start(bf16[64,4224]{1,0:T(8,128)(2,1)S(1)} %collective-permute-done.7.refs_1_), channel_id=1, source_target_pairs={{0,4},{1,3},{4,8},{5,1},{8,12},{9,5},{12,14},{13,9},{14,10},{15,13... | collective-permute-start | bytes 1622024 | tf_op jit(solution)/shard_map/gather_short_3/ppermute | solution.py:297
  30.0 3.3 %collective-permute-done.12.refs_1_ = bf16[64,4224]{1,0:T(8,128)(2,1)S(1)} collective-permute-done((bf16[64,4224]{1,0:T(8,128)(2,1)S(1)}, bf16[64,4224]{1,0:T(8,128)(2,1)S(1)}, u32[]{:S(2)}, u32[]{:S(2)}) %collective-permute-start.12) | collective-permute-done | bytes 540704 | tf_op jit(solution)/shard_map/gather_long_2/ppermute | solution.py:297
  33.3 2.1 %collective-permute-start.13 = (bf16[64,4224]{1,0:T(8,128)(2,1)S(1)}, bf16[64,4224]{1,0:T(8,128)(2,1)S(1)}, u32[]{:S(2)}, u32[]{:S(2)}) collective-permute-start(bf16[64,4224]{1,0:T(8,128)(2,1)S(1)} %collective-permute-done.12.refs_1_), channel_id=1, source_target_pairs={{0,4},{1,3},{4,8},{5,1},{8,12},{9,5},{12,14},{13,9},{14,10},{15,13... | collective-permute-start | bytes 1622024 | tf_op jit(solution)/shard_map/gather_long_3/ppermute | solution.py:297
  35.4 3.9 %expert.8 = (bf16[64,4096]{1,0:T(8,128)(2,1)S(1)}, bf16[64,4096]{1,0:T(8,128)(2,1)S(1)}) custom-call(bf16[64,4224]{1,0:T(8,128)(2,1)S(1)} %collective-permute-done.8.refs_0_, bf16[64,4224]{1,0:T(8,128)(2,1)S(1)} %collective-permute-done.7.refs_1_, f32[1,128]{1,0:T(1,128)S(1)} %compare_select_fusion.1.refs_2_.refs_4_, f32[1,1536]{1,0:T(1,128)S(1)} %copy-done.1, ...), custom_call_target="tpu_custom_call" | custom-call | flops 4831838208 | tf_op jit(solution)/shard_map/expert/pallas_call | solution.py:146
  39.5 5.5 %collective-permute-done.13.refs_3_ = bf16[64,4224]{1,0:T(8,128)(2,1)S(1)} collective-permute-done((bf16[64,4224]{1,0:T(8,128)(2,1)S(1)}, bf16[64,4224]{1,0:T(8,128)(2,1)S(1)}, u32[]{:S(2)}, u32[]{:S(2)}) %collective-permute-start.13) | collective-permute-done | bytes 540704 | tf_op jit(solution)/shard_map/gather_long_3/ppermute | solution.py:297
  44.9 2.1 %collective-permute-start.17 = (bf16[64,4224]{1,0:T(8,128)(2,1)S(1)}, bf16[64,4224]{1,0:T(8,128)(2,1)S(1)}, u32[]{:S(2)}, u32[]{:S(2)}) collective-permute-start(bf16[64,4224]{1,0:T(8,128)(2,1)S(1)} %collective-permute-done.13.refs_3_), channel_id=1, source_target_pairs={{0,4},{1,3},{4,8},{5,1},{8,12},{9,5},{12,14},{13,9},{14,10},{15,13... | collective-permute-start | bytes 1622024 | tf_op jit(solution)/shard_map/gather_long_4/ppermute | solution.py:297
  47.0 6.4 %expert.9 = (bf16[64,4096]{1,0:T(8,128)(2,1)S(1)}, bf16[64,4096]{1,0:T(8,128)(2,1)S(1)}, bf16[64,4096]{1,0:T(8,128)(2,1)S(1)}, bf16[64,4096]{1,0:T(8,128)(2,1)S(1)}) custom-call(bf16[64,4224]{1,0:T(8,128)(2,1)S(1)} %collective-permute-done.11.refs_0_, bf16[64,4224]{1,0:T(8,128)(2,1)S(1)} %collective-permute-done.14.refs_1_, ...), custom_call_target="tpu_custom_call" | custom-call | flops 9663676416 | tf_op jit(solution)/shard_map/expert/pallas_call | solution.py:146
  53.7 1.7 %collective-permute-done.15.refs_1_ = bf16[64,4096]{1,0:T(8,128)(2,1)S(1)} collective-permute-done((bf16[64,4096]{1,0:T(8,128)(2,1)S(1)}, bf16[64,4096]{1,0:T(8,128)(2,1)S(1)}, u32[]{:S(2)}, u32[]{:S(2)}) %collective-permute-start.15) | collective-permute-done | bytes 524320 | tf_op jit(solution)/shard_map/swap_out_3/ppermute | solution.py:297
  55.8 1.9 %collective-permute-start.16 = (bf16[64,4096]{1,0:T(8,128)(2,1)S(1)}, bf16[64,4096]{1,0:T(8,128)(2,1)S(1)}, u32[]{:S(2)}, u32[]{:S(2)}) collective-permute-start(bf16[64,4096]{1,0:T(8,128)(2,1)S(1)} %step_sum.5), channel_id=1, source_target_pairs={{0,4},{1,3},{4,8},{5,1},{8,12},{9,5},{12,14},{13,9},{14,10},{15,13... | collective-permute-start | bytes 1572872 | tf_op jit(solution)/shard_map/return_short_3/ppermute | solution.py:297
  57.7 4.0 %expert.10 = (bf16[64,4096]{1,0:T(8,128)(2,1)S(1)}, bf16[64,4096]{1,0:T(8,128)(2,1)S(1)}) custom-call(bf16[64,4224]{1,0:T(8,128)(2,1)S(1)} %collective-permute-done.18.refs_0_, bf16[64,4224]{1,0:T(8,128)(2,1)S(1)} %collective-permute-done.17.refs_1_, f32[1,128]{1,0:T(1,128)S(1)} %compare_select_fusion.1.refs_2_.refs_4_, f32[1,1536]{1,0:T(1,128)S(1)} %copy-done.1, ...), custom_call_target="tpu_custom_call" | custom-call | flops 4831838208 | tf_op jit(solution)/shard_map/expert/pallas_call | solution.py:146
  62.3 2.7 %collective-permute-done.16.refs_2_ = bf16[64,4096]{1,0:T(8,128)(2,1)S(1)} collective-permute-done((bf16[64,4096]{1,0:T(8,128)(2,1)S(1)}, bf16[64,4096]{1,0:T(8,128)(2,1)S(1)}, u32[]{:S(2)}, u32[]{:S(2)}) %collective-permute-start.16) | collective-permute-done | bytes 524320 | tf_op jit(solution)/shard_map/return_short_3/ppermute | solution.py:297
  65.1 1.9 %collective-permute-start.22 = (bf16[64,4096]{1,0:T(8,128)(2,1)S(1)}, bf16[64,4096]{1,0:T(8,128)(2,1)S(1)}, u32[]{:S(2)}, u32[]{:S(2)}) collective-permute-start(bf16[64,4096]{1,0:T(8,128)(2,1)S(1)} %step_sum.6), channel_id=1, source_target_pairs={{0,4},{1,3},{4,8},{5,1},{8,12},{9,5},{12,14},{13,9},{14,10},{15,13... | collective-permute-start | bytes 1572872 | tf_op jit(solution)/shard_map/return_long_4/ppermute | solution.py:297
  67.8 1.6 %collective-permute-start.20 = (bf16[64,4096]{1,0:T(8,128)(2,1)S(1)}, bf16[64,4096]{1,0:T(8,128)(2,1)S(1)}, u32[]{:S(2)}, u32[]{:S(2)}) collective-permute-start(bf16[64,4096]{1,0:T(8,128)(2,1)S(1)} %step_sum.7), channel_id=1, source_target_pairs={{0,4},{1,3},{4,8},{5,1},{8,12},{9,5},{12,14},{13,9},{14,10},{15,13... | collective-permute-start | bytes 1572872 | tf_op jit(solution)/shard_map/return_short_2/ppermute | solution.py:297
  69.4 4.9 %collective-permute-done.22.refs_2_ = bf16[64,4096]{1,0:T(8,128)(2,1)S(1)} collective-permute-done((bf16[64,4096]{1,0:T(8,128)(2,1)S(1)}, bf16[64,4096]{1,0:T(8,128)(2,1)S(1)}, u32[]{:S(2)}, u32[]{:S(2)}) %collective-permute-start.22) | collective-permute-done | bytes 524320 | tf_op jit(solution)/shard_map/return_long_4/ppermute | solution.py:297
  74.6 1.9 %collective-permute-start.27 = (bf16[64,4096]{1,0:T(8,128)(2,1)S(1)}, bf16[64,4096]{1,0:T(8,128)(2,1)S(1)}, u32[]{:S(2)}, u32[]{:S(2)}) collective-permute-start(bf16[64,4096]{1,0:T(8,128)(2,1)S(1)} %step_sum.8), channel_id=1, source_target_pairs={{0,4},{1,3},{4,8},{5,1},{8,12},{9,5},{12,14},{13,9},{14,10},{15,13... | collective-permute-start | bytes 1572872 | tf_op jit(solution)/shard_map/return_long_3/ppermute | solution.py:297
  76.5 3.9 %expert.11 = (bf16[64,4096]{1,0:T(8,128)(2,1)S(1)}, bf16[64,4096]{1,0:T(8,128)(2,1)S(1)}) custom-call(bf16[64,4224]{1,0:T(8,128)(2,1)S(1)} %collective-permute-done.25.refs_0_, bf16[64,4224]{1,0:T(8,128)(2,1)S(1)} %collective-permute-done.12.refs_1_, f32[1,128]{1,0:T(1,128)S(1)} %compare_select_fusion.1.refs_2_.refs_4_, f32[1,1536]{1,0:T(1,128)S(1)} %copy-done.1, ...), custom_call_target="tpu_custom_call" | custom-call | flops 4831838208 | tf_op jit(solution)/shard_map/expert/pallas_call | solution.py:146
  81.2 4.3 %collective-permute-done.27.refs_2_ = bf16[64,4096]{1,0:T(8,128)(2,1)S(1)} collective-permute-done((bf16[64,4096]{1,0:T(8,128)(2,1)S(1)}, bf16[64,4096]{1,0:T(8,128)(2,1)S(1)}, u32[]{:S(2)}, u32[]{:S(2)}) %collective-permute-start.27) | collective-permute-done | bytes 524320 | tf_op jit(solution)/shard_map/return_long_3/ppermute | solution.py:297
  85.8 1.9 %collective-permute-start.28 = (bf16[64,4096]{1,0:T(8,128)(2,1)S(1)}, bf16[64,4096]{1,0:T(8,128)(2,1)S(1)}, u32[]{:S(2)}, u32[]{:S(2)}) collective-permute-start(bf16[64,4096]{1,0:T(8,128)(2,1)S(1)} %step_sum.9), channel_id=1, source_target_pairs={{0,4},{1,3},{4,8},{5,1},{8,12},{9,5},{12,14},{13,9},{14,10},{15,13... | collective-permute-start | bytes 1572872 | tf_op jit(solution)/shard_map/return_long_2/ppermute | solution.py:297
  87.7 1.6 %collective-permute-start.23 = (bf16[32,4096]{1,0:T(8,128)(2,1)S(1)}, bf16[32,4096]{1,0:T(8,128)(2,1)S(1)}, u32[]{:S(2)}, u32[]{:S(2)}) collective-permute-start(bf16[32,4096]{1,0:T(8,128)(2,1)S(1)} %get-tuple-element.75), channel_id=1, source_target_pairs={{0,4},{1,3},{4,8},{5,1},{8,12},{9,5},{12,14},{13,9},{14,10},{15,13... | collective-permute-start | bytes 786440 | tf_op jit(solution)/shard_map/return_short_1/ppermute | solution.py:297
  89.6 5.4 %collective-permute-done.28.refs_2_ = bf16[64,4096]{1,0:T(8,128)(2,1)S(1)} collective-permute-done((bf16[64,4096]{1,0:T(8,128)(2,1)S(1)}, bf16[64,4096]{1,0:T(8,128)(2,1)S(1)}, u32[]{:S(2)}, u32[]{:S(2)}) %collective-permute-start.28) | collective-permute-done | bytes 524320 | tf_op jit(solution)/shard_map/return_long_2/ppermute | solution.py:297
  95.3 1.9 %collective-permute-start.30 = (bf16[32,4096]{1,0:T(8,128)(2,1)S(1)}, bf16[32,4096]{1,0:T(8,128)(2,1)S(1)}, u32[]{:S(2)}, u32[]{:S(2)}) collective-permute-start(bf16[32,4096]{1,0:T(8,128)(2,1)S(1)} %get-tuple-element.82), channel_id=1, source_target_pairs={{0,4},{1,3},{4,8},{5,1},{8,12},{9,5},{12,14},{13,9},{14,10},{15,13... | collective-permute-start | bytes 786440 | tf_op jit(solution)/shard_map/return_long_1/ppermute | solution.py:297
  97.8 2.2 %collective-permute-done.31.refs_3_ = bf16[32,4096]{1,0:T(8,128)(2,1)S(1)} collective-permute-done((bf16[32,4096]{1,0:T(8,128)(2,1)S(1)}, bf16[32,4096]{1,0:T(8,128)(2,1)S(1)}, u32[]{:S(2)}, u32[]{:S(2)}) %collective-permute-start.31) | collective-permute-done | bytes 262176 | tf_op jit(solution)/shard_map/return_short_1/ppermute | solution.py:297
  100.0 2.8 %collective-permute-done.29.refs_1_ = bf16[32,4096]{1,0:T(8,128)(2,1)S(1)} collective-permute-done((bf16[32,4096]{1,0:T(8,128)(2,1)S(1)}, bf16[32,4096]{1,0:T(8,128)(2,1)S(1)}, u32[]{:S(2)}, u32[]{:S(2)}) %collective-permute-start.29) | collective-permute-done | bytes 262176 | tf_op jit(solution)/shard_map/return_long_1/ppermute | solution.py:297
  102.9 3.4 %collective-permute-done.30.refs_2_ = bf16[32,4096]{1,0:T(8,128)(2,1)S(1)} collective-permute-done((bf16[32,4096]{1,0:T(8,128)(2,1)S(1)}, bf16[32,4096]{1,0:T(8,128)(2,1)S(1)}, u32[]{:S(2)}, u32[]{:S(2)}) %collective-permute-start.30) | collective-permute-done | bytes 262176 | tf_op jit(solution)/shard_map/return_long_1/ppermute | solution.py:297
  (54 shorter events, 8.1 us)
Async XLA Ops:
  1.3 10.9 %collective-permute-start = (bf16[64,4224]{1,0:T(8,128)(2,1)S(1)}, bf16[64,4224]{1,0:T(8,128)(2,1)S(1)}, u32[]{:S(2)}, u32[]{:S(2)}) collective-permute-start(bf16[64,4224]{1,0:T(8,128)(2,1)S(1)} %get-tuple-element.44.refs_0_), channel_id=1, source_target_pairs={{0,1},{1,0},{2,3},{3,2},{4,5},{5,4},{6,7},{7,6},{8,9},{9,8},{10,11... | collective-permute-start | bytes 1622024 | tf_op jit(solution)/shard_map/swap_in_0/ppermute | solution.py:297
  1.8 14.3 %collective-permute-start.2 = (bf16[64,4224]{1,0:T(8,128)(2,1)S(1)}, bf16[64,4224]{1,0:T(8,128)(2,1)S(1)}, u32[]{:S(2)}, u32[]{:S(2)}) collective-permute-start(bf16[64,4224]{1,0:T(8,128)(2,1)S(1)} %get-tuple-element.44.refs_0_), channel_id=1, source_target_pairs={{0,4},{1,3},{4,8},{5,1},{8,12},{9,5},{12,14},{13,9},{14,10},{15,13... | collective-permute-start | bytes 1622024 | tf_op jit(solution)/shard_map/gather_long_1/ppermute | solution.py:297
  4.5 13.1 %collective-permute-start.3 = (bf16[64,4224]{1,0:T(8,128)(2,1)S(1)}, bf16[64,4224]{1,0:T(8,128)(2,1)S(1)}, u32[]{:S(2)}, u32[]{:S(2)}) collective-permute-start(bf16[64,4224]{1,0:T(8,128)(2,1)S(1)} %get-tuple-element.50), channel_id=1, source_target_pairs={{0,3},{1,4},{4,1},{5,8},{8,5},{9,12},{12,9},{13,14},{14,13},{15,10... | collective-permute-start | bytes 1622024 | tf_op jit(solution)/shard_map/gather_long_1/ppermute | solution.py:297
  17.6 4.2 %collective-permute-start.4 = (bf16[64,4224]{1,0:T(8,128)(2,1)S(1)}, bf16[64,4224]{1,0:T(8,128)(2,1)S(1)}, u32[]{:S(2)}, u32[]{:S(2)}) collective-permute-start(bf16[64,4224]{1,0:T(8,128)(2,1)S(1)} %get-tuple-element.52.refs_2_), channel_id=1, source_target_pairs={{0,1},{1,0},{2,3},{3,2},{4,5},{5,4},{6,7},{7,6},{8,9},{9,8},{10,11... | collective-permute-start | bytes 1622024 | tf_op jit(solution)/shard_map/swap_in_1/ppermute | solution.py:297
  17.7 4.2 %collective-permute-start.5 = (bf16[64,4224]{1,0:T(8,128)(2,1)S(1)}, bf16[64,4224]{1,0:T(8,128)(2,1)S(1)}, u32[]{:S(2)}, u32[]{:S(2)}) collective-permute-start(bf16[64,4224]{1,0:T(8,128)(2,1)S(1)} %get-tuple-element.54.refs_3_), channel_id=1, source_target_pairs={{0,1},{1,0},{2,3},{3,2},{4,5},{5,4},{6,7},{7,6},{8,9},{9,8},{10,11... | collective-permute-start | bytes 1622024 | tf_op jit(solution)/shard_map/swap_in_1/ppermute | solution.py:297
  18.2 10.1 %collective-permute-start.7 = (bf16[64,4224]{1,0:T(8,128)(2,1)S(1)}, bf16[64,4224]{1,0:T(8,128)(2,1)S(1)}, u32[]{:S(2)}, u32[]{:S(2)}) collective-permute-start(bf16[64,4224]{1,0:T(8,128)(2,1)S(1)} %get-tuple-element.54.refs_3_), channel_id=1, source_target_pairs={{0,4},{1,3},{4,8},{5,1},{8,12},{9,5},{12,14},{13,9},{14,10},{15,13... | collective-permute-start | bytes 1622024 | tf_op jit(solution)/shard_map/gather_short_2/ppermute | solution.py:297
  20.3 13.1 %collective-permute-start.12 = (bf16[64,4224]{1,0:T(8,128)(2,1)S(1)}, bf16[64,4224]{1,0:T(8,128)(2,1)S(1)}, u32[]{:S(2)}, u32[]{:S(2)}) collective-permute-start(bf16[64,4224]{1,0:T(8,128)(2,1)S(1)} %get-tuple-element.52.refs_2_), channel_id=1, source_target_pairs={{0,4},{1,3},{4,8},{5,1},{8,12},{9,5},{12,14},{13,9},{14,10},{15,13... | collective-permute-start | bytes 1622024 | tf_op jit(solution)/shard_map/gather_long_2/ppermute | solution.py:297
  28.3 7.1 %collective-permute-start.8 = (bf16[64,4224]{1,0:T(8,128)(2,1)S(1)}, bf16[64,4224]{1,0:T(8,128)(2,1)S(1)}, u32[]{:S(2)}, u32[]{:S(2)}) collective-permute-start(bf16[64,4224]{1,0:T(8,128)(2,1)S(1)} %collective-permute-done.7.refs_1_), channel_id=1, source_target_pairs={{0,1},{1,0},{2,3},{3,2},{4,5},{5,4},{6,7},{7,6},{8,9},{9,8},{10,11... | collective-permute-start | bytes 1622024 | tf_op jit(solution)/shard_map/swap_in_2/ppermute | solution.py:297
  28.4 11.0 %collective-permute-start.10 = (bf16[64,4224]{1,0:T(8,128)(2,1)S(1)}, bf16[64,4224]{1,0:T(8,128)(2,1)S(1)}, u32[]{:S(2)}, u32[]{:S(2)}) collective-permute-start(bf16[64,4224]{1,0:T(8,128)(2,1)S(1)} %collective-permute-done.7.refs_1_), channel_id=1, source_target_pairs={{0,4},{1,3},{4,8},{5,1},{8,12},{9,5},{12,14},{13,9},{14,10},{15,13... | collective-permute-start | bytes 1622024 | tf_op jit(solution)/shard_map/gather_short_3/ppermute | solution.py:297
  33.3 11.6 %collective-permute-start.13 = (bf16[64,4224]{1,0:T(8,128)(2,1)S(1)}, bf16[64,4224]{1,0:T(8,128)(2,1)S(1)}, u32[]{:S(2)}, u32[]{:S(2)}) collective-permute-start(bf16[64,4224]{1,0:T(8,128)(2,1)S(1)} %collective-permute-done.12.refs_1_), channel_id=1, source_target_pairs={{0,4},{1,3},{4,8},{5,1},{8,12},{9,5},{12,14},{13,9},{14,10},{15,13... | collective-permute-start | bytes 1622024 | tf_op jit(solution)/shard_map/gather_long_3/ppermute | solution.py:297
  39.4 7.6 %collective-permute-start.11 = (bf16[64,4224]{1,0:T(8,128)(2,1)S(1)}, bf16[64,4224]{1,0:T(8,128)(2,1)S(1)}, u32[]{:S(2)}, u32[]{:S(2)}) collective-permute-start(bf16[64,4224]{1,0:T(8,128)(2,1)S(1)} %collective-permute-done.10.refs_2_), channel_id=1, source_target_pairs={{0,1},{1,0},{2,3},{3,2},{4,5},{5,4},{6,7},{7,6},{8,9},{9,8},{10,11... | collective-permute-start | bytes 1622024 | tf_op jit(solution)/shard_map/swap_in_3/ppermute | solution.py:297
  44.9 2.1 %collective-permute-start.14 = (bf16[64,4224]{1,0:T(8,128)(2,1)S(1)}, bf16[64,4224]{1,0:T(8,128)(2,1)S(1)}, u32[]{:S(2)}, u32[]{:S(2)}) collective-permute-start(bf16[64,4224]{1,0:T(8,128)(2,1)S(1)} %collective-permute-done.13.refs_3_), channel_id=1, source_target_pairs={{0,1},{1,0},{2,3},{3,2},{4,5},{5,4},{6,7},{7,6},{8,9},{9,8},{10,11... | collective-permute-start | bytes 1622024 | tf_op jit(solution)/shard_map/swap_in_3/ppermute | solution.py:297
  44.9 10.6 %collective-permute-start.17 = (bf16[64,4224]{1,0:T(8,128)(2,1)S(1)}, bf16[64,4224]{1,0:T(8,128)(2,1)S(1)}, u32[]{:S(2)}, u32[]{:S(2)}) collective-permute-start(bf16[64,4224]{1,0:T(8,128)(2,1)S(1)} %collective-permute-done.13.refs_3_), channel_id=1, source_target_pairs={{0,4},{1,3},{4,8},{5,1},{8,12},{9,5},{12,14},{13,9},{14,10},{15,13... | collective-permute-start | bytes 1622024 | tf_op jit(solution)/shard_map/gather_long_4/ppermute | solution.py:297
  53.4 2.0 %collective-permute-start.15 = (bf16[64,4096]{1,0:T(8,128)(2,1)S(1)}, bf16[64,4096]{1,0:T(8,128)(2,1)S(1)}, u32[]{:S(2)}, u32[]{:S(2)}) collective-permute-start(bf16[64,4096]{1,0:T(8,128)(2,1)S(1)} %get-tuple-element.65), channel_id=1, source_target_pairs={{0,1},{1,0},{2,3},{3,2},{4,5},{5,4},{6,7},{7,6},{8,9},{9,8},{10,11... | collective-permute-start | bytes 1572872 | tf_op jit(solution)/shard_map/swap_out_3/ppermute | solution.py:297
  55.6 2.1 %collective-permute-start.18 = (bf16[64,4224]{1,0:T(8,128)(2,1)S(1)}, bf16[64,4224]{1,0:T(8,128)(2,1)S(1)}, u32[]{:S(2)}, u32[]{:S(2)}) collective-permute-start(bf16[64,4224]{1,0:T(8,128)(2,1)S(1)} %collective-permute-done.17.refs_1_), channel_id=1, source_target_pairs={{0,1},{1,0},{2,3},{3,2},{4,5},{5,4},{6,7},{7,6},{8,9},{9,8},{10,11... | collective-permute-start | bytes 1622024 | tf_op jit(solution)/shard_map/swap_in_4/ppermute | solution.py:297
  55.8 9.2 %collective-permute-start.16 = (bf16[64,4096]{1,0:T(8,128)(2,1)S(1)}, bf16[64,4096]{1,0:T(8,128)(2,1)S(1)}, u32[]{:S(2)}, u32[]{:S(2)}) collective-permute-start(bf16[64,4096]{1,0:T(8,128)(2,1)S(1)} %step_sum.5), channel_id=1, source_target_pairs={{0,4},{1,3},{4,8},{5,1},{8,12},{9,5},{12,14},{13,9},{14,10},{15,13... | collective-permute-start | bytes 1572872 | tf_op jit(solution)/shard_map/return_short_3/ppermute | solution.py:297
  61.6 3.3 %collective-permute-start.19 = (bf16[64,4096]{1,0:T(8,128)(2,1)S(1)}, bf16[64,4096]{1,0:T(8,128)(2,1)S(1)}, u32[]{:S(2)}, u32[]{:S(2)}) collective-permute-start(bf16[64,4096]{1,0:T(8,128)(2,1)S(1)} %get-tuple-element.68), channel_id=1, source_target_pairs={{0,1},{1,0},{2,3},{3,2},{4,5},{5,4},{6,7},{7,6},{8,9},{9,8},{10,11... | collective-permute-start | bytes 1572872 | tf_op jit(solution)/shard_map/swap_out_4/ppermute | solution.py:297
  61.8 14.8 %collective-permute-start.25 = (bf16[64,4224]{1,0:T(8,128)(2,1)S(1)}, bf16[64,4224]{1,0:T(8,128)(2,1)S(1)}, u32[]{:S(2)}, u32[]{:S(2)}) collective-permute-start(bf16[64,4224]{1,0:T(8,128)(2,1)S(1)} %collective-permute-done.12.refs_1_), channel_id=1, source_target_pairs={{0,1},{1,0},{2,3},{3,2},{4,5},{5,4},{6,7},{7,6},{8,9},{9,8},{10,11... | collective-permute-start | bytes 1622024 | tf_op jit(solution)/shard_map/swap_in_2/ppermute | solution.py:297
  62.2 5.3 %collective-permute-start.9 = (bf16[64,4096]{1,0:T(8,128)(2,1)S(1)}, bf16[64,4096]{1,0:T(8,128)(2,1)S(1)}, u32[]{:S(2)}, u32[]{:S(2)}) collective-permute-start(bf16[64,4096]{1,0:T(8,128)(2,1)S(1)} %get-tuple-element.60), channel_id=1, source_target_pairs={{0,1},{1,0},{2,3},{3,2},{4,5},{5,4},{6,7},{7,6},{8,9},{9,8},{10,11... | collective-permute-start | bytes 1572872 | tf_op jit(solution)/shard_map/swap_out_2/ppermute | solution.py:297
  65.1 9.2 %collective-permute-start.22 = (bf16[64,4096]{1,0:T(8,128)(2,1)S(1)}, bf16[64,4096]{1,0:T(8,128)(2,1)S(1)}, u32[]{:S(2)}, u32[]{:S(2)}) collective-permute-start(bf16[64,4096]{1,0:T(8,128)(2,1)S(1)} %step_sum.6), channel_id=1, source_target_pairs={{0,4},{1,3},{4,8},{5,1},{8,12},{9,5},{12,14},{13,9},{14,10},{15,13... | collective-permute-start | bytes 1572872 | tf_op jit(solution)/shard_map/return_long_4/ppermute | solution.py:297
  67.1 7.3 %collective-permute-start.21 = (bf16[64,4096]{1,0:T(8,128)(2,1)S(1)}, bf16[64,4096]{1,0:T(8,128)(2,1)S(1)}, u32[]{:S(2)}, u32[]{:S(2)}) collective-permute-start(bf16[64,4096]{1,0:T(8,128)(2,1)S(1)} %get-tuple-element.72), channel_id=1, source_target_pairs={{0,1},{1,0},{2,3},{3,2},{4,5},{5,4},{6,7},{7,6},{8,9},{9,8},{10,11... | collective-permute-start | bytes 1572872 | tf_op jit(solution)/shard_map/swap_out_3/ppermute | solution.py:297
  67.1 14.0 %collective-permute-start.6 = (bf16[64,4096]{1,0:T(8,128)(2,1)S(1)}, bf16[64,4096]{1,0:T(8,128)(2,1)S(1)}, u32[]{:S(2)}, u32[]{:S(2)}) collective-permute-start(bf16[64,4096]{1,0:T(8,128)(2,1)S(1)} %get-tuple-element.56), channel_id=1, source_target_pairs={{0,1},{1,0},{2,3},{3,2},{4,5},{5,4},{6,7},{7,6},{8,9},{9,8},{10,11... | collective-permute-start | bytes 1572872 | tf_op jit(solution)/shard_map/swap_out_1/ppermute | solution.py:297
  67.8 13.3 %collective-permute-start.20 = (bf16[64,4096]{1,0:T(8,128)(2,1)S(1)}, bf16[64,4096]{1,0:T(8,128)(2,1)S(1)}, u32[]{:S(2)}, u32[]{:S(2)}) collective-permute-start(bf16[64,4096]{1,0:T(8,128)(2,1)S(1)} %step_sum.7), channel_id=1, source_target_pairs={{0,4},{1,3},{4,8},{5,1},{8,12},{9,5},{12,14},{13,9},{14,10},{15,13... | collective-permute-start | bytes 1572872 | tf_op jit(solution)/shard_map/return_short_2/ppermute | solution.py:297
  74.6 11.0 %collective-permute-start.27 = (bf16[64,4096]{1,0:T(8,128)(2,1)S(1)}, bf16[64,4096]{1,0:T(8,128)(2,1)S(1)}, u32[]{:S(2)}, u32[]{:S(2)}) collective-permute-start(bf16[64,4096]{1,0:T(8,128)(2,1)S(1)} %step_sum.8), channel_id=1, source_target_pairs={{0,4},{1,3},{4,8},{5,1},{8,12},{9,5},{12,14},{13,9},{14,10},{15,13... | collective-permute-start | bytes 1572872 | tf_op jit(solution)/shard_map/return_long_3/ppermute | solution.py:297
  80.5 5.1 %collective-permute-start.26 = (bf16[64,4096]{1,0:T(8,128)(2,1)S(1)}, bf16[64,4096]{1,0:T(8,128)(2,1)S(1)}, u32[]{:S(2)}, u32[]{:S(2)}) collective-permute-start(bf16[64,4096]{1,0:T(8,128)(2,1)S(1)} %get-tuple-element.78), channel_id=1, source_target_pairs={{0,1},{1,0},{2,3},{3,2},{4,5},{5,4},{6,7},{7,6},{8,9},{9,8},{10,11... | collective-permute-start | bytes 1572872 | tf_op jit(solution)/shard_map/swap_out_2/ppermute | solution.py:297
  80.5 9.0 %collective-permute-start.24 = (bf16[64,4096]{1,0:T(8,128)(2,1)S(1)}, bf16[64,4096]{1,0:T(8,128)(2,1)S(1)}, u32[]{:S(2)}, u32[]{:S(2)}) collective-permute-start(bf16[64,4096]{1,0:T(8,128)(2,1)S(1)} %get-tuple-element.76), channel_id=1, source_target_pairs={{0,1},{1,0},{2,3},{3,2},{4,5},{5,4},{6,7},{7,6},{8,9},{9,8},{10,11... | collective-permute-start | bytes 1572872 | tf_op jit(solution)/shard_map/swap_out_1/ppermute | solution.py:297
  85.8 9.2 %collective-permute-start.28 = (bf16[64,4096]{1,0:T(8,128)(2,1)S(1)}, bf16[64,4096]{1,0:T(8,128)(2,1)S(1)}, u32[]{:S(2)}, u32[]{:S(2)}) collective-permute-start(bf16[64,4096]{1,0:T(8,128)(2,1)S(1)} %step_sum.9), channel_id=1, source_target_pairs={{0,4},{1,3},{4,8},{5,1},{8,12},{9,5},{12,14},{13,9},{14,10},{15,13... | collective-permute-start | bytes 1572872 | tf_op jit(solution)/shard_map/return_long_2/ppermute | solution.py:297
  87.7 9.5 %collective-permute-start.1 = (bf16[64,4096]{1,0:T(8,128)(2,1)S(1)}, bf16[64,4096]{1,0:T(8,128)(2,1)S(1)}, u32[]{:S(2)}, u32[]{:S(2)}) collective-permute-start(bf16[64,4096]{1,0:T(8,128)(2,1)S(1)} %get-tuple-element.48), channel_id=1, source_target_pairs={{0,1},{1,0},{2,3},{3,2},{4,5},{5,4},{6,7},{7,6},{8,9},{9,8},{10,11... | collective-permute-start | bytes 1572872 | tf_op jit(solution)/shard_map/swap_out_0/ppermute | solution.py:297
  87.7 10.1 %collective-permute-start.23 = (bf16[32,4096]{1,0:T(8,128)(2,1)S(1)}, bf16[32,4096]{1,0:T(8,128)(2,1)S(1)}, u32[]{:S(2)}, u32[]{:S(2)}) collective-permute-start(bf16[32,4096]{1,0:T(8,128)(2,1)S(1)} %get-tuple-element.75), channel_id=1, source_target_pairs={{0,4},{1,3},{4,8},{5,1},{8,12},{9,5},{12,14},{13,9},{14,10},{15,13... | collective-permute-start | bytes 786440 | tf_op jit(solution)/shard_map/return_short_1/ppermute | solution.py:297
  89.3 10.7 %collective-permute-start.31 = (bf16[32,4096]{1,0:T(8,128)(2,1)S(1)}, bf16[32,4096]{1,0:T(8,128)(2,1)S(1)}, u32[]{:S(2)}, u32[]{:S(2)}) collective-permute-start(bf16[32,4096]{1,0:T(8,128)(2,1)S(1)} %get-tuple-element.79), channel_id=1, source_target_pairs={{0,5},{1,2},{4,9},{5,0},{8,13},{9,4},{12,15},{13,8},{14,11},{15,12... | collective-permute-start | bytes 786440 | tf_op jit(solution)/shard_map/return_short_1/ppermute | solution.py:297
  95.2 7.6 %collective-permute-start.29 = (bf16[32,4096]{1,0:T(8,128)(2,1)S(1)}, bf16[32,4096]{1,0:T(8,128)(2,1)S(1)}, u32[]{:S(2)}, u32[]{:S(2)}) collective-permute-start(bf16[32,4096]{1,0:T(8,128)(2,1)S(1)} %get-tuple-element.81), channel_id=1, source_target_pairs={{0,5},{1,2},{4,9},{5,0},{8,13},{9,4},{12,15},{13,8},{14,11},{15,12... | collective-permute-start | bytes 786440 | tf_op jit(solution)/shard_map/return_long_1/ppermute | solution.py:297
  95.3 11.0 %collective-permute-start.30 = (bf16[32,4096]{1,0:T(8,128)(2,1)S(1)}, bf16[32,4096]{1,0:T(8,128)(2,1)S(1)}, u32[]{:S(2)}, u32[]{:S(2)}) collective-permute-start(bf16[32,4096]{1,0:T(8,128)(2,1)S(1)} %get-tuple-element.82), channel_id=1, source_target_pairs={{0,4},{1,3},{4,8},{5,1},{8,12},{9,5},{12,14},{13,9},{14,10},{15,13... | collective-permute-start | bytes 786440 | tf_op jit(solution)/shard_map/return_long_1/ppermute | solution.py:297
  (2 other events, 24.3 us)

commit v13 on v12

--- a/solution.py
+++ b/solution.py
@@ -239,29 +239,58 @@
     )(same, cross)
 
 
-def last_kernel(core, mine, theirs, *refs):
-    *arrived, out = refs
+def near_kernel(mine, theirs, short_same, short_cross, out):
     half = out.shape[0] // 2
-    for which, place in ((0, core[0]), (1, 1 - core[0])):
-        there = pl.ds(pl.multiple_of(place * half, half), half)
+    for which, arrived in enumerate((short_same, short_cross)):
         here = slice(which * half, (which + 1) * half)
         for column in range(0, out.shape[1], WIDTH_CHUNK):
             columns = slice(column, column + WIDTH_CHUNK)
             total = mine[here, columns].astype(jnp.float32) + theirs[here, columns].astype(jnp.float32)
-            for ref in arrived[2 * which : 2 * which + 2]:
-                total += ref[:, columns].astype(jnp.float32)
-            out[there, columns] = total.astype(jnp.bfloat16)
-
-
-def last_sum(core, mine, theirs, *arrived):
+            out[here, columns] = total + arrived[:, columns].astype(jnp.float32)
+
+
+def near_sum(*terms):
+    return pl.pallas_call(
+        near_kernel,
+        in_specs=[VMEM] * 4,
+        out_specs=VMEM,
+        out_shape=jax.ShapeDtypeStruct(terms[0].shape, jnp.float32),
+        compiler_params=limits(4),
+        cost_estimate=pl.CostEstimate(flops=10_000_000_000, bytes_accessed=0, transcendentals=0),
+        name="near_sum",
+    )(*terms)
+
+
+def last_kernel(core, near, long_cross, long_same, out, here, sem):
+    half = out.shape[0] // 2
+    copies = []
+    for which, arrived in enumerate((long_cross, long_same)):
+        place = core[0] if which == 0 else 1 - core[0]
+        there = pl.ds(pl.multiple_of(place * half, half), half)
+        from_rows = slice(which * half, (which + 1) * half)
+        for chunk in range(0, out.shape[1] // WIDTH_CHUNK):
+            columns = slice(chunk * WIDTH_CHUNK, (chunk + 1) * WIDTH_CHUNK)
+            total = near[from_rows, columns] + arrived[:, columns].astype(jnp.float32)
+            here[from_rows, columns] = total.astype(jnp.bfloat16)
+            source = here.at[pl.ds(which * half, half), pl.ds(chunk * WIDTH_CHUNK, WIDTH_CHUNK)]
+            target = out.at[there, pl.ds(chunk * WIDTH_CHUNK, WIDTH_CHUNK)]
+            copies.append(pltpu.make_async_copy(source, target, sem.at[which, chunk]))
+            copies[-1].start()
+    for copy in copies:
+        copy.wait()
+
+
+def last_sum(core, near, *arrived):
+    rows, width = near.shape
     return pl.pallas_call(
         last_kernel,
-        in_specs=[SMEM] + [VMEM] * (2 + len(arrived)),
-        out_specs=VMEM,
-        out_shape=jax.ShapeDtypeStruct(mine.shape, jnp.bfloat16),
+        in_specs=[SMEM] + [VMEM] * 3,
+        out_specs=ANYWHERE,
+        out_shape=jax.ShapeDtypeStruct(near.shape, jnp.bfloat16),
+        scratch_shapes=[pltpu.VMEM(near.shape, jnp.bfloat16), pltpu.SemaphoreType.DMA((2, width // WIDTH_CHUNK))],
         compiler_params=limits(4),
         name="last_sum",
-    )(core, mine, theirs, *arrived)
+    )(core, near, *arrived)
 
 
 def together(*values):
@@ -341,9 +370,9 @@
 
     for distance in range(2, reach - 1):
         last = run([(distance, "short")], last)
-    run([(reach - 1, "short"), (reach - 1, "long")], last)
+    run([(reach - 1, "short")], last)
     short, totals = step(reach - 1, "short", ())
-    run([(reach, "long")], totals, 2)
+    run([(reach, "long"), (reach - 1, "long")], totals)
     given[reach, "long"] = after(given[reach, "long"], *short)
     long, totals = step(reach, "long", ())
     for distance in range(reach - 1, 0, -1):
@@ -356,10 +385,11 @@
         if distance > 1:
             long, totals = step(distance, "long", [after(x, *totals) for x in long])
         else:
-            long, totals = arrive("long", long)
-    short_cross, short_same = short
+            short_cross, short_same = short
+            near = near_sum(kept[0], given[0], short_same, short_cross)
+            long, totals = arrive("long", [after(x, near) for x in long])
     long_cross, long_same = long
-    return last_sum(core, kept[0], given[0], short_same, long_cross, long_same, short_cross)
+    return last_sum(core, near, long_cross, long_same)
 
 
 def solution(mesh):

time: 107 us -> 108 us (level)
  starting transfers between devices: 30 us -> 31.3 us
    ppermute x32, starting transfers between devices: 30 us -> 31.3 us  [send(): return lax.ppermute(x, 'expert', perm)]
  transfers between devices with their start and end apart: 32 -> 32, of which waited for: 12 -> 14; matrix products, arithmetic and copies ran while one was open for 0% -> 0% of each run, Pallas kernels for 34% -> 34%
where the time goes in v13:
time: 108 us
  Pallas kernels  38.7 us (36%)
  waiting for transfers between devices  37.4 us (35%)
  starting transfers between devices  31.3 us (29%)
    ppermute x32, waiting for transfers between devices, send(): return lax.ppermute(x, 'expert', perm)  37.4 us
    ppermute x32, starting transfers between devices, send(): return lax.ppermute(x, 'expert', perm)  31.3 us
    pallas_call x6, Pallas kernels, expert_part(): pl.pallas_call(functools.partial(expert_kernel, len(blocks)), in_specs=[V...  28.6 us
    pallas_call x1, Pallas kernels, keep(): pl.pallas_call(keep_kernel, in_specs=[ANYWHERE] * 2, out_specs=[VMEM] * 2...  6.38 us
  transfers between devices with their start and end apart: 32, of which 14 were waited for; matrix products, arithmetic and copies ran while one was open for 0% of the time, Pallas kernels for 34%

profile of v13, /device:TPU:0, one launch (start us, length us, event | category | flops | bytes accessed | tf_op | source)
XLA Modules:
  0.0 107.5 jit_solution(1643460952977846497)
XLA Ops:
  0.0 1.3 %pack.1 = (bf16[64,4224]{1,0:T(8,128)(2,1)S(1)}, bf16[64,4224]{1,0:T(8,128)(2,1)S(1)}) custom-call(s32[1]{0:T(128)} %bitcast.core, bf16[64,4096]{1,0:T(8,128)(2,1)} %tokens.1, s32[8,64]{1,0:T(8,128)} %bitcast.7, s32[8,64]{1,0:T(8,128)} %bitcast.8), custom_call_target="tpu_custom_call" | custom-call | tf_op jit(solution)/shard_map/pack/pallas_call | solution.py:64
  1.8 2.6 %collective-permute-start.2 = (bf16[64,4224]{1,0:T(8,128)(2,1)S(1)}, bf16[64,4224]{1,0:T(8,128)(2,1)S(1)}, u32[]{:S(2)}, u32[]{:S(2)}) collective-permute-start(bf16[64,4224]{1,0:T(8,128)(2,1)S(1)} %get-tuple-element.45.refs_0_), channel_id=1, source_target_pairs={{0,4},{1,3},{4,8},{5,1},{8,12},{9,5},{12,14},{13,9},{14,10},{15,13... | collective-permute-start | bytes 1622024 | tf_op jit(solution)/shard_map/gather_long_1/ppermute | solution.py:326
  4.5 1.3 %collective-permute-start.3 = (bf16[64,4224]{1,0:T(8,128)(2,1)S(1)}, bf16[64,4224]{1,0:T(8,128)(2,1)S(1)}, u32[]{:S(2)}, u32[]{:S(2)}) collective-permute-start(bf16[64,4224]{1,0:T(8,128)(2,1)S(1)} %get-tuple-element.51), channel_id=1, source_target_pairs={{0,3},{1,4},{4,1},{5,8},{8,5},{9,12},{12,9},{13,14},{14,13},{15,10... | collective-permute-start | bytes 1622024 | tf_op jit(solution)/shard_map/gather_long_1/ppermute | solution.py:326
  5.7 6.4 %keep.1 = (bf16[4096,1536]{1,0:T(8,128)(2,1)S(1)}, bf16[768,4096]{1,0:T(8,128)(2,1)S(1)}) custom-call(bf16[4096,1536]{1,0:T(8,128)(2,1)} %bitcast.5, bf16[768,4096]{1,0:T(8,128)(2,1)} %bitcast.6), custom_call_target="tpu_custom_call" | custom-call | bytes 18874368 | tf_op jit(solution)/shard_map/keep/pallas_call | solution.py:88
  12.2 4.0 %expert.6 = (bf16[64,4096]{1,0:T(8,128)(2,1)S(1)}, bf16[64,4096]{1,0:T(8,128)(2,1)S(1)}) custom-call(bf16[64,4224]{1,0:T(8,128)(2,1)S(1)} %get-tuple-element.45.refs_0_, bf16[64,4224]{1,0:T(8,128)(2,1)S(1)} %collective-permute-done.refs_1_, f32[1,128]{1,0:T(1,128)S(1)} %compare_select_fusion.1.refs_2_.refs_4_, f32[1,1536]{1,0:T(1,128)S(1)} %copy-done.1, ...), custom_call_target="tpu_custom_call" | custom-call | flops 4831838208 | tf_op jit(solution)/shard_map/expert/pallas_call | solution.py:146
  16.2 1.4 %collective-permute-done.3.cross = bf16[64,4224]{1,0:T(8,128)(2,1)S(1)} collective-permute-done((bf16[64,4224]{1,0:T(8,128)(2,1)S(1)}, bf16[64,4224]{1,0:T(8,128)(2,1)S(1)}, u32[]{:S(2)}, u32[]{:S(2)}) %collective-permute-start.3) | collective-permute-done | bytes 540704 | tf_op jit(solution)/shard_map/gather_long_1/ppermute | solution.py:326
  18.2 2.1 %collective-permute-start.7 = (bf16[64,4224]{1,0:T(8,128)(2,1)S(1)}, bf16[64,4224]{1,0:T(8,128)(2,1)S(1)}, u32[]{:S(2)}, u32[]{:S(2)}) collective-permute-start(bf16[64,4224]{1,0:T(8,128)(2,1)S(1)} %get-tuple-element.55.refs_3_), channel_id=1, source_target_pairs={{0,4},{1,3},{4,8},{5,1},{8,12},{9,5},{12,14},{13,9},{14,10},{15,13... | collective-permute-start | bytes 1622024 | tf_op jit(solution)/shard_map/gather_short_2/ppermute | solution.py:326
  20.3 1.6 %collective-permute-start.14 = (bf16[64,4224]{1,0:T(8,128)(2,1)S(1)}, bf16[64,4224]{1,0:T(8,128)(2,1)S(1)}, u32[]{:S(2)}, u32[]{:S(2)}) collective-permute-start(bf16[64,4224]{1,0:T(8,128)(2,1)S(1)} %get-tuple-element.53.refs_2_), channel_id=1, source_target_pairs={{0,4},{1,3},{4,8},{5,1},{8,12},{9,5},{12,14},{13,9},{14,10},{15,13... | collective-permute-start | bytes 1622024 | tf_op jit(solution)/shard_map/gather_long_2/ppermute | solution.py:326
  21.8 6.4 %expert.7 = (bf16[64,4096]{1,0:T(8,128)(2,1)S(1)}, bf16[64,4096]{1,0:T(8,128)(2,1)S(1)}, bf16[64,4096]{1,0:T(8,128)(2,1)S(1)}, bf16[64,4096]{1,0:T(8,128)(2,1)S(1)}) custom-call(bf16[64,4224]{1,0:T(8,128)(2,1)S(1)} %collective-permute-done.4.refs_0_, bf16[64,4224]{1,0:T(8,128)(2,1)S(1)} %collective-permute-done.5.refs_1_, ...), custom_call_target="tpu_custom_call" | custom-call | flops 9663676416 | tf_op jit(solution)/shard_map/expert/pallas_call | solution.py:146
  28.4 1.6 %collective-permute-start.10 = (bf16[64,4224]{1,0:T(8,128)(2,1)S(1)}, bf16[64,4224]{1,0:T(8,128)(2,1)S(1)}, u32[]{:S(2)}, u32[]{:S(2)}) collective-permute-start(bf16[64,4224]{1,0:T(8,128)(2,1)S(1)} %collective-permute-done.7.refs_1_), channel_id=1, source_target_pairs={{0,4},{1,3},{4,8},{5,1},{8,12},{9,5},{12,14},{13,9},{14,10},{15,13... | collective-permute-start | bytes 1622024 | tf_op jit(solution)/shard_map/gather_short_3/ppermute | solution.py:326
  30.0 3.3 %collective-permute-done.14.refs_1_ = bf16[64,4224]{1,0:T(8,128)(2,1)S(1)} collective-permute-done((bf16[64,4224]{1,0:T(8,128)(2,1)S(1)}, bf16[64,4224]{1,0:T(8,128)(2,1)S(1)}, u32[]{:S(2)}, u32[]{:S(2)}) %collective-permute-start.14) | collective-permute-done | bytes 540704 | tf_op jit(solution)/shard_map/gather_long_2/ppermute | solution.py:326
  33.3 2.1 %collective-permute-start.15 = (bf16[64,4224]{1,0:T(8,128)(2,1)S(1)}, bf16[64,4224]{1,0:T(8,128)(2,1)S(1)}, u32[]{:S(2)}, u32[]{:S(2)}) collective-permute-start(bf16[64,4224]{1,0:T(8,128)(2,1)S(1)} %collective-permute-done.14.refs_1_), channel_id=1, source_target_pairs={{0,4},{1,3},{4,8},{5,1},{8,12},{9,5},{12,14},{13,9},{14,10},{15,13... | collective-permute-start | bytes 1622024 | tf_op jit(solution)/shard_map/gather_long_3/ppermute | solution.py:326
  35.4 3.9 %expert.8 = (bf16[64,4096]{1,0:T(8,128)(2,1)S(1)}, bf16[64,4096]{1,0:T(8,128)(2,1)S(1)}) custom-call(bf16[64,4224]{1,0:T(8,128)(2,1)S(1)} %collective-permute-done.8.refs_0_, bf16[64,4224]{1,0:T(8,128)(2,1)S(1)} %collective-permute-done.7.refs_1_, f32[1,128]{1,0:T(1,128)S(1)} %compare_select_fusion.1.refs_2_.refs_4_, f32[1,1536]{1,0:T(1,128)S(1)} %copy-done.1, ...), custom_call_target="tpu_custom_call" | custom-call | flops 4831838208 | tf_op jit(solution)/shard_map/expert/pallas_call | solution.py:146
  39.5 5.5 %collective-permute-done.15.refs_3_ = bf16[64,4224]{1,0:T(8,128)(2,1)S(1)} collective-permute-done((bf16[64,4224]{1,0:T(8,128)(2,1)S(1)}, bf16[64,4224]{1,0:T(8,128)(2,1)S(1)}, u32[]{:S(2)}, u32[]{:S(2)}) %collective-permute-start.15) | collective-permute-done | bytes 540704 | tf_op jit(solution)/shard_map/gather_long_3/ppermute | solution.py:326
  44.9 2.1 %collective-permute-start.16 = (bf16[64,4224]{1,0:T(8,128)(2,1)S(1)}, bf16[64,4224]{1,0:T(8,128)(2,1)S(1)}, u32[]{:S(2)}, u32[]{:S(2)}) collective-permute-start(bf16[64,4224]{1,0:T(8,128)(2,1)S(1)} %collective-permute-done.15.refs_3_), channel_id=1, source_target_pairs={{0,4},{1,3},{4,8},{5,1},{8,12},{9,5},{12,14},{13,9},{14,10},{15,13... | collective-permute-start | bytes 1622024 | tf_op jit(solution)/shard_map/gather_long_4/ppermute | solution.py:326
  47.0 4.0 %expert.9 = (bf16[64,4096]{1,0:T(8,128)(2,1)S(1)}, bf16[64,4096]{1,0:T(8,128)(2,1)S(1)}) custom-call(bf16[64,4224]{1,0:T(8,128)(2,1)S(1)} %collective-permute-done.11.refs_0_, bf16[64,4224]{1,0:T(8,128)(2,1)S(1)} %collective-permute-done.10.refs_1_, f32[1,128]{1,0:T(1,128)S(1)} %compare_select_fusion.1.refs_2_.refs_4_, f32[1,1536]{1,0:T(1,128)S(1)} %copy-done.1, ...), custom_call_target="tpu_custom_call" | custom-call | flops 4831838208 | tf_op jit(solution)/shard_map/expert/pallas_call | solution.py:146
  51.0 1.9 %collective-permute-done.12.refs_1_ = bf16[64,4096]{1,0:T(8,128)(2,1)S(1)} collective-permute-done((bf16[64,4096]{1,0:T(8,128)(2,1)S(1)}, bf16[64,4096]{1,0:T(8,128)(2,1)S(1)}, u32[]{:S(2)}, u32[]{:S(2)}) %collective-permute-start.12) | collective-permute-done | bytes 524320 | tf_op jit(solution)/shard_map/swap_out_3/ppermute | solution.py:326
  54.8 2.1 %collective-permute-start.13 = (bf16[64,4096]{1,0:T(8,128)(2,1)S(1)}, bf16[64,4096]{1,0:T(8,128)(2,1)S(1)}, u32[]{:S(2)}, u32[]{:S(2)}) collective-permute-start(bf16[64,4096]{1,0:T(8,128)(2,1)S(1)} %step_sum.5), channel_id=1, source_target_pairs={{0,4},{1,3},{4,8},{5,1},{8,12},{9,5},{12,14},{13,9},{14,10},{15,13... | collective-permute-start | bytes 1572872 | tf_op jit(solution)/shard_map/return_short_3/ppermute | solution.py:326
  57.0 6.4 %expert.10 = (bf16[64,4096]{1,0:T(8,128)(2,1)S(1)}, bf16[64,4096]{1,0:T(8,128)(2,1)S(1)}, bf16[64,4096]{1,0:T(8,128)(2,1)S(1)}, bf16[64,4096]{1,0:T(8,128)(2,1)S(1)}) custom-call(bf16[64,4224]{1,0:T(8,128)(2,1)S(1)} %collective-permute-done.17.refs_0_, bf16[64,4224]{1,0:T(8,128)(2,1)S(1)} %collective-permute-done.18.refs_1_, ...), custom_call_target="tpu_custom_call" | custom-call | flops 9663676416 | tf_op jit(solution)/shard_map/expert/pallas_call | solution.py:146
  65.5 2.1 %collective-permute-start.22 = (bf16[64,4096]{1,0:T(8,128)(2,1)S(1)}, bf16[64,4096]{1,0:T(8,128)(2,1)S(1)}, u32[]{:S(2)}, u32[]{:S(2)}) collective-permute-start(bf16[64,4096]{1,0:T(8,128)(2,1)S(1)} %step_sum.6), channel_id=1, source_target_pairs={{0,4},{1,3},{4,8},{5,1},{8,12},{9,5},{12,14},{13,9},{14,10},{15,13... | collective-permute-start | bytes 1572872 | tf_op jit(solution)/shard_map/return_long_4/ppermute | solution.py:326
  68.4 1.6 %collective-permute-start.20 = (bf16[64,4096]{1,0:T(8,128)(2,1)S(1)}, bf16[64,4096]{1,0:T(8,128)(2,1)S(1)}, u32[]{:S(2)}, u32[]{:S(2)}) collective-permute-start(bf16[64,4096]{1,0:T(8,128)(2,1)S(1)} %step_sum.7), channel_id=1, source_target_pairs={{0,4},{1,3},{4,8},{5,1},{8,12},{9,5},{12,14},{13,9},{14,10},{15,13... | collective-permute-start | bytes 1572872 | tf_op jit(solution)/shard_map/return_short_2/ppermute | solution.py:326
  70.0 4.8 %collective-permute-done.22.refs_2_ = bf16[64,4096]{1,0:T(8,128)(2,1)S(1)} collective-permute-done((bf16[64,4096]{1,0:T(8,128)(2,1)S(1)}, bf16[64,4096]{1,0:T(8,128)(2,1)S(1)}, u32[]{:S(2)}, u32[]{:S(2)}) %collective-permute-start.22) | collective-permute-done | bytes 524320 | tf_op jit(solution)/shard_map/return_long_4/ppermute | solution.py:326
  75.0 2.1 %collective-permute-start.28 = (bf16[64,4096]{1,0:T(8,128)(2,1)S(1)}, bf16[64,4096]{1,0:T(8,128)(2,1)S(1)}, u32[]{:S(2)}, u32[]{:S(2)}) collective-permute-start(bf16[64,4096]{1,0:T(8,128)(2,1)S(1)} %step_sum.8), channel_id=1, source_target_pairs={{0,4},{1,3},{4,8},{5,1},{8,12},{9,5},{12,14},{13,9},{14,10},{15,13... | collective-permute-start | bytes 1572872 | tf_op jit(solution)/shard_map/return_long_3/ppermute | solution.py:326
  77.1 3.9 %expert.11 = (bf16[64,4096]{1,0:T(8,128)(2,1)S(1)}, bf16[64,4096]{1,0:T(8,128)(2,1)S(1)}) custom-call(bf16[64,4224]{1,0:T(8,128)(2,1)S(1)} %collective-permute-done.26.refs_0_, bf16[64,4224]{1,0:T(8,128)(2,1)S(1)} %collective-permute-done.14.refs_1_, f32[1,128]{1,0:T(1,128)S(1)} %compare_select_fusion.1.refs_2_.refs_4_, f32[1,1536]{1,0:T(1,128)S(1)} %copy-done.1, ...), custom_call_target="tpu_custom_call" | custom-call | flops 4831838208 | tf_op jit(solution)/shard_map/expert/pallas_call | solution.py:146
  81.8 1.6 %collective-permute-start.23 = (bf16[32,4096]{1,0:T(8,128)(2,1)S(1)}, bf16[32,4096]{1,0:T(8,128)(2,1)S(1)}, u32[]{:S(2)}, u32[]{:S(2)}) collective-permute-start(bf16[32,4096]{1,0:T(8,128)(2,1)S(1)} %get-tuple-element.76), channel_id=1, source_target_pairs={{0,4},{1,3},{4,8},{5,1},{8,12},{9,5},{12,14},{13,9},{14,10},{15,13... | collective-permute-start | bytes 786440 | tf_op jit(solution)/shard_map/return_short_1/ppermute | solution.py:326
  83.5 2.5 %collective-permute-done.28.refs_2_ = bf16[64,4096]{1,0:T(8,128)(2,1)S(1)} collective-permute-done((bf16[64,4096]{1,0:T(8,128)(2,1)S(1)}, bf16[64,4096]{1,0:T(8,128)(2,1)S(1)}, u32[]{:S(2)}, u32[]{:S(2)}) %collective-permute-start.28) | collective-permute-done | bytes 524320 | tf_op jit(solution)/shard_map/return_long_3/ppermute | solution.py:326
  86.2 2.1 %collective-permute-start.29 = (bf16[64,4096]{1,0:T(8,128)(2,1)S(1)}, bf16[64,4096]{1,0:T(8,128)(2,1)S(1)}, u32[]{:S(2)}, u32[]{:S(2)}) collective-permute-start(bf16[64,4096]{1,0:T(8,128)(2,1)S(1)} %step_sum.9), channel_id=1, source_target_pairs={{0,4},{1,3},{4,8},{5,1},{8,12},{9,5},{12,14},{13,9},{14,10},{15,13... | collective-permute-start | bytes 1572872 | tf_op jit(solution)/shard_map/return_long_2/ppermute | solution.py:326
  88.8 2.4 %collective-permute-done.24.short_cross = bf16[32,4096]{1,0:T(8,128)(2,1)S(1)} collective-permute-done((bf16[32,4096]{1,0:T(8,128)(2,1)S(1)}, bf16[32,4096]{1,0:T(8,128)(2,1)S(1)}, u32[]{:S(2)}, u32[]{:S(2)}) %collective-permute-start.24) | collective-permute-done | bytes 262176 | tf_op jit(solution)/shard_map/return_short_1/ppermute | solution.py:326
  91.4 5.9 %collective-permute-done.29.refs_2_ = bf16[64,4096]{1,0:T(8,128)(2,1)S(1)} collective-permute-done((bf16[64,4096]{1,0:T(8,128)(2,1)S(1)}, bf16[64,4096]{1,0:T(8,128)(2,1)S(1)}, u32[]{:S(2)}, u32[]{:S(2)}) %collective-permute-start.29) | collective-permute-done | bytes 524320 | tf_op jit(solution)/shard_map/return_long_2/ppermute | solution.py:326
  98.5 1.6 %collective-permute-start.31 = (bf16[32,4096]{1,0:T(8,128)(2,1)S(1)}, bf16[32,4096]{1,0:T(8,128)(2,1)S(1)}, u32[]{:S(2)}, u32[]{:S(2)}) collective-permute-start(bf16[32,4096]{1,0:T(8,128)(2,1)S(1)} %get-tuple-element.84), channel_id=1, source_target_pairs={{0,4},{1,3},{4,8},{5,1},{8,12},{9,5},{12,14},{13,9},{14,10},{15,13... | collective-permute-start | bytes 786440 | tf_op jit(solution)/shard_map/return_long_1/ppermute | solution.py:326
  100.0 3.3 %collective-permute-done.30.long_cross = bf16[32,4096]{1,0:T(8,128)(2,1)S(1)} collective-permute-done((bf16[32,4096]{1,0:T(8,128)(2,1)S(1)}, bf16[32,4096]{1,0:T(8,128)(2,1)S(1)}, u32[]{:S(2)}, u32[]{:S(2)}) %collective-permute-start.30) | collective-permute-done | bytes 262176 | tf_op jit(solution)/shard_map/return_long_1/ppermute | solution.py:326
  103.3 3.4 %collective-permute-done.31.long_same = bf16[32,4096]{1,0:T(8,128)(2,1)S(1)} collective-permute-done((bf16[32,4096]{1,0:T(8,128)(2,1)S(1)}, bf16[32,4096]{1,0:T(8,128)(2,1)S(1)}, u32[]{:S(2)}, u32[]{:S(2)}) %collective-permute-start.31) | collective-permute-done | bytes 262176 | tf_op jit(solution)/shard_map/return_long_1/ppermute | solution.py:326
  (55 shorter events, 10.1 us)
Async XLA Ops:
  1.3 10.9 %collective-permute-start = (bf16[64,4224]{1,0:T(8,128)(2,1)S(1)}, bf16[64,4224]{1,0:T(8,128)(2,1)S(1)}, u32[]{:S(2)}, u32[]{:S(2)}) collective-permute-start(bf16[64,4224]{1,0:T(8,128)(2,1)S(1)} %get-tuple-element.45.refs_0_), channel_id=1, source_target_pairs={{0,1},{1,0},{2,3},{3,2},{4,5},{5,4},{6,7},{7,6},{8,9},{9,8},{10,11... | collective-permute-start | bytes 1622024 | tf_op jit(solution)/shard_map/swap_in_0/ppermute | solution.py:326
  1.8 14.3 %collective-permute-start.2 = (bf16[64,4224]{1,0:T(8,128)(2,1)S(1)}, bf16[64,4224]{1,0:T(8,128)(2,1)S(1)}, u32[]{:S(2)}, u32[]{:S(2)}) collective-permute-start(bf16[64,4224]{1,0:T(8,128)(2,1)S(1)} %get-tuple-element.45.refs_0_), channel_id=1, source_target_pairs={{0,4},{1,3},{4,8},{5,1},{8,12},{9,5},{12,14},{13,9},{14,10},{15,13... | collective-permute-start | bytes 1622024 | tf_op jit(solution)/shard_map/gather_long_1/ppermute | solution.py:326
  4.5 13.1 %collective-permute-start.3 = (bf16[64,4224]{1,0:T(8,128)(2,1)S(1)}, bf16[64,4224]{1,0:T(8,128)(2,1)S(1)}, u32[]{:S(2)}, u32[]{:S(2)}) collective-permute-start(bf16[64,4224]{1,0:T(8,128)(2,1)S(1)} %get-tuple-element.51), channel_id=1, source_target_pairs={{0,3},{1,4},{4,1},{5,8},{8,5},{9,12},{12,9},{13,14},{14,13},{15,10... | collective-permute-start | bytes 1622024 | tf_op jit(solution)/shard_map/gather_long_1/ppermute | solution.py:326
  17.6 4.2 %collective-permute-start.4 = (bf16[64,4224]{1,0:T(8,128)(2,1)S(1)}, bf16[64,4224]{1,0:T(8,128)(2,1)S(1)}, u32[]{:S(2)}, u32[]{:S(2)}) collective-permute-start(bf16[64,4224]{1,0:T(8,128)(2,1)S(1)} %get-tuple-element.53.refs_2_), channel_id=1, source_target_pairs={{0,1},{1,0},{2,3},{3,2},{4,5},{5,4},{6,7},{7,6},{8,9},{9,8},{10,11... | collective-permute-start | bytes 1622024 | tf_op jit(solution)/shard_map/swap_in_1/ppermute | solution.py:326
  17.7 4.2 %collective-permute-start.5 = (bf16[64,4224]{1,0:T(8,128)(2,1)S(1)}, bf16[64,4224]{1,0:T(8,128)(2,1)S(1)}, u32[]{:S(2)}, u32[]{:S(2)}) collective-permute-start(bf16[64,4224]{1,0:T(8,128)(2,1)S(1)} %get-tuple-element.55.refs_3_), channel_id=1, source_target_pairs={{0,1},{1,0},{2,3},{3,2},{4,5},{5,4},{6,7},{7,6},{8,9},{9,8},{10,11... | collective-permute-start | bytes 1622024 | tf_op jit(solution)/shard_map/swap_in_1/ppermute | solution.py:326
  18.2 10.1 %collective-permute-start.7 = (bf16[64,4224]{1,0:T(8,128)(2,1)S(1)}, bf16[64,4224]{1,0:T(8,128)(2,1)S(1)}, u32[]{:S(2)}, u32[]{:S(2)}) collective-permute-start(bf16[64,4224]{1,0:T(8,128)(2,1)S(1)} %get-tuple-element.55.refs_3_), channel_id=1, source_target_pairs={{0,4},{1,3},{4,8},{5,1},{8,12},{9,5},{12,14},{13,9},{14,10},{15,13... | collective-permute-start | bytes 1622024 | tf_op jit(solution)/shard_map/gather_short_2/ppermute | solution.py:326
  20.3 13.1 %collective-permute-start.14 = (bf16[64,4224]{1,0:T(8,128)(2,1)S(1)}, bf16[64,4224]{1,0:T(8,128)(2,1)S(1)}, u32[]{:S(2)}, u32[]{:S(2)}) collective-permute-start(bf16[64,4224]{1,0:T(8,128)(2,1)S(1)} %get-tuple-element.53.refs_2_), channel_id=1, source_target_pairs={{0,4},{1,3},{4,8},{5,1},{8,12},{9,5},{12,14},{13,9},{14,10},{15,13... | collective-permute-start | bytes 1622024 | tf_op jit(solution)/shard_map/gather_long_2/ppermute | solution.py:326
  28.3 7.1 %collective-permute-start.8 = (bf16[64,4224]{1,0:T(8,128)(2,1)S(1)}, bf16[64,4224]{1,0:T(8,128)(2,1)S(1)}, u32[]{:S(2)}, u32[]{:S(2)}) collective-permute-start(bf16[64,4224]{1,0:T(8,128)(2,1)S(1)} %collective-permute-done.7.refs_1_), channel_id=1, source_target_pairs={{0,1},{1,0},{2,3},{3,2},{4,5},{5,4},{6,7},{7,6},{8,9},{9,8},{10,11... | collective-permute-start | bytes 1622024 | tf_op jit(solution)/shard_map/swap_in_2/ppermute | solution.py:326
  28.4 11.0 %collective-permute-start.10 = (bf16[64,4224]{1,0:T(8,128)(2,1)S(1)}, bf16[64,4224]{1,0:T(8,128)(2,1)S(1)}, u32[]{:S(2)}, u32[]{:S(2)}) collective-permute-start(bf16[64,4224]{1,0:T(8,128)(2,1)S(1)} %collective-permute-done.7.refs_1_), channel_id=1, source_target_pairs={{0,4},{1,3},{4,8},{5,1},{8,12},{9,5},{12,14},{13,9},{14,10},{15,13... | collective-permute-start | bytes 1622024 | tf_op jit(solution)/shard_map/gather_short_3/ppermute | solution.py:326
  33.3 11.6 %collective-permute-start.15 = (bf16[64,4224]{1,0:T(8,128)(2,1)S(1)}, bf16[64,4224]{1,0:T(8,128)(2,1)S(1)}, u32[]{:S(2)}, u32[]{:S(2)}) collective-permute-start(bf16[64,4224]{1,0:T(8,128)(2,1)S(1)} %collective-permute-done.14.refs_1_), channel_id=1, source_target_pairs={{0,4},{1,3},{4,8},{5,1},{8,12},{9,5},{12,14},{13,9},{14,10},{15,13... | collective-permute-start | bytes 1622024 | tf_op jit(solution)/shard_map/gather_long_3/ppermute | solution.py:326
  39.4 7.6 %collective-permute-start.11 = (bf16[64,4224]{1,0:T(8,128)(2,1)S(1)}, bf16[64,4224]{1,0:T(8,128)(2,1)S(1)}, u32[]{:S(2)}, u32[]{:S(2)}) collective-permute-start(bf16[64,4224]{1,0:T(8,128)(2,1)S(1)} %collective-permute-done.10.refs_1_), channel_id=1, source_target_pairs={{0,1},{1,0},{2,3},{3,2},{4,5},{5,4},{6,7},{7,6},{8,9},{9,8},{10,11... | collective-permute-start | bytes 1622024 | tf_op jit(solution)/shard_map/swap_in_3/ppermute | solution.py:326
  44.9 9.4 %collective-permute-start.16 = (bf16[64,4224]{1,0:T(8,128)(2,1)S(1)}, bf16[64,4224]{1,0:T(8,128)(2,1)S(1)}, u32[]{:S(2)}, u32[]{:S(2)}) collective-permute-start(bf16[64,4224]{1,0:T(8,128)(2,1)S(1)} %collective-permute-done.15.refs_3_), channel_id=1, source_target_pairs={{0,4},{1,3},{4,8},{5,1},{8,12},{9,5},{12,14},{13,9},{14,10},{15,13... | collective-permute-start | bytes 1622024 | tf_op jit(solution)/shard_map/gather_long_4/ppermute | solution.py:326
  51.0 2.0 %collective-permute-start.12 = (bf16[64,4096]{1,0:T(8,128)(2,1)S(1)}, bf16[64,4096]{1,0:T(8,128)(2,1)S(1)}, u32[]{:S(2)}, u32[]{:S(2)}) collective-permute-start(bf16[64,4096]{1,0:T(8,128)(2,1)S(1)} %get-tuple-element.64), channel_id=1, source_target_pairs={{0,1},{1,0},{2,3},{3,2},{4,5},{5,4},{6,7},{7,6},{8,9},{9,8},{10,11... | collective-permute-start | bytes 1572872 | tf_op jit(solution)/shard_map/swap_out_3/ppermute | solution.py:326
  54.3 2.6 %collective-permute-start.17 = (bf16[64,4224]{1,0:T(8,128)(2,1)S(1)}, bf16[64,4224]{1,0:T(8,128)(2,1)S(1)}, u32[]{:S(2)}, u32[]{:S(2)}) collective-permute-start(bf16[64,4224]{1,0:T(8,128)(2,1)S(1)} %collective-permute-done.16.refs_2_), channel_id=1, source_target_pairs={{0,1},{1,0},{2,3},{3,2},{4,5},{5,4},{6,7},{7,6},{8,9},{9,8},{10,11... | collective-permute-start | bytes 1622024 | tf_op jit(solution)/shard_map/swap_in_4/ppermute | solution.py:326
  54.3 2.7 %collective-permute-start.18 = (bf16[64,4224]{1,0:T(8,128)(2,1)S(1)}, bf16[64,4224]{1,0:T(8,128)(2,1)S(1)}, u32[]{:S(2)}, u32[]{:S(2)}) collective-permute-start(bf16[64,4224]{1,0:T(8,128)(2,1)S(1)} %collective-permute-done.15.refs_3_), channel_id=1, source_target_pairs={{0,1},{1,0},{2,3},{3,2},{4,5},{5,4},{6,7},{7,6},{8,9},{9,8},{10,11... | collective-permute-start | bytes 1622024 | tf_op jit(solution)/shard_map/swap_in_3/ppermute | solution.py:326
  54.8 9.3 %collective-permute-start.13 = (bf16[64,4096]{1,0:T(8,128)(2,1)S(1)}, bf16[64,4096]{1,0:T(8,128)(2,1)S(1)}, u32[]{:S(2)}, u32[]{:S(2)}) collective-permute-start(bf16[64,4096]{1,0:T(8,128)(2,1)S(1)} %step_sum.5), channel_id=1, source_target_pairs={{0,4},{1,3},{4,8},{5,1},{8,12},{9,5},{12,14},{13,9},{14,10},{15,13... | collective-permute-start | bytes 1572872 | tf_op jit(solution)/shard_map/return_short_3/ppermute | solution.py:326
  63.4 2.0 %collective-permute-start.19 = (bf16[64,4096]{1,0:T(8,128)(2,1)S(1)}, bf16[64,4096]{1,0:T(8,128)(2,1)S(1)}, u32[]{:S(2)}, u32[]{:S(2)}) collective-permute-start(bf16[64,4096]{1,0:T(8,128)(2,1)S(1)} %get-tuple-element.69), channel_id=1, source_target_pairs={{0,1},{1,0},{2,3},{3,2},{4,5},{5,4},{6,7},{7,6},{8,9},{9,8},{10,11... | collective-permute-start | bytes 1572872 | tf_op jit(solution)/shard_map/swap_out_4/ppermute | solution.py:326
  63.6 13.5 %collective-permute-start.26 = (bf16[64,4224]{1,0:T(8,128)(2,1)S(1)}, bf16[64,4224]{1,0:T(8,128)(2,1)S(1)}, u32[]{:S(2)}, u32[]{:S(2)}) collective-permute-start(bf16[64,4224]{1,0:T(8,128)(2,1)S(1)} %collective-permute-done.14.refs_1_), channel_id=1, source_target_pairs={{0,1},{1,0},{2,3},{3,2},{4,5},{5,4},{6,7},{7,6},{8,9},{9,8},{10,11... | collective-permute-start | bytes 1622024 | tf_op jit(solution)/shard_map/swap_in_2/ppermute | solution.py:326
  64.0 4.2 %collective-permute-start.9 = (bf16[64,4096]{1,0:T(8,128)(2,1)S(1)}, bf16[64,4096]{1,0:T(8,128)(2,1)S(1)}, u32[]{:S(2)}, u32[]{:S(2)}) collective-permute-start(bf16[64,4096]{1,0:T(8,128)(2,1)S(1)} %get-tuple-element.61), channel_id=1, source_target_pairs={{0,1},{1,0},{2,3},{3,2},{4,5},{5,4},{6,7},{7,6},{8,9},{9,8},{10,11... | collective-permute-start | bytes 1572872 | tf_op jit(solution)/shard_map/swap_out_2/ppermute | solution.py:326
  65.5 9.2 %collective-permute-start.22 = (bf16[64,4096]{1,0:T(8,128)(2,1)S(1)}, bf16[64,4096]{1,0:T(8,128)(2,1)S(1)}, u32[]{:S(2)}, u32[]{:S(2)}) collective-permute-start(bf16[64,4096]{1,0:T(8,128)(2,1)S(1)} %step_sum.6), channel_id=1, source_target_pairs={{0,4},{1,3},{4,8},{5,1},{8,12},{9,5},{12,14},{13,9},{14,10},{15,13... | collective-permute-start | bytes 1572872 | tf_op jit(solution)/shard_map/return_long_4/ppermute | solution.py:326
  67.7 7.1 %collective-permute-start.21 = (bf16[64,4096]{1,0:T(8,128)(2,1)S(1)}, bf16[64,4096]{1,0:T(8,128)(2,1)S(1)}, u32[]{:S(2)}, u32[]{:S(2)}) collective-permute-start(bf16[64,4096]{1,0:T(8,128)(2,1)S(1)} %get-tuple-element.73), channel_id=1, source_target_pairs={{0,1},{1,0},{2,3},{3,2},{4,5},{5,4},{6,7},{7,6},{8,9},{9,8},{10,11... | collective-permute-start | bytes 1572872 | tf_op jit(solution)/shard_map/swap_out_3/ppermute | solution.py:326
  67.7 14.0 %collective-permute-start.6 = (bf16[64,4096]{1,0:T(8,128)(2,1)S(1)}, bf16[64,4096]{1,0:T(8,128)(2,1)S(1)}, u32[]{:S(2)}, u32[]{:S(2)}) collective-permute-start(bf16[64,4096]{1,0:T(8,128)(2,1)S(1)} %get-tuple-element.57), channel_id=1, source_target_pairs={{0,1},{1,0},{2,3},{3,2},{4,5},{5,4},{6,7},{7,6},{8,9},{9,8},{10,11... | collective-permute-start | bytes 1572872 | tf_op jit(solution)/shard_map/swap_out_1/ppermute | solution.py:326
  68.4 13.3 %collective-permute-start.20 = (bf16[64,4096]{1,0:T(8,128)(2,1)S(1)}, bf16[64,4096]{1,0:T(8,128)(2,1)S(1)}, u32[]{:S(2)}, u32[]{:S(2)}) collective-permute-start(bf16[64,4096]{1,0:T(8,128)(2,1)S(1)} %step_sum.7), channel_id=1, source_target_pairs={{0,4},{1,3},{4,8},{5,1},{8,12},{9,5},{12,14},{13,9},{14,10},{15,13... | collective-permute-start | bytes 1572872 | tf_op jit(solution)/shard_map/return_short_2/ppermute | solution.py:326
  75.0 11.0 %collective-permute-start.28 = (bf16[64,4096]{1,0:T(8,128)(2,1)S(1)}, bf16[64,4096]{1,0:T(8,128)(2,1)S(1)}, u32[]{:S(2)}, u32[]{:S(2)}) collective-permute-start(bf16[64,4096]{1,0:T(8,128)(2,1)S(1)} %step_sum.8), channel_id=1, source_target_pairs={{0,4},{1,3},{4,8},{5,1},{8,12},{9,5},{12,14},{13,9},{14,10},{15,13... | collective-permute-start | bytes 1572872 | tf_op jit(solution)/shard_map/return_long_3/ppermute | solution.py:326
  81.1 4.9 %collective-permute-start.27 = (bf16[64,4096]{1,0:T(8,128)(2,1)S(1)}, bf16[64,4096]{1,0:T(8,128)(2,1)S(1)}, u32[]{:S(2)}, u32[]{:S(2)}) collective-permute-start(bf16[64,4096]{1,0:T(8,128)(2,1)S(1)} %get-tuple-element.80), channel_id=1, source_target_pairs={{0,1},{1,0},{2,3},{3,2},{4,5},{5,4},{6,7},{7,6},{8,9},{9,8},{10,11... | collective-permute-start | bytes 1572872 | tf_op jit(solution)/shard_map/swap_out_2/ppermute | solution.py:326
  81.1 7.2 %collective-permute-start.1 = (bf16[64,4096]{1,0:T(8,128)(2,1)S(1)}, bf16[64,4096]{1,0:T(8,128)(2,1)S(1)}, u32[]{:S(2)}, u32[]{:S(2)}) collective-permute-start(bf16[64,4096]{1,0:T(8,128)(2,1)S(1)} %get-tuple-element.49), channel_id=1, source_target_pairs={{0,1},{1,0},{2,3},{3,2},{4,5},{5,4},{6,7},{7,6},{8,9},{9,8},{10,11... | collective-permute-start | bytes 1572872 | tf_op jit(solution)/shard_map/swap_out_0/ppermute | solution.py:326
  81.8 7.0 %collective-permute-start.23 = (bf16[32,4096]{1,0:T(8,128)(2,1)S(1)}, bf16[32,4096]{1,0:T(8,128)(2,1)S(1)}, u32[]{:S(2)}, u32[]{:S(2)}) collective-permute-start(bf16[32,4096]{1,0:T(8,128)(2,1)S(1)} %get-tuple-element.76), channel_id=1, source_target_pairs={{0,4},{1,3},{4,8},{5,1},{8,12},{9,5},{12,14},{13,9},{14,10},{15,13... | collective-permute-start | bytes 786440 | tf_op jit(solution)/shard_map/return_short_1/ppermute | solution.py:326
  83.4 7.8 %collective-permute-start.24 = (bf16[32,4096]{1,0:T(8,128)(2,1)S(1)}, bf16[32,4096]{1,0:T(8,128)(2,1)S(1)}, u32[]{:S(2)}, u32[]{:S(2)}) collective-permute-start(bf16[32,4096]{1,0:T(8,128)(2,1)S(1)} %get-tuple-element.77), channel_id=1, source_target_pairs={{0,5},{1,2},{4,9},{5,0},{8,13},{9,4},{12,15},{13,8},{14,11},{15,12... | collective-permute-start | bytes 786440 | tf_op jit(solution)/shard_map/return_short_1/ppermute | solution.py:326
  86.0 11.2 %collective-permute-start.25 = (bf16[64,4096]{1,0:T(8,128)(2,1)S(1)}, bf16[64,4096]{1,0:T(8,128)(2,1)S(1)}, u32[]{:S(2)}, u32[]{:S(2)}) collective-permute-start(bf16[64,4096]{1,0:T(8,128)(2,1)S(1)} %get-tuple-element.78), channel_id=1, source_target_pairs={{0,1},{1,0},{2,3},{3,2},{4,5},{5,4},{6,7},{7,6},{8,9},{9,8},{10,11... | collective-permute-start | bytes 1572872 | tf_op jit(solution)/shard_map/swap_out_1/ppermute | solution.py:326
  86.2 11.0 %collective-permute-start.29 = (bf16[64,4096]{1,0:T(8,128)(2,1)S(1)}, bf16[64,4096]{1,0:T(8,128)(2,1)S(1)}, u32[]{:S(2)}, u32[]{:S(2)}) collective-permute-start(bf16[64,4096]{1,0:T(8,128)(2,1)S(1)} %step_sum.9), channel_id=1, source_target_pairs={{0,4},{1,3},{4,8},{5,1},{8,12},{9,5},{12,14},{13,9},{14,10},{15,13... | collective-permute-start | bytes 1572872 | tf_op jit(solution)/shard_map/return_long_2/ppermute | solution.py:326
  97.4 5.9 %collective-permute-start.30 = (bf16[32,4096]{1,0:T(8,128)(2,1)S(1)}, bf16[32,4096]{1,0:T(8,128)(2,1)S(1)}, u32[]{:S(2)}, u32[]{:S(2)}) collective-permute-start(bf16[32,4096]{1,0:T(8,128)(2,1)S(1)} %get-tuple-element.83), channel_id=1, source_target_pairs={{0,5},{1,2},{4,9},{5,0},{8,13},{9,4},{12,15},{13,8},{14,11},{15,12... | collective-permute-start | bytes 786440 | tf_op jit(solution)/shard_map/return_long_1/ppermute | solution.py:326
  98.5 8.2 %collective-permute-start.31 = (bf16[32,4096]{1,0:T(8,128)(2,1)S(1)}, bf16[32,4096]{1,0:T(8,128)(2,1)S(1)}, u32[]{:S(2)}, u32[]{:S(2)}) collective-permute-start(bf16[32,4096]{1,0:T(8,128)(2,1)S(1)} %get-tuple-element.84), channel_id=1, source_target_pairs={{0,4},{1,3},{4,8},{5,1},{8,12},{9,5},{12,14},{13,9},{14,10},{15,13... | collective-permute-start | bytes 786440 | tf_op jit(solution)/shard_map/return_long_1/ppermute | solution.py:326
  (2 other events, 24.3 us)

commit v14 on v13

--- a/solution.py
+++ b/solution.py
@@ -370,9 +370,10 @@
 
     for distance in range(2, reach - 1):
         last = run([(distance, "short")], last)
-    run([(reach - 1, "short")], last)
+    run([(reach - 1, "short")], last, 2)
+    second = run([(reach - 1, "long")], last, 2)
     short, totals = step(reach - 1, "short", ())
-    run([(reach, "long"), (reach - 1, "long")], totals)
+    run([(reach, "long")], [*totals, *second])
     given[reach, "long"] = after(given[reach, "long"], *short)
     long, totals = step(reach, "long", ())
     for distance in range(reach - 1, 0, -1):

time: 108 us -> 106 us (0.981)
  starting transfers between devices: 31.3 us -> 28.7 us
  Pallas kernels: 38.7 us -> 40.1 us
    ppermute x32, starting transfers between devices: 31.3 us -> 28.7 us  [send(): return lax.ppermute(x, 'expert', perm)]
    pallas_call x6 -> x7, Pallas kernels: 28.6 us -> 30.1 us  [expert_part(): pl.pallas_call(functools.partial(expert_kernel, len(blocks)), in_specs=[V...]
  transfers between devices with their start and end apart: 32 -> 32, of which waited for: 14 -> 11; matrix products, arithmetic and copies ran while one was open for 0% -> 0% of each run, Pallas kernels for 34% -> 35%
where the time goes in v14:
time: 106 us
  Pallas kernels  40.1 us (38%)
  waiting for transfers between devices  37.2 us (35%)
  starting transfers between devices  28.7 us (27%)
    ppermute x32, waiting for transfers between devices, send(): return lax.ppermute(x, 'expert', perm)  37.2 us
    pallas_call x7, Pallas kernels, expert_part(): pl.pallas_call(functools.partial(expert_kernel, len(blocks)), in_specs=[V...  30.1 us
    ppermute x32, starting transfers between devices, send(): return lax.ppermute(x, 'expert', perm)  28.7 us
    pallas_call x1, Pallas kernels, keep(): pl.pallas_call(keep_kernel, in_specs=[ANYWHERE] * 2, out_specs=[VMEM] * 2...  6.38 us
  transfers between devices with their start and end apart: 32, of which 11 were waited for; matrix products, arithmetic and copies ran while one was open for 0% of the time, Pallas kernels for 35%

profile of v14, /device:TPU:0, one launch (start us, length us, event | category | flops | bytes accessed | tf_op | source)
XLA Modules:
  0.0 106.3 jit_solution(5024394121650612854)
XLA Ops:
  0.0 1.3 %pack.1 = (bf16[64,4224]{1,0:T(8,128)(2,1)S(1)}, bf16[64,4224]{1,0:T(8,128)(2,1)S(1)}) custom-call(s32[1]{0:T(128)} %bitcast.core, bf16[64,4096]{1,0:T(8,128)(2,1)} %tokens.1, s32[8,64]{1,0:T(8,128)} %bitcast.7, s32[8,64]{1,0:T(8,128)} %bitcast.8), custom_call_target="tpu_custom_call" | custom-call | tf_op jit(solution)/shard_map/pack/pallas_call | solution.py:64
  1.8 2.6 %collective-permute-start.2 = (bf16[64,4224]{1,0:T(8,128)(2,1)S(1)}, bf16[64,4224]{1,0:T(8,128)(2,1)S(1)}, u32[]{:S(2)}, u32[]{:S(2)}) collective-permute-start(bf16[64,4224]{1,0:T(8,128)(2,1)S(1)} %get-tuple-element.45.refs_0_), channel_id=1, source_target_pairs={{0,4},{1,3},{4,8},{5,1},{8,12},{9,5},{12,14},{13,9},{14,10},{15,13... | collective-permute-start | bytes 1622024 | tf_op jit(solution)/shard_map/gather_long_1/ppermute | solution.py:326
  5.7 6.4 %keep.1 = (bf16[4096,1536]{1,0:T(8,128)(2,1)S(1)}, bf16[768,4096]{1,0:T(8,128)(2,1)S(1)}) custom-call(bf16[4096,1536]{1,0:T(8,128)(2,1)} %bitcast.5, bf16[768,4096]{1,0:T(8,128)(2,1)} %bitcast.6), custom_call_target="tpu_custom_call" | custom-call | bytes 18874368 | tf_op jit(solution)/shard_map/keep/pallas_call | solution.py:88
  12.2 3.9 %expert.7 = (bf16[64,4096]{1,0:T(8,128)(2,1)S(1)}, bf16[64,4096]{1,0:T(8,128)(2,1)S(1)}) custom-call(bf16[64,4224]{1,0:T(8,128)(2,1)S(1)} %get-tuple-element.45.refs_0_, bf16[64,4224]{1,0:T(8,128)(2,1)S(1)} %collective-permute-done.refs_1_, f32[1,128]{1,0:T(1,128)S(1)} %compare_select_fusion.1.refs_2_.refs_4_, f32[1,1536]{1,0:T(1,128)S(1)} %copy-done.1, ...), custom_call_target="tpu_custom_call" | custom-call | flops 4831838208 | tf_op jit(solution)/shard_map/expert/pallas_call | solution.py:146
  16.1 1.4 %collective-permute-done.3.cross = bf16[64,4224]{1,0:T(8,128)(2,1)S(1)} collective-permute-done((bf16[64,4224]{1,0:T(8,128)(2,1)S(1)}, bf16[64,4224]{1,0:T(8,128)(2,1)S(1)}, u32[]{:S(2)}, u32[]{:S(2)}) %collective-permute-start.3) | collective-permute-done | bytes 540704 | tf_op jit(solution)/shard_map/gather_long_1/ppermute | solution.py:326
  18.2 2.1 %collective-permute-start.7 = (bf16[64,4224]{1,0:T(8,128)(2,1)S(1)}, bf16[64,4224]{1,0:T(8,128)(2,1)S(1)}, u32[]{:S(2)}, u32[]{:S(2)}) collective-permute-start(bf16[64,4224]{1,0:T(8,128)(2,1)S(1)} %get-tuple-element.55.refs_3_), channel_id=1, source_target_pairs={{0,4},{1,3},{4,8},{5,1},{8,12},{9,5},{12,14},{13,9},{14,10},{15,13... | collective-permute-start | bytes 1622024 | tf_op jit(solution)/shard_map/gather_short_2/ppermute | solution.py:326
  20.3 1.6 %collective-permute-start.14 = (bf16[64,4224]{1,0:T(8,128)(2,1)S(1)}, bf16[64,4224]{1,0:T(8,128)(2,1)S(1)}, u32[]{:S(2)}, u32[]{:S(2)}) collective-permute-start(bf16[64,4224]{1,0:T(8,128)(2,1)S(1)} %get-tuple-element.53.refs_2_), channel_id=1, source_target_pairs={{0,4},{1,3},{4,8},{5,1},{8,12},{9,5},{12,14},{13,9},{14,10},{15,13... | collective-permute-start | bytes 1622024 | tf_op jit(solution)/shard_map/gather_long_2/ppermute | solution.py:326
  21.8 6.4 %expert.8 = (bf16[64,4096]{1,0:T(8,128)(2,1)S(1)}, bf16[64,4096]{1,0:T(8,128)(2,1)S(1)}, bf16[64,4096]{1,0:T(8,128)(2,1)S(1)}, bf16[64,4096]{1,0:T(8,128)(2,1)S(1)}) custom-call(bf16[64,4224]{1,0:T(8,128)(2,1)S(1)} %collective-permute-done.4.refs_0_, bf16[64,4224]{1,0:T(8,128)(2,1)S(1)} %collective-permute-done.5.refs_1_, ...), custom_call_target="tpu_custom_call" | custom-call | flops 9663676416 | tf_op jit(solution)/shard_map/expert/pallas_call | solution.py:146
  28.4 1.6 %collective-permute-start.10 = (bf16[64,4224]{1,0:T(8,128)(2,1)S(1)}, bf16[64,4224]{1,0:T(8,128)(2,1)S(1)}, u32[]{:S(2)}, u32[]{:S(2)}) collective-permute-start(bf16[64,4224]{1,0:T(8,128)(2,1)S(1)} %collective-permute-done.7.refs_1_), channel_id=1, source_target_pairs={{0,4},{1,3},{4,8},{5,1},{8,12},{9,5},{12,14},{13,9},{14,10},{15,13... | collective-permute-start | bytes 1622024 | tf_op jit(solution)/shard_map/gather_short_3/ppermute | solution.py:326
  30.0 3.3 %collective-permute-done.14.refs_1_ = bf16[64,4224]{1,0:T(8,128)(2,1)S(1)} collective-permute-done((bf16[64,4224]{1,0:T(8,128)(2,1)S(1)}, bf16[64,4224]{1,0:T(8,128)(2,1)S(1)}, u32[]{:S(2)}, u32[]{:S(2)}) %collective-permute-start.14) | collective-permute-done | bytes 540704 | tf_op jit(solution)/shard_map/gather_long_2/ppermute | solution.py:326
  33.3 2.1 %collective-permute-start.15 = (bf16[64,4224]{1,0:T(8,128)(2,1)S(1)}, bf16[64,4224]{1,0:T(8,128)(2,1)S(1)}, u32[]{:S(2)}, u32[]{:S(2)}) collective-permute-start(bf16[64,4224]{1,0:T(8,128)(2,1)S(1)} %collective-permute-done.14.refs_1_), channel_id=1, source_target_pairs={{0,4},{1,3},{4,8},{5,1},{8,12},{9,5},{12,14},{13,9},{14,10},{15,13... | collective-permute-start | bytes 1622024 | tf_op jit(solution)/shard_map/gather_long_3/ppermute | solution.py:326
  35.4 3.9 %expert.9 = (bf16[64,4096]{1,0:T(8,128)(2,1)S(1)}, bf16[64,4096]{1,0:T(8,128)(2,1)S(1)}) custom-call(bf16[64,4224]{1,0:T(8,128)(2,1)S(1)} %collective-permute-done.8.refs_0_, bf16[64,4224]{1,0:T(8,128)(2,1)S(1)} %collective-permute-done.7.refs_1_, f32[1,128]{1,0:T(1,128)S(1)} %compare_select_fusion.1.refs_2_.refs_4_, f32[1,1536]{1,0:T(1,128)S(1)} %copy-done.1, ...), custom_call_target="tpu_custom_call" | custom-call | flops 4831838208 | tf_op jit(solution)/shard_map/expert/pallas_call | solution.py:146
  39.5 5.5 %collective-permute-done.15.refs_1_ = bf16[64,4224]{1,0:T(8,128)(2,1)S(1)} collective-permute-done((bf16[64,4224]{1,0:T(8,128)(2,1)S(1)}, bf16[64,4224]{1,0:T(8,128)(2,1)S(1)}, u32[]{:S(2)}, u32[]{:S(2)}) %collective-permute-start.15) | collective-permute-done | bytes 540704 | tf_op jit(solution)/shard_map/gather_long_3/ppermute | solution.py:326
  44.9 2.1 %collective-permute-start.16 = (bf16[64,4224]{1,0:T(8,128)(2,1)S(1)}, bf16[64,4224]{1,0:T(8,128)(2,1)S(1)}, u32[]{:S(2)}, u32[]{:S(2)}) collective-permute-start(bf16[64,4224]{1,0:T(8,128)(2,1)S(1)} %collective-permute-done.15.refs_1_), channel_id=1, source_target_pairs={{0,4},{1,3},{4,8},{5,1},{8,12},{9,5},{12,14},{13,9},{14,10},{15,13... | collective-permute-start | bytes 1622024 | tf_op jit(solution)/shard_map/gather_long_4/ppermute | solution.py:326
  47.0 4.0 %expert.10 = (bf16[64,4096]{1,0:T(8,128)(2,1)S(1)}, bf16[64,4096]{1,0:T(8,128)(2,1)S(1)}) custom-call(bf16[64,4224]{1,0:T(8,128)(2,1)S(1)} %collective-permute-done.11.refs_0_, bf16[64,4224]{1,0:T(8,128)(2,1)S(1)} %collective-permute-done.10.refs_1_, f32[1,128]{1,0:T(1,128)S(1)} %compare_select_fusion.1.refs_2_.refs_4_, f32[1,1536]{1,0:T(1,128)S(1)} %copy-done.1, ...), custom_call_target="tpu_custom_call" | custom-call | flops 4831838208 | tf_op jit(solution)/shard_map/expert/pallas_call | solution.py:146
  51.2 3.9 %expert.11 = (bf16[64,4096]{1,0:T(8,128)(2,1)S(1)}, bf16[64,4096]{1,0:T(8,128)(2,1)S(1)}) custom-call(bf16[64,4224]{1,0:T(8,128)(2,1)S(1)} %collective-permute-done.17.refs_0_, bf16[64,4224]{1,0:T(8,128)(2,1)S(1)} %collective-permute-done.15.refs_1_, f32[1,128]{1,0:T(1,128)S(1)} %compare_select_fusion.1.refs_2_.refs_4_, f32[1,1536]{1,0:T(1,128)S(1)} %copy-done.1, ...), custom_call_target="tpu_custom_call" | custom-call | flops 4831838208 | tf_op jit(solution)/shard_map/expert/pallas_call | solution.py:146
  55.7 1.6 %collective-permute-start.13 = (bf16[64,4096]{1,0:T(8,128)(2,1)S(1)}, bf16[64,4096]{1,0:T(8,128)(2,1)S(1)}, u32[]{:S(2)}, u32[]{:S(2)}) collective-permute-start(bf16[64,4096]{1,0:T(8,128)(2,1)S(1)} %step_sum.5), channel_id=1, source_target_pairs={{0,4},{1,3},{4,8},{5,1},{8,12},{9,5},{12,14},{13,9},{14,10},{15,13... | collective-permute-start | bytes 1572872 | tf_op jit(solution)/shard_map/return_short_3/ppermute | solution.py:326
  57.3 4.0 %expert.12 = (bf16[64,4096]{1,0:T(8,128)(2,1)S(1)}, bf16[64,4096]{1,0:T(8,128)(2,1)S(1)}) custom-call(bf16[64,4224]{1,0:T(8,128)(2,1)S(1)} %collective-permute-done.18.refs_0_, bf16[64,4224]{1,0:T(8,128)(2,1)S(1)} %collective-permute-done.16.refs_1_, f32[1,128]{1,0:T(1,128)S(1)} %compare_select_fusion.1.refs_2_.refs_4_, f32[1,1536]{1,0:T(1,128)S(1)} %copy-done.1, ...), custom_call_target="tpu_custom_call" | custom-call | flops 4831838208 | tf_op jit(solution)/shard_map/expert/pallas_call | solution.py:146
  62.2 2.7 %collective-permute-done.13.refs_2_ = bf16[64,4096]{1,0:T(8,128)(2,1)S(1)} collective-permute-done((bf16[64,4096]{1,0:T(8,128)(2,1)S(1)}, bf16[64,4096]{1,0:T(8,128)(2,1)S(1)}, u32[]{:S(2)}, u32[]{:S(2)}) %collective-permute-start.13) | collective-permute-done | bytes 524320 | tf_op jit(solution)/shard_map/return_short_3/ppermute | solution.py:326
  65.0 1.7 %collective-permute-start.22 = (bf16[64,4096]{1,0:T(8,128)(2,1)S(1)}, bf16[64,4096]{1,0:T(8,128)(2,1)S(1)}, u32[]{:S(2)}, u32[]{:S(2)}) collective-permute-start(bf16[64,4096]{1,0:T(8,128)(2,1)S(1)} %step_sum.6), channel_id=1, source_target_pairs={{0,4},{1,3},{4,8},{5,1},{8,12},{9,5},{12,14},{13,9},{14,10},{15,13... | collective-permute-start | bytes 1572872 | tf_op jit(solution)/shard_map/return_long_4/ppermute | solution.py:326
  67.4 1.6 %collective-permute-start.20 = (bf16[64,4096]{1,0:T(8,128)(2,1)S(1)}, bf16[64,4096]{1,0:T(8,128)(2,1)S(1)}, u32[]{:S(2)}, u32[]{:S(2)}) collective-permute-start(bf16[64,4096]{1,0:T(8,128)(2,1)S(1)} %step_sum.7), channel_id=1, source_target_pairs={{0,4},{1,3},{4,8},{5,1},{8,12},{9,5},{12,14},{13,9},{14,10},{15,13... | collective-permute-start | bytes 1572872 | tf_op jit(solution)/shard_map/return_short_2/ppermute | solution.py:326
  69.0 5.3 %collective-permute-done.22.refs_2_ = bf16[64,4096]{1,0:T(8,128)(2,1)S(1)} collective-permute-done((bf16[64,4096]{1,0:T(8,128)(2,1)S(1)}, bf16[64,4096]{1,0:T(8,128)(2,1)S(1)}, u32[]{:S(2)}, u32[]{:S(2)}) %collective-permute-start.22) | collective-permute-done | bytes 524320 | tf_op jit(solution)/shard_map/return_long_4/ppermute | solution.py:326
  74.5 1.7 %collective-permute-start.28 = (bf16[64,4096]{1,0:T(8,128)(2,1)S(1)}, bf16[64,4096]{1,0:T(8,128)(2,1)S(1)}, u32[]{:S(2)}, u32[]{:S(2)}) collective-permute-start(bf16[64,4096]{1,0:T(8,128)(2,1)S(1)} %step_sum.8), channel_id=1, source_target_pairs={{0,4},{1,3},{4,8},{5,1},{8,12},{9,5},{12,14},{13,9},{14,10},{15,13... | collective-permute-start | bytes 1572872 | tf_op jit(solution)/shard_map/return_long_3/ppermute | solution.py:326
  76.1 3.9 %expert.13 = (bf16[64,4096]{1,0:T(8,128)(2,1)S(1)}, bf16[64,4096]{1,0:T(8,128)(2,1)S(1)}) custom-call(bf16[64,4224]{1,0:T(8,128)(2,1)S(1)} %collective-permute-done.26.refs_0_, bf16[64,4224]{1,0:T(8,128)(2,1)S(1)} %collective-permute-done.14.refs_1_, f32[1,128]{1,0:T(1,128)S(1)} %compare_select_fusion.1.refs_2_.refs_4_, f32[1,1536]{1,0:T(1,128)S(1)} %copy-done.1, ...), custom_call_target="tpu_custom_call" | custom-call | flops 4831838208 | tf_op jit(solution)/shard_map/expert/pallas_call | solution.py:146
  80.9 1.6 %collective-permute-start.23 = (bf16[32,4096]{1,0:T(8,128)(2,1)S(1)}, bf16[32,4096]{1,0:T(8,128)(2,1)S(1)}, u32[]{:S(2)}, u32[]{:S(2)}) collective-permute-start(bf16[32,4096]{1,0:T(8,128)(2,1)S(1)} %get-tuple-element.76), channel_id=1, source_target_pairs={{0,4},{1,3},{4,8},{5,1},{8,12},{9,5},{12,14},{13,9},{14,10},{15,13... | collective-permute-start | bytes 786440 | tf_op jit(solution)/shard_map/return_short_1/ppermute | solution.py:326
  82.5 3.0 %collective-permute-done.28.refs_2_ = bf16[64,4096]{1,0:T(8,128)(2,1)S(1)} collective-permute-done((bf16[64,4096]{1,0:T(8,128)(2,1)S(1)}, bf16[64,4096]{1,0:T(8,128)(2,1)S(1)}, u32[]{:S(2)}, u32[]{:S(2)}) %collective-permute-start.28) | collective-permute-done | bytes 524320 | tf_op jit(solution)/shard_map/return_long_3/ppermute | solution.py:326
  85.7 1.7 %collective-permute-start.29 = (bf16[64,4096]{1,0:T(8,128)(2,1)S(1)}, bf16[64,4096]{1,0:T(8,128)(2,1)S(1)}, u32[]{:S(2)}, u32[]{:S(2)}) collective-permute-start(bf16[64,4096]{1,0:T(8,128)(2,1)S(1)} %step_sum.9), channel_id=1, source_target_pairs={{0,4},{1,3},{4,8},{5,1},{8,12},{9,5},{12,14},{13,9},{14,10},{15,13... | collective-permute-start | bytes 1572872 | tf_op jit(solution)/shard_map/return_long_2/ppermute | solution.py:326
  88.3 1.9 %collective-permute-done.24.short_cross = bf16[32,4096]{1,0:T(8,128)(2,1)S(1)} collective-permute-done((bf16[32,4096]{1,0:T(8,128)(2,1)S(1)}, bf16[32,4096]{1,0:T(8,128)(2,1)S(1)}, u32[]{:S(2)}, u32[]{:S(2)}) %collective-permute-start.24) | collective-permute-done | bytes 262176 | tf_op jit(solution)/shard_map/return_short_1/ppermute | solution.py:326
  90.4 6.3 %collective-permute-done.29.refs_2_ = bf16[64,4096]{1,0:T(8,128)(2,1)S(1)} collective-permute-done((bf16[64,4096]{1,0:T(8,128)(2,1)S(1)}, bf16[64,4096]{1,0:T(8,128)(2,1)S(1)}, u32[]{:S(2)}, u32[]{:S(2)}) %collective-permute-start.29) | collective-permute-done | bytes 524320 | tf_op jit(solution)/shard_map/return_long_2/ppermute | solution.py:326
  97.0 1.7 %collective-permute-start.31 = (bf16[32,4096]{1,0:T(8,128)(2,1)S(1)}, bf16[32,4096]{1,0:T(8,128)(2,1)S(1)}, u32[]{:S(2)}, u32[]{:S(2)}) collective-permute-start(bf16[32,4096]{1,0:T(8,128)(2,1)S(1)} %get-tuple-element.84), channel_id=1, source_target_pairs={{0,4},{1,3},{4,8},{5,1},{8,12},{9,5},{12,14},{13,9},{14,10},{15,13... | collective-permute-start | bytes 786440 | tf_op jit(solution)/shard_map/return_long_1/ppermute | solution.py:326
  98.7 4.1 %collective-permute-done.30.long_cross = bf16[32,4096]{1,0:T(8,128)(2,1)S(1)} collective-permute-done((bf16[32,4096]{1,0:T(8,128)(2,1)S(1)}, bf16[32,4096]{1,0:T(8,128)(2,1)S(1)}, u32[]{:S(2)}, u32[]{:S(2)}) %collective-permute-start.30) | collective-permute-done | bytes 262176 | tf_op jit(solution)/shard_map/return_long_1/ppermute | solution.py:326
  102.8 2.7 %collective-permute-done.31.long_same = bf16[32,4096]{1,0:T(8,128)(2,1)S(1)} collective-permute-done((bf16[32,4096]{1,0:T(8,128)(2,1)S(1)}, bf16[32,4096]{1,0:T(8,128)(2,1)S(1)}, u32[]{:S(2)}, u32[]{:S(2)}) %collective-permute-start.31) | collective-permute-done | bytes 262176 | tf_op jit(solution)/shard_map/return_long_1/ppermute | solution.py:326
  (56 shorter events, 8.6 us)
Async XLA Ops:
  1.3 10.9 %collective-permute-start = (bf16[64,4224]{1,0:T(8,128)(2,1)S(1)}, bf16[64,4224]{1,0:T(8,128)(2,1)S(1)}, u32[]{:S(2)}, u32[]{:S(2)}) collective-permute-start(bf16[64,4224]{1,0:T(8,128)(2,1)S(1)} %get-tuple-element.45.refs_0_), channel_id=1, source_target_pairs={{0,1},{1,0},{2,3},{3,2},{4,5},{5,4},{6,7},{7,6},{8,9},{9,8},{10,11... | collective-permute-start | bytes 1622024 | tf_op jit(solution)/shard_map/swap_in_0/ppermute | solution.py:326
  1.8 14.3 %collective-permute-start.2 = (bf16[64,4224]{1,0:T(8,128)(2,1)S(1)}, bf16[64,4224]{1,0:T(8,128)(2,1)S(1)}, u32[]{:S(2)}, u32[]{:S(2)}) collective-permute-start(bf16[64,4224]{1,0:T(8,128)(2,1)S(1)} %get-tuple-element.45.refs_0_), channel_id=1, source_target_pairs={{0,4},{1,3},{4,8},{5,1},{8,12},{9,5},{12,14},{13,9},{14,10},{15,13... | collective-permute-start | bytes 1622024 | tf_op jit(solution)/shard_map/gather_long_1/ppermute | solution.py:326
  4.5 13.1 %collective-permute-start.3 = (bf16[64,4224]{1,0:T(8,128)(2,1)S(1)}, bf16[64,4224]{1,0:T(8,128)(2,1)S(1)}, u32[]{:S(2)}, u32[]{:S(2)}) collective-permute-start(bf16[64,4224]{1,0:T(8,128)(2,1)S(1)} %get-tuple-element.51), channel_id=1, source_target_pairs={{0,3},{1,4},{4,1},{5,8},{8,5},{9,12},{12,9},{13,14},{14,13},{15,10... | collective-permute-start | bytes 1622024 | tf_op jit(solution)/shard_map/gather_long_1/ppermute | solution.py:326
  17.6 4.2 %collective-permute-start.4 = (bf16[64,4224]{1,0:T(8,128)(2,1)S(1)}, bf16[64,4224]{1,0:T(8,128)(2,1)S(1)}, u32[]{:S(2)}, u32[]{:S(2)}) collective-permute-start(bf16[64,4224]{1,0:T(8,128)(2,1)S(1)} %get-tuple-element.53.refs_2_), channel_id=1, source_target_pairs={{0,1},{1,0},{2,3},{3,2},{4,5},{5,4},{6,7},{7,6},{8,9},{9,8},{10,11... | collective-permute-start | bytes 1622024 | tf_op jit(solution)/shard_map/swap_in_1/ppermute | solution.py:326
  17.7 4.2 %collective-permute-start.5 = (bf16[64,4224]{1,0:T(8,128)(2,1)S(1)}, bf16[64,4224]{1,0:T(8,128)(2,1)S(1)}, u32[]{:S(2)}, u32[]{:S(2)}) collective-permute-start(bf16[64,4224]{1,0:T(8,128)(2,1)S(1)} %get-tuple-element.55.refs_3_), channel_id=1, source_target_pairs={{0,1},{1,0},{2,3},{3,2},{4,5},{5,4},{6,7},{7,6},{8,9},{9,8},{10,11... | collective-permute-start | bytes 1622024 | tf_op jit(solution)/shard_map/swap_in_1/ppermute | solution.py:326
  18.2 10.1 %collective-permute-start.7 = (bf16[64,4224]{1,0:T(8,128)(2,1)S(1)}, bf16[64,4224]{1,0:T(8,128)(2,1)S(1)}, u32[]{:S(2)}, u32[]{:S(2)}) collective-permute-start(bf16[64,4224]{1,0:T(8,128)(2,1)S(1)} %get-tuple-element.55.refs_3_), channel_id=1, source_target_pairs={{0,4},{1,3},{4,8},{5,1},{8,12},{9,5},{12,14},{13,9},{14,10},{15,13... | collective-permute-start | bytes 1622024 | tf_op jit(solution)/shard_map/gather_short_2/ppermute | solution.py:326
  20.3 13.1 %collective-permute-start.14 = (bf16[64,4224]{1,0:T(8,128)(2,1)S(1)}, bf16[64,4224]{1,0:T(8,128)(2,1)S(1)}, u32[]{:S(2)}, u32[]{:S(2)}) collective-permute-start(bf16[64,4224]{1,0:T(8,128)(2,1)S(1)} %get-tuple-element.53.refs_2_), channel_id=1, source_target_pairs={{0,4},{1,3},{4,8},{5,1},{8,12},{9,5},{12,14},{13,9},{14,10},{15,13... | collective-permute-start | bytes 1622024 | tf_op jit(solution)/shard_map/gather_long_2/ppermute | solution.py:326
  28.3 7.1 %collective-permute-start.8 = (bf16[64,4224]{1,0:T(8,128)(2,1)S(1)}, bf16[64,4224]{1,0:T(8,128)(2,1)S(1)}, u32[]{:S(2)}, u32[]{:S(2)}) collective-permute-start(bf16[64,4224]{1,0:T(8,128)(2,1)S(1)} %collective-permute-done.7.refs_1_), channel_id=1, source_target_pairs={{0,1},{1,0},{2,3},{3,2},{4,5},{5,4},{6,7},{7,6},{8,9},{9,8},{10,11... | collective-permute-start | bytes 1622024 | tf_op jit(solution)/shard_map/swap_in_2/ppermute | solution.py:326
  28.4 11.0 %collective-permute-start.10 = (bf16[64,4224]{1,0:T(8,128)(2,1)S(1)}, bf16[64,4224]{1,0:T(8,128)(2,1)S(1)}, u32[]{:S(2)}, u32[]{:S(2)}) collective-permute-start(bf16[64,4224]{1,0:T(8,128)(2,1)S(1)} %collective-permute-done.7.refs_1_), channel_id=1, source_target_pairs={{0,4},{1,3},{4,8},{5,1},{8,12},{9,5},{12,14},{13,9},{14,10},{15,13... | collective-permute-start | bytes 1622024 | tf_op jit(solution)/shard_map/gather_short_3/ppermute | solution.py:326
  33.3 11.6 %collective-permute-start.15 = (bf16[64,4224]{1,0:T(8,128)(2,1)S(1)}, bf16[64,4224]{1,0:T(8,128)(2,1)S(1)}, u32[]{:S(2)}, u32[]{:S(2)}) collective-permute-start(bf16[64,4224]{1,0:T(8,128)(2,1)S(1)} %collective-permute-done.14.refs_1_), channel_id=1, source_target_pairs={{0,4},{1,3},{4,8},{5,1},{8,12},{9,5},{12,14},{13,9},{14,10},{15,13... | collective-permute-start | bytes 1622024 | tf_op jit(solution)/shard_map/gather_long_3/ppermute | solution.py:326
  39.4 7.6 %collective-permute-start.11 = (bf16[64,4224]{1,0:T(8,128)(2,1)S(1)}, bf16[64,4224]{1,0:T(8,128)(2,1)S(1)}, u32[]{:S(2)}, u32[]{:S(2)}) collective-permute-start(bf16[64,4224]{1,0:T(8,128)(2,1)S(1)} %collective-permute-done.10.refs_1_), channel_id=1, source_target_pairs={{0,1},{1,0},{2,3},{3,2},{4,5},{5,4},{6,7},{7,6},{8,9},{9,8},{10,11... | collective-permute-start | bytes 1622024 | tf_op jit(solution)/shard_map/swap_in_3/ppermute | solution.py:326
  44.9 6.3 %collective-permute-start.17 = (bf16[64,4224]{1,0:T(8,128)(2,1)S(1)}, bf16[64,4224]{1,0:T(8,128)(2,1)S(1)}, u32[]{:S(2)}, u32[]{:S(2)}) collective-permute-start(bf16[64,4224]{1,0:T(8,128)(2,1)S(1)} %collective-permute-done.15.refs_1_), channel_id=1, source_target_pairs={{0,1},{1,0},{2,3},{3,2},{4,5},{5,4},{6,7},{7,6},{8,9},{9,8},{10,11... | collective-permute-start | bytes 1622024 | tf_op jit(solution)/shard_map/swap_in_3/ppermute | solution.py:326
  44.9 10.4 %collective-permute-start.16 = (bf16[64,4224]{1,0:T(8,128)(2,1)S(1)}, bf16[64,4224]{1,0:T(8,128)(2,1)S(1)}, u32[]{:S(2)}, u32[]{:S(2)}) collective-permute-start(bf16[64,4224]{1,0:T(8,128)(2,1)S(1)} %collective-permute-done.15.refs_1_), channel_id=1, source_target_pairs={{0,4},{1,3},{4,8},{5,1},{8,12},{9,5},{12,14},{13,9},{14,10},{15,13... | collective-permute-start | bytes 1622024 | tf_op jit(solution)/shard_map/gather_long_4/ppermute | solution.py:326
  51.0 4.2 %collective-permute-start.12 = (bf16[64,4096]{1,0:T(8,128)(2,1)S(1)}, bf16[64,4096]{1,0:T(8,128)(2,1)S(1)}, u32[]{:S(2)}, u32[]{:S(2)}) collective-permute-start(bf16[64,4096]{1,0:T(8,128)(2,1)S(1)} %get-tuple-element.64), channel_id=1, source_target_pairs={{0,1},{1,0},{2,3},{3,2},{4,5},{5,4},{6,7},{7,6},{8,9},{9,8},{10,11... | collective-permute-start | bytes 1572872 | tf_op jit(solution)/shard_map/swap_out_3/ppermute | solution.py:326
  55.3 2.0 %collective-permute-start.18 = (bf16[64,4224]{1,0:T(8,128)(2,1)S(1)}, bf16[64,4224]{1,0:T(8,128)(2,1)S(1)}, u32[]{:S(2)}, u32[]{:S(2)}) collective-permute-start(bf16[64,4224]{1,0:T(8,128)(2,1)S(1)} %collective-permute-done.16.refs_1_), channel_id=1, source_target_pairs={{0,1},{1,0},{2,3},{3,2},{4,5},{5,4},{6,7},{7,6},{8,9},{9,8},{10,11... | collective-permute-start | bytes 1622024 | tf_op jit(solution)/shard_map/swap_in_4/ppermute | solution.py:326
  55.7 9.2 %collective-permute-start.13 = (bf16[64,4096]{1,0:T(8,128)(2,1)S(1)}, bf16[64,4096]{1,0:T(8,128)(2,1)S(1)}, u32[]{:S(2)}, u32[]{:S(2)}) collective-permute-start(bf16[64,4096]{1,0:T(8,128)(2,1)S(1)} %step_sum.5), channel_id=1, source_target_pairs={{0,4},{1,3},{4,8},{5,1},{8,12},{9,5},{12,14},{13,9},{14,10},{15,13... | collective-permute-start | bytes 1572872 | tf_op jit(solution)/shard_map/return_short_3/ppermute | solution.py:326
  61.3 3.6 %collective-permute-start.19 = (bf16[64,4096]{1,0:T(8,128)(2,1)S(1)}, bf16[64,4096]{1,0:T(8,128)(2,1)S(1)}, u32[]{:S(2)}, u32[]{:S(2)}) collective-permute-start(bf16[64,4096]{1,0:T(8,128)(2,1)S(1)} %get-tuple-element.70), channel_id=1, source_target_pairs={{0,1},{1,0},{2,3},{3,2},{4,5},{5,4},{6,7},{7,6},{8,9},{9,8},{10,11... | collective-permute-start | bytes 1572872 | tf_op jit(solution)/shard_map/swap_out_4/ppermute | solution.py:326
  61.7 14.5 %collective-permute-start.26 = (bf16[64,4224]{1,0:T(8,128)(2,1)S(1)}, bf16[64,4224]{1,0:T(8,128)(2,1)S(1)}, u32[]{:S(2)}, u32[]{:S(2)}) collective-permute-start(bf16[64,4224]{1,0:T(8,128)(2,1)S(1)} %collective-permute-done.14.refs_1_), channel_id=1, source_target_pairs={{0,1},{1,0},{2,3},{3,2},{4,5},{5,4},{6,7},{7,6},{8,9},{9,8},{10,11... | collective-permute-start | bytes 1622024 | tf_op jit(solution)/shard_map/swap_in_2/ppermute | solution.py:326
  61.8 5.3 %collective-permute-start.9 = (bf16[64,4096]{1,0:T(8,128)(2,1)S(1)}, bf16[64,4096]{1,0:T(8,128)(2,1)S(1)}, u32[]{:S(2)}, u32[]{:S(2)}) collective-permute-start(bf16[64,4096]{1,0:T(8,128)(2,1)S(1)} %get-tuple-element.61), channel_id=1, source_target_pairs={{0,1},{1,0},{2,3},{3,2},{4,5},{5,4},{6,7},{7,6},{8,9},{9,8},{10,11... | collective-permute-start | bytes 1572872 | tf_op jit(solution)/shard_map/swap_out_2/ppermute | solution.py:326
  65.0 9.2 %collective-permute-start.22 = (bf16[64,4096]{1,0:T(8,128)(2,1)S(1)}, bf16[64,4096]{1,0:T(8,128)(2,1)S(1)}, u32[]{:S(2)}, u32[]{:S(2)}) collective-permute-start(bf16[64,4096]{1,0:T(8,128)(2,1)S(1)} %step_sum.6), channel_id=1, source_target_pairs={{0,4},{1,3},{4,8},{5,1},{8,12},{9,5},{12,14},{13,9},{14,10},{15,13... | collective-permute-start | bytes 1572872 | tf_op jit(solution)/shard_map/return_long_4/ppermute | solution.py:326
  66.7 7.6 %collective-permute-start.21 = (bf16[64,4096]{1,0:T(8,128)(2,1)S(1)}, bf16[64,4096]{1,0:T(8,128)(2,1)S(1)}, u32[]{:S(2)}, u32[]{:S(2)}) collective-permute-start(bf16[64,4096]{1,0:T(8,128)(2,1)S(1)} %get-tuple-element.73), channel_id=1, source_target_pairs={{0,1},{1,0},{2,3},{3,2},{4,5},{5,4},{6,7},{7,6},{8,9},{9,8},{10,11... | collective-permute-start | bytes 1572872 | tf_op jit(solution)/shard_map/swap_out_3/ppermute | solution.py:326
  66.7 14.0 %collective-permute-start.6 = (bf16[64,4096]{1,0:T(8,128)(2,1)S(1)}, bf16[64,4096]{1,0:T(8,128)(2,1)S(1)}, u32[]{:S(2)}, u32[]{:S(2)}) collective-permute-start(bf16[64,4096]{1,0:T(8,128)(2,1)S(1)} %get-tuple-element.57), channel_id=1, source_target_pairs={{0,1},{1,0},{2,3},{3,2},{4,5},{5,4},{6,7},{7,6},{8,9},{9,8},{10,11... | collective-permute-start | bytes 1572872 | tf_op jit(solution)/shard_map/swap_out_1/ppermute | solution.py:326
  67.4 13.3 %collective-permute-start.20 = (bf16[64,4096]{1,0:T(8,128)(2,1)S(1)}, bf16[64,4096]{1,0:T(8,128)(2,1)S(1)}, u32[]{:S(2)}, u32[]{:S(2)}) collective-permute-start(bf16[64,4096]{1,0:T(8,128)(2,1)S(1)} %step_sum.7), channel_id=1, source_target_pairs={{0,4},{1,3},{4,8},{5,1},{8,12},{9,5},{12,14},{13,9},{14,10},{15,13... | collective-permute-start | bytes 1572872 | tf_op jit(solution)/shard_map/return_short_2/ppermute | solution.py:326
  74.5 11.0 %collective-permute-start.28 = (bf16[64,4096]{1,0:T(8,128)(2,1)S(1)}, bf16[64,4096]{1,0:T(8,128)(2,1)S(1)}, u32[]{:S(2)}, u32[]{:S(2)}) collective-permute-start(bf16[64,4096]{1,0:T(8,128)(2,1)S(1)} %step_sum.8), channel_id=1, source_target_pairs={{0,4},{1,3},{4,8},{5,1},{8,12},{9,5},{12,14},{13,9},{14,10},{15,13... | collective-permute-start | bytes 1572872 | tf_op jit(solution)/shard_map/return_long_3/ppermute | solution.py:326
  80.1 5.4 %collective-permute-start.27 = (bf16[64,4096]{1,0:T(8,128)(2,1)S(1)}, bf16[64,4096]{1,0:T(8,128)(2,1)S(1)}, u32[]{:S(2)}, u32[]{:S(2)}) collective-permute-start(bf16[64,4096]{1,0:T(8,128)(2,1)S(1)} %get-tuple-element.80), channel_id=1, source_target_pairs={{0,1},{1,0},{2,3},{3,2},{4,5},{5,4},{6,7},{7,6},{8,9},{9,8},{10,11... | collective-permute-start | bytes 1572872 | tf_op jit(solution)/shard_map/swap_out_2/ppermute | solution.py:326
  80.2 7.2 %collective-permute-start.1 = (bf16[64,4096]{1,0:T(8,128)(2,1)S(1)}, bf16[64,4096]{1,0:T(8,128)(2,1)S(1)}, u32[]{:S(2)}, u32[]{:S(2)}) collective-permute-start(bf16[64,4096]{1,0:T(8,128)(2,1)S(1)} %get-tuple-element.49), channel_id=1, source_target_pairs={{0,1},{1,0},{2,3},{3,2},{4,5},{5,4},{6,7},{7,6},{8,9},{9,8},{10,11... | collective-permute-start | bytes 1572872 | tf_op jit(solution)/shard_map/swap_out_0/ppermute | solution.py:326
  80.9 7.4 %collective-permute-start.23 = (bf16[32,4096]{1,0:T(8,128)(2,1)S(1)}, bf16[32,4096]{1,0:T(8,128)(2,1)S(1)}, u32[]{:S(2)}, u32[]{:S(2)}) collective-permute-start(bf16[32,4096]{1,0:T(8,128)(2,1)S(1)} %get-tuple-element.76), channel_id=1, source_target_pairs={{0,4},{1,3},{4,8},{5,1},{8,12},{9,5},{12,14},{13,9},{14,10},{15,13... | collective-permute-start | bytes 786440 | tf_op jit(solution)/shard_map/return_short_1/ppermute | solution.py:326
  82.5 7.7 %collective-permute-start.24 = (bf16[32,4096]{1,0:T(8,128)(2,1)S(1)}, bf16[32,4096]{1,0:T(8,128)(2,1)S(1)}, u32[]{:S(2)}, u32[]{:S(2)}) collective-permute-start(bf16[32,4096]{1,0:T(8,128)(2,1)S(1)} %get-tuple-element.77), channel_id=1, source_target_pairs={{0,5},{1,2},{4,9},{5,0},{8,13},{9,4},{12,15},{13,8},{14,11},{15,12... | collective-permute-start | bytes 786440 | tf_op jit(solution)/shard_map/return_short_1/ppermute | solution.py:326
  85.5 11.2 %collective-permute-start.25 = (bf16[64,4096]{1,0:T(8,128)(2,1)S(1)}, bf16[64,4096]{1,0:T(8,128)(2,1)S(1)}, u32[]{:S(2)}, u32[]{:S(2)}) collective-permute-start(bf16[64,4096]{1,0:T(8,128)(2,1)S(1)} %get-tuple-element.78), channel_id=1, source_target_pairs={{0,1},{1,0},{2,3},{3,2},{4,5},{5,4},{6,7},{7,6},{8,9},{9,8},{10,11... | collective-permute-start | bytes 1572872 | tf_op jit(solution)/shard_map/swap_out_1/ppermute | solution.py:326
  85.7 11.0 %collective-permute-start.29 = (bf16[64,4096]{1,0:T(8,128)(2,1)S(1)}, bf16[64,4096]{1,0:T(8,128)(2,1)S(1)}, u32[]{:S(2)}, u32[]{:S(2)}) collective-permute-start(bf16[64,4096]{1,0:T(8,128)(2,1)S(1)} %step_sum.9), channel_id=1, source_target_pairs={{0,4},{1,3},{4,8},{5,1},{8,12},{9,5},{12,14},{13,9},{14,10},{15,13... | collective-permute-start | bytes 1572872 | tf_op jit(solution)/shard_map/return_long_2/ppermute | solution.py:326
  96.9 5.9 %collective-permute-start.30 = (bf16[32,4096]{1,0:T(8,128)(2,1)S(1)}, bf16[32,4096]{1,0:T(8,128)(2,1)S(1)}, u32[]{:S(2)}, u32[]{:S(2)}) collective-permute-start(bf16[32,4096]{1,0:T(8,128)(2,1)S(1)} %get-tuple-element.83), channel_id=1, source_target_pairs={{0,5},{1,2},{4,9},{5,0},{8,13},{9,4},{12,15},{13,8},{14,11},{15,12... | collective-permute-start | bytes 786440 | tf_op jit(solution)/shard_map/return_long_1/ppermute | solution.py:326
  97.0 8.5 %collective-permute-start.31 = (bf16[32,4096]{1,0:T(8,128)(2,1)S(1)}, bf16[32,4096]{1,0:T(8,128)(2,1)S(1)}, u32[]{:S(2)}, u32[]{:S(2)}) collective-permute-start(bf16[32,4096]{1,0:T(8,128)(2,1)S(1)} %get-tuple-element.84), channel_id=1, source_target_pairs={{0,4},{1,3},{4,8},{5,1},{8,12},{9,5},{12,14},{13,9},{14,10},{15,13... | collective-permute-start | bytes 786440 | tf_op jit(solution)/shard_map/return_long_1/ppermute | solution.py:326
  (2 other events, 24.3 us)

commit v15 on v14

--- a/solution.py
+++ b/solution.py
@@ -123,7 +123,7 @@
         hidden[:, here] = (jax.nn.silu(sides[0]) * sides[1]).astype(jnp.bfloat16)
         return carry
 
-    lax.fori_loop(0, units // UNIT_CHUNK, unit_step, 0)
+    lax.fori_loop(0, units // UNIT_CHUNK, unit_step, 0, unroll=True)
 
     def width_step(chunk, carry):
         columns = pl.ds(pl.multiple_of(chunk * WIDTH_CHUNK, WIDTH_CHUNK), WIDTH_CHUNK)
@@ -135,7 +135,7 @@
             at += ref.shape[0]
         return carry
 
-    lax.fori_loop(0, width // WIDTH_CHUNK, width_step, 0)
+    lax.fori_loop(0, width // WIDTH_CHUNK, width_step, 0, unroll=True)
 
 
 def expert_part(blocks, out_rows, hint, pick, gate_up_w, gate_up_s, down_w, down_s):

time: 106 us -> 106 us (level)
  Pallas kernels: 40.1 us -> 32.4 us
  waiting for transfers between devices: 37.2 us -> 41.8 us
  starting transfers between devices: 28.7 us -> 31.2 us
    pallas_call x7, Pallas kernels: 30.1 us -> 22.4 us  [expert_part(): pl.pallas_call(functools.partial(expert_kernel, len(blocks)), in_specs=[V...]
    ppermute x32, waiting for transfers between devices: 37.2 us -> 41.8 us  [send(): return lax.ppermute(x, 'expert', perm)]
    ppermute x32, starting transfers between devices: 28.7 us -> 31.2 us  [send(): return lax.ppermute(x, 'expert', perm)]
  transfers between devices with their start and end apart: 32 -> 32, of which waited for: 11 -> 15; matrix products, arithmetic and copies ran while one was open for 0% -> 0% of each run, Pallas kernels for 35% -> 28%
where the time goes in v15:
time: 106 us
  waiting for transfers between devices  41.8 us (39%)
  Pallas kernels  32.4 us (31%)
  starting transfers between devices  31.2 us (29%)
    ppermute x32, waiting for transfers between devices, send(): return lax.ppermute(x, 'expert', perm)  41.8 us
    ppermute x32, starting transfers between devices, send(): return lax.ppermute(x, 'expert', perm)  31.2 us
    pallas_call x7, Pallas kernels, expert_part(): pl.pallas_call(functools.partial(expert_kernel, len(blocks)), in_specs=[V...  22.4 us
    pallas_call x1, Pallas kernels, keep(): pl.pallas_call(keep_kernel, in_specs=[ANYWHERE] * 2, out_specs=[VMEM] * 2...  6.38 us
  transfers between devices with their start and end apart: 32, of which 15 were waited for; matrix products, arithmetic and copies ran while one was open for 0% of the time, Pallas kernels for 28%

profile of v15, /device:TPU:0, one launch (start us, length us, event | category | flops | bytes accessed | tf_op | source)
XLA Modules:
  0.0 105.8 jit_solution(17826758412184817833)
XLA Ops:
  0.0 1.3 %pack.1 = (bf16[64,4224]{1,0:T(8,128)(2,1)S(1)}, bf16[64,4224]{1,0:T(8,128)(2,1)S(1)}) custom-call(s32[1]{0:T(128)} %bitcast.core, bf16[64,4096]{1,0:T(8,128)(2,1)} %tokens.1, s32[8,64]{1,0:T(8,128)} %bitcast.7, s32[8,64]{1,0:T(8,128)} %bitcast.8), custom_call_target="tpu_custom_call" | custom-call | tf_op jit(solution)/shard_map/pack/pallas_call | solution.py:64
  1.8 2.6 %collective-permute-start.2 = (bf16[64,4224]{1,0:T(8,128)(2,1)S(1)}, bf16[64,4224]{1,0:T(8,128)(2,1)S(1)}, u32[]{:S(2)}, u32[]{:S(2)}) collective-permute-start(bf16[64,4224]{1,0:T(8,128)(2,1)S(1)} %get-tuple-element.45.refs_0_), channel_id=1, source_target_pairs={{0,4},{1,3},{4,8},{5,1},{8,12},{9,5},{12,14},{13,9},{14,10},{15,13... | collective-permute-start | bytes 1622024 | tf_op jit(solution)/shard_map/gather_long_1/ppermute | solution.py:326
  5.7 6.4 %keep.1 = (bf16[4096,1536]{1,0:T(8,128)(2,1)S(1)}, bf16[768,4096]{1,0:T(8,128)(2,1)S(1)}) custom-call(bf16[4096,1536]{1,0:T(8,128)(2,1)} %bitcast.5, bf16[768,4096]{1,0:T(8,128)(2,1)} %bitcast.6), custom_call_target="tpu_custom_call" | custom-call | bytes 18874368 | tf_op jit(solution)/shard_map/keep/pallas_call | solution.py:88
  12.2 2.9 %expert.7 = (bf16[64,4096]{1,0:T(8,128)(2,1)S(1)}, bf16[64,4096]{1,0:T(8,128)(2,1)S(1)}) custom-call(bf16[64,4224]{1,0:T(8,128)(2,1)S(1)} %get-tuple-element.45.refs_0_, bf16[64,4224]{1,0:T(8,128)(2,1)S(1)} %collective-permute-done.refs_1_, f32[1,128]{1,0:T(1,128)S(1)} %compare_select_fusion.1.refs_2_.refs_4_, f32[1,1536]{1,0:T(1,128)S(1)} %copy-done.1, ...), custom_call_target="tpu_custom_call" | custom-call | flops 4831838208 | tf_op jit(solution)/shard_map/expert/pallas_call | solution.py:146
  16.1 1.4 %collective-permute-done.3.cross = bf16[64,4224]{1,0:T(8,128)(2,1)S(1)} collective-permute-done((bf16[64,4224]{1,0:T(8,128)(2,1)S(1)}, bf16[64,4224]{1,0:T(8,128)(2,1)S(1)}, u32[]{:S(2)}, u32[]{:S(2)}) %collective-permute-start.3) | collective-permute-done | bytes 540704 | tf_op jit(solution)/shard_map/gather_long_1/ppermute | solution.py:326
  18.2 2.1 %collective-permute-start.7 = (bf16[64,4224]{1,0:T(8,128)(2,1)S(1)}, bf16[64,4224]{1,0:T(8,128)(2,1)S(1)}, u32[]{:S(2)}, u32[]{:S(2)}) collective-permute-start(bf16[64,4224]{1,0:T(8,128)(2,1)S(1)} %get-tuple-element.55.refs_3_), channel_id=1, source_target_pairs={{0,4},{1,3},{4,8},{5,1},{8,12},{9,5},{12,14},{13,9},{14,10},{15,13... | collective-permute-start | bytes 1622024 | tf_op jit(solution)/shard_map/gather_short_2/ppermute | solution.py:326
  20.3 1.6 %collective-permute-start.14 = (bf16[64,4224]{1,0:T(8,128)(2,1)S(1)}, bf16[64,4224]{1,0:T(8,128)(2,1)S(1)}, u32[]{:S(2)}, u32[]{:S(2)}) collective-permute-start(bf16[64,4224]{1,0:T(8,128)(2,1)S(1)} %get-tuple-element.53.refs_2_), channel_id=1, source_target_pairs={{0,4},{1,3},{4,8},{5,1},{8,12},{9,5},{12,14},{13,9},{14,10},{15,13... | collective-permute-start | bytes 1622024 | tf_op jit(solution)/shard_map/gather_long_2/ppermute | solution.py:326
  21.8 5.2 %expert.8 = (bf16[64,4096]{1,0:T(8,128)(2,1)S(1)}, bf16[64,4096]{1,0:T(8,128)(2,1)S(1)}, bf16[64,4096]{1,0:T(8,128)(2,1)S(1)}, bf16[64,4096]{1,0:T(8,128)(2,1)S(1)}) custom-call(bf16[64,4224]{1,0:T(8,128)(2,1)S(1)} %collective-permute-done.4.refs_0_, bf16[64,4224]{1,0:T(8,128)(2,1)S(1)} %collective-permute-done.5.refs_1_, ...), custom_call_target="tpu_custom_call" | custom-call | flops 9663676416 | tf_op jit(solution)/shard_map/expert/pallas_call | solution.py:146
  27.5 2.1 %collective-permute-start.10 = (bf16[64,4224]{1,0:T(8,128)(2,1)S(1)}, bf16[64,4224]{1,0:T(8,128)(2,1)S(1)}, u32[]{:S(2)}, u32[]{:S(2)}) collective-permute-start(bf16[64,4224]{1,0:T(8,128)(2,1)S(1)} %collective-permute-done.7.refs_1_), channel_id=1, source_target_pairs={{0,4},{1,3},{4,8},{5,1},{8,12},{9,5},{12,14},{13,9},{14,10},{15,13... | collective-permute-start | bytes 1622024 | tf_op jit(solution)/shard_map/gather_short_3/ppermute | solution.py:326
  29.6 3.7 %collective-permute-done.14.refs_1_ = bf16[64,4224]{1,0:T(8,128)(2,1)S(1)} collective-permute-done((bf16[64,4224]{1,0:T(8,128)(2,1)S(1)}, bf16[64,4224]{1,0:T(8,128)(2,1)S(1)}, u32[]{:S(2)}, u32[]{:S(2)}) %collective-permute-start.14) | collective-permute-done | bytes 540704 | tf_op jit(solution)/shard_map/gather_long_2/ppermute | solution.py:326
  33.3 2.1 %collective-permute-start.15 = (bf16[64,4224]{1,0:T(8,128)(2,1)S(1)}, bf16[64,4224]{1,0:T(8,128)(2,1)S(1)}, u32[]{:S(2)}, u32[]{:S(2)}) collective-permute-start(bf16[64,4224]{1,0:T(8,128)(2,1)S(1)} %collective-permute-done.14.refs_1_), channel_id=1, source_target_pairs={{0,4},{1,3},{4,8},{5,1},{8,12},{9,5},{12,14},{13,9},{14,10},{15,13... | collective-permute-start | bytes 1622024 | tf_op jit(solution)/shard_map/gather_long_3/ppermute | solution.py:326
  35.4 2.9 %expert.9 = (bf16[64,4096]{1,0:T(8,128)(2,1)S(1)}, bf16[64,4096]{1,0:T(8,128)(2,1)S(1)}) custom-call(bf16[64,4224]{1,0:T(8,128)(2,1)S(1)} %collective-permute-done.8.refs_0_, bf16[64,4224]{1,0:T(8,128)(2,1)S(1)} %collective-permute-done.7.refs_1_, f32[1,128]{1,0:T(1,128)S(1)} %compare_select_fusion.1.refs_2_.refs_4_, f32[1,1536]{1,0:T(1,128)S(1)} %copy-done.1, ...), custom_call_target="tpu_custom_call" | custom-call | flops 4831838208 | tf_op jit(solution)/shard_map/expert/pallas_call | solution.py:146
  39.1 5.8 %collective-permute-done.15.refs_1_ = bf16[64,4224]{1,0:T(8,128)(2,1)S(1)} collective-permute-done((bf16[64,4224]{1,0:T(8,128)(2,1)S(1)}, bf16[64,4224]{1,0:T(8,128)(2,1)S(1)}, u32[]{:S(2)}, u32[]{:S(2)}) %collective-permute-start.15) | collective-permute-done | bytes 540704 | tf_op jit(solution)/shard_map/gather_long_3/ppermute | solution.py:326
  44.9 2.1 %collective-permute-start.16 = (bf16[64,4224]{1,0:T(8,128)(2,1)S(1)}, bf16[64,4224]{1,0:T(8,128)(2,1)S(1)}, u32[]{:S(2)}, u32[]{:S(2)}) collective-permute-start(bf16[64,4224]{1,0:T(8,128)(2,1)S(1)} %collective-permute-done.15.refs_1_), channel_id=1, source_target_pairs={{0,4},{1,3},{4,8},{5,1},{8,12},{9,5},{12,14},{13,9},{14,10},{15,13... | collective-permute-start | bytes 1622024 | tf_op jit(solution)/shard_map/gather_long_4/ppermute | solution.py:326
  47.0 2.9 %expert.10 = (bf16[64,4096]{1,0:T(8,128)(2,1)S(1)}, bf16[64,4096]{1,0:T(8,128)(2,1)S(1)}) custom-call(bf16[64,4224]{1,0:T(8,128)(2,1)S(1)} %collective-permute-done.11.refs_0_, bf16[64,4224]{1,0:T(8,128)(2,1)S(1)} %collective-permute-done.10.refs_1_, f32[1,128]{1,0:T(1,128)S(1)} %compare_select_fusion.1.refs_2_.refs_4_, f32[1,1536]{1,0:T(1,128)S(1)} %copy-done.1, ...), custom_call_target="tpu_custom_call" | custom-call | flops 4831838208 | tf_op jit(solution)/shard_map/expert/pallas_call | solution.py:146
  50.1 2.9 %expert.11 = (bf16[64,4096]{1,0:T(8,128)(2,1)S(1)}, bf16[64,4096]{1,0:T(8,128)(2,1)S(1)}) custom-call(bf16[64,4224]{1,0:T(8,128)(2,1)S(1)} %collective-permute-done.17.refs_0_, bf16[64,4224]{1,0:T(8,128)(2,1)S(1)} %collective-permute-done.15.refs_1_, f32[1,128]{1,0:T(1,128)S(1)} %compare_select_fusion.1.refs_2_.refs_4_, f32[1,1536]{1,0:T(1,128)S(1)} %copy-done.1, ...), custom_call_target="tpu_custom_call" | custom-call | flops 4831838208 | tf_op jit(solution)/shard_map/expert/pallas_call | solution.py:146
  54.3 2.1 %collective-permute-start.13 = (bf16[64,4096]{1,0:T(8,128)(2,1)S(1)}, bf16[64,4096]{1,0:T(8,128)(2,1)S(1)}, u32[]{:S(2)}, u32[]{:S(2)}) collective-permute-start(bf16[64,4096]{1,0:T(8,128)(2,1)S(1)} %step_sum.5), channel_id=1, source_target_pairs={{0,4},{1,3},{4,8},{5,1},{8,12},{9,5},{12,14},{13,9},{14,10},{15,13... | collective-permute-start | bytes 1572872 | tf_op jit(solution)/shard_map/return_short_3/ppermute | solution.py:326
  56.4 2.9 %expert.12 = (bf16[64,4096]{1,0:T(8,128)(2,1)S(1)}, bf16[64,4096]{1,0:T(8,128)(2,1)S(1)}) custom-call(bf16[64,4224]{1,0:T(8,128)(2,1)S(1)} %collective-permute-done.18.refs_0_, bf16[64,4224]{1,0:T(8,128)(2,1)S(1)} %collective-permute-done.16.refs_1_, f32[1,128]{1,0:T(1,128)S(1)} %compare_select_fusion.1.refs_2_.refs_4_, f32[1,1536]{1,0:T(1,128)S(1)} %copy-done.1, ...), custom_call_target="tpu_custom_call" | custom-call | flops 4831838208 | tf_op jit(solution)/shard_map/expert/pallas_call | solution.py:146
  60.0 3.5 %collective-permute-done.13.refs_2_ = bf16[64,4096]{1,0:T(8,128)(2,1)S(1)} collective-permute-done((bf16[64,4096]{1,0:T(8,128)(2,1)S(1)}, bf16[64,4096]{1,0:T(8,128)(2,1)S(1)}, u32[]{:S(2)}, u32[]{:S(2)}) %collective-permute-start.13) | collective-permute-done | bytes 524320 | tf_op jit(solution)/shard_map/return_short_3/ppermute | solution.py:326
  63.6 2.1 %collective-permute-start.22 = (bf16[64,4096]{1,0:T(8,128)(2,1)S(1)}, bf16[64,4096]{1,0:T(8,128)(2,1)S(1)}, u32[]{:S(2)}, u32[]{:S(2)}) collective-permute-start(bf16[64,4096]{1,0:T(8,128)(2,1)S(1)} %step_sum.6), channel_id=1, source_target_pairs={{0,4},{1,3},{4,8},{5,1},{8,12},{9,5},{12,14},{13,9},{14,10},{15,13... | collective-permute-start | bytes 1572872 | tf_op jit(solution)/shard_map/return_long_4/ppermute | solution.py:326
  66.4 1.6 %collective-permute-start.20 = (bf16[64,4096]{1,0:T(8,128)(2,1)S(1)}, bf16[64,4096]{1,0:T(8,128)(2,1)S(1)}, u32[]{:S(2)}, u32[]{:S(2)}) collective-permute-start(bf16[64,4096]{1,0:T(8,128)(2,1)S(1)} %step_sum.7), channel_id=1, source_target_pairs={{0,4},{1,3},{4,8},{5,1},{8,12},{9,5},{12,14},{13,9},{14,10},{15,13... | collective-permute-start | bytes 1572872 | tf_op jit(solution)/shard_map/return_short_2/ppermute | solution.py:326
  68.1 4.8 %collective-permute-done.22.refs_2_ = bf16[64,4096]{1,0:T(8,128)(2,1)S(1)} collective-permute-done((bf16[64,4096]{1,0:T(8,128)(2,1)S(1)}, bf16[64,4096]{1,0:T(8,128)(2,1)S(1)}, u32[]{:S(2)}, u32[]{:S(2)}) %collective-permute-start.22) | collective-permute-done | bytes 524320 | tf_op jit(solution)/shard_map/return_long_4/ppermute | solution.py:326
  73.1 2.3 %collective-permute-start.28 = (bf16[64,4096]{1,0:T(8,128)(2,1)S(1)}, bf16[64,4096]{1,0:T(8,128)(2,1)S(1)}, u32[]{:S(2)}, u32[]{:S(2)}) collective-permute-start(bf16[64,4096]{1,0:T(8,128)(2,1)S(1)} %step_sum.8), channel_id=1, source_target_pairs={{0,4},{1,3},{4,8},{5,1},{8,12},{9,5},{12,14},{13,9},{14,10},{15,13... | collective-permute-start | bytes 1572872 | tf_op jit(solution)/shard_map/return_long_3/ppermute | solution.py:326
  75.4 2.9 %expert.13 = (bf16[64,4096]{1,0:T(8,128)(2,1)S(1)}, bf16[64,4096]{1,0:T(8,128)(2,1)S(1)}) custom-call(bf16[64,4224]{1,0:T(8,128)(2,1)S(1)} %collective-permute-done.26.refs_0_, bf16[64,4224]{1,0:T(8,128)(2,1)S(1)} %collective-permute-done.14.refs_1_, f32[1,128]{1,0:T(1,128)S(1)} %compare_select_fusion.1.refs_2_.refs_4_, f32[1,1536]{1,0:T(1,128)S(1)} %copy-done.1, ...), custom_call_target="tpu_custom_call" | custom-call | flops 4831838208 | tf_op jit(solution)/shard_map/expert/pallas_call | solution.py:146
  79.1 1.7 %collective-permute-start.23 = (bf16[32,4096]{1,0:T(8,128)(2,1)S(1)}, bf16[32,4096]{1,0:T(8,128)(2,1)S(1)}, u32[]{:S(2)}, u32[]{:S(2)}) collective-permute-start(bf16[32,4096]{1,0:T(8,128)(2,1)S(1)} %get-tuple-element.76), channel_id=1, source_target_pairs={{0,4},{1,3},{4,8},{5,1},{8,12},{9,5},{12,14},{13,9},{14,10},{15,13... | collective-permute-start | bytes 786440 | tf_op jit(solution)/shard_map/return_short_1/ppermute | solution.py:326
  80.8 3.3 %collective-permute-done.28.refs_2_ = bf16[64,4096]{1,0:T(8,128)(2,1)S(1)} collective-permute-done((bf16[64,4096]{1,0:T(8,128)(2,1)S(1)}, bf16[64,4096]{1,0:T(8,128)(2,1)S(1)}, u32[]{:S(2)}, u32[]{:S(2)}) %collective-permute-start.28) | collective-permute-done | bytes 524320 | tf_op jit(solution)/shard_map/return_long_3/ppermute | solution.py:326
  84.3 2.1 %collective-permute-start.29 = (bf16[64,4096]{1,0:T(8,128)(2,1)S(1)}, bf16[64,4096]{1,0:T(8,128)(2,1)S(1)}, u32[]{:S(2)}, u32[]{:S(2)}) collective-permute-start(bf16[64,4096]{1,0:T(8,128)(2,1)S(1)} %step_sum.9), channel_id=1, source_target_pairs={{0,4},{1,3},{4,8},{5,1},{8,12},{9,5},{12,14},{13,9},{14,10},{15,13... | collective-permute-start | bytes 1572872 | tf_op jit(solution)/shard_map/return_long_2/ppermute | solution.py:326
  86.9 2.4 %collective-permute-done.24.short_cross = bf16[32,4096]{1,0:T(8,128)(2,1)S(1)} collective-permute-done((bf16[32,4096]{1,0:T(8,128)(2,1)S(1)}, bf16[32,4096]{1,0:T(8,128)(2,1)S(1)}, u32[]{:S(2)}, u32[]{:S(2)}) %collective-permute-start.24) | collective-permute-done | bytes 262176 | tf_op jit(solution)/shard_map/return_short_1/ppermute | solution.py:326
  89.5 5.8 %collective-permute-done.29.refs_2_ = bf16[64,4096]{1,0:T(8,128)(2,1)S(1)} collective-permute-done((bf16[64,4096]{1,0:T(8,128)(2,1)S(1)}, bf16[64,4096]{1,0:T(8,128)(2,1)S(1)}, u32[]{:S(2)}, u32[]{:S(2)}) %collective-permute-start.29) | collective-permute-done | bytes 524320 | tf_op jit(solution)/shard_map/return_long_2/ppermute | solution.py:326
  96.1 1.7 %collective-permute-start.31 = (bf16[32,4096]{1,0:T(8,128)(2,1)S(1)}, bf16[32,4096]{1,0:T(8,128)(2,1)S(1)}, u32[]{:S(2)}, u32[]{:S(2)}) collective-permute-start(bf16[32,4096]{1,0:T(8,128)(2,1)S(1)} %get-tuple-element.84), channel_id=1, source_target_pairs={{0,4},{1,3},{4,8},{5,1},{8,12},{9,5},{12,14},{13,9},{14,10},{15,13... | collective-permute-start | bytes 786440 | tf_op jit(solution)/shard_map/return_long_1/ppermute | solution.py:326
  97.7 3.7 %collective-permute-done.30.long_cross = bf16[32,4096]{1,0:T(8,128)(2,1)S(1)} collective-permute-done((bf16[32,4096]{1,0:T(8,128)(2,1)S(1)}, bf16[32,4096]{1,0:T(8,128)(2,1)S(1)}, u32[]{:S(2)}, u32[]{:S(2)}) %collective-permute-start.30) | collective-permute-done | bytes 262176 | tf_op jit(solution)/shard_map/return_long_1/ppermute | solution.py:326
  101.4 3.4 %collective-permute-done.31.long_same = bf16[32,4096]{1,0:T(8,128)(2,1)S(1)} collective-permute-done((bf16[32,4096]{1,0:T(8,128)(2,1)S(1)}, bf16[32,4096]{1,0:T(8,128)(2,1)S(1)}, u32[]{:S(2)}, u32[]{:S(2)}) %collective-permute-start.31) | collective-permute-done | bytes 262176 | tf_op jit(solution)/shard_map/return_long_1/ppermute | solution.py:326
  (56 shorter events, 11.4 us)
Async XLA Ops:
  1.3 10.9 %collective-permute-start = (bf16[64,4224]{1,0:T(8,128)(2,1)S(1)}, bf16[64,4224]{1,0:T(8,128)(2,1)S(1)}, u32[]{:S(2)}, u32[]{:S(2)}) collective-permute-start(bf16[64,4224]{1,0:T(8,128)(2,1)S(1)} %get-tuple-element.45.refs_0_), channel_id=1, source_target_pairs={{0,1},{1,0},{2,3},{3,2},{4,5},{5,4},{6,7},{7,6},{8,9},{9,8},{10,11... | collective-permute-start | bytes 1622024 | tf_op jit(solution)/shard_map/swap_in_0/ppermute | solution.py:326
  1.8 14.3 %collective-permute-start.2 = (bf16[64,4224]{1,0:T(8,128)(2,1)S(1)}, bf16[64,4224]{1,0:T(8,128)(2,1)S(1)}, u32[]{:S(2)}, u32[]{:S(2)}) collective-permute-start(bf16[64,4224]{1,0:T(8,128)(2,1)S(1)} %get-tuple-element.45.refs_0_), channel_id=1, source_target_pairs={{0,4},{1,3},{4,8},{5,1},{8,12},{9,5},{12,14},{13,9},{14,10},{15,13... | collective-permute-start | bytes 1622024 | tf_op jit(solution)/shard_map/gather_long_1/ppermute | solution.py:326
  4.5 13.1 %collective-permute-start.3 = (bf16[64,4224]{1,0:T(8,128)(2,1)S(1)}, bf16[64,4224]{1,0:T(8,128)(2,1)S(1)}, u32[]{:S(2)}, u32[]{:S(2)}) collective-permute-start(bf16[64,4224]{1,0:T(8,128)(2,1)S(1)} %get-tuple-element.51), channel_id=1, source_target_pairs={{0,3},{1,4},{4,1},{5,8},{8,5},{9,12},{12,9},{13,14},{14,13},{15,10... | collective-permute-start | bytes 1622024 | tf_op jit(solution)/shard_map/gather_long_1/ppermute | solution.py:326
  17.6 4.2 %collective-permute-start.4 = (bf16[64,4224]{1,0:T(8,128)(2,1)S(1)}, bf16[64,4224]{1,0:T(8,128)(2,1)S(1)}, u32[]{:S(2)}, u32[]{:S(2)}) collective-permute-start(bf16[64,4224]{1,0:T(8,128)(2,1)S(1)} %get-tuple-element.53.refs_2_), channel_id=1, source_target_pairs={{0,1},{1,0},{2,3},{3,2},{4,5},{5,4},{6,7},{7,6},{8,9},{9,8},{10,11... | collective-permute-start | bytes 1622024 | tf_op jit(solution)/shard_map/swap_in_1/ppermute | solution.py:326
  17.7 4.2 %collective-permute-start.5 = (bf16[64,4224]{1,0:T(8,128)(2,1)S(1)}, bf16[64,4224]{1,0:T(8,128)(2,1)S(1)}, u32[]{:S(2)}, u32[]{:S(2)}) collective-permute-start(bf16[64,4224]{1,0:T(8,128)(2,1)S(1)} %get-tuple-element.55.refs_3_), channel_id=1, source_target_pairs={{0,1},{1,0},{2,3},{3,2},{4,5},{5,4},{6,7},{7,6},{8,9},{9,8},{10,11... | collective-permute-start | bytes 1622024 | tf_op jit(solution)/shard_map/swap_in_1/ppermute | solution.py:326
  18.2 9.4 %collective-permute-start.7 = (bf16[64,4224]{1,0:T(8,128)(2,1)S(1)}, bf16[64,4224]{1,0:T(8,128)(2,1)S(1)}, u32[]{:S(2)}, u32[]{:S(2)}) collective-permute-start(bf16[64,4224]{1,0:T(8,128)(2,1)S(1)} %get-tuple-element.55.refs_3_), channel_id=1, source_target_pairs={{0,4},{1,3},{4,8},{5,1},{8,12},{9,5},{12,14},{13,9},{14,10},{15,13... | collective-permute-start | bytes 1622024 | tf_op jit(solution)/shard_map/gather_short_2/ppermute | solution.py:326
  20.3 13.1 %collective-permute-start.14 = (bf16[64,4224]{1,0:T(8,128)(2,1)S(1)}, bf16[64,4224]{1,0:T(8,128)(2,1)S(1)}, u32[]{:S(2)}, u32[]{:S(2)}) collective-permute-start(bf16[64,4224]{1,0:T(8,128)(2,1)S(1)} %get-tuple-element.53.refs_2_), channel_id=1, source_target_pairs={{0,4},{1,3},{4,8},{5,1},{8,12},{9,5},{12,14},{13,9},{14,10},{15,13... | collective-permute-start | bytes 1622024 | tf_op jit(solution)/shard_map/gather_long_2/ppermute | solution.py:326
  27.5 7.9 %collective-permute-start.8 = (bf16[64,4224]{1,0:T(8,128)(2,1)S(1)}, bf16[64,4224]{1,0:T(8,128)(2,1)S(1)}, u32[]{:S(2)}, u32[]{:S(2)}) collective-permute-start(bf16[64,4224]{1,0:T(8,128)(2,1)S(1)} %collective-permute-done.7.refs_1_), channel_id=1, source_target_pairs={{0,1},{1,0},{2,3},{3,2},{4,5},{5,4},{6,7},{7,6},{8,9},{9,8},{10,11... | collective-permute-start | bytes 1622024 | tf_op jit(solution)/shard_map/swap_in_2/ppermute | solution.py:326
  27.5 11.6 %collective-permute-start.10 = (bf16[64,4224]{1,0:T(8,128)(2,1)S(1)}, bf16[64,4224]{1,0:T(8,128)(2,1)S(1)}, u32[]{:S(2)}, u32[]{:S(2)}) collective-permute-start(bf16[64,4224]{1,0:T(8,128)(2,1)S(1)} %collective-permute-done.7.refs_1_), channel_id=1, source_target_pairs={{0,4},{1,3},{4,8},{5,1},{8,12},{9,5},{12,14},{13,9},{14,10},{15,13... | collective-permute-start | bytes 1622024 | tf_op jit(solution)/shard_map/gather_short_3/ppermute | solution.py:326
  33.3 11.6 %collective-permute-start.15 = (bf16[64,4224]{1,0:T(8,128)(2,1)S(1)}, bf16[64,4224]{1,0:T(8,128)(2,1)S(1)}, u32[]{:S(2)}, u32[]{:S(2)}) collective-permute-start(bf16[64,4224]{1,0:T(8,128)(2,1)S(1)} %collective-permute-done.14.refs_1_), channel_id=1, source_target_pairs={{0,4},{1,3},{4,8},{5,1},{8,12},{9,5},{12,14},{13,9},{14,10},{15,13... | collective-permute-start | bytes 1622024 | tf_op jit(solution)/shard_map/gather_long_3/ppermute | solution.py:326
  39.1 7.9 %collective-permute-start.11 = (bf16[64,4224]{1,0:T(8,128)(2,1)S(1)}, bf16[64,4224]{1,0:T(8,128)(2,1)S(1)}, u32[]{:S(2)}, u32[]{:S(2)}) collective-permute-start(bf16[64,4224]{1,0:T(8,128)(2,1)S(1)} %collective-permute-done.10.refs_1_), channel_id=1, source_target_pairs={{0,1},{1,0},{2,3},{3,2},{4,5},{5,4},{6,7},{7,6},{8,9},{9,8},{10,11... | collective-permute-start | bytes 1622024 | tf_op jit(solution)/shard_map/swap_in_3/ppermute | solution.py:326
  44.9 5.2 %collective-permute-start.17 = (bf16[64,4224]{1,0:T(8,128)(2,1)S(1)}, bf16[64,4224]{1,0:T(8,128)(2,1)S(1)}, u32[]{:S(2)}, u32[]{:S(2)}) collective-permute-start(bf16[64,4224]{1,0:T(8,128)(2,1)S(1)} %collective-permute-done.15.refs_1_), channel_id=1, source_target_pairs={{0,1},{1,0},{2,3},{3,2},{4,5},{5,4},{6,7},{7,6},{8,9},{9,8},{10,11... | collective-permute-start | bytes 1622024 | tf_op jit(solution)/shard_map/swap_in_3/ppermute | solution.py:326
  44.9 9.4 %collective-permute-start.16 = (bf16[64,4224]{1,0:T(8,128)(2,1)S(1)}, bf16[64,4224]{1,0:T(8,128)(2,1)S(1)}, u32[]{:S(2)}, u32[]{:S(2)}) collective-permute-start(bf16[64,4224]{1,0:T(8,128)(2,1)S(1)} %collective-permute-done.15.refs_1_), channel_id=1, source_target_pairs={{0,4},{1,3},{4,8},{5,1},{8,12},{9,5},{12,14},{13,9},{14,10},{15,13... | collective-permute-start | bytes 1622024 | tf_op jit(solution)/shard_map/gather_long_4/ppermute | solution.py:326
  49.9 3.1 %collective-permute-start.12 = (bf16[64,4096]{1,0:T(8,128)(2,1)S(1)}, bf16[64,4096]{1,0:T(8,128)(2,1)S(1)}, u32[]{:S(2)}, u32[]{:S(2)}) collective-permute-start(bf16[64,4096]{1,0:T(8,128)(2,1)S(1)} %get-tuple-element.64), channel_id=1, source_target_pairs={{0,1},{1,0},{2,3},{3,2},{4,5},{5,4},{6,7},{7,6},{8,9},{9,8},{10,11... | collective-permute-start | bytes 1572872 | tf_op jit(solution)/shard_map/swap_out_3/ppermute | solution.py:326
  54.3 2.1 %collective-permute-start.18 = (bf16[64,4224]{1,0:T(8,128)(2,1)S(1)}, bf16[64,4224]{1,0:T(8,128)(2,1)S(1)}, u32[]{:S(2)}, u32[]{:S(2)}) collective-permute-start(bf16[64,4224]{1,0:T(8,128)(2,1)S(1)} %collective-permute-done.16.refs_1_), channel_id=1, source_target_pairs={{0,1},{1,0},{2,3},{3,2},{4,5},{5,4},{6,7},{7,6},{8,9},{9,8},{10,11... | collective-permute-start | bytes 1622024 | tf_op jit(solution)/shard_map/swap_in_4/ppermute | solution.py:326
  54.3 9.2 %collective-permute-start.13 = (bf16[64,4096]{1,0:T(8,128)(2,1)S(1)}, bf16[64,4096]{1,0:T(8,128)(2,1)S(1)}, u32[]{:S(2)}, u32[]{:S(2)}) collective-permute-start(bf16[64,4096]{1,0:T(8,128)(2,1)S(1)} %step_sum.5), channel_id=1, source_target_pairs={{0,4},{1,3},{4,8},{5,1},{8,12},{9,5},{12,14},{13,9},{14,10},{15,13... | collective-permute-start | bytes 1572872 | tf_op jit(solution)/shard_map/return_short_3/ppermute | solution.py:326
  59.2 4.2 %collective-permute-start.19 = (bf16[64,4096]{1,0:T(8,128)(2,1)S(1)}, bf16[64,4096]{1,0:T(8,128)(2,1)S(1)}, u32[]{:S(2)}, u32[]{:S(2)}) collective-permute-start(bf16[64,4096]{1,0:T(8,128)(2,1)S(1)} %get-tuple-element.70), channel_id=1, source_target_pairs={{0,1},{1,0},{2,3},{3,2},{4,5},{5,4},{6,7},{7,6},{8,9},{9,8},{10,11... | collective-permute-start | bytes 1572872 | tf_op jit(solution)/shard_map/swap_out_4/ppermute | solution.py:326
  59.5 15.9 %collective-permute-start.26 = (bf16[64,4224]{1,0:T(8,128)(2,1)S(1)}, bf16[64,4224]{1,0:T(8,128)(2,1)S(1)}, u32[]{:S(2)}, u32[]{:S(2)}) collective-permute-start(bf16[64,4224]{1,0:T(8,128)(2,1)S(1)} %collective-permute-done.14.refs_1_), channel_id=1, source_target_pairs={{0,1},{1,0},{2,3},{3,2},{4,5},{5,4},{6,7},{7,6},{8,9},{9,8},{10,11... | collective-permute-start | bytes 1622024 | tf_op jit(solution)/shard_map/swap_in_2/ppermute | solution.py:326
  59.8 6.4 %collective-permute-start.9 = (bf16[64,4096]{1,0:T(8,128)(2,1)S(1)}, bf16[64,4096]{1,0:T(8,128)(2,1)S(1)}, u32[]{:S(2)}, u32[]{:S(2)}) collective-permute-start(bf16[64,4096]{1,0:T(8,128)(2,1)S(1)} %get-tuple-element.61), channel_id=1, source_target_pairs={{0,1},{1,0},{2,3},{3,2},{4,5},{5,4},{6,7},{7,6},{8,9},{9,8},{10,11... | collective-permute-start | bytes 1572872 | tf_op jit(solution)/shard_map/swap_out_2/ppermute | solution.py:326
  63.6 9.2 %collective-permute-start.22 = (bf16[64,4096]{1,0:T(8,128)(2,1)S(1)}, bf16[64,4096]{1,0:T(8,128)(2,1)S(1)}, u32[]{:S(2)}, u32[]{:S(2)}) collective-permute-start(bf16[64,4096]{1,0:T(8,128)(2,1)S(1)} %step_sum.6), channel_id=1, source_target_pairs={{0,4},{1,3},{4,8},{5,1},{8,12},{9,5},{12,14},{13,9},{14,10},{15,13... | collective-permute-start | bytes 1572872 | tf_op jit(solution)/shard_map/return_long_4/ppermute | solution.py:326
  65.7 7.1 %collective-permute-start.21 = (bf16[64,4096]{1,0:T(8,128)(2,1)S(1)}, bf16[64,4096]{1,0:T(8,128)(2,1)S(1)}, u32[]{:S(2)}, u32[]{:S(2)}) collective-permute-start(bf16[64,4096]{1,0:T(8,128)(2,1)S(1)} %get-tuple-element.73), channel_id=1, source_target_pairs={{0,1},{1,0},{2,3},{3,2},{4,5},{5,4},{6,7},{7,6},{8,9},{9,8},{10,11... | collective-permute-start | bytes 1572872 | tf_op jit(solution)/shard_map/swap_out_3/ppermute | solution.py:326
  65.7 13.1 %collective-permute-start.6 = (bf16[64,4096]{1,0:T(8,128)(2,1)S(1)}, bf16[64,4096]{1,0:T(8,128)(2,1)S(1)}, u32[]{:S(2)}, u32[]{:S(2)}) collective-permute-start(bf16[64,4096]{1,0:T(8,128)(2,1)S(1)} %get-tuple-element.57), channel_id=1, source_target_pairs={{0,1},{1,0},{2,3},{3,2},{4,5},{5,4},{6,7},{7,6},{8,9},{9,8},{10,11... | collective-permute-start | bytes 1572872 | tf_op jit(solution)/shard_map/swap_out_1/ppermute | solution.py:326
  66.4 12.4 %collective-permute-start.20 = (bf16[64,4096]{1,0:T(8,128)(2,1)S(1)}, bf16[64,4096]{1,0:T(8,128)(2,1)S(1)}, u32[]{:S(2)}, u32[]{:S(2)}) collective-permute-start(bf16[64,4096]{1,0:T(8,128)(2,1)S(1)} %step_sum.7), channel_id=1, source_target_pairs={{0,4},{1,3},{4,8},{5,1},{8,12},{9,5},{12,14},{13,9},{14,10},{15,13... | collective-permute-start | bytes 1572872 | tf_op jit(solution)/shard_map/return_short_2/ppermute | solution.py:326
  73.1 11.0 %collective-permute-start.28 = (bf16[64,4096]{1,0:T(8,128)(2,1)S(1)}, bf16[64,4096]{1,0:T(8,128)(2,1)S(1)}, u32[]{:S(2)}, u32[]{:S(2)}) collective-permute-start(bf16[64,4096]{1,0:T(8,128)(2,1)S(1)} %step_sum.8), channel_id=1, source_target_pairs={{0,4},{1,3},{4,8},{5,1},{8,12},{9,5},{12,14},{13,9},{14,10},{15,13... | collective-permute-start | bytes 1572872 | tf_op jit(solution)/shard_map/return_long_3/ppermute | solution.py:326
  78.3 5.8 %collective-permute-start.27 = (bf16[64,4096]{1,0:T(8,128)(2,1)S(1)}, bf16[64,4096]{1,0:T(8,128)(2,1)S(1)}, u32[]{:S(2)}, u32[]{:S(2)}) collective-permute-start(bf16[64,4096]{1,0:T(8,128)(2,1)S(1)} %get-tuple-element.80), channel_id=1, source_target_pairs={{0,1},{1,0},{2,3},{3,2},{4,5},{5,4},{6,7},{7,6},{8,9},{9,8},{10,11... | collective-permute-start | bytes 1572872 | tf_op jit(solution)/shard_map/swap_out_2/ppermute | solution.py:326
  78.4 8.1 %collective-permute-start.1 = (bf16[64,4096]{1,0:T(8,128)(2,1)S(1)}, bf16[64,4096]{1,0:T(8,128)(2,1)S(1)}, u32[]{:S(2)}, u32[]{:S(2)}) collective-permute-start(bf16[64,4096]{1,0:T(8,128)(2,1)S(1)} %get-tuple-element.49), channel_id=1, source_target_pairs={{0,1},{1,0},{2,3},{3,2},{4,5},{5,4},{6,7},{7,6},{8,9},{9,8},{10,11... | collective-permute-start | bytes 1572872 | tf_op jit(solution)/shard_map/swap_out_0/ppermute | solution.py:326
  79.1 7.8 %collective-permute-start.23 = (bf16[32,4096]{1,0:T(8,128)(2,1)S(1)}, bf16[32,4096]{1,0:T(8,128)(2,1)S(1)}, u32[]{:S(2)}, u32[]{:S(2)}) collective-permute-start(bf16[32,4096]{1,0:T(8,128)(2,1)S(1)} %get-tuple-element.76), channel_id=1, source_target_pairs={{0,4},{1,3},{4,8},{5,1},{8,12},{9,5},{12,14},{13,9},{14,10},{15,13... | collective-permute-start | bytes 786440 | tf_op jit(solution)/shard_map/return_short_1/ppermute | solution.py:326
  80.8 8.5 %collective-permute-start.24 = (bf16[32,4096]{1,0:T(8,128)(2,1)S(1)}, bf16[32,4096]{1,0:T(8,128)(2,1)S(1)}, u32[]{:S(2)}, u32[]{:S(2)}) collective-permute-start(bf16[32,4096]{1,0:T(8,128)(2,1)S(1)} %get-tuple-element.77), channel_id=1, source_target_pairs={{0,5},{1,2},{4,9},{5,0},{8,13},{9,4},{12,15},{13,8},{14,11},{15,12... | collective-permute-start | bytes 786440 | tf_op jit(solution)/shard_map/return_short_1/ppermute | solution.py:326
  84.1 11.2 %collective-permute-start.25 = (bf16[64,4096]{1,0:T(8,128)(2,1)S(1)}, bf16[64,4096]{1,0:T(8,128)(2,1)S(1)}, u32[]{:S(2)}, u32[]{:S(2)}) collective-permute-start(bf16[64,4096]{1,0:T(8,128)(2,1)S(1)} %get-tuple-element.78), channel_id=1, source_target_pairs={{0,1},{1,0},{2,3},{3,2},{4,5},{5,4},{6,7},{7,6},{8,9},{9,8},{10,11... | collective-permute-start | bytes 1572872 | tf_op jit(solution)/shard_map/swap_out_1/ppermute | solution.py:326
  84.3 11.0 %collective-permute-start.29 = (bf16[64,4096]{1,0:T(8,128)(2,1)S(1)}, bf16[64,4096]{1,0:T(8,128)(2,1)S(1)}, u32[]{:S(2)}, u32[]{:S(2)}) collective-permute-start(bf16[64,4096]{1,0:T(8,128)(2,1)S(1)} %step_sum.9), channel_id=1, source_target_pairs={{0,4},{1,3},{4,8},{5,1},{8,12},{9,5},{12,14},{13,9},{14,10},{15,13... | collective-permute-start | bytes 1572872 | tf_op jit(solution)/shard_map/return_long_2/ppermute | solution.py:326
  95.5 5.9 %collective-permute-start.30 = (bf16[32,4096]{1,0:T(8,128)(2,1)S(1)}, bf16[32,4096]{1,0:T(8,128)(2,1)S(1)}, u32[]{:S(2)}, u32[]{:S(2)}) collective-permute-start(bf16[32,4096]{1,0:T(8,128)(2,1)S(1)} %get-tuple-element.83), channel_id=1, source_target_pairs={{0,5},{1,2},{4,9},{5,0},{8,13},{9,4},{12,15},{13,8},{14,11},{15,12... | collective-permute-start | bytes 786440 | tf_op jit(solution)/shard_map/return_long_1/ppermute | solution.py:326
  96.1 8.7 %collective-permute-start.31 = (bf16[32,4096]{1,0:T(8,128)(2,1)S(1)}, bf16[32,4096]{1,0:T(8,128)(2,1)S(1)}, u32[]{:S(2)}, u32[]{:S(2)}) collective-permute-start(bf16[32,4096]{1,0:T(8,128)(2,1)S(1)} %get-tuple-element.84), channel_id=1, source_target_pairs={{0,4},{1,3},{4,8},{5,1},{8,12},{9,5},{12,14},{13,9},{14,10},{15,13... | collective-permute-start | bytes 786440 | tf_op jit(solution)/shard_map/return_long_1/ppermute | solution.py:326
  (2 other events, 24.3 us)

commit v16 on v15

--- a/solution.py
+++ b/solution.py
@@ -374,7 +374,6 @@
     second = run([(reach - 1, "long")], last, 2)
     short, totals = step(reach - 1, "short", ())
     run([(reach, "long")], [*totals, *second])
-    given[reach, "long"] = after(given[reach, "long"], *short)
     long, totals = step(reach, "long", ())
     for distance in range(reach - 1, 0, -1):
         if 1 < distance < reach - 1:

time: 106 us -> 108 us (1.019)
  waiting for transfers between devices: 41.8 us -> 43.7 us
    ppermute x32, waiting for transfers between devices: 41.8 us -> 43.7 us  [send(): return lax.ppermute(x, 'expert', perm)]
  transfers between devices with their start and end apart: 32 -> 32, of which waited for: 15 -> 16; matrix products, arithmetic and copies ran while one was open for 0% -> 0% of each run, Pallas kernels for 28% -> 25%
where the time goes in v16:
time: 108 us; the launch traced here: 107 us
  waiting for transfers between devices  43.7 us (40%)
  Pallas kernels  32.4 us (30%)
  starting transfers between devices  30.9 us (29%)
    ppermute x32, waiting for transfers between devices, send(): return lax.ppermute(x, 'expert', perm)  43.7 us
    ppermute x32, starting transfers between devices, send(): return lax.ppermute(x, 'expert', perm)  30.9 us
    pallas_call x7, Pallas kernels, expert_part(): pl.pallas_call(functools.partial(expert_kernel, len(blocks)), in_specs=[V...  22.4 us
    pallas_call x1, Pallas kernels, keep(): pl.pallas_call(keep_kernel, in_specs=[ANYWHERE] * 2, out_specs=[VMEM] * 2...  6.38 us
  transfers between devices with their start and end apart: 32, of which 16 were waited for; matrix products, arithmetic and copies ran while one was open for 0% of the time, Pallas kernels for 25%

profile of v16, /device:TPU:0, one launch (start us, length us, event | category | flops | bytes accessed | tf_op | source)
XLA Modules:
  0.0 107.4 jit_solution(13048876005350867176)
XLA Ops:
  1.8 2.6 %collective-permute-start.2 = (bf16[64,4224]{1,0:T(8,128)(2,1)S(1)}, bf16[64,4224]{1,0:T(8,128)(2,1)S(1)}, u32[]{:S(2)}, u32[]{:S(2)}) collective-permute-start(bf16[64,4224]{1,0:T(8,128)(2,1)S(1)} %get-tuple-element.44.refs_0_), channel_id=1, source_target_pairs={{0,4},{1,3},{4,8},{5,1},{8,12},{9,5},{12,14},{13,9},{14,10},{15,13... | collective-permute-start | bytes 1622024 | tf_op jit(solution)/shard_map/gather_long_1/ppermute | solution.py:326
  5.7 6.4 %keep.1 = (bf16[4096,1536]{1,0:T(8,128)(2,1)S(1)}, bf16[768,4096]{1,0:T(8,128)(2,1)S(1)}) custom-call(bf16[4096,1536]{1,0:T(8,128)(2,1)} %bitcast.5, bf16[768,4096]{1,0:T(8,128)(2,1)} %bitcast.6), custom_call_target="tpu_custom_call" | custom-call | bytes 18874368 | tf_op jit(solution)/shard_map/keep/pallas_call | solution.py:88
  12.2 2.9 %expert.7 = (bf16[64,4096]{1,0:T(8,128)(2,1)S(1)}, bf16[64,4096]{1,0:T(8,128)(2,1)S(1)}) custom-call(bf16[64,4224]{1,0:T(8,128)(2,1)S(1)} %get-tuple-element.44.refs_0_, bf16[64,4224]{1,0:T(8,128)(2,1)S(1)} %collective-permute-done.refs_1_, f32[1,128]{1,0:T(1,128)S(1)} %compare_select_fusion.1.refs_2_.refs_4_, f32[1,1536]{1,0:T(1,128)S(1)} %copy-done.1, ...), custom_call_target="tpu_custom_call" | custom-call | flops 4831838208 | tf_op jit(solution)/shard_map/expert/pallas_call | solution.py:146
  16.1 1.4 %collective-permute-done.3.cross = bf16[64,4224]{1,0:T(8,128)(2,1)S(1)} collective-permute-done((bf16[64,4224]{1,0:T(8,128)(2,1)S(1)}, bf16[64,4224]{1,0:T(8,128)(2,1)S(1)}, u32[]{:S(2)}, u32[]{:S(2)}) %collective-permute-start.3) | collective-permute-done | bytes 540704 | tf_op jit(solution)/shard_map/gather_long_1/ppermute | solution.py:326
  18.2 2.1 %collective-permute-start.7 = (bf16[64,4224]{1,0:T(8,128)(2,1)S(1)}, bf16[64,4224]{1,0:T(8,128)(2,1)S(1)}, u32[]{:S(2)}, u32[]{:S(2)}) collective-permute-start(bf16[64,4224]{1,0:T(8,128)(2,1)S(1)} %get-tuple-element.54.refs_3_), channel_id=1, source_target_pairs={{0,4},{1,3},{4,8},{5,1},{8,12},{9,5},{12,14},{13,9},{14,10},{15,13... | collective-permute-start | bytes 1622024 | tf_op jit(solution)/shard_map/gather_short_2/ppermute | solution.py:326
  20.3 1.6 %collective-permute-start.14 = (bf16[64,4224]{1,0:T(8,128)(2,1)S(1)}, bf16[64,4224]{1,0:T(8,128)(2,1)S(1)}, u32[]{:S(2)}, u32[]{:S(2)}) collective-permute-start(bf16[64,4224]{1,0:T(8,128)(2,1)S(1)} %get-tuple-element.52.refs_2_), channel_id=1, source_target_pairs={{0,4},{1,3},{4,8},{5,1},{8,12},{9,5},{12,14},{13,9},{14,10},{15,13... | collective-permute-start | bytes 1622024 | tf_op jit(solution)/shard_map/gather_long_2/ppermute | solution.py:326
  21.8 5.2 %expert.8 = (bf16[64,4096]{1,0:T(8,128)(2,1)S(1)}, bf16[64,4096]{1,0:T(8,128)(2,1)S(1)}, bf16[64,4096]{1,0:T(8,128)(2,1)S(1)}, bf16[64,4096]{1,0:T(8,128)(2,1)S(1)}) custom-call(bf16[64,4224]{1,0:T(8,128)(2,1)S(1)} %collective-permute-done.4.refs_0_, bf16[64,4224]{1,0:T(8,128)(2,1)S(1)} %collective-permute-done.5.refs_1_, ...), custom_call_target="tpu_custom_call" | custom-call | flops 9663676416 | tf_op jit(solution)/shard_map/expert/pallas_call | solution.py:146
  27.5 2.1 %collective-permute-start.10 = (bf16[64,4224]{1,0:T(8,128)(2,1)S(1)}, bf16[64,4224]{1,0:T(8,128)(2,1)S(1)}, u32[]{:S(2)}, u32[]{:S(2)}) collective-permute-start(bf16[64,4224]{1,0:T(8,128)(2,1)S(1)} %collective-permute-done.7.refs_1_), channel_id=1, source_target_pairs={{0,4},{1,3},{4,8},{5,1},{8,12},{9,5},{12,14},{13,9},{14,10},{15,13... | collective-permute-start | bytes 1622024 | tf_op jit(solution)/shard_map/gather_short_3/ppermute | solution.py:326
  29.6 3.7 %collective-permute-done.14.refs_1_ = bf16[64,4224]{1,0:T(8,128)(2,1)S(1)} collective-permute-done((bf16[64,4224]{1,0:T(8,128)(2,1)S(1)}, bf16[64,4224]{1,0:T(8,128)(2,1)S(1)}, u32[]{:S(2)}, u32[]{:S(2)}) %collective-permute-start.14) | collective-permute-done | bytes 540704 | tf_op jit(solution)/shard_map/gather_long_2/ppermute | solution.py:326
  33.3 2.1 %collective-permute-start.15 = (bf16[64,4224]{1,0:T(8,128)(2,1)S(1)}, bf16[64,4224]{1,0:T(8,128)(2,1)S(1)}, u32[]{:S(2)}, u32[]{:S(2)}) collective-permute-start(bf16[64,4224]{1,0:T(8,128)(2,1)S(1)} %collective-permute-done.14.refs_1_), channel_id=1, source_target_pairs={{0,4},{1,3},{4,8},{5,1},{8,12},{9,5},{12,14},{13,9},{14,10},{15,13... | collective-permute-start | bytes 1622024 | tf_op jit(solution)/shard_map/gather_long_3/ppermute | solution.py:326
  35.4 2.9 %expert.9 = (bf16[64,4096]{1,0:T(8,128)(2,1)S(1)}, bf16[64,4096]{1,0:T(8,128)(2,1)S(1)}) custom-call(bf16[64,4224]{1,0:T(8,128)(2,1)S(1)} %collective-permute-done.8.refs_0_, bf16[64,4224]{1,0:T(8,128)(2,1)S(1)} %collective-permute-done.7.refs_1_, f32[1,128]{1,0:T(1,128)S(1)} %compare_select_fusion.1.refs_2_.refs_4_, f32[1,1536]{1,0:T(1,128)S(1)} %copy-done.1, ...), custom_call_target="tpu_custom_call" | custom-call | flops 4831838208 | tf_op jit(solution)/shard_map/expert/pallas_call | solution.py:146
  39.1 5.8 %collective-permute-done.15.refs_1_ = bf16[64,4224]{1,0:T(8,128)(2,1)S(1)} collective-permute-done((bf16[64,4224]{1,0:T(8,128)(2,1)S(1)}, bf16[64,4224]{1,0:T(8,128)(2,1)S(1)}, u32[]{:S(2)}, u32[]{:S(2)}) %collective-permute-start.15) | collective-permute-done | bytes 540704 | tf_op jit(solution)/shard_map/gather_long_3/ppermute | solution.py:326
  44.9 2.1 %collective-permute-start.16 = (bf16[64,4224]{1,0:T(8,128)(2,1)S(1)}, bf16[64,4224]{1,0:T(8,128)(2,1)S(1)}, u32[]{:S(2)}, u32[]{:S(2)}) collective-permute-start(bf16[64,4224]{1,0:T(8,128)(2,1)S(1)} %collective-permute-done.15.refs_1_), channel_id=1, source_target_pairs={{0,4},{1,3},{4,8},{5,1},{8,12},{9,5},{12,14},{13,9},{14,10},{15,13... | collective-permute-start | bytes 1622024 | tf_op jit(solution)/shard_map/gather_long_4/ppermute | solution.py:326
  47.0 2.9 %expert.10 = (bf16[64,4096]{1,0:T(8,128)(2,1)S(1)}, bf16[64,4096]{1,0:T(8,128)(2,1)S(1)}) custom-call(bf16[64,4224]{1,0:T(8,128)(2,1)S(1)} %collective-permute-done.11.refs_0_, bf16[64,4224]{1,0:T(8,128)(2,1)S(1)} %collective-permute-done.10.refs_1_, f32[1,128]{1,0:T(1,128)S(1)} %compare_select_fusion.1.refs_2_.refs_4_, f32[1,1536]{1,0:T(1,128)S(1)} %copy-done.1, ...), custom_call_target="tpu_custom_call" | custom-call | flops 4831838208 | tf_op jit(solution)/shard_map/expert/pallas_call | solution.py:146
  50.1 2.9 %expert.11 = (bf16[64,4096]{1,0:T(8,128)(2,1)S(1)}, bf16[64,4096]{1,0:T(8,128)(2,1)S(1)}) custom-call(bf16[64,4224]{1,0:T(8,128)(2,1)S(1)} %collective-permute-done.17.refs_0_, bf16[64,4224]{1,0:T(8,128)(2,1)S(1)} %collective-permute-done.15.refs_1_, f32[1,128]{1,0:T(1,128)S(1)} %compare_select_fusion.1.refs_2_.refs_4_, f32[1,1536]{1,0:T(1,128)S(1)} %copy-done.1, ...), custom_call_target="tpu_custom_call" | custom-call | flops 4831838208 | tf_op jit(solution)/shard_map/expert/pallas_call | solution.py:146
  54.3 1.9 %collective-permute-done.18.refs_0_ = bf16[64,4224]{1,0:T(8,128)(2,1)S(1)} collective-permute-done((bf16[64,4224]{1,0:T(8,128)(2,1)S(1)}, bf16[64,4224]{1,0:T(8,128)(2,1)S(1)}, u32[]{:S(2)}, u32[]{:S(2)}) %collective-permute-start.18) | collective-permute-done | bytes 540704 | tf_op jit(solution)/shard_map/swap_in_4/ppermute | solution.py:326
  56.2 2.9 %expert.12 = (bf16[64,4096]{1,0:T(8,128)(2,1)S(1)}, bf16[64,4096]{1,0:T(8,128)(2,1)S(1)}) custom-call(bf16[64,4224]{1,0:T(8,128)(2,1)S(1)} %collective-permute-done.18.refs_0_, bf16[64,4224]{1,0:T(8,128)(2,1)S(1)} %collective-permute-done.16.refs_1_, f32[1,128]{1,0:T(1,128)S(1)} %compare_select_fusion.1.refs_2_.refs_4_, f32[1,1536]{1,0:T(1,128)S(1)} %copy-done.1, ...), custom_call_target="tpu_custom_call" | custom-call | flops 4831838208 | tf_op jit(solution)/shard_map/expert/pallas_call | solution.py:146
  59.7 2.1 %collective-permute-start.13 = (bf16[64,4096]{1,0:T(8,128)(2,1)S(1)}, bf16[64,4096]{1,0:T(8,128)(2,1)S(1)}, u32[]{:S(2)}, u32[]{:S(2)}) collective-permute-start(bf16[64,4096]{1,0:T(8,128)(2,1)S(1)} %step_sum.5), channel_id=1, source_target_pairs={{0,4},{1,3},{4,8},{5,1},{8,12},{9,5},{12,14},{13,9},{14,10},{15,13... | collective-permute-start | bytes 1572872 | tf_op jit(solution)/shard_map/return_short_3/ppermute | solution.py:326
  61.9 1.6 %collective-permute-start.22 = (bf16[64,4096]{1,0:T(8,128)(2,1)S(1)}, bf16[64,4096]{1,0:T(8,128)(2,1)S(1)}, u32[]{:S(2)}, u32[]{:S(2)}) collective-permute-start(bf16[64,4096]{1,0:T(8,128)(2,1)S(1)} %step_sum.6), channel_id=1, source_target_pairs={{0,4},{1,3},{4,8},{5,1},{8,12},{9,5},{12,14},{13,9},{14,10},{15,13... | collective-permute-start | bytes 1572872 | tf_op jit(solution)/shard_map/return_long_4/ppermute | solution.py:326
  63.5 5.3 %collective-permute-done.13.refs_2_ = bf16[64,4096]{1,0:T(8,128)(2,1)S(1)} collective-permute-done((bf16[64,4096]{1,0:T(8,128)(2,1)S(1)}, bf16[64,4096]{1,0:T(8,128)(2,1)S(1)}, u32[]{:S(2)}, u32[]{:S(2)}) %collective-permute-start.13) | collective-permute-done | bytes 524320 | tf_op jit(solution)/shard_map/return_short_3/ppermute | solution.py:326
  69.1 2.1 %collective-permute-start.20 = (bf16[64,4096]{1,0:T(8,128)(2,1)S(1)}, bf16[64,4096]{1,0:T(8,128)(2,1)S(1)}, u32[]{:S(2)}, u32[]{:S(2)}) collective-permute-start(bf16[64,4096]{1,0:T(8,128)(2,1)S(1)} %step_sum.7), channel_id=1, source_target_pairs={{0,4},{1,3},{4,8},{5,1},{8,12},{9,5},{12,14},{13,9},{14,10},{15,13... | collective-permute-start | bytes 1572872 | tf_op jit(solution)/shard_map/return_short_2/ppermute | solution.py:326
  71.2 3.3 %collective-permute-done.22.refs_2_ = bf16[64,4096]{1,0:T(8,128)(2,1)S(1)} collective-permute-done((bf16[64,4096]{1,0:T(8,128)(2,1)S(1)}, bf16[64,4096]{1,0:T(8,128)(2,1)S(1)}, u32[]{:S(2)}, u32[]{:S(2)}) %collective-permute-start.22) | collective-permute-done | bytes 524320 | tf_op jit(solution)/shard_map/return_long_4/ppermute | solution.py:326
  74.7 2.3 %collective-permute-start.28 = (bf16[64,4096]{1,0:T(8,128)(2,1)S(1)}, bf16[64,4096]{1,0:T(8,128)(2,1)S(1)}, u32[]{:S(2)}, u32[]{:S(2)}) collective-permute-start(bf16[64,4096]{1,0:T(8,128)(2,1)S(1)} %step_sum.8), channel_id=1, source_target_pairs={{0,4},{1,3},{4,8},{5,1},{8,12},{9,5},{12,14},{13,9},{14,10},{15,13... | collective-permute-start | bytes 1572872 | tf_op jit(solution)/shard_map/return_long_3/ppermute | solution.py:326
  77.0 2.9 %expert.13 = (bf16[64,4096]{1,0:T(8,128)(2,1)S(1)}, bf16[64,4096]{1,0:T(8,128)(2,1)S(1)}) custom-call(bf16[64,4224]{1,0:T(8,128)(2,1)S(1)} %collective-permute-done.26.refs_0_, bf16[64,4224]{1,0:T(8,128)(2,1)S(1)} %collective-permute-done.14.refs_1_, f32[1,128]{1,0:T(1,128)S(1)} %compare_select_fusion.1.refs_2_.refs_4_, f32[1,1536]{1,0:T(1,128)S(1)} %copy-done.1, ...), custom_call_target="tpu_custom_call" | custom-call | flops 4831838208 | tf_op jit(solution)/shard_map/expert/pallas_call | solution.py:146
  80.7 1.7 %collective-permute-start.23 = (bf16[32,4096]{1,0:T(8,128)(2,1)S(1)}, bf16[32,4096]{1,0:T(8,128)(2,1)S(1)}, u32[]{:S(2)}, u32[]{:S(2)}) collective-permute-start(bf16[32,4096]{1,0:T(8,128)(2,1)S(1)} %get-tuple-element.74), channel_id=1, source_target_pairs={{0,4},{1,3},{4,8},{5,1},{8,12},{9,5},{12,14},{13,9},{14,10},{15,13... | collective-permute-start | bytes 786440 | tf_op jit(solution)/shard_map/return_short_1/ppermute | solution.py:326
  82.4 3.3 %collective-permute-done.28.refs_2_ = bf16[64,4096]{1,0:T(8,128)(2,1)S(1)} collective-permute-done((bf16[64,4096]{1,0:T(8,128)(2,1)S(1)}, bf16[64,4096]{1,0:T(8,128)(2,1)S(1)}, u32[]{:S(2)}, u32[]{:S(2)}) %collective-permute-start.28) | collective-permute-done | bytes 524320 | tf_op jit(solution)/shard_map/return_long_3/ppermute | solution.py:326
  85.9 2.1 %collective-permute-start.29 = (bf16[64,4096]{1,0:T(8,128)(2,1)S(1)}, bf16[64,4096]{1,0:T(8,128)(2,1)S(1)}, u32[]{:S(2)}, u32[]{:S(2)}) collective-permute-start(bf16[64,4096]{1,0:T(8,128)(2,1)S(1)} %step_sum.9), channel_id=1, source_target_pairs={{0,4},{1,3},{4,8},{5,1},{8,12},{9,5},{12,14},{13,9},{14,10},{15,13... | collective-permute-start | bytes 1572872 | tf_op jit(solution)/shard_map/return_long_2/ppermute | solution.py:326
  88.5 2.4 %collective-permute-done.24.short_cross = bf16[32,4096]{1,0:T(8,128)(2,1)S(1)} collective-permute-done((bf16[32,4096]{1,0:T(8,128)(2,1)S(1)}, bf16[32,4096]{1,0:T(8,128)(2,1)S(1)}, u32[]{:S(2)}, u32[]{:S(2)}) %collective-permute-start.24) | collective-permute-done | bytes 262176 | tf_op jit(solution)/shard_map/return_short_1/ppermute | solution.py:326
  91.1 5.9 %collective-permute-done.29.refs_2_ = bf16[64,4096]{1,0:T(8,128)(2,1)S(1)} collective-permute-done((bf16[64,4096]{1,0:T(8,128)(2,1)S(1)}, bf16[64,4096]{1,0:T(8,128)(2,1)S(1)}, u32[]{:S(2)}, u32[]{:S(2)}) %collective-permute-start.29) | collective-permute-done | bytes 524320 | tf_op jit(solution)/shard_map/return_long_2/ppermute | solution.py:326
  98.2 1.6 %collective-permute-start.31 = (bf16[32,4096]{1,0:T(8,128)(2,1)S(1)}, bf16[32,4096]{1,0:T(8,128)(2,1)S(1)}, u32[]{:S(2)}, u32[]{:S(2)}) collective-permute-start(bf16[32,4096]{1,0:T(8,128)(2,1)S(1)} %get-tuple-element.82), channel_id=1, source_target_pairs={{0,4},{1,3},{4,8},{5,1},{8,12},{9,5},{12,14},{13,9},{14,10},{15,13... | collective-permute-start | bytes 786440 | tf_op jit(solution)/shard_map/return_long_1/ppermute | solution.py:326
  99.7 3.3 %collective-permute-done.30.long_cross = bf16[32,4096]{1,0:T(8,128)(2,1)S(1)} collective-permute-done((bf16[32,4096]{1,0:T(8,128)(2,1)S(1)}, bf16[32,4096]{1,0:T(8,128)(2,1)S(1)}, u32[]{:S(2)}, u32[]{:S(2)}) %collective-permute-start.30) | collective-permute-done | bytes 262176 | tf_op jit(solution)/shard_map/return_long_1/ppermute | solution.py:326
  103.0 3.4 %collective-permute-done.31.long_same = bf16[32,4096]{1,0:T(8,128)(2,1)S(1)} collective-permute-done((bf16[32,4096]{1,0:T(8,128)(2,1)S(1)}, bf16[32,4096]{1,0:T(8,128)(2,1)S(1)}, u32[]{:S(2)}, u32[]{:S(2)}) %collective-permute-start.31) | collective-permute-done | bytes 262176 | tf_op jit(solution)/shard_map/return_long_1/ppermute | solution.py:326
  (56 shorter events, 12.5 us)
Async XLA Ops:
  1.3 10.9 %collective-permute-start = (bf16[64,4224]{1,0:T(8,128)(2,1)S(1)}, bf16[64,4224]{1,0:T(8,128)(2,1)S(1)}, u32[]{:S(2)}, u32[]{:S(2)}) collective-permute-start(bf16[64,4224]{1,0:T(8,128)(2,1)S(1)} %get-tuple-element.44.refs_0_), channel_id=1, source_target_pairs={{0,1},{1,0},{2,3},{3,2},{4,5},{5,4},{6,7},{7,6},{8,9},{9,8},{10,11... | collective-permute-start | bytes 1622024 | tf_op jit(solution)/shard_map/swap_in_0/ppermute | solution.py:326
  1.8 14.3 %collective-permute-start.2 = (bf16[64,4224]{1,0:T(8,128)(2,1)S(1)}, bf16[64,4224]{1,0:T(8,128)(2,1)S(1)}, u32[]{:S(2)}, u32[]{:S(2)}) collective-permute-start(bf16[64,4224]{1,0:T(8,128)(2,1)S(1)} %get-tuple-element.44.refs_0_), channel_id=1, source_target_pairs={{0,4},{1,3},{4,8},{5,1},{8,12},{9,5},{12,14},{13,9},{14,10},{15,13... | collective-permute-start | bytes 1622024 | tf_op jit(solution)/shard_map/gather_long_1/ppermute | solution.py:326
  4.5 13.1 %collective-permute-start.3 = (bf16[64,4224]{1,0:T(8,128)(2,1)S(1)}, bf16[64,4224]{1,0:T(8,128)(2,1)S(1)}, u32[]{:S(2)}, u32[]{:S(2)}) collective-permute-start(bf16[64,4224]{1,0:T(8,128)(2,1)S(1)} %get-tuple-element.50), channel_id=1, source_target_pairs={{0,3},{1,4},{4,1},{5,8},{8,5},{9,12},{12,9},{13,14},{14,13},{15,10... | collective-permute-start | bytes 1622024 | tf_op jit(solution)/shard_map/gather_long_1/ppermute | solution.py:326
  17.6 4.2 %collective-permute-start.4 = (bf16[64,4224]{1,0:T(8,128)(2,1)S(1)}, bf16[64,4224]{1,0:T(8,128)(2,1)S(1)}, u32[]{:S(2)}, u32[]{:S(2)}) collective-permute-start(bf16[64,4224]{1,0:T(8,128)(2,1)S(1)} %get-tuple-element.52.refs_2_), channel_id=1, source_target_pairs={{0,1},{1,0},{2,3},{3,2},{4,5},{5,4},{6,7},{7,6},{8,9},{9,8},{10,11... | collective-permute-start | bytes 1622024 | tf_op jit(solution)/shard_map/swap_in_1/ppermute | solution.py:326
  17.7 4.2 %collective-permute-start.5 = (bf16[64,4224]{1,0:T(8,128)(2,1)S(1)}, bf16[64,4224]{1,0:T(8,128)(2,1)S(1)}, u32[]{:S(2)}, u32[]{:S(2)}) collective-permute-start(bf16[64,4224]{1,0:T(8,128)(2,1)S(1)} %get-tuple-element.54.refs_3_), channel_id=1, source_target_pairs={{0,1},{1,0},{2,3},{3,2},{4,5},{5,4},{6,7},{7,6},{8,9},{9,8},{10,11... | collective-permute-start | bytes 1622024 | tf_op jit(solution)/shard_map/swap_in_1/ppermute | solution.py:326
  18.2 9.4 %collective-permute-start.7 = (bf16[64,4224]{1,0:T(8,128)(2,1)S(1)}, bf16[64,4224]{1,0:T(8,128)(2,1)S(1)}, u32[]{:S(2)}, u32[]{:S(2)}) collective-permute-start(bf16[64,4224]{1,0:T(8,128)(2,1)S(1)} %get-tuple-element.54.refs_3_), channel_id=1, source_target_pairs={{0,4},{1,3},{4,8},{5,1},{8,12},{9,5},{12,14},{13,9},{14,10},{15,13... | collective-permute-start | bytes 1622024 | tf_op jit(solution)/shard_map/gather_short_2/ppermute | solution.py:326
  20.3 13.1 %collective-permute-start.14 = (bf16[64,4224]{1,0:T(8,128)(2,1)S(1)}, bf16[64,4224]{1,0:T(8,128)(2,1)S(1)}, u32[]{:S(2)}, u32[]{:S(2)}) collective-permute-start(bf16[64,4224]{1,0:T(8,128)(2,1)S(1)} %get-tuple-element.52.refs_2_), channel_id=1, source_target_pairs={{0,4},{1,3},{4,8},{5,1},{8,12},{9,5},{12,14},{13,9},{14,10},{15,13... | collective-permute-start | bytes 1622024 | tf_op jit(solution)/shard_map/gather_long_2/ppermute | solution.py:326
  27.5 7.9 %collective-permute-start.8 = (bf16[64,4224]{1,0:T(8,128)(2,1)S(1)}, bf16[64,4224]{1,0:T(8,128)(2,1)S(1)}, u32[]{:S(2)}, u32[]{:S(2)}) collective-permute-start(bf16[64,4224]{1,0:T(8,128)(2,1)S(1)} %collective-permute-done.7.refs_1_), channel_id=1, source_target_pairs={{0,1},{1,0},{2,3},{3,2},{4,5},{5,4},{6,7},{7,6},{8,9},{9,8},{10,11... | collective-permute-start | bytes 1622024 | tf_op jit(solution)/shard_map/swap_in_2/ppermute | solution.py:326
  27.5 11.6 %collective-permute-start.10 = (bf16[64,4224]{1,0:T(8,128)(2,1)S(1)}, bf16[64,4224]{1,0:T(8,128)(2,1)S(1)}, u32[]{:S(2)}, u32[]{:S(2)}) collective-permute-start(bf16[64,4224]{1,0:T(8,128)(2,1)S(1)} %collective-permute-done.7.refs_1_), channel_id=1, source_target_pairs={{0,4},{1,3},{4,8},{5,1},{8,12},{9,5},{12,14},{13,9},{14,10},{15,13... | collective-permute-start | bytes 1622024 | tf_op jit(solution)/shard_map/gather_short_3/ppermute | solution.py:326
  33.3 11.6 %collective-permute-start.15 = (bf16[64,4224]{1,0:T(8,128)(2,1)S(1)}, bf16[64,4224]{1,0:T(8,128)(2,1)S(1)}, u32[]{:S(2)}, u32[]{:S(2)}) collective-permute-start(bf16[64,4224]{1,0:T(8,128)(2,1)S(1)} %collective-permute-done.14.refs_1_), channel_id=1, source_target_pairs={{0,4},{1,3},{4,8},{5,1},{8,12},{9,5},{12,14},{13,9},{14,10},{15,13... | collective-permute-start | bytes 1622024 | tf_op jit(solution)/shard_map/gather_long_3/ppermute | solution.py:326
  39.1 7.9 %collective-permute-start.11 = (bf16[64,4224]{1,0:T(8,128)(2,1)S(1)}, bf16[64,4224]{1,0:T(8,128)(2,1)S(1)}, u32[]{:S(2)}, u32[]{:S(2)}) collective-permute-start(bf16[64,4224]{1,0:T(8,128)(2,1)S(1)} %collective-permute-done.10.refs_1_), channel_id=1, source_target_pairs={{0,1},{1,0},{2,3},{3,2},{4,5},{5,4},{6,7},{7,6},{8,9},{9,8},{10,11... | collective-permute-start | bytes 1622024 | tf_op jit(solution)/shard_map/swap_in_3/ppermute | solution.py:326
  44.9 5.2 %collective-permute-start.17 = (bf16[64,4224]{1,0:T(8,128)(2,1)S(1)}, bf16[64,4224]{1,0:T(8,128)(2,1)S(1)}, u32[]{:S(2)}, u32[]{:S(2)}) collective-permute-start(bf16[64,4224]{1,0:T(8,128)(2,1)S(1)} %collective-permute-done.15.refs_1_), channel_id=1, source_target_pairs={{0,1},{1,0},{2,3},{3,2},{4,5},{5,4},{6,7},{7,6},{8,9},{9,8},{10,11... | collective-permute-start | bytes 1622024 | tf_op jit(solution)/shard_map/swap_in_3/ppermute | solution.py:326
  44.9 9.4 %collective-permute-start.16 = (bf16[64,4224]{1,0:T(8,128)(2,1)S(1)}, bf16[64,4224]{1,0:T(8,128)(2,1)S(1)}, u32[]{:S(2)}, u32[]{:S(2)}) collective-permute-start(bf16[64,4224]{1,0:T(8,128)(2,1)S(1)} %collective-permute-done.15.refs_1_), channel_id=1, source_target_pairs={{0,4},{1,3},{4,8},{5,1},{8,12},{9,5},{12,14},{13,9},{14,10},{15,13... | collective-permute-start | bytes 1622024 | tf_op jit(solution)/shard_map/gather_long_4/ppermute | solution.py:326
  49.9 3.1 %collective-permute-start.12 = (bf16[64,4096]{1,0:T(8,128)(2,1)S(1)}, bf16[64,4096]{1,0:T(8,128)(2,1)S(1)}, u32[]{:S(2)}, u32[]{:S(2)}) collective-permute-start(bf16[64,4096]{1,0:T(8,128)(2,1)S(1)} %get-tuple-element.63), channel_id=1, source_target_pairs={{0,1},{1,0},{2,3},{3,2},{4,5},{5,4},{6,7},{7,6},{8,9},{9,8},{10,11... | collective-permute-start | bytes 1572872 | tf_op jit(solution)/shard_map/swap_out_3/ppermute | solution.py:326
  54.3 1.9 %collective-permute-start.18 = (bf16[64,4224]{1,0:T(8,128)(2,1)S(1)}, bf16[64,4224]{1,0:T(8,128)(2,1)S(1)}, u32[]{:S(2)}, u32[]{:S(2)}) collective-permute-start(bf16[64,4224]{1,0:T(8,128)(2,1)S(1)} %collective-permute-done.16.refs_1_), channel_id=1, source_target_pairs={{0,1},{1,0},{2,3},{3,2},{4,5},{5,4},{6,7},{7,6},{8,9},{9,8},{10,11... | collective-permute-start | bytes 1622024 | tf_op jit(solution)/shard_map/swap_in_4/ppermute | solution.py:326
  59.1 2.7 %collective-permute-start.19 = (bf16[64,4096]{1,0:T(8,128)(2,1)S(1)}, bf16[64,4096]{1,0:T(8,128)(2,1)S(1)}, u32[]{:S(2)}, u32[]{:S(2)}) collective-permute-start(bf16[64,4096]{1,0:T(8,128)(2,1)S(1)} %get-tuple-element.69), channel_id=1, source_target_pairs={{0,1},{1,0},{2,3},{3,2},{4,5},{5,4},{6,7},{7,6},{8,9},{9,8},{10,11... | collective-permute-start | bytes 1572872 | tf_op jit(solution)/shard_map/swap_out_4/ppermute | solution.py:326
  59.3 17.7 %collective-permute-start.26 = (bf16[64,4224]{1,0:T(8,128)(2,1)S(1)}, bf16[64,4224]{1,0:T(8,128)(2,1)S(1)}, u32[]{:S(2)}, u32[]{:S(2)}) collective-permute-start(bf16[64,4224]{1,0:T(8,128)(2,1)S(1)} %collective-permute-done.14.refs_1_), channel_id=1, source_target_pairs={{0,1},{1,0},{2,3},{3,2},{4,5},{5,4},{6,7},{7,6},{8,9},{9,8},{10,11... | collective-permute-start | bytes 1622024 | tf_op jit(solution)/shard_map/swap_in_2/ppermute | solution.py:326
  59.7 9.2 %collective-permute-start.13 = (bf16[64,4096]{1,0:T(8,128)(2,1)S(1)}, bf16[64,4096]{1,0:T(8,128)(2,1)S(1)}, u32[]{:S(2)}, u32[]{:S(2)}) collective-permute-start(bf16[64,4096]{1,0:T(8,128)(2,1)S(1)} %step_sum.5), channel_id=1, source_target_pairs={{0,4},{1,3},{4,8},{5,1},{8,12},{9,5},{12,14},{13,9},{14,10},{15,13... | collective-permute-start | bytes 1572872 | tf_op jit(solution)/shard_map/return_short_3/ppermute | solution.py:326
  61.7 7.1 %collective-permute-start.9 = (bf16[64,4096]{1,0:T(8,128)(2,1)S(1)}, bf16[64,4096]{1,0:T(8,128)(2,1)S(1)}, u32[]{:S(2)}, u32[]{:S(2)}) collective-permute-start(bf16[64,4096]{1,0:T(8,128)(2,1)S(1)} %get-tuple-element.60), channel_id=1, source_target_pairs={{0,1},{1,0},{2,3},{3,2},{4,5},{5,4},{6,7},{7,6},{8,9},{9,8},{10,11... | collective-permute-start | bytes 1572872 | tf_op jit(solution)/shard_map/swap_out_2/ppermute | solution.py:326
  61.9 12.6 %collective-permute-start.22 = (bf16[64,4096]{1,0:T(8,128)(2,1)S(1)}, bf16[64,4096]{1,0:T(8,128)(2,1)S(1)}, u32[]{:S(2)}, u32[]{:S(2)}) collective-permute-start(bf16[64,4096]{1,0:T(8,128)(2,1)S(1)} %step_sum.6), channel_id=1, source_target_pairs={{0,4},{1,3},{4,8},{5,1},{8,12},{9,5},{12,14},{13,9},{14,10},{15,13... | collective-permute-start | bytes 1572872 | tf_op jit(solution)/shard_map/return_long_4/ppermute | solution.py:326
  63.5 11.0 %collective-permute-start.21 = (bf16[64,4096]{1,0:T(8,128)(2,1)S(1)}, bf16[64,4096]{1,0:T(8,128)(2,1)S(1)}, u32[]{:S(2)}, u32[]{:S(2)}) collective-permute-start(bf16[64,4096]{1,0:T(8,128)(2,1)S(1)} %get-tuple-element.71), channel_id=1, source_target_pairs={{0,1},{1,0},{2,3},{3,2},{4,5},{5,4},{6,7},{7,6},{8,9},{9,8},{10,11... | collective-permute-start | bytes 1572872 | tf_op jit(solution)/shard_map/swap_out_3/ppermute | solution.py:326
  68.9 11.6 %collective-permute-start.6 = (bf16[64,4096]{1,0:T(8,128)(2,1)S(1)}, bf16[64,4096]{1,0:T(8,128)(2,1)S(1)}, u32[]{:S(2)}, u32[]{:S(2)}) collective-permute-start(bf16[64,4096]{1,0:T(8,128)(2,1)S(1)} %get-tuple-element.56), channel_id=1, source_target_pairs={{0,1},{1,0},{2,3},{3,2},{4,5},{5,4},{6,7},{7,6},{8,9},{9,8},{10,11... | collective-permute-start | bytes 1572872 | tf_op jit(solution)/shard_map/swap_out_1/ppermute | solution.py:326
  69.1 11.4 %collective-permute-start.20 = (bf16[64,4096]{1,0:T(8,128)(2,1)S(1)}, bf16[64,4096]{1,0:T(8,128)(2,1)S(1)}, u32[]{:S(2)}, u32[]{:S(2)}) collective-permute-start(bf16[64,4096]{1,0:T(8,128)(2,1)S(1)} %step_sum.7), channel_id=1, source_target_pairs={{0,4},{1,3},{4,8},{5,1},{8,12},{9,5},{12,14},{13,9},{14,10},{15,13... | collective-permute-start | bytes 1572872 | tf_op jit(solution)/shard_map/return_short_2/ppermute | solution.py:326
  74.7 11.0 %collective-permute-start.28 = (bf16[64,4096]{1,0:T(8,128)(2,1)S(1)}, bf16[64,4096]{1,0:T(8,128)(2,1)S(1)}, u32[]{:S(2)}, u32[]{:S(2)}) collective-permute-start(bf16[64,4096]{1,0:T(8,128)(2,1)S(1)} %step_sum.8), channel_id=1, source_target_pairs={{0,4},{1,3},{4,8},{5,1},{8,12},{9,5},{12,14},{13,9},{14,10},{15,13... | collective-permute-start | bytes 1572872 | tf_op jit(solution)/shard_map/return_long_3/ppermute | solution.py:326
  79.9 5.8 %collective-permute-start.27 = (bf16[64,4096]{1,0:T(8,128)(2,1)S(1)}, bf16[64,4096]{1,0:T(8,128)(2,1)S(1)}, u32[]{:S(2)}, u32[]{:S(2)}) collective-permute-start(bf16[64,4096]{1,0:T(8,128)(2,1)S(1)} %get-tuple-element.78), channel_id=1, source_target_pairs={{0,1},{1,0},{2,3},{3,2},{4,5},{5,4},{6,7},{7,6},{8,9},{9,8},{10,11... | collective-permute-start | bytes 1572872 | tf_op jit(solution)/shard_map/swap_out_2/ppermute | solution.py:326
  80.0 8.1 %collective-permute-start.1 = (bf16[64,4096]{1,0:T(8,128)(2,1)S(1)}, bf16[64,4096]{1,0:T(8,128)(2,1)S(1)}, u32[]{:S(2)}, u32[]{:S(2)}) collective-permute-start(bf16[64,4096]{1,0:T(8,128)(2,1)S(1)} %get-tuple-element.48), channel_id=1, source_target_pairs={{0,1},{1,0},{2,3},{3,2},{4,5},{5,4},{6,7},{7,6},{8,9},{9,8},{10,11... | collective-permute-start | bytes 1572872 | tf_op jit(solution)/shard_map/swap_out_0/ppermute | solution.py:326
  80.7 7.8 %collective-permute-start.23 = (bf16[32,4096]{1,0:T(8,128)(2,1)S(1)}, bf16[32,4096]{1,0:T(8,128)(2,1)S(1)}, u32[]{:S(2)}, u32[]{:S(2)}) collective-permute-start(bf16[32,4096]{1,0:T(8,128)(2,1)S(1)} %get-tuple-element.74), channel_id=1, source_target_pairs={{0,4},{1,3},{4,8},{5,1},{8,12},{9,5},{12,14},{13,9},{14,10},{15,13... | collective-permute-start | bytes 786440 | tf_op jit(solution)/shard_map/return_short_1/ppermute | solution.py:326
  82.4 8.5 %collective-permute-start.24 = (bf16[32,4096]{1,0:T(8,128)(2,1)S(1)}, bf16[32,4096]{1,0:T(8,128)(2,1)S(1)}, u32[]{:S(2)}, u32[]{:S(2)}) collective-permute-start(bf16[32,4096]{1,0:T(8,128)(2,1)S(1)} %get-tuple-element.75), channel_id=1, source_target_pairs={{0,5},{1,2},{4,9},{5,0},{8,13},{9,4},{12,15},{13,8},{14,11},{15,12... | collective-permute-start | bytes 786440 | tf_op jit(solution)/shard_map/return_short_1/ppermute | solution.py:326
  85.7 11.2 %collective-permute-start.25 = (bf16[64,4096]{1,0:T(8,128)(2,1)S(1)}, bf16[64,4096]{1,0:T(8,128)(2,1)S(1)}, u32[]{:S(2)}, u32[]{:S(2)}) collective-permute-start(bf16[64,4096]{1,0:T(8,128)(2,1)S(1)} %get-tuple-element.76), channel_id=1, source_target_pairs={{0,1},{1,0},{2,3},{3,2},{4,5},{5,4},{6,7},{7,6},{8,9},{9,8},{10,11... | collective-permute-start | bytes 1572872 | tf_op jit(solution)/shard_map/swap_out_1/ppermute | solution.py:326
  85.9 11.0 %collective-permute-start.29 = (bf16[64,4096]{1,0:T(8,128)(2,1)S(1)}, bf16[64,4096]{1,0:T(8,128)(2,1)S(1)}, u32[]{:S(2)}, u32[]{:S(2)}) collective-permute-start(bf16[64,4096]{1,0:T(8,128)(2,1)S(1)} %step_sum.9), channel_id=1, source_target_pairs={{0,4},{1,3},{4,8},{5,1},{8,12},{9,5},{12,14},{13,9},{14,10},{15,13... | collective-permute-start | bytes 1572872 | tf_op jit(solution)/shard_map/return_long_2/ppermute | solution.py:326
  97.1 5.9 %collective-permute-start.30 = (bf16[32,4096]{1,0:T(8,128)(2,1)S(1)}, bf16[32,4096]{1,0:T(8,128)(2,1)S(1)}, u32[]{:S(2)}, u32[]{:S(2)}) collective-permute-start(bf16[32,4096]{1,0:T(8,128)(2,1)S(1)} %get-tuple-element.81), channel_id=1, source_target_pairs={{0,5},{1,2},{4,9},{5,0},{8,13},{9,4},{12,15},{13,8},{14,11},{15,12... | collective-permute-start | bytes 786440 | tf_op jit(solution)/shard_map/return_long_1/ppermute | solution.py:326
  98.2 8.2 %collective-permute-start.31 = (bf16[32,4096]{1,0:T(8,128)(2,1)S(1)}, bf16[32,4096]{1,0:T(8,128)(2,1)S(1)}, u32[]{:S(2)}, u32[]{:S(2)}) collective-permute-start(bf16[32,4096]{1,0:T(8,128)(2,1)S(1)} %get-tuple-element.82), channel_id=1, source_target_pairs={{0,4},{1,3},{4,8},{5,1},{8,12},{9,5},{12,14},{13,9},{14,10},{15,13... | collective-permute-start | bytes 786440 | tf_op jit(solution)/shard_map/return_long_1/ppermute | solution.py:326
  (2 other events, 24.3 us)

commit v17 on v16

--- a/solution.py
+++ b/solution.py
@@ -373,7 +373,11 @@
     run([(reach - 1, "short")], last, 2)
     second = run([(reach - 1, "long")], last, 2)
     short, totals = step(reach - 1, "short", ())
-    run([(reach, "long")], [*totals, *second])
+    far = after(blocks[reach, "long"], *totals, *second)
+    far_other = send(far, swap, f"swap_in_{reach}")
+    far_given = expert_part([far], [rows], 2, *weights)
+    given[reach, "long"] = send(far_given[0], swap, f"swap_out_{reach}")
+    kept[reach, "long"] = expert_part([after(far_other, *far_given)], [rows], 2, *weights)[0]
     long, totals = step(reach, "long", ())
     for distance in range(reach - 1, 0, -1):
         if 1 < distance < reach - 1:

time: 108 us -> 107 us (level)
  waiting for transfers between devices: 43.7 us -> 38.6 us
  Pallas kernels: 32.4 us -> 36.3 us
    ppermute x32, waiting for transfers between devices: 43.7 us -> 38.6 us  [send(): return lax.ppermute(x, 'expert', perm)]
    pallas_call x7 -> x8, Pallas kernels: 22.4 us -> 26.3 us  [expert_part(): pl.pallas_call(functools.partial(expert_kernel, len(blocks)), in_specs=[V...]
  transfers between devices with their start and end apart: 32 -> 32, of which waited for: 16 -> 15; matrix products, arithmetic and copies ran while one was open for 0% -> 0% of each run, Pallas kernels for 25% -> 32%
where the time goes in v17:
time: 107 us
  waiting for transfers between devices  38.6 us (36%)
  Pallas kernels  36.3 us (34%)
  starting transfers between devices  31.2 us (29%)
    ppermute x32, waiting for transfers between devices, send(): return lax.ppermute(x, 'expert', perm)  38.6 us
    ppermute x32, starting transfers between devices, send(): return lax.ppermute(x, 'expert', perm)  31.2 us
    pallas_call x8, Pallas kernels, expert_part(): pl.pallas_call(functools.partial(expert_kernel, len(blocks)), in_specs=[V...  26.3 us
    pallas_call x1, Pallas kernels, keep(): pl.pallas_call(keep_kernel, in_specs=[ANYWHERE] * 2, out_specs=[VMEM] * 2...  6.38 us
  transfers between devices with their start and end apart: 32, of which 15 were waited for; matrix products, arithmetic and copies ran while one was open for 0% of the time, Pallas kernels for 32%

profile of v17, /device:TPU:0, one launch (start us, length us, event | category | flops | bytes accessed | tf_op | source)
XLA Modules:
  0.0 106.5 jit_solution(6642946518915230826)
XLA Ops:
  1.8 2.6 %collective-permute-start.2 = (bf16[64,4224]{1,0:T(8,128)(2,1)S(1)}, bf16[64,4224]{1,0:T(8,128)(2,1)S(1)}, u32[]{:S(2)}, u32[]{:S(2)}) collective-permute-start(bf16[64,4224]{1,0:T(8,128)(2,1)S(1)} %get-tuple-element.43.refs_0_), channel_id=1, source_target_pairs={{0,4},{1,3},{4,8},{5,1},{8,12},{9,5},{12,14},{13,9},{14,10},{15,13... | collective-permute-start | bytes 1622024 | tf_op jit(solution)/shard_map/gather_long_1/ppermute | solution.py:326
  5.7 6.4 %keep.1 = (bf16[4096,1536]{1,0:T(8,128)(2,1)S(1)}, bf16[768,4096]{1,0:T(8,128)(2,1)S(1)}) custom-call(bf16[4096,1536]{1,0:T(8,128)(2,1)} %bitcast.5, bf16[768,4096]{1,0:T(8,128)(2,1)} %bitcast.6), custom_call_target="tpu_custom_call" | custom-call | bytes 18874368 | tf_op jit(solution)/shard_map/keep/pallas_call | solution.py:88
  12.2 2.9 %expert.8 = (bf16[64,4096]{1,0:T(8,128)(2,1)S(1)}, bf16[64,4096]{1,0:T(8,128)(2,1)S(1)}) custom-call(bf16[64,4224]{1,0:T(8,128)(2,1)S(1)} %get-tuple-element.43.refs_0_, bf16[64,4224]{1,0:T(8,128)(2,1)S(1)} %collective-permute-done.refs_1_, f32[1,128]{1,0:T(1,128)S(1)} %compare_select_fusion.1.refs_2_.refs_4_.refs_1_, f32[1,1536]{1,0:T(1,128)S(1)} %copy-done.1, ...), custom_call_target="tpu_custom_call" | custom-call | flops 4831838208 | tf_op jit(solution)/shard_map/expert/pallas_call | solution.py:146
  16.1 1.4 %collective-permute-done.3.cross = bf16[64,4224]{1,0:T(8,128)(2,1)S(1)} collective-permute-done((bf16[64,4224]{1,0:T(8,128)(2,1)S(1)}, bf16[64,4224]{1,0:T(8,128)(2,1)S(1)}, u32[]{:S(2)}, u32[]{:S(2)}) %collective-permute-start.3) | collective-permute-done | bytes 540704 | tf_op jit(solution)/shard_map/gather_long_1/ppermute | solution.py:326
  18.2 2.1 %collective-permute-start.7 = (bf16[64,4224]{1,0:T(8,128)(2,1)S(1)}, bf16[64,4224]{1,0:T(8,128)(2,1)S(1)}, u32[]{:S(2)}, u32[]{:S(2)}) collective-permute-start(bf16[64,4224]{1,0:T(8,128)(2,1)S(1)} %get-tuple-element.53.refs_3_), channel_id=1, source_target_pairs={{0,4},{1,3},{4,8},{5,1},{8,12},{9,5},{12,14},{13,9},{14,10},{15,13... | collective-permute-start | bytes 1622024 | tf_op jit(solution)/shard_map/gather_short_2/ppermute | solution.py:326
  20.3 1.6 %collective-permute-start.14 = (bf16[64,4224]{1,0:T(8,128)(2,1)S(1)}, bf16[64,4224]{1,0:T(8,128)(2,1)S(1)}, u32[]{:S(2)}, u32[]{:S(2)}) collective-permute-start(bf16[64,4224]{1,0:T(8,128)(2,1)S(1)} %get-tuple-element.51.refs_2_), channel_id=1, source_target_pairs={{0,4},{1,3},{4,8},{5,1},{8,12},{9,5},{12,14},{13,9},{14,10},{15,13... | collective-permute-start | bytes 1622024 | tf_op jit(solution)/shard_map/gather_long_2/ppermute | solution.py:326
  21.8 5.2 %expert.9 = (bf16[64,4096]{1,0:T(8,128)(2,1)S(1)}, bf16[64,4096]{1,0:T(8,128)(2,1)S(1)}, bf16[64,4096]{1,0:T(8,128)(2,1)S(1)}, bf16[64,4096]{1,0:T(8,128)(2,1)S(1)}) custom-call(bf16[64,4224]{1,0:T(8,128)(2,1)S(1)} %collective-permute-done.4.refs_0_, bf16[64,4224]{1,0:T(8,128)(2,1)S(1)} %collective-permute-done.5.refs_1_, ...), custom_call_target="tpu_custom_call" | custom-call | flops 9663676416 | tf_op jit(solution)/shard_map/expert/pallas_call | solution.py:146
  27.5 2.1 %collective-permute-start.10 = (bf16[64,4224]{1,0:T(8,128)(2,1)S(1)}, bf16[64,4224]{1,0:T(8,128)(2,1)S(1)}, u32[]{:S(2)}, u32[]{:S(2)}) collective-permute-start(bf16[64,4224]{1,0:T(8,128)(2,1)S(1)} %collective-permute-done.7.refs_1_), channel_id=1, source_target_pairs={{0,4},{1,3},{4,8},{5,1},{8,12},{9,5},{12,14},{13,9},{14,10},{15,13... | collective-permute-start | bytes 1622024 | tf_op jit(solution)/shard_map/gather_short_3/ppermute | solution.py:326
  29.6 3.7 %collective-permute-done.14.refs_1_ = bf16[64,4224]{1,0:T(8,128)(2,1)S(1)} collective-permute-done((bf16[64,4224]{1,0:T(8,128)(2,1)S(1)}, bf16[64,4224]{1,0:T(8,128)(2,1)S(1)}, u32[]{:S(2)}, u32[]{:S(2)}) %collective-permute-start.14) | collective-permute-done | bytes 540704 | tf_op jit(solution)/shard_map/gather_long_2/ppermute | solution.py:326
  33.3 2.1 %collective-permute-start.15 = (bf16[64,4224]{1,0:T(8,128)(2,1)S(1)}, bf16[64,4224]{1,0:T(8,128)(2,1)S(1)}, u32[]{:S(2)}, u32[]{:S(2)}) collective-permute-start(bf16[64,4224]{1,0:T(8,128)(2,1)S(1)} %collective-permute-done.14.refs_1_), channel_id=1, source_target_pairs={{0,4},{1,3},{4,8},{5,1},{8,12},{9,5},{12,14},{13,9},{14,10},{15,13... | collective-permute-start | bytes 1622024 | tf_op jit(solution)/shard_map/gather_long_3/ppermute | solution.py:326
  35.4 2.9 %expert.10 = (bf16[64,4096]{1,0:T(8,128)(2,1)S(1)}, bf16[64,4096]{1,0:T(8,128)(2,1)S(1)}) custom-call(bf16[64,4224]{1,0:T(8,128)(2,1)S(1)} %collective-permute-done.8.refs_0_, bf16[64,4224]{1,0:T(8,128)(2,1)S(1)} %collective-permute-done.7.refs_1_, f32[1,128]{1,0:T(1,128)S(1)} %compare_select_fusion.1.refs_2_.refs_4_.refs_1_, f32[1,1536]{1,0:T(1,128)S(1)} %copy-done.1, ...), custom_call_target="tpu_custom_call" | custom-call | flops 4831838208 | tf_op jit(solution)/shard_map/expert/pallas_call | solution.py:146
  39.1 5.8 %collective-permute-done.15.refs_1_ = bf16[64,4224]{1,0:T(8,128)(2,1)S(1)} collective-permute-done((bf16[64,4224]{1,0:T(8,128)(2,1)S(1)}, bf16[64,4224]{1,0:T(8,128)(2,1)S(1)}, u32[]{:S(2)}, u32[]{:S(2)}) %collective-permute-start.15) | collective-permute-done | bytes 540704 | tf_op jit(solution)/shard_map/gather_long_3/ppermute | solution.py:326
  44.9 2.1 %collective-permute-start.16 = (bf16[64,4224]{1,0:T(8,128)(2,1)S(1)}, bf16[64,4224]{1,0:T(8,128)(2,1)S(1)}, u32[]{:S(2)}, u32[]{:S(2)}) collective-permute-start(bf16[64,4224]{1,0:T(8,128)(2,1)S(1)} %collective-permute-done.15.refs_1_), channel_id=1, source_target_pairs={{0,4},{1,3},{4,8},{5,1},{8,12},{9,5},{12,14},{13,9},{14,10},{15,13... | collective-permute-start | bytes 1622024 | tf_op jit(solution)/shard_map/gather_long_4/ppermute | solution.py:326
  47.0 2.9 %expert.11 = (bf16[64,4096]{1,0:T(8,128)(2,1)S(1)}, bf16[64,4096]{1,0:T(8,128)(2,1)S(1)}) custom-call(bf16[64,4224]{1,0:T(8,128)(2,1)S(1)} %collective-permute-done.11.refs_0_, bf16[64,4224]{1,0:T(8,128)(2,1)S(1)} %collective-permute-done.10.refs_1_, f32[1,128]{1,0:T(1,128)S(1)} %compare_select_fusion.1.refs_2_.refs_4_.refs_1_, f32[1,1536]{1,0:T(1,128)S(1)} %copy-done.1, ...), custom_call_target="tpu_custom_call" | custom-call | flops 4831838208 | tf_op jit(solution)/shard_map/expert/pallas_call | solution.py:146
  50.1 2.9 %expert.12 = (bf16[64,4096]{1,0:T(8,128)(2,1)S(1)}, bf16[64,4096]{1,0:T(8,128)(2,1)S(1)}) custom-call(bf16[64,4224]{1,0:T(8,128)(2,1)S(1)} %collective-permute-done.17.refs_0_, bf16[64,4224]{1,0:T(8,128)(2,1)S(1)} %collective-permute-done.15.refs_1_, f32[1,128]{1,0:T(1,128)S(1)} %compare_select_fusion.1.refs_2_.refs_4_.refs_1_, f32[1,1536]{1,0:T(1,128)S(1)} %copy-done.1, ...), custom_call_target="tpu_custom_call" | custom-call | flops 4831838208 | tf_op jit(solution)/shard_map/expert/pallas_call | solution.py:146
  54.3 3.4 %expert.13 = bf16[64,4096]{1,0:T(8,128)(2,1)S(1)} custom-call(bf16[64,4224]{1,0:T(8,128)(2,1)S(1)} %collective-permute-done.16.refs_0_, f32[1,128]{1,0:T(1,128)S(1)} %compare_select_fusion.1.refs_2_.refs_4_.refs_1_, f32[1,1536]{1,0:T(1,128)S(1)} %copy-done.1, f32[1,4096]{1,0:T(1,128)S(1)} %copy-done, ...), custom_call_target="tpu_custom_call" | custom-call | flops 2415919104 | tf_op jit(solution)/shard_map/expert/pallas_call | solution.py:146
  58.8 2.1 %collective-permute-start.13 = (bf16[64,4096]{1,0:T(8,128)(2,1)S(1)}, bf16[64,4096]{1,0:T(8,128)(2,1)S(1)}, u32[]{:S(2)}, u32[]{:S(2)}) collective-permute-start(bf16[64,4096]{1,0:T(8,128)(2,1)S(1)} %step_sum.5), channel_id=1, source_target_pairs={{0,4},{1,3},{4,8},{5,1},{8,12},{9,5},{12,14},{13,9},{14,10},{15,13... | collective-permute-start | bytes 1572872 | tf_op jit(solution)/shard_map/return_short_3/ppermute | solution.py:326
  60.9 3.4 %expert.14.refs_0_ = bf16[64,4096]{1,0:T(8,128)(2,1)S(1)} custom-call(bf16[64,4224]{1,0:T(8,128)(2,1)S(1)} %collective-permute-done.18.refs_0_, f32[1,128]{1,0:T(1,128)S(1)} %compare_select_fusion.1.refs_2_.refs_4_.refs_1_, f32[1,1536]{1,0:T(1,128)S(1)} %copy-done.1, f32[1,4096]{1,0:T(1,128)S(1)} %copy-done, ...), custom_call_target="tpu_custom_call" | custom-call | flops 2415919104 | tf_op jit(solution)/shard_map/expert/pallas_call | solution.py:146
  64.4 1.6 %collective-permute-start.22 = (bf16[64,4096]{1,0:T(8,128)(2,1)S(1)}, bf16[64,4096]{1,0:T(8,128)(2,1)S(1)}, u32[]{:S(2)}, u32[]{:S(2)}) collective-permute-start(bf16[64,4096]{1,0:T(8,128)(2,1)S(1)} %step_sum.6), channel_id=1, source_target_pairs={{0,4},{1,3},{4,8},{5,1},{8,12},{9,5},{12,14},{13,9},{14,10},{15,13... | collective-permute-start | bytes 1572872 | tf_op jit(solution)/shard_map/return_long_4/ppermute | solution.py:326
  66.0 1.9 %collective-permute-done.13.refs_2_ = bf16[64,4096]{1,0:T(8,128)(2,1)S(1)} collective-permute-done((bf16[64,4096]{1,0:T(8,128)(2,1)S(1)}, bf16[64,4096]{1,0:T(8,128)(2,1)S(1)}, u32[]{:S(2)}, u32[]{:S(2)}) %collective-permute-start.13) | collective-permute-done | bytes 524320 | tf_op jit(solution)/shard_map/return_short_3/ppermute | solution.py:326
  68.2 2.1 %collective-permute-start.20 = (bf16[64,4096]{1,0:T(8,128)(2,1)S(1)}, bf16[64,4096]{1,0:T(8,128)(2,1)S(1)}, u32[]{:S(2)}, u32[]{:S(2)}) collective-permute-start(bf16[64,4096]{1,0:T(8,128)(2,1)S(1)} %step_sum.7), channel_id=1, source_target_pairs={{0,4},{1,3},{4,8},{5,1},{8,12},{9,5},{12,14},{13,9},{14,10},{15,13... | collective-permute-start | bytes 1572872 | tf_op jit(solution)/shard_map/return_short_2/ppermute | solution.py:326
  70.3 3.4 %collective-permute-done.22.refs_2_ = bf16[64,4096]{1,0:T(8,128)(2,1)S(1)} collective-permute-done((bf16[64,4096]{1,0:T(8,128)(2,1)S(1)}, bf16[64,4096]{1,0:T(8,128)(2,1)S(1)}, u32[]{:S(2)}, u32[]{:S(2)}) %collective-permute-start.22) | collective-permute-done | bytes 524320 | tf_op jit(solution)/shard_map/return_long_4/ppermute | solution.py:326
  73.9 2.3 %collective-permute-start.28 = (bf16[64,4096]{1,0:T(8,128)(2,1)S(1)}, bf16[64,4096]{1,0:T(8,128)(2,1)S(1)}, u32[]{:S(2)}, u32[]{:S(2)}) collective-permute-start(bf16[64,4096]{1,0:T(8,128)(2,1)S(1)} %step_sum.8), channel_id=1, source_target_pairs={{0,4},{1,3},{4,8},{5,1},{8,12},{9,5},{12,14},{13,9},{14,10},{15,13... | collective-permute-start | bytes 1572872 | tf_op jit(solution)/shard_map/return_long_3/ppermute | solution.py:326
  76.1 2.9 %expert.15 = (bf16[64,4096]{1,0:T(8,128)(2,1)S(1)}, bf16[64,4096]{1,0:T(8,128)(2,1)S(1)}) custom-call(bf16[64,4224]{1,0:T(8,128)(2,1)S(1)} %collective-permute-done.26.refs_0_, bf16[64,4224]{1,0:T(8,128)(2,1)S(1)} %collective-permute-done.14.refs_1_, f32[1,128]{1,0:T(1,128)S(1)} %compare_select_fusion.1.refs_2_.refs_4_.refs_1_, f32[1,1536]{1,0:T(1,128)S(1)} %copy-done.1, ...), custom_call_target="tpu_custom_call" | custom-call | flops 4831838208 | tf_op jit(solution)/shard_map/expert/pallas_call | solution.py:146
  79.8 1.7 %collective-permute-start.23 = (bf16[32,4096]{1,0:T(8,128)(2,1)S(1)}, bf16[32,4096]{1,0:T(8,128)(2,1)S(1)}, u32[]{:S(2)}, u32[]{:S(2)}) collective-permute-start(bf16[32,4096]{1,0:T(8,128)(2,1)S(1)} %get-tuple-element.72), channel_id=1, source_target_pairs={{0,4},{1,3},{4,8},{5,1},{8,12},{9,5},{12,14},{13,9},{14,10},{15,13... | collective-permute-start | bytes 786440 | tf_op jit(solution)/shard_map/return_short_1/ppermute | solution.py:326
  81.5 3.4 %collective-permute-done.28.refs_2_ = bf16[64,4096]{1,0:T(8,128)(2,1)S(1)} collective-permute-done((bf16[64,4096]{1,0:T(8,128)(2,1)S(1)}, bf16[64,4096]{1,0:T(8,128)(2,1)S(1)}, u32[]{:S(2)}, u32[]{:S(2)}) %collective-permute-start.28) | collective-permute-done | bytes 524320 | tf_op jit(solution)/shard_map/return_long_3/ppermute | solution.py:326
  85.1 2.1 %collective-permute-start.29 = (bf16[64,4096]{1,0:T(8,128)(2,1)S(1)}, bf16[64,4096]{1,0:T(8,128)(2,1)S(1)}, u32[]{:S(2)}, u32[]{:S(2)}) collective-permute-start(bf16[64,4096]{1,0:T(8,128)(2,1)S(1)} %step_sum.9), channel_id=1, source_target_pairs={{0,4},{1,3},{4,8},{5,1},{8,12},{9,5},{12,14},{13,9},{14,10},{15,13... | collective-permute-start | bytes 1572872 | tf_op jit(solution)/shard_map/return_long_2/ppermute | solution.py:326
  87.7 2.3 %collective-permute-done.24.short_cross = bf16[32,4096]{1,0:T(8,128)(2,1)S(1)} collective-permute-done((bf16[32,4096]{1,0:T(8,128)(2,1)S(1)}, bf16[32,4096]{1,0:T(8,128)(2,1)S(1)}, u32[]{:S(2)}, u32[]{:S(2)}) %collective-permute-start.24) | collective-permute-done | bytes 262176 | tf_op jit(solution)/shard_map/return_short_1/ppermute | solution.py:326
  90.2 5.9 %collective-permute-done.29.refs_2_ = bf16[64,4096]{1,0:T(8,128)(2,1)S(1)} collective-permute-done((bf16[64,4096]{1,0:T(8,128)(2,1)S(1)}, bf16[64,4096]{1,0:T(8,128)(2,1)S(1)}, u32[]{:S(2)}, u32[]{:S(2)}) %collective-permute-start.29) | collective-permute-done | bytes 524320 | tf_op jit(solution)/shard_map/return_long_2/ppermute | solution.py:326
  97.2 1.6 %collective-permute-start.31 = (bf16[32,4096]{1,0:T(8,128)(2,1)S(1)}, bf16[32,4096]{1,0:T(8,128)(2,1)S(1)}, u32[]{:S(2)}, u32[]{:S(2)}) collective-permute-start(bf16[32,4096]{1,0:T(8,128)(2,1)S(1)} %get-tuple-element.80), channel_id=1, source_target_pairs={{0,4},{1,3},{4,8},{5,1},{8,12},{9,5},{12,14},{13,9},{14,10},{15,13... | collective-permute-start | bytes 786440 | tf_op jit(solution)/shard_map/return_long_1/ppermute | solution.py:326
  98.8 3.4 %collective-permute-done.30.long_cross = bf16[32,4096]{1,0:T(8,128)(2,1)S(1)} collective-permute-done((bf16[32,4096]{1,0:T(8,128)(2,1)S(1)}, bf16[32,4096]{1,0:T(8,128)(2,1)S(1)}, u32[]{:S(2)}, u32[]{:S(2)}) %collective-permute-start.30) | collective-permute-done | bytes 262176 | tf_op jit(solution)/shard_map/return_long_1/ppermute | solution.py:326
  102.2 3.3 %collective-permute-done.31.long_same = bf16[32,4096]{1,0:T(8,128)(2,1)S(1)} collective-permute-done((bf16[32,4096]{1,0:T(8,128)(2,1)S(1)}, bf16[32,4096]{1,0:T(8,128)(2,1)S(1)}, u32[]{:S(2)}, u32[]{:S(2)}) %collective-permute-start.31) | collective-permute-done | bytes 262176 | tf_op jit(solution)/shard_map/return_long_1/ppermute | solution.py:326
  (57 shorter events, 12.9 us)
Async XLA Ops:
  1.3 10.9 %collective-permute-start = (bf16[64,4224]{1,0:T(8,128)(2,1)S(1)}, bf16[64,4224]{1,0:T(8,128)(2,1)S(1)}, u32[]{:S(2)}, u32[]{:S(2)}) collective-permute-start(bf16[64,4224]{1,0:T(8,128)(2,1)S(1)} %get-tuple-element.43.refs_0_), channel_id=1, source_target_pairs={{0,1},{1,0},{2,3},{3,2},{4,5},{5,4},{6,7},{7,6},{8,9},{9,8},{10,11... | collective-permute-start | bytes 1622024 | tf_op jit(solution)/shard_map/swap_in_0/ppermute | solution.py:326
  1.8 14.3 %collective-permute-start.2 = (bf16[64,4224]{1,0:T(8,128)(2,1)S(1)}, bf16[64,4224]{1,0:T(8,128)(2,1)S(1)}, u32[]{:S(2)}, u32[]{:S(2)}) collective-permute-start(bf16[64,4224]{1,0:T(8,128)(2,1)S(1)} %get-tuple-element.43.refs_0_), channel_id=1, source_target_pairs={{0,4},{1,3},{4,8},{5,1},{8,12},{9,5},{12,14},{13,9},{14,10},{15,13... | collective-permute-start | bytes 1622024 | tf_op jit(solution)/shard_map/gather_long_1/ppermute | solution.py:326
  4.5 13.1 %collective-permute-start.3 = (bf16[64,4224]{1,0:T(8,128)(2,1)S(1)}, bf16[64,4224]{1,0:T(8,128)(2,1)S(1)}, u32[]{:S(2)}, u32[]{:S(2)}) collective-permute-start(bf16[64,4224]{1,0:T(8,128)(2,1)S(1)} %get-tuple-element.49), channel_id=1, source_target_pairs={{0,3},{1,4},{4,1},{5,8},{8,5},{9,12},{12,9},{13,14},{14,13},{15,10... | collective-permute-start | bytes 1622024 | tf_op jit(solution)/shard_map/gather_long_1/ppermute | solution.py:326
  17.6 4.2 %collective-permute-start.4 = (bf16[64,4224]{1,0:T(8,128)(2,1)S(1)}, bf16[64,4224]{1,0:T(8,128)(2,1)S(1)}, u32[]{:S(2)}, u32[]{:S(2)}) collective-permute-start(bf16[64,4224]{1,0:T(8,128)(2,1)S(1)} %get-tuple-element.51.refs_2_), channel_id=1, source_target_pairs={{0,1},{1,0},{2,3},{3,2},{4,5},{5,4},{6,7},{7,6},{8,9},{9,8},{10,11... | collective-permute-start | bytes 1622024 | tf_op jit(solution)/shard_map/swap_in_1/ppermute | solution.py:326
  17.7 4.2 %collective-permute-start.5 = (bf16[64,4224]{1,0:T(8,128)(2,1)S(1)}, bf16[64,4224]{1,0:T(8,128)(2,1)S(1)}, u32[]{:S(2)}, u32[]{:S(2)}) collective-permute-start(bf16[64,4224]{1,0:T(8,128)(2,1)S(1)} %get-tuple-element.53.refs_3_), channel_id=1, source_target_pairs={{0,1},{1,0},{2,3},{3,2},{4,5},{5,4},{6,7},{7,6},{8,9},{9,8},{10,11... | collective-permute-start | bytes 1622024 | tf_op jit(solution)/shard_map/swap_in_1/ppermute | solution.py:326
  18.2 9.4 %collective-permute-start.7 = (bf16[64,4224]{1,0:T(8,128)(2,1)S(1)}, bf16[64,4224]{1,0:T(8,128)(2,1)S(1)}, u32[]{:S(2)}, u32[]{:S(2)}) collective-permute-start(bf16[64,4224]{1,0:T(8,128)(2,1)S(1)} %get-tuple-element.53.refs_3_), channel_id=1, source_target_pairs={{0,4},{1,3},{4,8},{5,1},{8,12},{9,5},{12,14},{13,9},{14,10},{15,13... | collective-permute-start | bytes 1622024 | tf_op jit(solution)/shard_map/gather_short_2/ppermute | solution.py:326
  20.3 13.1 %collective-permute-start.14 = (bf16[64,4224]{1,0:T(8,128)(2,1)S(1)}, bf16[64,4224]{1,0:T(8,128)(2,1)S(1)}, u32[]{:S(2)}, u32[]{:S(2)}) collective-permute-start(bf16[64,4224]{1,0:T(8,128)(2,1)S(1)} %get-tuple-element.51.refs_2_), channel_id=1, source_target_pairs={{0,4},{1,3},{4,8},{5,1},{8,12},{9,5},{12,14},{13,9},{14,10},{15,13... | collective-permute-start | bytes 1622024 | tf_op jit(solution)/shard_map/gather_long_2/ppermute | solution.py:326
  27.5 7.9 %collective-permute-start.8 = (bf16[64,4224]{1,0:T(8,128)(2,1)S(1)}, bf16[64,4224]{1,0:T(8,128)(2,1)S(1)}, u32[]{:S(2)}, u32[]{:S(2)}) collective-permute-start(bf16[64,4224]{1,0:T(8,128)(2,1)S(1)} %collective-permute-done.7.refs_1_), channel_id=1, source_target_pairs={{0,1},{1,0},{2,3},{3,2},{4,5},{5,4},{6,7},{7,6},{8,9},{9,8},{10,11... | collective-permute-start | bytes 1622024 | tf_op jit(solution)/shard_map/swap_in_2/ppermute | solution.py:326
  27.5 11.6 %collective-permute-start.10 = (bf16[64,4224]{1,0:T(8,128)(2,1)S(1)}, bf16[64,4224]{1,0:T(8,128)(2,1)S(1)}, u32[]{:S(2)}, u32[]{:S(2)}) collective-permute-start(bf16[64,4224]{1,0:T(8,128)(2,1)S(1)} %collective-permute-done.7.refs_1_), channel_id=1, source_target_pairs={{0,4},{1,3},{4,8},{5,1},{8,12},{9,5},{12,14},{13,9},{14,10},{15,13... | collective-permute-start | bytes 1622024 | tf_op jit(solution)/shard_map/gather_short_3/ppermute | solution.py:326
  33.3 11.6 %collective-permute-start.15 = (bf16[64,4224]{1,0:T(8,128)(2,1)S(1)}, bf16[64,4224]{1,0:T(8,128)(2,1)S(1)}, u32[]{:S(2)}, u32[]{:S(2)}) collective-permute-start(bf16[64,4224]{1,0:T(8,128)(2,1)S(1)} %collective-permute-done.14.refs_1_), channel_id=1, source_target_pairs={{0,4},{1,3},{4,8},{5,1},{8,12},{9,5},{12,14},{13,9},{14,10},{15,13... | collective-permute-start | bytes 1622024 | tf_op jit(solution)/shard_map/gather_long_3/ppermute | solution.py:326
  39.1 7.9 %collective-permute-start.11 = (bf16[64,4224]{1,0:T(8,128)(2,1)S(1)}, bf16[64,4224]{1,0:T(8,128)(2,1)S(1)}, u32[]{:S(2)}, u32[]{:S(2)}) collective-permute-start(bf16[64,4224]{1,0:T(8,128)(2,1)S(1)} %collective-permute-done.10.refs_1_), channel_id=1, source_target_pairs={{0,1},{1,0},{2,3},{3,2},{4,5},{5,4},{6,7},{7,6},{8,9},{9,8},{10,11... | collective-permute-start | bytes 1622024 | tf_op jit(solution)/shard_map/swap_in_3/ppermute | solution.py:326
  44.9 5.2 %collective-permute-start.17 = (bf16[64,4224]{1,0:T(8,128)(2,1)S(1)}, bf16[64,4224]{1,0:T(8,128)(2,1)S(1)}, u32[]{:S(2)}, u32[]{:S(2)}) collective-permute-start(bf16[64,4224]{1,0:T(8,128)(2,1)S(1)} %collective-permute-done.15.refs_1_), channel_id=1, source_target_pairs={{0,1},{1,0},{2,3},{3,2},{4,5},{5,4},{6,7},{7,6},{8,9},{9,8},{10,11... | collective-permute-start | bytes 1622024 | tf_op jit(solution)/shard_map/swap_in_3/ppermute | solution.py:326
  44.9 9.4 %collective-permute-start.16 = (bf16[64,4224]{1,0:T(8,128)(2,1)S(1)}, bf16[64,4224]{1,0:T(8,128)(2,1)S(1)}, u32[]{:S(2)}, u32[]{:S(2)}) collective-permute-start(bf16[64,4224]{1,0:T(8,128)(2,1)S(1)} %collective-permute-done.15.refs_1_), channel_id=1, source_target_pairs={{0,4},{1,3},{4,8},{5,1},{8,12},{9,5},{12,14},{13,9},{14,10},{15,13... | collective-permute-start | bytes 1622024 | tf_op jit(solution)/shard_map/gather_long_4/ppermute | solution.py:326
  49.9 3.1 %collective-permute-start.12 = (bf16[64,4096]{1,0:T(8,128)(2,1)S(1)}, bf16[64,4096]{1,0:T(8,128)(2,1)S(1)}, u32[]{:S(2)}, u32[]{:S(2)}) collective-permute-start(bf16[64,4096]{1,0:T(8,128)(2,1)S(1)} %get-tuple-element.62), channel_id=1, source_target_pairs={{0,1},{1,0},{2,3},{3,2},{4,5},{5,4},{6,7},{7,6},{8,9},{9,8},{10,11... | collective-permute-start | bytes 1572872 | tf_op jit(solution)/shard_map/swap_out_3/ppermute | solution.py:326
  54.3 6.6 %collective-permute-start.18 = (bf16[64,4224]{1,0:T(8,128)(2,1)S(1)}, bf16[64,4224]{1,0:T(8,128)(2,1)S(1)}, u32[]{:S(2)}, u32[]{:S(2)}) collective-permute-start(bf16[64,4224]{1,0:T(8,128)(2,1)S(1)} %collective-permute-done.16.refs_0_), channel_id=1, source_target_pairs={{0,1},{1,0},{2,3},{3,2},{4,5},{5,4},{6,7},{7,6},{8,9},{9,8},{10,11... | collective-permute-start | bytes 1622024 | tf_op jit(solution)/shard_map/swap_in_4/ppermute | solution.py:326
  57.7 6.6 %collective-permute-start.19 = (bf16[64,4096]{1,0:T(8,128)(2,1)S(1)}, bf16[64,4096]{1,0:T(8,128)(2,1)S(1)}, u32[]{:S(2)}, u32[]{:S(2)}) collective-permute-start(bf16[64,4096]{1,0:T(8,128)(2,1)S(1)} %expert.13), channel_id=1, source_target_pairs={{0,1},{1,0},{2,3},{3,2},{4,5},{5,4},{6,7},{7,6},{8,9},{9,8},{10,11... | collective-permute-start | bytes 1572872 | tf_op jit(solution)/shard_map/swap_out_4/ppermute | solution.py:326
  58.3 17.9 %collective-permute-start.26 = (bf16[64,4224]{1,0:T(8,128)(2,1)S(1)}, bf16[64,4224]{1,0:T(8,128)(2,1)S(1)}, u32[]{:S(2)}, u32[]{:S(2)}) collective-permute-start(bf16[64,4224]{1,0:T(8,128)(2,1)S(1)} %collective-permute-done.14.refs_1_), channel_id=1, source_target_pairs={{0,1},{1,0},{2,3},{3,2},{4,5},{5,4},{6,7},{7,6},{8,9},{9,8},{10,11... | collective-permute-start | bytes 1622024 | tf_op jit(solution)/shard_map/swap_in_2/ppermute | solution.py:326
  58.4 9.6 %collective-permute-start.9 = (bf16[64,4096]{1,0:T(8,128)(2,1)S(1)}, bf16[64,4096]{1,0:T(8,128)(2,1)S(1)}, u32[]{:S(2)}, u32[]{:S(2)}) collective-permute-start(bf16[64,4096]{1,0:T(8,128)(2,1)S(1)} %get-tuple-element.59), channel_id=1, source_target_pairs={{0,1},{1,0},{2,3},{3,2},{4,5},{5,4},{6,7},{7,6},{8,9},{9,8},{10,11... | collective-permute-start | bytes 1572872 | tf_op jit(solution)/shard_map/swap_out_2/ppermute | solution.py:326
  58.8 9.2 %collective-permute-start.13 = (bf16[64,4096]{1,0:T(8,128)(2,1)S(1)}, bf16[64,4096]{1,0:T(8,128)(2,1)S(1)}, u32[]{:S(2)}, u32[]{:S(2)}) collective-permute-start(bf16[64,4096]{1,0:T(8,128)(2,1)S(1)} %step_sum.5), channel_id=1, source_target_pairs={{0,4},{1,3},{4,8},{5,1},{8,12},{9,5},{12,14},{13,9},{14,10},{15,13... | collective-permute-start | bytes 1572872 | tf_op jit(solution)/shard_map/return_short_3/ppermute | solution.py:326
  64.4 9.2 %collective-permute-start.22 = (bf16[64,4096]{1,0:T(8,128)(2,1)S(1)}, bf16[64,4096]{1,0:T(8,128)(2,1)S(1)}, u32[]{:S(2)}, u32[]{:S(2)}) collective-permute-start(bf16[64,4096]{1,0:T(8,128)(2,1)S(1)} %step_sum.6), channel_id=1, source_target_pairs={{0,4},{1,3},{4,8},{5,1},{8,12},{9,5},{12,14},{13,9},{14,10},{15,13... | collective-permute-start | bytes 1572872 | tf_op jit(solution)/shard_map/return_long_4/ppermute | solution.py:326
  66.0 7.6 %collective-permute-start.21 = (bf16[64,4096]{1,0:T(8,128)(2,1)S(1)}, bf16[64,4096]{1,0:T(8,128)(2,1)S(1)}, u32[]{:S(2)}, u32[]{:S(2)}) collective-permute-start(bf16[64,4096]{1,0:T(8,128)(2,1)S(1)} %get-tuple-element.69), channel_id=1, source_target_pairs={{0,1},{1,0},{2,3},{3,2},{4,5},{5,4},{6,7},{7,6},{8,9},{9,8},{10,11... | collective-permute-start | bytes 1572872 | tf_op jit(solution)/shard_map/swap_out_3/ppermute | solution.py:326
  68.0 11.6 %collective-permute-start.6 = (bf16[64,4096]{1,0:T(8,128)(2,1)S(1)}, bf16[64,4096]{1,0:T(8,128)(2,1)S(1)}, u32[]{:S(2)}, u32[]{:S(2)}) collective-permute-start(bf16[64,4096]{1,0:T(8,128)(2,1)S(1)} %get-tuple-element.55), channel_id=1, source_target_pairs={{0,1},{1,0},{2,3},{3,2},{4,5},{5,4},{6,7},{7,6},{8,9},{9,8},{10,11... | collective-permute-start | bytes 1572872 | tf_op jit(solution)/shard_map/swap_out_1/ppermute | solution.py:326
  68.2 11.4 %collective-permute-start.20 = (bf16[64,4096]{1,0:T(8,128)(2,1)S(1)}, bf16[64,4096]{1,0:T(8,128)(2,1)S(1)}, u32[]{:S(2)}, u32[]{:S(2)}) collective-permute-start(bf16[64,4096]{1,0:T(8,128)(2,1)S(1)} %step_sum.7), channel_id=1, source_target_pairs={{0,4},{1,3},{4,8},{5,1},{8,12},{9,5},{12,14},{13,9},{14,10},{15,13... | collective-permute-start | bytes 1572872 | tf_op jit(solution)/shard_map/return_short_2/ppermute | solution.py:326
  73.9 11.0 %collective-permute-start.28 = (bf16[64,4096]{1,0:T(8,128)(2,1)S(1)}, bf16[64,4096]{1,0:T(8,128)(2,1)S(1)}, u32[]{:S(2)}, u32[]{:S(2)}) collective-permute-start(bf16[64,4096]{1,0:T(8,128)(2,1)S(1)} %step_sum.8), channel_id=1, source_target_pairs={{0,4},{1,3},{4,8},{5,1},{8,12},{9,5},{12,14},{13,9},{14,10},{15,13... | collective-permute-start | bytes 1572872 | tf_op jit(solution)/shard_map/return_long_3/ppermute | solution.py:326
  79.0 5.9 %collective-permute-start.27 = (bf16[64,4096]{1,0:T(8,128)(2,1)S(1)}, bf16[64,4096]{1,0:T(8,128)(2,1)S(1)}, u32[]{:S(2)}, u32[]{:S(2)}) collective-permute-start(bf16[64,4096]{1,0:T(8,128)(2,1)S(1)} %get-tuple-element.76), channel_id=1, source_target_pairs={{0,1},{1,0},{2,3},{3,2},{4,5},{5,4},{6,7},{7,6},{8,9},{9,8},{10,11... | collective-permute-start | bytes 1572872 | tf_op jit(solution)/shard_map/swap_out_2/ppermute | solution.py:326
  79.1 8.1 %collective-permute-start.1 = (bf16[64,4096]{1,0:T(8,128)(2,1)S(1)}, bf16[64,4096]{1,0:T(8,128)(2,1)S(1)}, u32[]{:S(2)}, u32[]{:S(2)}) collective-permute-start(bf16[64,4096]{1,0:T(8,128)(2,1)S(1)} %get-tuple-element.47), channel_id=1, source_target_pairs={{0,1},{1,0},{2,3},{3,2},{4,5},{5,4},{6,7},{7,6},{8,9},{9,8},{10,11... | collective-permute-start | bytes 1572872 | tf_op jit(solution)/shard_map/swap_out_0/ppermute | solution.py:326
  79.8 7.9 %collective-permute-start.23 = (bf16[32,4096]{1,0:T(8,128)(2,1)S(1)}, bf16[32,4096]{1,0:T(8,128)(2,1)S(1)}, u32[]{:S(2)}, u32[]{:S(2)}) collective-permute-start(bf16[32,4096]{1,0:T(8,128)(2,1)S(1)} %get-tuple-element.72), channel_id=1, source_target_pairs={{0,4},{1,3},{4,8},{5,1},{8,12},{9,5},{12,14},{13,9},{14,10},{15,13... | collective-permute-start | bytes 786440 | tf_op jit(solution)/shard_map/return_short_1/ppermute | solution.py:326
  81.5 8.5 %collective-permute-start.24 = (bf16[32,4096]{1,0:T(8,128)(2,1)S(1)}, bf16[32,4096]{1,0:T(8,128)(2,1)S(1)}, u32[]{:S(2)}, u32[]{:S(2)}) collective-permute-start(bf16[32,4096]{1,0:T(8,128)(2,1)S(1)} %get-tuple-element.73), channel_id=1, source_target_pairs={{0,5},{1,2},{4,9},{5,0},{8,13},{9,4},{12,15},{13,8},{14,11},{15,12... | collective-permute-start | bytes 786440 | tf_op jit(solution)/shard_map/return_short_1/ppermute | solution.py:326
  84.9 11.2 %collective-permute-start.25 = (bf16[64,4096]{1,0:T(8,128)(2,1)S(1)}, bf16[64,4096]{1,0:T(8,128)(2,1)S(1)}, u32[]{:S(2)}, u32[]{:S(2)}) collective-permute-start(bf16[64,4096]{1,0:T(8,128)(2,1)S(1)} %get-tuple-element.74), channel_id=1, source_target_pairs={{0,1},{1,0},{2,3},{3,2},{4,5},{5,4},{6,7},{7,6},{8,9},{9,8},{10,11... | collective-permute-start | bytes 1572872 | tf_op jit(solution)/shard_map/swap_out_1/ppermute | solution.py:326
  85.1 11.0 %collective-permute-start.29 = (bf16[64,4096]{1,0:T(8,128)(2,1)S(1)}, bf16[64,4096]{1,0:T(8,128)(2,1)S(1)}, u32[]{:S(2)}, u32[]{:S(2)}) collective-permute-start(bf16[64,4096]{1,0:T(8,128)(2,1)S(1)} %step_sum.9), channel_id=1, source_target_pairs={{0,4},{1,3},{4,8},{5,1},{8,12},{9,5},{12,14},{13,9},{14,10},{15,13... | collective-permute-start | bytes 1572872 | tf_op jit(solution)/shard_map/return_long_2/ppermute | solution.py:326
  96.3 5.9 %collective-permute-start.30 = (bf16[32,4096]{1,0:T(8,128)(2,1)S(1)}, bf16[32,4096]{1,0:T(8,128)(2,1)S(1)}, u32[]{:S(2)}, u32[]{:S(2)}) collective-permute-start(bf16[32,4096]{1,0:T(8,128)(2,1)S(1)} %get-tuple-element.79), channel_id=1, source_target_pairs={{0,5},{1,2},{4,9},{5,0},{8,13},{9,4},{12,15},{13,8},{14,11},{15,12... | collective-permute-start | bytes 786440 | tf_op jit(solution)/shard_map/return_long_1/ppermute | solution.py:326
  97.2 8.3 %collective-permute-start.31 = (bf16[32,4096]{1,0:T(8,128)(2,1)S(1)}, bf16[32,4096]{1,0:T(8,128)(2,1)S(1)}, u32[]{:S(2)}, u32[]{:S(2)}) collective-permute-start(bf16[32,4096]{1,0:T(8,128)(2,1)S(1)} %get-tuple-element.80), channel_id=1, source_target_pairs={{0,4},{1,3},{4,8},{5,1},{8,12},{9,5},{12,14},{13,9},{14,10},{15,13... | collective-permute-start | bytes 786440 | tf_op jit(solution)/shard_map/return_long_1/ppermute | solution.py:326
  (2 other events, 24.3 us)

commit v18 on v17

--- a/solution.py
+++ b/solution.py
@@ -378,6 +378,7 @@
     far_given = expert_part([far], [rows], 2, *weights)
     given[reach, "long"] = send(far_given[0], swap, f"swap_out_{reach}")
     kept[reach, "long"] = expert_part([after(far_other, *far_given)], [rows], 2, *weights)[0]
+    given[reach, "long"] = after(given[reach, "long"], *short)
     long, totals = step(reach, "long", ())
     for distance in range(reach - 1, 0, -1):
         if 1 < distance < reach - 1:

time: 107 us -> 108 us (level)
  waiting for transfers between devices: 38.6 us -> 42.8 us
  starting transfers between devices: 31.2 us -> 28.1 us
    ppermute x32, waiting for transfers between devices: 38.6 us -> 42.8 us  [send(): return lax.ppermute(x, 'expert', perm)]
    ppermute x32, starting transfers between devices: 31.2 us -> 28.1 us  [send(): return lax.ppermute(x, 'expert', perm)]
where the time goes in v18:
time: 108 us
  waiting for transfers between devices  42.8 us (40%)
  Pallas kernels  36.3 us (34%)
  starting transfers between devices  28.1 us (26%)
    ppermute x32, waiting for transfers between devices, send(): return lax.ppermute(x, 'expert', perm)  42.8 us
    ppermute x32, starting transfers between devices, send(): return lax.ppermute(x, 'expert', perm)  28.1 us
    pallas_call x8, Pallas kernels, expert_part(): pl.pallas_call(functools.partial(expert_kernel, len(blocks)), in_specs=[V...  26.4 us
    pallas_call x1, Pallas kernels, keep(): pl.pallas_call(keep_kernel, in_specs=[ANYWHERE] * 2, out_specs=[VMEM] * 2...  6.38 us
  transfers between devices with their start and end apart: 32, of which 15 were waited for; matrix products, arithmetic and copies ran while one was open for 0% of the time, Pallas kernels for 32%

profile of v18, /device:TPU:0, one launch (start us, length us, event | category | flops | bytes accessed | tf_op | source)
XLA Modules:
  0.0 107.7 jit_solution(14416229200938312166)
XLA Ops:
  1.8 2.6 %collective-permute-start.2 = (bf16[64,4224]{1,0:T(8,128)(2,1)S(1)}, bf16[64,4224]{1,0:T(8,128)(2,1)S(1)}, u32[]{:S(2)}, u32[]{:S(2)}) collective-permute-start(bf16[64,4224]{1,0:T(8,128)(2,1)S(1)} %get-tuple-element.44.refs_0_), channel_id=1, source_target_pairs={{0,4},{1,3},{4,8},{5,1},{8,12},{9,5},{12,14},{13,9},{14,10},{15,13... | collective-permute-start | bytes 1622024 | tf_op jit(solution)/shard_map/gather_long_1/ppermute | solution.py:326
  5.7 6.4 %keep.1 = (bf16[4096,1536]{1,0:T(8,128)(2,1)S(1)}, bf16[768,4096]{1,0:T(8,128)(2,1)S(1)}) custom-call(bf16[4096,1536]{1,0:T(8,128)(2,1)} %bitcast.5, bf16[768,4096]{1,0:T(8,128)(2,1)} %bitcast.6), custom_call_target="tpu_custom_call" | custom-call | bytes 18874368 | tf_op jit(solution)/shard_map/keep/pallas_call | solution.py:88
  12.2 2.9 %expert.8 = (bf16[64,4096]{1,0:T(8,128)(2,1)S(1)}, bf16[64,4096]{1,0:T(8,128)(2,1)S(1)}) custom-call(bf16[64,4224]{1,0:T(8,128)(2,1)S(1)} %get-tuple-element.44.refs_0_, bf16[64,4224]{1,0:T(8,128)(2,1)S(1)} %collective-permute-done.refs_1_, f32[1,128]{1,0:T(1,128)S(1)} %compare_select_fusion.1.refs_2_.refs_4_.refs_1_, f32[1,1536]{1,0:T(1,128)S(1)} %copy-done.1, ...), custom_call_target="tpu_custom_call" | custom-call | flops 4831838208 | tf_op jit(solution)/shard_map/expert/pallas_call | solution.py:146
  16.1 1.4 %collective-permute-done.3.cross = bf16[64,4224]{1,0:T(8,128)(2,1)S(1)} collective-permute-done((bf16[64,4224]{1,0:T(8,128)(2,1)S(1)}, bf16[64,4224]{1,0:T(8,128)(2,1)S(1)}, u32[]{:S(2)}, u32[]{:S(2)}) %collective-permute-start.3) | collective-permute-done | bytes 540704 | tf_op jit(solution)/shard_map/gather_long_1/ppermute | solution.py:326
  18.2 2.1 %collective-permute-start.7 = (bf16[64,4224]{1,0:T(8,128)(2,1)S(1)}, bf16[64,4224]{1,0:T(8,128)(2,1)S(1)}, u32[]{:S(2)}, u32[]{:S(2)}) collective-permute-start(bf16[64,4224]{1,0:T(8,128)(2,1)S(1)} %get-tuple-element.54.refs_3_), channel_id=1, source_target_pairs={{0,4},{1,3},{4,8},{5,1},{8,12},{9,5},{12,14},{13,9},{14,10},{15,13... | collective-permute-start | bytes 1622024 | tf_op jit(solution)/shard_map/gather_short_2/ppermute | solution.py:326
  20.3 1.6 %collective-permute-start.14 = (bf16[64,4224]{1,0:T(8,128)(2,1)S(1)}, bf16[64,4224]{1,0:T(8,128)(2,1)S(1)}, u32[]{:S(2)}, u32[]{:S(2)}) collective-permute-start(bf16[64,4224]{1,0:T(8,128)(2,1)S(1)} %get-tuple-element.52.refs_2_), channel_id=1, source_target_pairs={{0,4},{1,3},{4,8},{5,1},{8,12},{9,5},{12,14},{13,9},{14,10},{15,13... | collective-permute-start | bytes 1622024 | tf_op jit(solution)/shard_map/gather_long_2/ppermute | solution.py:326
  21.8 5.2 %expert.9 = (bf16[64,4096]{1,0:T(8,128)(2,1)S(1)}, bf16[64,4096]{1,0:T(8,128)(2,1)S(1)}, bf16[64,4096]{1,0:T(8,128)(2,1)S(1)}, bf16[64,4096]{1,0:T(8,128)(2,1)S(1)}) custom-call(bf16[64,4224]{1,0:T(8,128)(2,1)S(1)} %collective-permute-done.4.refs_0_, bf16[64,4224]{1,0:T(8,128)(2,1)S(1)} %collective-permute-done.5.refs_1_, ...), custom_call_target="tpu_custom_call" | custom-call | flops 9663676416 | tf_op jit(solution)/shard_map/expert/pallas_call | solution.py:146
  27.5 2.1 %collective-permute-start.10 = (bf16[64,4224]{1,0:T(8,128)(2,1)S(1)}, bf16[64,4224]{1,0:T(8,128)(2,1)S(1)}, u32[]{:S(2)}, u32[]{:S(2)}) collective-permute-start(bf16[64,4224]{1,0:T(8,128)(2,1)S(1)} %collective-permute-done.7.refs_1_), channel_id=1, source_target_pairs={{0,4},{1,3},{4,8},{5,1},{8,12},{9,5},{12,14},{13,9},{14,10},{15,13... | collective-permute-start | bytes 1622024 | tf_op jit(solution)/shard_map/gather_short_3/ppermute | solution.py:326
  29.6 3.7 %collective-permute-done.14.refs_1_ = bf16[64,4224]{1,0:T(8,128)(2,1)S(1)} collective-permute-done((bf16[64,4224]{1,0:T(8,128)(2,1)S(1)}, bf16[64,4224]{1,0:T(8,128)(2,1)S(1)}, u32[]{:S(2)}, u32[]{:S(2)}) %collective-permute-start.14) | collective-permute-done | bytes 540704 | tf_op jit(solution)/shard_map/gather_long_2/ppermute | solution.py:326
  33.3 2.1 %collective-permute-start.15 = (bf16[64,4224]{1,0:T(8,128)(2,1)S(1)}, bf16[64,4224]{1,0:T(8,128)(2,1)S(1)}, u32[]{:S(2)}, u32[]{:S(2)}) collective-permute-start(bf16[64,4224]{1,0:T(8,128)(2,1)S(1)} %collective-permute-done.14.refs_1_), channel_id=1, source_target_pairs={{0,4},{1,3},{4,8},{5,1},{8,12},{9,5},{12,14},{13,9},{14,10},{15,13... | collective-permute-start | bytes 1622024 | tf_op jit(solution)/shard_map/gather_long_3/ppermute | solution.py:326
  35.4 2.9 %expert.10 = (bf16[64,4096]{1,0:T(8,128)(2,1)S(1)}, bf16[64,4096]{1,0:T(8,128)(2,1)S(1)}) custom-call(bf16[64,4224]{1,0:T(8,128)(2,1)S(1)} %collective-permute-done.8.refs_0_, bf16[64,4224]{1,0:T(8,128)(2,1)S(1)} %collective-permute-done.7.refs_1_, f32[1,128]{1,0:T(1,128)S(1)} %compare_select_fusion.1.refs_2_.refs_4_.refs_1_, f32[1,1536]{1,0:T(1,128)S(1)} %copy-done.1, ...), custom_call_target="tpu_custom_call" | custom-call | flops 4831838208 | tf_op jit(solution)/shard_map/expert/pallas_call | solution.py:146
  39.1 5.8 %collective-permute-done.15.refs_1_ = bf16[64,4224]{1,0:T(8,128)(2,1)S(1)} collective-permute-done((bf16[64,4224]{1,0:T(8,128)(2,1)S(1)}, bf16[64,4224]{1,0:T(8,128)(2,1)S(1)}, u32[]{:S(2)}, u32[]{:S(2)}) %collective-permute-start.15) | collective-permute-done | bytes 540704 | tf_op jit(solution)/shard_map/gather_long_3/ppermute | solution.py:326
  44.9 2.1 %collective-permute-start.16 = (bf16[64,4224]{1,0:T(8,128)(2,1)S(1)}, bf16[64,4224]{1,0:T(8,128)(2,1)S(1)}, u32[]{:S(2)}, u32[]{:S(2)}) collective-permute-start(bf16[64,4224]{1,0:T(8,128)(2,1)S(1)} %collective-permute-done.15.refs_1_), channel_id=1, source_target_pairs={{0,4},{1,3},{4,8},{5,1},{8,12},{9,5},{12,14},{13,9},{14,10},{15,13... | collective-permute-start | bytes 1622024 | tf_op jit(solution)/shard_map/gather_long_4/ppermute | solution.py:326
  47.0 2.9 %expert.11 = (bf16[64,4096]{1,0:T(8,128)(2,1)S(1)}, bf16[64,4096]{1,0:T(8,128)(2,1)S(1)}) custom-call(bf16[64,4224]{1,0:T(8,128)(2,1)S(1)} %collective-permute-done.11.refs_0_, bf16[64,4224]{1,0:T(8,128)(2,1)S(1)} %collective-permute-done.10.refs_1_, f32[1,128]{1,0:T(1,128)S(1)} %compare_select_fusion.1.refs_2_.refs_4_.refs_1_, f32[1,1536]{1,0:T(1,128)S(1)} %copy-done.1, ...), custom_call_target="tpu_custom_call" | custom-call | flops 4831838208 | tf_op jit(solution)/shard_map/expert/pallas_call | solution.py:146
  50.1 2.9 %expert.12 = (bf16[64,4096]{1,0:T(8,128)(2,1)S(1)}, bf16[64,4096]{1,0:T(8,128)(2,1)S(1)}) custom-call(bf16[64,4224]{1,0:T(8,128)(2,1)S(1)} %collective-permute-done.17.refs_0_, bf16[64,4224]{1,0:T(8,128)(2,1)S(1)} %collective-permute-done.15.refs_1_, f32[1,128]{1,0:T(1,128)S(1)} %compare_select_fusion.1.refs_2_.refs_4_.refs_1_, f32[1,1536]{1,0:T(1,128)S(1)} %copy-done.1, ...), custom_call_target="tpu_custom_call" | custom-call | flops 4831838208 | tf_op jit(solution)/shard_map/expert/pallas_call | solution.py:146
  53.1 1.5 %collective-permute-start.13 = (bf16[64,4096]{1,0:T(8,128)(2,1)S(1)}, bf16[64,4096]{1,0:T(8,128)(2,1)S(1)}, u32[]{:S(2)}, u32[]{:S(2)}) collective-permute-start(bf16[64,4096]{1,0:T(8,128)(2,1)S(1)} %step_sum.5), channel_id=1, source_target_pairs={{0,4},{1,3},{4,8},{5,1},{8,12},{9,5},{12,14},{13,9},{14,10},{15,13... | collective-permute-start | bytes 1572872 | tf_op jit(solution)/shard_map/return_short_3/ppermute | solution.py:326
  54.6 3.4 %expert.13 = bf16[64,4096]{1,0:T(8,128)(2,1)S(1)} custom-call(bf16[64,4224]{1,0:T(8,128)(2,1)S(1)} %collective-permute-done.16.refs_0_, f32[1,128]{1,0:T(1,128)S(1)} %compare_select_fusion.1.refs_2_.refs_4_.refs_1_, f32[1,1536]{1,0:T(1,128)S(1)} %copy-done.1, f32[1,4096]{1,0:T(1,128)S(1)} %copy-done, ...), custom_call_target="tpu_custom_call" | custom-call | flops 2415919104 | tf_op jit(solution)/shard_map/expert/pallas_call | solution.py:146
  59.1 3.2 %collective-permute-done.13.refs_2_ = bf16[64,4096]{1,0:T(8,128)(2,1)S(1)} collective-permute-done((bf16[64,4096]{1,0:T(8,128)(2,1)S(1)}, bf16[64,4096]{1,0:T(8,128)(2,1)S(1)}, u32[]{:S(2)}, u32[]{:S(2)}) %collective-permute-start.13) | collective-permute-done | bytes 524320 | tf_op jit(solution)/shard_map/return_short_3/ppermute | solution.py:326
  62.4 3.4 %expert.14.refs_0_ = bf16[64,4096]{1,0:T(8,128)(2,1)S(1)} custom-call(bf16[64,4224]{1,0:T(8,128)(2,1)S(1)} %collective-permute-done.18.refs_0_, f32[1,128]{1,0:T(1,128)S(1)} %compare_select_fusion.1.refs_2_.refs_4_.refs_1_, f32[1,1536]{1,0:T(1,128)S(1)} %copy-done.1, f32[1,4096]{1,0:T(1,128)S(1)} %copy-done, ...), custom_call_target="tpu_custom_call" | custom-call | flops 2415919104 | tf_op jit(solution)/shard_map/expert/pallas_call | solution.py:146
  65.9 1.5 %collective-permute-start.22 = (bf16[64,4096]{1,0:T(8,128)(2,1)S(1)}, bf16[64,4096]{1,0:T(8,128)(2,1)S(1)}, u32[]{:S(2)}, u32[]{:S(2)}) collective-permute-start(bf16[64,4096]{1,0:T(8,128)(2,1)S(1)} %step_sum.6), channel_id=1, source_target_pairs={{0,4},{1,3},{4,8},{5,1},{8,12},{9,5},{12,14},{13,9},{14,10},{15,13... | collective-permute-start | bytes 1572872 | tf_op jit(solution)/shard_map/return_long_4/ppermute | solution.py:326
  68.1 1.6 %collective-permute-start.20 = (bf16[64,4096]{1,0:T(8,128)(2,1)S(1)}, bf16[64,4096]{1,0:T(8,128)(2,1)S(1)}, u32[]{:S(2)}, u32[]{:S(2)}) collective-permute-start(bf16[64,4096]{1,0:T(8,128)(2,1)S(1)} %step_sum.7), channel_id=1, source_target_pairs={{0,4},{1,3},{4,8},{5,1},{8,12},{9,5},{12,14},{13,9},{14,10},{15,13... | collective-permute-start | bytes 1572872 | tf_op jit(solution)/shard_map/return_short_2/ppermute | solution.py:326
  69.7 5.4 %collective-permute-done.22.refs_2_ = bf16[64,4096]{1,0:T(8,128)(2,1)S(1)} collective-permute-done((bf16[64,4096]{1,0:T(8,128)(2,1)S(1)}, bf16[64,4096]{1,0:T(8,128)(2,1)S(1)}, u32[]{:S(2)}, u32[]{:S(2)}) %collective-permute-start.22) | collective-permute-done | bytes 524320 | tf_op jit(solution)/shard_map/return_long_4/ppermute | solution.py:326
  75.4 1.7 %collective-permute-start.28 = (bf16[64,4096]{1,0:T(8,128)(2,1)S(1)}, bf16[64,4096]{1,0:T(8,128)(2,1)S(1)}, u32[]{:S(2)}, u32[]{:S(2)}) collective-permute-start(bf16[64,4096]{1,0:T(8,128)(2,1)S(1)} %step_sum.8), channel_id=1, source_target_pairs={{0,4},{1,3},{4,8},{5,1},{8,12},{9,5},{12,14},{13,9},{14,10},{15,13... | collective-permute-start | bytes 1572872 | tf_op jit(solution)/shard_map/return_long_3/ppermute | solution.py:326
  77.1 2.9 %expert.15 = (bf16[64,4096]{1,0:T(8,128)(2,1)S(1)}, bf16[64,4096]{1,0:T(8,128)(2,1)S(1)}) custom-call(bf16[64,4224]{1,0:T(8,128)(2,1)S(1)} %collective-permute-done.26.refs_0_, bf16[64,4224]{1,0:T(8,128)(2,1)S(1)} %collective-permute-done.14.refs_1_, f32[1,128]{1,0:T(1,128)S(1)} %compare_select_fusion.1.refs_2_.refs_4_.refs_1_, f32[1,1536]{1,0:T(1,128)S(1)} %copy-done.1, ...), custom_call_target="tpu_custom_call" | custom-call | flops 4831838208 | tf_op jit(solution)/shard_map/expert/pallas_call | solution.py:146
  81.0 1.5 %collective-permute-start.23 = (bf16[32,4096]{1,0:T(8,128)(2,1)S(1)}, bf16[32,4096]{1,0:T(8,128)(2,1)S(1)}, u32[]{:S(2)}, u32[]{:S(2)}) collective-permute-start(bf16[32,4096]{1,0:T(8,128)(2,1)S(1)} %get-tuple-element.74), channel_id=1, source_target_pairs={{0,4},{1,3},{4,8},{5,1},{8,12},{9,5},{12,14},{13,9},{14,10},{15,13... | collective-permute-start | bytes 786440 | tf_op jit(solution)/shard_map/return_short_1/ppermute | solution.py:326
  82.4 3.9 %collective-permute-done.28.refs_2_ = bf16[64,4096]{1,0:T(8,128)(2,1)S(1)} collective-permute-done((bf16[64,4096]{1,0:T(8,128)(2,1)S(1)}, bf16[64,4096]{1,0:T(8,128)(2,1)S(1)}, u32[]{:S(2)}, u32[]{:S(2)}) %collective-permute-start.28) | collective-permute-done | bytes 524320 | tf_op jit(solution)/shard_map/return_long_3/ppermute | solution.py:326
  86.6 1.5 %collective-permute-start.29 = (bf16[64,4096]{1,0:T(8,128)(2,1)S(1)}, bf16[64,4096]{1,0:T(8,128)(2,1)S(1)}, u32[]{:S(2)}, u32[]{:S(2)}) collective-permute-start(bf16[64,4096]{1,0:T(8,128)(2,1)S(1)} %step_sum.9), channel_id=1, source_target_pairs={{0,4},{1,3},{4,8},{5,1},{8,12},{9,5},{12,14},{13,9},{14,10},{15,13... | collective-permute-start | bytes 1572872 | tf_op jit(solution)/shard_map/return_long_2/ppermute | solution.py:326
  89.2 1.8 %collective-permute-done.24.short_cross = bf16[32,4096]{1,0:T(8,128)(2,1)S(1)} collective-permute-done((bf16[32,4096]{1,0:T(8,128)(2,1)S(1)}, bf16[32,4096]{1,0:T(8,128)(2,1)S(1)}, u32[]{:S(2)}, u32[]{:S(2)}) %collective-permute-start.24) | collective-permute-done | bytes 262176 | tf_op jit(solution)/shard_map/return_short_1/ppermute | solution.py:326
  91.1 6.5 %collective-permute-done.29.refs_2_ = bf16[64,4096]{1,0:T(8,128)(2,1)S(1)} collective-permute-done((bf16[64,4096]{1,0:T(8,128)(2,1)S(1)}, bf16[64,4096]{1,0:T(8,128)(2,1)S(1)}, u32[]{:S(2)}, u32[]{:S(2)}) %collective-permute-start.29) | collective-permute-done | bytes 524320 | tf_op jit(solution)/shard_map/return_long_2/ppermute | solution.py:326
  97.9 1.5 %collective-permute-start.31 = (bf16[32,4096]{1,0:T(8,128)(2,1)S(1)}, bf16[32,4096]{1,0:T(8,128)(2,1)S(1)}, u32[]{:S(2)}, u32[]{:S(2)}) collective-permute-start(bf16[32,4096]{1,0:T(8,128)(2,1)S(1)} %get-tuple-element.82), channel_id=1, source_target_pairs={{0,4},{1,3},{4,8},{5,1},{8,12},{9,5},{12,14},{13,9},{14,10},{15,13... | collective-permute-start | bytes 786440 | tf_op jit(solution)/shard_map/return_long_1/ppermute | solution.py:326
  99.4 4.3 %collective-permute-done.30.long_cross = bf16[32,4096]{1,0:T(8,128)(2,1)S(1)} collective-permute-done((bf16[32,4096]{1,0:T(8,128)(2,1)S(1)}, bf16[32,4096]{1,0:T(8,128)(2,1)S(1)}, u32[]{:S(2)}, u32[]{:S(2)}) %collective-permute-start.30) | collective-permute-done | bytes 262176 | tf_op jit(solution)/shard_map/return_long_1/ppermute | solution.py:326
  103.7 2.9 %collective-permute-done.31.long_same = bf16[32,4096]{1,0:T(8,128)(2,1)S(1)} collective-permute-done((bf16[32,4096]{1,0:T(8,128)(2,1)S(1)}, bf16[32,4096]{1,0:T(8,128)(2,1)S(1)}, u32[]{:S(2)}, u32[]{:S(2)}) %collective-permute-start.31) | collective-permute-done | bytes 262176 | tf_op jit(solution)/shard_map/return_long_1/ppermute | solution.py:326
  (57 shorter events, 12.3 us)
Async XLA Ops:
  1.3 10.9 %collective-permute-start = (bf16[64,4224]{1,0:T(8,128)(2,1)S(1)}, bf16[64,4224]{1,0:T(8,128)(2,1)S(1)}, u32[]{:S(2)}, u32[]{:S(2)}) collective-permute-start(bf16[64,4224]{1,0:T(8,128)(2,1)S(1)} %get-tuple-element.44.refs_0_), channel_id=1, source_target_pairs={{0,1},{1,0},{2,3},{3,2},{4,5},{5,4},{6,7},{7,6},{8,9},{9,8},{10,11... | collective-permute-start | bytes 1622024 | tf_op jit(solution)/shard_map/swap_in_0/ppermute | solution.py:326
  1.8 14.3 %collective-permute-start.2 = (bf16[64,4224]{1,0:T(8,128)(2,1)S(1)}, bf16[64,4224]{1,0:T(8,128)(2,1)S(1)}, u32[]{:S(2)}, u32[]{:S(2)}) collective-permute-start(bf16[64,4224]{1,0:T(8,128)(2,1)S(1)} %get-tuple-element.44.refs_0_), channel_id=1, source_target_pairs={{0,4},{1,3},{4,8},{5,1},{8,12},{9,5},{12,14},{13,9},{14,10},{15,13... | collective-permute-start | bytes 1622024 | tf_op jit(solution)/shard_map/gather_long_1/ppermute | solution.py:326
  4.5 13.1 %collective-permute-start.3 = (bf16[64,4224]{1,0:T(8,128)(2,1)S(1)}, bf16[64,4224]{1,0:T(8,128)(2,1)S(1)}, u32[]{:S(2)}, u32[]{:S(2)}) collective-permute-start(bf16[64,4224]{1,0:T(8,128)(2,1)S(1)} %get-tuple-element.50), channel_id=1, source_target_pairs={{0,3},{1,4},{4,1},{5,8},{8,5},{9,12},{12,9},{13,14},{14,13},{15,10... | collective-permute-start | bytes 1622024 | tf_op jit(solution)/shard_map/gather_long_1/ppermute | solution.py:326
  17.6 4.2 %collective-permute-start.4 = (bf16[64,4224]{1,0:T(8,128)(2,1)S(1)}, bf16[64,4224]{1,0:T(8,128)(2,1)S(1)}, u32[]{:S(2)}, u32[]{:S(2)}) collective-permute-start(bf16[64,4224]{1,0:T(8,128)(2,1)S(1)} %get-tuple-element.52.refs_2_), channel_id=1, source_target_pairs={{0,1},{1,0},{2,3},{3,2},{4,5},{5,4},{6,7},{7,6},{8,9},{9,8},{10,11... | collective-permute-start | bytes 1622024 | tf_op jit(solution)/shard_map/swap_in_1/ppermute | solution.py:326
  17.7 4.2 %collective-permute-start.5 = (bf16[64,4224]{1,0:T(8,128)(2,1)S(1)}, bf16[64,4224]{1,0:T(8,128)(2,1)S(1)}, u32[]{:S(2)}, u32[]{:S(2)}) collective-permute-start(bf16[64,4224]{1,0:T(8,128)(2,1)S(1)} %get-tuple-element.54.refs_3_), channel_id=1, source_target_pairs={{0,1},{1,0},{2,3},{3,2},{4,5},{5,4},{6,7},{7,6},{8,9},{9,8},{10,11... | collective-permute-start | bytes 1622024 | tf_op jit(solution)/shard_map/swap_in_1/ppermute | solution.py:326
  18.2 9.4 %collective-permute-start.7 = (bf16[64,4224]{1,0:T(8,128)(2,1)S(1)}, bf16[64,4224]{1,0:T(8,128)(2,1)S(1)}, u32[]{:S(2)}, u32[]{:S(2)}) collective-permute-start(bf16[64,4224]{1,0:T(8,128)(2,1)S(1)} %get-tuple-element.54.refs_3_), channel_id=1, source_target_pairs={{0,4},{1,3},{4,8},{5,1},{8,12},{9,5},{12,14},{13,9},{14,10},{15,13... | collective-permute-start | bytes 1622024 | tf_op jit(solution)/shard_map/gather_short_2/ppermute | solution.py:326
  20.3 13.1 %collective-permute-start.14 = (bf16[64,4224]{1,0:T(8,128)(2,1)S(1)}, bf16[64,4224]{1,0:T(8,128)(2,1)S(1)}, u32[]{:S(2)}, u32[]{:S(2)}) collective-permute-start(bf16[64,4224]{1,0:T(8,128)(2,1)S(1)} %get-tuple-element.52.refs_2_), channel_id=1, source_target_pairs={{0,4},{1,3},{4,8},{5,1},{8,12},{9,5},{12,14},{13,9},{14,10},{15,13... | collective-permute-start | bytes 1622024 | tf_op jit(solution)/shard_map/gather_long_2/ppermute | solution.py:326
  27.5 7.9 %collective-permute-start.8 = (bf16[64,4224]{1,0:T(8,128)(2,1)S(1)}, bf16[64,4224]{1,0:T(8,128)(2,1)S(1)}, u32[]{:S(2)}, u32[]{:S(2)}) collective-permute-start(bf16[64,4224]{1,0:T(8,128)(2,1)S(1)} %collective-permute-done.7.refs_1_), channel_id=1, source_target_pairs={{0,1},{1,0},{2,3},{3,2},{4,5},{5,4},{6,7},{7,6},{8,9},{9,8},{10,11... | collective-permute-start | bytes 1622024 | tf_op jit(solution)/shard_map/swap_in_2/ppermute | solution.py:326
  27.5 11.6 %collective-permute-start.10 = (bf16[64,4224]{1,0:T(8,128)(2,1)S(1)}, bf16[64,4224]{1,0:T(8,128)(2,1)S(1)}, u32[]{:S(2)}, u32[]{:S(2)}) collective-permute-start(bf16[64,4224]{1,0:T(8,128)(2,1)S(1)} %collective-permute-done.7.refs_1_), channel_id=1, source_target_pairs={{0,4},{1,3},{4,8},{5,1},{8,12},{9,5},{12,14},{13,9},{14,10},{15,13... | collective-permute-start | bytes 1622024 | tf_op jit(solution)/shard_map/gather_short_3/ppermute | solution.py:326
  33.3 11.6 %collective-permute-start.15 = (bf16[64,4224]{1,0:T(8,128)(2,1)S(1)}, bf16[64,4224]{1,0:T(8,128)(2,1)S(1)}, u32[]{:S(2)}, u32[]{:S(2)}) collective-permute-start(bf16[64,4224]{1,0:T(8,128)(2,1)S(1)} %collective-permute-done.14.refs_1_), channel_id=1, source_target_pairs={{0,4},{1,3},{4,8},{5,1},{8,12},{9,5},{12,14},{13,9},{14,10},{15,13... | collective-permute-start | bytes 1622024 | tf_op jit(solution)/shard_map/gather_long_3/ppermute | solution.py:326
  39.1 7.9 %collective-permute-start.11 = (bf16[64,4224]{1,0:T(8,128)(2,1)S(1)}, bf16[64,4224]{1,0:T(8,128)(2,1)S(1)}, u32[]{:S(2)}, u32[]{:S(2)}) collective-permute-start(bf16[64,4224]{1,0:T(8,128)(2,1)S(1)} %collective-permute-done.10.refs_1_), channel_id=1, source_target_pairs={{0,1},{1,0},{2,3},{3,2},{4,5},{5,4},{6,7},{7,6},{8,9},{9,8},{10,11... | collective-permute-start | bytes 1622024 | tf_op jit(solution)/shard_map/swap_in_3/ppermute | solution.py:326
  44.9 5.2 %collective-permute-start.17 = (bf16[64,4224]{1,0:T(8,128)(2,1)S(1)}, bf16[64,4224]{1,0:T(8,128)(2,1)S(1)}, u32[]{:S(2)}, u32[]{:S(2)}) collective-permute-start(bf16[64,4224]{1,0:T(8,128)(2,1)S(1)} %collective-permute-done.15.refs_1_), channel_id=1, source_target_pairs={{0,1},{1,0},{2,3},{3,2},{4,5},{5,4},{6,7},{7,6},{8,9},{9,8},{10,11... | collective-permute-start | bytes 1622024 | tf_op jit(solution)/shard_map/swap_in_3/ppermute | solution.py:326
  44.9 9.7 %collective-permute-start.16 = (bf16[64,4224]{1,0:T(8,128)(2,1)S(1)}, bf16[64,4224]{1,0:T(8,128)(2,1)S(1)}, u32[]{:S(2)}, u32[]{:S(2)}) collective-permute-start(bf16[64,4224]{1,0:T(8,128)(2,1)S(1)} %collective-permute-done.15.refs_1_), channel_id=1, source_target_pairs={{0,4},{1,3},{4,8},{5,1},{8,12},{9,5},{12,14},{13,9},{14,10},{15,13... | collective-permute-start | bytes 1622024 | tf_op jit(solution)/shard_map/gather_long_4/ppermute | solution.py:326
  49.9 3.1 %collective-permute-start.12 = (bf16[64,4096]{1,0:T(8,128)(2,1)S(1)}, bf16[64,4096]{1,0:T(8,128)(2,1)S(1)}, u32[]{:S(2)}, u32[]{:S(2)}) collective-permute-start(bf16[64,4096]{1,0:T(8,128)(2,1)S(1)} %get-tuple-element.63), channel_id=1, source_target_pairs={{0,1},{1,0},{2,3},{3,2},{4,5},{5,4},{6,7},{7,6},{8,9},{9,8},{10,11... | collective-permute-start | bytes 1572872 | tf_op jit(solution)/shard_map/swap_out_3/ppermute | solution.py:326
  53.1 9.2 %collective-permute-start.13 = (bf16[64,4096]{1,0:T(8,128)(2,1)S(1)}, bf16[64,4096]{1,0:T(8,128)(2,1)S(1)}, u32[]{:S(2)}, u32[]{:S(2)}) collective-permute-start(bf16[64,4096]{1,0:T(8,128)(2,1)S(1)} %step_sum.5), channel_id=1, source_target_pairs={{0,4},{1,3},{4,8},{5,1},{8,12},{9,5},{12,14},{13,9},{14,10},{15,13... | collective-permute-start | bytes 1572872 | tf_op jit(solution)/shard_map/return_short_3/ppermute | solution.py:326
  54.6 7.8 %collective-permute-start.18 = (bf16[64,4224]{1,0:T(8,128)(2,1)S(1)}, bf16[64,4224]{1,0:T(8,128)(2,1)S(1)}, u32[]{:S(2)}, u32[]{:S(2)}) collective-permute-start(bf16[64,4224]{1,0:T(8,128)(2,1)S(1)} %collective-permute-done.16.refs_0_), channel_id=1, source_target_pairs={{0,1},{1,0},{2,3},{3,2},{4,5},{5,4},{6,7},{7,6},{8,9},{9,8},{10,11... | collective-permute-start | bytes 1622024 | tf_op jit(solution)/shard_map/swap_in_4/ppermute | solution.py:326
  58.0 4.3 %collective-permute-start.19 = (bf16[64,4096]{1,0:T(8,128)(2,1)S(1)}, bf16[64,4096]{1,0:T(8,128)(2,1)S(1)}, u32[]{:S(2)}, u32[]{:S(2)}) collective-permute-start(bf16[64,4096]{1,0:T(8,128)(2,1)S(1)} %expert.13), channel_id=1, source_target_pairs={{0,1},{1,0},{2,3},{3,2},{4,5},{5,4},{6,7},{7,6},{8,9},{9,8},{10,11... | collective-permute-start | bytes 1572872 | tf_op jit(solution)/shard_map/swap_out_4/ppermute | solution.py:326
  58.6 18.5 %collective-permute-start.26 = (bf16[64,4224]{1,0:T(8,128)(2,1)S(1)}, bf16[64,4224]{1,0:T(8,128)(2,1)S(1)}, u32[]{:S(2)}, u32[]{:S(2)}) collective-permute-start(bf16[64,4224]{1,0:T(8,128)(2,1)S(1)} %collective-permute-done.14.refs_1_), channel_id=1, source_target_pairs={{0,1},{1,0},{2,3},{3,2},{4,5},{5,4},{6,7},{7,6},{8,9},{9,8},{10,11... | collective-permute-start | bytes 1622024 | tf_op jit(solution)/shard_map/swap_in_2/ppermute | solution.py:326
  58.7 9.2 %collective-permute-start.9 = (bf16[64,4096]{1,0:T(8,128)(2,1)S(1)}, bf16[64,4096]{1,0:T(8,128)(2,1)S(1)}, u32[]{:S(2)}, u32[]{:S(2)}) collective-permute-start(bf16[64,4096]{1,0:T(8,128)(2,1)S(1)} %get-tuple-element.60), channel_id=1, source_target_pairs={{0,1},{1,0},{2,3},{3,2},{4,5},{5,4},{6,7},{7,6},{8,9},{9,8},{10,11... | collective-permute-start | bytes 1572872 | tf_op jit(solution)/shard_map/swap_out_2/ppermute | solution.py:326
  65.9 9.2 %collective-permute-start.22 = (bf16[64,4096]{1,0:T(8,128)(2,1)S(1)}, bf16[64,4096]{1,0:T(8,128)(2,1)S(1)}, u32[]{:S(2)}, u32[]{:S(2)}) collective-permute-start(bf16[64,4096]{1,0:T(8,128)(2,1)S(1)} %step_sum.6), channel_id=1, source_target_pairs={{0,4},{1,3},{4,8},{5,1},{8,12},{9,5},{12,14},{13,9},{14,10},{15,13... | collective-permute-start | bytes 1572872 | tf_op jit(solution)/shard_map/return_long_4/ppermute | solution.py:326
  67.4 7.8 %collective-permute-start.21 = (bf16[64,4096]{1,0:T(8,128)(2,1)S(1)}, bf16[64,4096]{1,0:T(8,128)(2,1)S(1)}, u32[]{:S(2)}, u32[]{:S(2)}) collective-permute-start(bf16[64,4096]{1,0:T(8,128)(2,1)S(1)} %get-tuple-element.71), channel_id=1, source_target_pairs={{0,1},{1,0},{2,3},{3,2},{4,5},{5,4},{6,7},{7,6},{8,9},{9,8},{10,11... | collective-permute-start | bytes 1572872 | tf_op jit(solution)/shard_map/swap_out_3/ppermute | solution.py:326
  67.4 13.4 %collective-permute-start.6 = (bf16[64,4096]{1,0:T(8,128)(2,1)S(1)}, bf16[64,4096]{1,0:T(8,128)(2,1)S(1)}, u32[]{:S(2)}, u32[]{:S(2)}) collective-permute-start(bf16[64,4096]{1,0:T(8,128)(2,1)S(1)} %get-tuple-element.56), channel_id=1, source_target_pairs={{0,1},{1,0},{2,3},{3,2},{4,5},{5,4},{6,7},{7,6},{8,9},{9,8},{10,11... | collective-permute-start | bytes 1572872 | tf_op jit(solution)/shard_map/swap_out_1/ppermute | solution.py:326
  68.1 12.7 %collective-permute-start.20 = (bf16[64,4096]{1,0:T(8,128)(2,1)S(1)}, bf16[64,4096]{1,0:T(8,128)(2,1)S(1)}, u32[]{:S(2)}, u32[]{:S(2)}) collective-permute-start(bf16[64,4096]{1,0:T(8,128)(2,1)S(1)} %step_sum.7), channel_id=1, source_target_pairs={{0,4},{1,3},{4,8},{5,1},{8,12},{9,5},{12,14},{13,9},{14,10},{15,13... | collective-permute-start | bytes 1572872 | tf_op jit(solution)/shard_map/return_short_2/ppermute | solution.py:326
  75.4 11.0 %collective-permute-start.28 = (bf16[64,4096]{1,0:T(8,128)(2,1)S(1)}, bf16[64,4096]{1,0:T(8,128)(2,1)S(1)}, u32[]{:S(2)}, u32[]{:S(2)}) collective-permute-start(bf16[64,4096]{1,0:T(8,128)(2,1)S(1)} %step_sum.8), channel_id=1, source_target_pairs={{0,4},{1,3},{4,8},{5,1},{8,12},{9,5},{12,14},{13,9},{14,10},{15,13... | collective-permute-start | bytes 1572872 | tf_op jit(solution)/shard_map/return_long_3/ppermute | solution.py:326
  79.9 6.5 %collective-permute-start.27 = (bf16[64,4096]{1,0:T(8,128)(2,1)S(1)}, bf16[64,4096]{1,0:T(8,128)(2,1)S(1)}, u32[]{:S(2)}, u32[]{:S(2)}) collective-permute-start(bf16[64,4096]{1,0:T(8,128)(2,1)S(1)} %get-tuple-element.78), channel_id=1, source_target_pairs={{0,1},{1,0},{2,3},{3,2},{4,5},{5,4},{6,7},{7,6},{8,9},{9,8},{10,11... | collective-permute-start | bytes 1572872 | tf_op jit(solution)/shard_map/swap_out_2/ppermute | solution.py:326
  80.0 8.1 %collective-permute-start.1 = (bf16[64,4096]{1,0:T(8,128)(2,1)S(1)}, bf16[64,4096]{1,0:T(8,128)(2,1)S(1)}, u32[]{:S(2)}, u32[]{:S(2)}) collective-permute-start(bf16[64,4096]{1,0:T(8,128)(2,1)S(1)} %get-tuple-element.48), channel_id=1, source_target_pairs={{0,1},{1,0},{2,3},{3,2},{4,5},{5,4},{6,7},{7,6},{8,9},{9,8},{10,11... | collective-permute-start | bytes 1572872 | tf_op jit(solution)/shard_map/swap_out_0/ppermute | solution.py:326
  81.0 8.2 %collective-permute-start.23 = (bf16[32,4096]{1,0:T(8,128)(2,1)S(1)}, bf16[32,4096]{1,0:T(8,128)(2,1)S(1)}, u32[]{:S(2)}, u32[]{:S(2)}) collective-permute-start(bf16[32,4096]{1,0:T(8,128)(2,1)S(1)} %get-tuple-element.74), channel_id=1, source_target_pairs={{0,4},{1,3},{4,8},{5,1},{8,12},{9,5},{12,14},{13,9},{14,10},{15,13... | collective-permute-start | bytes 786440 | tf_op jit(solution)/shard_map/return_short_1/ppermute | solution.py:326
  82.4 8.5 %collective-permute-start.24 = (bf16[32,4096]{1,0:T(8,128)(2,1)S(1)}, bf16[32,4096]{1,0:T(8,128)(2,1)S(1)}, u32[]{:S(2)}, u32[]{:S(2)}) collective-permute-start(bf16[32,4096]{1,0:T(8,128)(2,1)S(1)} %get-tuple-element.75), channel_id=1, source_target_pairs={{0,5},{1,2},{4,9},{5,0},{8,13},{9,4},{12,15},{13,8},{14,11},{15,12... | collective-permute-start | bytes 786440 | tf_op jit(solution)/shard_map/return_short_1/ppermute | solution.py:326
  86.4 11.2 %collective-permute-start.25 = (bf16[64,4096]{1,0:T(8,128)(2,1)S(1)}, bf16[64,4096]{1,0:T(8,128)(2,1)S(1)}, u32[]{:S(2)}, u32[]{:S(2)}) collective-permute-start(bf16[64,4096]{1,0:T(8,128)(2,1)S(1)} %get-tuple-element.76), channel_id=1, source_target_pairs={{0,1},{1,0},{2,3},{3,2},{4,5},{5,4},{6,7},{7,6},{8,9},{9,8},{10,11... | collective-permute-start | bytes 1572872 | tf_op jit(solution)/shard_map/swap_out_1/ppermute | solution.py:326
  86.6 11.0 %collective-permute-start.29 = (bf16[64,4096]{1,0:T(8,128)(2,1)S(1)}, bf16[64,4096]{1,0:T(8,128)(2,1)S(1)}, u32[]{:S(2)}, u32[]{:S(2)}) collective-permute-start(bf16[64,4096]{1,0:T(8,128)(2,1)S(1)} %step_sum.9), channel_id=1, source_target_pairs={{0,4},{1,3},{4,8},{5,1},{8,12},{9,5},{12,14},{13,9},{14,10},{15,13... | collective-permute-start | bytes 1572872 | tf_op jit(solution)/shard_map/return_long_2/ppermute | solution.py:326
  97.8 5.9 %collective-permute-start.30 = (bf16[32,4096]{1,0:T(8,128)(2,1)S(1)}, bf16[32,4096]{1,0:T(8,128)(2,1)S(1)}, u32[]{:S(2)}, u32[]{:S(2)}) collective-permute-start(bf16[32,4096]{1,0:T(8,128)(2,1)S(1)} %get-tuple-element.81), channel_id=1, source_target_pairs={{0,5},{1,2},{4,9},{5,0},{8,13},{9,4},{12,15},{13,8},{14,11},{15,12... | collective-permute-start | bytes 786440 | tf_op jit(solution)/shard_map/return_long_1/ppermute | solution.py:326
  97.9 8.7 %collective-permute-start.31 = (bf16[32,4096]{1,0:T(8,128)(2,1)S(1)}, bf16[32,4096]{1,0:T(8,128)(2,1)S(1)}, u32[]{:S(2)}, u32[]{:S(2)}) collective-permute-start(bf16[32,4096]{1,0:T(8,128)(2,1)S(1)} %get-tuple-element.82), channel_id=1, source_target_pairs={{0,4},{1,3},{4,8},{5,1},{8,12},{9,5},{12,14},{13,9},{14,10},{15,13... | collective-permute-start | bytes 786440 | tf_op jit(solution)/shard_map/return_long_1/ppermute | solution.py:326
  (2 other events, 24.3 us)

commit v19 on v15

--- a/solution.py
+++ b/solution.py
@@ -9,7 +9,7 @@
 
 DENOMINATOR = 32768.0
 LANES = 128
-UNIT_CHUNK = 256
+UNIT_CHUNK = 768
 WIDTH_CHUNK = 1024
 ANYWHERE = pl.BlockSpec(memory_space=pl.ANY)
 VMEM = pl.BlockSpec(memory_space=pltpu.VMEM)

time: 106 us -> 106 us (level)
  no operation moved by 1% of the time
where the time goes in v19:
time: 106 us
  waiting for transfers between devices  41.8 us (39%)
  Pallas kernels  32.4 us (31%)
  starting transfers between devices  31.2 us (29%)
    ppermute x32, waiting for transfers between devices, send(): return lax.ppermute(x, 'expert', perm)  41.8 us
    ppermute x32, starting transfers between devices, send(): return lax.ppermute(x, 'expert', perm)  31.2 us
    pallas_call x7, Pallas kernels, expert_part(): pl.pallas_call(functools.partial(expert_kernel, len(blocks)), in_specs=[V...  22.4 us
    pallas_call x1, Pallas kernels, keep(): pl.pallas_call(keep_kernel, in_specs=[ANYWHERE] * 2, out_specs=[VMEM] * 2...  6.38 us
  transfers between devices with their start and end apart: 32, of which 15 were waited for; matrix products, arithmetic and copies ran while one was open for 0% of the time, Pallas kernels for 28%

profile of v19, /device:TPU:0, one launch (start us, length us, event | category | flops | bytes accessed | tf_op | source)
XLA Modules:
  0.0 105.8 jit_solution(12502849489773592261)
XLA Ops:
  0.0 1.3 %pack.1 = (bf16[64,4224]{1,0:T(8,128)(2,1)S(1)}, bf16[64,4224]{1,0:T(8,128)(2,1)S(1)}) custom-call(s32[1]{0:T(128)} %bitcast.core, bf16[64,4096]{1,0:T(8,128)(2,1)} %tokens.1, s32[8,64]{1,0:T(8,128)} %bitcast.7, s32[8,64]{1,0:T(8,128)} %bitcast.8), custom_call_target="tpu_custom_call" | custom-call | tf_op jit(solution)/shard_map/pack/pallas_call | solution.py:64
  1.8 2.6 %collective-permute-start.2 = (bf16[64,4224]{1,0:T(8,128)(2,1)S(1)}, bf16[64,4224]{1,0:T(8,128)(2,1)S(1)}, u32[]{:S(2)}, u32[]{:S(2)}) collective-permute-start(bf16[64,4224]{1,0:T(8,128)(2,1)S(1)} %get-tuple-element.45.refs_0_), channel_id=1, source_target_pairs={{0,4},{1,3},{4,8},{5,1},{8,12},{9,5},{12,14},{13,9},{14,10},{15,13... | collective-permute-start | bytes 1622024 | tf_op jit(solution)/shard_map/gather_long_1/ppermute | solution.py:326
  5.7 6.4 %keep.1 = (bf16[4096,1536]{1,0:T(8,128)(2,1)S(1)}, bf16[768,4096]{1,0:T(8,128)(2,1)S(1)}) custom-call(bf16[4096,1536]{1,0:T(8,128)(2,1)} %bitcast.5, bf16[768,4096]{1,0:T(8,128)(2,1)} %bitcast.6), custom_call_target="tpu_custom_call" | custom-call | bytes 18874368 | tf_op jit(solution)/shard_map/keep/pallas_call | solution.py:88
  12.2 2.9 %expert.7 = (bf16[64,4096]{1,0:T(8,128)(2,1)S(1)}, bf16[64,4096]{1,0:T(8,128)(2,1)S(1)}) custom-call(bf16[64,4224]{1,0:T(8,128)(2,1)S(1)} %get-tuple-element.45.refs_0_, bf16[64,4224]{1,0:T(8,128)(2,1)S(1)} %collective-permute-done.refs_1_, f32[1,128]{1,0:T(1,128)S(1)} %compare_select_fusion.1.refs_2_.refs_4_, f32[1,1536]{1,0:T(1,128)S(1)} %copy-done.1, ...), custom_call_target="tpu_custom_call" | custom-call | flops 4831838208 | tf_op jit(solution)/shard_map/expert/pallas_call | solution.py:146
  16.1 1.4 %collective-permute-done.3.cross = bf16[64,4224]{1,0:T(8,128)(2,1)S(1)} collective-permute-done((bf16[64,4224]{1,0:T(8,128)(2,1)S(1)}, bf16[64,4224]{1,0:T(8,128)(2,1)S(1)}, u32[]{:S(2)}, u32[]{:S(2)}) %collective-permute-start.3) | collective-permute-done | bytes 540704 | tf_op jit(solution)/shard_map/gather_long_1/ppermute | solution.py:326
  18.2 2.1 %collective-permute-start.7 = (bf16[64,4224]{1,0:T(8,128)(2,1)S(1)}, bf16[64,4224]{1,0:T(8,128)(2,1)S(1)}, u32[]{:S(2)}, u32[]{:S(2)}) collective-permute-start(bf16[64,4224]{1,0:T(8,128)(2,1)S(1)} %get-tuple-element.55.refs_3_), channel_id=1, source_target_pairs={{0,4},{1,3},{4,8},{5,1},{8,12},{9,5},{12,14},{13,9},{14,10},{15,13... | collective-permute-start | bytes 1622024 | tf_op jit(solution)/shard_map/gather_short_2/ppermute | solution.py:326
  20.3 1.6 %collective-permute-start.14 = (bf16[64,4224]{1,0:T(8,128)(2,1)S(1)}, bf16[64,4224]{1,0:T(8,128)(2,1)S(1)}, u32[]{:S(2)}, u32[]{:S(2)}) collective-permute-start(bf16[64,4224]{1,0:T(8,128)(2,1)S(1)} %get-tuple-element.53.refs_2_), channel_id=1, source_target_pairs={{0,4},{1,3},{4,8},{5,1},{8,12},{9,5},{12,14},{13,9},{14,10},{15,13... | collective-permute-start | bytes 1622024 | tf_op jit(solution)/shard_map/gather_long_2/ppermute | solution.py:326
  21.8 5.3 %expert.8 = (bf16[64,4096]{1,0:T(8,128)(2,1)S(1)}, bf16[64,4096]{1,0:T(8,128)(2,1)S(1)}, bf16[64,4096]{1,0:T(8,128)(2,1)S(1)}, bf16[64,4096]{1,0:T(8,128)(2,1)S(1)}) custom-call(bf16[64,4224]{1,0:T(8,128)(2,1)S(1)} %collective-permute-done.4.refs_0_, bf16[64,4224]{1,0:T(8,128)(2,1)S(1)} %collective-permute-done.5.refs_1_, ...), custom_call_target="tpu_custom_call" | custom-call | flops 9663676416 | tf_op jit(solution)/shard_map/expert/pallas_call | solution.py:146
  27.5 2.1 %collective-permute-start.10 = (bf16[64,4224]{1,0:T(8,128)(2,1)S(1)}, bf16[64,4224]{1,0:T(8,128)(2,1)S(1)}, u32[]{:S(2)}, u32[]{:S(2)}) collective-permute-start(bf16[64,4224]{1,0:T(8,128)(2,1)S(1)} %collective-permute-done.7.refs_1_), channel_id=1, source_target_pairs={{0,4},{1,3},{4,8},{5,1},{8,12},{9,5},{12,14},{13,9},{14,10},{15,13... | collective-permute-start | bytes 1622024 | tf_op jit(solution)/shard_map/gather_short_3/ppermute | solution.py:326
  29.6 3.7 %collective-permute-done.14.refs_1_ = bf16[64,4224]{1,0:T(8,128)(2,1)S(1)} collective-permute-done((bf16[64,4224]{1,0:T(8,128)(2,1)S(1)}, bf16[64,4224]{1,0:T(8,128)(2,1)S(1)}, u32[]{:S(2)}, u32[]{:S(2)}) %collective-permute-start.14) | collective-permute-done | bytes 540704 | tf_op jit(solution)/shard_map/gather_long_2/ppermute | solution.py:326
  33.3 2.1 %collective-permute-start.15 = (bf16[64,4224]{1,0:T(8,128)(2,1)S(1)}, bf16[64,4224]{1,0:T(8,128)(2,1)S(1)}, u32[]{:S(2)}, u32[]{:S(2)}) collective-permute-start(bf16[64,4224]{1,0:T(8,128)(2,1)S(1)} %collective-permute-done.14.refs_1_), channel_id=1, source_target_pairs={{0,4},{1,3},{4,8},{5,1},{8,12},{9,5},{12,14},{13,9},{14,10},{15,13... | collective-permute-start | bytes 1622024 | tf_op jit(solution)/shard_map/gather_long_3/ppermute | solution.py:326
  35.4 2.9 %expert.9 = (bf16[64,4096]{1,0:T(8,128)(2,1)S(1)}, bf16[64,4096]{1,0:T(8,128)(2,1)S(1)}) custom-call(bf16[64,4224]{1,0:T(8,128)(2,1)S(1)} %collective-permute-done.8.refs_0_, bf16[64,4224]{1,0:T(8,128)(2,1)S(1)} %collective-permute-done.7.refs_1_, f32[1,128]{1,0:T(1,128)S(1)} %compare_select_fusion.1.refs_2_.refs_4_, f32[1,1536]{1,0:T(1,128)S(1)} %copy-done.1, ...), custom_call_target="tpu_custom_call" | custom-call | flops 4831838208 | tf_op jit(solution)/shard_map/expert/pallas_call | solution.py:146
  39.1 5.8 %collective-permute-done.15.refs_1_ = bf16[64,4224]{1,0:T(8,128)(2,1)S(1)} collective-permute-done((bf16[64,4224]{1,0:T(8,128)(2,1)S(1)}, bf16[64,4224]{1,0:T(8,128)(2,1)S(1)}, u32[]{:S(2)}, u32[]{:S(2)}) %collective-permute-start.15) | collective-permute-done | bytes 540704 | tf_op jit(solution)/shard_map/gather_long_3/ppermute | solution.py:326
  44.9 2.1 %collective-permute-start.16 = (bf16[64,4224]{1,0:T(8,128)(2,1)S(1)}, bf16[64,4224]{1,0:T(8,128)(2,1)S(1)}, u32[]{:S(2)}, u32[]{:S(2)}) collective-permute-start(bf16[64,4224]{1,0:T(8,128)(2,1)S(1)} %collective-permute-done.15.refs_1_), channel_id=1, source_target_pairs={{0,4},{1,3},{4,8},{5,1},{8,12},{9,5},{12,14},{13,9},{14,10},{15,13... | collective-permute-start | bytes 1622024 | tf_op jit(solution)/shard_map/gather_long_4/ppermute | solution.py:326
  47.0 2.9 %expert.10 = (bf16[64,4096]{1,0:T(8,128)(2,1)S(1)}, bf16[64,4096]{1,0:T(8,128)(2,1)S(1)}) custom-call(bf16[64,4224]{1,0:T(8,128)(2,1)S(1)} %collective-permute-done.11.refs_0_, bf16[64,4224]{1,0:T(8,128)(2,1)S(1)} %collective-permute-done.10.refs_1_, f32[1,128]{1,0:T(1,128)S(1)} %compare_select_fusion.1.refs_2_.refs_4_, f32[1,1536]{1,0:T(1,128)S(1)} %copy-done.1, ...), custom_call_target="tpu_custom_call" | custom-call | flops 4831838208 | tf_op jit(solution)/shard_map/expert/pallas_call | solution.py:146
  50.1 2.8 %expert.11 = (bf16[64,4096]{1,0:T(8,128)(2,1)S(1)}, bf16[64,4096]{1,0:T(8,128)(2,1)S(1)}) custom-call(bf16[64,4224]{1,0:T(8,128)(2,1)S(1)} %collective-permute-done.17.refs_0_, bf16[64,4224]{1,0:T(8,128)(2,1)S(1)} %collective-permute-done.15.refs_1_, f32[1,128]{1,0:T(1,128)S(1)} %compare_select_fusion.1.refs_2_.refs_4_, f32[1,1536]{1,0:T(1,128)S(1)} %copy-done.1, ...), custom_call_target="tpu_custom_call" | custom-call | flops 4831838208 | tf_op jit(solution)/shard_map/expert/pallas_call | solution.py:146
  54.3 2.1 %collective-permute-start.13 = (bf16[64,4096]{1,0:T(8,128)(2,1)S(1)}, bf16[64,4096]{1,0:T(8,128)(2,1)S(1)}, u32[]{:S(2)}, u32[]{:S(2)}) collective-permute-start(bf16[64,4096]{1,0:T(8,128)(2,1)S(1)} %step_sum.5), channel_id=1, source_target_pairs={{0,4},{1,3},{4,8},{5,1},{8,12},{9,5},{12,14},{13,9},{14,10},{15,13... | collective-permute-start | bytes 1572872 | tf_op jit(solution)/shard_map/return_short_3/ppermute | solution.py:326
  56.4 2.8 %expert.12 = (bf16[64,4096]{1,0:T(8,128)(2,1)S(1)}, bf16[64,4096]{1,0:T(8,128)(2,1)S(1)}) custom-call(bf16[64,4224]{1,0:T(8,128)(2,1)S(1)} %collective-permute-done.18.refs_0_, bf16[64,4224]{1,0:T(8,128)(2,1)S(1)} %collective-permute-done.16.refs_1_, f32[1,128]{1,0:T(1,128)S(1)} %compare_select_fusion.1.refs_2_.refs_4_, f32[1,1536]{1,0:T(1,128)S(1)} %copy-done.1, ...), custom_call_target="tpu_custom_call" | custom-call | flops 4831838208 | tf_op jit(solution)/shard_map/expert/pallas_call | solution.py:146
  59.9 3.5 %collective-permute-done.13.refs_2_ = bf16[64,4096]{1,0:T(8,128)(2,1)S(1)} collective-permute-done((bf16[64,4096]{1,0:T(8,128)(2,1)S(1)}, bf16[64,4096]{1,0:T(8,128)(2,1)S(1)}, u32[]{:S(2)}, u32[]{:S(2)}) %collective-permute-start.13) | collective-permute-done | bytes 524320 | tf_op jit(solution)/shard_map/return_short_3/ppermute | solution.py:326
  63.6 2.1 %collective-permute-start.22 = (bf16[64,4096]{1,0:T(8,128)(2,1)S(1)}, bf16[64,4096]{1,0:T(8,128)(2,1)S(1)}, u32[]{:S(2)}, u32[]{:S(2)}) collective-permute-start(bf16[64,4096]{1,0:T(8,128)(2,1)S(1)} %step_sum.6), channel_id=1, source_target_pairs={{0,4},{1,3},{4,8},{5,1},{8,12},{9,5},{12,14},{13,9},{14,10},{15,13... | collective-permute-start | bytes 1572872 | tf_op jit(solution)/shard_map/return_long_4/ppermute | solution.py:326
  66.4 1.6 %collective-permute-start.20 = (bf16[64,4096]{1,0:T(8,128)(2,1)S(1)}, bf16[64,4096]{1,0:T(8,128)(2,1)S(1)}, u32[]{:S(2)}, u32[]{:S(2)}) collective-permute-start(bf16[64,4096]{1,0:T(8,128)(2,1)S(1)} %step_sum.7), channel_id=1, source_target_pairs={{0,4},{1,3},{4,8},{5,1},{8,12},{9,5},{12,14},{13,9},{14,10},{15,13... | collective-permute-start | bytes 1572872 | tf_op jit(solution)/shard_map/return_short_2/ppermute | solution.py:326
  68.1 4.8 %collective-permute-done.22.refs_2_ = bf16[64,4096]{1,0:T(8,128)(2,1)S(1)} collective-permute-done((bf16[64,4096]{1,0:T(8,128)(2,1)S(1)}, bf16[64,4096]{1,0:T(8,128)(2,1)S(1)}, u32[]{:S(2)}, u32[]{:S(2)}) %collective-permute-start.22) | collective-permute-done | bytes 524320 | tf_op jit(solution)/shard_map/return_long_4/ppermute | solution.py:326
  73.1 2.1 %collective-permute-start.28 = (bf16[64,4096]{1,0:T(8,128)(2,1)S(1)}, bf16[64,4096]{1,0:T(8,128)(2,1)S(1)}, u32[]{:S(2)}, u32[]{:S(2)}) collective-permute-start(bf16[64,4096]{1,0:T(8,128)(2,1)S(1)} %step_sum.8), channel_id=1, source_target_pairs={{0,4},{1,3},{4,8},{5,1},{8,12},{9,5},{12,14},{13,9},{14,10},{15,13... | collective-permute-start | bytes 1572872 | tf_op jit(solution)/shard_map/return_long_3/ppermute | solution.py:326
  75.2 2.9 %expert.13 = (bf16[64,4096]{1,0:T(8,128)(2,1)S(1)}, bf16[64,4096]{1,0:T(8,128)(2,1)S(1)}) custom-call(bf16[64,4224]{1,0:T(8,128)(2,1)S(1)} %collective-permute-done.26.refs_0_, bf16[64,4224]{1,0:T(8,128)(2,1)S(1)} %collective-permute-done.14.refs_1_, f32[1,128]{1,0:T(1,128)S(1)} %compare_select_fusion.1.refs_2_.refs_4_, f32[1,1536]{1,0:T(1,128)S(1)} %copy-done.1, ...), custom_call_target="tpu_custom_call" | custom-call | flops 4831838208 | tf_op jit(solution)/shard_map/expert/pallas_call | solution.py:146
  78.8 1.9 %collective-permute-start.23 = (bf16[32,4096]{1,0:T(8,128)(2,1)S(1)}, bf16[32,4096]{1,0:T(8,128)(2,1)S(1)}, u32[]{:S(2)}, u32[]{:S(2)}) collective-permute-start(bf16[32,4096]{1,0:T(8,128)(2,1)S(1)} %get-tuple-element.76), channel_id=1, source_target_pairs={{0,4},{1,3},{4,8},{5,1},{8,12},{9,5},{12,14},{13,9},{14,10},{15,13... | collective-permute-start | bytes 786440 | tf_op jit(solution)/shard_map/return_short_1/ppermute | solution.py:326
  80.8 3.3 %collective-permute-done.28.refs_2_ = bf16[64,4096]{1,0:T(8,128)(2,1)S(1)} collective-permute-done((bf16[64,4096]{1,0:T(8,128)(2,1)S(1)}, bf16[64,4096]{1,0:T(8,128)(2,1)S(1)}, u32[]{:S(2)}, u32[]{:S(2)}) %collective-permute-start.28) | collective-permute-done | bytes 524320 | tf_op jit(solution)/shard_map/return_long_3/ppermute | solution.py:326
  84.3 2.1 %collective-permute-start.29 = (bf16[64,4096]{1,0:T(8,128)(2,1)S(1)}, bf16[64,4096]{1,0:T(8,128)(2,1)S(1)}, u32[]{:S(2)}, u32[]{:S(2)}) collective-permute-start(bf16[64,4096]{1,0:T(8,128)(2,1)S(1)} %step_sum.9), channel_id=1, source_target_pairs={{0,4},{1,3},{4,8},{5,1},{8,12},{9,5},{12,14},{13,9},{14,10},{15,13... | collective-permute-start | bytes 1572872 | tf_op jit(solution)/shard_map/return_long_2/ppermute | solution.py:326
  86.9 2.4 %collective-permute-done.24.short_cross = bf16[32,4096]{1,0:T(8,128)(2,1)S(1)} collective-permute-done((bf16[32,4096]{1,0:T(8,128)(2,1)S(1)}, bf16[32,4096]{1,0:T(8,128)(2,1)S(1)}, u32[]{:S(2)}, u32[]{:S(2)}) %collective-permute-start.24) | collective-permute-done | bytes 262176 | tf_op jit(solution)/shard_map/return_short_1/ppermute | solution.py:326
  89.5 5.8 %collective-permute-done.29.refs_2_ = bf16[64,4096]{1,0:T(8,128)(2,1)S(1)} collective-permute-done((bf16[64,4096]{1,0:T(8,128)(2,1)S(1)}, bf16[64,4096]{1,0:T(8,128)(2,1)S(1)}, u32[]{:S(2)}, u32[]{:S(2)}) %collective-permute-start.29) | collective-permute-done | bytes 524320 | tf_op jit(solution)/shard_map/return_long_2/ppermute | solution.py:326
  96.1 1.7 %collective-permute-start.31 = (bf16[32,4096]{1,0:T(8,128)(2,1)S(1)}, bf16[32,4096]{1,0:T(8,128)(2,1)S(1)}, u32[]{:S(2)}, u32[]{:S(2)}) collective-permute-start(bf16[32,4096]{1,0:T(8,128)(2,1)S(1)} %get-tuple-element.84), channel_id=1, source_target_pairs={{0,4},{1,3},{4,8},{5,1},{8,12},{9,5},{12,14},{13,9},{14,10},{15,13... | collective-permute-start | bytes 786440 | tf_op jit(solution)/shard_map/return_long_1/ppermute | solution.py:326
  97.7 3.7 %collective-permute-done.30.long_cross = bf16[32,4096]{1,0:T(8,128)(2,1)S(1)} collective-permute-done((bf16[32,4096]{1,0:T(8,128)(2,1)S(1)}, bf16[32,4096]{1,0:T(8,128)(2,1)S(1)}, u32[]{:S(2)}, u32[]{:S(2)}) %collective-permute-start.30) | collective-permute-done | bytes 262176 | tf_op jit(solution)/shard_map/return_long_1/ppermute | solution.py:326
  101.4 3.4 %collective-permute-done.31.long_same = bf16[32,4096]{1,0:T(8,128)(2,1)S(1)} collective-permute-done((bf16[32,4096]{1,0:T(8,128)(2,1)S(1)}, bf16[32,4096]{1,0:T(8,128)(2,1)S(1)}, u32[]{:S(2)}, u32[]{:S(2)}) %collective-permute-start.31) | collective-permute-done | bytes 262176 | tf_op jit(solution)/shard_map/return_long_1/ppermute | solution.py:326
  (56 shorter events, 11.4 us)
Async XLA Ops:
  1.3 10.9 %collective-permute-start = (bf16[64,4224]{1,0:T(8,128)(2,1)S(1)}, bf16[64,4224]{1,0:T(8,128)(2,1)S(1)}, u32[]{:S(2)}, u32[]{:S(2)}) collective-permute-start(bf16[64,4224]{1,0:T(8,128)(2,1)S(1)} %get-tuple-element.45.refs_0_), channel_id=1, source_target_pairs={{0,1},{1,0},{2,3},{3,2},{4,5},{5,4},{6,7},{7,6},{8,9},{9,8},{10,11... | collective-permute-start | bytes 1622024 | tf_op jit(solution)/shard_map/swap_in_0/ppermute | solution.py:326
  1.8 14.3 %collective-permute-start.2 = (bf16[64,4224]{1,0:T(8,128)(2,1)S(1)}, bf16[64,4224]{1,0:T(8,128)(2,1)S(1)}, u32[]{:S(2)}, u32[]{:S(2)}) collective-permute-start(bf16[64,4224]{1,0:T(8,128)(2,1)S(1)} %get-tuple-element.45.refs_0_), channel_id=1, source_target_pairs={{0,4},{1,3},{4,8},{5,1},{8,12},{9,5},{12,14},{13,9},{14,10},{15,13... | collective-permute-start | bytes 1622024 | tf_op jit(solution)/shard_map/gather_long_1/ppermute | solution.py:326
  4.5 13.1 %collective-permute-start.3 = (bf16[64,4224]{1,0:T(8,128)(2,1)S(1)}, bf16[64,4224]{1,0:T(8,128)(2,1)S(1)}, u32[]{:S(2)}, u32[]{:S(2)}) collective-permute-start(bf16[64,4224]{1,0:T(8,128)(2,1)S(1)} %get-tuple-element.51), channel_id=1, source_target_pairs={{0,3},{1,4},{4,1},{5,8},{8,5},{9,12},{12,9},{13,14},{14,13},{15,10... | collective-permute-start | bytes 1622024 | tf_op jit(solution)/shard_map/gather_long_1/ppermute | solution.py:326
  17.6 4.2 %collective-permute-start.4 = (bf16[64,4224]{1,0:T(8,128)(2,1)S(1)}, bf16[64,4224]{1,0:T(8,128)(2,1)S(1)}, u32[]{:S(2)}, u32[]{:S(2)}) collective-permute-start(bf16[64,4224]{1,0:T(8,128)(2,1)S(1)} %get-tuple-element.53.refs_2_), channel_id=1, source_target_pairs={{0,1},{1,0},{2,3},{3,2},{4,5},{5,4},{6,7},{7,6},{8,9},{9,8},{10,11... | collective-permute-start | bytes 1622024 | tf_op jit(solution)/shard_map/swap_in_1/ppermute | solution.py:326
  17.7 4.2 %collective-permute-start.5 = (bf16[64,4224]{1,0:T(8,128)(2,1)S(1)}, bf16[64,4224]{1,0:T(8,128)(2,1)S(1)}, u32[]{:S(2)}, u32[]{:S(2)}) collective-permute-start(bf16[64,4224]{1,0:T(8,128)(2,1)S(1)} %get-tuple-element.55.refs_3_), channel_id=1, source_target_pairs={{0,1},{1,0},{2,3},{3,2},{4,5},{5,4},{6,7},{7,6},{8,9},{9,8},{10,11... | collective-permute-start | bytes 1622024 | tf_op jit(solution)/shard_map/swap_in_1/ppermute | solution.py:326
  18.2 9.4 %collective-permute-start.7 = (bf16[64,4224]{1,0:T(8,128)(2,1)S(1)}, bf16[64,4224]{1,0:T(8,128)(2,1)S(1)}, u32[]{:S(2)}, u32[]{:S(2)}) collective-permute-start(bf16[64,4224]{1,0:T(8,128)(2,1)S(1)} %get-tuple-element.55.refs_3_), channel_id=1, source_target_pairs={{0,4},{1,3},{4,8},{5,1},{8,12},{9,5},{12,14},{13,9},{14,10},{15,13... | collective-permute-start | bytes 1622024 | tf_op jit(solution)/shard_map/gather_short_2/ppermute | solution.py:326
  20.3 13.1 %collective-permute-start.14 = (bf16[64,4224]{1,0:T(8,128)(2,1)S(1)}, bf16[64,4224]{1,0:T(8,128)(2,1)S(1)}, u32[]{:S(2)}, u32[]{:S(2)}) collective-permute-start(bf16[64,4224]{1,0:T(8,128)(2,1)S(1)} %get-tuple-element.53.refs_2_), channel_id=1, source_target_pairs={{0,4},{1,3},{4,8},{5,1},{8,12},{9,5},{12,14},{13,9},{14,10},{15,13... | collective-permute-start | bytes 1622024 | tf_op jit(solution)/shard_map/gather_long_2/ppermute | solution.py:326
  27.5 7.9 %collective-permute-start.8 = (bf16[64,4224]{1,0:T(8,128)(2,1)S(1)}, bf16[64,4224]{1,0:T(8,128)(2,1)S(1)}, u32[]{:S(2)}, u32[]{:S(2)}) collective-permute-start(bf16[64,4224]{1,0:T(8,128)(2,1)S(1)} %collective-permute-done.7.refs_1_), channel_id=1, source_target_pairs={{0,1},{1,0},{2,3},{3,2},{4,5},{5,4},{6,7},{7,6},{8,9},{9,8},{10,11... | collective-permute-start | bytes 1622024 | tf_op jit(solution)/shard_map/swap_in_2/ppermute | solution.py:326
  27.5 11.6 %collective-permute-start.10 = (bf16[64,4224]{1,0:T(8,128)(2,1)S(1)}, bf16[64,4224]{1,0:T(8,128)(2,1)S(1)}, u32[]{:S(2)}, u32[]{:S(2)}) collective-permute-start(bf16[64,4224]{1,0:T(8,128)(2,1)S(1)} %collective-permute-done.7.refs_1_), channel_id=1, source_target_pairs={{0,4},{1,3},{4,8},{5,1},{8,12},{9,5},{12,14},{13,9},{14,10},{15,13... | collective-permute-start | bytes 1622024 | tf_op jit(solution)/shard_map/gather_short_3/ppermute | solution.py:326
  33.3 11.6 %collective-permute-start.15 = (bf16[64,4224]{1,0:T(8,128)(2,1)S(1)}, bf16[64,4224]{1,0:T(8,128)(2,1)S(1)}, u32[]{:S(2)}, u32[]{:S(2)}) collective-permute-start(bf16[64,4224]{1,0:T(8,128)(2,1)S(1)} %collective-permute-done.14.refs_1_), channel_id=1, source_target_pairs={{0,4},{1,3},{4,8},{5,1},{8,12},{9,5},{12,14},{13,9},{14,10},{15,13... | collective-permute-start | bytes 1622024 | tf_op jit(solution)/shard_map/gather_long_3/ppermute | solution.py:326
  39.1 7.9 %collective-permute-start.11 = (bf16[64,4224]{1,0:T(8,128)(2,1)S(1)}, bf16[64,4224]{1,0:T(8,128)(2,1)S(1)}, u32[]{:S(2)}, u32[]{:S(2)}) collective-permute-start(bf16[64,4224]{1,0:T(8,128)(2,1)S(1)} %collective-permute-done.10.refs_1_), channel_id=1, source_target_pairs={{0,1},{1,0},{2,3},{3,2},{4,5},{5,4},{6,7},{7,6},{8,9},{9,8},{10,11... | collective-permute-start | bytes 1622024 | tf_op jit(solution)/shard_map/swap_in_3/ppermute | solution.py:326
  44.9 5.2 %collective-permute-start.17 = (bf16[64,4224]{1,0:T(8,128)(2,1)S(1)}, bf16[64,4224]{1,0:T(8,128)(2,1)S(1)}, u32[]{:S(2)}, u32[]{:S(2)}) collective-permute-start(bf16[64,4224]{1,0:T(8,128)(2,1)S(1)} %collective-permute-done.15.refs_1_), channel_id=1, source_target_pairs={{0,1},{1,0},{2,3},{3,2},{4,5},{5,4},{6,7},{7,6},{8,9},{9,8},{10,11... | collective-permute-start | bytes 1622024 | tf_op jit(solution)/shard_map/swap_in_3/ppermute | solution.py:326
  44.9 9.4 %collective-permute-start.16 = (bf16[64,4224]{1,0:T(8,128)(2,1)S(1)}, bf16[64,4224]{1,0:T(8,128)(2,1)S(1)}, u32[]{:S(2)}, u32[]{:S(2)}) collective-permute-start(bf16[64,4224]{1,0:T(8,128)(2,1)S(1)} %collective-permute-done.15.refs_1_), channel_id=1, source_target_pairs={{0,4},{1,3},{4,8},{5,1},{8,12},{9,5},{12,14},{13,9},{14,10},{15,13... | collective-permute-start | bytes 1622024 | tf_op jit(solution)/shard_map/gather_long_4/ppermute | solution.py:326
  49.9 3.1 %collective-permute-start.12 = (bf16[64,4096]{1,0:T(8,128)(2,1)S(1)}, bf16[64,4096]{1,0:T(8,128)(2,1)S(1)}, u32[]{:S(2)}, u32[]{:S(2)}) collective-permute-start(bf16[64,4096]{1,0:T(8,128)(2,1)S(1)} %get-tuple-element.64), channel_id=1, source_target_pairs={{0,1},{1,0},{2,3},{3,2},{4,5},{5,4},{6,7},{7,6},{8,9},{9,8},{10,11... | collective-permute-start | bytes 1572872 | tf_op jit(solution)/shard_map/swap_out_3/ppermute | solution.py:326
  54.3 2.1 %collective-permute-start.18 = (bf16[64,4224]{1,0:T(8,128)(2,1)S(1)}, bf16[64,4224]{1,0:T(8,128)(2,1)S(1)}, u32[]{:S(2)}, u32[]{:S(2)}) collective-permute-start(bf16[64,4224]{1,0:T(8,128)(2,1)S(1)} %collective-permute-done.16.refs_1_), channel_id=1, source_target_pairs={{0,1},{1,0},{2,3},{3,2},{4,5},{5,4},{6,7},{7,6},{8,9},{9,8},{10,11... | collective-permute-start | bytes 1622024 | tf_op jit(solution)/shard_map/swap_in_4/ppermute | solution.py:326
  54.3 9.2 %collective-permute-start.13 = (bf16[64,4096]{1,0:T(8,128)(2,1)S(1)}, bf16[64,4096]{1,0:T(8,128)(2,1)S(1)}, u32[]{:S(2)}, u32[]{:S(2)}) collective-permute-start(bf16[64,4096]{1,0:T(8,128)(2,1)S(1)} %step_sum.5), channel_id=1, source_target_pairs={{0,4},{1,3},{4,8},{5,1},{8,12},{9,5},{12,14},{13,9},{14,10},{15,13... | collective-permute-start | bytes 1572872 | tf_op jit(solution)/shard_map/return_short_3/ppermute | solution.py:326
  59.2 4.3 %collective-permute-start.19 = (bf16[64,4096]{1,0:T(8,128)(2,1)S(1)}, bf16[64,4096]{1,0:T(8,128)(2,1)S(1)}, u32[]{:S(2)}, u32[]{:S(2)}) collective-permute-start(bf16[64,4096]{1,0:T(8,128)(2,1)S(1)} %get-tuple-element.70), channel_id=1, source_target_pairs={{0,1},{1,0},{2,3},{3,2},{4,5},{5,4},{6,7},{7,6},{8,9},{9,8},{10,11... | collective-permute-start | bytes 1572872 | tf_op jit(solution)/shard_map/swap_out_4/ppermute | solution.py:326
  59.4 15.8 %collective-permute-start.26 = (bf16[64,4224]{1,0:T(8,128)(2,1)S(1)}, bf16[64,4224]{1,0:T(8,128)(2,1)S(1)}, u32[]{:S(2)}, u32[]{:S(2)}) collective-permute-start(bf16[64,4224]{1,0:T(8,128)(2,1)S(1)} %collective-permute-done.14.refs_1_), channel_id=1, source_target_pairs={{0,1},{1,0},{2,3},{3,2},{4,5},{5,4},{6,7},{7,6},{8,9},{9,8},{10,11... | collective-permute-start | bytes 1622024 | tf_op jit(solution)/shard_map/swap_in_2/ppermute | solution.py:326
  59.8 6.5 %collective-permute-start.9 = (bf16[64,4096]{1,0:T(8,128)(2,1)S(1)}, bf16[64,4096]{1,0:T(8,128)(2,1)S(1)}, u32[]{:S(2)}, u32[]{:S(2)}) collective-permute-start(bf16[64,4096]{1,0:T(8,128)(2,1)S(1)} %get-tuple-element.61), channel_id=1, source_target_pairs={{0,1},{1,0},{2,3},{3,2},{4,5},{5,4},{6,7},{7,6},{8,9},{9,8},{10,11... | collective-permute-start | bytes 1572872 | tf_op jit(solution)/shard_map/swap_out_2/ppermute | solution.py:326
  63.6 9.2 %collective-permute-start.22 = (bf16[64,4096]{1,0:T(8,128)(2,1)S(1)}, bf16[64,4096]{1,0:T(8,128)(2,1)S(1)}, u32[]{:S(2)}, u32[]{:S(2)}) collective-permute-start(bf16[64,4096]{1,0:T(8,128)(2,1)S(1)} %step_sum.6), channel_id=1, source_target_pairs={{0,4},{1,3},{4,8},{5,1},{8,12},{9,5},{12,14},{13,9},{14,10},{15,13... | collective-permute-start | bytes 1572872 | tf_op jit(solution)/shard_map/return_long_4/ppermute | solution.py:326
  65.7 7.1 %collective-permute-start.21 = (bf16[64,4096]{1,0:T(8,128)(2,1)S(1)}, bf16[64,4096]{1,0:T(8,128)(2,1)S(1)}, u32[]{:S(2)}, u32[]{:S(2)}) collective-permute-start(bf16[64,4096]{1,0:T(8,128)(2,1)S(1)} %get-tuple-element.73), channel_id=1, source_target_pairs={{0,1},{1,0},{2,3},{3,2},{4,5},{5,4},{6,7},{7,6},{8,9},{9,8},{10,11... | collective-permute-start | bytes 1572872 | tf_op jit(solution)/shard_map/swap_out_3/ppermute | solution.py:326
  65.7 12.9 %collective-permute-start.6 = (bf16[64,4096]{1,0:T(8,128)(2,1)S(1)}, bf16[64,4096]{1,0:T(8,128)(2,1)S(1)}, u32[]{:S(2)}, u32[]{:S(2)}) collective-permute-start(bf16[64,4096]{1,0:T(8,128)(2,1)S(1)} %get-tuple-element.57), channel_id=1, source_target_pairs={{0,1},{1,0},{2,3},{3,2},{4,5},{5,4},{6,7},{7,6},{8,9},{9,8},{10,11... | collective-permute-start | bytes 1572872 | tf_op jit(solution)/shard_map/swap_out_1/ppermute | solution.py:326
  66.4 12.2 %collective-permute-start.20 = (bf16[64,4096]{1,0:T(8,128)(2,1)S(1)}, bf16[64,4096]{1,0:T(8,128)(2,1)S(1)}, u32[]{:S(2)}, u32[]{:S(2)}) collective-permute-start(bf16[64,4096]{1,0:T(8,128)(2,1)S(1)} %step_sum.7), channel_id=1, source_target_pairs={{0,4},{1,3},{4,8},{5,1},{8,12},{9,5},{12,14},{13,9},{14,10},{15,13... | collective-permute-start | bytes 1572872 | tf_op jit(solution)/shard_map/return_short_2/ppermute | solution.py:326
  73.1 11.0 %collective-permute-start.28 = (bf16[64,4096]{1,0:T(8,128)(2,1)S(1)}, bf16[64,4096]{1,0:T(8,128)(2,1)S(1)}, u32[]{:S(2)}, u32[]{:S(2)}) collective-permute-start(bf16[64,4096]{1,0:T(8,128)(2,1)S(1)} %step_sum.8), channel_id=1, source_target_pairs={{0,4},{1,3},{4,8},{5,1},{8,12},{9,5},{12,14},{13,9},{14,10},{15,13... | collective-permute-start | bytes 1572872 | tf_op jit(solution)/shard_map/return_long_3/ppermute | solution.py:326
  78.1 6.0 %collective-permute-start.27 = (bf16[64,4096]{1,0:T(8,128)(2,1)S(1)}, bf16[64,4096]{1,0:T(8,128)(2,1)S(1)}, u32[]{:S(2)}, u32[]{:S(2)}) collective-permute-start(bf16[64,4096]{1,0:T(8,128)(2,1)S(1)} %get-tuple-element.80), channel_id=1, source_target_pairs={{0,1},{1,0},{2,3},{3,2},{4,5},{5,4},{6,7},{7,6},{8,9},{9,8},{10,11... | collective-permute-start | bytes 1572872 | tf_op jit(solution)/shard_map/swap_out_2/ppermute | solution.py:326
  78.1 8.3 %collective-permute-start.1 = (bf16[64,4096]{1,0:T(8,128)(2,1)S(1)}, bf16[64,4096]{1,0:T(8,128)(2,1)S(1)}, u32[]{:S(2)}, u32[]{:S(2)}) collective-permute-start(bf16[64,4096]{1,0:T(8,128)(2,1)S(1)} %get-tuple-element.49), channel_id=1, source_target_pairs={{0,1},{1,0},{2,3},{3,2},{4,5},{5,4},{6,7},{7,6},{8,9},{9,8},{10,11... | collective-permute-start | bytes 1572872 | tf_op jit(solution)/shard_map/swap_out_0/ppermute | solution.py:326
  78.8 8.0 %collective-permute-start.23 = (bf16[32,4096]{1,0:T(8,128)(2,1)S(1)}, bf16[32,4096]{1,0:T(8,128)(2,1)S(1)}, u32[]{:S(2)}, u32[]{:S(2)}) collective-permute-start(bf16[32,4096]{1,0:T(8,128)(2,1)S(1)} %get-tuple-element.76), channel_id=1, source_target_pairs={{0,4},{1,3},{4,8},{5,1},{8,12},{9,5},{12,14},{13,9},{14,10},{15,13... | collective-permute-start | bytes 786440 | tf_op jit(solution)/shard_map/return_short_1/ppermute | solution.py:326
  80.8 8.5 %collective-permute-start.24 = (bf16[32,4096]{1,0:T(8,128)(2,1)S(1)}, bf16[32,4096]{1,0:T(8,128)(2,1)S(1)}, u32[]{:S(2)}, u32[]{:S(2)}) collective-permute-start(bf16[32,4096]{1,0:T(8,128)(2,1)S(1)} %get-tuple-element.77), channel_id=1, source_target_pairs={{0,5},{1,2},{4,9},{5,0},{8,13},{9,4},{12,15},{13,8},{14,11},{15,12... | collective-permute-start | bytes 786440 | tf_op jit(solution)/shard_map/return_short_1/ppermute | solution.py:326
  84.1 11.2 %collective-permute-start.25 = (bf16[64,4096]{1,0:T(8,128)(2,1)S(1)}, bf16[64,4096]{1,0:T(8,128)(2,1)S(1)}, u32[]{:S(2)}, u32[]{:S(2)}) collective-permute-start(bf16[64,4096]{1,0:T(8,128)(2,1)S(1)} %get-tuple-element.78), channel_id=1, source_target_pairs={{0,1},{1,0},{2,3},{3,2},{4,5},{5,4},{6,7},{7,6},{8,9},{9,8},{10,11... | collective-permute-start | bytes 1572872 | tf_op jit(solution)/shard_map/swap_out_1/ppermute | solution.py:326
  84.3 11.0 %collective-permute-start.29 = (bf16[64,4096]{1,0:T(8,128)(2,1)S(1)}, bf16[64,4096]{1,0:T(8,128)(2,1)S(1)}, u32[]{:S(2)}, u32[]{:S(2)}) collective-permute-start(bf16[64,4096]{1,0:T(8,128)(2,1)S(1)} %step_sum.9), channel_id=1, source_target_pairs={{0,4},{1,3},{4,8},{5,1},{8,12},{9,5},{12,14},{13,9},{14,10},{15,13... | collective-permute-start | bytes 1572872 | tf_op jit(solution)/shard_map/return_long_2/ppermute | solution.py:326
  95.5 5.9 %collective-permute-start.30 = (bf16[32,4096]{1,0:T(8,128)(2,1)S(1)}, bf16[32,4096]{1,0:T(8,128)(2,1)S(1)}, u32[]{:S(2)}, u32[]{:S(2)}) collective-permute-start(bf16[32,4096]{1,0:T(8,128)(2,1)S(1)} %get-tuple-element.83), channel_id=1, source_target_pairs={{0,5},{1,2},{4,9},{5,0},{8,13},{9,4},{12,15},{13,8},{14,11},{15,12... | collective-permute-start | bytes 786440 | tf_op jit(solution)/shard_map/return_long_1/ppermute | solution.py:326
  96.1 8.7 %collective-permute-start.31 = (bf16[32,4096]{1,0:T(8,128)(2,1)S(1)}, bf16[32,4096]{1,0:T(8,128)(2,1)S(1)}, u32[]{:S(2)}, u32[]{:S(2)}) collective-permute-start(bf16[32,4096]{1,0:T(8,128)(2,1)S(1)} %get-tuple-element.84), channel_id=1, source_target_pairs={{0,4},{1,3},{4,8},{5,1},{8,12},{9,5},{12,14},{13,9},{14,10},{15,13... | collective-permute-start | bytes 786440 | tf_op jit(solution)/shard_map/return_long_1/ppermute | solution.py:326
  (2 other events, 24.3 us)
